TPU v7x, 32 devices: a whole 2x2x4 slice. The times are simulated.
32 devices in a mesh: groups: 2 (over x), wide: 16 (over z, y, core).
Axes of the slice: x: 2, y: 2, z: 4, core: 2. Of those that a mesh axis runs over, the one named last changes fastest.
Arguments:
- train_act: bfloat16 [512, 4096], P(('groups', 'wide')), parts along dimension 0, may hold values from -6 to 6
- train_grad: bfloat16 [512, 32768], P(('groups', 'wide')), parts along dimension 0, may hold values from -6 to 6
- seq_ids: int32 [512], P(('groups', 'wide')), parts along dimension 0, may hold values from 0 to 7, never falling along the last dimension, each value on 1 to 64 neighbouring positions
- act_basis: bfloat16 [512, 4096], replicated, may hold values from -0.25 to 0.25
- grad_basis: bfloat16 [512, 32768], P(None, 'wide'), may hold values from -0.25 to 0.25
- eigenvalues: bfloat16 [32768, 4096], P('wide'), may hold values from 0.099609375 to 10
- query_factors: bfloat16 [32, 16, 36864], P('wide'), may hold values from -6 to 6
- owners: int32 [2], replicated, may hold values from 0 to 15, as said below
Outputs:
- scores: float32 [16, 2], P('groups'), parts along dimension 0
There are 2 independent parts, one for each index of `groups`. A program takes and returns all parts, laid end to end along the dimension named above; an argument that names none is the same for every part. Nothing has to cross between parts.
Inputs may be any that keep to these rules, and one draw needn't show every extreme that they name: The owners of different query batches are different devices, and one batch is always owned by the last device along wide.
All inputs are finite; a program needn't handle non-finite values.
Results may differ from a plain program's by a relative error of at most 0.0065.
Values may be sent and summed in bfloat16 or wider, within the bound.
No kernel may reach another device: no remote copies, remote signals or barrier semaphores. Data moves between devices by JAX's collectives and lax.ppermute only.
A program may use at most 192 MiB of HBM per device.

v0:
```python
import math

import jax
import jax.numpy as jnp
from jax import lax
from jax.sharding import PartitionSpec as P

D = 4096
FF = 32768
SEQ_MEAN = 32
QT = 16


damping = 0.1


def spread(x, axis, root):
    mine = lax.axis_index(axis) == root
    return lax.psum(jnp.where(mine, x, jnp.zeros_like(x)), axis)


def rotate_blocks(values, basis_cols):
    row_count = values.shape[0]
    out_width = basis_cols.shape[1]
    block_size = basis_cols.shape[0]
    block_count = max(1, out_width // block_size)
    inner_width = values.shape[1] // block_count
    outer_width = out_width // block_count
    blocks = values.reshape(row_count, block_count, inner_width)
    table_view = basis_cols.reshape(inner_width, block_count, outer_width)
    turned = jnp.einsum("tkr,rkc->tkc", blocks, table_view, preferred_element_type=jnp.float32)
    return turned.reshape(row_count, out_width).astype(jnp.bfloat16)


def precondition(grad_part, act_part, inverse):
    outer_sum = lax.dot_general(
        grad_part, act_part, (((0,), (0,)), ((), ())), preferred_element_type=jnp.float32
    )
    return (outer_sum * inverse).astype(jnp.bfloat16)


def score_rows(act_rows, member_rows, grad_rows, stacked, batch_count):
    row_count = act_rows.shape[0]
    image_rows = lax.dot_general(
        act_rows, stacked, (((1,), (1,)), ((), ())), preferred_element_type=jnp.float32
    )
    image_rows = image_rows.reshape(row_count, batch_count, grad_rows.shape[1])
    token_score = jnp.sum(image_rows * grad_rows[:, None, :], axis=2)
    return lax.dot_general(
        member_rows.astype(jnp.float32),
        token_score,
        (((0,), (0,)), ((), ())),
        precision=lax.Precision.HIGHEST,
    )


def per_device(
    train_act, train_grad, seq_ids, act_basis, grad_basis, eigenvalues, query_factors, owners
):
    wide_count = lax.axis_size("wide")
    my_index = lax.axis_index("wide")
    tok_local = train_act.shape[0]
    seq_count = tok_local * wide_count // SEQ_MEAN
    col_width = grad_basis.shape[1]
    hidden_width = train_grad.shape[1]
    batch_count = owners.shape[0]
    score_scale = 1.0 / math.sqrt(FF * D * QT * SEQ_MEAN)
    rot_act = rotate_blocks(train_act, act_basis)
    member = (seq_ids[:, None] == jnp.arange(seq_count, dtype=jnp.int32)[None, :]).astype(
        jnp.bfloat16
    )
    raw_cols = lax.all_to_all(train_grad, "wide", split_axis=1, concat_axis=0, tiled=True)
    rot_grad = rotate_blocks(raw_cols, grad_basis)
    shared_list = []
    for batch_index in range(batch_count):
        shared_list.append(spread(query_factors[batch_index], "wide", owners[batch_index]))
    inverse = 1.0 / (eigenvalues.astype(jnp.float32) + damping)
    precond_list = []
    for shared in shared_list:
        grad_part = lax.dynamic_slice_in_dim(shared, my_index * col_width, col_width, 1)
        act_part = shared[:, hidden_width:]
        precond_list.append(precondition(grad_part, act_part, inverse))
    stacked = jnp.concatenate(precond_list, axis=0)
    act_rows = lax.all_gather(rot_act, "wide", axis=0, tiled=True)
    member_rows = lax.all_gather(member, "wide", axis=0, tiled=True)
    totals = score_rows(act_rows, member_rows, rot_grad, stacked, batch_count)
    return lax.psum(totals, "wide") * score_scale


def solution(mesh):
    return jax.shard_map(
        per_device,
        mesh=mesh,
        in_specs=(
            P(("groups", "wide"), None),
            P(("groups", "wide"), None),
            P(("groups", "wide")),
            P(),
            P(None, "wide"),
            P("wide", None),
            P("wide", None, None),
            P(),
        ),
        out_specs=P("groups", None),
        check_vma=False,
    )
```

profile of v0, /device:TPU:0, one launch (start us, length us, event | category | flops | bytes accessed | tf_op | source)
XLA Modules:
  0.0 240.3 jit_solution(6262789265676834845)
XLA Ops:
  6.5 1.3 fusion.26
  9.1 3.2 %select_bitcast_fusion.1 = (bf16[16,36864]{1,0:T(8,128)(2,1)}, bf16[16,36864]{1,0:T(8,128)(2,1)}) fusion(bf16[2,16,36864]{2,1,0:T(8,128)(2,1)} %param.14, pred[]{:T(512)S(6)} %eq.22, pred[]{:T(512)S(6)} %eq.23), kind=kLoop, calls=%fused_computation.14 | loop fusion | flops 1179648 | bytes 4718594 | tf_op jit(solution)/shard_map/jit(_where)/select_n | solution.py:19
  12.3 1.1 copy.49
  13.4 7.4 %all-to-all-start = ((bf16[16,16,2048]{2,0,1:T(8,128)(2,1)}), bf16[16,16,2048]{2,0,1:T(8,128)(2,1)S(1)}, u32[]{:S(2)}, u32[]{:S(2)}) async-start(bf16[16,16,2048]{2,0,1:T(8,128)(2,1)} %bitcast.38), calls=%async_computation | async-start | bytes 2097152 | tf_op jit(solution)/shard_map/all_to_all | solution.py:72
  20.8 0.0 all-gather.3.cloned.1.call-start
  20.9 2.9 %fusion.11 = bf16[8,2,8,512]{3,2,1,0:T(8,128)(2,1)S(1)} fusion(bf16[64,8,8,512]{3,2,1,0:T(8,128)(2,1)} %bitcast.41, bf16[2,8,8,512]{3,2,1,0:T(8,128)(2,1)S(1)} %bitcast.45), kind=kOutput, calls=%fused_computation.16 | convolution fusion | flops 67174400 | bytes 4456448 | tf_op jit(solution)/shard_map/tkr,rkc->tkc/dot_general | solution.py:31
  23.8 0.7 copy.33
  24.4 2.9 %copy.29 = bf16[512,2048]{0,1:T(8,128)(2,1)S(1)} copy(bf16[512,2048]{1,0:T(8,128)(2,1)} %param.12) | data formatting | bytes 4194304 | tf_op jit(solution)/shard_map/reshape | solution.py:30
  27.4 35.8 %all-gather = bf16[16,16,8]{1,2,0:T(8,128)(2,1)S(1)} all-gather(bf16[1,16,8]{1,2,0:T(8,128)(2,1)S(1)} %fusion.22), channel_id=1, replica_groups=mesh['groups'=2,'wide'=16] {'wide'}, dimensions={0}, use_global_device_ids=true | all-gather | bytes 4352 | tf_op jit(solution)/shard_map/all_gather | solution.py:85
  63.2 0.1 reshape.46
  63.3 67.3 %all-reduce.3.cloned.1.call-done = (bf16[16,36864]{1,0:T(8,128)(2,1)}, bf16[16,36864]{1,0:T(8,128)(2,1)}) async-done(((bf16[16,36864]{1,0:T(8,128)(2,1)}, bf16[16,36864]{1,0:T(8,128)(2,1)}), (bf16[16,36864]{1,0:T(8,128)(2,1)}, bf16[16,36864]{1,0:T(8,128)(2,1)})) %all-reduce.3.cloned.1.call-update) | async-done | bytes 2359312 | tf_op jit(solution)/shard_map/psum | solution.py:19
  130.6 12.0 %multiply_convert_fusion.1 = bf16[2048,4096]{1,0:T(8,128)(2,1)} fusion(bf16[2048,4096]{1,0:T(8,128)(2,1)} %param.13, bf16[16,36864]{1,0:T(8,128)(2,1)} %get-tuple-element.6, s32[]{:T(128)S(6)} %select_n.27), kind=kOutput, calls=%fused_computation.5 | convolution fusion | flops 310378496 | bytes 33751044 | tf_op jit(solution)/shard_map/dot_general | solution.py:36
  142.6 11.9 %multiply_convert_fusion = bf16[2048,4096]{1,0:T(8,128)(2,1)} fusion(bf16[2048,4096]{1,0:T(8,128)(2,1)} %param.13, bf16[16,36864]{1,0:T(8,128)(2,1)} %get-tuple-element.5, s32[]{:T(128)S(6)} %select_n.27), kind=kOutput, calls=%fused_computation.4 | convolution fusion | flops 310378496 | bytes 33751044 | tf_op jit(solution)/shard_map/dot_general | solution.py:36
  154.5 1.0 copy-done
  155.5 1.8 reshape.43
  157.4 2.1 fusion.7
  159.5 1.9 copy.28
  161.4 12.3 %all-gather.3.cloned.1.call-done = bf16[256,4096]{1,0:T(8,128)(2,1)} async-done(((bf16[16,4096]{1,0:T(8,128)(2,1)}), bf16[256,4096]{1,0:T(8,128)(2,1)}) %all-gather.3.cloned.1.call-update) | async-done | bytes 2097168 | tf_op jit(solution)/shard_map/all_gather | solution.py:84
  173.7 16.7 %fusion = f32[256,4096]{1,0:T(8,128)} fusion(bf16[256,4096]{1,0:T(8,128)(2,1)} %all-gather.3.cloned.1.call-done, bf16[2048,4096]{1,0:T(8,128)(2,1)} %multiply_convert_fusion, bf16[2048,4096]{1,0:T(8,128)(2,1)} %multiply_convert_fusion.1), kind=kOutput, calls=%fused_computation | convolution fusion | flops 8657043456 | bytes 39845888 | tf_op jit(solution)/shard_map/dot_general | solution.py:44
  190.4 6.6 %reshape.41 = f32[256,2,2048]{2,1,0:T(2,128)} reshape(f32[256,4096]{1,0:T(8,128)} %fusion) | data formatting | bytes 8388608 | tf_op jit(solution)/shard_map/reshape | solution.py:47
  197.0 4.2 %multiply_reduce_fusion = f32[256,2]{1,0:T(8,128)S(1)} fusion(f32[256,2,2048]{2,1,0:T(2,128)} %reshape.41, f32[256,2048]{1,0:T(8,128)S(1)} %copy.28), kind=kLoop, calls=%fused_computation.10 | loop fusion | flops 2096640 | bytes 6293504 | tf_op jit(solution)/shard_map/reduce_sum | solution.py:48
  201.2 0.2 fusion.27
  201.5 31.4 %psum.23 = f32[8,2]{0,1:T(2,128)S(1)} all-reduce(f32[8,2]{0,1:T(2,128)S(1)} %fusion.27), channel_id=1, replica_groups=mesh['groups'=2,'wide'=16] {'wide'}, use_global_device_ids=true, to_apply=%region_3.4 | all-reduce | flops 16 | bytes 128 | tf_op jit(solution)/shard_map/psum | solution.py:87
  232.9 0.6 broadcast_multiply_fusion
  (13 shorter events, 0.1 us)
Async XLA Ops:
  6.5 5.8 %copy-start.1 = (bf16[16,32768]{1,0:T(8,128)(2,1)S(1)}, bf16[16,32768]{1,0:T(8,128)(2,1)}, u32[]{:S(2)}) copy-start(bf16[16,32768]{1,0:T(8,128)(2,1)} %param.9) | copy-start | bytes 3145732
  6.5 124.1 %all-reduce.3.cloned.1.call-start = ((), (), s32[]{:S(2)}) async-start(), calls=%async_computation.2 | async-start | bytes 4718592 | tf_op jit(solution)/shard_map/psum | solution.py:19
  12.3 8.6 %copy-start.2 = (bf16[16,4096]{1,0:T(8,128)(2,1)S(1)}, bf16[16,4096]{1,0:T(8,128)(2,1)}, u32[]{:S(2)}) copy-start(bf16[16,4096]{1,0:T(8,128)(2,1)} %param.8) | copy-start | bytes 393220
  13.4 141.1 %all-to-all-start = ((bf16[16,16,2048]{2,0,1:T(8,128)(2,1)}), bf16[16,16,2048]{2,0,1:T(8,128)(2,1)S(1)}, u32[]{:S(2)}, u32[]{:S(2)}) async-start(bf16[16,16,2048]{2,0,1:T(8,128)(2,1)} %bitcast.38), calls=%async_computation | async-start | bytes 2097152 | tf_op jit(solution)/shard_map/all_to_all | solution.py:72
  20.8 152.9 %all-gather.3.cloned.1.call-start = ((), (), s32[]{:S(2)}) async-start(), calls=%async_computation.1 | async-start | bytes 2228224 | tf_op jit(solution)/shard_map/all_gather | solution.py:84
  20.9 6.5 %copy-start.3 = (s32[16]{0:T(128)S(1)}, s32[16]{0:T(128)}, u32[]{:S(2)}) copy-start(s32[16]{0:T(128)} %param.10) | copy-start | bytes 196
  154.5 1.0 copy-start
Sparse Core Ops, SparseCore 0:
  12.5 118.1 all-reduce.2
  132.8 40.8 all-gather.2
where the time goes:
time: 241 us; the launch traced here: 240 us
  waiting for transfers between devices  79.7 us (33%)
  blocking collectives  67.2 us (28%)
  matrix products  45.9 us (19%)
  local copies, waits for them, and re-layouts  17.4 us (7%)
  between operations  14.7 us (6%)
  other arithmetic  7.98 us (3%)
  starting transfers between devices  7.43 us (3%)
    psum x1, waiting for transfers between devices, spread(): return lax.psum(jnp.where(mine, x, jnp.zeros_like(x)), axis)  67.3 us
    all_gather x1, blocking collectives, per_device(): member_rows = lax.all_gather(member, 'wide', axis=0, tiled=True)  35.8 us
    psum x1, blocking collectives, per_device(): return lax.psum(totals, 'wide') * score_scale  31.4 us
    dot_general x2, matrix products, precondition(): lax.dot_general(grad_part, act_part, (((0,), (0,)), ((), ())), preferred_...  23.9 us
    dot_general x1, matrix products, score_rows(): lax.dot_general(act_rows, stacked, (((1,), (1,)), ((), ())), preferred_el...  16.7 us
    all_gather x1, waiting for transfers between devices, per_device(): act_rows = lax.all_gather(rot_act, 'wide', axis=0, tiled=True)  12.3 us
    all_to_all x1, starting transfers between devices, per_device(): lax.all_to_all(train_grad, 'wide', split_axis=1, concat_axis=0, tiled=True)  7.39 us
    reshape x1, local copies, waits for them, and re-layouts, score_rows(): image_rows = image_rows.reshape(row_count, batch_count, grad_rows.shape[1])  6.58 us
  transfers between devices with their start and end apart: 3, of which 2 were waited for; matrix products, arithmetic and copies ran while one was open for 16% of the time, Pallas kernels for 0%

commit v1 on v0

v1 whole, which is shorter than its diff:
```python
import functools
import math

import jax
import jax.numpy as jnp
from jax import lax
from jax.experimental import pallas as pl
from jax.experimental.pallas import tpu as pltpu
from jax.sharding import PartitionSpec as P

D = 4096
FF = 32768
SEQ_MEAN = 32
QT = 16


damping = 0.1


def image_kernel(batch_count, act_ref, basis_ref, left_ref, right_ref, eig_ref, out_ref, rot_ref, pre_ref):
    rows = eig_ref.shape[0]
    depth = basis_ref.shape[0]
    width = act_ref.shape[1]
    blocks = width // depth

    @pl.when(pl.program_id(0) == 0)
    def _():
        for k in range(blocks):
            cols = slice(k * depth, (k + 1) * depth)
            turned = jnp.dot(act_ref[:, cols], basis_ref[:, cols], preferred_element_type=jnp.float32)
            rot_ref[cols, :] = turned.astype(jnp.bfloat16).T

    def produce(k, carry):
        cols = pl.ds(pl.multiple_of(k * depth, depth), depth)
        inverse = 1.0 / (eig_ref[:, cols].astype(jnp.float32) + damping)
        for b in range(batch_count):
            u = slice(b * QT, (b + 1) * QT)
            outer_sum = lax.dot_general(
                left_ref[u, :], right_ref[u, cols], (((0,), (0,)), ((), ())),
                preferred_element_type=jnp.float32,
            )
            pre_ref[b * rows:(b + 1) * rows, cols] = (outer_sum * inverse).astype(jnp.bfloat16)
        return carry

    lax.fori_loop(0, blocks, produce, 0)
    for b in range(batch_count):
        out_ref[b] = jnp.dot(
            pre_ref[b * rows:(b + 1) * rows, :], rot_ref[...], preferred_element_type=jnp.float32
        )


def images(act_all, act_basis, left, right, eigenvalues, batch_count):
    tokens, width = act_all.shape
    hidden = eigenvalues.shape[0]
    rows = min(256, hidden)
    whole = lambda s: pl.BlockSpec(s, lambda i: (0, 0), pipeline_mode=pl.Buffered(1))
    return pl.pallas_call(
        functools.partial(image_kernel, batch_count),
        grid=(hidden // rows,),
        in_specs=[
            whole(act_all.shape),
            whole(act_basis.shape),
            pl.BlockSpec((left.shape[0], rows), lambda i: (0, i)),
            whole(right.shape),
            pl.BlockSpec((rows, width), lambda i: (i, 0)),
        ],
        out_specs=pl.BlockSpec((batch_count, rows, tokens), lambda i: (0, i, 0)),
        out_shape=jax.ShapeDtypeStruct((batch_count, hidden, tokens), jnp.float32),
        scratch_shapes=[
            pltpu.VMEM((width, tokens), jnp.bfloat16),
            pltpu.VMEM((batch_count * rows, width), jnp.bfloat16),
        ],
        compiler_params=pltpu.CompilerParams(vmem_limit_bytes=56 * 1024 * 1024),
        cost_estimate=pl.CostEstimate(
            flops=2 * hidden * width * (tokens + 256) * batch_count,
            bytes_accessed=2 * hidden * width,
            transcendentals=0,
        ),
    )(act_all, act_basis, left, right, eigenvalues)


def score_kernel(batch_count, seq_count, grad_ref, basis_ref, image_ref, ids_ref, out_ref):
    depth = basis_ref.shape[0]
    hidden = basis_ref.shape[1]
    tokens = grad_ref.shape[0]
    inner = min(depth, hidden)
    token = [jnp.zeros((1, tokens), jnp.float32) for _ in range(batch_count)]
    for k in range(hidden // inner):
        cols = slice(k * inner, (k + 1) * inner)
        turned = jnp.dot(
            grad_ref[:, cols], basis_ref[:, cols], preferred_element_type=jnp.float32
        ).astype(jnp.bfloat16).T.astype(jnp.float32)
        for b in range(batch_count):
            token[b] += jnp.sum(image_ref[b, cols, :] * turned, axis=0, keepdims=True)
    seqs = lax.broadcasted_iota(jnp.int32, (seq_count, tokens), 0)
    member = ids_ref[...] == seqs
    for b in range(batch_count):
        out_ref[b] = jnp.sum(jnp.where(member, token[b], 0.0), axis=1, keepdims=True)


def score_parts(grads, grad_basis, image, ids, batch_count, seq_count):
    return pl.pallas_call(
        functools.partial(score_kernel, batch_count, seq_count),
        out_shape=jax.ShapeDtypeStruct((batch_count, seq_count, 1), jnp.float32),
        compiler_params=pltpu.CompilerParams(vmem_limit_bytes=56 * 1024 * 1024),
        cost_estimate=pl.CostEstimate(
            flops=2 * grads.shape[0] * grads.shape[1] * grad_basis.shape[0],
            bytes_accessed=4 * image.size,
            transcendentals=0,
        ),
    )(grads, grad_basis, image, ids)


def swap(x, axis, bit):
    count = lax.axis_size(axis)
    return lax.ppermute(x, axis, [(i, i ^ bit) for i in range(count)])


def per_device(
    train_act, train_grad, seq_ids, act_basis, grad_basis, eigenvalues, query_factors, owners
):
    wide_count = lax.axis_size("wide")
    me = lax.axis_index("wide")
    group = lax.axis_index("groups")
    tok_local = train_act.shape[0]
    seq_count = tok_local * wide_count // SEQ_MEAN
    cols = grad_basis.shape[1]
    hidden = train_grad.shape[1]
    batch_count = owners.shape[0]
    score_scale = 1.0 / math.sqrt(FF * D * QT * SEQ_MEAN)

    raw_cols = lax.all_to_all(train_grad, "wide", split_axis=1, concat_axis=0, tiled=True)

    ids_cols = jnp.broadcast_to(seq_ids[:, None].astype(jnp.bfloat16), (tok_local, 128))
    act_ids = lax.all_gather(jnp.concatenate([train_act, ids_cols], axis=1), "wide", axis=0, tiled=True)
    act_all = act_ids[:, :train_act.shape[1]]
    ids = act_ids[:, train_act.shape[1]].astype(jnp.int32)[None, :]

    batch = group % batch_count
    owner = owners[batch]
    mine = query_factors[batch]
    act_piece = (mine.shape[1] - hidden) // wide_count
    held = jnp.concatenate(
        [
            mine[:, :hidden].reshape(QT, wide_count, cols),
            mine[:, hidden:].reshape(QT, wide_count, act_piece),
        ],
        axis=2,
    ).transpose(1, 0, 2)
    bit = 1
    while bit < wide_count:
        pairs = held.reshape(held.shape[0] // 2, 2, QT, cols + act_piece)
        my_bit = (me // bit) % 2
        keep = jnp.where(my_bit == 1, pairs[:, 1], pairs[:, 0])
        give = jnp.where(my_bit == 1, pairs[:, 0], pairs[:, 1])
        got = swap(give, "wide", bit)
        held = jnp.where((owner // bit) % 2 == my_bit, keep, got)
        bit *= 2
    first = held[0]
    other = swap(first, "groups", 1)
    both = jnp.where(batch == 0, jnp.stack([first, other]), jnp.stack([other, first]))
    left = both[:, :, :cols].reshape(batch_count * QT, cols)
    right = lax.all_gather(
        both[:, :, cols:].reshape(batch_count * QT, act_piece), "wide", axis=1, tiled=True
    )

    image = images(act_all, act_basis, left, right, eigenvalues, batch_count)
    parts = score_parts(raw_cols, grad_basis, image, ids, batch_count, seq_count)
    totals = parts[:, :, 0].T
    bit = 1
    while bit < wide_count:
        totals = totals + swap(totals, "wide", bit)
        bit *= 2
    return totals * score_scale


def solution(mesh):
    return jax.shard_map(
        per_device,
        mesh=mesh,
        in_specs=(
            P(("groups", "wide"), None),
            P(("groups", "wide"), None),
            P(("groups", "wide")),
            P(),
            P(None, "wide"),
            P("wide", None),
            P("wide", None, None),
            P(),
        ),
        out_specs=P("groups", None),
        check_vma=False,
    )
```

time: 241 us -> 159 us (0.66)
  waiting for transfers between devices: 79.7 us -> 19.2 us
  matrix products: 45.9 us -> 0 us
  Pallas kernels: 0 us -> 40.9 us
  blocking collectives: 67.2 us -> 39.9 us
  starting transfers between devices: 7.43 us -> 24.1 us
  local copies, waits for them, and re-layouts: 17.4 us -> 11.4 us
    psum x1 -> x0, waiting for transfers between devices: 67.3 us -> none  [spread(): return lax.psum(jnp.where(mine, x, jnp.zeros_like(x)), axis)]
    dot_general x6 -> x0, matrix products: 45.9 us -> none  [the longest x2 23.9 us: precondition(): lax.dot_general(grad_part, act_part, (((0,), (0,)), ((), ())), preferred_...]
    pallas_call x0 -> x2, Pallas kernels: none -> 40.9 us  [the longest x1 36.2 us: images(): pl.pallas_call(functools.partial(image_kernel, batch_count), grid=(hidden...]
    psum x1 -> x0, blocking collectives: 31.4 us -> none  [per_device(): return lax.psum(totals, 'wide') * score_scale]
    ppermute x0 -> x9, starting transfers between devices: none -> 19.4 us  [swap(): return lax.ppermute(x, axis, [(i, i ^ bit) for i in range(count)])]
    ppermute x0 -> x9, waiting for transfers between devices: none -> 19.1 us  [swap(): return lax.ppermute(x, axis, [(i, i ^ bit) for i in range(count)])]
    all_gather x1, waiting for transfers between devices: 12.3 us -> 0.01 us  [per_device(): lax.all_gather(jnp.concatenate([train_act, ids_cols], axis=1), 'wide', ax...]
    reshape x3 -> x0, local copies, waits for them, and re-layouts: 11.3 us -> none  [the longest x1 6.58 us: score_rows(): image_rows = image_rows.reshape(row_count, batch_count, grad_rows.shape[1])]
  transfers between devices with their start and end apart: 3 -> 11, of which waited for: 2 -> 7; matrix products, arithmetic and copies ran while one was open for 16% -> 6% of each run, Pallas kernels for 0% -> 23%
where the time goes in v1:
time: 159 us
  Pallas kernels  40.9 us (26%)
  blocking collectives  39.9 us (25%)
  starting transfers between devices  24.1 us (15%)
  waiting for transfers between devices  19.2 us (12%)
  between operations  16.3 us (10%)
  local copies, waits for them, and re-layouts  11.4 us (7%)
  other arithmetic  6.9 us (4%)
    all_gather x1, blocking collectives, per_device(): lax.all_gather(both[:, :, cols:].reshape(batch_count * QT, act_piece), 'w...  39.9 us
    pallas_call x1, Pallas kernels, images(): pl.pallas_call(functools.partial(image_kernel, batch_count), grid=(hidden...  36.2 us
    ppermute x9, starting transfers between devices, swap(): return lax.ppermute(x, axis, [(i, i ^ bit) for i in range(count)])  19.4 us
    ppermute x9, waiting for transfers between devices, swap(): return lax.ppermute(x, axis, [(i, i ^ bit) for i in range(count)])  19.1 us
    all_to_all x1, starting transfers between devices, per_device(): lax.all_to_all(train_grad, 'wide', split_axis=1, concat_axis=0, tiled=True)  4.76 us
    pallas_call x1, Pallas kernels, score_parts(): pl.pallas_call(functools.partial(score_kernel, batch_count, seq_count), o...  4.72 us
    unnamed x14, local copies, waits for them, and re-layouts  4.06 us
  transfers between devices with their start and end apart: 11, of which 7 were waited for; matrix products, arithmetic and copies ran while one was open for 6% of the time, Pallas kernels for 23%

profile of v1, /device:TPU:0, one launch (start us, length us, event | category | flops | bytes accessed | tf_op | source)
XLA Modules:
  0.0 158.6 jit_solution(10113907636407810750)
XLA Ops:
  6.5 1.7 %copy-done = bf16[2,16,36864]{2,1,0:T(8,128)(2,1)S(1)} copy-done((bf16[2,16,36864]{2,1,0:T(8,128)(2,1)S(1)}, bf16[2,16,36864]{2,1,0:T(8,128)(2,1)}, u32[]{:S(2)}) %copy-start) | copy-done | bytes 2359320
  13.4 1.2 bitcast_select_fusion
  15.4 2.6 %collective-permute-start.1 = (bf16[4,16,2304]{2,1,0:T(8,128)(2,1)S(1)}, bf16[4,16,2304]{2,1,0:T(8,128)(2,1)S(1)}, u32[]{:S(2)}, u32[]{:S(2)}) collective-permute-start(bf16[4,16,2304]{2,1,0:T(8,128)(2,1)S(1)} %select_bitcast_fusion.1), channel_id=1, source_target_pairs={{0,2},{1,3},{2,0},{3,1},{4,6},{5,7},{6,4},{7,5},{8,10},{9,11},{10,... | collective-permute-start | bytes 884744 | tf_op jit(solution)/shard_map/ppermute | solution.py:116
  19.5 5.1 %collective-permute-done.1 = bf16[4,16,2304]{2,1,0:T(8,128)(2,1)S(1)} collective-permute-done((bf16[4,16,2304]{2,1,0:T(8,128)(2,1)S(1)}, bf16[4,16,2304]{2,1,0:T(8,128)(2,1)S(1)}, u32[]{:S(2)}, u32[]{:S(2)}) %collective-permute-start.1) | collective-permute-done | bytes 294944 | tf_op jit(solution)/shard_map/ppermute | solution.py:116
  24.6 1.1 bitcast_select_fusion.1
  25.7 1.9 %collective-permute-start.2 = (bf16[2,16,2304]{2,1,0:T(8,128)(2,1)S(1)}, bf16[2,16,2304]{2,1,0:T(8,128)(2,1)S(1)}, u32[]{:S(2)}, u32[]{:S(2)}) collective-permute-start(bf16[2,16,2304]{2,1,0:T(8,128)(2,1)S(1)} %fusion), channel_id=1, source_target_pairs={{0,4},{1,5},{2,6},{3,7},{4,0},{5,1},{6,2},{7,3},{8,12},{9,13},{10,... | collective-permute-start | bytes 442376 | tf_op jit(solution)/shard_map/ppermute | solution.py:116
  27.6 4.8 %collective-permute-done.2 = bf16[2,16,2304]{2,1,0:T(8,128)(2,1)S(1)} collective-permute-done((bf16[2,16,2304]{2,1,0:T(8,128)(2,1)S(1)}, bf16[2,16,2304]{2,1,0:T(8,128)(2,1)S(1)}, u32[]{:S(2)}, u32[]{:S(2)}) %collective-permute-start.2) | collective-permute-done | bytes 147488 | tf_op jit(solution)/shard_map/ppermute | solution.py:116
  32.4 4.4 %collective-permute-start.3 = (bf16[1,16,2304]{2,1,0:T(8,128)(2,1)S(1)}, bf16[1,16,2304]{2,1,0:T(8,128)(2,1)S(1)}, u32[]{:S(2)}, u32[]{:S(2)}) collective-permute-start(bf16[1,16,2304]{2,1,0:T(8,128)(2,1)S(1)} %select_bitcast_fusion.2), channel_id=1, source_target_pairs={{0,8},{1,9},{2,10},{3,11},{4,12},{5,13},{6,14},{7,15},{8,0},{9,1},... | collective-permute-start | bytes 221192 | tf_op jit(solution)/shard_map/ppermute | solution.py:116
  36.9 3.1 %collective-permute-done.3 = bf16[1,16,2304]{2,1,0:T(8,128)(2,1)S(1)} collective-permute-done((bf16[1,16,2304]{2,1,0:T(8,128)(2,1)S(1)}, bf16[1,16,2304]{2,1,0:T(8,128)(2,1)S(1)}, u32[]{:S(2)}, u32[]{:S(2)}) %collective-permute-start.3) | collective-permute-done | bytes 73760 | tf_op jit(solution)/shard_map/ppermute | solution.py:116
  40.0 1.9 %collective-permute-start.4 = (bf16[16,2304]{1,0:T(8,128)(2,1)S(1)}, bf16[16,2304]{1,0:T(8,128)(2,1)S(1)}, u32[]{:S(2)}, u32[]{:S(2)}) collective-permute-start(bf16[16,2304]{1,0:T(8,128)(2,1)S(1)} %bitcast.77), channel_id=1, source_target_pairs={{0,16},{16,0},{1,17},{17,1},{2,18},{18,2},{3,19},{19,3},{4,20},{20... | collective-permute-start | bytes 221192 | tf_op jit(solution)/shard_map/ppermute | solution.py:116
  41.9 2.3 %copy.32 = bf16[2,16,8,2048]{3,2,0,1:T(8,128)(2,1)} copy(bf16[2,16,8,2048]{3,2,1,0:T(8,128)(2,1)} %bitcast.74) | data formatting | bytes 2097152 | tf_op jit(solution)/shard_map/all_to_all | solution.py:132
  44.2 4.8 %all-to-all-start = ((bf16[16,16,2048]{2,0,1:T(8,128)(2,1)}), bf16[16,16,2048]{2,0,1:T(8,128)(2,1)S(1)}, u32[]{:S(2)}, u32[]{:S(2)}) async-start(bf16[16,16,2048]{2,0,1:T(8,128)(2,1)} %bitcast.69), calls=%async_computation | async-start | bytes 2097152 | tf_op jit(solution)/shard_map/all_to_all | solution.py:132
  49.7 39.9 %all_gather.7.right_ref = bf16[32,4096]{1,0:T(8,128)(2,1)} all-gather(bf16[32,256]{1,0:T(8,128)(2,1)S(1)} %bitcast.80), channel_id=1, replica_groups=mesh['groups'=2,'wide'=16] {'wide'}, dimensions={1}, use_global_device_ids=true | all-gather | bytes 278528 | tf_op jit(solution)/shard_map/all_gather | solution.py:163
  89.6 3.1 %slice.64.act_ref = bf16[256,4096]{1,0:T(8,128)(2,1)} slice(bf16[256,4224]{1,0:T(8,128)(2,1)} %all-gather.2.cloned.1.call-done), slice={[0:256], [0:4096]} | slice | bytes 4194304 | tf_op jit(solution)/shard_map/slice | solution.py:136
  92.7 1.5 convert_reduce_fusion
  94.2 36.2 %shard_map.82.image_ref = f32[2,2048,256]{2,1,0:T(8,128)} custom-call(bf16[256,4096]{1,0:T(8,128)(2,1)} %slice.64.act_ref, bf16[512,4096]{1,0:T(8,128)(2,1)} %basis_ref.2, bf16[32,2048]{1,0:T(8,128)(2,1)} %bitcast.78, bf16[32,4096]{1,0:T(8,128)(2,1)} %all_gather.7.right_ref, bf16[2048,4096]{1,0:T(8,128)(2,1)} %eig_ref.1), custom_call_target="tpu_custom_call" | custom-call | flops 17179869184 | bytes 16777216 | tf_op jit(solution)/shard_map/pallas_call | solution.py:57
  130.4 1.0 copy-done.2
  131.4 4.7 %shard_map.83 = f32[2,8,1]{2,1,0:T(8,128)} custom-call(bf16[256,2048]{1,0:T(8,128)(2,1)} %bitcast.68, bf16[512,2048]{1,0:T(8,128)(2,1)} %basis_ref.3, f32[2,2048,256]{2,1,0:T(8,128)} %shard_map.82.image_ref, s32[1,256]{1,0:T(1,128)} %bitcast.81), custom_call_target="tpu_custom_call" | custom-call | flops 536870912 | bytes 4194304 | tf_op jit(solution)/shard_map/pallas_call | solution.py:102
  138.1 1.4 collective-permute-start.6
  139.4 2.2 %collective-permute-done.6 = f32[8,2]{0,1:T(2,128)S(1)} collective-permute-done((f32[8,2]{0,1:T(2,128)S(1)}, f32[8,2]{0,1:T(2,128)S(1)}, u32[]{:S(2)}, u32[]{:S(2)}) %collective-permute-start.6) | collective-permute-done | bytes 96 | tf_op jit(solution)/shard_map/ppermute | solution.py:116
  141.7 3.5 %collective-permute-start.7 = (f32[8,2]{0,1:T(2,128)S(1)}, f32[8,2]{0,1:T(2,128)S(1)}, u32[]{:S(2)}, u32[]{:S(2)}) collective-permute-start(f32[8,2]{0,1:T(2,128)S(1)} %add.63), channel_id=1, source_target_pairs={{0,4},{1,5},{2,6},{3,7},{4,0},{5,1},{6,2},{7,3},{8,12},{9,13},{10,... | collective-permute-start | bytes 200 | tf_op jit(solution)/shard_map/ppermute | solution.py:116
  145.1 1.5 collective-permute-done.7
  146.7 2.9 %collective-permute-start.8 = (f32[8,2]{0,1:T(2,128)S(1)}, f32[8,2]{0,1:T(2,128)S(1)}, u32[]{:S(2)}, u32[]{:S(2)}) collective-permute-start(f32[8,2]{0,1:T(2,128)S(1)} %add.64), channel_id=1, source_target_pairs={{0,8},{1,9},{2,10},{3,11},{4,12},{5,13},{6,14},{7,15},{8,0},{9,1},... | collective-permute-start | bytes 200 | tf_op jit(solution)/shard_map/ppermute | solution.py:116
  149.6 1.5 collective-permute-done.8
  (44 shorter events, 8.0 us)
Async XLA Ops:
  6.5 1.7 %copy-start = (bf16[2,16,36864]{2,1,0:T(8,128)(2,1)S(1)}, bf16[2,16,36864]{2,1,0:T(8,128)(2,1)}, u32[]{:S(2)}) copy-start(bf16[2,16,36864]{2,1,0:T(8,128)(2,1)} %param.14) | copy-start | bytes 7077892
  6.5 83.0 %all-gather.2.cloned.1.call-start = ((), (), s32[]{:S(2)}) async-start(), calls=%async_computation.1 | async-start | bytes 2297856 | tf_op jit(solution)/shard_map/all_gather | solution.py:135
  9.1 1.7 %copy-start.4 = (s32[2]{0:T(128)S(1)}, s32[2]{0:T(128)}, u32[]{:S(2)}) copy-start(s32[2]{0:T(128)} %param.15) | copy-start | bytes 28
  9.1 4.3 %copy-start.5 = (s32[16]{0:T(128)S(1)}, s32[16]{0:T(128)}, u32[]{:S(2)}) copy-start(s32[16]{0:T(128)} %param.10) | copy-start | bytes 196
  10.4 3.0 %collective-permute-start = (bf16[8,16,2304]{2,1,0:T(8,128)(2,1)}, bf16[8,16,2304]{2,1,0:T(8,128)(2,1)}, u32[]{:S(2)}, u32[]{:S(2)}) collective-permute-start(bf16[8,16,2304]{2,1,0:T(8,128)(2,1)} %select_bitcast_fusion), channel_id=1, source_target_pairs={{0,1},{1,0},{2,3},{3,2},{4,5},{5,4},{6,7},{7,6},{8,9},{9,8},{10,11... | collective-permute-start | bytes 1769480 | tf_op jit(solution)/shard_map/ppermute | solution.py:116
  13.4 4.7 %copy-start.3 = (bf16[16,4096]{1,0:T(8,128)(2,1)S(1)}, bf16[16,4096]{1,0:T(8,128)(2,1)}, u32[]{:S(2)}) copy-start(bf16[16,4096]{1,0:T(8,128)(2,1)} %param.8) | copy-start | bytes 393220
  14.6 0.8 copy-start.1
  15.4 9.2 %collective-permute-start.1 = (bf16[4,16,2304]{2,1,0:T(8,128)(2,1)S(1)}, bf16[4,16,2304]{2,1,0:T(8,128)(2,1)S(1)}, u32[]{:S(2)}, u32[]{:S(2)}) collective-permute-start(bf16[4,16,2304]{2,1,0:T(8,128)(2,1)S(1)} %select_bitcast_fusion.1), channel_id=1, source_target_pairs={{0,2},{1,3},{2,0},{3,1},{4,6},{5,7},{6,4},{7,5},{8,10},{9,11},{10,... | collective-permute-start | bytes 884744 | tf_op jit(solution)/shard_map/ppermute | solution.py:116
  25.7 6.7 %collective-permute-start.2 = (bf16[2,16,2304]{2,1,0:T(8,128)(2,1)S(1)}, bf16[2,16,2304]{2,1,0:T(8,128)(2,1)S(1)}, u32[]{:S(2)}, u32[]{:S(2)}) collective-permute-start(bf16[2,16,2304]{2,1,0:T(8,128)(2,1)S(1)} %fusion), channel_id=1, source_target_pairs={{0,4},{1,5},{2,6},{3,7},{4,0},{5,1},{6,2},{7,3},{8,12},{9,13},{10,... | collective-permute-start | bytes 442376 | tf_op jit(solution)/shard_map/ppermute | solution.py:116
  32.4 7.5 %collective-permute-start.3 = (bf16[1,16,2304]{2,1,0:T(8,128)(2,1)S(1)}, bf16[1,16,2304]{2,1,0:T(8,128)(2,1)S(1)}, u32[]{:S(2)}, u32[]{:S(2)}) collective-permute-start(bf16[1,16,2304]{2,1,0:T(8,128)(2,1)S(1)} %select_bitcast_fusion.2), channel_id=1, source_target_pairs={{0,8},{1,9},{2,10},{3,11},{4,12},{5,13},{6,14},{7,15},{8,0},{9,1},... | collective-permute-start | bytes 221192 | tf_op jit(solution)/shard_map/ppermute | solution.py:116
  40.0 9.0 %collective-permute-start.4 = (bf16[16,2304]{1,0:T(8,128)(2,1)S(1)}, bf16[16,2304]{1,0:T(8,128)(2,1)S(1)}, u32[]{:S(2)}, u32[]{:S(2)}) collective-permute-start(bf16[16,2304]{1,0:T(8,128)(2,1)S(1)} %bitcast.77), channel_id=1, source_target_pairs={{0,16},{16,0},{1,17},{17,1},{2,18},{18,2},{3,19},{19,3},{4,20},{20... | collective-permute-start | bytes 221192 | tf_op jit(solution)/shard_map/ppermute | solution.py:116
  44.2 86.2 %all-to-all-start = ((bf16[16,16,2048]{2,0,1:T(8,128)(2,1)}), bf16[16,16,2048]{2,0,1:T(8,128)(2,1)S(1)}, u32[]{:S(2)}, u32[]{:S(2)}) async-start(bf16[16,16,2048]{2,0,1:T(8,128)(2,1)} %bitcast.69), calls=%async_computation | async-start | bytes 2097152 | tf_op jit(solution)/shard_map/all_to_all | solution.py:132
  130.4 1.0 copy-start.2
  136.9 1.2 collective-permute-start.5
  138.1 3.6 %collective-permute-start.6 = (f32[8,2]{0,1:T(2,128)S(1)}, f32[8,2]{0,1:T(2,128)S(1)}, u32[]{:S(2)}, u32[]{:S(2)}) collective-permute-start(f32[8,2]{0,1:T(2,128)S(1)} %bitcast_add_fusion), channel_id=1, source_target_pairs={{0,2},{1,3},{2,0},{3,1},{4,6},{5,7},{6,4},{7,5},{8,10},{9,11},{10,... | collective-permute-start | bytes 200 | tf_op jit(solution)/shard_map/ppermute | solution.py:116
  141.7 5.0 %collective-permute-start.7 = (f32[8,2]{0,1:T(2,128)S(1)}, f32[8,2]{0,1:T(2,128)S(1)}, u32[]{:S(2)}, u32[]{:S(2)}) collective-permute-start(f32[8,2]{0,1:T(2,128)S(1)} %add.63), channel_id=1, source_target_pairs={{0,4},{1,5},{2,6},{3,7},{4,0},{5,1},{6,2},{7,3},{8,12},{9,13},{10,... | collective-permute-start | bytes 200 | tf_op jit(solution)/shard_map/ppermute | solution.py:116
  146.7 4.5 %collective-permute-start.8 = (f32[8,2]{0,1:T(2,128)S(1)}, f32[8,2]{0,1:T(2,128)S(1)}, u32[]{:S(2)}, u32[]{:S(2)}) collective-permute-start(f32[8,2]{0,1:T(2,128)S(1)} %add.64), channel_id=1, source_target_pairs={{0,8},{1,9},{2,10},{3,11},{4,12},{5,13},{6,14},{7,15},{8,0},{9,1},... | collective-permute-start | bytes 200 | tf_op jit(solution)/shard_map/ppermute | solution.py:116
Sparse Core Ops, SparseCore 0:
  18.9 49.0 all-gather.1

commit v2 on v0

v2 whole, which is shorter than its diff:
```python
import functools
import math

import jax
import jax.numpy as jnp
from jax import lax
from jax.experimental import pallas as pl
from jax.experimental.pallas import tpu as pltpu
from jax.sharding import PartitionSpec as P

D = 4096
FF = 32768
SEQ_MEAN = 32
QT = 16
LANES = 128


damping = 0.1


def params(mib):
    return pltpu.CompilerParams(vmem_limit_bytes=mib * 1024 * 1024)


def whole_block(shape):
    return pl.BlockSpec(shape, lambda *_: (0,) * len(shape), pipeline_mode=pl.Buffered(1))


def swap(x, axis, bit):
    count = lax.axis_size(axis)
    return lax.ppermute(x, axis, [(i, i ^ bit) for i in range(count)])


def cut_grads_kernel(me_ref, grad_ref, *out_refs):
    cols = out_refs[0].shape[1]
    for r, out_ref in enumerate(out_refs):
        at = pl.multiple_of((me_ref[0] ^ r) * cols, cols)
        out_ref[...] = grad_ref[:, pl.ds(at, cols)]


def cut_grads(me, grads, count):
    rows, hidden = grads.shape
    piece = jax.ShapeDtypeStruct((rows, hidden // count), grads.dtype)
    return pl.pallas_call(
        cut_grads_kernel,
        in_specs=[pl.BlockSpec(memory_space=pltpu.SMEM), pl.BlockSpec(memory_space=pltpu.VMEM)],
        out_specs=[pl.BlockSpec(memory_space=pltpu.VMEM)] * count,
        out_shape=[piece] * count,
        compiler_params=params(16),
        cost_estimate=pl.CostEstimate(flops=0, bytes_accessed=4 * grads.size, transcendentals=0),
    )(me, grads)


def cut_factors_kernel(order, hidden, me_ref, fac_ref, keep_ref, give_ref):
    cols = hidden // len(order)
    half = (fac_ref.shape[2] - hidden) // 2
    batch = me_ref[1]
    mine = me_ref[0]
    for part, out_ref in enumerate((keep_ref, give_ref)):
        picked = order[part * len(order) // 2:(part + 1) * len(order) // 2]
        for place, r in enumerate(picked):
            at = pl.multiple_of((mine ^ r) * cols, cols)
            out_ref[:, place * cols:(place + 1) * cols] = fac_ref[batch, :, pl.ds(at, cols)]
        at = pl.multiple_of(hidden + ((mine & 1) ^ part) * half, LANES)
        out_ref[:, len(picked) * cols:] = fac_ref[batch, :, pl.ds(at, half)]


def cut_factors(me_batch, factors, order, hidden):
    rows, width = factors.shape[1:]
    half = jax.ShapeDtypeStruct((rows, width // 2), factors.dtype)
    return pl.pallas_call(
        functools.partial(cut_factors_kernel, order, hidden),
        in_specs=[pl.BlockSpec(memory_space=pltpu.SMEM), pl.BlockSpec(memory_space=pltpu.VMEM)],
        out_specs=[pl.BlockSpec(memory_space=pltpu.VMEM)] * 2,
        out_shape=[half] * 2,
        compiler_params=params(16),
        cost_estimate=pl.CostEstimate(flops=0, bytes_accessed=4 * factors.size, transcendentals=0),
    )(me_batch, factors)


def image_kernel(count, batch_count, me_ref, *refs):
    act_refs = refs[:count]
    basis_ref = refs[count]
    left_refs = refs[count + 1:count + 1 + batch_count]
    half_refs = refs[count + 1 + batch_count:count + 1 + 3 * batch_count]
    eig_ref, out_ref, ids_ref = refs[count + 1 + 3 * batch_count:count + 4 + 3 * batch_count]
    rot_ref, right_ref, turn_ref, pre_a, pre_b = refs[count + 4 + 3 * batch_count:]
    rows = eig_ref.shape[0]
    depth, width = basis_ref.shape
    half = pre_a.shape[0] // batch_count
    chunk = pre_a.shape[1]
    per = width // chunk
    phases = (rows // half) * per
    tile = min(256, chunk)

    @pl.when(pl.program_id(0) == 0)
    def _():
        for k in range(width // depth):
            cols = slice(k * depth, (k + 1) * depth)
            act = jnp.concatenate([ref[:, cols] for ref in act_refs], axis=0)
            turned = jnp.dot(act, basis_ref[:, cols], preferred_element_type=jnp.float32)
            rot_ref[cols, :] = turned.astype(jnp.bfloat16).T
        ids = jnp.concatenate([ref[:, width:] for ref in act_refs], axis=0)
        ids_ref[...] = ids.astype(jnp.float32).T[:ids_ref.shape[0], :]
        side = width // 2
        for b in range(batch_count):
            for other in range(2):
                at = pl.multiple_of(((me_ref[0] & 1) ^ other) * side, side)
                right_ref[b, :, pl.ds(at, side)] = half_refs[2 * b + other][...]

    for b in range(batch_count):
        turn_ref[b] = left_refs[b][...].T
    out_ref[...] = jnp.zeros_like(out_ref)

    def place(k):
        return pl.multiple_of((k // per) * half, half), (k % per) * chunk

    def produce(k, s, pre):
        row, col = place(k)
        cols = pl.ds(pl.multiple_of(col + s * tile, tile), tile)
        damped = eig_ref[pl.ds(row, half), cols].astype(jnp.float32) + damping
        guess = pl.reciprocal(damped, approx=True)
        inverse = guess * (2.0 - damped * guess)
        for b in range(batch_count):
            outer_sum = jnp.dot(
                turn_ref[b, pl.ds(row, half), :], right_ref[b, :, cols],
                preferred_element_type=jnp.float32,
            )
            pre[b * half:(b + 1) * half, s * tile:(s + 1) * tile] = (
                outer_sum * inverse
            ).astype(jnp.bfloat16)

    def absorb(k, b, pre):
        row, col = place(k)
        rot = rot_ref[pl.ds(pl.multiple_of(col, chunk), chunk), :]
        out_ref[b, pl.ds(row, half), :] += jnp.dot(
            pre[b * half:(b + 1) * half, :], rot, preferred_element_type=jnp.float32
        )

    def both(k, pre_now, pre_next):
        subs = chunk // tile
        for b in range(batch_count):
            for s in range(b * subs // batch_count, (b + 1) * subs // batch_count):
                produce(k + 1, s, pre_next)
            absorb(k, b, pre_now)

    for s in range(chunk // tile):
        produce(0, s, pre_a)

    def pair(q, carry):
        both(2 * q, pre_a, pre_b)
        both(2 * q + 1, pre_b, pre_a)
        return carry

    lax.fori_loop(0, phases // 2 - 1, pair, 0)
    both(phases - 2, pre_a, pre_b)
    for b in range(batch_count):
        absorb(phases - 1, b, pre_b)


def images(me, act_pieces, act_basis, lefts, halves, eigenvalues):
    count, batch_count = len(act_pieces), len(lefts)
    tokens = count * act_pieces[0].shape[0]
    hidden, width = eigenvalues.shape
    rows = min(512, hidden)
    half = min(256, rows)
    chunk = min(1024, width // 2)
    return pl.pallas_call(
        functools.partial(image_kernel, count, batch_count),
        grid=(hidden // rows,),
        in_specs=[pl.BlockSpec(memory_space=pltpu.SMEM)]
        + [whole_block(x.shape) for x in act_pieces]
        + [whole_block(act_basis.shape)]
        + [pl.BlockSpec((QT, rows), lambda i: (0, i)) for x in lefts]
        + [whole_block(x.shape) for x in halves]
        + [pl.BlockSpec((rows, width), lambda i: (i, 0))],
        out_specs=[
            pl.BlockSpec((batch_count, rows, tokens), lambda i: (0, i, 0)),
            pl.BlockSpec((8, tokens), lambda i: (0, 0)),
        ],
        out_shape=[
            jax.ShapeDtypeStruct((batch_count, hidden, tokens), jnp.float32),
            jax.ShapeDtypeStruct((8, tokens), jnp.float32),
        ],
        scratch_shapes=[
            pltpu.VMEM((width, tokens), jnp.bfloat16),
            pltpu.VMEM((batch_count, QT, width), jnp.bfloat16),
            pltpu.VMEM((batch_count, rows, QT), jnp.bfloat16),
            pltpu.VMEM((batch_count * half, chunk), jnp.bfloat16),
            pltpu.VMEM((batch_count * half, chunk), jnp.bfloat16),
        ],
        compiler_params=params(32 if tokens <= 256 else 56),
        cost_estimate=pl.CostEstimate(
            flops=2 * hidden * width * (tokens + 256) * batch_count,
            bytes_accessed=2 * hidden * width,
            transcendentals=0,
        ),
    )(me, *act_pieces, act_basis, *lefts, *halves, eigenvalues)


def score_kernel(count, batch_count, seq_count, *refs):
    grad_refs = refs[:count]
    basis_ref, image_ref, ids_ref, out_ref, token_ref = refs[count:]
    step = pl.program_id(0)

    @pl.when(step == 0)
    def _():
        token_ref[...] = jnp.zeros_like(token_ref)

    grads = jnp.concatenate([ref[...] for ref in grad_refs], axis=0)
    turned = jnp.dot(grads, basis_ref[...], preferred_element_type=jnp.float32)
    turned = turned.astype(jnp.bfloat16).T.astype(jnp.float32)
    for b in range(batch_count):
        token_ref[b:b + 1, :] += jnp.sum(image_ref[b] * turned, axis=0, keepdims=True)

    @pl.when(step == pl.num_programs(0) - 1)
    def _():
        tokens = token_ref.shape[1]
        seqs = lax.broadcasted_iota(jnp.int32, (seq_count, tokens), 0).astype(jnp.float32)
        member = ids_ref[0:1, :] == seqs
        for b in range(batch_count):
            out_ref[b] = jnp.sum(jnp.where(member, token_ref[b:b + 1, :], 0.0), axis=1, keepdims=True)


def score_parts(grad_pieces, grad_basis, image, ids, seq_count):
    count, batch_count = len(grad_pieces), image.shape[0]
    rows, hidden = grad_pieces[0].shape
    inner = min(grad_basis.shape[0], hidden)
    tokens = count * rows
    return pl.pallas_call(
        functools.partial(score_kernel, count, batch_count, seq_count),
        grid=(hidden // inner,),
        in_specs=[pl.BlockSpec((rows, inner), lambda i: (0, i)) for _ in grad_pieces]
        + [
            pl.BlockSpec((grad_basis.shape[0], inner), lambda i: (0, i)),
            pl.BlockSpec((batch_count, inner, tokens), lambda i: (0, i, 0)),
            pl.BlockSpec(ids.shape, lambda i: (0, 0)),
        ],
        out_specs=pl.BlockSpec((batch_count, seq_count, 1), lambda i: (0, 0, 0)),
        out_shape=jax.ShapeDtypeStruct((batch_count, seq_count, 1), jnp.float32),
        scratch_shapes=[pltpu.VMEM((8, tokens), jnp.float32)],
        compiler_params=params(16 if tokens <= 256 else 40),
        cost_estimate=pl.CostEstimate(
            flops=2 * tokens * hidden * grad_basis.shape[0],
            bytes_accessed=4 * image.size,
            transcendentals=0,
        ),
    )(*grad_pieces, grad_basis, image, ids)


def per_device(
    train_act, train_grad, seq_ids, act_basis, grad_basis, eigenvalues, query_factors, owners
):
    wide_count = lax.axis_size("wide")
    bits = [1 << n for n in range(wide_count.bit_length() - 1)]
    me = lax.axis_index("wide")
    tok_local = train_act.shape[0]
    seq_count = tok_local * wide_count // SEQ_MEAN
    cols = grad_basis.shape[1]
    hidden = train_grad.shape[1]
    batch_count = owners.shape[0]
    score_scale = 1.0 / math.sqrt(FF * D * QT * SEQ_MEAN)
    batch = lax.axis_index("groups") % batch_count
    place = jnp.stack([me, batch]).astype(jnp.int32)

    order = [0]
    for bit in reversed(bits):
        order = order + [r + bit for r in order]
    order = sorted(order, key=lambda r: [r & bit for bit in bits])
    keep, give = cut_factors(place, query_factors, order, hidden)
    owner = owners[batch]
    got = swap(give, "wide", 1)
    held = jnp.where((owner & 1) == (me & 1), keep, got)
    count = wide_count // 2
    for bit in bits[1:]:
        count //= 2
        got = swap(held[:, count * cols:], "wide", bit)
        keep = jnp.concatenate([held[:, :count * cols], held[:, 2 * count * cols:]], axis=1)
        held = jnp.where((owner & bit) == (me & bit), keep, got)
    other = swap(held, "groups", 1)
    lefts = [held[:, :cols], other[:, :cols]]
    halves = []
    for x in (held, other):
        halves += [x[:, cols:], swap(x[:, cols:], "wide", 1)]

    ids_cols = jnp.broadcast_to(seq_ids[:, None].astype(jnp.bfloat16), (tok_local, LANES))
    acts = {0: jnp.concatenate([train_act, ids_cols], axis=1)}
    for bit in reversed(bits):
        acts.update({r + bit: swap(x, "wide", bit) for r, x in acts.items()})
    act_pieces = [acts[r] for r in range(wide_count)]

    sent = cut_grads(place, train_grad, wide_count)
    grad_pieces = [sent[0]] + [swap(sent[r], "wide", r) for r in range(1, wide_count)]

    image, ids = images(place, act_pieces, act_basis, lefts, halves, eigenvalues)
    parts = score_parts(grad_pieces, grad_basis, image, ids, seq_count)[:, :, 0]
    for bit in bits:
        parts = parts + swap(parts, "wide", bit)
    mine, others = parts[0], parts[1]
    first = jnp.where(batch == 0, mine, others)
    second = jnp.where(batch == 0, others, mine)
    return jnp.stack([first, second], axis=1) * score_scale


def solution(mesh):
    return jax.shard_map(
        per_device,
        mesh=mesh,
        in_specs=(
            P(("groups", "wide"), None),
            P(("groups", "wide"), None),
            P(("groups", "wide")),
            P(),
            P(None, "wide"),
            P("wide", None),
            P("wide", None, None),
            P(),
        ),
        out_specs=P("groups", None),
        check_vma=False,
    )
```

time: 241 us -> 108 us (0.45)
  blocking collectives: 67.2 us -> 0 us
  waiting for transfers between devices: 79.7 us -> 21 us
  matrix products: 45.9 us -> 0 us
  starting transfers between devices: 7.43 us -> 48 us
  Pallas kernels: 0 us -> 29.9 us
  local copies, waits for them, and re-layouts: 17.4 us -> 5.35 us
  between operations: 14.7 us -> 2.82 us
  other arithmetic: 7.98 us -> 1.02 us
    psum x1 -> x0, waiting for transfers between devices: 67.3 us -> none  [spread(): return lax.psum(jnp.where(mine, x, jnp.zeros_like(x)), axis)]
    ppermute x0 -> x41, starting transfers between devices: none -> 48 us  [swap(): return lax.ppermute(x, axis, [(i, i ^ bit) for i in range(count)])]
    dot_general x6 -> x0, matrix products: 45.9 us -> none  [the longest x2 23.9 us: precondition(): lax.dot_general(grad_part, act_part, (((0,), (0,)), ((), ())), preferred_...]
    all_gather x1 -> x0, blocking collectives: 35.8 us -> none  [per_device(): member_rows = lax.all_gather(member, 'wide', axis=0, tiled=True)]
    psum x1 -> x0, blocking collectives: 31.4 us -> none  [per_device(): return lax.psum(totals, 'wide') * score_scale]
    pallas_call x0 -> x4, Pallas kernels: none -> 29.9 us  [the longest x1 26 us: images(): pl.pallas_call(functools.partial(image_kernel, count, batch_count), grid=...]
    ppermute x0 -> x41, waiting for transfers between devices: none -> 21 us  [swap(): return lax.ppermute(x, axis, [(i, i ^ bit) for i in range(count)])]
    all_gather x1 -> x0, waiting for transfers between devices: 12.3 us -> none  [per_device(): act_rows = lax.all_gather(rot_act, 'wide', axis=0, tiled=True)]
  transfers between devices with their start and end apart: 3 -> 41, of which waited for: 2 -> 11; matrix products, arithmetic and copies ran while one was open for 16% -> 2% of each run, Pallas kernels for 0% -> 25%
where the time goes in v2:
time: 108 us
  starting transfers between devices  48 us (44%)
  Pallas kernels  29.9 us (28%)
  waiting for transfers between devices  21 us (19%)
  local copies, waits for them, and re-layouts  5.35 us (5%)
  between operations  2.82 us (3%)
    ppermute x41, starting transfers between devices, swap(): return lax.ppermute(x, axis, [(i, i ^ bit) for i in range(count)])  48 us
    pallas_call x1, Pallas kernels, images(): pl.pallas_call(functools.partial(image_kernel, count, batch_count), grid=...  26 us
    ppermute x41, waiting for transfers between devices, swap(): return lax.ppermute(x, axis, [(i, i ^ bit) for i in range(count)])  21 us
    unnamed x12, local copies, waits for them, and re-layouts  3.87 us
    pallas_call x1, Pallas kernels, score_parts(): pl.pallas_call(functools.partial(score_kernel, count, batch_count, seq_co...  2.66 us
  transfers between devices with their start and end apart: 41, of which 11 were waited for; matrix products, arithmetic and copies ran while one was open for 2% of the time, Pallas kernels for 25%

profile of v2, /device:TPU:0, one launch (start us, length us, event | category | flops | bytes accessed | tf_op | source)
XLA Modules:
  0.0 108.2 jit_solution(11450636924668358822)
XLA Ops:
  0.1 1.7 %copy-done = bf16[2,16,36864]{2,1,0:T(8,128)(2,1)S(1)} copy-done((bf16[2,16,36864]{2,1,0:T(8,128)(2,1)S(1)}, bf16[2,16,36864]{2,1,0:T(8,128)(2,1)}, u32[]{:S(2)}) %copy-start) | copy-done | bytes 2359320
  4.9 2.6 %collective-permute-start.31 = (bf16[16,10240]{1,0:T(8,128)(2,1)S(1)}, bf16[16,10240]{1,0:T(8,128)(2,1)S(1)}, u32[]{:S(2)}, u32[]{:S(2)}) collective-permute-start(bf16[16,10240]{1,0:T(8,128)(2,1)S(1)} %slice.64), channel_id=1, source_target_pairs={{0,2},{1,3},{2,0},{3,1},{4,6},{5,7},{6,4},{7,5},{8,10},{9,11},{10,... | collective-permute-start | bytes 983048 | tf_op jit(solution)/shard_map/ppermute | solution.py:31
  8.8 3.4 %collective-permute-start.10 = (bf16[16,2048]{1,0:T(8,128)(2,1)S(1)}, bf16[16,2048]{1,0:T(8,128)(2,1)S(1)}, u32[]{:S(2)}, u32[]{:S(2)}) collective-permute-start(bf16[16,2048]{1,0:T(8,128)(2,1)S(1)} %get-tuple-element.36), channel_id=1, source_target_pairs={{0,11},{1,10},{2,9},{3,8},{4,15},{5,14},{6,13},{7,12},{8,3},{9,2},... | collective-permute-start | bytes 196616 | tf_op jit(solution)/shard_map/ppermute | solution.py:31
  14.2 3.3 %collective-permute-done.31 = bf16[16,10240]{1,0:T(8,128)(2,1)S(1)} collective-permute-done((bf16[16,10240]{1,0:T(8,128)(2,1)S(1)}, bf16[16,10240]{1,0:T(8,128)(2,1)S(1)}, u32[]{:S(2)}, u32[]{:S(2)}) %collective-permute-start.31) | collective-permute-done | bytes 327712 | tf_op jit(solution)/shard_map/ppermute | solution.py:31
  17.7 2.1 %collective-permute-start.32 = (bf16[16,6144]{1,0:T(8,128)(2,1)S(1)}, bf16[16,6144]{1,0:T(8,128)(2,1)S(1)}, u32[]{:S(2)}, u32[]{:S(2)}) collective-permute-start(bf16[16,6144]{1,0:T(8,128)(2,1)S(1)} %slice.67), channel_id=1, source_target_pairs={{0,4},{1,5},{2,6},{3,7},{4,0},{5,1},{6,2},{7,3},{8,12},{9,13},{10,... | collective-permute-start | bytes 589832 | tf_op jit(solution)/shard_map/ppermute | solution.py:31
  22.2 2.5 %collective-permute-start.13 = (bf16[16,2048]{1,0:T(8,128)(2,1)S(1)}, bf16[16,2048]{1,0:T(8,128)(2,1)S(1)}, u32[]{:S(2)}, u32[]{:S(2)}) collective-permute-start(bf16[16,2048]{1,0:T(8,128)(2,1)S(1)} %get-tuple-element.39), channel_id=1, source_target_pairs={{0,14},{1,15},{2,12},{3,13},{4,10},{5,11},{6,8},{7,9},{8,6},{9,7},... | collective-permute-start | bytes 196616 | tf_op jit(solution)/shard_map/ppermute | solution.py:31
  24.7 3.1 %collective-permute-start.14 = (bf16[16,2048]{1,0:T(8,128)(2,1)S(1)}, bf16[16,2048]{1,0:T(8,128)(2,1)S(1)}, u32[]{:S(2)}, u32[]{:S(2)}) collective-permute-start(bf16[16,2048]{1,0:T(8,128)(2,1)S(1)} %get-tuple-element.40), channel_id=1, source_target_pairs={{0,15},{1,14},{2,13},{3,12},{4,11},{5,10},{6,9},{7,8},{8,7},{9,6},... | collective-permute-start | bytes 196616 | tf_op jit(solution)/shard_map/ppermute | solution.py:31
  30.2 5.6 %collective-permute-start.4 = (bf16[16,2048]{1,0:T(8,128)(2,1)S(1)}, bf16[16,2048]{1,0:T(8,128)(2,1)S(1)}, u32[]{:S(2)}, u32[]{:S(2)}) collective-permute-start(bf16[16,2048]{1,0:T(8,128)(2,1)S(1)} %get-tuple-element.30), channel_id=1, source_target_pairs={{0,5},{1,4},{2,7},{3,6},{4,1},{5,0},{6,3},{7,2},{8,13},{9,12},{10,... | collective-permute-start | bytes 196616 | tf_op jit(solution)/shard_map/ppermute | solution.py:31
  35.8 3.1 %collective-permute-start.33 = (bf16[16,4096]{1,0:T(8,128)(2,1)S(1)}, bf16[16,4096]{1,0:T(8,128)(2,1)S(1)}, u32[]{:S(2)}, u32[]{:S(2)}) collective-permute-start(bf16[16,4096]{1,0:T(8,128)(2,1)S(1)} %slice.70), channel_id=1, source_target_pairs={{0,8},{1,9},{2,10},{3,11},{4,12},{5,13},{6,14},{7,15},{8,0},{9,1},... | collective-permute-start | bytes 393224 | tf_op jit(solution)/shard_map/ppermute | solution.py:31
  39.3 2.5 %collective-permute-done.4.refs_5_ = bf16[16,2048]{1,0:T(8,128)(2,1)S(1)} collective-permute-done((bf16[16,2048]{1,0:T(8,128)(2,1)S(1)}, bf16[16,2048]{1,0:T(8,128)(2,1)S(1)}, u32[]{:S(2)}, u32[]{:S(2)}) %collective-permute-start.4) | collective-permute-done | bytes 65568 | tf_op jit(solution)/shard_map/ppermute | solution.py:31
  41.9 2.8 %collective-permute-done.33 = bf16[16,4096]{1,0:T(8,128)(2,1)S(1)} collective-permute-done((bf16[16,4096]{1,0:T(8,128)(2,1)S(1)}, bf16[16,4096]{1,0:T(8,128)(2,1)S(1)}, u32[]{:S(2)}, u32[]{:S(2)}) %collective-permute-start.33) | collective-permute-done | bytes 131104 | tf_op jit(solution)/shard_map/ppermute | solution.py:31
  51.2 1.7 %collective-permute-done.20.refs_6_ = bf16[16,4224]{1,0:T(8,128)(2,1)S(1)} collective-permute-done((bf16[16,4224]{1,0:T(8,128)(2,1)S(1)}, bf16[16,4224]{1,0:T(8,128)(2,1)S(1)}, u32[]{:S(2)}, u32[]{:S(2)}) %collective-permute-start.20) | collective-permute-done | bytes 135200 | tf_op jit(solution)/shard_map/ppermute | solution.py:31
  53.5 2.0 %collective-permute-done.28.refs_14_ = bf16[16,4224]{1,0:T(8,128)(2,1)S(1)} collective-permute-done((bf16[16,4224]{1,0:T(8,128)(2,1)S(1)}, bf16[16,4224]{1,0:T(8,128)(2,1)S(1)}, u32[]{:S(2)}, u32[]{:S(2)}) %collective-permute-start.28) | collective-permute-done | bytes 135200 | tf_op jit(solution)/shard_map/ppermute | solution.py:31
  57.3 1.6 %collective-permute-start.6 = (bf16[16,2048]{1,0:T(8,128)(2,1)S(1)}, bf16[16,2048]{1,0:T(8,128)(2,1)S(1)}, u32[]{:S(2)}, u32[]{:S(2)}) collective-permute-start(bf16[16,2048]{1,0:T(8,128)(2,1)S(1)} %get-tuple-element.32), channel_id=1, source_target_pairs={{0,7},{1,6},{2,5},{3,4},{4,3},{5,2},{6,1},{7,0},{8,15},{9,14},{10,... | collective-permute-start | bytes 196616 | tf_op jit(solution)/shard_map/ppermute | solution.py:31
  59.0 1.6 %collective-permute-start.7 = (bf16[16,2048]{1,0:T(8,128)(2,1)S(1)}, bf16[16,2048]{1,0:T(8,128)(2,1)S(1)}, u32[]{:S(2)}, u32[]{:S(2)}) collective-permute-start(bf16[16,2048]{1,0:T(8,128)(2,1)S(1)} %get-tuple-element.33), channel_id=1, source_target_pairs={{0,8},{1,9},{2,10},{3,11},{4,12},{5,13},{6,14},{7,15},{8,0},{9,1},... | collective-permute-start | bytes 196616 | tf_op jit(solution)/shard_map/ppermute | solution.py:31
  63.2 2.2 %copy-done.3 = bf16[512,4096]{1,0:T(8,128)(2,1)S(1)} copy-done((bf16[512,4096]{1,0:T(8,128)(2,1)S(1)}, bf16[512,4096]{1,0:T(8,128)(2,1)}, u32[]{:S(2)}) %copy-start.3) | copy-done | bytes 4194328
  65.4 26.0 %shard_map.84 = (f32[2,2048,256]{2,1,0:T(8,128)S(1)}, f32[8,256]{1,0:T(8,128)S(1)}) custom-call(s32[2]{0:T(128)S(1)} %pad_add_fusion.me_ref, bf16[16,4224]{1,0:T(8,128)(2,1)S(1)} %pad_maximum_fusion.refs_0_, bf16[16,4224]{1,0:T(8,128)(2,1)S(1)} %collective-permute-done.15.refs_1_, bf16[16,4224]{1,0:T(8,128)(2,1)S(1)} %collective-permute-done.16.refs_2_, ...), custom_call_target="tpu_custom_call" | custom-call | flops 17179869184 | bytes 16777216 | tf_op jit(solution)/shard_map/pallas_call | solution.py:168
  91.5 2.7 %shard_map.85 = f32[2,8,1]{2,1,0:T(8,128)S(1)} custom-call(bf16[16,2048]{1,0:T(8,128)(2,1)S(1)} %get-tuple-element.25.refs_0_, bf16[16,2048]{1,0:T(8,128)(2,1)S(1)} %collective-permute-done.refs_1_, bf16[16,2048]{1,0:T(8,128)(2,1)S(1)} %collective-permute-done.1.refs_2_, bf16[16,2048]{1,0:T(8,128)(2,1)S(1)} %collective-permute-done.2.refs_3_, ...), custom_call_target="tpu_custom_call" | custom-call | flops 536870912 | bytes 4194304 | tf_op jit(solution)/shard_map/pallas_call | solution.py:230
  95.4 1.5 %collective-permute-start.38 = (f32[2,8]{1,0:T(2,128)S(1)}, f32[2,8]{1,0:T(2,128)S(1)}, u32[]{:S(2)}, u32[]{:S(2)}) collective-permute-start(f32[2,8]{1,0:T(2,128)S(1)} %add.21), channel_id=1, source_target_pairs={{0,2},{1,3},{2,0},{3,1},{4,6},{5,7},{6,4},{7,5},{8,10},{9,11},{10,... | collective-permute-start | bytes 200 | tf_op jit(solution)/shard_map/ppermute | solution.py:31
  96.9 2.0 %collective-permute-done.38 = f32[2,8]{1,0:T(2,128)S(1)} collective-permute-done((f32[2,8]{1,0:T(2,128)S(1)}, f32[2,8]{1,0:T(2,128)S(1)}, u32[]{:S(2)}, u32[]{:S(2)}) %collective-permute-start.38) | collective-permute-done | bytes 96 | tf_op jit(solution)/shard_map/ppermute | solution.py:31
  99.0 2.6 %collective-permute-start.39 = (f32[2,8]{1,0:T(2,128)S(1)}, f32[2,8]{1,0:T(2,128)S(1)}, u32[]{:S(2)}, u32[]{:S(2)}) collective-permute-start(f32[2,8]{1,0:T(2,128)S(1)} %add.22), channel_id=1, source_target_pairs={{0,4},{1,5},{2,6},{3,7},{4,0},{5,1},{6,2},{7,3},{8,12},{9,13},{10,... | collective-permute-start | bytes 200 | tf_op jit(solution)/shard_map/ppermute | solution.py:31
  101.6 1.5 %collective-permute-done.39 = f32[2,8]{1,0:T(2,128)S(1)} collective-permute-done((f32[2,8]{1,0:T(2,128)S(1)}, f32[2,8]{1,0:T(2,128)S(1)}, u32[]{:S(2)}, u32[]{:S(2)}) %collective-permute-start.39) | collective-permute-done | bytes 96 | tf_op jit(solution)/shard_map/ppermute | solution.py:31
  103.1 2.0 %collective-permute-start.40 = (f32[2,8]{1,0:T(2,128)S(1)}, f32[2,8]{1,0:T(2,128)S(1)}, u32[]{:S(2)}, u32[]{:S(2)}) collective-permute-start(f32[2,8]{1,0:T(2,128)S(1)} %add.23), channel_id=1, source_target_pairs={{0,8},{1,9},{2,10},{3,11},{4,12},{5,13},{6,14},{7,15},{8,0},{9,1},... | collective-permute-start | bytes 200 | tf_op jit(solution)/shard_map/ppermute | solution.py:31
  105.1 2.5 %collective-permute-done.40 = f32[2,8]{1,0:T(2,128)S(1)} collective-permute-done((f32[2,8]{1,0:T(2,128)S(1)}, f32[2,8]{1,0:T(2,128)S(1)}, u32[]{:S(2)}, u32[]{:S(2)}) %collective-permute-start.40) | collective-permute-done | bytes 96 | tf_op jit(solution)/shard_map/ppermute | solution.py:31
  (100 shorter events, 22.5 us)
Async XLA Ops:
  4.9 12.6 %collective-permute-start.31 = (bf16[16,10240]{1,0:T(8,128)(2,1)S(1)}, bf16[16,10240]{1,0:T(8,128)(2,1)S(1)}, u32[]{:S(2)}, u32[]{:S(2)}) collective-permute-start(bf16[16,10240]{1,0:T(8,128)(2,1)S(1)} %slice.64), channel_id=1, source_target_pairs={{0,2},{1,3},{2,0},{3,1},{4,6},{5,7},{6,4},{7,5},{8,10},{9,11},{10,... | collective-permute-start | bytes 983048 | tf_op jit(solution)/shard_map/ppermute | solution.py:31
  8.2 12.9 %collective-permute-start = (bf16[16,2048]{1,0:T(8,128)(2,1)S(1)}, bf16[16,2048]{1,0:T(8,128)(2,1)S(1)}, u32[]{:S(2)}, u32[]{:S(2)}) collective-permute-start(bf16[16,2048]{1,0:T(8,128)(2,1)S(1)} %get-tuple-element.26), channel_id=1, source_target_pairs={{0,1},{1,0},{2,3},{3,2},{4,5},{5,4},{6,7},{7,6},{8,9},{9,8},{10,11... | collective-permute-start | bytes 196616 | tf_op jit(solution)/shard_map/ppermute | solution.py:31
  8.4 13.7 %collective-permute-start.1 = (bf16[16,2048]{1,0:T(8,128)(2,1)S(1)}, bf16[16,2048]{1,0:T(8,128)(2,1)S(1)}, u32[]{:S(2)}, u32[]{:S(2)}) collective-permute-start(bf16[16,2048]{1,0:T(8,128)(2,1)S(1)} %get-tuple-element.27), channel_id=1, source_target_pairs={{0,2},{1,3},{2,0},{3,1},{4,6},{5,7},{6,4},{7,5},{8,10},{9,11},{10,... | collective-permute-start | bytes 196616 | tf_op jit(solution)/shard_map/ppermute | solution.py:31
  8.8 19.2 %collective-permute-start.10 = (bf16[16,2048]{1,0:T(8,128)(2,1)S(1)}, bf16[16,2048]{1,0:T(8,128)(2,1)S(1)}, u32[]{:S(2)}, u32[]{:S(2)}) collective-permute-start(bf16[16,2048]{1,0:T(8,128)(2,1)S(1)} %get-tuple-element.36), channel_id=1, source_target_pairs={{0,11},{1,10},{2,9},{3,8},{4,15},{5,14},{6,13},{7,12},{8,3},{9,2},... | collective-permute-start | bytes 196616 | tf_op jit(solution)/shard_map/ppermute | solution.py:31
  12.2 15.8 %collective-permute-start.11 = (bf16[16,2048]{1,0:T(8,128)(2,1)S(1)}, bf16[16,2048]{1,0:T(8,128)(2,1)S(1)}, u32[]{:S(2)}, u32[]{:S(2)}) collective-permute-start(bf16[16,2048]{1,0:T(8,128)(2,1)S(1)} %get-tuple-element.37), channel_id=1, source_target_pairs={{0,12},{1,13},{2,14},{3,15},{4,8},{5,9},{6,10},{7,11},{8,4},{9,5},... | collective-permute-start | bytes 196616 | tf_op jit(solution)/shard_map/ppermute | solution.py:31
  17.7 7.0 %collective-permute-start.32 = (bf16[16,6144]{1,0:T(8,128)(2,1)S(1)}, bf16[16,6144]{1,0:T(8,128)(2,1)S(1)}, u32[]{:S(2)}, u32[]{:S(2)}) collective-permute-start(bf16[16,6144]{1,0:T(8,128)(2,1)S(1)} %slice.67), channel_id=1, source_target_pairs={{0,4},{1,5},{2,6},{3,7},{4,0},{5,1},{6,2},{7,3},{8,12},{9,13},{10,... | collective-permute-start | bytes 589832 | tf_op jit(solution)/shard_map/ppermute | solution.py:31
  21.1 7.7 %collective-permute-start.12 = (bf16[16,2048]{1,0:T(8,128)(2,1)S(1)}, bf16[16,2048]{1,0:T(8,128)(2,1)S(1)}, u32[]{:S(2)}, u32[]{:S(2)}) collective-permute-start(bf16[16,2048]{1,0:T(8,128)(2,1)S(1)} %get-tuple-element.38), channel_id=1, source_target_pairs={{0,13},{1,12},{2,15},{3,14},{4,9},{5,8},{6,11},{7,10},{8,5},{9,4},... | collective-permute-start | bytes 196616 | tf_op jit(solution)/shard_map/ppermute | solution.py:31
  22.2 8.0 %collective-permute-start.13 = (bf16[16,2048]{1,0:T(8,128)(2,1)S(1)}, bf16[16,2048]{1,0:T(8,128)(2,1)S(1)}, u32[]{:S(2)}, u32[]{:S(2)}) collective-permute-start(bf16[16,2048]{1,0:T(8,128)(2,1)S(1)} %get-tuple-element.39), channel_id=1, source_target_pairs={{0,14},{1,15},{2,12},{3,13},{4,10},{5,11},{6,8},{7,9},{8,6},{9,7},... | collective-permute-start | bytes 196616 | tf_op jit(solution)/shard_map/ppermute | solution.py:31
  24.7 11.0 %collective-permute-start.14 = (bf16[16,2048]{1,0:T(8,128)(2,1)S(1)}, bf16[16,2048]{1,0:T(8,128)(2,1)S(1)}, u32[]{:S(2)}, u32[]{:S(2)}) collective-permute-start(bf16[16,2048]{1,0:T(8,128)(2,1)S(1)} %get-tuple-element.40), channel_id=1, source_target_pairs={{0,15},{1,14},{2,13},{3,12},{4,11},{5,10},{6,9},{7,8},{8,7},{9,6},... | collective-permute-start | bytes 196616 | tf_op jit(solution)/shard_map/ppermute | solution.py:31
  27.9 14.0 %collective-permute-start.22 = (bf16[16,4224]{1,0:T(8,128)(2,1)S(1)}, bf16[16,4224]{1,0:T(8,128)(2,1)S(1)}, u32[]{:S(2)}, u32[]{:S(2)}) collective-permute-start(bf16[16,4224]{1,0:T(8,128)(2,1)S(1)} %pad_maximum_fusion.refs_0_), channel_id=1, source_target_pairs={{0,8},{1,9},{2,10},{3,11},{4,12},{5,13},{6,14},{7,15},{8,0},{9,1},... | collective-permute-start | bytes 405512 | tf_op jit(solution)/shard_map/ppermute | solution.py:31
  28.0 10.9 %collective-permute-start.2 = (bf16[16,2048]{1,0:T(8,128)(2,1)S(1)}, bf16[16,2048]{1,0:T(8,128)(2,1)S(1)}, u32[]{:S(2)}, u32[]{:S(2)}) collective-permute-start(bf16[16,2048]{1,0:T(8,128)(2,1)S(1)} %get-tuple-element.28), channel_id=1, source_target_pairs={{0,3},{1,2},{2,1},{3,0},{4,7},{5,6},{6,5},{7,4},{8,11},{9,10},{10,... | collective-permute-start | bytes 196616 | tf_op jit(solution)/shard_map/ppermute | solution.py:31
  28.9 10.1 %collective-permute-start.3 = (bf16[16,2048]{1,0:T(8,128)(2,1)S(1)}, bf16[16,2048]{1,0:T(8,128)(2,1)S(1)}, u32[]{:S(2)}, u32[]{:S(2)}) collective-permute-start(bf16[16,2048]{1,0:T(8,128)(2,1)S(1)} %get-tuple-element.29), channel_id=1, source_target_pairs={{0,4},{1,5},{2,6},{3,7},{4,0},{5,1},{6,2},{7,3},{8,12},{9,13},{10,... | collective-permute-start | bytes 196616 | tf_op jit(solution)/shard_map/ppermute | solution.py:31
  30.2 11.6 %collective-permute-start.4 = (bf16[16,2048]{1,0:T(8,128)(2,1)S(1)}, bf16[16,2048]{1,0:T(8,128)(2,1)S(1)}, u32[]{:S(2)}, u32[]{:S(2)}) collective-permute-start(bf16[16,2048]{1,0:T(8,128)(2,1)S(1)} %get-tuple-element.30), channel_id=1, source_target_pairs={{0,5},{1,4},{2,7},{3,6},{4,1},{5,0},{6,3},{7,2},{8,13},{9,12},{10,... | collective-permute-start | bytes 196616 | tf_op jit(solution)/shard_map/ppermute | solution.py:31
  35.8 8.9 %collective-permute-start.33 = (bf16[16,4096]{1,0:T(8,128)(2,1)S(1)}, bf16[16,4096]{1,0:T(8,128)(2,1)S(1)}, u32[]{:S(2)}, u32[]{:S(2)}) collective-permute-start(bf16[16,4096]{1,0:T(8,128)(2,1)S(1)} %slice.70), channel_id=1, source_target_pairs={{0,8},{1,9},{2,10},{3,11},{4,12},{5,13},{6,14},{7,15},{8,0},{9,1},... | collective-permute-start | bytes 393224 | tf_op jit(solution)/shard_map/ppermute | solution.py:31
  38.9 7.7 %collective-permute-start.18 = (bf16[16,4224]{1,0:T(8,128)(2,1)S(1)}, bf16[16,4224]{1,0:T(8,128)(2,1)S(1)}, u32[]{:S(2)}, u32[]{:S(2)}) collective-permute-start(bf16[16,4224]{1,0:T(8,128)(2,1)S(1)} %pad_maximum_fusion.refs_0_), channel_id=1, source_target_pairs={{0,4},{1,5},{2,6},{3,7},{4,0},{5,1},{6,2},{7,3},{8,12},{9,13},{10,... | collective-permute-start | bytes 405512 | tf_op jit(solution)/shard_map/ppermute | solution.py:31
  39.0 7.6 %collective-permute-start.16 = (bf16[16,4224]{1,0:T(8,128)(2,1)S(1)}, bf16[16,4224]{1,0:T(8,128)(2,1)S(1)}, u32[]{:S(2)}, u32[]{:S(2)}) collective-permute-start(bf16[16,4224]{1,0:T(8,128)(2,1)S(1)} %pad_maximum_fusion.refs_0_), channel_id=1, source_target_pairs={{0,2},{1,3},{2,0},{3,1},{4,6},{5,7},{6,4},{7,5},{8,10},{9,11},{10,... | collective-permute-start | bytes 405512 | tf_op jit(solution)/shard_map/ppermute | solution.py:31
  41.9 7.0 %collective-permute-start.26 = (bf16[16,4224]{1,0:T(8,128)(2,1)S(1)}, bf16[16,4224]{1,0:T(8,128)(2,1)S(1)}, u32[]{:S(2)}, u32[]{:S(2)}) collective-permute-start(bf16[16,4224]{1,0:T(8,128)(2,1)S(1)} %collective-permute-done.22.refs_8_), channel_id=1, source_target_pairs={{0,4},{1,5},{2,6},{3,7},{4,0},{5,1},{6,2},{7,3},{8,12},{9,13},{10,... | collective-permute-start | bytes 405512 | tf_op jit(solution)/shard_map/ppermute | solution.py:31
  46.6 6.4 %collective-permute-start.23 = (bf16[16,4224]{1,0:T(8,128)(2,1)S(1)}, bf16[16,4224]{1,0:T(8,128)(2,1)S(1)}, u32[]{:S(2)}, u32[]{:S(2)}) collective-permute-start(bf16[16,4224]{1,0:T(8,128)(2,1)S(1)} %collective-permute-done.22.refs_8_), channel_id=1, source_target_pairs={{0,1},{1,0},{2,3},{3,2},{4,5},{5,4},{6,7},{7,6},{8,9},{9,8},{10,11... | collective-permute-start | bytes 405512 | tf_op jit(solution)/shard_map/ppermute | solution.py:31
  48.8 6.7 %collective-permute-start.28 = (bf16[16,4224]{1,0:T(8,128)(2,1)S(1)}, bf16[16,4224]{1,0:T(8,128)(2,1)S(1)}, u32[]{:S(2)}, u32[]{:S(2)}) collective-permute-start(bf16[16,4224]{1,0:T(8,128)(2,1)S(1)} %collective-permute-done.26.refs_12_), channel_id=1, source_target_pairs={{0,2},{1,3},{2,0},{3,1},{4,6},{5,7},{6,4},{7,5},{8,10},{9,11},{10,... | collective-permute-start | bytes 405512 | tf_op jit(solution)/shard_map/ppermute | solution.py:31
  56.6 34.8 %collective-permute-start.5 = (bf16[16,2048]{1,0:T(8,128)(2,1)S(1)}, bf16[16,2048]{1,0:T(8,128)(2,1)S(1)}, u32[]{:S(2)}, u32[]{:S(2)}) collective-permute-start(bf16[16,2048]{1,0:T(8,128)(2,1)S(1)} %get-tuple-element.31), channel_id=1, source_target_pairs={{0,6},{1,7},{2,4},{3,5},{4,2},{5,3},{6,0},{7,1},{8,14},{9,15},{10,... | collective-permute-start | bytes 196616 | tf_op jit(solution)/shard_map/ppermute | solution.py:31
  57.3 34.1 %collective-permute-start.6 = (bf16[16,2048]{1,0:T(8,128)(2,1)S(1)}, bf16[16,2048]{1,0:T(8,128)(2,1)S(1)}, u32[]{:S(2)}, u32[]{:S(2)}) collective-permute-start(bf16[16,2048]{1,0:T(8,128)(2,1)S(1)} %get-tuple-element.32), channel_id=1, source_target_pairs={{0,7},{1,6},{2,5},{3,4},{4,3},{5,2},{6,1},{7,0},{8,15},{9,14},{10,... | collective-permute-start | bytes 196616 | tf_op jit(solution)/shard_map/ppermute | solution.py:31
  59.0 32.5 %collective-permute-start.7 = (bf16[16,2048]{1,0:T(8,128)(2,1)S(1)}, bf16[16,2048]{1,0:T(8,128)(2,1)S(1)}, u32[]{:S(2)}, u32[]{:S(2)}) collective-permute-start(bf16[16,2048]{1,0:T(8,128)(2,1)S(1)} %get-tuple-element.33), channel_id=1, source_target_pairs={{0,8},{1,9},{2,10},{3,11},{4,12},{5,13},{6,14},{7,15},{8,0},{9,1},... | collective-permute-start | bytes 196616 | tf_op jit(solution)/shard_map/ppermute | solution.py:31
  60.6 30.9 %collective-permute-start.8 = (bf16[16,2048]{1,0:T(8,128)(2,1)S(1)}, bf16[16,2048]{1,0:T(8,128)(2,1)S(1)}, u32[]{:S(2)}, u32[]{:S(2)}) collective-permute-start(bf16[16,2048]{1,0:T(8,128)(2,1)S(1)} %get-tuple-element.34), channel_id=1, source_target_pairs={{0,9},{1,8},{2,11},{3,10},{4,13},{5,12},{6,15},{7,14},{8,1},{9,0},... | collective-permute-start | bytes 196616 | tf_op jit(solution)/shard_map/ppermute | solution.py:31
  61.9 29.5 %collective-permute-start.9 = (bf16[16,2048]{1,0:T(8,128)(2,1)S(1)}, bf16[16,2048]{1,0:T(8,128)(2,1)S(1)}, u32[]{:S(2)}, u32[]{:S(2)}) collective-permute-start(bf16[16,2048]{1,0:T(8,128)(2,1)S(1)} %get-tuple-element.35), channel_id=1, source_target_pairs={{0,10},{1,11},{2,8},{3,9},{4,14},{5,15},{6,12},{7,13},{8,2},{9,3},... | collective-permute-start | bytes 196616 | tf_op jit(solution)/shard_map/ppermute | solution.py:31
  (23 other events, 137.7 us)

commit v3 on v2

--- a/solution.py
+++ b/solution.py
@@ -31,62 +31,186 @@
     return lax.ppermute(x, axis, [(i, i ^ bit) for i in range(count)])
 
 
-def cut_grads_kernel(me_ref, grad_ref, *out_refs):
-    cols = out_refs[0].shape[1]
-    for r, out_ref in enumerate(out_refs):
-        at = pl.multiple_of((me_ref[0] ^ r) * cols, cols)
-        out_ref[...] = grad_ref[:, pl.ds(at, cols)]
-
-
-def cut_grads(me, grads, count):
+def run_copies(pairs, sems):
+    copies = [pltpu.make_async_copy(src, dst, sems.at[n]) for n, (src, dst) in enumerate(pairs)]
+    for copy in copies:
+        copy.start()
+    for copy in copies:
+        copy.wait()
+
+
+def in_smem(n):
+    return [pl.BlockSpec(memory_space=pltpu.SMEM)] * n
+
+
+def in_vmem(n):
+    return [pl.BlockSpec(memory_space=pltpu.VMEM)] * n
+
+
+def in_place(n):
+    return [pl.BlockSpec(memory_space=pl.ANY)] * n
+
+
+def in_hbm(n):
+    return [pl.BlockSpec(memory_space=pltpu.HBM)] * n
+
+
+def cut_factors_kernel(order, hidden, place_ref, fac_ref, keep_ref, give_ref, sems):
+    cols = hidden // len(order)
+    half = (fac_ref.shape[2] - hidden) // 2
+    me, batch = place_ref[0], place_ref[1]
+    pairs = []
+    for part, out_ref in enumerate((keep_ref, give_ref)):
+        picked = order[part * len(order) // 2:(part + 1) * len(order) // 2]
+        for at, r in enumerate(picked):
+            src = pl.multiple_of((me ^ r) * cols, cols)
+            pairs.append((
+                fac_ref.at[batch, :, pl.ds(src, cols)],
+                out_ref.at[:, at * cols:(at + 1) * cols],
+            ))
+        src = pl.multiple_of(hidden + ((me & 1) ^ part) * half, LANES)
+        pairs.append((fac_ref.at[batch, :, pl.ds(src, half)], out_ref.at[:, len(picked) * cols:]))
+    run_copies(pairs, sems)
+
+
+def cut_factors(place, factors, order, hidden):
+    rows, width = factors.shape[1:]
+    half = jax.ShapeDtypeStruct((rows, width // 2), factors.dtype)
+    return pl.pallas_call(
+        functools.partial(cut_factors_kernel, order, hidden),
+        in_specs=in_smem(1) + in_hbm(1),
+        out_specs=in_vmem(2),
+        out_shape=[half] * 2,
+        scratch_shapes=[pltpu.SemaphoreType.DMA((len(order) + 2,))],
+        compiler_params=params(60),
+        cost_estimate=pl.CostEstimate(flops=0, bytes_accessed=2 * factors.size, transcendentals=0),
+    )(place, factors)
+
+
+def pick_kernel(bit, cols, place_ref, owners_ref, keep_ref, got_ref, *out_refs):
+    owner = owners_ref[place_ref[1]]
+    same = ((owner ^ place_ref[0]) & bit) == 0
+    count = (keep_ref.shape[1] - out_refs[0].shape[1]) // cols
+
+    def fill(ref):
+        if len(out_refs) == 1:
+            out_refs[0][...] = ref[...]
+        else:
+            for part, out_ref in enumerate(out_refs):
+                out_ref[:, :count * cols] = ref[:, part * count * cols:(part + 1) * count * cols]
+                out_ref[:, count * cols:] = ref[:, 2 * count * cols:]
+
+    @pl.when(same)
+    def _():
+        fill(keep_ref)
+
+    @pl.when(jnp.logical_not(same))
+    def _():
+        fill(got_ref)
+
+
+def pick(place, owners, keep, got, bit, cols, count):
+    rows, width = keep.shape
+    if count > 1:
+        out = [jax.ShapeDtypeStruct((rows, width - count // 2 * cols), keep.dtype)] * 2
+    else:
+        out = [jax.ShapeDtypeStruct((rows, width), keep.dtype)]
+    return pl.pallas_call(
+        functools.partial(pick_kernel, bit, cols),
+        in_specs=in_smem(2) + in_vmem(2),
+        out_specs=in_vmem(len(out)),
+        out_shape=out,
+        compiler_params=params(16),
+        cost_estimate=pl.CostEstimate(flops=0, bytes_accessed=6 * keep.size, transcendentals=0),
+    )(place, owners, keep, got)
+
+
+def cut_grads_kernel(place_ref, grad_ref, _, out_ref, sems):
+    count = sems.shape[0]
+    cols = out_ref.shape[1] // count
+    pairs = []
+    for q in range(count):
+        src = pl.multiple_of((place_ref[0] ^ (2 * q + 1)) * cols, cols)
+        pairs.append((grad_ref.at[:, pl.ds(src, cols)], out_ref.at[:, q * cols:(q + 1) * cols]))
+    run_copies(pairs, sems)
+
+
+def cut_grads(place, grads, after, wide_count):
     rows, hidden = grads.shape
-    piece = jax.ShapeDtypeStruct((rows, hidden // count), grads.dtype)
     return pl.pallas_call(
         cut_grads_kernel,
-        in_specs=[pl.BlockSpec(memory_space=pltpu.SMEM), pl.BlockSpec(memory_space=pltpu.VMEM)],
-        out_specs=[pl.BlockSpec(memory_space=pltpu.VMEM)] * count,
+        in_specs=in_smem(1) + in_place(2),
+        out_specs=in_vmem(1)[0],
+        out_shape=jax.ShapeDtypeStruct((rows, hidden // 2), grads.dtype),
+        scratch_shapes=[pltpu.SemaphoreType.DMA((wide_count // 2,))],
+        compiler_params=params(16),
+        cost_estimate=pl.CostEstimate(flops=0, bytes_accessed=2 * grads.size, transcendentals=0),
+    )(place, grads, after)
+
+
+def pack_grads_kernel(count, place_ref, grad_ref, got_ref, *refs):
+    out_refs, sems = refs[-count - 1:-1], refs[-1]
+    rows, cols = grad_ref.shape[0], out_refs[0].shape[1]
+    pairs = []
+    for q, out_ref in enumerate(out_refs):
+        src = pl.multiple_of((place_ref[0] ^ (2 * q)) * cols, cols)
+        pairs.append((grad_ref.at[:, pl.ds(src, cols)], out_ref.at[:rows, :]))
+        pairs.append((got_ref.at[:, q * cols:(q + 1) * cols], out_ref.at[rows:, :]))
+    run_copies(pairs, sems)
+
+
+def pack_grads(place, grads, got, after, wide_count):
+    rows, hidden = grads.shape
+    count = wide_count // 2
+    piece = jax.ShapeDtypeStruct((2 * rows, hidden // wide_count), grads.dtype)
+    return pl.pallas_call(
+        functools.partial(pack_grads_kernel, count),
+        in_specs=in_smem(1) + in_place(2 + len(after)),
+        out_specs=in_vmem(count),
         out_shape=[piece] * count,
+        scratch_shapes=[pltpu.SemaphoreType.DMA((2 * count,))],
         compiler_params=params(16),
         cost_estimate=pl.CostEstimate(flops=0, bytes_accessed=4 * grads.size, transcendentals=0),
-    )(me, grads)
-
-
-def cut_factors_kernel(order, hidden, me_ref, fac_ref, keep_ref, give_ref):
-    cols = hidden // len(order)
-    half = (fac_ref.shape[2] - hidden) // 2
-    batch = me_ref[1]
-    mine = me_ref[0]
-    for part, out_ref in enumerate((keep_ref, give_ref)):
-        picked = order[part * len(order) // 2:(part + 1) * len(order) // 2]
-        for place, r in enumerate(picked):
-            at = pl.multiple_of((mine ^ r) * cols, cols)
-            out_ref[:, place * cols:(place + 1) * cols] = fac_ref[batch, :, pl.ds(at, cols)]
-        at = pl.multiple_of(hidden + ((mine & 1) ^ part) * half, LANES)
-        out_ref[:, len(picked) * cols:] = fac_ref[batch, :, pl.ds(at, half)]
-
-
-def cut_factors(me_batch, factors, order, hidden):
-    rows, width = factors.shape[1:]
-    half = jax.ShapeDtypeStruct((rows, width // 2), factors.dtype)
-    return pl.pallas_call(
-        functools.partial(cut_factors_kernel, order, hidden),
-        in_specs=[pl.BlockSpec(memory_space=pltpu.SMEM), pl.BlockSpec(memory_space=pltpu.VMEM)],
-        out_specs=[pl.BlockSpec(memory_space=pltpu.VMEM)] * 2,
-        out_shape=[half] * 2,
+    )(place, grads, got, *after)
+
+
+def rotate_kernel(ids_ref, act_ref, basis_ref, _, out_ref):
+    rows, width = act_ref.shape
+    depth = basis_ref.shape[0]
+    for k in range(width // depth):
+        cols = slice(k * depth, (k + 1) * depth)
+        out_ref[:, cols] = jnp.dot(
+            act_ref[:, cols], basis_ref[:, cols], preferred_element_type=jnp.float32
+        ).astype(jnp.bfloat16)
+    row = lax.broadcasted_iota(jnp.int32, (rows, LANES), 0)
+    ids = jnp.zeros((rows, LANES), jnp.int32)
+    for t in range(rows):
+        ids = jnp.where(row == t, ids_ref[t], ids)
+    out_ref[:, width:] = ids.astype(jnp.float32).astype(jnp.bfloat16)
+
+
+def rotate(ids, act, basis, after):
+    rows, width = act.shape
+    return pl.pallas_call(
+        rotate_kernel,
+        in_specs=in_smem(1) + in_vmem(2) + in_place(1),
+        out_specs=in_vmem(1)[0],
+        out_shape=jax.ShapeDtypeStruct((rows, width + LANES), act.dtype),
         compiler_params=params(16),
-        cost_estimate=pl.CostEstimate(flops=0, bytes_accessed=4 * factors.size, transcendentals=0),
-    )(me_batch, factors)
-
-
-def image_kernel(count, batch_count, me_ref, *refs):
+        cost_estimate=pl.CostEstimate(
+            flops=2 * rows * width * basis.shape[0], bytes_accessed=2 * basis.size, transcendentals=0
+        ),
+    )(ids, act, basis, after)
+
+
+def image_kernel(order, count, batch_count, me_ref, *refs):
     act_refs = refs[:count]
-    basis_ref = refs[count]
-    left_refs = refs[count + 1:count + 1 + batch_count]
-    half_refs = refs[count + 1 + batch_count:count + 1 + 3 * batch_count]
-    eig_ref, out_ref, ids_ref = refs[count + 1 + 3 * batch_count:count + 4 + 3 * batch_count]
-    rot_ref, right_ref, turn_ref, pre_a, pre_b = refs[count + 4 + 3 * batch_count:]
-    rows = eig_ref.shape[0]
-    depth, width = basis_ref.shape
+    left_refs = refs[count:count + batch_count]
+    half_refs = refs[count + batch_count:count + 3 * batch_count]
+    eig_ref, out_ref, ids_ref = refs[count + 3 * batch_count:count + 3 + 3 * batch_count]
+    rot_ref, right_ref, turn_ref, pre_a, pre_b = refs[count + 3 + 3 * batch_count:]
+    act_refs = [act_refs[n].at[at:at + size, :] for n, at, size in order]
+    rows, width = eig_ref.shape
     half = pre_a.shape[0] // batch_count
     chunk = pre_a.shape[1]
     per = width // chunk
@@ -95,18 +219,17 @@
 
     @pl.when(pl.program_id(0) == 0)
     def _():
-        for k in range(width // depth):
-            cols = slice(k * depth, (k + 1) * depth)
-            act = jnp.concatenate([ref[:, cols] for ref in act_refs], axis=0)
-            turned = jnp.dot(act, basis_ref[:, cols], preferred_element_type=jnp.float32)
-            rot_ref[cols, :] = turned.astype(jnp.bfloat16).T
+        for k in range(width // chunk):
+            cols = slice(k * chunk, (k + 1) * chunk)
+            rot_ref[cols, :] = jnp.concatenate([ref[:, cols] for ref in act_refs], axis=0).T
         ids = jnp.concatenate([ref[:, width:] for ref in act_refs], axis=0)
         ids_ref[...] = ids.astype(jnp.float32).T[:ids_ref.shape[0], :]
         side = width // 2
         for b in range(batch_count):
             for other in range(2):
                 at = pl.multiple_of(((me_ref[0] & 1) ^ other) * side, side)
-                right_ref[b, :, pl.ds(at, side)] = half_refs[2 * b + other][...]
+                ref = half_refs[2 * b + other]
+                right_ref[b, :, pl.ds(at, side)] = ref[:, ref.shape[1] - side:]
 
     for b in range(batch_count):
         turn_ref[b] = left_refs[b][...].T
@@ -130,19 +253,17 @@
                 outer_sum * inverse
             ).astype(jnp.bfloat16)
 
-    def absorb(k, b, pre):
+    def absorb(k, pre):
         row, col = place(k)
         rot = rot_ref[pl.ds(pl.multiple_of(col, chunk), chunk), :]
-        out_ref[b, pl.ds(row, half), :] += jnp.dot(
-            pre[b * half:(b + 1) * half, :], rot, preferred_element_type=jnp.float32
-        )
+        more = jnp.dot(pre[...], rot, preferred_element_type=jnp.float32)
+        for b in range(batch_count):
+            out_ref[b, pl.ds(row, half), :] += more[b * half:(b + 1) * half, :]
 
     def both(k, pre_now, pre_next):
-        subs = chunk // tile
-        for b in range(batch_count):
-            for s in range(b * subs // batch_count, (b + 1) * subs // batch_count):
-                produce(k + 1, s, pre_next)
-            absorb(k, b, pre_now)
+        absorb(k, pre_now)
+        for s in range(chunk // tile):
+            produce(k + 1, s, pre_next)
 
     for s in range(chunk // tile):
         produce(0, s, pre_a)
@@ -154,23 +275,21 @@
 
     lax.fori_loop(0, phases // 2 - 1, pair, 0)
     both(phases - 2, pre_a, pre_b)
-    for b in range(batch_count):
-        absorb(phases - 1, b, pre_b)
-
-
-def images(me, act_pieces, act_basis, lefts, halves, eigenvalues):
+    absorb(phases - 1, pre_b)
+
+
+def images(me, act_pieces, order, lefts, halves, eigenvalues):
     count, batch_count = len(act_pieces), len(lefts)
-    tokens = count * act_pieces[0].shape[0]
+    tokens = sum(x.shape[0] for x in act_pieces)
     hidden, width = eigenvalues.shape
     rows = min(512, hidden)
     half = min(256, rows)
     chunk = min(1024, width // 2)
     return pl.pallas_call(
-        functools.partial(image_kernel, count, batch_count),
+        functools.partial(image_kernel, order, count, batch_count),
         grid=(hidden // rows,),
-        in_specs=[pl.BlockSpec(memory_space=pltpu.SMEM)]
+        in_specs=in_smem(1)
         + [whole_block(x.shape) for x in act_pieces]
-        + [whole_block(act_basis.shape)]
         + [pl.BlockSpec((QT, rows), lambda i: (0, i)) for x in lefts]
         + [whole_block(x.shape) for x in halves]
         + [pl.BlockSpec((rows, width), lambda i: (i, 0))],
@@ -195,7 +314,7 @@
             bytes_accessed=2 * hidden * width,
             transcendentals=0,
         ),
-    )(me, *act_pieces, act_basis, *lefts, *halves, eigenvalues)
+    )(me, *act_pieces, *lefts, *halves, eigenvalues)
 
 
 def score_kernel(count, batch_count, seq_count, *refs):
@@ -268,34 +387,42 @@
         order = order + [r + bit for r in order]
     order = sorted(order, key=lambda r: [r & bit for bit in bits])
     keep, give = cut_factors(place, query_factors, order, hidden)
-    owner = owners[batch]
-    got = swap(give, "wide", 1)
-    held = jnp.where((owner & 1) == (me & 1), keep, got)
     count = wide_count // 2
-    for bit in bits[1:]:
+    for bit in bits:
+        got = swap(give, "wide", bit)
+        picked = pick(place, owners, keep, got, bit, cols, count)
+        keep, give = picked[0], picked[-1]
         count //= 2
-        got = swap(held[:, count * cols:], "wide", bit)
-        keep = jnp.concatenate([held[:, :count * cols], held[:, 2 * count * cols:]], axis=1)
-        held = jnp.where((owner & bit) == (me & bit), keep, got)
+        if bit == 1:
+            rot = rotate(seq_ids, train_act, act_basis, give)
+            grads_out = cut_grads(place, train_grad, rot, wide_count)
+    held = keep
     other = swap(held, "groups", 1)
-    lefts = [held[:, :cols], other[:, :cols]]
+    lefts = [held, other]
     halves = []
     for x in (held, other):
-        halves += [x[:, cols:], swap(x[:, cols:], "wide", 1)]
-
-    ids_cols = jnp.broadcast_to(seq_ids[:, None].astype(jnp.bfloat16), (tok_local, LANES))
-    acts = {0: jnp.concatenate([train_act, ids_cols], axis=1)}
-    for bit in reversed(bits):
+        halves += [x, swap(x[:, cols:], "wide", 1)]
+
+    acts = {0: rot}
+    for bit in reversed(bits[2:]):
         acts.update({r + bit: swap(x, "wide", bit) for r, x in acts.items()})
-    act_pieces = [acts[r] for r in range(wide_count)]
-
-    sent = cut_grads(place, train_grad, wide_count)
-    grad_pieces = [sent[0]] + [swap(sent[r], "wide", r) for r in range(1, wide_count)]
-
-    image, ids = images(place, act_pieces, act_basis, lefts, halves, eigenvalues)
+    far = jnp.concatenate([acts[r] for r in range(4, wide_count, 4)], axis=0)
+    acts = [acts[0], far]
+    for bit in (2, 1):
+        acts = [x for piece in acts for x in (piece, swap(piece, "wide", bit))]
+    token_order = [(r, 0, tok_local) for r in range(4)]
+    token_order += [(4 + r % 4, (r // 4 - 1) * tok_local, tok_local) for r in range(4, wide_count)]
+
+    grads_got = swap(grads_out, "wide", 1)
+    sent = pack_grads(place, train_grad, grads_got, [far], wide_count)
+    grad_pieces = [sent[0]] + [swap(sent[q], "wide", 2 * q) for q in range(1, wide_count // 2)]
+
+    image, ids = images(place, acts, token_order, lefts, halves, eigenvalues)
     parts = score_parts(grad_pieces, grad_basis, image, ids, seq_count)[:, :, 0]
-    for bit in bits:
-        parts = parts + swap(parts, "wide", bit)
+    parts = lax.all_to_all(
+        jnp.broadcast_to(parts[None], (wide_count,) + parts.shape), "wide", 0, 0
+    )
+    parts = jnp.sum(parts, axis=0)
     mine, others = parts[0], parts[1]
     first = jnp.where(batch == 0, mine, others)
     second = jnp.where(batch == 0, others, mine)

time: 108 us -> 113 us (1.046)
  starting transfers between devices: 48 us -> 29.3 us
  waiting for transfers between devices: 21 us -> 38.5 us
  Pallas kernels: 29.9 us -> 36.2 us
  between operations: 2.82 us -> 0.21 us
  local copies, waits for them, and re-layouts: 5.35 us -> 6.82 us
    ppermute x41 -> x24, starting transfers between devices: 48 us -> 25.8 us  [swap(): return lax.ppermute(x, axis, [(i, i ^ bit) for i in range(count)])]
    ppermute x41 -> x24, waiting for transfers between devices: 21 us -> 32.1 us  [swap(): return lax.ppermute(x, axis, [(i, i ^ bit) for i in range(count)])]
    all_to_all x0 -> x1, waiting for transfers between devices: none -> 6.45 us  [per_device(): lax.all_to_all(jnp.broadcast_to(parts[None], (wide_count,) + parts.shape)...]
    pallas_call x2 -> x8, Pallas kernels: 26.6 us -> 30.5 us  [the longest x1 24.6 us: images(): pl.pallas_call(functools.partial(image_kernel, order, count, batch_count)...]
    all_to_all x0 -> x1, starting transfers between devices: none -> 3.48 us  [per_device(): lax.all_to_all(jnp.broadcast_to(parts[None], (wide_count,) + parts.shape)...]
    pallas_call x1, Pallas kernels: 0.62 us -> 3.28 us  [cut_factors(): pl.pallas_call(functools.partial(cut_factors_kernel, order, hidden), in_s...]
    unnamed x12 -> x22, local copies, waits for them, and re-layouts: 3.87 us -> 6.18 us
    dynamic_slice x1 -> x0, local copies, waits for them, and re-layouts: 1.29 us -> none  [per_device(): owner = owners[batch]]
  transfers between devices with their start and end apart: 41 -> 25, of which waited for: 11 -> 10; matrix products, arithmetic and copies ran while one was open for 2% -> 0% of each run, Pallas kernels for 25% -> 26%
where the time goes in v3:
time: 113 us; the launch traced here: 112 us
  waiting for transfers between devices  38.5 us (34%)
  Pallas kernels  36.2 us (32%)
  starting transfers between devices  29.3 us (26%)
  local copies, waits for them, and re-layouts  6.82 us (6%)
  other arithmetic  1.37 us (1%)
    ppermute x24, waiting for transfers between devices, swap(): return lax.ppermute(x, axis, [(i, i ^ bit) for i in range(count)])  32.1 us
    ppermute x24, starting transfers between devices, swap(): return lax.ppermute(x, axis, [(i, i ^ bit) for i in range(count)])  25.8 us
    pallas_call x1, Pallas kernels, images(): pl.pallas_call(functools.partial(image_kernel, order, count, batch_count)...  24.6 us
    all_to_all x1, waiting for transfers between devices, per_device(): lax.all_to_all(jnp.broadcast_to(parts[None], (wide_count,) + parts.shape)...  6.45 us
    unnamed x22, local copies, waits for them, and re-layouts  6.18 us
    all_to_all x1, starting transfers between devices, per_device(): lax.all_to_all(jnp.broadcast_to(parts[None], (wide_count,) + parts.shape)...  3.48 us
    pallas_call x1, Pallas kernels, cut_factors(): pl.pallas_call(functools.partial(cut_factors_kernel, order, hidden), in_s...  3.28 us
    pallas_call x1, Pallas kernels, score_parts(): pl.pallas_call(functools.partial(score_kernel, count, batch_count, seq_co...  2.39 us
  transfers between devices with their start and end apart: 25, of which 10 were waited for; matrix products, arithmetic and copies ran while one was open for 0% of the time, Pallas kernels for 26%

profile of v3, /device:TPU:0, one launch (start us, length us, event | category | flops | bytes accessed | tf_op | source)
XLA Modules:
  0.0 112.4 jit_solution(8920046923195402306)
XLA Ops:
  0.7 3.3 %shard_map.82 = (bf16[16,18432]{1,0:T(8,128)(2,1)}, bf16[16,18432]{1,0:T(8,128)(2,1)}) custom-call(s32[2]{0:T(128)} %pad_add_fusion.place_ref.me_ref, bf16[2,16,36864]{2,1,0:T(8,128)(2,1)} %fac_ref.1), custom_call_target="tpu_custom_call" | custom-call | bytes 2359296 | tf_op jit(solution)/shard_map/pallas_call | solution.py:79
  4.5 1.8 %collective-permute-done.got_ref = bf16[16,18432]{1,0:T(8,128)(2,1)S(1)} collective-permute-done((bf16[16,18432]{1,0:T(8,128)(2,1)}, bf16[16,18432]{1,0:T(8,128)(2,1)S(1)}, u32[]{:S(2)}, u32[]{:S(2)}) %collective-permute-start) | collective-permute-done | bytes 589856 | tf_op jit(solution)/shard_map/ppermute | solution.py:31
  9.3 2.2 %copy-done.1 = bf16[512,4096]{1,0:T(8,128)(2,1)S(1)} copy-done((bf16[512,4096]{1,0:T(8,128)(2,1)S(1)}, bf16[512,4096]{1,0:T(8,128)(2,1)}, u32[]{:S(2)}) %copy-start.1) | copy-done | bytes 4194328
  14.3 3.0 %collective-permute-start.2 = (bf16[16,4224]{1,0:T(8,128)(2,1)S(1)}, bf16[16,4224]{1,0:T(8,128)(2,1)S(1)}, u32[]{:S(2)}, u32[]{:S(2)}) collective-permute-start(bf16[16,4224]{1,0:T(8,128)(2,1)S(1)} %shard_map.84._.refs_0_), channel_id=1, source_target_pairs={{0,4},{1,5},{2,6},{3,7},{4,0},{5,1},{6,2},{7,3},{8,12},{9,13},{10,... | collective-permute-start | bytes 405512 | tf_op jit(solution)/shard_map/ppermute | solution.py:31
  17.2 1.5 %collective-permute-start.18 = (bf16[16,10240]{1,0:T(8,128)(2,1)S(1)}, bf16[16,10240]{1,0:T(8,128)(2,1)S(1)}, u32[]{:S(2)}, u32[]{:S(2)}) collective-permute-start(bf16[16,10240]{1,0:T(8,128)(2,1)S(1)} %get-tuple-element.25._), channel_id=1, source_target_pairs={{0,2},{1,3},{2,0},{3,1},{4,6},{5,7},{6,4},{7,5},{8,10},{9,11},{10,... | collective-permute-start | bytes 983048 | tf_op jit(solution)/shard_map/ppermute | solution.py:31
  18.8 2.6 %collective-permute-start.3 = (bf16[16,4224]{1,0:T(8,128)(2,1)S(1)}, bf16[16,4224]{1,0:T(8,128)(2,1)S(1)}, u32[]{:S(2)}, u32[]{:S(2)}) collective-permute-start(bf16[16,4224]{1,0:T(8,128)(2,1)S(1)} %shard_map.84._.refs_0_), channel_id=1, source_target_pairs={{0,8},{1,9},{2,10},{3,11},{4,12},{5,13},{6,14},{7,15},{8,0},{9,1},... | collective-permute-start | bytes 405512 | tf_op jit(solution)/shard_map/ppermute | solution.py:31
  21.4 6.3 %collective-permute-done.3 = bf16[16,4224]{1,0:T(8,128)(2,1)S(1)} collective-permute-done((bf16[16,4224]{1,0:T(8,128)(2,1)S(1)}, bf16[16,4224]{1,0:T(8,128)(2,1)S(1)}, u32[]{:S(2)}, u32[]{:S(2)}) %collective-permute-start.3) | collective-permute-done | bytes 135200 | tf_op jit(solution)/shard_map/ppermute | solution.py:31
  27.6 5.0 %collective-permute-done.4 = bf16[16,4224]{1,0:T(8,128)(2,1)S(1)} collective-permute-done((bf16[16,4224]{1,0:T(8,128)(2,1)S(1)}, bf16[16,4224]{1,0:T(8,128)(2,1)S(1)}, u32[]{:S(2)}, u32[]{:S(2)}) %collective-permute-start.4) | collective-permute-done | bytes 135200 | tf_op jit(solution)/shard_map/ppermute | solution.py:31
  35.2 1.3 %collective-permute-start.13 = (bf16[16,4224]{1,0:T(8,128)(2,1)S(1)}, bf16[16,4224]{1,0:T(8,128)(2,1)S(1)}, u32[]{:S(2)}, u32[]{:S(2)}) collective-permute-start(bf16[16,4224]{1,0:T(8,128)(2,1)S(1)} %shard_map.84._.refs_0_), channel_id=1, source_target_pairs={{0,2},{1,3},{2,0},{3,1},{4,6},{5,7},{6,4},{7,5},{8,10},{9,11},{10,... | collective-permute-start | bytes 405512 | tf_op jit(solution)/shard_map/ppermute | solution.py:31
  36.8 6.5 %collective-permute-done.16.refs_6_ = bf16[48,4224]{1,0:T(8,128)(2,1)S(1)} collective-permute-done((bf16[48,4224]{1,0:T(8,128)(2,1)S(1)}, bf16[48,4224]{1,0:T(8,128)(2,1)S(1)}, u32[]{:S(2)}, u32[]{:S(2)}) %collective-permute-start.16) | collective-permute-done | bytes 405536 | tf_op jit(solution)/shard_map/ppermute | solution.py:31
  46.1 1.4 %shard_map.86 = (bf16[32,2048]{1,0:T(8,128)(2,1)S(1)}, bf16[32,2048]{1,0:T(8,128)(2,1)S(1)}, bf16[32,2048]{1,0:T(8,128)(2,1)S(1)}, bf16[32,2048]{1,0:T(8,128)(2,...) custom-call(s32[2]{0:T(128)S(1)} %copy-done.5, ...), custom_call_target="tpu_custom_call" | custom-call | bytes 2097152 | tf_op jit(solution)/shard_map/pallas_call | solution.py:166
  47.5 5.9 %collective-permute-done.20.got_ref = bf16[16,4096]{1,0:T(8,128)(2,1)S(1)} collective-permute-done((bf16[16,4096]{1,0:T(8,128)(2,1)S(1)}, bf16[16,4096]{1,0:T(8,128)(2,1)S(1)}, u32[]{:S(2)}, u32[]{:S(2)}) %collective-permute-start.20) | collective-permute-done | bytes 131104 | tf_op jit(solution)/shard_map/ppermute | solution.py:31
  54.0 1.6 %collective-permute-start.21 = (bf16[16,4096]{1,0:T(8,128)(2,1)S(1)}, bf16[16,4096]{1,0:T(8,128)(2,1)S(1)}, u32[]{:S(2)}, u32[]{:S(2)}) collective-permute-start(bf16[16,4096]{1,0:T(8,128)(2,1)S(1)} %shard_map.89.refs_8_.refs_10_), channel_id=1, source_target_pairs={{0,16},{16,0},{1,17},{17,1},{2,18},{18,2},{3,19},{19,3},{4,20},{20... | collective-permute-start | bytes 393224 | tf_op jit(solution)/shard_map/ppermute | solution.py:31
  55.6 2.4 %collective-permute-start.10 = (bf16[32,2048]{1,0:T(8,128)(2,1)S(1)}, bf16[32,2048]{1,0:T(8,128)(2,1)S(1)}, u32[]{:S(2)}, u32[]{:S(2)}) collective-permute-start(bf16[32,2048]{1,0:T(8,128)(2,1)S(1)} %get-tuple-element.32), channel_id=1, source_target_pairs={{0,12},{1,13},{2,14},{3,15},{4,8},{5,9},{6,10},{7,11},{8,4},{9,5},... | collective-permute-start | bytes 393224 | tf_op jit(solution)/shard_map/ppermute | solution.py:31
  57.9 1.5 %collective-permute-start.11 = (bf16[32,2048]{1,0:T(8,128)(2,1)S(1)}, bf16[32,2048]{1,0:T(8,128)(2,1)S(1)}, u32[]{:S(2)}, u32[]{:S(2)}) collective-permute-start(bf16[32,2048]{1,0:T(8,128)(2,1)S(1)} %get-tuple-element.33), channel_id=1, source_target_pairs={{0,14},{1,15},{2,12},{3,13},{4,10},{5,11},{6,8},{7,9},{8,6},{9,7},... | collective-permute-start | bytes 393224 | tf_op jit(solution)/shard_map/ppermute | solution.py:31
  59.5 4.0 %collective-permute-done.10.refs_6_ = bf16[32,2048]{1,0:T(8,128)(2,1)S(1)} collective-permute-done((bf16[32,2048]{1,0:T(8,128)(2,1)S(1)}, bf16[32,2048]{1,0:T(8,128)(2,1)S(1)}, u32[]{:S(2)}, u32[]{:S(2)}) %collective-permute-start.10) | collective-permute-done | bytes 131104 | tf_op jit(solution)/shard_map/ppermute | solution.py:31
  63.5 2.1 %collective-permute-done.11.refs_7_ = bf16[32,2048]{1,0:T(8,128)(2,1)S(1)} collective-permute-done((bf16[32,2048]{1,0:T(8,128)(2,1)S(1)}, bf16[32,2048]{1,0:T(8,128)(2,1)S(1)}, u32[]{:S(2)}, u32[]{:S(2)}) %collective-permute-start.11) | collective-permute-done | bytes 131104 | tf_op jit(solution)/shard_map/ppermute | solution.py:31
  66.9 3.3 %collective-permute-start.6 = (bf16[32,2048]{1,0:T(8,128)(2,1)S(1)}, bf16[32,2048]{1,0:T(8,128)(2,1)S(1)}, u32[]{:S(2)}, u32[]{:S(2)}) collective-permute-start(bf16[32,2048]{1,0:T(8,128)(2,1)S(1)} %get-tuple-element.28), channel_id=1, source_target_pairs={{0,4},{1,5},{2,6},{3,7},{4,0},{5,1},{6,2},{7,3},{8,12},{9,13},{10,... | collective-permute-start | bytes 393224 | tf_op jit(solution)/shard_map/ppermute | solution.py:31
  70.2 2.1 %collective-permute-start.8 = (bf16[32,2048]{1,0:T(8,128)(2,1)S(1)}, bf16[32,2048]{1,0:T(8,128)(2,1)S(1)}, u32[]{:S(2)}, u32[]{:S(2)}) collective-permute-start(bf16[32,2048]{1,0:T(8,128)(2,1)S(1)} %get-tuple-element.30), channel_id=1, source_target_pairs={{0,8},{1,9},{2,10},{3,11},{4,12},{5,13},{6,14},{7,15},{8,0},{9,1},... | collective-permute-start | bytes 393224 | tf_op jit(solution)/shard_map/ppermute | solution.py:31
  72.2 1.8 %collective-permute-start.9 = (bf16[32,2048]{1,0:T(8,128)(2,1)S(1)}, bf16[32,2048]{1,0:T(8,128)(2,1)S(1)}, u32[]{:S(2)}, u32[]{:S(2)}) collective-permute-start(bf16[32,2048]{1,0:T(8,128)(2,1)S(1)} %get-tuple-element.31), channel_id=1, source_target_pairs={{0,10},{1,11},{2,8},{3,9},{4,14},{5,15},{6,12},{7,13},{8,2},{9,3},... | collective-permute-start | bytes 393224 | tf_op jit(solution)/shard_map/ppermute | solution.py:31
  74.1 24.6 %shard_map.90 = (f32[2,2048,256]{2,1,0:T(8,128)S(1)}, f32[8,256]{1,0:T(8,128)S(1)}) custom-call(s32[2]{0:T(128)S(1)} %copy-done.6, bf16[16,4224]{1,0:T(8,128)(2,1)S(1)} %shard_map.84._.refs_0_, bf16[16,4224]{1,0:T(8,128)(2,1)S(1)} %collective-permute-done.12.refs_1_, bf16[16,4224]{1,0:T(8,128)(2,1)S(1)} %collective-permute-done.13.refs_2_, ...), custom_call_target="tpu_custom_call" | custom-call | flops 17179869184 | bytes 16777216 | tf_op jit(solution)/shard_map/pallas_call | solution.py:288
  98.8 2.4 %shard_map.91 = f32[2,8,1]{2,1,0:T(8,128)S(1)} custom-call(bf16[32,2048]{1,0:T(8,128)(2,1)S(1)} %get-tuple-element.26.refs_0_, bf16[32,2048]{1,0:T(8,128)(2,1)S(1)} %collective-permute-done.5.refs_1_, bf16[32,2048]{1,0:T(8,128)(2,1)S(1)} %collective-permute-done.6.refs_2_, bf16[32,2048]{1,0:T(8,128)(2,1)S(1)} %collective-permute-done.7.refs_3_, ...), custom_call_target="tpu_custom_call" | custom-call | flops 536870912 | bytes 4194304 | tf_op jit(solution)/shard_map/pallas_call | solution.py:349
  101.8 3.5 %all-to-all-start = ((f32[16,2,8]{2,1,0:T(2,128)}), f32[16,2,8]{2,1,0:T(2,128)S(1)}, u32[]{:S(2)}, u32[]{:S(2)}) async-start(f32[16,2,8]{2,1,0:T(2,128)} %broadcast_in_dim.8), calls=%async_computation | async-start | bytes 32768 | tf_op jit(solution)/shard_map/all_to_all | solution.py:422
  105.3 6.5 %all-to-all-done = f32[16,2,8]{2,1,0:T(2,128)S(1)} async-done(((f32[16,2,8]{2,1,0:T(2,128)}), f32[16,2,8]{2,1,0:T(2,128)S(1)}, u32[]{:S(2)}, u32[]{:S(2)}) %all-to-all-start) | async-done | bytes 1056 | tf_op jit(solution)/shard_map/all_to_all | solution.py:422
  (67 shorter events, 15.8 us)
Async XLA Ops:
  14.3 7.1 %collective-permute-start.2 = (bf16[16,4224]{1,0:T(8,128)(2,1)S(1)}, bf16[16,4224]{1,0:T(8,128)(2,1)S(1)}, u32[]{:S(2)}, u32[]{:S(2)}) collective-permute-start(bf16[16,4224]{1,0:T(8,128)(2,1)S(1)} %shard_map.84._.refs_0_), channel_id=1, source_target_pairs={{0,4},{1,5},{2,6},{3,7},{4,0},{5,1},{6,2},{7,3},{8,12},{9,13},{10,... | collective-permute-start | bytes 405512 | tf_op jit(solution)/shard_map/ppermute | solution.py:31
  17.2 17.1 %collective-permute-start.18 = (bf16[16,10240]{1,0:T(8,128)(2,1)S(1)}, bf16[16,10240]{1,0:T(8,128)(2,1)S(1)}, u32[]{:S(2)}, u32[]{:S(2)}) collective-permute-start(bf16[16,10240]{1,0:T(8,128)(2,1)S(1)} %get-tuple-element.25._), channel_id=1, source_target_pairs={{0,2},{1,3},{2,0},{3,1},{4,6},{5,7},{6,4},{7,5},{8,10},{9,11},{10,... | collective-permute-start | bytes 983048 | tf_op jit(solution)/shard_map/ppermute | solution.py:31
  18.8 8.9 %collective-permute-start.3 = (bf16[16,4224]{1,0:T(8,128)(2,1)S(1)}, bf16[16,4224]{1,0:T(8,128)(2,1)S(1)}, u32[]{:S(2)}, u32[]{:S(2)}) collective-permute-start(bf16[16,4224]{1,0:T(8,128)(2,1)S(1)} %shard_map.84._.refs_0_), channel_id=1, source_target_pairs={{0,8},{1,9},{2,10},{3,11},{4,12},{5,13},{6,14},{7,15},{8,0},{9,1},... | collective-permute-start | bytes 405512 | tf_op jit(solution)/shard_map/ppermute | solution.py:31
  27.6 5.0 %collective-permute-start.4 = (bf16[16,4224]{1,0:T(8,128)(2,1)S(1)}, bf16[16,4224]{1,0:T(8,128)(2,1)S(1)}, u32[]{:S(2)}, u32[]{:S(2)}) collective-permute-start(bf16[16,4224]{1,0:T(8,128)(2,1)S(1)} %collective-permute-done.3), channel_id=1, source_target_pairs={{0,4},{1,5},{2,6},{3,7},{4,0},{5,1},{6,2},{7,3},{8,12},{9,13},{10,... | collective-permute-start | bytes 405512 | tf_op jit(solution)/shard_map/ppermute | solution.py:31
  32.6 10.7 %collective-permute-start.16 = (bf16[48,4224]{1,0:T(8,128)(2,1)S(1)}, bf16[48,4224]{1,0:T(8,128)(2,1)S(1)}, u32[]{:S(2)}, u32[]{:S(2)}) collective-permute-start(bf16[48,4224]{1,0:T(8,128)(2,1)S(1)} %constant_dynamic-update-slice_fusion.refs_0_.refs_4_), channel_id=1, source_target_pairs={{0,2},{1,3},{2,0},{3,1},{4,6},{5,7},{6,4},{7,5},{8,10},{9,11},{10,... | collective-permute-start | bytes 1216520 | tf_op jit(solution)/shard_map/ppermute | solution.py:31
  34.2 11.8 %collective-permute-start.1 = (bf16[16,16384]{1,0:T(8,128)(2,1)S(1)}, bf16[16,16384]{1,0:T(8,128)(2,1)S(1)}, u32[]{:S(2)}, u32[]{:S(2)}) collective-permute-start(bf16[16,16384]{1,0:T(8,128)(2,1)S(1)} %shard_map.85), channel_id=1, source_target_pairs={{0,1},{1,0},{2,3},{3,2},{4,5},{5,4},{6,7},{7,6},{8,9},{9,8},{10,11... | collective-permute-start | bytes 1572872 | tf_op jit(solution)/shard_map/ppermute | solution.py:31
  34.9 8.4 %collective-permute-start.19 = (bf16[16,6144]{1,0:T(8,128)(2,1)S(1)}, bf16[16,6144]{1,0:T(8,128)(2,1)S(1)}, u32[]{:S(2)}, u32[]{:S(2)}) collective-permute-start(bf16[16,6144]{1,0:T(8,128)(2,1)S(1)} %get-tuple-element.36), channel_id=1, source_target_pairs={{0,4},{1,5},{2,6},{3,7},{4,0},{5,1},{6,2},{7,3},{8,12},{9,13},{10,... | collective-permute-start | bytes 589832 | tf_op jit(solution)/shard_map/ppermute | solution.py:31
  35.2 9.5 %collective-permute-start.13 = (bf16[16,4224]{1,0:T(8,128)(2,1)S(1)}, bf16[16,4224]{1,0:T(8,128)(2,1)S(1)}, u32[]{:S(2)}, u32[]{:S(2)}) collective-permute-start(bf16[16,4224]{1,0:T(8,128)(2,1)S(1)} %shard_map.84._.refs_0_), channel_id=1, source_target_pairs={{0,2},{1,3},{2,0},{3,1},{4,6},{5,7},{6,4},{7,5},{8,10},{9,11},{10,... | collective-permute-start | bytes 405512 | tf_op jit(solution)/shard_map/ppermute | solution.py:31
  36.6 30.3 %collective-permute-start.15 = (bf16[48,4224]{1,0:T(8,128)(2,1)S(1)}, bf16[48,4224]{1,0:T(8,128)(2,1)S(1)}, u32[]{:S(2)}, u32[]{:S(2)}) collective-permute-start(bf16[48,4224]{1,0:T(8,128)(2,1)S(1)} %constant_dynamic-update-slice_fusion.refs_0_.refs_4_), channel_id=1, source_target_pairs={{0,1},{1,0},{2,3},{3,2},{4,5},{5,4},{6,7},{7,6},{8,9},{9,8},{10,11... | collective-permute-start | bytes 1216520 | tf_op jit(solution)/shard_map/ppermute | solution.py:31
  43.3 28.9 %collective-permute-start.17 = (bf16[48,4224]{1,0:T(8,128)(2,1)S(1)}, bf16[48,4224]{1,0:T(8,128)(2,1)S(1)}, u32[]{:S(2)}, u32[]{:S(2)}) collective-permute-start(bf16[48,4224]{1,0:T(8,128)(2,1)S(1)} %collective-permute-done.16.refs_6_), channel_id=1, source_target_pairs={{0,1},{1,0},{2,3},{3,2},{4,5},{5,4},{6,7},{7,6},{8,9},{9,8},{10,11... | collective-permute-start | bytes 1216520 | tf_op jit(solution)/shard_map/ppermute | solution.py:31
  43.3 12.3 %collective-permute-start.12 = (bf16[16,4224]{1,0:T(8,128)(2,1)S(1)}, bf16[16,4224]{1,0:T(8,128)(2,1)S(1)}, u32[]{:S(2)}, u32[]{:S(2)}) collective-permute-start(bf16[16,4224]{1,0:T(8,128)(2,1)S(1)} %shard_map.84._.refs_0_), channel_id=1, source_target_pairs={{0,1},{1,0},{2,3},{3,2},{4,5},{5,4},{6,7},{7,6},{8,9},{9,8},{10,11... | collective-permute-start | bytes 405512 | tf_op jit(solution)/shard_map/ppermute | solution.py:31
  44.8 8.7 %collective-permute-start.20 = (bf16[16,4096]{1,0:T(8,128)(2,1)S(1)}, bf16[16,4096]{1,0:T(8,128)(2,1)S(1)}, u32[]{:S(2)}, u32[]{:S(2)}) collective-permute-start(bf16[16,4096]{1,0:T(8,128)(2,1)S(1)} %get-tuple-element.38), channel_id=1, source_target_pairs={{0,8},{1,9},{2,10},{3,11},{4,12},{5,13},{6,14},{7,15},{8,0},{9,1},... | collective-permute-start | bytes 393224 | tf_op jit(solution)/shard_map/ppermute | solution.py:31
  46.1 11.9 %collective-permute-start.14 = (bf16[16,4224]{1,0:T(8,128)(2,1)S(1)}, bf16[16,4224]{1,0:T(8,128)(2,1)S(1)}, u32[]{:S(2)}, u32[]{:S(2)}) collective-permute-start(bf16[16,4224]{1,0:T(8,128)(2,1)S(1)} %collective-permute-done.13.refs_2_), channel_id=1, source_target_pairs={{0,1},{1,0},{2,3},{3,2},{4,5},{5,4},{6,7},{7,6},{8,9},{9,8},{10,11... | collective-permute-start | bytes 405512 | tf_op jit(solution)/shard_map/ppermute | solution.py:31
  54.0 5.5 %collective-permute-start.21 = (bf16[16,4096]{1,0:T(8,128)(2,1)S(1)}, bf16[16,4096]{1,0:T(8,128)(2,1)S(1)}, u32[]{:S(2)}, u32[]{:S(2)}) collective-permute-start(bf16[16,4096]{1,0:T(8,128)(2,1)S(1)} %shard_map.89.refs_8_.refs_10_), channel_id=1, source_target_pairs={{0,16},{16,0},{1,17},{17,1},{2,18},{18,2},{3,19},{19,3},{4,20},{20... | collective-permute-start | bytes 393224 | tf_op jit(solution)/shard_map/ppermute | solution.py:31
  55.6 7.9 %collective-permute-start.10 = (bf16[32,2048]{1,0:T(8,128)(2,1)S(1)}, bf16[32,2048]{1,0:T(8,128)(2,1)S(1)}, u32[]{:S(2)}, u32[]{:S(2)}) collective-permute-start(bf16[32,2048]{1,0:T(8,128)(2,1)S(1)} %get-tuple-element.32), channel_id=1, source_target_pairs={{0,12},{1,13},{2,14},{3,15},{4,8},{5,9},{6,10},{7,11},{8,4},{9,5},... | collective-permute-start | bytes 393224 | tf_op jit(solution)/shard_map/ppermute | solution.py:31
  57.9 7.7 %collective-permute-start.11 = (bf16[32,2048]{1,0:T(8,128)(2,1)S(1)}, bf16[32,2048]{1,0:T(8,128)(2,1)S(1)}, u32[]{:S(2)}, u32[]{:S(2)}) collective-permute-start(bf16[32,2048]{1,0:T(8,128)(2,1)S(1)} %get-tuple-element.33), channel_id=1, source_target_pairs={{0,14},{1,15},{2,12},{3,13},{4,10},{5,11},{6,8},{7,9},{8,6},{9,7},... | collective-permute-start | bytes 393224 | tf_op jit(solution)/shard_map/ppermute | solution.py:31
  59.5 10.7 %collective-permute-start.22 = (bf16[16,2048]{1,0:T(8,128)(2,1)S(1)}, bf16[16,2048]{1,0:T(8,128)(2,1)S(1)}, u32[]{:S(2)}, u32[]{:S(2)}) collective-permute-start(bf16[16,2048]{1,0:T(8,128)(2,1)S(1)} %slice.16), channel_id=1, source_target_pairs={{0,1},{1,0},{2,3},{3,2},{4,5},{5,4},{6,7},{7,6},{8,9},{9,8},{10,11... | collective-permute-start | bytes 196616 | tf_op jit(solution)/shard_map/ppermute | solution.py:31
  63.5 6.7 %collective-permute-start.23 = (bf16[16,2048]{1,0:T(8,128)(2,1)S(1)}, bf16[16,2048]{1,0:T(8,128)(2,1)S(1)}, u32[]{:S(2)}, u32[]{:S(2)}) collective-permute-start(bf16[16,2048]{1,0:T(8,128)(2,1)S(1)} %slice.17), channel_id=1, source_target_pairs={{0,1},{1,0},{2,3},{3,2},{4,5},{5,4},{6,7},{7,6},{8,9},{9,8},{10,11... | collective-permute-start | bytes 196616 | tf_op jit(solution)/shard_map/ppermute | solution.py:31
  65.6 33.1 %collective-permute-start.5 = (bf16[32,2048]{1,0:T(8,128)(2,1)S(1)}, bf16[32,2048]{1,0:T(8,128)(2,1)S(1)}, u32[]{:S(2)}, u32[]{:S(2)}) collective-permute-start(bf16[32,2048]{1,0:T(8,128)(2,1)S(1)} %get-tuple-element.27), channel_id=1, source_target_pairs={{0,2},{1,3},{2,0},{3,1},{4,6},{5,7},{6,4},{7,5},{8,10},{9,11},{10,... | collective-permute-start | bytes 393224 | tf_op jit(solution)/shard_map/ppermute | solution.py:31
  66.9 31.8 %collective-permute-start.6 = (bf16[32,2048]{1,0:T(8,128)(2,1)S(1)}, bf16[32,2048]{1,0:T(8,128)(2,1)S(1)}, u32[]{:S(2)}, u32[]{:S(2)}) collective-permute-start(bf16[32,2048]{1,0:T(8,128)(2,1)S(1)} %get-tuple-element.28), channel_id=1, source_target_pairs={{0,4},{1,5},{2,6},{3,7},{4,0},{5,1},{6,2},{7,3},{8,12},{9,13},{10,... | collective-permute-start | bytes 393224 | tf_op jit(solution)/shard_map/ppermute | solution.py:31
  70.2 28.6 %collective-permute-start.7 = (bf16[32,2048]{1,0:T(8,128)(2,1)S(1)}, bf16[32,2048]{1,0:T(8,128)(2,1)S(1)}, u32[]{:S(2)}, u32[]{:S(2)}) collective-permute-start(bf16[32,2048]{1,0:T(8,128)(2,1)S(1)} %get-tuple-element.29), channel_id=1, source_target_pairs={{0,6},{1,7},{2,4},{3,5},{4,2},{5,3},{6,0},{7,1},{8,14},{9,15},{10,... | collective-permute-start | bytes 393224 | tf_op jit(solution)/shard_map/ppermute | solution.py:31
  70.2 28.6 %collective-permute-start.8 = (bf16[32,2048]{1,0:T(8,128)(2,1)S(1)}, bf16[32,2048]{1,0:T(8,128)(2,1)S(1)}, u32[]{:S(2)}, u32[]{:S(2)}) collective-permute-start(bf16[32,2048]{1,0:T(8,128)(2,1)S(1)} %get-tuple-element.30), channel_id=1, source_target_pairs={{0,8},{1,9},{2,10},{3,11},{4,12},{5,13},{6,14},{7,15},{8,0},{9,1},... | collective-permute-start | bytes 393224 | tf_op jit(solution)/shard_map/ppermute | solution.py:31
  72.2 26.5 %collective-permute-start.9 = (bf16[32,2048]{1,0:T(8,128)(2,1)S(1)}, bf16[32,2048]{1,0:T(8,128)(2,1)S(1)}, u32[]{:S(2)}, u32[]{:S(2)}) collective-permute-start(bf16[32,2048]{1,0:T(8,128)(2,1)S(1)} %get-tuple-element.31), channel_id=1, source_target_pairs={{0,10},{1,11},{2,8},{3,9},{4,14},{5,15},{6,12},{7,13},{8,2},{9,3},... | collective-permute-start | bytes 393224 | tf_op jit(solution)/shard_map/ppermute | solution.py:31
  101.8 9.9 %all-to-all-start = ((f32[16,2,8]{2,1,0:T(2,128)}), f32[16,2,8]{2,1,0:T(2,128)S(1)}, u32[]{:S(2)}, u32[]{:S(2)}) async-start(f32[16,2,8]{2,1,0:T(2,128)} %broadcast_in_dim.8), calls=%async_computation | async-start | bytes 32768 | tf_op jit(solution)/shard_map/all_to_all | solution.py:422
  (11 other events, 153.0 us)

commit v4 on v3

v4 whole, which is shorter than its diff:
```python
import functools
import math

import jax
import jax.numpy as jnp
from jax import lax
from jax.experimental import pallas as pl
from jax.experimental.pallas import tpu as pltpu
from jax.sharding import PartitionSpec as P

D = 4096
FF = 32768
SEQ_MEAN = 32
QT = 16
LANES = 128


damping = 0.1


def params(mib):
    return pltpu.CompilerParams(vmem_limit_bytes=mib * 1024 * 1024)


def whole_block(shape):
    return pl.BlockSpec(shape, lambda *_: (0,) * len(shape), pipeline_mode=pl.Buffered(1))


def swap(x, axis, bit):
    count = lax.axis_size(axis)
    return lax.ppermute(x, axis, [(i, i ^ bit) for i in range(count)])


def in_smem(n):
    return [pl.BlockSpec(memory_space=pltpu.SMEM)] * n


def in_vmem(n):
    return [pl.BlockSpec(memory_space=pltpu.VMEM)] * n


def in_place(n):
    return [pl.BlockSpec(memory_space=pl.ANY)] * n


def cut_factors_kernel(order, hidden, batch_count, fac_ref, keep_ref, give_ref):
    cols = hidden // len(order)
    half = (fac_ref.shape[2] - hidden) // 2
    me, batch = lax.axis_index("wide"), lax.rem(lax.axis_index("groups"), batch_count)
    for part, out_ref in enumerate((keep_ref, give_ref)):
        picked = order[part * len(order) // 2:(part + 1) * len(order) // 2]
        for at, r in enumerate(picked):
            src = pl.multiple_of((me ^ r) * cols, cols)
            out_ref[:, at * cols:(at + 1) * cols] = fac_ref[batch, :, pl.ds(src, cols)]
        src = pl.multiple_of(hidden + ((me & 1) ^ part) * half, LANES)
        out_ref[:, len(picked) * cols:] = fac_ref[batch, :, pl.ds(src, half)]


def cut_factors(factors, order, hidden, batch_count):
    rows, width = factors.shape[1:]
    half = jax.ShapeDtypeStruct((rows, width // 2), factors.dtype)
    return pl.pallas_call(
        functools.partial(cut_factors_kernel, order, hidden, batch_count),
        in_specs=in_vmem(1),
        out_specs=in_vmem(2),
        out_shape=[half] * 2,
        compiler_params=params(16),
        cost_estimate=pl.CostEstimate(flops=0, bytes_accessed=factors.size, transcendentals=0),
    )(factors)


def pick_kernel(bit, cols, batch_count, parts, join, owners_ref, keep_ref, got_ref, *refs):
    me, batch = lax.axis_index("wide"), lax.rem(lax.axis_index("groups"), batch_count)
    join_refs, out_refs = refs[:join], refs[join:]
    same = ((owners_ref[batch] ^ me) & bit) == 0
    count = (keep_ref.shape[1] - out_refs[0].shape[1]) // cols

    def fill(ref):
        if parts == 1:
            out_refs[0][...] = ref[...]
        else:
            for part in range(parts):
                out_ref = out_refs[part]
                out_ref[:, :count * cols] = ref[:, part * count * cols:(part + 1) * count * cols]
                out_ref[:, count * cols:] = ref[:, 2 * count * cols:]

    @pl.when(same)
    def _():
        fill(keep_ref)

    @pl.when(jnp.logical_not(same))
    def _():
        fill(got_ref)

    at = 0
    for ref in join_refs:
        out_refs[-1][at:at + ref.shape[0], :] = ref[...]
        at += ref.shape[0]


def pick(owners, keep, got, bit, cols, count, join=()):
    rows, width = keep.shape
    if count > 1:
        out = [jax.ShapeDtypeStruct((rows, width - count // 2 * cols), keep.dtype)] * 2
    else:
        out = [jax.ShapeDtypeStruct((rows, width), keep.dtype)]
    parts = len(out)
    if join:
        out.append(jax.ShapeDtypeStruct(
            (sum(x.shape[0] for x in join), join[0].shape[1]), join[0].dtype
        ))
    return pl.pallas_call(
        functools.partial(pick_kernel, bit, cols, owners.shape[0], parts, len(join)),
        in_specs=in_smem(1) + in_vmem(2 + len(join)),
        out_specs=in_vmem(len(out)),
        out_shape=out,
        compiler_params=params(16),
        cost_estimate=pl.CostEstimate(flops=0, bytes_accessed=2 * keep.size, transcendentals=0),
    )(owners, keep, got, *join)


def cut_grads_kernel(grad_ref, _, out_ref):
    count, rows, cols = out_ref.shape
    for to in range(count):
        out_ref[to] = grad_ref[:, to * cols:(to + 1) * cols]


def cut_grads(grads, after, count):
    rows, hidden = grads.shape
    return pl.pallas_call(
        cut_grads_kernel,
        in_specs=in_vmem(1) + in_place(1),
        out_specs=in_vmem(1)[0],
        out_shape=jax.ShapeDtypeStruct((count, rows, hidden // count), grads.dtype),
        compiler_params=params(16),
        cost_estimate=pl.CostEstimate(flops=0, bytes_accessed=grads.size, transcendentals=0),
    )(grads, after)


def rotate_kernel(ids_ref, act_ref, basis_ref, _, out_ref, held_ref, sems):
    rows, width = act_ref.shape
    depth = basis_ref.shape[0]
    copies = []
    for k in range(width // depth):
        cols = slice(k * depth, (k + 1) * depth)
        copy = pltpu.make_async_copy(basis_ref.at[:, cols], held_ref.at[k], sems.at[k])
        copy.start()
        copies.append(copy)
    row = lax.broadcasted_iota(jnp.int32, (rows, LANES), 0)
    ids = jnp.zeros((rows, LANES), jnp.int32)
    for t in range(rows):
        ids = jnp.where(row == t, ids_ref[t], ids)
    out_ref[:, width:] = ids.astype(jnp.float32).astype(jnp.bfloat16)
    for k, copy in enumerate(copies):
        cols = slice(k * depth, (k + 1) * depth)
        copy.wait()
        out_ref[:, cols] = jnp.dot(
            act_ref[:, cols], held_ref[k], preferred_element_type=jnp.float32
        ).astype(jnp.bfloat16)


def rotate(ids, act, basis, after):
    rows, width = act.shape
    depth = basis.shape[0]
    return pl.pallas_call(
        rotate_kernel,
        in_specs=in_smem(1) + in_vmem(1) + in_place(2),
        out_specs=in_vmem(1)[0],
        out_shape=jax.ShapeDtypeStruct((rows, width + LANES), act.dtype),
        scratch_shapes=[
            pltpu.VMEM((width // depth, depth, depth), jnp.bfloat16),
            pltpu.SemaphoreType.DMA((width // depth,)),
        ],
        compiler_params=params(55),
        cost_estimate=pl.CostEstimate(
            flops=2 * rows * width * basis.shape[0], bytes_accessed=basis.size, transcendentals=0
        ),
    )(ids, act, basis, after)


def image_kernel(order, count, batch_count, *refs):
    act_refs = refs[:count]
    left_refs = refs[count:count + batch_count]
    half_refs = refs[count + batch_count:count + 3 * batch_count]
    eig_ref, out_ref, ids_ref = refs[count + 3 * batch_count:count + 3 + 3 * batch_count]
    rot_ref, right_ref, turn_ref, pre_a, pre_b = refs[count + 3 + 3 * batch_count:]
    act_refs = [act_refs[n].at[at:at + size, :] for n, at, size in order]
    rows, width = eig_ref.shape
    half = pre_a.shape[0] // batch_count
    chunk = pre_a.shape[1]
    per = width // chunk
    phases = (rows // half) * per
    tile = min(256, chunk)

    @pl.when(pl.program_id(0) == 0)
    def _():
        for k in range(width // chunk):
            cols = slice(k * chunk, (k + 1) * chunk)
            rot_ref[cols, :] = jnp.concatenate([ref[:, cols] for ref in act_refs], axis=0).T
        ids = jnp.concatenate([ref[:, width:] for ref in act_refs], axis=0)
        ids_ref[...] = ids.astype(jnp.float32).T[:ids_ref.shape[0], :]
        side = width // 2
        for b in range(batch_count):
            for other in range(2):
                at = pl.multiple_of(((lax.axis_index("wide") & 1) ^ other) * side, side)
                ref = half_refs[2 * b + other]
                right_ref[b, :, pl.ds(at, side)] = ref[:, ref.shape[1] - side:]

    for b in range(batch_count):
        turn_ref[b] = left_refs[b][...].T
    out_ref[...] = jnp.zeros_like(out_ref)

    def place(k):
        return pl.multiple_of((k // per) * half, half), (k % per) * chunk

    def produce(k, s, pre):
        row, col = place(k)
        cols = pl.ds(pl.multiple_of(col + s * tile, tile), tile)
        damped = eig_ref[pl.ds(row, half), cols].astype(jnp.float32) + damping
        inverse = pl.reciprocal(damped, approx=True)
        for b in range(batch_count):
            outer_sum = jnp.dot(
                turn_ref[b, pl.ds(row, half), :], right_ref[b, :, cols],
                preferred_element_type=jnp.float32,
            )
            pre[b * half:(b + 1) * half, s * tile:(s + 1) * tile] = (
                outer_sum * inverse
            ).astype(jnp.bfloat16)

    def absorb(k, pre):
        row, col = place(k)
        rot = rot_ref[pl.ds(pl.multiple_of(col, chunk), chunk), :]
        more = jnp.dot(pre[...], rot, preferred_element_type=jnp.float32)
        for b in range(batch_count):
            out_ref[b, pl.ds(row, half), :] += more[b * half:(b + 1) * half, :]

    def both(k, pre_now, pre_next):
        absorb(k, pre_now)
        for s in range(chunk // tile):
            produce(k + 1, s, pre_next)

    for s in range(chunk // tile):
        produce(0, s, pre_a)

    def pair(q, carry):
        both(2 * q, pre_a, pre_b)
        both(2 * q + 1, pre_b, pre_a)
        return carry

    lax.fori_loop(0, phases // 2 - 1, pair, 0)
    both(phases - 2, pre_a, pre_b)
    absorb(phases - 1, pre_b)


def images(act_pieces, order, lefts, halves, eigenvalues):
    count, batch_count = len(act_pieces), len(lefts)
    tokens = sum(x.shape[0] for x in act_pieces)
    hidden, width = eigenvalues.shape
    rows = min(512, hidden)
    half = min(256, rows)
    chunk = min(1024, width // 2)
    return pl.pallas_call(
        functools.partial(image_kernel, order, count, batch_count),
        grid=(hidden // rows,),
        in_specs=[whole_block(x.shape) for x in act_pieces]
        + [pl.BlockSpec((QT, rows), lambda i: (0, i)) for x in lefts]
        + [whole_block(x.shape) for x in halves]
        + [pl.BlockSpec((rows, width), lambda i: (i, 0))],
        out_specs=[
            pl.BlockSpec((batch_count, rows, tokens), lambda i: (0, i, 0)),
            pl.BlockSpec((8, tokens), lambda i: (0, 0)),
        ],
        out_shape=[
            jax.ShapeDtypeStruct((batch_count, hidden, tokens), jnp.float32),
            jax.ShapeDtypeStruct((8, tokens), jnp.float32),
        ],
        scratch_shapes=[
            pltpu.VMEM((width, tokens), jnp.bfloat16),
            pltpu.VMEM((batch_count, QT, width), jnp.bfloat16),
            pltpu.VMEM((batch_count, rows, QT), jnp.bfloat16),
            pltpu.VMEM((batch_count * half, chunk), jnp.bfloat16),
            pltpu.VMEM((batch_count * half, chunk), jnp.bfloat16),
        ],
        compiler_params=params(32 if tokens <= 256 else 56),
        cost_estimate=pl.CostEstimate(
            flops=2 * hidden * width * (tokens + 256) * batch_count,
            bytes_accessed=2 * hidden * width,
            transcendentals=0,
        ),
    )(*act_pieces, *lefts, *halves, eigenvalues)


def score_kernel(batch_count, seq_count, grad_ref, basis_ref, image_ref, ids_ref, out_ref, token_ref):
    step = pl.program_id(0)
    me = lax.axis_index("wide")

    @pl.when(step == 0)
    def _():
        token_ref[...] = jnp.zeros_like(token_ref)

    grads = jnp.concatenate([grad_ref[me ^ r] for r in range(grad_ref.shape[0])], axis=0)
    turned = jnp.dot(grads, basis_ref[...], preferred_element_type=jnp.float32)
    turned = turned.astype(jnp.bfloat16).T.astype(jnp.float32)
    for b in range(batch_count):
        token_ref[b:b + 1, :] += jnp.sum(image_ref[b] * turned, axis=0, keepdims=True)

    @pl.when(step == pl.num_programs(0) - 1)
    def _():
        tokens = token_ref.shape[1]
        seqs = lax.broadcasted_iota(jnp.int32, (seq_count, tokens), 0).astype(jnp.float32)
        member = ids_ref[0:1, :] == seqs
        for b in range(batch_count):
            out_ref[b] = jnp.sum(jnp.where(member, token_ref[b:b + 1, :], 0.0), axis=1, keepdims=True)


def score_parts(grads, grad_basis, image, ids, seq_count):
    batch_count = image.shape[0]
    count, rows, hidden = grads.shape
    inner = min(grad_basis.shape[0], hidden)
    tokens = count * rows
    return pl.pallas_call(
        functools.partial(score_kernel, batch_count, seq_count),
        grid=(hidden // inner,),
        in_specs=[
            pl.BlockSpec((count, rows, inner), lambda i: (0, 0, i)),
            pl.BlockSpec((grad_basis.shape[0], inner), lambda i: (0, i)),
            pl.BlockSpec((batch_count, inner, tokens), lambda i: (0, i, 0)),
            pl.BlockSpec(ids.shape, lambda i: (0, 0)),
        ],
        out_specs=pl.BlockSpec((batch_count, seq_count, 1), lambda i: (0, 0, 0)),
        out_shape=jax.ShapeDtypeStruct((batch_count, seq_count, 1), jnp.float32),
        scratch_shapes=[pltpu.VMEM((8, tokens), jnp.float32)],
        compiler_params=params(16 if tokens <= 256 else 40),
        cost_estimate=pl.CostEstimate(
            flops=2 * tokens * hidden * grad_basis.shape[0],
            bytes_accessed=4 * image.size,
            transcendentals=0,
        ),
    )(grads, grad_basis, image, ids)


def per_device(
    train_act, train_grad, seq_ids, act_basis, grad_basis, eigenvalues, query_factors, owners
):
    wide_count = lax.axis_size("wide")
    bits = [1 << n for n in range(wide_count.bit_length() - 1)]
    me = lax.axis_index("wide")
    tok_local = train_act.shape[0]
    seq_count = tok_local * wide_count // SEQ_MEAN
    cols = grad_basis.shape[1]
    hidden = train_grad.shape[1]
    batch_count = owners.shape[0]
    score_scale = 1.0 / math.sqrt(FF * D * QT * SEQ_MEAN)
    batch = lax.axis_index("groups") % batch_count

    order = [0]
    for bit in reversed(bits):
        order = order + [r + bit for r in order]
    order = sorted(order, key=lambda r: [r & bit for bit in bits])
    keep, give = cut_factors(query_factors, order, hidden, batch_count)
    rot = rotate(seq_ids, train_act, act_basis, give)
    joined, ranks = rot, [0]
    far = bits[:1:-1]
    count = wide_count // 2
    for step, bit in enumerate(bits):
        got = swap(give, "wide", bit)
        join = ()
        if 1 <= step < len(far):
            join = (joined, swap(joined, "wide", far[step - 1]))
            ranks = ranks + [r + far[step - 1] for r in ranks]
        picked = list(pick(owners, keep, got, bit, cols, count, join))
        if join:
            joined = picked.pop()
        keep, give = picked[0], picked[-1]
        count //= 2
        if step == len(bits) - 2:
            sent = cut_grads(train_grad, give, wide_count)
            grads = lax.all_to_all(sent, "wide", 0, 0)
    held = keep
    acts = [(joined, ranks)]
    for bit in (far[-1], 2, 1):
        acts += [(swap(x, "wide", bit), [r + bit for r in has]) for x, has in acts]
    token_order = [None] * wide_count
    for n, (_, has) in enumerate(acts):
        for at, r in enumerate(has):
            token_order[r] = (n, at * tok_local, tok_local)
    acts = [x for x, _ in acts]

    other = swap(held, "groups", 1)
    lefts = [held, other]
    halves = []
    for x in (held, other):
        halves += [x, swap(x[:, cols:], "wide", 1)]

    image, ids = images(acts, token_order, lefts, halves, eigenvalues)
    parts = score_parts(grads, grad_basis, image, ids, seq_count)[:, :, 0]
    for near in (bits[:2], bits[2:]):
        step = near[0]
        others = [swap(parts, "wide", step * n) for n in range(1, 1 << len(near))]
        parts = parts + sum(others)
    mine, others = parts[0], parts[1]
    first = jnp.where(batch == 0, mine, others)
    second = jnp.where(batch == 0, others, mine)
    return jnp.stack([first, second], axis=1) * score_scale


def solution(mesh):
    return jax.shard_map(
        per_device,
        mesh=mesh,
        in_specs=(
            P(("groups", "wide"), None),
            P(("groups", "wide"), None),
            P(("groups", "wide")),
            P(),
            P(None, "wide"),
            P("wide", None),
            P("wide", None, None),
            P(),
        ),
        out_specs=P("groups", None),
        check_vma=False,
    )
```

time: 113 us -> 130 us (1.15)
  waiting for transfers between devices: 38.5 us -> 55.7 us
  local copies, waits for them, and re-layouts: 6.82 us -> 11.3 us
  starting transfers between devices: 29.3 us -> 26.9 us
    ppermute x24 -> x21, waiting for transfers between devices: 32.1 us -> 55.7 us  [swap(): return lax.ppermute(x, axis, [(i, i ^ bit) for i in range(count)])]
    all_to_all x1, waiting for transfers between devices: 6.45 us -> 0.01 us  [per_device(): grads = lax.all_to_all(sent, 'wide', 0, 0)]
    ppermute x24 -> x21, starting transfers between devices: 25.8 us -> 21 us  [swap(): return lax.ppermute(x, axis, [(i, i ^ bit) for i in range(count)])]
    unnamed x22 -> x26, local copies, waits for them, and re-layouts: 6.18 us -> 10 us
    all_to_all x1, starting transfers between devices: 3.48 us -> 5.83 us  [per_device(): grads = lax.all_to_all(sent, 'wide', 0, 0)]
    pallas_call x9 -> x8, Pallas kernels: 11.6 us -> 9.99 us  [the longest x1 4.14 us: rotate(): pl.pallas_call(rotate_kernel, in_specs=in_smem(1) + in_vmem(1) + in_place...]
  transfers between devices with their start and end apart: 25 -> 22, of which waited for: 10 -> 11; matrix products, arithmetic and copies ran while one was open for 0% -> 1% of each run, Pallas kernels for 26% -> 24%
where the time goes in v4:
time: 130 us
  waiting for transfers between devices  55.7 us (43%)
  Pallas kernels  35 us (27%)
  starting transfers between devices  26.9 us (21%)
  local copies, waits for them, and re-layouts  11.3 us (9%)
    ppermute x21, waiting for transfers between devices, swap(): return lax.ppermute(x, axis, [(i, i ^ bit) for i in range(count)])  55.7 us
    pallas_call x1, Pallas kernels, images(): pl.pallas_call(functools.partial(image_kernel, order, count, batch_count)...  25 us
    ppermute x21, starting transfers between devices, swap(): return lax.ppermute(x, axis, [(i, i ^ bit) for i in range(count)])  21 us
    unnamed x26, local copies, waits for them, and re-layouts  10 us
    all_to_all x1, starting transfers between devices, per_device(): grads = lax.all_to_all(sent, 'wide', 0, 0)  5.83 us
    pallas_call x1, Pallas kernels, rotate(): pl.pallas_call(rotate_kernel, in_specs=in_smem(1) + in_vmem(1) + in_place...  4.14 us
  transfers between devices with their start and end apart: 22, of which 11 were waited for; matrix products, arithmetic and copies ran while one was open for 1% of the time, Pallas kernels for 24%

profile of v4, /device:TPU:0, one launch (start us, length us, event | category | flops | bytes accessed | tf_op | source)
XLA Modules:
  0.0 129.6 jit_solution(16267372315473765653)
XLA Ops:
  0.0 1.7 %copy-done.2 = bf16[2,16,36864]{2,1,0:T(8,128)(2,1)S(1)} copy-done((bf16[2,16,36864]{2,1,0:T(8,128)(2,1)S(1)}, bf16[2,16,36864]{2,1,0:T(8,128)(2,1)}, u32[]{:S(2)}) %copy-start.2) | copy-done | bytes 2359320
  2.3 1.6 %collective-permute-done.got_ref = bf16[16,18432]{1,0:T(8,128)(2,1)S(1)} collective-permute-done((bf16[16,18432]{1,0:T(8,128)(2,1)S(1)}, bf16[16,18432]{1,0:T(8,128)(2,1)S(1)}, u32[]{:S(2)}, u32[]{:S(2)}) %collective-permute-start) | collective-permute-done | bytes 589856 | tf_op jit(solution)/shard_map/ppermute | solution.py:31
  5.2 3.0 %collective-permute-start.1 = (bf16[16,10240]{1,0:T(8,128)(2,1)S(1)}, bf16[16,10240]{1,0:T(8,128)(2,1)S(1)}, u32[]{:S(2)}, u32[]{:S(2)}) collective-permute-start(bf16[16,10240]{1,0:T(8,128)(2,1)S(1)} %get-tuple-element.19), channel_id=1, source_target_pairs={{0,2},{1,3},{2,0},{3,1},{4,6},{5,7},{6,4},{7,5},{8,10},{9,11},{10,... | collective-permute-start | bytes 983048 | tf_op jit(solution)/shard_map/ppermute | solution.py:31
  8.1 4.1 %shard_map.84.refs_0_ = bf16[16,4224]{1,0:T(8,128)(2,1)} custom-call(s32[16]{0:T(128)} %ids_ref.1, bf16[16,4096]{1,0:T(8,128)(2,1)} %act_ref.1, bf16[512,4096]{1,0:T(8,128)(2,1)} %basis_ref.2, bf16[16,18432]{1,0:T(8,128)(2,1)} %copy-done.5), custom_call_target="tpu_custom_call" | custom-call | flops 67108864 | bytes 2097152 | tf_op jit(solution)/shard_map/pallas_call | solution.py:165
  12.3 2.7 %collective-permute-start.2 = (bf16[16,4224]{1,0:T(8,128)(2,1)}, bf16[16,4224]{1,0:T(8,128)(2,1)S(1)}, u32[]{:S(2)}, u32[]{:S(2)}) collective-permute-start(bf16[16,4224]{1,0:T(8,128)(2,1)} %shard_map.84.refs_0_), channel_id=1, source_target_pairs={{0,8},{1,9},{2,10},{3,11},{4,12},{5,13},{6,14},{7,15},{8,0},{9,1},... | collective-permute-start | bytes 405512 | tf_op jit(solution)/shard_map/ppermute | solution.py:31
  14.9 6.8 %collective-permute-done.2.refs_1_ = bf16[16,4224]{1,0:T(8,128)(2,1)S(1)} collective-permute-done((bf16[16,4224]{1,0:T(8,128)(2,1)}, bf16[16,4224]{1,0:T(8,128)(2,1)S(1)}, u32[]{:S(2)}, u32[]{:S(2)}) %collective-permute-start.2) | collective-permute-done | bytes 135200 | tf_op jit(solution)/shard_map/ppermute | solution.py:31
  24.1 1.2 collective-permute-start.3
  25.8 7.0 %collective-permute-done.4.refs_1_ = bf16[32,4224]{1,0:T(8,128)(2,1)} collective-permute-done((bf16[32,4224]{1,0:T(8,128)(2,1)S(1)}, bf16[32,4224]{1,0:T(8,128)(2,1)}, u32[]{:S(2)}, u32[]{:S(2)}) %collective-permute-start.4) | collective-permute-done | bytes 270368 | tf_op jit(solution)/shard_map/ppermute | solution.py:31
  33.3 1.7 %collective-permute-done.3.got_ref = bf16[16,6144]{1,0:T(8,128)(2,1)S(1)} collective-permute-done((bf16[16,6144]{1,0:T(8,128)(2,1)S(1)}, bf16[16,6144]{1,0:T(8,128)(2,1)S(1)}, u32[]{:S(2)}, u32[]{:S(2)}) %collective-permute-start.3) | collective-permute-done | bytes 196640 | tf_op jit(solution)/shard_map/ppermute | solution.py:31
  36.7 5.8 %all-to-all-start = ((bf16[16,16,2048]{2,1,0:T(8,128)(2,1)}), bf16[16,16,2048]{2,1,0:T(8,128)(2,1)S(1)}, u32[]{:S(2)}, u32[]{:S(2)}) async-start(bf16[16,16,2048]{2,1,0:T(8,128)(2,1)} %shard_map.87), calls=%async_computation | async-start | bytes 2097152 | tf_op jit(solution)/shard_map/all_to_all | solution.py:378
  42.9 2.6 %collective-permute-start.11 = (bf16[16,4096]{1,0:T(8,128)(2,1)S(1)}, bf16[16,4096]{1,0:T(8,128)(2,1)S(1)}, u32[]{:S(2)}, u32[]{:S(2)}) collective-permute-start(bf16[16,4096]{1,0:T(8,128)(2,1)S(1)} %get-tuple-element.22._), channel_id=1, source_target_pairs={{0,8},{1,9},{2,10},{3,11},{4,12},{5,13},{6,14},{7,15},{8,0},{9,1},... | collective-permute-start | bytes 393224 | tf_op jit(solution)/shard_map/ppermute | solution.py:31
  46.1 28.6 %collective-permute-done.11.got_ref = bf16[16,4096]{1,0:T(8,128)(2,1)S(1)} collective-permute-done((bf16[16,4096]{1,0:T(8,128)(2,1)S(1)}, bf16[16,4096]{1,0:T(8,128)(2,1)S(1)}, u32[]{:S(2)}, u32[]{:S(2)}) %collective-permute-start.11) | collective-permute-done | bytes 131104 | tf_op jit(solution)/shard_map/ppermute | solution.py:31
  75.2 1.6 %collective-permute-start.12 = (bf16[16,4096]{1,0:T(8,128)(2,1)S(1)}, bf16[16,4096]{1,0:T(8,128)(2,1)S(1)}, u32[]{:S(2)}, u32[]{:S(2)}) collective-permute-start(bf16[16,4096]{1,0:T(8,128)(2,1)S(1)} %shard_map.88.refs_8_.refs_10_), channel_id=1, source_target_pairs={{0,16},{16,0},{1,17},{17,1},{2,18},{18,2},{3,19},{19,3},{4,20},{20... | collective-permute-start | bytes 393224 | tf_op jit(solution)/shard_map/ppermute | solution.py:31
  77.4 2.9 %collective-permute-done.12.refs_9_.refs_12_ = bf16[16,4096]{1,0:T(8,128)(2,1)S(1)} collective-permute-done((bf16[16,4096]{1,0:T(8,128)(2,1)S(1)}, bf16[16,4096]{1,0:T(8,128)(2,1)S(1)}, u32[]{:S(2)}, u32[]{:S(2)}) %collective-permute-start.12) | collective-permute-done | bytes 131104 | tf_op jit(solution)/shard_map/ppermute | solution.py:31
  82.2 1.1 collective-permute-done.14.refs_13_
  85.2 25.0 %shard_map.89 = (f32[2,2048,256]{2,1,0:T(8,128)S(1)}, f32[8,256]{1,0:T(8,128)S(1)}) custom-call(bf16[32,4224]{1,0:T(8,128)(2,1)S(1)} %copy-done.10, bf16[32,4224]{1,0:T(8,128)(2,1)} %collective-permute-done.4.refs_1_, bf16[32,4224]{1,0:T(8,128)(2,1)} %collective-permute-done.5.refs_2_, bf16[32,4224]{1,0:T(8,128)(2,1)} %collective-permute-done.6.refs_3_, ...), custom_call_target="tpu_custom_call" | custom-call | flops 17179869184 | bytes 16777216 | tf_op jit(solution)/shard_map/pallas_call | solution.py:262
  110.2 2.0 %copy-done = f32[2,2048,256]{2,1,0:T(8,128)} copy-done((f32[2,2048,256]{2,1,0:T(8,128)}, f32[2,2048,256]{2,1,0:T(8,128)S(1)}, u32[]{:S(2)}) %copy-start) | copy-done | bytes 4194328
  112.2 2.2 %copy-done.1 = f32[2,2048,256]{2,1,0:T(8,128)S(1)} copy-done((f32[2,2048,256]{2,1,0:T(8,128)S(1)}, f32[2,2048,256]{2,1,0:T(8,128)}, u32[]{:S(2)}) %copy-start.1) | copy-done | bytes 4194328
  114.4 2.3 %shard_map.90 = f32[2,8,1]{2,1,0:T(8,128)S(1)} custom-call(bf16[16,16,2048]{2,1,0:T(8,128)(2,1)S(1)} %all-to-all-done.grad_ref, bf16[512,2048]{1,0:T(8,128)(2,1)S(1)} %copy-done.3, f32[2,2048,256]{2,1,0:T(8,128)S(1)} %copy-done.1, f32[8,256]{1,0:T(8,128)S(1)} %get-tuple-element.26.ids_ref), custom_call_target="tpu_custom_call" | custom-call | flops 536870912 | bytes 4194304 | tf_op jit(solution)/shard_map/pallas_call | solution.py:321
  117.2 1.5 %collective-permute-start.16 = (f32[2,8]{1,0:T(2,128)S(1)}, f32[2,8]{1,0:T(2,128)S(1)}, u32[]{:S(2)}, u32[]{:S(2)}) collective-permute-start(f32[2,8]{1,0:T(2,128)S(1)} %reduce), channel_id=1, source_target_pairs={{0,2},{1,3},{2,0},{3,1},{4,6},{5,7},{6,4},{7,5},{8,10},{9,11},{10,... | collective-permute-start | bytes 200 | tf_op jit(solution)/shard_map/ppermute | solution.py:31
  118.7 2.0 %collective-permute-done.16 = f32[2,8]{1,0:T(2,128)S(1)} collective-permute-done((f32[2,8]{1,0:T(2,128)S(1)}, f32[2,8]{1,0:T(2,128)S(1)}, u32[]{:S(2)}, u32[]{:S(2)}) %collective-permute-start.16) | collective-permute-done | bytes 96 | tf_op jit(solution)/shard_map/ppermute | solution.py:31
  121.7 2.0 %collective-permute-start.19 = (f32[2,8]{1,0:T(2,128)S(1)}, f32[2,8]{1,0:T(2,128)S(1)}, u32[]{:S(2)}, u32[]{:S(2)}) collective-permute-start(f32[2,8]{1,0:T(2,128)S(1)} %add_add_fusion.1), channel_id=1, source_target_pairs={{0,8},{1,9},{2,10},{3,11},{4,12},{5,13},{6,14},{7,15},{8,0},{9,1},... | collective-permute-start | bytes 200 | tf_op jit(solution)/shard_map/ppermute | solution.py:31
  123.6 2.4 %collective-permute-start.20 = (f32[2,8]{1,0:T(2,128)S(1)}, f32[2,8]{1,0:T(2,128)S(1)}, u32[]{:S(2)}, u32[]{:S(2)}) collective-permute-start(f32[2,8]{1,0:T(2,128)S(1)} %add_add_fusion.1), channel_id=1, source_target_pairs={{0,12},{1,13},{2,14},{3,15},{4,8},{5,9},{6,10},{7,11},{8,4},{9,5},... | collective-permute-start | bytes 200 | tf_op jit(solution)/shard_map/ppermute | solution.py:31
  126.2 2.8 %collective-permute-done.20 = f32[2,8]{1,0:T(2,128)S(1)} collective-permute-done((f32[2,8]{1,0:T(2,128)S(1)}, f32[2,8]{1,0:T(2,128)S(1)}, u32[]{:S(2)}, u32[]{:S(2)}) %collective-permute-start.20) | collective-permute-done | bytes 96 | tf_op jit(solution)/shard_map/ppermute | solution.py:31
  (62 shorter events, 14.9 us)
Async XLA Ops:
  1.8 33.8 %copy-start.4 = (bf16[16,32768]{1,0:T(8,128)(2,1)S(1)}, bf16[16,32768]{1,0:T(8,128)(2,1)}, u32[]{:S(2)}) copy-start(bf16[16,32768]{1,0:T(8,128)(2,1)} %grad_ref.1) | copy-start | bytes 3145732
  1.8 2.1 %collective-permute-start = (bf16[16,18432]{1,0:T(8,128)(2,1)S(1)}, bf16[16,18432]{1,0:T(8,128)(2,1)S(1)}, u32[]{:S(2)}, u32[]{:S(2)}) collective-permute-start(bf16[16,18432]{1,0:T(8,128)(2,1)S(1)} %get-tuple-element.17._), channel_id=1, source_target_pairs={{0,1},{1,0},{2,3},{3,2},{4,5},{5,4},{6,7},{7,6},{8,9},{9,8},{10,11... | collective-permute-start | bytes 1769480 | tf_op jit(solution)/shard_map/ppermute | solution.py:31
  5.2 16.5 %collective-permute-start.1 = (bf16[16,10240]{1,0:T(8,128)(2,1)S(1)}, bf16[16,10240]{1,0:T(8,128)(2,1)S(1)}, u32[]{:S(2)}, u32[]{:S(2)}) collective-permute-start(bf16[16,10240]{1,0:T(8,128)(2,1)S(1)} %get-tuple-element.19), channel_id=1, source_target_pairs={{0,2},{1,3},{2,0},{3,1},{4,6},{5,7},{6,4},{7,5},{8,10},{9,11},{10,... | collective-permute-start | bytes 983048 | tf_op jit(solution)/shard_map/ppermute | solution.py:31
  12.3 9.4 %collective-permute-start.2 = (bf16[16,4224]{1,0:T(8,128)(2,1)}, bf16[16,4224]{1,0:T(8,128)(2,1)S(1)}, u32[]{:S(2)}, u32[]{:S(2)}) collective-permute-start(bf16[16,4224]{1,0:T(8,128)(2,1)} %shard_map.84.refs_0_), channel_id=1, source_target_pairs={{0,8},{1,9},{2,10},{3,11},{4,12},{5,13},{6,14},{7,15},{8,0},{9,1},... | collective-permute-start | bytes 405512 | tf_op jit(solution)/shard_map/ppermute | solution.py:31
  23.2 58.9 %copy-start.9 = (bf16[32,4224]{1,0:T(8,128)(2,1)}, bf16[32,4224]{1,0:T(8,128)(2,1)S(1)}, u32[]{:S(2)}) copy-start(bf16[32,4224]{1,0:T(8,128)(2,1)S(1)} %get-tuple-element.23.refs_0_) | copy-start | bytes 811012
  23.2 9.6 %collective-permute-start.4 = (bf16[32,4224]{1,0:T(8,128)(2,1)S(1)}, bf16[32,4224]{1,0:T(8,128)(2,1)}, u32[]{:S(2)}, u32[]{:S(2)}) collective-permute-start(bf16[32,4224]{1,0:T(8,128)(2,1)S(1)} %get-tuple-element.23.refs_0_), channel_id=1, source_target_pairs={{0,4},{1,5},{2,6},{3,7},{4,0},{5,1},{6,2},{7,3},{8,12},{9,13},{10,... | collective-permute-start | bytes 811016 | tf_op jit(solution)/shard_map/ppermute | solution.py:31
  24.1 10.9 %collective-permute-start.3 = (bf16[16,6144]{1,0:T(8,128)(2,1)S(1)}, bf16[16,6144]{1,0:T(8,128)(2,1)S(1)}, u32[]{:S(2)}, u32[]{:S(2)}) collective-permute-start(bf16[16,6144]{1,0:T(8,128)(2,1)S(1)} %get-tuple-element.21), channel_id=1, source_target_pairs={{0,4},{1,5},{2,6},{3,7},{4,0},{5,1},{6,2},{7,3},{8,12},{9,13},{10,... | collective-permute-start | bytes 589832 | tf_op jit(solution)/shard_map/ppermute | solution.py:31
  25.3 20.2 %collective-permute-start.5 = (bf16[32,4224]{1,0:T(8,128)(2,1)S(1)}, bf16[32,4224]{1,0:T(8,128)(2,1)}, u32[]{:S(2)}, u32[]{:S(2)}) collective-permute-start(bf16[32,4224]{1,0:T(8,128)(2,1)S(1)} %get-tuple-element.23.refs_0_), channel_id=1, source_target_pairs={{0,2},{1,3},{2,0},{3,1},{4,6},{5,7},{6,4},{7,5},{8,10},{9,11},{10,... | collective-permute-start | bytes 811016 | tf_op jit(solution)/shard_map/ppermute | solution.py:31
  32.8 13.2 %collective-permute-start.6 = (bf16[32,4224]{1,0:T(8,128)(2,1)}, bf16[32,4224]{1,0:T(8,128)(2,1)}, u32[]{:S(2)}, u32[]{:S(2)}) collective-permute-start(bf16[32,4224]{1,0:T(8,128)(2,1)} %collective-permute-done.4.refs_1_), channel_id=1, source_target_pairs={{0,2},{1,3},{2,0},{3,1},{4,6},{5,7},{6,4},{7,5},{8,10},{9,11},{10,... | collective-permute-start | bytes 811016 | tf_op jit(solution)/shard_map/ppermute | solution.py:31
  36.7 75.5 %all-to-all-start = ((bf16[16,16,2048]{2,1,0:T(8,128)(2,1)}), bf16[16,16,2048]{2,1,0:T(8,128)(2,1)S(1)}, u32[]{:S(2)}, u32[]{:S(2)}) async-start(bf16[16,16,2048]{2,1,0:T(8,128)(2,1)} %shard_map.87), calls=%async_computation | async-start | bytes 2097152 | tf_op jit(solution)/shard_map/all_to_all | solution.py:378
  42.5 38.5 %collective-permute-start.7 = (bf16[32,4224]{1,0:T(8,128)(2,1)S(1)}, bf16[32,4224]{1,0:T(8,128)(2,1)S(1)}, u32[]{:S(2)}, u32[]{:S(2)}) collective-permute-start(bf16[32,4224]{1,0:T(8,128)(2,1)S(1)} %get-tuple-element.23.refs_0_), channel_id=1, source_target_pairs={{0,1},{1,0},{2,3},{3,2},{4,5},{5,4},{6,7},{7,6},{8,9},{9,8},{10,11... | collective-permute-start | bytes 811016 | tf_op jit(solution)/shard_map/ppermute | solution.py:31
  42.9 31.8 %collective-permute-start.11 = (bf16[16,4096]{1,0:T(8,128)(2,1)S(1)}, bf16[16,4096]{1,0:T(8,128)(2,1)S(1)}, u32[]{:S(2)}, u32[]{:S(2)}) collective-permute-start(bf16[16,4096]{1,0:T(8,128)(2,1)S(1)} %get-tuple-element.22._), channel_id=1, source_target_pairs={{0,8},{1,9},{2,10},{3,11},{4,12},{5,13},{6,14},{7,15},{8,0},{9,1},... | collective-permute-start | bytes 393224 | tf_op jit(solution)/shard_map/ppermute | solution.py:31
  45.5 37.8 %collective-permute-start.8 = (bf16[32,4224]{1,0:T(8,128)(2,1)}, bf16[32,4224]{1,0:T(8,128)(2,1)}, u32[]{:S(2)}, u32[]{:S(2)}) collective-permute-start(bf16[32,4224]{1,0:T(8,128)(2,1)} %collective-permute-done.4.refs_1_), channel_id=1, source_target_pairs={{0,1},{1,0},{2,3},{3,2},{4,5},{5,4},{6,7},{7,6},{8,9},{9,8},{10,11... | collective-permute-start | bytes 811016 | tf_op jit(solution)/shard_map/ppermute | solution.py:31
  45.6 37.8 %collective-permute-start.9 = (bf16[32,4224]{1,0:T(8,128)(2,1)}, bf16[32,4224]{1,0:T(8,128)(2,1)}, u32[]{:S(2)}, u32[]{:S(2)}) collective-permute-start(bf16[32,4224]{1,0:T(8,128)(2,1)} %collective-permute-done.5.refs_2_), channel_id=1, source_target_pairs={{0,1},{1,0},{2,3},{3,2},{4,5},{5,4},{6,7},{7,6},{8,9},{9,8},{10,11... | collective-permute-start | bytes 811016 | tf_op jit(solution)/shard_map/ppermute | solution.py:31
  46.0 37.3 %collective-permute-start.10 = (bf16[32,4224]{1,0:T(8,128)(2,1)}, bf16[32,4224]{1,0:T(8,128)(2,1)}, u32[]{:S(2)}, u32[]{:S(2)}) collective-permute-start(bf16[32,4224]{1,0:T(8,128)(2,1)} %collective-permute-done.6.refs_3_), channel_id=1, source_target_pairs={{0,1},{1,0},{2,3},{3,2},{4,5},{5,4},{6,7},{7,6},{8,9},{9,8},{10,11... | collective-permute-start | bytes 811016 | tf_op jit(solution)/shard_map/ppermute | solution.py:31
  75.2 5.1 %collective-permute-start.12 = (bf16[16,4096]{1,0:T(8,128)(2,1)S(1)}, bf16[16,4096]{1,0:T(8,128)(2,1)S(1)}, u32[]{:S(2)}, u32[]{:S(2)}) collective-permute-start(bf16[16,4096]{1,0:T(8,128)(2,1)S(1)} %shard_map.88.refs_8_.refs_10_), channel_id=1, source_target_pairs={{0,16},{16,0},{1,17},{17,1},{2,18},{18,2},{3,19},{19,3},{4,20},{20... | collective-permute-start | bytes 393224 | tf_op jit(solution)/shard_map/ppermute | solution.py:31
  80.3 1.9 %collective-permute-start.13 = (bf16[16,2048]{1,0:T(8,128)(2,1)}, bf16[16,2048]{1,0:T(8,128)(2,1)S(1)}, u32[]{:S(2)}, u32[]{:S(2)}) collective-permute-start(bf16[16,2048]{1,0:T(8,128)(2,1)} %slice.16), channel_id=1, source_target_pairs={{0,1},{1,0},{2,3},{3,2},{4,5},{5,4},{6,7},{7,6},{8,9},{9,8},{10,11... | collective-permute-start | bytes 196616 | tf_op jit(solution)/shard_map/ppermute | solution.py:31
  81.7 1.6 %collective-permute-start.14 = (bf16[16,2048]{1,0:T(8,128)(2,1)}, bf16[16,2048]{1,0:T(8,128)(2,1)S(1)}, u32[]{:S(2)}, u32[]{:S(2)}) collective-permute-start(bf16[16,2048]{1,0:T(8,128)(2,1)} %slice.17), channel_id=1, source_target_pairs={{0,1},{1,0},{2,3},{3,2},{4,5},{5,4},{6,7},{7,6},{8,9},{9,8},{10,11... | collective-permute-start | bytes 196616 | tf_op jit(solution)/shard_map/ppermute | solution.py:31
  116.8 1.9 %collective-permute-start.15 = (f32[2,8]{1,0:T(2,128)S(1)}, f32[2,8]{1,0:T(2,128)S(1)}, u32[]{:S(2)}, u32[]{:S(2)}) collective-permute-start(f32[2,8]{1,0:T(2,128)S(1)} %reduce), channel_id=1, source_target_pairs={{0,1},{1,0},{2,3},{3,2},{4,5},{5,4},{6,7},{7,6},{8,9},{9,8},{10,11... | collective-permute-start | bytes 200 | tf_op jit(solution)/shard_map/ppermute | solution.py:31
  117.2 3.6 %collective-permute-start.16 = (f32[2,8]{1,0:T(2,128)S(1)}, f32[2,8]{1,0:T(2,128)S(1)}, u32[]{:S(2)}, u32[]{:S(2)}) collective-permute-start(f32[2,8]{1,0:T(2,128)S(1)} %reduce), channel_id=1, source_target_pairs={{0,2},{1,3},{2,0},{3,1},{4,6},{5,7},{6,4},{7,5},{8,10},{9,11},{10,... | collective-permute-start | bytes 200 | tf_op jit(solution)/shard_map/ppermute | solution.py:31
  118.6 3.0 %collective-permute-start.17 = (f32[2,8]{1,0:T(2,128)S(1)}, f32[2,8]{1,0:T(2,128)S(1)}, u32[]{:S(2)}, u32[]{:S(2)}) collective-permute-start(f32[2,8]{1,0:T(2,128)S(1)} %reduce), channel_id=1, source_target_pairs={{0,3},{1,2},{2,1},{3,0},{4,7},{5,6},{6,5},{7,4},{8,11},{9,10},{10,... | collective-permute-start | bytes 200 | tf_op jit(solution)/shard_map/ppermute | solution.py:31
  121.6 4.4 %collective-permute-start.18 = (f32[2,8]{1,0:T(2,128)S(1)}, f32[2,8]{1,0:T(2,128)S(1)}, u32[]{:S(2)}, u32[]{:S(2)}) collective-permute-start(f32[2,8]{1,0:T(2,128)S(1)} %add_add_fusion.1), channel_id=1, source_target_pairs={{0,4},{1,5},{2,6},{3,7},{4,0},{5,1},{6,2},{7,3},{8,12},{9,13},{10,... | collective-permute-start | bytes 200 | tf_op jit(solution)/shard_map/ppermute | solution.py:31
  121.7 4.5 %collective-permute-start.19 = (f32[2,8]{1,0:T(2,128)S(1)}, f32[2,8]{1,0:T(2,128)S(1)}, u32[]{:S(2)}, u32[]{:S(2)}) collective-permute-start(f32[2,8]{1,0:T(2,128)S(1)} %add_add_fusion.1), channel_id=1, source_target_pairs={{0,8},{1,9},{2,10},{3,11},{4,12},{5,13},{6,14},{7,15},{8,0},{9,1},... | collective-permute-start | bytes 200 | tf_op jit(solution)/shard_map/ppermute | solution.py:31
  123.6 5.4 %collective-permute-start.20 = (f32[2,8]{1,0:T(2,128)S(1)}, f32[2,8]{1,0:T(2,128)S(1)}, u32[]{:S(2)}, u32[]{:S(2)}) collective-permute-start(f32[2,8]{1,0:T(2,128)S(1)} %add_add_fusion.1), channel_id=1, source_target_pairs={{0,12},{1,13},{2,14},{3,15},{4,8},{5,9},{6,10},{7,11},{8,4},{9,5},... | collective-permute-start | bytes 200 | tf_op jit(solution)/shard_map/ppermute | solution.py:31
  (11 other events, 66.5 us)

commit v5 on v4

--- a/solution.py
+++ b/solution.py
@@ -69,17 +69,18 @@
     )(factors)
 
 
-def pick_kernel(bit, cols, batch_count, parts, join, owners_ref, keep_ref, got_ref, *refs):
+def pick_kernel(bit, cols, batch_count, last, join, owners_ref, keep_ref, got_ref, *refs):
     me, batch = lax.axis_index("wide"), lax.rem(lax.axis_index("groups"), batch_count)
     join_refs, out_refs = refs[:join], refs[join:]
     same = ((owners_ref[batch] ^ me) & bit) == 0
     count = (keep_ref.shape[1] - out_refs[0].shape[1]) // cols
 
     def fill(ref):
-        if parts == 1:
-            out_refs[0][...] = ref[...]
+        if last:
+            out_refs[0][...] = ref[:, :cols]
+            out_refs[1][...] = ref[:, cols:]
         else:
-            for part in range(parts):
+            for part in range(2):
                 out_ref = out_refs[part]
                 out_ref[:, :count * cols] = ref[:, part * count * cols:(part + 1) * count * cols]
                 out_ref[:, count * cols:] = ref[:, 2 * count * cols:]
@@ -101,16 +102,16 @@
 def pick(owners, keep, got, bit, cols, count, join=()):
     rows, width = keep.shape
     if count > 1:
-        out = [jax.ShapeDtypeStruct((rows, width - count // 2 * cols), keep.dtype)] * 2
+        widths = [width - count // 2 * cols] * 2
     else:
-        out = [jax.ShapeDtypeStruct((rows, width), keep.dtype)]
-    parts = len(out)
+        widths = [cols, width - cols]
+    out = [jax.ShapeDtypeStruct((rows, w), keep.dtype) for w in widths]
     if join:
         out.append(jax.ShapeDtypeStruct(
             (sum(x.shape[0] for x in join), join[0].shape[1]), join[0].dtype
         ))
     return pl.pallas_call(
-        functools.partial(pick_kernel, bit, cols, owners.shape[0], parts, len(join)),
+        functools.partial(pick_kernel, bit, cols, owners.shape[0], count == 1, len(join)),
         in_specs=in_smem(1) + in_vmem(2 + len(join)),
         out_specs=in_vmem(len(out)),
         out_shape=out,
@@ -137,54 +138,63 @@
     )(grads, after)
 
 
-def rotate_kernel(ids_ref, act_ref, basis_ref, _, out_ref, held_ref, sems):
+def label_kernel(ids_ref, act_ref, out_ref):
     rows, width = act_ref.shape
-    depth = basis_ref.shape[0]
-    copies = []
-    for k in range(width // depth):
-        cols = slice(k * depth, (k + 1) * depth)
-        copy = pltpu.make_async_copy(basis_ref.at[:, cols], held_ref.at[k], sems.at[k])
-        copy.start()
-        copies.append(copy)
     row = lax.broadcasted_iota(jnp.int32, (rows, LANES), 0)
     ids = jnp.zeros((rows, LANES), jnp.int32)
     for t in range(rows):
         ids = jnp.where(row == t, ids_ref[t], ids)
+    out_ref[:, :width] = act_ref[...]
     out_ref[:, width:] = ids.astype(jnp.float32).astype(jnp.bfloat16)
-    for k, copy in enumerate(copies):
-        cols = slice(k * depth, (k + 1) * depth)
-        copy.wait()
-        out_ref[:, cols] = jnp.dot(
-            act_ref[:, cols], held_ref[k], preferred_element_type=jnp.float32
-        ).astype(jnp.bfloat16)
-
-
-def rotate(ids, act, basis, after):
+
+
+def label(ids, act):
     rows, width = act.shape
-    depth = basis.shape[0]
-    return pl.pallas_call(
-        rotate_kernel,
-        in_specs=in_smem(1) + in_vmem(1) + in_place(2),
+    return pl.pallas_call(
+        label_kernel,
+        in_specs=in_smem(1) + in_vmem(1),
         out_specs=in_vmem(1)[0],
         out_shape=jax.ShapeDtypeStruct((rows, width + LANES), act.dtype),
-        scratch_shapes=[
-            pltpu.VMEM((width // depth, depth, depth), jnp.bfloat16),
-            pltpu.SemaphoreType.DMA((width // depth,)),
+        compiler_params=params(16),
+        cost_estimate=pl.CostEstimate(flops=0, bytes_accessed=act.size, transcendentals=0),
+    )(ids, act)
+
+
+def rotate_kernel(order, *refs):
+    act_refs, (basis_ref, out_ref, ids_ref) = refs[:-3], refs[-3:]
+    act_refs = [act_refs[n].at[at:at + size, :] for n, at, size in order]
+    depth, width = basis_ref.shape
+    for k in range(width // depth):
+        cols = slice(k * depth, (k + 1) * depth)
+        act = jnp.concatenate([ref[:, cols] for ref in act_refs], axis=0)
+        out_ref[:, cols] = jnp.dot(
+            act, basis_ref[:, cols], preferred_element_type=jnp.float32
+        ).astype(jnp.bfloat16)
+    ids = jnp.concatenate([ref[:, width:] for ref in act_refs], axis=0)
+    ids_ref[...] = ids.astype(jnp.float32)
+
+
+def rotate(act_pieces, order, basis):
+    tokens = sum(x.shape[0] for x in act_pieces)
+    width = basis.shape[1]
+    return pl.pallas_call(
+        functools.partial(rotate_kernel, order),
+        in_specs=in_vmem(len(act_pieces) + 1),
+        out_specs=in_vmem(2),
+        out_shape=[
+            jax.ShapeDtypeStruct((tokens, width), jnp.bfloat16),
+            jax.ShapeDtypeStruct((tokens, LANES), jnp.float32),
         ],
-        compiler_params=params(55),
+        compiler_params=params(20 if tokens <= 256 else 40),
         cost_estimate=pl.CostEstimate(
-            flops=2 * rows * width * basis.shape[0], bytes_accessed=basis.size, transcendentals=0
+            flops=2 * tokens * width * basis.shape[0], bytes_accessed=basis.size, transcendentals=0
         ),
-    )(ids, act, basis, after)
-
-
-def image_kernel(order, count, batch_count, *refs):
-    act_refs = refs[:count]
-    left_refs = refs[count:count + batch_count]
-    half_refs = refs[count + batch_count:count + 3 * batch_count]
-    eig_ref, out_ref, ids_ref = refs[count + 3 * batch_count:count + 3 + 3 * batch_count]
-    rot_ref, right_ref, turn_ref, pre_a, pre_b = refs[count + 3 + 3 * batch_count:]
-    act_refs = [act_refs[n].at[at:at + size, :] for n, at, size in order]
+    )(*act_pieces, basis)
+
+
+def image_kernel(batch_count, rot_ref, *refs):
+    left_refs, half_refs = refs[:batch_count], refs[batch_count:3 * batch_count]
+    eig_ref, out_ref, right_ref, turn_ref, pre_a, pre_b = refs[3 * batch_count:]
     rows, width = eig_ref.shape
     half = pre_a.shape[0] // batch_count
     chunk = pre_a.shape[1]
@@ -194,17 +204,11 @@
 
     @pl.when(pl.program_id(0) == 0)
     def _():
-        for k in range(width // chunk):
-            cols = slice(k * chunk, (k + 1) * chunk)
-            rot_ref[cols, :] = jnp.concatenate([ref[:, cols] for ref in act_refs], axis=0).T
-        ids = jnp.concatenate([ref[:, width:] for ref in act_refs], axis=0)
-        ids_ref[...] = ids.astype(jnp.float32).T[:ids_ref.shape[0], :]
         side = width // 2
         for b in range(batch_count):
             for other in range(2):
                 at = pl.multiple_of(((lax.axis_index("wide") & 1) ^ other) * side, side)
-                ref = half_refs[2 * b + other]
-                right_ref[b, :, pl.ds(at, side)] = ref[:, ref.shape[1] - side:]
+                right_ref[b, :, pl.ds(at, side)] = half_refs[2 * b + other][...]
 
     for b in range(batch_count):
         turn_ref[b] = left_refs[b][...].T
@@ -229,10 +233,12 @@
 
     def absorb(k, pre):
         row, col = place(k)
-        rot = rot_ref[pl.ds(pl.multiple_of(col, chunk), chunk), :]
-        more = jnp.dot(pre[...], rot, preferred_element_type=jnp.float32)
+        rot = rot_ref[:, pl.ds(pl.multiple_of(col, chunk), chunk)]
+        more = lax.dot_general(
+            rot, pre[...], (((1,), (1,)), ((), ())), preferred_element_type=jnp.float32
+        )
         for b in range(batch_count):
-            out_ref[b, pl.ds(row, half), :] += more[b * half:(b + 1) * half, :]
+            out_ref[b, :, pl.ds(row, half)] += more[:, b * half:(b + 1) * half]
 
     def both(k, pre_now, pre_next):
         absorb(k, pre_now)
@@ -252,30 +258,22 @@
     absorb(phases - 1, pre_b)
 
 
-def images(act_pieces, order, lefts, halves, eigenvalues):
-    count, batch_count = len(act_pieces), len(lefts)
-    tokens = sum(x.shape[0] for x in act_pieces)
+def images(rot, lefts, halves, eigenvalues):
+    batch_count, tokens = len(lefts), rot.shape[0]
     hidden, width = eigenvalues.shape
     rows = min(512, hidden)
     half = min(256, rows)
     chunk = min(1024, width // 2)
     return pl.pallas_call(
-        functools.partial(image_kernel, order, count, batch_count),
+        functools.partial(image_kernel, batch_count),
         grid=(hidden // rows,),
-        in_specs=[whole_block(x.shape) for x in act_pieces]
+        in_specs=[whole_block(rot.shape)]
         + [pl.BlockSpec((QT, rows), lambda i: (0, i)) for x in lefts]
         + [whole_block(x.shape) for x in halves]
         + [pl.BlockSpec((rows, width), lambda i: (i, 0))],
-        out_specs=[
-            pl.BlockSpec((batch_count, rows, tokens), lambda i: (0, i, 0)),
-            pl.BlockSpec((8, tokens), lambda i: (0, 0)),
-        ],
-        out_shape=[
-            jax.ShapeDtypeStruct((batch_count, hidden, tokens), jnp.float32),
-            jax.ShapeDtypeStruct((8, tokens), jnp.float32),
-        ],
+        out_specs=pl.BlockSpec((batch_count, tokens, rows), lambda i: (0, 0, i)),
+        out_shape=jax.ShapeDtypeStruct((batch_count, tokens, hidden), jnp.float32),
         scratch_shapes=[
-            pltpu.VMEM((width, tokens), jnp.bfloat16),
             pltpu.VMEM((batch_count, QT, width), jnp.bfloat16),
             pltpu.VMEM((batch_count, rows, QT), jnp.bfloat16),
             pltpu.VMEM((batch_count * half, chunk), jnp.bfloat16),
@@ -287,10 +285,10 @@
             bytes_accessed=2 * hidden * width,
             transcendentals=0,
         ),
-    )(*act_pieces, *lefts, *halves, eigenvalues)
-
-
-def score_kernel(batch_count, seq_count, grad_ref, basis_ref, image_ref, ids_ref, out_ref, token_ref):
+    )(rot, *lefts, *halves, eigenvalues)
+
+
+def score_kernel(batch_count, grad_ref, basis_ref, image_ref, ids_ref, out_ref, token_ref):
     step = pl.program_id(0)
     me = lax.axis_index("wide")
 
@@ -300,36 +298,35 @@
 
     grads = jnp.concatenate([grad_ref[me ^ r] for r in range(grad_ref.shape[0])], axis=0)
     turned = jnp.dot(grads, basis_ref[...], preferred_element_type=jnp.float32)
-    turned = turned.astype(jnp.bfloat16).T.astype(jnp.float32)
+    turned = turned.astype(jnp.bfloat16).astype(jnp.float32)
     for b in range(batch_count):
-        token_ref[b:b + 1, :] += jnp.sum(image_ref[b] * turned, axis=0, keepdims=True)
+        token_ref[b] += jnp.sum(image_ref[b] * turned, axis=1, keepdims=True)
 
     @pl.when(step == pl.num_programs(0) - 1)
     def _():
-        tokens = token_ref.shape[1]
-        seqs = lax.broadcasted_iota(jnp.int32, (seq_count, tokens), 0).astype(jnp.float32)
-        member = ids_ref[0:1, :] == seqs
+        seqs = lax.broadcasted_iota(jnp.int32, ids_ref.shape, 1).astype(jnp.float32)
+        member = ids_ref[...] == seqs
         for b in range(batch_count):
-            out_ref[b] = jnp.sum(jnp.where(member, token_ref[b:b + 1, :], 0.0), axis=1, keepdims=True)
+            sums = jnp.sum(jnp.where(member, token_ref[b], 0.0), axis=0, keepdims=True)
+            out_ref[b:b + 1, :] = sums[:, :out_ref.shape[1]]
 
 
 def score_parts(grads, grad_basis, image, ids, seq_count):
-    batch_count = image.shape[0]
+    batch_count, tokens = image.shape[:2]
     count, rows, hidden = grads.shape
     inner = min(grad_basis.shape[0], hidden)
-    tokens = count * rows
-    return pl.pallas_call(
-        functools.partial(score_kernel, batch_count, seq_count),
+    return pl.pallas_call(
+        functools.partial(score_kernel, batch_count),
         grid=(hidden // inner,),
         in_specs=[
             pl.BlockSpec((count, rows, inner), lambda i: (0, 0, i)),
             pl.BlockSpec((grad_basis.shape[0], inner), lambda i: (0, i)),
-            pl.BlockSpec((batch_count, inner, tokens), lambda i: (0, i, 0)),
+            pl.BlockSpec((batch_count, tokens, inner), lambda i: (0, 0, i)),
             pl.BlockSpec(ids.shape, lambda i: (0, 0)),
         ],
-        out_specs=pl.BlockSpec((batch_count, seq_count, 1), lambda i: (0, 0, 0)),
-        out_shape=jax.ShapeDtypeStruct((batch_count, seq_count, 1), jnp.float32),
-        scratch_shapes=[pltpu.VMEM((8, tokens), jnp.float32)],
+        out_specs=pl.BlockSpec((batch_count, seq_count), lambda i: (0, 0)),
+        out_shape=jax.ShapeDtypeStruct((batch_count, seq_count), jnp.float32),
+        scratch_shapes=[pltpu.VMEM((batch_count, tokens, 1), jnp.float32)],
         compiler_params=params(16 if tokens <= 256 else 40),
         cost_estimate=pl.CostEstimate(
             flops=2 * tokens * hidden * grad_basis.shape[0],
@@ -357,43 +354,40 @@
     for bit in reversed(bits):
         order = order + [r + bit for r in order]
     order = sorted(order, key=lambda r: [r & bit for bit in bits])
+    joined, ranks = label(seq_ids, train_act), [0]
+    far = bits[:1:-1]
     keep, give = cut_factors(query_factors, order, hidden, batch_count)
-    rot = rotate(seq_ids, train_act, act_basis, give)
-    joined, ranks = rot, [0]
-    far = bits[:1:-1]
     count = wide_count // 2
     for step, bit in enumerate(bits):
+        join = ()
+        if step < len(far):
+            join = (joined, swap(joined, "wide", far[step]))
+            ranks = ranks + [r + far[step] for r in ranks]
         got = swap(give, "wide", bit)
-        join = ()
-        if 1 <= step < len(far):
-            join = (joined, swap(joined, "wide", far[step - 1]))
-            ranks = ranks + [r + far[step - 1] for r in ranks]
         picked = list(pick(owners, keep, got, bit, cols, count, join))
         if join:
             joined = picked.pop()
-        keep, give = picked[0], picked[-1]
+        keep, give = picked
         count //= 2
-        if step == len(bits) - 2:
-            sent = cut_grads(train_grad, give, wide_count)
-            grads = lax.all_to_all(sent, "wide", 0, 0)
-    held = keep
+    left, right = keep, give
     acts = [(joined, ranks)]
-    for bit in (far[-1], 2, 1):
+    for bit in (2, 1):
         acts += [(swap(x, "wide", bit), [r + bit for r in has]) for x, has in acts]
     token_order = [None] * wide_count
     for n, (_, has) in enumerate(acts):
         for at, r in enumerate(has):
             token_order[r] = (n, at * tok_local, tok_local)
-    acts = [x for x, _ in acts]
-
-    other = swap(held, "groups", 1)
-    lefts = [held, other]
+    rot, ids = rotate([x for x, _ in acts], token_order, act_basis)
+
+    lefts = [left, swap(left, "groups", 1)]
     halves = []
-    for x in (held, other):
-        halves += [x, swap(x[:, cols:], "wide", 1)]
-
-    image, ids = images(acts, token_order, lefts, halves, eigenvalues)
-    parts = score_parts(grads, grad_basis, image, ids, seq_count)[:, :, 0]
+    for x in (right, swap(right, "groups", 1)):
+        halves += [x, swap(x, "wide", 1)]
+
+    grads = lax.all_to_all(cut_grads(train_grad, right, wide_count), "wide", 0, 0)
+
+    image = images(rot, lefts, halves, eigenvalues)
+    parts = score_parts(grads, grad_basis, image, ids, seq_count)
     for near in (bits[:2], bits[2:]):
         step = near[0]
         others = [swap(parts, "wide", step * n) for n in range(1, 1 << len(near))]

time: 130 us -> 112 us (0.86)
  waiting for transfers between devices: 55.7 us -> 41.9 us
  Pallas kernels: 35 us -> 32 us
    ppermute x21 -> x19, waiting for transfers between devices: 55.7 us -> 41.9 us  [swap(): return lax.ppermute(x, axis, [(i, i ^ bit) for i in range(count)])]
    pallas_call x3 -> x4, Pallas kernels: 31.5 us -> 28.4 us  [the longest x1 24.3 us: images(): pl.pallas_call(functools.partial(image_kernel, batch_count), grid=(hidden...]
    unnamed x26 -> x20, local copies, waits for them, and re-layouts: 10 us -> 10.9 us
    ppermute x21 -> x19, starting transfers between devices: 21 us -> 21 us  [swap(): return lax.ppermute(x, axis, [(i, i ^ bit) for i in range(count)])]
  transfers between devices with their start and end apart: 22 -> 20, of which waited for: 11 -> 10; matrix products, arithmetic and copies ran while one was open for 1% -> 0% of each run, Pallas kernels for 24% -> 25%
where the time goes in v5:
time: 112 us
  waiting for transfers between devices  41.9 us (37%)
  Pallas kernels  32 us (29%)
  starting transfers between devices  25.9 us (23%)
  local copies, waits for them, and re-layouts  10.9 us (10%)
    ppermute x19, waiting for transfers between devices, swap(): return lax.ppermute(x, axis, [(i, i ^ bit) for i in range(count)])  41.9 us
    pallas_call x1, Pallas kernels, images(): pl.pallas_call(functools.partial(image_kernel, batch_count), grid=(hidden...  24.3 us
    ppermute x19, starting transfers between devices, swap(): return lax.ppermute(x, axis, [(i, i ^ bit) for i in range(count)])  21 us
    unnamed x20, local copies, waits for them, and re-layouts  10.9 us
    all_to_all x1, starting transfers between devices, per_device(): lax.all_to_all(cut_grads(train_grad, right, wide_count), 'wide', 0, 0)  4.92 us
    pallas_call x4, Pallas kernels, pick(): pl.pallas_call(functools.partial(pick_kernel, bit, cols, owners.shape[0],...  2.4 us
    pallas_call x1, Pallas kernels, score_parts(): pl.pallas_call(functools.partial(score_kernel, batch_count), grid=(hidden...  2.35 us
  transfers between devices with their start and end apart: 20, of which 10 were waited for; matrix products, arithmetic and copies ran while one was open for 0% of the time, Pallas kernels for 25%

profile of v5, /device:TPU:0, one launch (start us, length us, event | category | flops | bytes accessed | tf_op | source)
XLA Modules:
  0.0 111.5 jit_solution(12765830516345581898)
XLA Ops:
  0.0 1.7 %copy-done.3 = bf16[2,16,36864]{2,1,0:T(8,128)(2,1)S(1)} copy-done((bf16[2,16,36864]{2,1,0:T(8,128)(2,1)S(1)}, bf16[2,16,36864]{2,1,0:T(8,128)(2,1)}, u32[]{:S(2)}) %copy-start.3) | copy-done | bytes 2359320
  4.4 3.7 %collective-permute-start.1 = (bf16[16,4224]{1,0:T(8,128)(2,1)S(1)}, bf16[16,4224]{1,0:T(8,128)(2,1)S(1)}, u32[]{:S(2)}, u32[]{:S(2)}) collective-permute-start(bf16[16,4224]{1,0:T(8,128)(2,1)S(1)} %shard_map.83.refs_0_), channel_id=1, source_target_pairs={{0,8},{1,9},{2,10},{3,11},{4,12},{5,13},{6,14},{7,15},{8,0},{9,1},... | collective-permute-start | bytes 405512 | tf_op jit(solution)/shard_map/ppermute | solution.py:31
  8.1 7.1 %collective-permute-done.1.refs_1_ = bf16[16,4224]{1,0:T(8,128)(2,1)S(1)} collective-permute-done((bf16[16,4224]{1,0:T(8,128)(2,1)S(1)}, bf16[16,4224]{1,0:T(8,128)(2,1)S(1)}, u32[]{:S(2)}, u32[]{:S(2)}) %collective-permute-start.1) | collective-permute-done | bytes 135200 | tf_op jit(solution)/shard_map/ppermute | solution.py:31
  16.5 1.7 %collective-permute-start.2 = (bf16[16,10240]{1,0:T(8,128)(2,1)S(1)}, bf16[16,10240]{1,0:T(8,128)(2,1)S(1)}, u32[]{:S(2)}, u32[]{:S(2)}) collective-permute-start(bf16[16,10240]{1,0:T(8,128)(2,1)S(1)} %get-tuple-element.22), channel_id=1, source_target_pairs={{0,2},{1,3},{2,0},{3,1},{4,6},{5,7},{6,4},{7,5},{8,10},{9,11},{10,... | collective-permute-start | bytes 983048 | tf_op jit(solution)/shard_map/ppermute | solution.py:31
  18.8 7.1 %collective-permute-done.3.refs_1_ = bf16[32,4224]{1,0:T(8,128)(2,1)S(1)} collective-permute-done((bf16[32,4224]{1,0:T(8,128)(2,1)S(1)}, bf16[32,4224]{1,0:T(8,128)(2,1)S(1)}, u32[]{:S(2)}, u32[]{:S(2)}) %collective-permute-start.3) | collective-permute-done | bytes 270368 | tf_op jit(solution)/shard_map/ppermute | solution.py:31
  27.3 1.5 %collective-permute-start.6 = (bf16[64,4224]{1,0:T(8,128)(2,1)S(1)}, bf16[64,4224]{1,0:T(8,128)(2,1)S(1)}, u32[]{:S(2)}, u32[]{:S(2)}) collective-permute-start(bf16[64,4224]{1,0:T(8,128)(2,1)S(1)} %get-tuple-element.29.refs_0_), channel_id=1, source_target_pairs={{0,2},{1,3},{2,0},{3,1},{4,6},{5,7},{6,4},{7,5},{8,10},{9,11},{10,... | collective-permute-start | bytes 1622024 | tf_op jit(solution)/shard_map/ppermute | solution.py:31
  29.9 10.6 %collective-permute-done.6.refs_1_ = bf16[64,4224]{1,0:T(8,128)(2,1)S(1)} collective-permute-done((bf16[64,4224]{1,0:T(8,128)(2,1)S(1)}, bf16[64,4224]{1,0:T(8,128)(2,1)S(1)}, u32[]{:S(2)}, u32[]{:S(2)}) %collective-permute-start.6) | collective-permute-done | bytes 540704 | tf_op jit(solution)/shard_map/ppermute | solution.py:31
  41.1 3.0 %collective-permute-start.5 = (bf16[16,4096]{1,0:T(8,128)(2,1)S(1)}, bf16[16,4096]{1,0:T(8,128)(2,1)S(1)}, u32[]{:S(2)}, u32[]{:S(2)}) collective-permute-start(bf16[16,4096]{1,0:T(8,128)(2,1)S(1)} %get-tuple-element.27), channel_id=1, source_target_pairs={{0,8},{1,9},{2,10},{3,11},{4,12},{5,13},{6,14},{7,15},{8,0},{9,1},... | collective-permute-start | bytes 393224 | tf_op jit(solution)/shard_map/ppermute | solution.py:31
  44.0 7.0 %collective-permute-done.5.got_ref = bf16[16,4096]{1,0:T(8,128)(2,1)S(1)} collective-permute-done((bf16[16,4096]{1,0:T(8,128)(2,1)S(1)}, bf16[16,4096]{1,0:T(8,128)(2,1)S(1)}, u32[]{:S(2)}, u32[]{:S(2)}) %collective-permute-start.5) | collective-permute-done | bytes 131104 | tf_op jit(solution)/shard_map/ppermute | solution.py:31
  52.7 4.9 %all-to-all-start = ((bf16[16,16,2048]{2,1,0:T(8,128)(2,1)}), bf16[16,16,2048]{2,1,0:T(8,128)(2,1)S(1)}, u32[]{:S(2)}, u32[]{:S(2)}) async-start(bf16[16,16,2048]{2,1,0:T(8,128)(2,1)} %shard_map.88), calls=%async_computation | async-start | bytes 2097152 | tf_op jit(solution)/shard_map/all_to_all | solution.py:387
  57.6 1.6 %collective-permute-start.11 = (bf16[16,2048]{1,0:T(8,128)(2,1)S(1)}, bf16[16,2048]{1,0:T(8,128)(2,1)S(1)}, u32[]{:S(2)}, u32[]{:S(2)}) collective-permute-start(bf16[16,2048]{1,0:T(8,128)(2,1)S(1)} %get-tuple-element.28._.refs_2_), channel_id=1, source_target_pairs={{0,16},{16,0},{1,17},{17,1},{2,18},{18,2},{3,19},{19,3},{4,20},{20... | collective-permute-start | bytes 196616 | tf_op jit(solution)/shard_map/ppermute | solution.py:31
  59.8 2.3 %collective-permute-done.11.refs_4_ = bf16[16,2048]{1,0:T(8,128)(2,1)S(1)} collective-permute-done((bf16[16,2048]{1,0:T(8,128)(2,1)S(1)}, bf16[16,2048]{1,0:T(8,128)(2,1)S(1)}, u32[]{:S(2)}, u32[]{:S(2)}) %collective-permute-start.11) | collective-permute-done | bytes 65568 | tf_op jit(solution)/shard_map/ppermute | solution.py:31
  62.1 2.2 %copy-done = bf16[512,4096]{1,0:T(8,128)(2,1)S(1)} copy-done((bf16[512,4096]{1,0:T(8,128)(2,1)S(1)}, bf16[512,4096]{1,0:T(8,128)(2,1)}, u32[]{:S(2)}) %copy-start) | copy-done | bytes 4194328
  64.2 1.3 %shard_map.89 = (bf16[256,4096]{1,0:T(8,128)(2,1)S(1)}, f32[256,128]{1,0:T(8,128)S(1)}) custom-call(bf16[64,4224]{1,0:T(8,128)(2,1)S(1)} %get-tuple-element.29.refs_0_, bf16[64,4224]{1,0:T(8,128)(2,1)S(1)} %collective-permute-done.6.refs_1_, bf16[64,4224]{1,0:T(8,128)(2,1)S(1)} %collective-permute-done.7.refs_2_, ...), custom_call_target="tpu_custom_call" | custom-call | flops 1073741824 | bytes 2097152 | tf_op jit(solution)/shard_map/pallas_call | solution.py:180
  65.5 24.3 %shard_map.90.image_ref = f32[2,256,2048]{2,1,0:T(8,128)S(1)} custom-call(bf16[256,4096]{1,0:T(8,128)(2,1)S(1)} %get-tuple-element.30.rot_ref, bf16[16,2048]{1,0:T(8,128)(2,1)S(1)} %get-tuple-element.31.refs_0_, bf16[16,2048]{1,0:T(8,128)(2,1)S(1)} %collective-permute-done.9.refs_1_, bf16[16,2048]{1,0:T(8,128)(2,1)S(1)} %get-tuple-element.28._.refs_2_, ...), custom_call_target="tpu_custom_call" | custom-call | flops 17179869184 | bytes 16777216 | tf_op jit(solution)/shard_map/pallas_call | solution.py:267
  89.8 2.0 %copy-done.1 = f32[2,256,2048]{2,1,0:T(8,128)} copy-done((f32[2,256,2048]{2,1,0:T(8,128)}, f32[2,256,2048]{2,1,0:T(8,128)S(1)}, u32[]{:S(2)}) %copy-start.1) | copy-done | bytes 4194328
  91.8 2.2 %copy-done.2 = f32[2,256,2048]{2,1,0:T(8,128)S(1)} copy-done((f32[2,256,2048]{2,1,0:T(8,128)S(1)}, f32[2,256,2048]{2,1,0:T(8,128)}, u32[]{:S(2)}) %copy-start.2) | copy-done | bytes 4194328
  94.0 2.4 %shard_map.91 = f32[2,8]{1,0:T(2,128)S(1)} custom-call(bf16[16,16,2048]{2,1,0:T(8,128)(2,1)S(1)} %all-to-all-done.grad_ref, bf16[512,2048]{1,0:T(8,128)(2,1)S(1)} %copy-done.4, f32[2,256,2048]{2,1,0:T(8,128)S(1)} %copy-done.2, f32[256,128]{1,0:T(8,128)S(1)} %get-tuple-element.32.ids_ref), custom_call_target="tpu_custom_call" | custom-call | flops 536870912 | bytes 4194304 | tf_op jit(solution)/shard_map/pallas_call | solution.py:318
  96.9 1.8 %collective-permute-start.14 = (f32[2,8]{1,0:T(2,128)S(1)}, f32[2,8]{1,0:T(2,128)S(1)}, u32[]{:S(2)}, u32[]{:S(2)}) collective-permute-start(f32[2,8]{1,0:T(2,128)S(1)} %shard_map.91), channel_id=1, source_target_pairs={{0,2},{1,3},{2,0},{3,1},{4,6},{5,7},{6,4},{7,5},{8,10},{9,11},{10,... | collective-permute-start | bytes 200 | tf_op jit(solution)/shard_map/ppermute | solution.py:31
  98.7 1.8 %collective-permute-done.14 = f32[2,8]{1,0:T(2,128)S(1)} collective-permute-done((f32[2,8]{1,0:T(2,128)S(1)}, f32[2,8]{1,0:T(2,128)S(1)}, u32[]{:S(2)}, u32[]{:S(2)}) %collective-permute-start.14) | collective-permute-done | bytes 96 | tf_op jit(solution)/shard_map/ppermute | solution.py:31
  101.7 1.5 %collective-permute-start.16 = (f32[2,8]{1,0:T(2,128)S(1)}, f32[2,8]{1,0:T(2,128)S(1)}, u32[]{:S(2)}, u32[]{:S(2)}) collective-permute-start(f32[2,8]{1,0:T(2,128)S(1)} %add_add_fusion.1), channel_id=1, source_target_pairs={{0,4},{1,5},{2,6},{3,7},{4,0},{5,1},{6,2},{7,3},{8,12},{9,13},{10,... | collective-permute-start | bytes 200 | tf_op jit(solution)/shard_map/ppermute | solution.py:31
  103.2 2.4 %collective-permute-start.17 = (f32[2,8]{1,0:T(2,128)S(1)}, f32[2,8]{1,0:T(2,128)S(1)}, u32[]{:S(2)}, u32[]{:S(2)}) collective-permute-start(f32[2,8]{1,0:T(2,128)S(1)} %add_add_fusion.1), channel_id=1, source_target_pairs={{0,8},{1,9},{2,10},{3,11},{4,12},{5,13},{6,14},{7,15},{8,0},{9,1},... | collective-permute-start | bytes 200 | tf_op jit(solution)/shard_map/ppermute | solution.py:31
  106.1 1.6 %collective-permute-done.17 = f32[2,8]{1,0:T(2,128)S(1)} collective-permute-done((f32[2,8]{1,0:T(2,128)S(1)}, f32[2,8]{1,0:T(2,128)S(1)}, u32[]{:S(2)}, u32[]{:S(2)}) %collective-permute-start.17) | collective-permute-done | bytes 96 | tf_op jit(solution)/shard_map/ppermute | solution.py:31
  107.6 3.3 %collective-permute-done.18 = f32[2,8]{1,0:T(2,128)S(1)} collective-permute-done((f32[2,8]{1,0:T(2,128)S(1)}, f32[2,8]{1,0:T(2,128)S(1)}, u32[]{:S(2)}, u32[]{:S(2)}) %collective-permute-start.18) | collective-permute-done | bytes 96 | tf_op jit(solution)/shard_map/ppermute | solution.py:31
  (50 shorter events, 13.0 us)
Async XLA Ops:
  1.7 49.9 %copy-start.5 = (bf16[16,32768]{1,0:T(8,128)(2,1)S(1)}, bf16[16,32768]{1,0:T(8,128)(2,1)}, u32[]{:S(2)}) copy-start(bf16[16,32768]{1,0:T(8,128)(2,1)} %grad_ref.1) | copy-start | bytes 3145732
  1.7 13.5 %collective-permute-start = (bf16[16,18432]{1,0:T(8,128)(2,1)S(1)}, bf16[16,18432]{1,0:T(8,128)(2,1)S(1)}, u32[]{:S(2)}, u32[]{:S(2)}) collective-permute-start(bf16[16,18432]{1,0:T(8,128)(2,1)S(1)} %get-tuple-element.20), channel_id=1, source_target_pairs={{0,1},{1,0},{2,3},{3,2},{4,5},{5,4},{6,7},{7,6},{8,9},{9,8},{10,11... | collective-permute-start | bytes 1769480 | tf_op jit(solution)/shard_map/ppermute | solution.py:31
  4.4 10.8 %collective-permute-start.1 = (bf16[16,4224]{1,0:T(8,128)(2,1)S(1)}, bf16[16,4224]{1,0:T(8,128)(2,1)S(1)}, u32[]{:S(2)}, u32[]{:S(2)}) collective-permute-start(bf16[16,4224]{1,0:T(8,128)(2,1)S(1)} %shard_map.83.refs_0_), channel_id=1, source_target_pairs={{0,8},{1,9},{2,10},{3,11},{4,12},{5,13},{6,14},{7,15},{8,0},{9,1},... | collective-permute-start | bytes 405512 | tf_op jit(solution)/shard_map/ppermute | solution.py:31
  16.5 9.5 %collective-permute-start.2 = (bf16[16,10240]{1,0:T(8,128)(2,1)S(1)}, bf16[16,10240]{1,0:T(8,128)(2,1)S(1)}, u32[]{:S(2)}, u32[]{:S(2)}) collective-permute-start(bf16[16,10240]{1,0:T(8,128)(2,1)S(1)} %get-tuple-element.22), channel_id=1, source_target_pairs={{0,2},{1,3},{2,0},{3,1},{4,6},{5,7},{6,4},{7,5},{8,10},{9,11},{10,... | collective-permute-start | bytes 983048 | tf_op jit(solution)/shard_map/ppermute | solution.py:31
  18.1 7.7 %collective-permute-start.3 = (bf16[32,4224]{1,0:T(8,128)(2,1)S(1)}, bf16[32,4224]{1,0:T(8,128)(2,1)S(1)}, u32[]{:S(2)}, u32[]{:S(2)}) collective-permute-start(bf16[32,4224]{1,0:T(8,128)(2,1)S(1)} %get-tuple-element.23.refs_0_), channel_id=1, source_target_pairs={{0,4},{1,5},{2,6},{3,7},{4,0},{5,1},{6,2},{7,3},{8,12},{9,13},{10,... | collective-permute-start | bytes 811016 | tf_op jit(solution)/shard_map/ppermute | solution.py:31
  27.3 13.2 %collective-permute-start.6 = (bf16[64,4224]{1,0:T(8,128)(2,1)S(1)}, bf16[64,4224]{1,0:T(8,128)(2,1)S(1)}, u32[]{:S(2)}, u32[]{:S(2)}) collective-permute-start(bf16[64,4224]{1,0:T(8,128)(2,1)S(1)} %get-tuple-element.29.refs_0_), channel_id=1, source_target_pairs={{0,2},{1,3},{2,0},{3,1},{4,6},{5,7},{6,4},{7,5},{8,10},{9,11},{10,... | collective-permute-start | bytes 1622024 | tf_op jit(solution)/shard_map/ppermute | solution.py:31
  28.7 11.8 %collective-permute-start.4 = (bf16[16,6144]{1,0:T(8,128)(2,1)S(1)}, bf16[16,6144]{1,0:T(8,128)(2,1)S(1)}, u32[]{:S(2)}, u32[]{:S(2)}) collective-permute-start(bf16[16,6144]{1,0:T(8,128)(2,1)S(1)} %get-tuple-element.25), channel_id=1, source_target_pairs={{0,4},{1,5},{2,6},{3,7},{4,0},{5,1},{6,2},{7,3},{8,12},{9,13},{10,... | collective-permute-start | bytes 589832 | tf_op jit(solution)/shard_map/ppermute | solution.py:31
  29.8 32.2 %collective-permute-start.7 = (bf16[64,4224]{1,0:T(8,128)(2,1)S(1)}, bf16[64,4224]{1,0:T(8,128)(2,1)S(1)}, u32[]{:S(2)}, u32[]{:S(2)}) collective-permute-start(bf16[64,4224]{1,0:T(8,128)(2,1)S(1)} %get-tuple-element.29.refs_0_), channel_id=1, source_target_pairs={{0,1},{1,0},{2,3},{3,2},{4,5},{5,4},{6,7},{7,6},{8,9},{9,8},{10,11... | collective-permute-start | bytes 1622024 | tf_op jit(solution)/shard_map/ppermute | solution.py:31
  40.5 21.5 %collective-permute-start.8 = (bf16[64,4224]{1,0:T(8,128)(2,1)S(1)}, bf16[64,4224]{1,0:T(8,128)(2,1)S(1)}, u32[]{:S(2)}, u32[]{:S(2)}) collective-permute-start(bf16[64,4224]{1,0:T(8,128)(2,1)S(1)} %collective-permute-done.6.refs_1_), channel_id=1, source_target_pairs={{0,1},{1,0},{2,3},{3,2},{4,5},{5,4},{6,7},{7,6},{8,9},{9,8},{10,11... | collective-permute-start | bytes 1622024 | tf_op jit(solution)/shard_map/ppermute | solution.py:31
  41.1 9.9 %collective-permute-start.5 = (bf16[16,4096]{1,0:T(8,128)(2,1)S(1)}, bf16[16,4096]{1,0:T(8,128)(2,1)S(1)}, u32[]{:S(2)}, u32[]{:S(2)}) collective-permute-start(bf16[16,4096]{1,0:T(8,128)(2,1)S(1)} %get-tuple-element.27), channel_id=1, source_target_pairs={{0,8},{1,9},{2,10},{3,11},{4,12},{5,13},{6,14},{7,15},{8,0},{9,1},... | collective-permute-start | bytes 393224 | tf_op jit(solution)/shard_map/ppermute | solution.py:31
  52.7 39.1 %all-to-all-start = ((bf16[16,16,2048]{2,1,0:T(8,128)(2,1)}), bf16[16,16,2048]{2,1,0:T(8,128)(2,1)S(1)}, u32[]{:S(2)}, u32[]{:S(2)}) async-start(bf16[16,16,2048]{2,1,0:T(8,128)(2,1)} %shard_map.88), calls=%async_computation | async-start | bytes 2097152 | tf_op jit(solution)/shard_map/all_to_all | solution.py:387
  57.6 4.4 %collective-permute-start.11 = (bf16[16,2048]{1,0:T(8,128)(2,1)S(1)}, bf16[16,2048]{1,0:T(8,128)(2,1)S(1)}, u32[]{:S(2)}, u32[]{:S(2)}) collective-permute-start(bf16[16,2048]{1,0:T(8,128)(2,1)S(1)} %get-tuple-element.28._.refs_2_), channel_id=1, source_target_pairs={{0,16},{16,0},{1,17},{17,1},{2,18},{18,2},{3,19},{19,3},{4,20},{20... | collective-permute-start | bytes 196616 | tf_op jit(solution)/shard_map/ppermute | solution.py:31
  59.2 6.3 %collective-permute-start.10 = (bf16[16,2048]{1,0:T(8,128)(2,1)S(1)}, bf16[16,2048]{1,0:T(8,128)(2,1)S(1)}, u32[]{:S(2)}, u32[]{:S(2)}) collective-permute-start(bf16[16,2048]{1,0:T(8,128)(2,1)S(1)} %get-tuple-element.28._.refs_2_), channel_id=1, source_target_pairs={{0,1},{1,0},{2,3},{3,2},{4,5},{5,4},{6,7},{7,6},{8,9},{9,8},{10,11... | collective-permute-start | bytes 196616 | tf_op jit(solution)/shard_map/ppermute | solution.py:31
  59.3 6.3 %collective-permute-start.9 = (bf16[16,2048]{1,0:T(8,128)(2,1)S(1)}, bf16[16,2048]{1,0:T(8,128)(2,1)S(1)}, u32[]{:S(2)}, u32[]{:S(2)}) collective-permute-start(bf16[16,2048]{1,0:T(8,128)(2,1)S(1)} %get-tuple-element.31.refs_0_), channel_id=1, source_target_pairs={{0,16},{16,0},{1,17},{17,1},{2,18},{18,2},{3,19},{19,3},{4,20},{20... | collective-permute-start | bytes 196616 | tf_op jit(solution)/shard_map/ppermute | solution.py:31
  62.0 3.5 %collective-permute-start.12 = (bf16[16,2048]{1,0:T(8,128)(2,1)S(1)}, bf16[16,2048]{1,0:T(8,128)(2,1)S(1)}, u32[]{:S(2)}, u32[]{:S(2)}) collective-permute-start(bf16[16,2048]{1,0:T(8,128)(2,1)S(1)} %collective-permute-done.11.refs_4_), channel_id=1, source_target_pairs={{0,1},{1,0},{2,3},{3,2},{4,5},{5,4},{6,7},{7,6},{8,9},{9,8},{10,11... | collective-permute-start | bytes 196616 | tf_op jit(solution)/shard_map/ppermute | solution.py:31
  62.1 2.2 %copy-start = (bf16[512,4096]{1,0:T(8,128)(2,1)S(1)}, bf16[512,4096]{1,0:T(8,128)(2,1)}, u32[]{:S(2)}) copy-start(bf16[512,4096]{1,0:T(8,128)(2,1)} %refs_4_.1) | copy-start | bytes 12582916
  65.5 26.3 %copy-start.4 = (bf16[512,2048]{1,0:T(8,128)(2,1)S(1)}, bf16[512,2048]{1,0:T(8,128)(2,1)}, u32[]{:S(2)}) copy-start(bf16[512,2048]{1,0:T(8,128)(2,1)} %basis_ref.1) | copy-start | bytes 6291460
  91.8 2.2 %copy-start.2 = (f32[2,256,2048]{2,1,0:T(8,128)S(1)}, f32[2,256,2048]{2,1,0:T(8,128)}, u32[]{:S(2)}) copy-start(f32[2,256,2048]{2,1,0:T(8,128)} %copy-done.1) | copy-start | bytes 12582916
  96.3 2.4 %collective-permute-start.13 = (f32[2,8]{1,0:T(2,128)S(1)}, f32[2,8]{1,0:T(2,128)S(1)}, u32[]{:S(2)}, u32[]{:S(2)}) collective-permute-start(f32[2,8]{1,0:T(2,128)S(1)} %shard_map.91), channel_id=1, source_target_pairs={{0,1},{1,0},{2,3},{3,2},{4,5},{5,4},{6,7},{7,6},{8,9},{9,8},{10,11... | collective-permute-start | bytes 200 | tf_op jit(solution)/shard_map/ppermute | solution.py:31
  96.9 3.6 %collective-permute-start.14 = (f32[2,8]{1,0:T(2,128)S(1)}, f32[2,8]{1,0:T(2,128)S(1)}, u32[]{:S(2)}, u32[]{:S(2)}) collective-permute-start(f32[2,8]{1,0:T(2,128)S(1)} %shard_map.91), channel_id=1, source_target_pairs={{0,2},{1,3},{2,0},{3,1},{4,6},{5,7},{6,4},{7,5},{8,10},{9,11},{10,... | collective-permute-start | bytes 200 | tf_op jit(solution)/shard_map/ppermute | solution.py:31
  98.7 3.0 %collective-permute-start.15 = (f32[2,8]{1,0:T(2,128)S(1)}, f32[2,8]{1,0:T(2,128)S(1)}, u32[]{:S(2)}, u32[]{:S(2)}) collective-permute-start(f32[2,8]{1,0:T(2,128)S(1)} %shard_map.91), channel_id=1, source_target_pairs={{0,3},{1,2},{2,1},{3,0},{4,7},{5,6},{6,5},{7,4},{8,11},{9,10},{10,... | collective-permute-start | bytes 200 | tf_op jit(solution)/shard_map/ppermute | solution.py:31
  101.7 4.4 %collective-permute-start.16 = (f32[2,8]{1,0:T(2,128)S(1)}, f32[2,8]{1,0:T(2,128)S(1)}, u32[]{:S(2)}, u32[]{:S(2)}) collective-permute-start(f32[2,8]{1,0:T(2,128)S(1)} %add_add_fusion.1), channel_id=1, source_target_pairs={{0,4},{1,5},{2,6},{3,7},{4,0},{5,1},{6,2},{7,3},{8,12},{9,13},{10,... | collective-permute-start | bytes 200 | tf_op jit(solution)/shard_map/ppermute | solution.py:31
  103.2 4.5 %collective-permute-start.17 = (f32[2,8]{1,0:T(2,128)S(1)}, f32[2,8]{1,0:T(2,128)S(1)}, u32[]{:S(2)}, u32[]{:S(2)}) collective-permute-start(f32[2,8]{1,0:T(2,128)S(1)} %add_add_fusion.1), channel_id=1, source_target_pairs={{0,8},{1,9},{2,10},{3,11},{4,12},{5,13},{6,14},{7,15},{8,0},{9,1},... | collective-permute-start | bytes 200 | tf_op jit(solution)/shard_map/ppermute | solution.py:31
  105.5 5.4 %collective-permute-start.18 = (f32[2,8]{1,0:T(2,128)S(1)}, f32[2,8]{1,0:T(2,128)S(1)}, u32[]{:S(2)}, u32[]{:S(2)}) collective-permute-start(f32[2,8]{1,0:T(2,128)S(1)} %add_add_fusion.1), channel_id=1, source_target_pairs={{0,12},{1,13},{2,14},{3,15},{4,8},{5,9},{6,10},{7,11},{8,4},{9,5},... | collective-permute-start | bytes 200 | tf_op jit(solution)/shard_map/ppermute | solution.py:31
  (6 other events, 6.5 us)

commit v6 on v5

v6 whole, which is shorter than its diff:
```python
import functools
import math

import jax
import jax.numpy as jnp
from jax import lax
from jax.experimental import pallas as pl
from jax.experimental.pallas import tpu as pltpu
from jax.sharding import PartitionSpec as P

D = 4096
FF = 32768
SEQ_MEAN = 32
QT = 16
LANES = 128


damping = 0.1


def params(mib):
    return pltpu.CompilerParams(vmem_limit_bytes=mib * 1024 * 1024)


def whole_block(shape):
    return pl.BlockSpec(shape, lambda *_: (0,) * len(shape), pipeline_mode=pl.Buffered(1))


def swap(x, axis, bit):
    count = lax.axis_size(axis)
    return lax.ppermute(x, axis, [(i, i ^ bit) for i in range(count)])


def in_smem(n):
    return [pl.BlockSpec(memory_space=pltpu.SMEM)] * n


def in_vmem(n):
    return [pl.BlockSpec(memory_space=pltpu.VMEM)] * n


def in_place(n):
    return [pl.BlockSpec(memory_space=pl.ANY)] * n


def cut_factors_kernel(order, hidden, batch_count, owners_ref, fac_ref, keep_ref, give_ref, flag_ref):
    cols = hidden // len(order)
    half = (fac_ref.shape[2] - hidden) // 2
    me, batch = lax.axis_index("wide"), lax.rem(lax.axis_index("groups"), batch_count)
    for part, out_ref in enumerate((keep_ref, give_ref)):
        picked = order[part * len(order) // 2:(part + 1) * len(order) // 2]
        for at, r in enumerate(picked):
            src = pl.multiple_of((me ^ r) * cols, cols)
            out_ref[:, at * cols:(at + 1) * cols] = fac_ref[batch, :, pl.ds(src, cols)]
        src = pl.multiple_of(hidden + ((me & 1) ^ part) * half, LANES)
        out_ref[:, len(picked) * cols:] = fac_ref[batch, :, pl.ds(src, half)]
    apart = owners_ref[batch] ^ me
    lane = lax.broadcasted_iota(jnp.int32, flag_ref.shape, 1)
    flags = jnp.zeros(flag_ref.shape, jnp.float32)
    for step in range(len(order).bit_length() - 1):
        same = jnp.where((apart & (1 << step)) == 0, 1.0, 0.0)
        flags = jnp.where(lane == step, same, flags)
    flag_ref[...] = flags.astype(flag_ref.dtype)


def cut_factors(owners, factors, order, hidden):
    batch_count, rows, width = owners.shape[0], *factors.shape[1:]
    half = jax.ShapeDtypeStruct((rows, width // 2), factors.dtype)
    return pl.pallas_call(
        functools.partial(cut_factors_kernel, order, hidden, batch_count),
        in_specs=in_smem(1) + in_vmem(1),
        out_specs=in_vmem(3),
        out_shape=[half] * 2 + [jax.ShapeDtypeStruct((rows, LANES), factors.dtype)],
        compiler_params=params(16),
        cost_estimate=pl.CostEstimate(flops=0, bytes_accessed=factors.size, transcendentals=0),
    )(owners, factors)


def pick_kernel(step, cols, last, flag_ref, keep_ref, got_ref, *refs):
    first_ref, second_ref = refs[-2:]
    same = flag_ref[:, step:step + 1]
    differs = 1 - same

    def chosen(at, size):
        place = slice(at, at + size)
        return keep_ref[:, place] * same + got_ref[:, place] * differs

    if last:
        first_ref[...] = chosen(0, cols)
        second_ref[...] = chosen(cols, keep_ref.shape[1] - cols)
    else:
        size = keep_ref.shape[1] - first_ref.shape[1]
        shared = chosen(2 * size, keep_ref.shape[1] - 2 * size)
        for part, out_ref in enumerate((first_ref, second_ref)):
            out_ref[:, :size] = chosen(part * size, size)
            out_ref[:, size:] = shared


def pick(flags, keep, got, step, cols, count, after):
    rows, width = keep.shape
    if count > 1:
        widths = [width - count // 2 * cols] * 2
    else:
        widths = [cols, width - cols]
    return pl.pallas_call(
        functools.partial(pick_kernel, step, cols, count == 1),
        in_specs=in_vmem(3) + in_place(len(after)),
        out_specs=in_vmem(2),
        out_shape=[jax.ShapeDtypeStruct((rows, w), keep.dtype) for w in widths],
        compiler_params=params(16),
        cost_estimate=pl.CostEstimate(flops=0, bytes_accessed=2 * keep.size, transcendentals=0),
    )(flags, keep, got, *after)


def join_kernel(first_ref, second_ref, _, out_ref):
    rows = first_ref.shape[0]
    out_ref[:rows, :] = first_ref[...]
    out_ref[rows:, :] = second_ref[...]


def join(first, second, after):
    rows, width = first.shape
    return pl.pallas_call(
        join_kernel,
        in_specs=in_vmem(2) + in_place(1),
        out_specs=in_vmem(1)[0],
        out_shape=jax.ShapeDtypeStruct((2 * rows, width), first.dtype),
        compiler_params=params(16),
        cost_estimate=pl.CostEstimate(flops=0, bytes_accessed=first.size, transcendentals=0),
    )(first, second, after)


def mark_kernel(give_ref, out_ref):
    out_ref[...] = give_ref[:, :out_ref.shape[1]]


def mark(give):
    return pl.pallas_call(
        mark_kernel,
        in_specs=in_vmem(1),
        out_specs=in_vmem(1)[0],
        out_shape=jax.ShapeDtypeStruct((give.shape[0], LANES), give.dtype),
        compiler_params=params(16),
        cost_estimate=pl.CostEstimate(flops=0, bytes_accessed=1, transcendentals=0),
    )(give)


def cut_grads_kernel(ids_ref, grad_ref, _, out_ref):
    count, rows, width = out_ref.shape
    cols = width - LANES
    row = lax.broadcasted_iota(jnp.int32, (rows, LANES), 0)
    ids = jnp.zeros((rows, LANES), jnp.int32)
    for t in range(rows):
        ids = jnp.where(row == t, ids_ref[t], ids)
    ids = ids.astype(jnp.float32).astype(out_ref.dtype)
    for to in range(count):
        out_ref[to, :, :cols] = grad_ref[:, to * cols:(to + 1) * cols]
        out_ref[to, :, cols:] = ids


def cut_grads(ids, grads, after, count):
    rows, hidden = grads.shape
    return pl.pallas_call(
        cut_grads_kernel,
        in_specs=in_smem(1) + in_vmem(1) + in_place(1),
        out_specs=in_vmem(1)[0],
        out_shape=jax.ShapeDtypeStruct((count, rows, hidden // count + LANES), grads.dtype),
        compiler_params=params(16),
        cost_estimate=pl.CostEstimate(flops=0, bytes_accessed=grads.size, transcendentals=0),
    )(ids, grads, after)


def rotate_kernel(order, *refs):
    act_refs, (basis_ref, out_ref, held_ref, sems) = refs[:-4], refs[-4:]
    act_refs = [act_refs[n].at[at:at + size, :] for n, at, size in order]
    depth, width = basis_ref.shape
    places = [slice(k * depth, (k + 1) * depth) for k in range(width // depth)]
    copies = [
        pltpu.make_async_copy(basis_ref.at[:, cols], held_ref.at[k], sems.at[k])
        for k, cols in enumerate(places)
    ]
    for copy in copies:
        copy.start()
    for k, cols in enumerate(places):
        act = jnp.concatenate([ref[:, cols] for ref in act_refs], axis=0)
        copies[k].wait()
        out_ref[:, cols] = jnp.dot(
            act, held_ref[k], preferred_element_type=jnp.float32
        ).astype(jnp.bfloat16)


def rotate(act_pieces, order, basis):
    tokens = sum(x.shape[0] for x in act_pieces)
    depth, width = basis.shape
    count = width // depth
    return pl.pallas_call(
        functools.partial(rotate_kernel, order),
        in_specs=in_vmem(len(act_pieces)) + in_place(1),
        out_specs=in_vmem(1)[0],
        out_shape=jax.ShapeDtypeStruct((tokens, width), jnp.bfloat16),
        scratch_shapes=[
            pltpu.VMEM((count, depth, depth), jnp.bfloat16),
            pltpu.SemaphoreType.DMA((count,)),
        ],
        compiler_params=params(48 if tokens <= 256 else 40),
        cost_estimate=pl.CostEstimate(
            flops=2 * tokens * width * depth, bytes_accessed=basis.size, transcendentals=0
        ),
    )(*act_pieces, basis)


def image_kernel(batch_count, rot_ref, *refs):
    left_refs, half_refs = refs[:batch_count], refs[batch_count:3 * batch_count]
    eig_ref, out_ref, right_ref, turn_ref, pre_a, pre_b = refs[3 * batch_count:]
    rows, width = eig_ref.shape
    half = pre_a.shape[0] // batch_count
    chunk = pre_a.shape[1]
    per = width // chunk
    phases = (rows // half) * per
    tile = min(256, chunk)

    @pl.when(pl.program_id(0) == 0)
    def _():
        side = width // 2
        for b in range(batch_count):
            for other in range(2):
                at = pl.multiple_of(((lax.axis_index("wide") & 1) ^ other) * side, side)
                right_ref[b, :, pl.ds(at, side)] = half_refs[2 * b + other][...]

    for b in range(batch_count):
        turn_ref[b] = left_refs[b][...].T
    out_ref[...] = jnp.zeros_like(out_ref)

    def place(k):
        return pl.multiple_of((k // per) * half, half), (k % per) * chunk

    def produce(k, s, pre):
        row, col = place(k)
        cols = pl.ds(pl.multiple_of(col + s * tile, tile), tile)
        part = min(128, half)
        for at in range(0, half, part):
            some = pl.ds(pl.multiple_of(row + at, part), part)
            damped = eig_ref[some, cols].astype(jnp.float32) + damping
            inverse = pl.reciprocal(damped, approx=True)
            for b in range(batch_count):
                outer_sum = jnp.dot(
                    turn_ref[b, some, :], right_ref[b, :, cols], preferred_element_type=jnp.float32
                )
                pre[b * half + at:b * half + at + part, s * tile:(s + 1) * tile] = (
                    outer_sum * inverse
                ).astype(jnp.bfloat16)

    def absorb(k, pre):
        row, col = place(k)
        rot = rot_ref[:, pl.ds(pl.multiple_of(col, chunk), chunk)]
        for b in range(batch_count):
            out_ref[b, :, pl.ds(row, half)] += lax.dot_general(
                rot, pre[b * half:(b + 1) * half, :], (((1,), (1,)), ((), ())),
                preferred_element_type=jnp.float32,
            )

    def both(k, pre_now, pre_next):
        absorb(k, pre_now)
        for s in range(chunk // tile):
            produce(k + 1, s, pre_next)

    for s in range(chunk // tile):
        produce(0, s, pre_a)

    def pair(q, carry):
        both(2 * q, pre_a, pre_b)
        both(2 * q + 1, pre_b, pre_a)
        return carry

    lax.fori_loop(0, phases // 2 - 1, pair, 0)
    both(phases - 2, pre_a, pre_b)
    absorb(phases - 1, pre_b)


def images(rot, lefts, halves, eigenvalues):
    batch_count, tokens = len(lefts), rot.shape[0]
    hidden, width = eigenvalues.shape
    rows = min(512, hidden)
    half = min(256, rows)
    chunk = min(1024, width // 2)
    return pl.pallas_call(
        functools.partial(image_kernel, batch_count),
        grid=(hidden // rows,),
        in_specs=[whole_block(rot.shape)]
        + [pl.BlockSpec((QT, rows), lambda i: (0, i)) for x in lefts]
        + [whole_block(x.shape) for x in halves]
        + [pl.BlockSpec((rows, width), lambda i: (i, 0))],
        out_specs=pl.BlockSpec((batch_count, tokens, rows), lambda i: (0, 0, i)),
        out_shape=jax.ShapeDtypeStruct((batch_count, tokens, hidden), jnp.float32),
        scratch_shapes=[
            pltpu.VMEM((batch_count, QT, width), jnp.bfloat16),
            pltpu.VMEM((batch_count, rows, QT), jnp.bfloat16),
            pltpu.VMEM((batch_count * half, chunk), jnp.bfloat16),
            pltpu.VMEM((batch_count * half, chunk), jnp.bfloat16),
        ],
        compiler_params=params(32 if tokens <= 256 else 56),
        cost_estimate=pl.CostEstimate(
            flops=2 * hidden * width * (tokens + 256) * batch_count,
            bytes_accessed=2 * hidden * width,
            transcendentals=0,
        ),
    )(rot, *lefts, *halves, eigenvalues)


def score_kernel(batch_count, grad_ref, basis_ref, image_ref, ids_ref, out_ref, token_ref):
    step = pl.program_id(0)
    me = lax.axis_index("wide")

    @pl.when(step == 0)
    def _():
        token_ref[...] = jnp.zeros_like(token_ref)

    order = [me ^ r for r in range(grad_ref.shape[0])]
    grads = jnp.concatenate([grad_ref[n] for n in order], axis=0)
    turned = jnp.dot(grads, basis_ref[...], preferred_element_type=jnp.float32)
    turned = turned.astype(jnp.bfloat16).astype(jnp.float32)
    for b in range(batch_count):
        token_ref[b] += jnp.sum(image_ref[b] * turned, axis=1, keepdims=True)

    @pl.when(step == pl.num_programs(0) - 1)
    def _():
        ids = jnp.concatenate([ids_ref[n] for n in order], axis=0).astype(jnp.float32)
        seqs = lax.broadcasted_iota(jnp.int32, ids.shape, 1).astype(jnp.float32)
        member = ids == seqs
        for b in range(batch_count):
            sums = jnp.sum(jnp.where(member, token_ref[b], 0.0), axis=0, keepdims=True)
            out_ref[b:b + 1, :] = sums[:, :out_ref.shape[1]]


def score_parts(grads, grad_basis, image, seq_count):
    batch_count, tokens = image.shape[:2]
    count, rows, width = grads.shape
    hidden = width - LANES
    inner = min(grad_basis.shape[0], hidden)
    return pl.pallas_call(
        functools.partial(score_kernel, batch_count),
        grid=(hidden // inner,),
        in_specs=[
            pl.BlockSpec((count, rows, inner), lambda i: (0, 0, i)),
            pl.BlockSpec((grad_basis.shape[0], inner), lambda i: (0, i)),
            pl.BlockSpec((batch_count, tokens, inner), lambda i: (0, 0, i)),
            pl.BlockSpec((count, rows, LANES), lambda i: (0, 0, hidden // LANES)),
        ],
        out_specs=pl.BlockSpec((batch_count, seq_count), lambda i: (0, 0)),
        out_shape=jax.ShapeDtypeStruct((batch_count, seq_count), jnp.float32),
        scratch_shapes=[pltpu.VMEM((batch_count, tokens, 1), jnp.float32)],
        compiler_params=params(44),
        cost_estimate=pl.CostEstimate(
            flops=2 * tokens * hidden * grad_basis.shape[0],
            bytes_accessed=4 * image.size,
            transcendentals=0,
        ),
    )(grads, grad_basis, image, grads)


def per_device(
    train_act, train_grad, seq_ids, act_basis, grad_basis, eigenvalues, query_factors, owners
):
    wide_count = lax.axis_size("wide")
    bits = [1 << n for n in range(wide_count.bit_length() - 1)]
    me = lax.axis_index("wide")
    tok_local = train_act.shape[0]
    seq_count = tok_local * wide_count // SEQ_MEAN
    cols = grad_basis.shape[1]
    hidden = train_grad.shape[1]
    batch_count = owners.shape[0]
    score_scale = 1.0 / math.sqrt(FF * D * QT * SEQ_MEAN)
    batch = lax.axis_index("groups") % batch_count

    order = [0]
    for bit in reversed(bits):
        order = order + [r + bit for r in order]
    order = sorted(order, key=lambda r: [r & bit for bit in bits])
    acts, ranks = train_act, [0]
    far = bits[:1:-1]
    keep, give, flags = cut_factors(owners, query_factors, order, hidden)
    count = wide_count // 2
    after = []
    for step, bit in enumerate(bits):
        got = swap(give, "wide", bit)
        keep, give = pick(flags, keep, got, step, cols, count, after)
        count //= 2
        after = []
        if step < len(far):
            acts = join(acts, swap(acts, "wide", far[step]), give)
            ranks = ranks + [r + far[step] for r in ranks]
            after = [acts]
        if step == len(bits) - 2:
            sent = cut_grads(seq_ids, train_grad, swap(mark(give), "wide", 1), wide_count)
            grads = lax.all_to_all(sent, "wide", 0, 0)
    left, right = keep, give
    pieces = [(acts, ranks)]
    for bit in (2, 1):
        pieces += [(swap(x, "wide", bit), [r + bit for r in has]) for x, has in pieces]
    token_order = [None] * wide_count
    for n, (_, has) in enumerate(pieces):
        for at, r in enumerate(has):
            token_order[r] = (n, at * tok_local, tok_local)
    rot = rotate([x for x, _ in pieces], token_order, act_basis)

    lefts = [left, swap(left, "groups", 1)]
    halves = []
    for x in (right, swap(right, "groups", 1)):
        halves += [x, swap(x, "wide", 1)]

    image = images(rot, lefts, halves, eigenvalues)
    parts = score_parts(grads, grad_basis, image, seq_count)
    for near in (bits[:2], bits[2:]):
        step = near[0]
        others = [swap(parts, "wide", step * n) for n in range(1, 1 << len(near))]
        parts = parts + sum(others)
    mine, others = parts[0], parts[1]
    first = jnp.where(batch == 0, mine, others)
    second = jnp.where(batch == 0, others, mine)
    return jnp.stack([first, second], axis=1) * score_scale


def solution(mesh):
    return jax.shard_map(
        per_device,
        mesh=mesh,
        in_specs=(
            P(("groups", "wide"), None),
            P(("groups", "wide"), None),
            P(("groups", "wide")),
            P(),
            P(None, "wide"),
            P("wide", None),
            P("wide", None, None),
            P(),
        ),
        out_specs=P("groups", None),
        check_vma=False,
    )
```

time: 112 us -> 132 us (1.18)
  waiting for transfers between devices: 41.9 us -> 62.6 us
  local copies, waits for them, and re-layouts: 10.9 us -> 6.48 us
  Pallas kernels: 32 us -> 34.2 us
  starting transfers between devices: 25.9 us -> 27.6 us
    ppermute x19 -> x20, waiting for transfers between devices: 41.9 us -> 62.6 us  [swap(): return lax.ppermute(x, axis, [(i, i ^ bit) for i in range(count)])]
    unnamed x20 -> x16, local copies, waits for them, and re-layouts: 10.9 us -> 6.48 us
    pallas_call x1, Pallas kernels: 1.25 us -> 3.67 us  [rotate(): pl.pallas_call(functools.partial(rotate_kernel, order), in_specs=in_vmem(...]
    pallas_call x6 -> x8, Pallas kernels: 4.05 us -> 2.19 us  [the longest x1 1.65 us: cut_grads(): pl.pallas_call(cut_grads_kernel, in_specs=in_smem(1) + in_vmem(1) + in_pl...]
    all_to_all x1, starting transfers between devices: 4.92 us -> 6.37 us  [per_device(): grads = lax.all_to_all(sent, 'wide', 0, 0)]
    ppermute x19 -> x20, starting transfers between devices: 21 us -> 21.2 us  [swap(): return lax.ppermute(x, axis, [(i, i ^ bit) for i in range(count)])]
  transfers between devices with their start and end apart: 20 -> 21, of which waited for: 10 -> 11; matrix products, arithmetic and copies ran while one was open for 0% -> 0% of each run, Pallas kernels for 25% -> 24%
where the time goes in v6:
time: 132 us
  waiting for transfers between devices  62.6 us (47%)
  Pallas kernels  34.2 us (26%)
  starting transfers between devices  27.6 us (21%)
  local copies, waits for them, and re-layouts  6.48 us (5%)
    ppermute x20, waiting for transfers between devices, swap(): return lax.ppermute(x, axis, [(i, i ^ bit) for i in range(count)])  62.6 us
    pallas_call x1, Pallas kernels, images(): pl.pallas_call(functools.partial(image_kernel, batch_count), grid=(hidden...  25.2 us
    ppermute x20, starting transfers between devices, swap(): return lax.ppermute(x, axis, [(i, i ^ bit) for i in range(count)])  21.2 us
    unnamed x16, local copies, waits for them, and re-layouts  6.48 us
    all_to_all x1, starting transfers between devices, per_device(): grads = lax.all_to_all(sent, 'wide', 0, 0)  6.37 us
    pallas_call x1, Pallas kernels, rotate(): pl.pallas_call(functools.partial(rotate_kernel, order), in_specs=in_vmem(...  3.67 us
  transfers between devices with their start and end apart: 21, of which 11 were waited for; matrix products, arithmetic and copies ran while one was open for 0% of the time, Pallas kernels for 24%

profile of v6, /device:TPU:0, one launch (start us, length us, event | category | flops | bytes accessed | tf_op | source)
XLA Modules:
  0.0 131.6 jit_solution(15476627275758605231)
XLA Ops:
  0.0 1.7 %copy-done.2 = bf16[2,16,36864]{2,1,0:T(8,128)(2,1)S(1)} copy-done((bf16[2,16,36864]{2,1,0:T(8,128)(2,1)S(1)}, bf16[2,16,36864]{2,1,0:T(8,128)(2,1)}, u32[]{:S(2)}) %copy-start.2) | copy-done | bytes 2359320
  3.5 3.8 %collective-permute-start.2 = (bf16[16,4096]{1,0:T(8,128)(2,1)S(1)}, bf16[16,4096]{1,0:T(8,128)(2,1)S(1)}, u32[]{:S(2)}, u32[]{:S(2)}) collective-permute-start(bf16[16,4096]{1,0:T(8,128)(2,1)S(1)} %copy-done.5), channel_id=1, source_target_pairs={{0,8},{1,9},{2,10},{3,11},{4,12},{5,13},{6,14},{7,15},{8,0},{9,1},... | collective-permute-start | bytes 393224 | tf_op jit(solution)/shard_map/ppermute | solution.py:31
  7.5 1.6 %collective-permute-start.1 = (bf16[16,10240]{1,0:T(8,128)(2,1)S(1)}, bf16[16,10240]{1,0:T(8,128)(2,1)S(1)}, u32[]{:S(2)}, u32[]{:S(2)}) collective-permute-start(bf16[16,10240]{1,0:T(8,128)(2,1)S(1)} %get-tuple-element.20._), channel_id=1, source_target_pairs={{0,2},{1,3},{2,0},{3,1},{4,6},{5,7},{6,4},{7,5},{8,10},{9,11},{10,... | collective-permute-start | bytes 983048 | tf_op jit(solution)/shard_map/ppermute | solution.py:31
  9.0 5.0 %collective-permute-done.2.second_ref = bf16[16,4096]{1,0:T(8,128)(2,1)S(1)} collective-permute-done((bf16[16,4096]{1,0:T(8,128)(2,1)S(1)}, bf16[16,4096]{1,0:T(8,128)(2,1)S(1)}, u32[]{:S(2)}, u32[]{:S(2)}) %collective-permute-start.2) | collective-permute-done | bytes 131104 | tf_op jit(solution)/shard_map/ppermute | solution.py:31
  14.9 2.3 %collective-permute-done.1.got_ref = bf16[16,10240]{1,0:T(8,128)(2,1)S(1)} collective-permute-done((bf16[16,10240]{1,0:T(8,128)(2,1)S(1)}, bf16[16,10240]{1,0:T(8,128)(2,1)S(1)}, u32[]{:S(2)}, u32[]{:S(2)}) %collective-permute-start.1) | collective-permute-done | bytes 327712 | tf_op jit(solution)/shard_map/ppermute | solution.py:31
  17.3 4.9 %collective-permute-done.4.second_ref = bf16[32,4096]{1,0:T(8,128)(2,1)S(1)} collective-permute-done((bf16[32,4096]{1,0:T(8,128)(2,1)S(1)}, bf16[32,4096]{1,0:T(8,128)(2,1)S(1)}, u32[]{:S(2)}, u32[]{:S(2)}) %collective-permute-start.4) | collective-permute-done | bytes 262176 | tf_op jit(solution)/shard_map/ppermute | solution.py:31
  22.2 1.3 %collective-permute-start.6 = (bf16[64,4096]{1,0:T(8,128)(2,1)S(1)}, bf16[64,4096]{1,0:T(8,128)(2,1)S(1)}, u32[]{:S(2)}, u32[]{:S(2)}) collective-permute-start(bf16[64,4096]{1,0:T(8,128)(2,1)S(1)} %shard_map.86.refs_0_), channel_id=1, source_target_pairs={{0,2},{1,3},{2,0},{3,1},{4,6},{5,7},{6,4},{7,5},{8,10},{9,11},{10,... | collective-permute-start | bytes 1572872 | tf_op jit(solution)/shard_map/ppermute | solution.py:31
  24.8 10.3 %collective-permute-done.6.refs_1_ = bf16[64,4096]{1,0:T(8,128)(2,1)S(1)} collective-permute-done((bf16[64,4096]{1,0:T(8,128)(2,1)S(1)}, bf16[64,4096]{1,0:T(8,128)(2,1)S(1)}, u32[]{:S(2)}, u32[]{:S(2)}) %collective-permute-start.6) | collective-permute-done | bytes 524320 | tf_op jit(solution)/shard_map/ppermute | solution.py:31
  37.0 1.7 %shard_map.89 = bf16[16,16,2176]{2,1,0:T(8,128)(2,1)} custom-call(s32[16]{0:T(128)S(1)} %copy-done.7, bf16[16,32768]{1,0:T(8,128)(2,1)S(1)} %copy-done.4, bf16[16,128]{1,0:T(8,128)(2,1)S(1)} %collective-permute-done.5._), custom_call_target="tpu_custom_call" | custom-call | bytes 524288 | tf_op jit(solution)/shard_map/pallas_call | solution.py:163
  38.6 6.4 %all-to-all-start = ((bf16[16,16,2176]{2,1,0:T(8,128)(2,1)}), bf16[16,16,2176]{2,1,0:T(8,128)(2,1)S(1)}, u32[]{:S(2)}, u32[]{:S(2)}) async-start(bf16[16,16,2176]{2,1,0:T(8,128)(2,1)} %shard_map.89), calls=%async_computation | async-start | bytes 2228224 | tf_op jit(solution)/shard_map/all_to_all | solution.py:395
  45.0 2.8 %collective-permute-start.9 = (bf16[16,4096]{1,0:T(8,128)(2,1)S(1)}, bf16[16,4096]{1,0:T(8,128)(2,1)S(1)}, u32[]{:S(2)}, u32[]{:S(2)}) collective-permute-start(bf16[16,4096]{1,0:T(8,128)(2,1)S(1)} %get-tuple-element.23.give_ref), channel_id=1, source_target_pairs={{0,8},{1,9},{2,10},{3,11},{4,12},{5,13},{6,14},{7,15},{8,0},{9,1},... | collective-permute-start | bytes 393224 | tf_op jit(solution)/shard_map/ppermute | solution.py:31
  47.8 30.8 %collective-permute-done.9.got_ref = bf16[16,4096]{1,0:T(8,128)(2,1)S(1)} collective-permute-done((bf16[16,4096]{1,0:T(8,128)(2,1)S(1)}, bf16[16,4096]{1,0:T(8,128)(2,1)S(1)}, u32[]{:S(2)}, u32[]{:S(2)}) %collective-permute-start.9) | collective-permute-done | bytes 131104 | tf_op jit(solution)/shard_map/ppermute | solution.py:31
  78.7 1.6 %collective-permute-start.12 = (bf16[16,2048]{1,0:T(8,128)(2,1)S(1)}, bf16[16,2048]{1,0:T(8,128)(2,1)S(1)}, u32[]{:S(2)}, u32[]{:S(2)}) collective-permute-start(bf16[16,2048]{1,0:T(8,128)(2,1)S(1)} %get-tuple-element.26.refs_2_), channel_id=1, source_target_pairs={{0,16},{16,0},{1,17},{17,1},{2,18},{18,2},{3,19},{19,3},{4,20},{20... | collective-permute-start | bytes 196616 | tf_op jit(solution)/shard_map/ppermute | solution.py:31
  80.8 2.2 %collective-permute-done.12.refs_4_ = bf16[16,2048]{1,0:T(8,128)(2,1)S(1)} collective-permute-done((bf16[16,2048]{1,0:T(8,128)(2,1)S(1)}, bf16[16,2048]{1,0:T(8,128)(2,1)S(1)}, u32[]{:S(2)}, u32[]{:S(2)}) %collective-permute-start.12) | collective-permute-done | bytes 65568 | tf_op jit(solution)/shard_map/ppermute | solution.py:31
  83.1 3.7 %shard_map.90.rot_ref = bf16[256,4096]{1,0:T(8,128)(2,1)S(1)} custom-call(bf16[64,4096]{1,0:T(8,128)(2,1)S(1)} %shard_map.86.refs_0_, bf16[64,4096]{1,0:T(8,128)(2,1)S(1)} %collective-permute-done.6.refs_1_, bf16[64,4096]{1,0:T(8,128)(2,1)S(1)} %collective-permute-done.7.refs_2_, bf16[64,4096]{1,0:T(8,128)(2,1)S(1)} %collective-permute-done.8.refs_3_, ...), custom_call_target="tpu_custom_call" | custom-call | flops 1073741824 | bytes 2097152 | tf_op jit(solution)/shard_map/pallas_call | solution.py:196
  86.8 25.2 %shard_map.92.image_ref = f32[2,256,2048]{2,1,0:T(8,128)S(1)} custom-call(bf16[256,4096]{1,0:T(8,128)(2,1)S(1)} %shard_map.90.rot_ref, bf16[16,2048]{1,0:T(8,128)(2,1)S(1)} %get-tuple-element.25.refs_0_, bf16[16,2048]{1,0:T(8,128)(2,1)S(1)} %collective-permute-done.10.refs_1_, bf16[16,2048]{1,0:T(8,128)(2,1)S(1)} %get-tuple-element.26.refs_2_, ...), custom_call_target="tpu_custom_call" | custom-call | flops 17179869184 | bytes 16777216 | tf_op jit(solution)/shard_map/pallas_call | solution.py:286
  112.0 2.0 %copy-done = f32[2,256,2048]{2,1,0:T(8,128)} copy-done((f32[2,256,2048]{2,1,0:T(8,128)}, f32[2,256,2048]{2,1,0:T(8,128)S(1)}, u32[]{:S(2)}) %copy-start) | copy-done | bytes 4194328
  114.0 2.2 %copy-done.1 = f32[2,256,2048]{2,1,0:T(8,128)S(1)} copy-done((f32[2,256,2048]{2,1,0:T(8,128)S(1)}, f32[2,256,2048]{2,1,0:T(8,128)}, u32[]{:S(2)}) %copy-start.1) | copy-done | bytes 4194328
  116.1 2.5 %shard_map.93 = f32[2,8]{1,0:T(2,128)S(1)} custom-call(bf16[16,16,2176]{2,1,0:T(8,128)(2,1)S(1)} %all-to-all-done.grad_ref.ids_ref, bf16[512,2048]{1,0:T(8,128)(2,1)S(1)} %copy-done.3, f32[2,256,2048]{2,1,0:T(8,128)S(1)} %copy-done.1, bf16[16,16,2176]{2,1,0:T(8,128)(2,1)S(1)} %all-to-all-done.grad_ref.ids_ref), custom_call_target="tpu_custom_call" | custom-call | flops 536870912 | bytes 4194304 | tf_op jit(solution)/shard_map/pallas_call | solution.py:340
  119.2 1.5 %collective-permute-start.15 = (f32[2,8]{1,0:T(2,128)S(1)}, f32[2,8]{1,0:T(2,128)S(1)}, u32[]{:S(2)}, u32[]{:S(2)}) collective-permute-start(f32[2,8]{1,0:T(2,128)S(1)} %shard_map.93), channel_id=1, source_target_pairs={{0,2},{1,3},{2,0},{3,1},{4,6},{5,7},{6,4},{7,5},{8,10},{9,11},{10,... | collective-permute-start | bytes 200 | tf_op jit(solution)/shard_map/ppermute | solution.py:31
  120.7 2.0 %collective-permute-done.15 = f32[2,8]{1,0:T(2,128)S(1)} collective-permute-done((f32[2,8]{1,0:T(2,128)S(1)}, f32[2,8]{1,0:T(2,128)S(1)}, u32[]{:S(2)}, u32[]{:S(2)}) %collective-permute-start.15) | collective-permute-done | bytes 96 | tf_op jit(solution)/shard_map/ppermute | solution.py:31
  123.7 1.9 %collective-permute-start.18 = (f32[2,8]{1,0:T(2,128)S(1)}, f32[2,8]{1,0:T(2,128)S(1)}, u32[]{:S(2)}, u32[]{:S(2)}) collective-permute-start(f32[2,8]{1,0:T(2,128)S(1)} %add_add_fusion.1), channel_id=1, source_target_pairs={{0,8},{1,9},{2,10},{3,11},{4,12},{5,13},{6,14},{7,15},{8,0},{9,1},... | collective-permute-start | bytes 200 | tf_op jit(solution)/shard_map/ppermute | solution.py:31
  125.7 2.5 %collective-permute-start.19 = (f32[2,8]{1,0:T(2,128)S(1)}, f32[2,8]{1,0:T(2,128)S(1)}, u32[]{:S(2)}, u32[]{:S(2)}) collective-permute-start(f32[2,8]{1,0:T(2,128)S(1)} %add_add_fusion.1), channel_id=1, source_target_pairs={{0,12},{1,13},{2,14},{3,15},{4,8},{5,9},{6,10},{7,11},{8,4},{9,5},... | collective-permute-start | bytes 200 | tf_op jit(solution)/shard_map/ppermute | solution.py:31
  128.3 2.8 %collective-permute-done.19 = f32[2,8]{1,0:T(2,128)S(1)} collective-permute-done((f32[2,8]{1,0:T(2,128)S(1)}, f32[2,8]{1,0:T(2,128)S(1)}, u32[]{:S(2)}, u32[]{:S(2)}) %collective-permute-start.19) | collective-permute-done | bytes 96 | tf_op jit(solution)/shard_map/ppermute | solution.py:31
  (50 shorter events, 9.0 us)
Async XLA Ops:
  3.0 4.3 %collective-permute-start = (bf16[16,18432]{1,0:T(8,128)(2,1)S(1)}, bf16[16,18432]{1,0:T(8,128)(2,1)S(1)}, u32[]{:S(2)}, u32[]{:S(2)}) collective-permute-start(bf16[16,18432]{1,0:T(8,128)(2,1)S(1)} %get-tuple-element.18), channel_id=1, source_target_pairs={{0,1},{1,0},{2,3},{3,2},{4,5},{5,4},{6,7},{7,6},{8,9},{9,8},{10,11... | collective-permute-start | bytes 1769480 | tf_op jit(solution)/shard_map/ppermute | solution.py:31
  3.5 10.6 %collective-permute-start.2 = (bf16[16,4096]{1,0:T(8,128)(2,1)S(1)}, bf16[16,4096]{1,0:T(8,128)(2,1)S(1)}, u32[]{:S(2)}, u32[]{:S(2)}) collective-permute-start(bf16[16,4096]{1,0:T(8,128)(2,1)S(1)} %copy-done.5), channel_id=1, source_target_pairs={{0,8},{1,9},{2,10},{3,11},{4,12},{5,13},{6,14},{7,15},{8,0},{9,1},... | collective-permute-start | bytes 393224 | tf_op jit(solution)/shard_map/ppermute | solution.py:31
  7.3 29.7 %copy-start.4 = (bf16[16,32768]{1,0:T(8,128)(2,1)S(1)}, bf16[16,32768]{1,0:T(8,128)(2,1)}, u32[]{:S(2)}) copy-start(bf16[16,32768]{1,0:T(8,128)(2,1)} %grad_ref.1) | copy-start | bytes 3145732
  7.3 29.7 %copy-start.7 = (s32[16]{0:T(128)S(1)}, s32[16]{0:T(128)}, u32[]{:S(2)}) copy-start(s32[16]{0:T(128)} %ids_ref.1) | copy-start | bytes 196
  7.5 9.7 %collective-permute-start.1 = (bf16[16,10240]{1,0:T(8,128)(2,1)S(1)}, bf16[16,10240]{1,0:T(8,128)(2,1)S(1)}, u32[]{:S(2)}, u32[]{:S(2)}) collective-permute-start(bf16[16,10240]{1,0:T(8,128)(2,1)S(1)} %get-tuple-element.20._), channel_id=1, source_target_pairs={{0,2},{1,3},{2,0},{3,1},{4,6},{5,7},{6,4},{7,5},{8,10},{9,11},{10,... | collective-permute-start | bytes 983048 | tf_op jit(solution)/shard_map/ppermute | solution.py:31
  14.1 8.1 %collective-permute-start.4 = (bf16[32,4096]{1,0:T(8,128)(2,1)S(1)}, bf16[32,4096]{1,0:T(8,128)(2,1)S(1)}, u32[]{:S(2)}, u32[]{:S(2)}) collective-permute-start(bf16[32,4096]{1,0:T(8,128)(2,1)S(1)} %shard_map.84.refs_0_.first_ref), channel_id=1, source_target_pairs={{0,4},{1,5},{2,6},{3,7},{4,0},{5,1},{6,2},{7,3},{8,12},{9,13},{10,... | collective-permute-start | bytes 786440 | tf_op jit(solution)/shard_map/ppermute | solution.py:31
  22.2 12.8 %collective-permute-start.6 = (bf16[64,4096]{1,0:T(8,128)(2,1)S(1)}, bf16[64,4096]{1,0:T(8,128)(2,1)S(1)}, u32[]{:S(2)}, u32[]{:S(2)}) collective-permute-start(bf16[64,4096]{1,0:T(8,128)(2,1)S(1)} %shard_map.86.refs_0_), channel_id=1, source_target_pairs={{0,2},{1,3},{2,0},{3,1},{4,6},{5,7},{6,4},{7,5},{8,10},{9,11},{10,... | collective-permute-start | bytes 1572872 | tf_op jit(solution)/shard_map/ppermute | solution.py:31
  23.5 11.5 %collective-permute-start.3 = (bf16[16,6144]{1,0:T(8,128)(2,1)S(1)}, bf16[16,6144]{1,0:T(8,128)(2,1)S(1)}, u32[]{:S(2)}, u32[]{:S(2)}) collective-permute-start(bf16[16,6144]{1,0:T(8,128)(2,1)S(1)} %get-tuple-element.22._), channel_id=1, source_target_pairs={{0,4},{1,5},{2,6},{3,7},{4,0},{5,1},{6,2},{7,3},{8,12},{9,13},{10,... | collective-permute-start | bytes 589832 | tf_op jit(solution)/shard_map/ppermute | solution.py:31
  24.7 58.3 %collective-permute-start.7 = (bf16[64,4096]{1,0:T(8,128)(2,1)S(1)}, bf16[64,4096]{1,0:T(8,128)(2,1)S(1)}, u32[]{:S(2)}, u32[]{:S(2)}) collective-permute-start(bf16[64,4096]{1,0:T(8,128)(2,1)S(1)} %shard_map.86.refs_0_), channel_id=1, source_target_pairs={{0,1},{1,0},{2,3},{3,2},{4,5},{5,4},{6,7},{7,6},{8,9},{9,8},{10,11... | collective-permute-start | bytes 1572872 | tf_op jit(solution)/shard_map/ppermute | solution.py:31
  35.1 48.0 %collective-permute-start.8 = (bf16[64,4096]{1,0:T(8,128)(2,1)S(1)}, bf16[64,4096]{1,0:T(8,128)(2,1)S(1)}, u32[]{:S(2)}, u32[]{:S(2)}) collective-permute-start(bf16[64,4096]{1,0:T(8,128)(2,1)S(1)} %collective-permute-done.6.refs_1_), channel_id=1, source_target_pairs={{0,1},{1,0},{2,3},{3,2},{4,5},{5,4},{6,7},{7,6},{8,9},{9,8},{10,11... | collective-permute-start | bytes 1572872 | tf_op jit(solution)/shard_map/ppermute | solution.py:31
  35.2 1.8 %collective-permute-start.5 = (bf16[16,128]{1,0:T(8,128)(2,1)S(1)}, bf16[16,128]{1,0:T(8,128)(2,1)S(1)}, u32[]{:S(2)}, u32[]{:S(2)}) collective-permute-start(bf16[16,128]{1,0:T(8,128)(2,1)S(1)} %shard_map.88), channel_id=1, source_target_pairs={{0,1},{1,0},{2,3},{3,2},{4,5},{5,4},{6,7},{7,6},{8,9},{9,8},{10,11... | collective-permute-start | bytes 12296 | tf_op jit(solution)/shard_map/ppermute | solution.py:31
  38.6 75.3 %all-to-all-start = ((bf16[16,16,2176]{2,1,0:T(8,128)(2,1)}), bf16[16,16,2176]{2,1,0:T(8,128)(2,1)S(1)}, u32[]{:S(2)}, u32[]{:S(2)}) async-start(bf16[16,16,2176]{2,1,0:T(8,128)(2,1)} %shard_map.89), calls=%async_computation | async-start | bytes 2228224 | tf_op jit(solution)/shard_map/all_to_all | solution.py:395
  45.0 33.6 %collective-permute-start.9 = (bf16[16,4096]{1,0:T(8,128)(2,1)S(1)}, bf16[16,4096]{1,0:T(8,128)(2,1)S(1)}, u32[]{:S(2)}, u32[]{:S(2)}) collective-permute-start(bf16[16,4096]{1,0:T(8,128)(2,1)S(1)} %get-tuple-element.23.give_ref), channel_id=1, source_target_pairs={{0,8},{1,9},{2,10},{3,11},{4,12},{5,13},{6,14},{7,15},{8,0},{9,1},... | collective-permute-start | bytes 393224 | tf_op jit(solution)/shard_map/ppermute | solution.py:31
  78.7 4.3 %collective-permute-start.12 = (bf16[16,2048]{1,0:T(8,128)(2,1)S(1)}, bf16[16,2048]{1,0:T(8,128)(2,1)S(1)}, u32[]{:S(2)}, u32[]{:S(2)}) collective-permute-start(bf16[16,2048]{1,0:T(8,128)(2,1)S(1)} %get-tuple-element.26.refs_2_), channel_id=1, source_target_pairs={{0,16},{16,0},{1,17},{17,1},{2,18},{18,2},{3,19},{19,3},{4,20},{20... | collective-permute-start | bytes 196616 | tf_op jit(solution)/shard_map/ppermute | solution.py:31
  80.3 6.5 %collective-permute-start.11 = (bf16[16,2048]{1,0:T(8,128)(2,1)S(1)}, bf16[16,2048]{1,0:T(8,128)(2,1)S(1)}, u32[]{:S(2)}, u32[]{:S(2)}) collective-permute-start(bf16[16,2048]{1,0:T(8,128)(2,1)S(1)} %get-tuple-element.26.refs_2_), channel_id=1, source_target_pairs={{0,1},{1,0},{2,3},{3,2},{4,5},{5,4},{6,7},{7,6},{8,9},{9,8},{10,11... | collective-permute-start | bytes 196616 | tf_op jit(solution)/shard_map/ppermute | solution.py:31
  80.3 6.5 %collective-permute-start.10 = (bf16[16,2048]{1,0:T(8,128)(2,1)S(1)}, bf16[16,2048]{1,0:T(8,128)(2,1)S(1)}, u32[]{:S(2)}, u32[]{:S(2)}) collective-permute-start(bf16[16,2048]{1,0:T(8,128)(2,1)S(1)} %get-tuple-element.25.refs_0_), channel_id=1, source_target_pairs={{0,16},{16,0},{1,17},{17,1},{2,18},{18,2},{3,19},{19,3},{4,20},{20... | collective-permute-start | bytes 196616 | tf_op jit(solution)/shard_map/ppermute | solution.py:31
  83.0 3.7 %collective-permute-start.13 = (bf16[16,2048]{1,0:T(8,128)(2,1)S(1)}, bf16[16,2048]{1,0:T(8,128)(2,1)S(1)}, u32[]{:S(2)}, u32[]{:S(2)}) collective-permute-start(bf16[16,2048]{1,0:T(8,128)(2,1)S(1)} %collective-permute-done.12.refs_4_), channel_id=1, source_target_pairs={{0,1},{1,0},{2,3},{3,2},{4,5},{5,4},{6,7},{7,6},{8,9},{9,8},{10,11... | collective-permute-start | bytes 196616 | tf_op jit(solution)/shard_map/ppermute | solution.py:31
  86.7 27.2 %copy-start.3 = (bf16[512,2048]{1,0:T(8,128)(2,1)S(1)}, bf16[512,2048]{1,0:T(8,128)(2,1)}, u32[]{:S(2)}) copy-start(bf16[512,2048]{1,0:T(8,128)(2,1)} %basis_ref.1) | copy-start | bytes 6291460
  118.6 2.1 %collective-permute-start.14 = (f32[2,8]{1,0:T(2,128)S(1)}, f32[2,8]{1,0:T(2,128)S(1)}, u32[]{:S(2)}, u32[]{:S(2)}) collective-permute-start(f32[2,8]{1,0:T(2,128)S(1)} %shard_map.93), channel_id=1, source_target_pairs={{0,1},{1,0},{2,3},{3,2},{4,5},{5,4},{6,7},{7,6},{8,9},{9,8},{10,11... | collective-permute-start | bytes 200 | tf_op jit(solution)/shard_map/ppermute | solution.py:31
  119.2 3.6 %collective-permute-start.15 = (f32[2,8]{1,0:T(2,128)S(1)}, f32[2,8]{1,0:T(2,128)S(1)}, u32[]{:S(2)}, u32[]{:S(2)}) collective-permute-start(f32[2,8]{1,0:T(2,128)S(1)} %shard_map.93), channel_id=1, source_target_pairs={{0,2},{1,3},{2,0},{3,1},{4,6},{5,7},{6,4},{7,5},{8,10},{9,11},{10,... | collective-permute-start | bytes 200 | tf_op jit(solution)/shard_map/ppermute | solution.py:31
  120.7 3.0 %collective-permute-start.16 = (f32[2,8]{1,0:T(2,128)S(1)}, f32[2,8]{1,0:T(2,128)S(1)}, u32[]{:S(2)}, u32[]{:S(2)}) collective-permute-start(f32[2,8]{1,0:T(2,128)S(1)} %shard_map.93), channel_id=1, source_target_pairs={{0,3},{1,2},{2,1},{3,0},{4,7},{5,6},{6,5},{7,4},{8,11},{9,10},{10,... | collective-permute-start | bytes 200 | tf_op jit(solution)/shard_map/ppermute | solution.py:31
  123.7 4.4 %collective-permute-start.17 = (f32[2,8]{1,0:T(2,128)S(1)}, f32[2,8]{1,0:T(2,128)S(1)}, u32[]{:S(2)}, u32[]{:S(2)}) collective-permute-start(f32[2,8]{1,0:T(2,128)S(1)} %add_add_fusion.1), channel_id=1, source_target_pairs={{0,4},{1,5},{2,6},{3,7},{4,0},{5,1},{6,2},{7,3},{8,12},{9,13},{10,... | collective-permute-start | bytes 200 | tf_op jit(solution)/shard_map/ppermute | solution.py:31
  123.7 4.5 %collective-permute-start.18 = (f32[2,8]{1,0:T(2,128)S(1)}, f32[2,8]{1,0:T(2,128)S(1)}, u32[]{:S(2)}, u32[]{:S(2)}) collective-permute-start(f32[2,8]{1,0:T(2,128)S(1)} %add_add_fusion.1), channel_id=1, source_target_pairs={{0,8},{1,9},{2,10},{3,11},{4,12},{5,13},{6,14},{7,15},{8,0},{9,1},... | collective-permute-start | bytes 200 | tf_op jit(solution)/shard_map/ppermute | solution.py:31
  125.7 5.4 %collective-permute-start.19 = (f32[2,8]{1,0:T(2,128)S(1)}, f32[2,8]{1,0:T(2,128)S(1)}, u32[]{:S(2)}, u32[]{:S(2)}) collective-permute-start(f32[2,8]{1,0:T(2,128)S(1)} %add_add_fusion.1), channel_id=1, source_target_pairs={{0,12},{1,13},{2,14},{3,15},{4,8},{5,9},{6,10},{7,11},{8,4},{9,5},... | collective-permute-start | bytes 200 | tf_op jit(solution)/shard_map/ppermute | solution.py:31
  (5 other events, 7.6 us)

commit v7 on v6

--- a/solution.py
+++ b/solution.py
@@ -130,19 +130,20 @@
     )(first, second, after)
 
 
-def mark_kernel(give_ref, out_ref):
-    out_ref[...] = give_ref[:, :out_ref.shape[1]]
-
-
-def mark(give):
-    return pl.pallas_call(
-        mark_kernel,
-        in_specs=in_vmem(1),
-        out_specs=in_vmem(1)[0],
-        out_shape=jax.ShapeDtypeStruct((give.shape[0], LANES), give.dtype),
-        compiler_params=params(16),
+def gate_kernel(*_):
+    pass
+
+
+def gate(array, after):
+    return pl.pallas_call(
+        gate_kernel,
+        in_specs=in_place(1 + len(after)),
+        out_specs=in_place(1)[0],
+        out_shape=jax.ShapeDtypeStruct(array.shape, array.dtype),
+        input_output_aliases={0: 0},
+        compiler_params=params(1),
         cost_estimate=pl.CostEstimate(flops=0, bytes_accessed=1, transcendentals=0),
-    )(give)
+    )(array, *after)
 
 
 def cut_grads_kernel(ids_ref, grad_ref, _, out_ref):
@@ -170,9 +171,8 @@
     )(ids, grads, after)
 
 
-def rotate_kernel(order, *refs):
+def rotate_kernel(*refs):
     act_refs, (basis_ref, out_ref, held_ref, sems) = refs[:-4], refs[-4:]
-    act_refs = [act_refs[n].at[at:at + size, :] for n, at, size in order]
     depth, width = basis_ref.shape
     places = [slice(k * depth, (k + 1) * depth) for k in range(width // depth)]
     copies = [
@@ -184,20 +184,19 @@
     for k, cols in enumerate(places):
         act = jnp.concatenate([ref[:, cols] for ref in act_refs], axis=0)
         copies[k].wait()
-        out_ref[:, cols] = jnp.dot(
-            act, held_ref[k], preferred_element_type=jnp.float32
-        ).astype(jnp.bfloat16)
-
-
-def rotate(act_pieces, order, basis):
+        turned = jnp.dot(act, held_ref[k], preferred_element_type=jnp.float32)
+        out_ref[cols, :] = turned.astype(jnp.bfloat16).T
+
+
+def rotate(act_pieces, basis):
     tokens = sum(x.shape[0] for x in act_pieces)
     depth, width = basis.shape
     count = width // depth
     return pl.pallas_call(
-        functools.partial(rotate_kernel, order),
+        rotate_kernel,
         in_specs=in_vmem(len(act_pieces)) + in_place(1),
         out_specs=in_vmem(1)[0],
-        out_shape=jax.ShapeDtypeStruct((tokens, width), jnp.bfloat16),
+        out_shape=jax.ShapeDtypeStruct((width, tokens), jnp.bfloat16),
         scratch_shapes=[
             pltpu.VMEM((count, depth, depth), jnp.bfloat16),
             pltpu.SemaphoreType.DMA((count,)),
@@ -213,10 +212,8 @@
     left_refs, half_refs = refs[:batch_count], refs[batch_count:3 * batch_count]
     eig_ref, out_ref, right_ref, turn_ref, pre_a, pre_b = refs[3 * batch_count:]
     rows, width = eig_ref.shape
-    half = pre_a.shape[0] // batch_count
     chunk = pre_a.shape[1]
-    per = width // chunk
-    phases = (rows // half) * per
+    phases = width // chunk
     tile = min(256, chunk)
 
     @pl.when(pl.program_id(0) == 0)
@@ -229,60 +226,42 @@
 
     for b in range(batch_count):
         turn_ref[b] = left_refs[b][...].T
-    out_ref[...] = jnp.zeros_like(out_ref)
-
-    def place(k):
-        return pl.multiple_of((k // per) * half, half), (k % per) * chunk
 
     def produce(k, s, pre):
-        row, col = place(k)
-        cols = pl.ds(pl.multiple_of(col + s * tile, tile), tile)
-        part = min(128, half)
-        for at in range(0, half, part):
-            some = pl.ds(pl.multiple_of(row + at, part), part)
-            damped = eig_ref[some, cols].astype(jnp.float32) + damping
-            inverse = pl.reciprocal(damped, approx=True)
-            for b in range(batch_count):
-                outer_sum = jnp.dot(
-                    turn_ref[b, some, :], right_ref[b, :, cols], preferred_element_type=jnp.float32
-                )
-                pre[b * half + at:b * half + at + part, s * tile:(s + 1) * tile] = (
-                    outer_sum * inverse
-                ).astype(jnp.bfloat16)
+        cols = slice(k * chunk + s * tile, k * chunk + (s + 1) * tile)
+        damped = eig_ref[:, cols].astype(jnp.float32) + damping
+        inverse = pl.reciprocal(damped, approx=True)
+        for b in range(batch_count):
+            outer_sum = jnp.dot(
+                turn_ref[b], right_ref[b, :, cols], preferred_element_type=jnp.float32
+            )
+            pre[b * rows:(b + 1) * rows, s * tile:(s + 1) * tile] = (
+                outer_sum * inverse
+            ).astype(jnp.bfloat16)
 
     def absorb(k, pre):
-        row, col = place(k)
-        rot = rot_ref[:, pl.ds(pl.multiple_of(col, chunk), chunk)]
+        more = jnp.dot(
+            pre[...], rot_ref[k * chunk:(k + 1) * chunk, :], preferred_element_type=jnp.float32
+        )
         for b in range(batch_count):
-            out_ref[b, :, pl.ds(row, half)] += lax.dot_general(
-                rot, pre[b * half:(b + 1) * half, :], (((1,), (1,)), ((), ())),
-                preferred_element_type=jnp.float32,
-            )
-
-    def both(k, pre_now, pre_next):
-        absorb(k, pre_now)
-        for s in range(chunk // tile):
-            produce(k + 1, s, pre_next)
+            part = more[b * rows:(b + 1) * rows, :]
+            out_ref[b] = part if k == 0 else out_ref[b] + part
 
     for s in range(chunk // tile):
         produce(0, s, pre_a)
-
-    def pair(q, carry):
-        both(2 * q, pre_a, pre_b)
-        both(2 * q + 1, pre_b, pre_a)
-        return carry
-
-    lax.fori_loop(0, phases // 2 - 1, pair, 0)
-    both(phases - 2, pre_a, pre_b)
-    absorb(phases - 1, pre_b)
+    for k in range(phases):
+        now, later = (pre_a, pre_b) if k % 2 == 0 else (pre_b, pre_a)
+        if k + 1 < phases:
+            for s in range(chunk // tile):
+                produce(k + 1, s, later)
+        absorb(k, now)
 
 
 def images(rot, lefts, halves, eigenvalues):
-    batch_count, tokens = len(lefts), rot.shape[0]
+    batch_count, tokens = len(lefts), rot.shape[1]
     hidden, width = eigenvalues.shape
     rows = min(512, hidden)
-    half = min(256, rows)
-    chunk = min(1024, width // 2)
+    chunk = min(1024 if tokens <= 256 else 512, width // 2)
     return pl.pallas_call(
         functools.partial(image_kernel, batch_count),
         grid=(hidden // rows,),
@@ -290,15 +269,15 @@
         + [pl.BlockSpec((QT, rows), lambda i: (0, i)) for x in lefts]
         + [whole_block(x.shape) for x in halves]
         + [pl.BlockSpec((rows, width), lambda i: (i, 0))],
-        out_specs=pl.BlockSpec((batch_count, tokens, rows), lambda i: (0, 0, i)),
-        out_shape=jax.ShapeDtypeStruct((batch_count, tokens, hidden), jnp.float32),
+        out_specs=pl.BlockSpec((batch_count, rows, tokens), lambda i: (0, i, 0)),
+        out_shape=jax.ShapeDtypeStruct((batch_count, hidden, tokens), jnp.float32),
         scratch_shapes=[
             pltpu.VMEM((batch_count, QT, width), jnp.bfloat16),
             pltpu.VMEM((batch_count, rows, QT), jnp.bfloat16),
-            pltpu.VMEM((batch_count * half, chunk), jnp.bfloat16),
-            pltpu.VMEM((batch_count * half, chunk), jnp.bfloat16),
+            pltpu.VMEM((batch_count * rows, chunk), jnp.bfloat16),
+            pltpu.VMEM((batch_count * rows, chunk), jnp.bfloat16),
         ],
-        compiler_params=params(32 if tokens <= 256 else 56),
+        compiler_params=params(50),
         cost_estimate=pl.CostEstimate(
             flops=2 * hidden * width * (tokens + 256) * batch_count,
             bytes_accessed=2 * hidden * width,
@@ -307,7 +286,7 @@
     )(rot, *lefts, *halves, eigenvalues)
 
 
-def score_kernel(batch_count, grad_ref, basis_ref, image_ref, ids_ref, out_ref, token_ref):
+def score_kernel(batch_count, ranks, grad_ref, basis_ref, image_ref, ids_ref, out_ref, token_ref):
     step = pl.program_id(0)
     me = lax.axis_index("wide")
 
@@ -315,47 +294,46 @@
     def _():
         token_ref[...] = jnp.zeros_like(token_ref)
 
-    order = [me ^ r for r in range(grad_ref.shape[0])]
-    grads = jnp.concatenate([grad_ref[n] for n in order], axis=0)
+    grads = jnp.concatenate([grad_ref[me ^ r] for r in ranks], axis=0)
     turned = jnp.dot(grads, basis_ref[...], preferred_element_type=jnp.float32)
-    turned = turned.astype(jnp.bfloat16).astype(jnp.float32)
+    turned = turned.astype(jnp.bfloat16).T.astype(jnp.float32)
     for b in range(batch_count):
-        token_ref[b] += jnp.sum(image_ref[b] * turned, axis=1, keepdims=True)
+        token_ref[b:b + 1, :] += jnp.sum(image_ref[b] * turned, axis=0, keepdims=True)
 
     @pl.when(step == pl.num_programs(0) - 1)
     def _():
-        ids = jnp.concatenate([ids_ref[n] for n in order], axis=0).astype(jnp.float32)
+        ids = jnp.concatenate([ids_ref[me ^ r] for r in ranks], axis=0).astype(jnp.float32)
         seqs = lax.broadcasted_iota(jnp.int32, ids.shape, 1).astype(jnp.float32)
-        member = ids == seqs
+        member = jnp.where(ids == seqs, 1.0, 0.0).T
         for b in range(batch_count):
-            sums = jnp.sum(jnp.where(member, token_ref[b], 0.0), axis=0, keepdims=True)
-            out_ref[b:b + 1, :] = sums[:, :out_ref.shape[1]]
-
-
-def score_parts(grads, grad_basis, image, seq_count):
-    batch_count, tokens = image.shape[:2]
+            sums = jnp.sum(member * token_ref[b:b + 1, :], axis=1, keepdims=True)
+            out_ref[b] = sums[:out_ref.shape[1], :]
+
+
+def score_parts(grads, ranks, grad_basis, image, seq_count):
+    batch_count, _, tokens = image.shape
     count, rows, width = grads.shape
     hidden = width - LANES
     inner = min(grad_basis.shape[0], hidden)
     return pl.pallas_call(
-        functools.partial(score_kernel, batch_count),
+        functools.partial(score_kernel, batch_count, ranks),
         grid=(hidden // inner,),
         in_specs=[
             pl.BlockSpec((count, rows, inner), lambda i: (0, 0, i)),
             pl.BlockSpec((grad_basis.shape[0], inner), lambda i: (0, i)),
-            pl.BlockSpec((batch_count, tokens, inner), lambda i: (0, 0, i)),
+            pl.BlockSpec((batch_count, inner, tokens), lambda i: (0, i, 0)),
             pl.BlockSpec((count, rows, LANES), lambda i: (0, 0, hidden // LANES)),
         ],
-        out_specs=pl.BlockSpec((batch_count, seq_count), lambda i: (0, 0)),
-        out_shape=jax.ShapeDtypeStruct((batch_count, seq_count), jnp.float32),
-        scratch_shapes=[pltpu.VMEM((batch_count, tokens, 1), jnp.float32)],
-        compiler_params=params(44),
+        out_specs=pl.BlockSpec((batch_count, seq_count, 1), lambda i: (0, 0, 0)),
+        out_shape=jax.ShapeDtypeStruct((batch_count, seq_count, 1), jnp.float32),
+        scratch_shapes=[pltpu.VMEM((8, tokens), jnp.float32)],
+        compiler_params=params(56),
         cost_estimate=pl.CostEstimate(
             flops=2 * tokens * hidden * grad_basis.shape[0],
             bytes_accessed=4 * image.size,
             transcendentals=0,
         ),
-    )(grads, grad_basis, image, grads)
+    )(grads, grad_basis, image, grads)[:, :, 0]
 
 
 def per_device(
@@ -381,35 +359,43 @@
     keep, give, flags = cut_factors(owners, query_factors, order, hidden)
     count = wide_count // 2
     after = []
+    pieces = []
     for step, bit in enumerate(bits):
         got = swap(give, "wide", bit)
         keep, give = pick(flags, keep, got, step, cols, count, after)
         count //= 2
         after = []
-        if step < len(far):
+        if step < len(far) - 1:
             acts = join(acts, swap(acts, "wide", far[step]), give)
             ranks = ranks + [r + far[step] for r in ranks]
             after = [acts]
-        if step == len(bits) - 2:
-            sent = cut_grads(seq_ids, train_grad, swap(mark(give), "wide", 1), wide_count)
-            grads = lax.all_to_all(sent, "wide", 0, 0)
+        elif step == len(far) - 1:
+            last = swap(acts, "wide", far[step])
+            held = gate(acts, [give])
+            pieces = [(acts, ranks), (swap(held, "wide", 2), [r + 2 for r in ranks])]
+            after = [held]
+        elif step == len(far):
+            ranks = [r + far[-1] for r in ranks]
+            held = gate(last, [give])
+            pieces += [(held, ranks), (swap(held, "wide", 2), [r + 2 for r in ranks])]
+            sent = cut_grads(seq_ids, train_grad, give, wide_count)
     left, right = keep, give
-    pieces = [(acts, ranks)]
-    for bit in (2, 1):
-        pieces += [(swap(x, "wide", bit), [r + bit for r in has]) for x, has in pieces]
-    token_order = [None] * wide_count
-    for n, (_, has) in enumerate(pieces):
-        for at, r in enumerate(has):
-            token_order[r] = (n, at * tok_local, tok_local)
-    rot = rotate([x for x, _ in pieces], token_order, act_basis)
+    for n in (1, 3):
+        pieces[n] = (gate(pieces[n][0], [right]), pieces[n][1])
+    pieces += [(swap(x, "wide", 1), [r + 1 for r in has]) for x, has in pieces]
+    rot = rotate([x for x, _ in pieces], act_basis)
+    ranks = [r for _, has in pieces for r in has]
 
     lefts = [left, swap(left, "groups", 1)]
+    other = swap(right, "groups", 1)
     halves = []
-    for x in (right, swap(right, "groups", 1)):
+    for x in (right, other):
         halves += [x, swap(x, "wide", 1)]
 
+    grads = lax.all_to_all(gate(sent, [rot, other]), "wide", 0, 0)
+
     image = images(rot, lefts, halves, eigenvalues)
-    parts = score_parts(grads, grad_basis, image, seq_count)
+    parts = score_parts(grads, ranks, grad_basis, image, seq_count)
     for near in (bits[:2], bits[2:]):
         step = near[0]
         others = [swap(parts, "wide", step * n) for n in range(1, 1 << len(near))]

time: 132 us -> 98.1 us (0.74)
  waiting for transfers between devices: 62.6 us -> 30.9 us
  local copies, waits for them, and re-layouts: 6.48 us -> 2.35 us
    ppermute x20 -> x22, waiting for transfers between devices: 62.6 us -> 30.9 us  [swap(): return lax.ppermute(x, axis, [(i, i ^ bit) for i in range(count)])]
    unnamed x16 -> x11, local copies, waits for them, and re-layouts: 6.48 us -> 2.35 us
    pallas_call x3 -> x7, Pallas kernels: 6.14 us -> 9.55 us  [the longest x1 5.29 us: score_parts(): pl.pallas_call(functools.partial(score_kernel, batch_count, ranks), grid=...]
    pallas_call x1, Pallas kernels: 25.2 us -> 22.1 us  [images(): pl.pallas_call(functools.partial(image_kernel, batch_count), grid=(hidden...]
    ppermute x20 -> x22, starting transfers between devices: 21.2 us -> 22.7 us  [swap(): return lax.ppermute(x, axis, [(i, i ^ bit) for i in range(count)])]
  transfers between devices with their start and end apart: 21 -> 23, of which waited for: 11 -> 9; matrix products, arithmetic and copies ran while one was open for 0% -> 0% of each run, Pallas kernels for 24% -> 29%
where the time goes in v7:
time: 98.1 us; the launch traced here: 97.7 us
  Pallas kernels  34.4 us (35%)
  waiting for transfers between devices  30.9 us (31%)
  starting transfers between devices  28.6 us (29%)
  local copies, waits for them, and re-layouts  2.35 us (2%)
  other arithmetic  1.37 us (1%)
    ppermute x22, waiting for transfers between devices, swap(): return lax.ppermute(x, axis, [(i, i ^ bit) for i in range(count)])  30.9 us
    ppermute x22, starting transfers between devices, swap(): return lax.ppermute(x, axis, [(i, i ^ bit) for i in range(count)])  22.7 us
    pallas_call x1, Pallas kernels, images(): pl.pallas_call(functools.partial(image_kernel, batch_count), grid=(hidden...  22.1 us
    all_to_all x1, starting transfers between devices, per_device(): grads = lax.all_to_all(gate(sent, [rot, other]), 'wide', 0, 0)  5.89 us
    pallas_call x1, Pallas kernels, score_parts(): pl.pallas_call(functools.partial(score_kernel, batch_count, ranks), grid=...  5.29 us
    pallas_call x1, Pallas kernels, rotate(): pl.pallas_call(rotate_kernel, in_specs=in_vmem(len(act_pieces)) + in_plac...  4.25 us
    unnamed x11, local copies, waits for them, and re-layouts  2.35 us
  transfers between devices with their start and end apart: 23, of which 9 were waited for; matrix products, arithmetic and copies ran while one was open for 0% of the time, Pallas kernels for 29%

profile of v7, /device:TPU:0, one launch (start us, length us, event | category | flops | bytes accessed | tf_op | source)
XLA Modules:
  0.0 97.7 jit_solution(5956550158313247065)
XLA Ops:
  0.0 1.7 %copy-done = bf16[2,16,36864]{2,1,0:T(8,128)(2,1)S(1)} copy-done((bf16[2,16,36864]{2,1,0:T(8,128)(2,1)S(1)}, bf16[2,16,36864]{2,1,0:T(8,128)(2,1)}, u32[]{:S(2)}) %copy-start) | copy-done | bytes 2359320
  3.5 1.6 %collective-permute-done.got_ref = bf16[16,18432]{1,0:T(8,128)(2,1)S(1)} collective-permute-done((bf16[16,18432]{1,0:T(8,128)(2,1)S(1)}, bf16[16,18432]{1,0:T(8,128)(2,1)S(1)}, u32[]{:S(2)}, u32[]{:S(2)}) %collective-permute-start) | collective-permute-done | bytes 589856 | tf_op jit(solution)/shard_map/ppermute | solution.py:31
  5.3 3.0 %collective-permute-start.1 = (bf16[16,10240]{1,0:T(8,128)(2,1)S(1)}, bf16[16,10240]{1,0:T(8,128)(2,1)S(1)}, u32[]{:S(2)}, u32[]{:S(2)}) collective-permute-start(bf16[16,10240]{1,0:T(8,128)(2,1)S(1)} %get-tuple-element.20._), channel_id=1, source_target_pairs={{0,2},{1,3},{2,0},{3,1},{4,6},{5,7},{6,4},{7,5},{8,10},{9,11},{10,... | collective-permute-start | bytes 983048 | tf_op jit(solution)/shard_map/ppermute | solution.py:31
  8.2 2.6 %collective-permute-start.2 = (bf16[16,4096]{1,0:T(8,128)(2,1)S(1)}, bf16[16,4096]{1,0:T(8,128)(2,1)S(1)}, u32[]{:S(2)}, u32[]{:S(2)}) collective-permute-start(bf16[16,4096]{1,0:T(8,128)(2,1)S(1)} %copy-done.2), channel_id=1, source_target_pairs={{0,8},{1,9},{2,10},{3,11},{4,12},{5,13},{6,14},{7,15},{8,0},{9,1},... | collective-permute-start | bytes 393224 | tf_op jit(solution)/shard_map/ppermute | solution.py:31
  10.8 6.4 %collective-permute-done.2.second_ref = bf16[16,4096]{1,0:T(8,128)(2,1)S(1)} collective-permute-done((bf16[16,4096]{1,0:T(8,128)(2,1)S(1)}, bf16[16,4096]{1,0:T(8,128)(2,1)S(1)}, u32[]{:S(2)}, u32[]{:S(2)}) %collective-permute-start.2) | collective-permute-done | bytes 131104 | tf_op jit(solution)/shard_map/ppermute | solution.py:31
  18.1 1.4 %collective-permute-start.3 = (bf16[16,6144]{1,0:T(8,128)(2,1)S(1)}, bf16[16,6144]{1,0:T(8,128)(2,1)S(1)}, u32[]{:S(2)}, u32[]{:S(2)}) collective-permute-start(bf16[16,6144]{1,0:T(8,128)(2,1)S(1)} %get-tuple-element.22.__1_), channel_id=1, source_target_pairs={{0,4},{1,5},{2,6},{3,7},{4,0},{5,1},{6,2},{7,3},{8,12},{9,13},{10,... | collective-permute-start | bytes 589832 | tf_op jit(solution)/shard_map/ppermute | solution.py:31
  20.1 8.6 %collective-permute-done.3.got_ref = bf16[16,6144]{1,0:T(8,128)(2,1)S(1)} collective-permute-done((bf16[16,6144]{1,0:T(8,128)(2,1)S(1)}, bf16[16,6144]{1,0:T(8,128)(2,1)S(1)}, u32[]{:S(2)}, u32[]{:S(2)}) %collective-permute-start.3) | collective-permute-done | bytes 196640 | tf_op jit(solution)/shard_map/ppermute | solution.py:31
  28.8 0.8 collective-permute-start.7
  29.7 3.1 %collective-permute-start.5 = (bf16[16,4096]{1,0:T(8,128)(2,1)S(1)}, bf16[16,4096]{1,0:T(8,128)(2,1)S(1)}, u32[]{:S(2)}, u32[]{:S(2)}) collective-permute-start(bf16[16,4096]{1,0:T(8,128)(2,1)S(1)} %get-tuple-element.23._.__1_), channel_id=1, source_target_pairs={{0,8},{1,9},{2,10},{3,11},{4,12},{5,13},{6,14},{7,15},{8,0},{9,1},... | collective-permute-start | bytes 393224 | tf_op jit(solution)/shard_map/ppermute | solution.py:31
  33.3 5.2 %collective-permute-done.5.got_ref = bf16[16,4096]{1,0:T(8,128)(2,1)S(1)} collective-permute-done((bf16[16,4096]{1,0:T(8,128)(2,1)S(1)}, bf16[16,4096]{1,0:T(8,128)(2,1)S(1)}, u32[]{:S(2)}, u32[]{:S(2)}) %collective-permute-start.5) | collective-permute-done | bytes 131104 | tf_op jit(solution)/shard_map/ppermute | solution.py:31
  39.1 1.6 %shard_map.88.__0_ = bf16[16,16,2176]{2,1,0:T(8,128)(2,1)} custom-call(s32[16]{0:T(128)S(1)} %copy-done.4, bf16[16,32768]{1,0:T(8,128)(2,1)S(1)} %copy-done.1, bf16[16,4096]{1,0:T(8,128)(2,1)S(1)} %get-tuple-element.23._.__1_), custom_call_target="tpu_custom_call" | custom-call | bytes 524288 | tf_op jit(solution)/shard_map/pallas_call | solution.py:164
  40.8 1.5 %collective-permute-start.12 = (bf16[16,2048]{1,0:T(8,128)(2,1)S(1)}, bf16[16,2048]{1,0:T(8,128)(2,1)S(1)}, u32[]{:S(2)}, u32[]{:S(2)}) collective-permute-start(bf16[16,2048]{1,0:T(8,128)(2,1)S(1)} %get-tuple-element.25.__1_.refs_2_), channel_id=1, source_target_pairs={{0,16},{16,0},{1,17},{17,1},{2,18},{18,2},{3,19},{19,3},{4,20},{20... | collective-permute-start | bytes 196616 | tf_op jit(solution)/shard_map/ppermute | solution.py:31
  42.3 4.3 %shard_map.93.__1_.rot_ref = bf16[4096,256]{1,0:T(8,128)(2,1)S(1)} custom-call(bf16[32,4096]{1,0:T(8,128)(2,1)S(1)} %shard_map.84.refs_0_, bf16[32,4096]{1,0:T(8,128)(2,1)S(1)} %shard_map.90.refs_1_, bf16[32,4096]{1,0:T(8,128)(2,1)S(1)} %shard_map.91.refs_2_, bf16[32,4096]{1,0:T(8,128)(2,1)S(1)} %shard_map.92.refs_3_, ...), custom_call_target="tpu_custom_call" | custom-call | flops 1073741824 | bytes 2097152 | tf_op jit(solution)/shard_map/pallas_call | solution.py:195
  46.6 5.9 %all-to-all-start = ((bf16[16,16,2176]{2,1,0:T(8,128)(2,1)}), bf16[16,16,2176]{2,1,0:T(8,128)(2,1)}, u32[]{:S(2)}, u32[]{:S(2)}) async-start(bf16[16,16,2176]{2,1,0:T(8,128)(2,1)} %shard_map.94), calls=%async_computation | async-start | bytes 2228224 | tf_op jit(solution)/shard_map/all_to_all | solution.py:395
  53.6 3.2 %collective-permute-done.13.refs_1_ = bf16[16,2048]{1,0:T(8,128)(2,1)S(1)} collective-permute-done((bf16[16,2048]{1,0:T(8,128)(2,1)S(1)}, bf16[16,2048]{1,0:T(8,128)(2,1)S(1)}, u32[]{:S(2)}, u32[]{:S(2)}) %collective-permute-start.13) | collective-permute-done | bytes 65568 | tf_op jit(solution)/shard_map/ppermute | solution.py:31
  56.8 22.1 %shard_map.95.image_ref = f32[2,2048,256]{2,1,0:T(8,128)} custom-call(bf16[4096,256]{1,0:T(8,128)(2,1)S(1)} %shard_map.93.__1_.rot_ref, bf16[16,2048]{1,0:T(8,128)(2,1)S(1)} %get-tuple-element.26.refs_0_, bf16[16,2048]{1,0:T(8,128)(2,1)S(1)} %collective-permute-done.13.refs_1_, bf16[16,2048]{1,0:T(8,128)(2,1)S(1)} %get-tuple-element.25.__1_.refs_2_, ...), custom_call_target="tpu_custom_call" | custom-call | flops 17179869184 | bytes 16777216 | tf_op jit(solution)/shard_map/pallas_call | solution.py:265
  78.9 5.3 %shard_map.96 = f32[2,8,1]{2,1,0:T(8,128)} custom-call(bf16[16,16,2176]{2,1,0:T(8,128)(2,1)} %all-to-all-done.grad_ref.ids_ref, bf16[512,2048]{1,0:T(8,128)(2,1)} %basis_ref.1, f32[2,2048,256]{2,1,0:T(8,128)} %shard_map.95.image_ref, bf16[16,16,2176]{2,1,0:T(8,128)(2,1)} %all-to-all-done.grad_ref.ids_ref), custom_call_target="tpu_custom_call" | custom-call | flops 536870912 | bytes 4194304 | tf_op jit(solution)/shard_map/pallas_call | solution.py:318
  85.0 0.8 collective-permute-start.18
  85.8 1.0 %collective-permute-start.17 = (f32[2,8]{1,0:T(2,128)S(1)}, f32[2,8]{1,0:T(2,128)S(1)}, u32[]{:S(2)}, u32[]{:S(2)}) collective-permute-start(f32[2,8]{1,0:T(2,128)S(1)} %reduce), channel_id=1, source_target_pairs={{0,2},{1,3},{2,0},{3,1},{4,6},{5,7},{6,4},{7,5},{8,10},{9,11},{10,... | collective-permute-start | bytes 200 | tf_op jit(solution)/shard_map/ppermute | solution.py:31
  86.9 1.1 %collective-permute-done.18 = f32[2,8]{1,0:T(2,128)S(1)} collective-permute-done((f32[2,8]{1,0:T(2,128)S(1)}, f32[2,8]{1,0:T(2,128)S(1)}, u32[]{:S(2)}, u32[]{:S(2)}) %collective-permute-start.18) | collective-permute-done | bytes 96 | tf_op jit(solution)/shard_map/ppermute | solution.py:31
  88.0 1.4 %collective-permute-done.17 = f32[2,8]{1,0:T(2,128)S(1)} collective-permute-done((f32[2,8]{1,0:T(2,128)S(1)}, f32[2,8]{1,0:T(2,128)S(1)}, u32[]{:S(2)}, u32[]{:S(2)}) %collective-permute-start.17) | collective-permute-done | bytes 96 | tf_op jit(solution)/shard_map/ppermute | solution.py:31
  89.3 3.3 %collective-permute-start.21 = (f32[2,8]{1,0:T(2,128)S(1)}, f32[2,8]{1,0:T(2,128)S(1)}, u32[]{:S(2)}, u32[]{:S(2)}) collective-permute-start(f32[2,8]{1,0:T(2,128)S(1)} %add_add_fusion.1), channel_id=1, source_target_pairs={{0,12},{1,13},{2,14},{3,15},{4,8},{5,9},{6,10},{7,11},{8,4},{9,5},... | collective-permute-start | bytes 200 | tf_op jit(solution)/shard_map/ppermute | solution.py:31
  93.8 1.0 %collective-permute-done.21 = f32[2,8]{1,0:T(2,128)S(1)} collective-permute-done((f32[2,8]{1,0:T(2,128)S(1)}, f32[2,8]{1,0:T(2,128)S(1)}, u32[]{:S(2)}, u32[]{:S(2)}) %collective-permute-start.21) | collective-permute-done | bytes 96 | tf_op jit(solution)/shard_map/ppermute | solution.py:31
  94.8 2.4 %collective-permute-done.20 = f32[2,8]{1,0:T(2,128)S(1)} collective-permute-done((f32[2,8]{1,0:T(2,128)S(1)}, f32[2,8]{1,0:T(2,128)S(1)}, u32[]{:S(2)}, u32[]{:S(2)}) %collective-permute-start.20) | collective-permute-done | bytes 96 | tf_op jit(solution)/shard_map/ppermute | solution.py:31
  (53 shorter events, 8.4 us)
Async XLA Ops:
  3.0 2.1 %collective-permute-start = (bf16[16,18432]{1,0:T(8,128)(2,1)S(1)}, bf16[16,18432]{1,0:T(8,128)(2,1)S(1)}, u32[]{:S(2)}, u32[]{:S(2)}) collective-permute-start(bf16[16,18432]{1,0:T(8,128)(2,1)S(1)} %get-tuple-element.18), channel_id=1, source_target_pairs={{0,1},{1,0},{2,3},{3,2},{4,5},{5,4},{6,7},{7,6},{8,9},{9,8},{10,11... | collective-permute-start | bytes 1769480 | tf_op jit(solution)/shard_map/ppermute | solution.py:31
  5.3 12.7 %collective-permute-start.1 = (bf16[16,10240]{1,0:T(8,128)(2,1)S(1)}, bf16[16,10240]{1,0:T(8,128)(2,1)S(1)}, u32[]{:S(2)}, u32[]{:S(2)}) collective-permute-start(bf16[16,10240]{1,0:T(8,128)(2,1)S(1)} %get-tuple-element.20._), channel_id=1, source_target_pairs={{0,2},{1,3},{2,0},{3,1},{4,6},{5,7},{6,4},{7,5},{8,10},{9,11},{10,... | collective-permute-start | bytes 983048 | tf_op jit(solution)/shard_map/ppermute | solution.py:31
  8.2 9.0 %collective-permute-start.2 = (bf16[16,4096]{1,0:T(8,128)(2,1)S(1)}, bf16[16,4096]{1,0:T(8,128)(2,1)S(1)}, u32[]{:S(2)}, u32[]{:S(2)}) collective-permute-start(bf16[16,4096]{1,0:T(8,128)(2,1)S(1)} %copy-done.2), channel_id=1, source_target_pairs={{0,8},{1,9},{2,10},{3,11},{4,12},{5,13},{6,14},{7,15},{8,0},{9,1},... | collective-permute-start | bytes 393224 | tf_op jit(solution)/shard_map/ppermute | solution.py:31
  17.2 11.6 %collective-permute-start.6 = (bf16[32,4096]{1,0:T(8,128)(2,1)S(1)}, bf16[32,4096]{1,0:T(8,128)(2,1)S(1)}, u32[]{:S(2)}, u32[]{:S(2)}) collective-permute-start(bf16[32,4096]{1,0:T(8,128)(2,1)S(1)} %shard_map.84.refs_0_), channel_id=1, source_target_pairs={{0,4},{1,5},{2,6},{3,7},{4,0},{5,1},{6,2},{7,3},{8,12},{9,13},{10,... | collective-permute-start | bytes 786440 | tf_op jit(solution)/shard_map/ppermute | solution.py:31
  18.1 21.0 %copy-start.1 = (bf16[16,32768]{1,0:T(8,128)(2,1)S(1)}, bf16[16,32768]{1,0:T(8,128)(2,1)}, u32[]{:S(2)}) copy-start(bf16[16,32768]{1,0:T(8,128)(2,1)} %grad_ref.1) | copy-start | bytes 3145732
  18.1 10.6 %collective-permute-start.3 = (bf16[16,6144]{1,0:T(8,128)(2,1)S(1)}, bf16[16,6144]{1,0:T(8,128)(2,1)S(1)}, u32[]{:S(2)}, u32[]{:S(2)}) collective-permute-start(bf16[16,6144]{1,0:T(8,128)(2,1)S(1)} %get-tuple-element.22.__1_), channel_id=1, source_target_pairs={{0,4},{1,5},{2,6},{3,7},{4,0},{5,1},{6,2},{7,3},{8,12},{9,13},{10,... | collective-permute-start | bytes 589832 | tf_op jit(solution)/shard_map/ppermute | solution.py:31
  19.6 18.9 %collective-permute-start.4 = (bf16[32,4096]{1,0:T(8,128)(2,1)S(1)}, bf16[32,4096]{1,0:T(8,128)(2,1)S(1)}, u32[]{:S(2)}, u32[]{:S(2)}) collective-permute-start(bf16[32,4096]{1,0:T(8,128)(2,1)S(1)} %shard_map.86.refs_0_), channel_id=1, source_target_pairs={{0,2},{1,3},{2,0},{3,1},{4,6},{5,7},{6,4},{7,5},{8,10},{9,11},{10,... | collective-permute-start | bytes 786440 | tf_op jit(solution)/shard_map/ppermute | solution.py:31
  28.8 9.8 %collective-permute-start.7 = (bf16[32,4096]{1,0:T(8,128)(2,1)S(1)}, bf16[32,4096]{1,0:T(8,128)(2,1)S(1)}, u32[]{:S(2)}, u32[]{:S(2)}) collective-permute-start(bf16[32,4096]{1,0:T(8,128)(2,1)S(1)} %shard_map.91.refs_2_), channel_id=1, source_target_pairs={{0,2},{1,3},{2,0},{3,1},{4,6},{5,7},{6,4},{7,5},{8,10},{9,11},{10,... | collective-permute-start | bytes 786440 | tf_op jit(solution)/shard_map/ppermute | solution.py:31
  29.7 8.7 %collective-permute-start.5 = (bf16[16,4096]{1,0:T(8,128)(2,1)S(1)}, bf16[16,4096]{1,0:T(8,128)(2,1)S(1)}, u32[]{:S(2)}, u32[]{:S(2)}) collective-permute-start(bf16[16,4096]{1,0:T(8,128)(2,1)S(1)} %get-tuple-element.23._.__1_), channel_id=1, source_target_pairs={{0,8},{1,9},{2,10},{3,11},{4,12},{5,13},{6,14},{7,15},{8,0},{9,1},... | collective-permute-start | bytes 393224 | tf_op jit(solution)/shard_map/ppermute | solution.py:31
  32.7 9.5 %collective-permute-start.8 = (bf16[32,4096]{1,0:T(8,128)(2,1)S(1)}, bf16[32,4096]{1,0:T(8,128)(2,1)S(1)}, u32[]{:S(2)}, u32[]{:S(2)}) collective-permute-start(bf16[32,4096]{1,0:T(8,128)(2,1)S(1)} %shard_map.84.refs_0_), channel_id=1, source_target_pairs={{0,1},{1,0},{2,3},{3,2},{4,5},{5,4},{6,7},{7,6},{8,9},{9,8},{10,11... | collective-permute-start | bytes 786440 | tf_op jit(solution)/shard_map/ppermute | solution.py:31
  32.8 9.5 %collective-permute-start.10 = (bf16[32,4096]{1,0:T(8,128)(2,1)S(1)}, bf16[32,4096]{1,0:T(8,128)(2,1)S(1)}, u32[]{:S(2)}, u32[]{:S(2)}) collective-permute-start(bf16[32,4096]{1,0:T(8,128)(2,1)S(1)} %shard_map.91.refs_2_), channel_id=1, source_target_pairs={{0,1},{1,0},{2,3},{3,2},{4,5},{5,4},{6,7},{7,6},{8,9},{9,8},{10,11... | collective-permute-start | bytes 786440 | tf_op jit(solution)/shard_map/ppermute | solution.py:31
  38.5 3.7 %collective-permute-start.9 = (bf16[32,4096]{1,0:T(8,128)(2,1)S(1)}, bf16[32,4096]{1,0:T(8,128)(2,1)S(1)}, u32[]{:S(2)}, u32[]{:S(2)}) collective-permute-start(bf16[32,4096]{1,0:T(8,128)(2,1)S(1)} %shard_map.90.refs_1_), channel_id=1, source_target_pairs={{0,1},{1,0},{2,3},{3,2},{4,5},{5,4},{6,7},{7,6},{8,9},{9,8},{10,11... | collective-permute-start | bytes 786440 | tf_op jit(solution)/shard_map/ppermute | solution.py:31
  38.6 3.6 %collective-permute-start.11 = (bf16[32,4096]{1,0:T(8,128)(2,1)S(1)}, bf16[32,4096]{1,0:T(8,128)(2,1)S(1)}, u32[]{:S(2)}, u32[]{:S(2)}) collective-permute-start(bf16[32,4096]{1,0:T(8,128)(2,1)S(1)} %shard_map.92.refs_3_), channel_id=1, source_target_pairs={{0,1},{1,0},{2,3},{3,2},{4,5},{5,4},{6,7},{7,6},{8,9},{9,8},{10,11... | collective-permute-start | bytes 786440 | tf_op jit(solution)/shard_map/ppermute | solution.py:31
  40.8 5.8 %collective-permute-start.12 = (bf16[16,2048]{1,0:T(8,128)(2,1)S(1)}, bf16[16,2048]{1,0:T(8,128)(2,1)S(1)}, u32[]{:S(2)}, u32[]{:S(2)}) collective-permute-start(bf16[16,2048]{1,0:T(8,128)(2,1)S(1)} %get-tuple-element.25.__1_.refs_2_), channel_id=1, source_target_pairs={{0,16},{16,0},{1,17},{17,1},{2,18},{18,2},{3,19},{19,3},{4,20},{20... | collective-permute-start | bytes 196616 | tf_op jit(solution)/shard_map/ppermute | solution.py:31
  46.6 32.3 %all-to-all-start = ((bf16[16,16,2176]{2,1,0:T(8,128)(2,1)}), bf16[16,16,2176]{2,1,0:T(8,128)(2,1)}, u32[]{:S(2)}, u32[]{:S(2)}) async-start(bf16[16,16,2176]{2,1,0:T(8,128)(2,1)} %shard_map.94), calls=%async_computation | async-start | bytes 2228224 | tf_op jit(solution)/shard_map/all_to_all | solution.py:395
  52.5 4.4 %collective-permute-start.13 = (bf16[16,2048]{1,0:T(8,128)(2,1)S(1)}, bf16[16,2048]{1,0:T(8,128)(2,1)S(1)}, u32[]{:S(2)}, u32[]{:S(2)}) collective-permute-start(bf16[16,2048]{1,0:T(8,128)(2,1)S(1)} %get-tuple-element.26.refs_0_), channel_id=1, source_target_pairs={{0,16},{16,0},{1,17},{17,1},{2,18},{18,2},{3,19},{19,3},{4,20},{20... | collective-permute-start | bytes 196616 | tf_op jit(solution)/shard_map/ppermute | solution.py:31
  53.1 3.8 %collective-permute-start.14 = (bf16[16,2048]{1,0:T(8,128)(2,1)S(1)}, bf16[16,2048]{1,0:T(8,128)(2,1)S(1)}, u32[]{:S(2)}, u32[]{:S(2)}) collective-permute-start(bf16[16,2048]{1,0:T(8,128)(2,1)S(1)} %get-tuple-element.25.__1_.refs_2_), channel_id=1, source_target_pairs={{0,1},{1,0},{2,3},{3,2},{4,5},{5,4},{6,7},{7,6},{8,9},{9,8},{10,11... | collective-permute-start | bytes 196616 | tf_op jit(solution)/shard_map/ppermute | solution.py:31
  53.1 3.7 %collective-permute-start.15 = (bf16[16,2048]{1,0:T(8,128)(2,1)S(1)}, bf16[16,2048]{1,0:T(8,128)(2,1)S(1)}, u32[]{:S(2)}, u32[]{:S(2)}) collective-permute-start(bf16[16,2048]{1,0:T(8,128)(2,1)S(1)} %collective-permute-done.12.__2_.refs_4_), channel_id=1, source_target_pairs={{0,1},{1,0},{2,3},{3,2},{4,5},{5,4},{6,7},{7,6},{8,9},{9,8},{10,11... | collective-permute-start | bytes 196616 | tf_op jit(solution)/shard_map/ppermute | solution.py:31
  85.0 3.0 %collective-permute-start.18 = (f32[2,8]{1,0:T(2,128)S(1)}, f32[2,8]{1,0:T(2,128)S(1)}, u32[]{:S(2)}, u32[]{:S(2)}) collective-permute-start(f32[2,8]{1,0:T(2,128)S(1)} %reduce), channel_id=1, source_target_pairs={{0,3},{1,2},{2,1},{3,0},{4,7},{5,6},{6,5},{7,4},{8,11},{9,10},{10,... | collective-permute-start | bytes 200 | tf_op jit(solution)/shard_map/ppermute | solution.py:31
  85.8 3.6 %collective-permute-start.17 = (f32[2,8]{1,0:T(2,128)S(1)}, f32[2,8]{1,0:T(2,128)S(1)}, u32[]{:S(2)}, u32[]{:S(2)}) collective-permute-start(f32[2,8]{1,0:T(2,128)S(1)} %reduce), channel_id=1, source_target_pairs={{0,2},{1,3},{2,0},{3,1},{4,6},{5,7},{6,4},{7,5},{8,10},{9,11},{10,... | collective-permute-start | bytes 200 | tf_op jit(solution)/shard_map/ppermute | solution.py:31
  86.8 2.5 %collective-permute-start.16 = (f32[2,8]{1,0:T(2,128)S(1)}, f32[2,8]{1,0:T(2,128)S(1)}, u32[]{:S(2)}, u32[]{:S(2)}) collective-permute-start(f32[2,8]{1,0:T(2,128)S(1)} %reduce), channel_id=1, source_target_pairs={{0,1},{1,0},{2,3},{3,2},{4,5},{5,4},{6,7},{7,6},{8,9},{9,8},{10,11... | collective-permute-start | bytes 200 | tf_op jit(solution)/shard_map/ppermute | solution.py:31
  89.3 5.4 %collective-permute-start.21 = (f32[2,8]{1,0:T(2,128)S(1)}, f32[2,8]{1,0:T(2,128)S(1)}, u32[]{:S(2)}, u32[]{:S(2)}) collective-permute-start(f32[2,8]{1,0:T(2,128)S(1)} %add_add_fusion.1), channel_id=1, source_target_pairs={{0,12},{1,13},{2,14},{3,15},{4,8},{5,9},{6,10},{7,11},{8,4},{9,5},... | collective-permute-start | bytes 200 | tf_op jit(solution)/shard_map/ppermute | solution.py:31
  92.7 4.5 %collective-permute-start.20 = (f32[2,8]{1,0:T(2,128)S(1)}, f32[2,8]{1,0:T(2,128)S(1)}, u32[]{:S(2)}, u32[]{:S(2)}) collective-permute-start(f32[2,8]{1,0:T(2,128)S(1)} %add_add_fusion.1), channel_id=1, source_target_pairs={{0,8},{1,9},{2,10},{3,11},{4,12},{5,13},{6,14},{7,15},{8,0},{9,1},... | collective-permute-start | bytes 200 | tf_op jit(solution)/shard_map/ppermute | solution.py:31
  93.2 4.0 %collective-permute-start.19 = (f32[2,8]{1,0:T(2,128)S(1)}, f32[2,8]{1,0:T(2,128)S(1)}, u32[]{:S(2)}, u32[]{:S(2)}) collective-permute-start(f32[2,8]{1,0:T(2,128)S(1)} %add_add_fusion.1), channel_id=1, source_target_pairs={{0,4},{1,5},{2,6},{3,7},{4,0},{5,1},{6,2},{7,3},{8,12},{9,13},{10,... | collective-permute-start | bytes 200 | tf_op jit(solution)/shard_map/ppermute | solution.py:31
  (4 other events, 29.3 us)

commit v8 on v7

--- a/solution.py
+++ b/solution.py
@@ -43,7 +43,7 @@
     return [pl.BlockSpec(memory_space=pl.ANY)] * n
 
 
-def cut_factors_kernel(order, hidden, batch_count, owners_ref, fac_ref, keep_ref, give_ref, flag_ref):
+def cut_factors_kernel(order, hidden, batch_count, fac_ref, keep_ref, give_ref):
     cols = hidden // len(order)
     half = (fac_ref.shape[2] - hidden) // 2
     me, batch = lax.axis_index("wide"), lax.rem(lax.axis_index("groups"), batch_count)
@@ -54,26 +54,41 @@
             out_ref[:, at * cols:(at + 1) * cols] = fac_ref[batch, :, pl.ds(src, cols)]
         src = pl.multiple_of(hidden + ((me & 1) ^ part) * half, LANES)
         out_ref[:, len(picked) * cols:] = fac_ref[batch, :, pl.ds(src, half)]
+
+
+def cut_factors(factors, order, hidden, batch_count):
+    rows, width = factors.shape[1:]
+    half = jax.ShapeDtypeStruct((rows, width // 2), factors.dtype)
+    return pl.pallas_call(
+        functools.partial(cut_factors_kernel, order, hidden, batch_count),
+        in_specs=in_vmem(1),
+        out_specs=in_vmem(2),
+        out_shape=[half] * 2,
+        compiler_params=params(16),
+        cost_estimate=pl.CostEstimate(flops=0, bytes_accessed=factors.size, transcendentals=0),
+    )(factors)
+
+
+def flags_kernel(ways, batch_count, owners_ref, _, flag_ref):
+    me, batch = lax.axis_index("wide"), lax.rem(lax.axis_index("groups"), batch_count)
     apart = owners_ref[batch] ^ me
     lane = lax.broadcasted_iota(jnp.int32, flag_ref.shape, 1)
     flags = jnp.zeros(flag_ref.shape, jnp.float32)
-    for step in range(len(order).bit_length() - 1):
-        same = jnp.where((apart & (1 << step)) == 0, 1.0, 0.0)
+    for step, bit in enumerate(ways):
+        same = jnp.where((apart & bit) == 0, 1.0, 0.0)
         flags = jnp.where(lane == step, same, flags)
     flag_ref[...] = flags.astype(flag_ref.dtype)
 
 
-def cut_factors(owners, factors, order, hidden):
-    batch_count, rows, width = owners.shape[0], *factors.shape[1:]
-    half = jax.ShapeDtypeStruct((rows, width // 2), factors.dtype)
-    return pl.pallas_call(
-        functools.partial(cut_factors_kernel, order, hidden, batch_count),
-        in_specs=in_smem(1) + in_vmem(1),
-        out_specs=in_vmem(3),
-        out_shape=[half] * 2 + [jax.ShapeDtypeStruct((rows, LANES), factors.dtype)],
+def owner_flags(owners, ways, after):
+    return pl.pallas_call(
+        functools.partial(flags_kernel, ways, owners.shape[0]),
+        in_specs=in_smem(1) + in_place(1),
+        out_specs=in_vmem(1)[0],
+        out_shape=jax.ShapeDtypeStruct((after.shape[0], LANES), after.dtype),
         compiler_params=params(16),
-        cost_estimate=pl.CostEstimate(flops=0, bytes_accessed=factors.size, transcendentals=0),
-    )(owners, factors)
+        cost_estimate=pl.CostEstimate(flops=0, bytes_accessed=1, transcendentals=0),
+    )(owners, after)
 
 
 def pick_kernel(step, cols, last, flag_ref, keep_ref, got_ref, *refs):
@@ -171,8 +186,8 @@
     )(ids, grads, after)
 
 
-def rotate_kernel(*refs):
-    act_refs, (basis_ref, out_ref, held_ref, sems) = refs[:-4], refs[-4:]
+def rotate_kernel(act_count, *refs):
+    act_refs, (basis_ref, out_ref, held_ref, sems) = refs[:act_count], refs[act_count:]
     depth, width = basis_ref.shape
     places = [slice(k * depth, (k + 1) * depth) for k in range(width // depth)]
     copies = [
@@ -193,83 +208,132 @@
     depth, width = basis.shape
     count = width // depth
     return pl.pallas_call(
-        rotate_kernel,
+        functools.partial(rotate_kernel, len(act_pieces)),
         in_specs=in_vmem(len(act_pieces)) + in_place(1),
-        out_specs=in_vmem(1)[0],
-        out_shape=jax.ShapeDtypeStruct((width, tokens), jnp.bfloat16),
-        scratch_shapes=[
-            pltpu.VMEM((count, depth, depth), jnp.bfloat16),
-            pltpu.SemaphoreType.DMA((count,)),
+        out_specs=in_vmem(2),
+        out_shape=[
+            jax.ShapeDtypeStruct((width, tokens), jnp.bfloat16),
+            jax.ShapeDtypeStruct((count, depth, depth), jnp.bfloat16),
         ],
-        compiler_params=params(48 if tokens <= 256 else 40),
+        scratch_shapes=[pltpu.SemaphoreType.DMA((count,))],
+        compiler_params=params(46 if tokens <= 256 else 32),
         cost_estimate=pl.CostEstimate(
             flops=2 * tokens * width * depth, bytes_accessed=basis.size, transcendentals=0
         ),
     )(*act_pieces, basis)
 
 
-def image_kernel(batch_count, rot_ref, *refs):
+def rotate_rest_kernel(act_count, *refs):
+    act_refs, (held_ref, first_ref, out_ref) = refs[:act_count], refs[act_count:]
+    depth = held_ref.shape[1]
+    done = first_ref.shape[1]
+    out_ref[:, :done] = first_ref[...]
+    for k in range(held_ref.shape[0]):
+        cols = slice(k * depth, (k + 1) * depth)
+        act = jnp.concatenate([ref[:, cols] for ref in act_refs], axis=0)
+        turned = jnp.dot(act, held_ref[k], preferred_element_type=jnp.float32)
+        out_ref[cols, done:] = turned.astype(jnp.bfloat16).T
+
+
+def rotate_rest(act_pieces, held, first):
+    width, done = first.shape
+    tokens = done + sum(x.shape[0] for x in act_pieces)
+    return pl.pallas_call(
+        functools.partial(rotate_rest_kernel, len(act_pieces)),
+        in_specs=in_vmem(len(act_pieces) + 2),
+        out_specs=in_vmem(1)[0],
+        out_shape=jax.ShapeDtypeStruct((width, tokens), jnp.bfloat16),
+        compiler_params=params(16 if tokens <= 256 else 32),
+        cost_estimate=pl.CostEstimate(
+            flops=2 * tokens * held.size, bytes_accessed=held.size, transcendentals=0
+        ),
+    )(*act_pieces, held, first)
+
+
+def image_kernel(batch_count, total, per, rot_ref, *refs):
     left_refs, half_refs = refs[:batch_count], refs[batch_count:3 * batch_count]
     eig_ref, out_ref, right_ref, turn_ref, pre_a, pre_b = refs[3 * batch_count:]
-    rows, width = eig_ref.shape
-    chunk = pre_a.shape[1]
-    phases = width // chunk
+    rows, chunk = eig_ref.shape
     tile = min(256, chunk)
-
-    @pl.when(pl.program_id(0) == 0)
-    def _():
-        side = width // 2
+    s = pl.program_id(0)
+
+    @pl.when(s == 0)
+    def _():
+        side = right_ref.shape[2] // 2
         for b in range(batch_count):
             for other in range(2):
                 at = pl.multiple_of(((lax.axis_index("wide") & 1) ^ other) * side, side)
                 right_ref[b, :, pl.ds(at, side)] = half_refs[2 * b + other][...]
 
-    for b in range(batch_count):
-        turn_ref[b] = left_refs[b][...].T
-
-    def produce(k, s, pre):
-        cols = slice(k * chunk + s * tile, k * chunk + (s + 1) * tile)
-        damped = eig_ref[:, cols].astype(jnp.float32) + damping
-        inverse = pl.reciprocal(damped, approx=True)
+    @pl.when(jnp.logical_and(lax.rem(s, per) == 0, s < total))
+    def _():
         for b in range(batch_count):
-            outer_sum = jnp.dot(
-                turn_ref[b], right_ref[b, :, cols], preferred_element_type=jnp.float32
+            turn_ref[b] = left_refs[b][...].T
+
+    @pl.when(lax.rem(s, per) == 1)
+    def _():
+        out_ref[...] = jnp.zeros_like(out_ref)
+
+    def produce(pre):
+        start = lax.rem(s, per) * chunk
+        for at in range(0, chunk, tile):
+            cols = pl.ds(pl.multiple_of(start + at, tile), tile)
+            damped = eig_ref[:, at:at + tile].astype(jnp.float32) + damping
+            inverse = pl.reciprocal(damped, approx=True)
+            for b in range(batch_count):
+                outer_sum = jnp.dot(
+                    turn_ref[b], right_ref[b, :, cols], preferred_element_type=jnp.float32
+                )
+                pre[b * rows:(b + 1) * rows, at:at + tile] = (
+                    outer_sum * inverse
+                ).astype(jnp.bfloat16)
+
+    def absorb(pre):
+        rot = rot_ref[pl.ds(pl.multiple_of(lax.rem(s - 1, per) * chunk, chunk), chunk), :]
+        for b in range(batch_count):
+            out_ref[b] += jnp.dot(
+                pre[b * rows:(b + 1) * rows, :], rot, preferred_element_type=jnp.float32
             )
-            pre[b * rows:(b + 1) * rows, s * tile:(s + 1) * tile] = (
-                outer_sum * inverse
-            ).astype(jnp.bfloat16)
-
-    def absorb(k, pre):
-        more = jnp.dot(
-            pre[...], rot_ref[k * chunk:(k + 1) * chunk, :], preferred_element_type=jnp.float32
-        )
-        for b in range(batch_count):
-            part = more[b * rows:(b + 1) * rows, :]
-            out_ref[b] = part if k == 0 else out_ref[b] + part
-
-    for s in range(chunk // tile):
-        produce(0, s, pre_a)
-    for k in range(phases):
-        now, later = (pre_a, pre_b) if k % 2 == 0 else (pre_b, pre_a)
-        if k + 1 < phases:
-            for s in range(chunk // tile):
-                produce(k + 1, s, later)
-        absorb(k, now)
+
+    between = jnp.logical_and(s > 0, s < total)
+    odd = lax.rem(s, 2) == 1
+
+    @pl.when(s == 0)
+    def _():
+        produce(pre_a)
+
+    @pl.when(jnp.logical_and(between, odd))
+    def _():
+        produce(pre_b)
+        absorb(pre_a)
+
+    @pl.when(jnp.logical_and(between, jnp.logical_not(odd)))
+    def _():
+        produce(pre_a)
+        absorb(pre_b)
+
+    @pl.when(s == total)
+    def _():
+        absorb(pre_a if total % 2 else pre_b)
 
 
 def images(rot, lefts, halves, eigenvalues):
     batch_count, tokens = len(lefts), rot.shape[1]
     hidden, width = eigenvalues.shape
-    rows = min(512, hidden)
-    chunk = min(1024 if tokens <= 256 else 512, width // 2)
-    return pl.pallas_call(
-        functools.partial(image_kernel, batch_count),
-        grid=(hidden // rows,),
+    rows = min(1024, hidden)
+    chunk = min(1024, width // 2)
+    per = width // chunk
+    total = hidden // rows * per
+    now = lambda s: jnp.minimum(s, total - 1)
+    before = lambda s: jnp.maximum(s - 1, 0)
+    return pl.pallas_call(
+        functools.partial(image_kernel, batch_count, total, per),
+        grid=(total + 1,),
         in_specs=[whole_block(rot.shape)]
-        + [pl.BlockSpec((QT, rows), lambda i: (0, i)) for x in lefts]
+        + [pl.BlockSpec((QT, rows), lambda s: (0, now(s) // per)) for _ in lefts]
         + [whole_block(x.shape) for x in halves]
-        + [pl.BlockSpec((rows, width), lambda i: (i, 0))],
-        out_specs=pl.BlockSpec((batch_count, rows, tokens), lambda i: (0, i, 0)),
+        + [pl.BlockSpec((rows, chunk), lambda s: (now(s) // per, now(s) % per))],
+        out_specs=pl.BlockSpec((batch_count, rows, tokens), lambda s: (0, before(s) // per, 0)),
         out_shape=jax.ShapeDtypeStruct((batch_count, hidden, tokens), jnp.float32),
         scratch_shapes=[
             pltpu.VMEM((batch_count, QT, width), jnp.bfloat16),
@@ -277,7 +341,7 @@
             pltpu.VMEM((batch_count * rows, chunk), jnp.bfloat16),
             pltpu.VMEM((batch_count * rows, chunk), jnp.bfloat16),
         ],
-        compiler_params=params(50),
+        compiler_params=params(44),
         cost_estimate=pl.CostEstimate(
             flops=2 * hidden * width * (tokens + 256) * batch_count,
             bytes_accessed=2 * hidden * width,
@@ -327,13 +391,13 @@
         out_specs=pl.BlockSpec((batch_count, seq_count, 1), lambda i: (0, 0, 0)),
         out_shape=jax.ShapeDtypeStruct((batch_count, seq_count, 1), jnp.float32),
         scratch_shapes=[pltpu.VMEM((8, tokens), jnp.float32)],
-        compiler_params=params(56),
+        compiler_params=params(44),
         cost_estimate=pl.CostEstimate(
             flops=2 * tokens * hidden * grad_basis.shape[0],
             bytes_accessed=4 * image.size,
             transcendentals=0,
         ),
-    )(grads, grad_basis, image, grads)[:, :, 0]
+    )(grads, grad_basis, image, grads)
 
 
 def per_device(
@@ -350,17 +414,19 @@
     score_scale = 1.0 / math.sqrt(FF * D * QT * SEQ_MEAN)
     batch = lax.axis_index("groups") % batch_count
 
+    ways = bits[:2] + bits[:1:-1]
     order = [0]
     for bit in reversed(bits):
         order = order + [r + bit for r in order]
-    order = sorted(order, key=lambda r: [r & bit for bit in bits])
+    order = sorted(order, key=lambda r: [r & bit for bit in ways])
     acts, ranks = train_act, [0]
     far = bits[:1:-1]
-    keep, give, flags = cut_factors(owners, query_factors, order, hidden)
+    keep, give = cut_factors(query_factors, order, hidden, batch_count)
+    flags = owner_flags(owners, ways, keep)
     count = wide_count // 2
     after = []
     pieces = []
-    for step, bit in enumerate(bits):
+    for step, bit in enumerate(ways):
         got = swap(give, "wide", bit)
         keep, give = pick(flags, keep, got, step, cols, count, after)
         count //= 2
@@ -372,35 +438,38 @@
         elif step == len(far) - 1:
             last = swap(acts, "wide", far[step])
             held = gate(acts, [give])
-            pieces = [(acts, ranks), (swap(held, "wide", 2), [r + 2 for r in ranks])]
-            after = [held]
+            near = [(acts, ranks)]
+            over = [(swap(held, "wide", 2), [r + 2 for r in ranks])]
+            sent = cut_grads(seq_ids, train_grad, give, wide_count)
+            after = [held, sent]
         elif step == len(far):
             ranks = [r + far[-1] for r in ranks]
             held = gate(last, [give])
-            pieces += [(held, ranks), (swap(held, "wide", 2), [r + 2 for r in ranks])]
-            sent = cut_grads(seq_ids, train_grad, give, wide_count)
+            near += [(held, ranks)]
+            over += [(swap(held, "wide", 2), [r + 2 for r in ranks])]
+            near += [(swap(x, "wide", 1), [r + 1 for r in has]) for x, has in near]
+            first, basis = rotate([x for x, _ in near], act_basis)
+            after = [first]
     left, right = keep, give
-    for n in (1, 3):
-        pieces[n] = (gate(pieces[n][0], [right]), pieces[n][1])
-    pieces += [(swap(x, "wide", 1), [r + 1 for r in has]) for x, has in pieces]
-    rot = rotate([x for x, _ in pieces], act_basis)
-    ranks = [r for _, has in pieces for r in has]
 
     lefts = [left, swap(left, "groups", 1)]
     other = swap(right, "groups", 1)
     halves = []
     for x in (right, other):
         halves += [x, swap(x, "wide", 1)]
-
-    grads = lax.all_to_all(gate(sent, [rot, other]), "wide", 0, 0)
+    over = [(gate(x, [right]), has) for x, has in over]
+    over += [(swap(x, "wide", 1), [r + 1 for r in has]) for x, has in over]
+    rot = rotate_rest([x for x, _ in over], basis, first)
+    ranks = [r for _, has in near + over for r in has]
+
+    grads = lax.all_to_all(gate(sent, [rot, halves[-1]]), "wide", 0, 0)
 
     image = images(rot, lefts, halves, eigenvalues)
     parts = score_parts(grads, ranks, grad_basis, image, seq_count)
-    for near in (bits[:2], bits[2:]):
-        step = near[0]
-        others = [swap(parts, "wide", step * n) for n in range(1, 1 << len(near))]
+    for some in (bits[:2], bits[2:]):
+        others = [swap(parts, "wide", some[0] * n) for n in range(1, 1 << len(some))]
         parts = parts + sum(others)
-    mine, others = parts[0], parts[1]
+    mine, others = parts[0, :, 0], parts[1, :, 0]
     first = jnp.where(batch == 0, mine, others)
     second = jnp.where(batch == 0, others, mine)
     return jnp.stack([first, second], axis=1) * score_scale

time: 98.1 us -> 104 us (1.060)
  local copies, waits for them, and re-layouts: 2.35 us -> 7.48 us
  starting transfers between devices: 28.6 us -> 31.5 us
  Pallas kernels: 34.4 us -> 32 us
    unnamed x11 -> x17, local copies, waits for them, and re-layouts: 2.35 us -> 7.48 us
    ppermute x22, starting transfers between devices: 22.7 us -> 25.5 us  [swap(): return lax.ppermute(x, axis, [(i, i ^ bit) for i in range(count)])]
    pallas_call x1, Pallas kernels: 5.29 us -> 2.5 us  [score_parts(): pl.pallas_call(functools.partial(score_kernel, batch_count, ranks), grid=...]
    pallas_call x2 -> x4, Pallas kernels: 26.3 us -> 27.3 us  [the longest x1 22 us: images(): pl.pallas_call(functools.partial(image_kernel, batch_count, total, per),...]
  transfers between devices with their start and end apart: 23 -> 23, of which waited for: 9 -> 12; matrix products, arithmetic and copies ran while one was open for 0% -> 0% of each run, Pallas kernels for 29% -> 28%
where the time goes in v8:
time: 104 us; the launch traced here: 103 us
  Pallas kernels  32 us (31%)
  starting transfers between devices  31.5 us (30%)
  waiting for transfers between devices  31.4 us (30%)
  local copies, waits for them, and re-layouts  7.48 us (7%)
    ppermute x22, waiting for transfers between devices, swap(): return lax.ppermute(x, axis, [(i, i ^ bit) for i in range(count)])  31.4 us
    ppermute x22, starting transfers between devices, swap(): return lax.ppermute(x, axis, [(i, i ^ bit) for i in range(count)])  25.5 us
    pallas_call x1, Pallas kernels, images(): pl.pallas_call(functools.partial(image_kernel, batch_count, total, per),...  22 us
    unnamed x17, local copies, waits for them, and re-layouts  7.48 us
    all_to_all x1, starting transfers between devices, per_device(): grads = lax.all_to_all(gate(sent, [rot, halves[-1]]), 'wide', 0, 0)  5.97 us
    pallas_call x1, Pallas kernels, rotate(): pl.pallas_call(functools.partial(rotate_kernel, len(act_pieces)), in_spec...  3.63 us
    pallas_call x1, Pallas kernels, score_parts(): pl.pallas_call(functools.partial(score_kernel, batch_count, ranks), grid=...  2.5 us
  transfers between devices with their start and end apart: 23, of which 12 were waited for; matrix products, arithmetic and copies ran while one was open for 0% of the time, Pallas kernels for 28%

profile of v8, /device:TPU:0, one launch (start us, length us, event | category | flops | bytes accessed | tf_op | source)
XLA Modules:
  0.0 103.3 jit_solution(6305988754150640633)
XLA Ops:
  0.0 1.7 %copy-done.2 = bf16[2,16,36864]{2,1,0:T(8,128)(2,1)S(1)} copy-done((bf16[2,16,36864]{2,1,0:T(8,128)(2,1)S(1)}, bf16[2,16,36864]{2,1,0:T(8,128)(2,1)}, u32[]{:S(2)}) %copy-start.2) | copy-done | bytes 2359320
  4.1 3.0 %collective-permute-start.1 = (bf16[16,10240]{1,0:T(8,128)(2,1)S(1)}, bf16[16,10240]{1,0:T(8,128)(2,1)S(1)}, u32[]{:S(2)}, u32[]{:S(2)}) collective-permute-start(bf16[16,10240]{1,0:T(8,128)(2,1)S(1)} %get-tuple-element.20._), channel_id=1, source_target_pairs={{0,2},{1,3},{2,0},{3,1},{4,6},{5,7},{6,4},{7,5},{8,10},{9,11},{10,... | collective-permute-start | bytes 983048 | tf_op jit(solution)/shard_map/ppermute | solution.py:31
  7.0 2.6 %collective-permute-start.2 = (bf16[16,4096]{1,0:T(8,128)(2,1)S(1)}, bf16[16,4096]{1,0:T(8,128)(2,1)S(1)}, u32[]{:S(2)}, u32[]{:S(2)}) collective-permute-start(bf16[16,4096]{1,0:T(8,128)(2,1)S(1)} %copy-done.5), channel_id=1, source_target_pairs={{0,8},{1,9},{2,10},{3,11},{4,12},{5,13},{6,14},{7,15},{8,0},{9,1},... | collective-permute-start | bytes 393224 | tf_op jit(solution)/shard_map/ppermute | solution.py:31
  9.6 6.4 %collective-permute-done.2.second_ref = bf16[16,4096]{1,0:T(8,128)(2,1)S(1)} collective-permute-done((bf16[16,4096]{1,0:T(8,128)(2,1)S(1)}, bf16[16,4096]{1,0:T(8,128)(2,1)S(1)}, u32[]{:S(2)}, u32[]{:S(2)}) %collective-permute-start.2) | collective-permute-done | bytes 131104 | tf_op jit(solution)/shard_map/ppermute | solution.py:31
  16.9 3.4 %collective-permute-start.4 = (bf16[16,6144]{1,0:T(8,128)(2,1)S(1)}, bf16[16,6144]{1,0:T(8,128)(2,1)S(1)}, u32[]{:S(2)}, u32[]{:S(2)}) collective-permute-start(bf16[16,6144]{1,0:T(8,128)(2,1)S(1)} %get-tuple-element.21._.__1_), channel_id=1, source_target_pairs={{0,8},{1,9},{2,10},{3,11},{4,12},{5,13},{6,14},{7,15},{8,0},{9,1},... | collective-permute-start | bytes 589832 | tf_op jit(solution)/shard_map/ppermute | solution.py:31
  20.5 1.7 %shard_map.87.refs_1_.__0_ = bf16[16,16,2176]{2,1,0:T(8,128)(2,1)} custom-call(s32[16]{0:T(128)S(1)} %copy-done.6, bf16[16,32768]{1,0:T(8,128)(2,1)S(1)} %copy-done.4, bf16[16,6144]{1,0:T(8,128)(2,1)S(1)} %get-tuple-element.21._.__1_), custom_call_target="tpu_custom_call" | custom-call | bytes 524288 | tf_op jit(solution)/shard_map/pallas_call | solution.py:179
  22.1 4.6 %collective-permute-done.4.got_ref = bf16[16,6144]{1,0:T(8,128)(2,1)S(1)} collective-permute-done((bf16[16,6144]{1,0:T(8,128)(2,1)S(1)}, bf16[16,6144]{1,0:T(8,128)(2,1)S(1)}, u32[]{:S(2)}, u32[]{:S(2)}) %collective-permute-start.4) | collective-permute-done | bytes 196640 | tf_op jit(solution)/shard_map/ppermute | solution.py:31
  29.5 3.6 %collective-permute-start.5 = (bf16[16,4096]{1,0:T(8,128)(2,1)S(1)}, bf16[16,4096]{1,0:T(8,128)(2,1)S(1)}, u32[]{:S(2)}, u32[]{:S(2)}) collective-permute-start(bf16[16,4096]{1,0:T(8,128)(2,1)S(1)} %get-tuple-element.24.__1_), channel_id=1, source_target_pairs={{0,4},{1,5},{2,6},{3,7},{4,0},{5,1},{6,2},{7,3},{8,12},{9,13},{10,... | collective-permute-start | bytes 393224 | tf_op jit(solution)/shard_map/ppermute | solution.py:31
  33.1 3.6 %shard_map.91 = (bf16[4096,128]{1,0:T(8,128)(2,1)S(1)}, bf16[8,512,512]{2,1,0:T(8,128)(2,1)S(1)}) custom-call(bf16[32,4096]{1,0:T(8,128)(2,1)S(1)} %shard_map.85.refs_0_, bf16[32,4096]{1,0:T(8,128)(2,1)S(1)} %shard_map.90.refs_1_, bf16[32,4096]{1,0:T(8,128)(2,1)S(1)} %collective-permute-done.7.refs_2_, bf16[32,4096]{1,0:T(8,128)(2,1)S(1)} %collective-permute-done.8.refs_3_, ...), custom_call_target="tpu_custom_call" | custom-call | flops 536870912 | bytes 2097152 | tf_op jit(solution)/shard_map/pallas_call | solution.py:210
  37.0 4.9 %collective-permute-done.3.__0_ = bf16[32,4096]{1,0:T(8,128)(2,1)S(1)} collective-permute-done((bf16[32,4096]{1,0:T(8,128)(2,1)S(1)}, bf16[32,4096]{1,0:T(8,128)(2,1)S(1)}, u32[]{:S(2)}, u32[]{:S(2)}) %collective-permute-start.3) | collective-permute-done | bytes 262176 | tf_op jit(solution)/shard_map/ppermute | solution.py:31
  43.3 3.0 %collective-permute-done.12.refs_4_ = bf16[16,2048]{1,0:T(8,128)(2,1)S(1)} collective-permute-done((bf16[16,2048]{1,0:T(8,128)(2,1)S(1)}, bf16[16,2048]{1,0:T(8,128)(2,1)S(1)}, u32[]{:S(2)}, u32[]{:S(2)}) %collective-permute-start.12) | collective-permute-done | bytes 65568 | tf_op jit(solution)/shard_map/ppermute | solution.py:31
  47.6 6.0 %all-to-all-start = ((bf16[16,16,2176]{2,1,0:T(8,128)(2,1)}), bf16[16,16,2176]{2,1,0:T(8,128)(2,1)S(1)}, u32[]{:S(2)}, u32[]{:S(2)}) async-start(bf16[16,16,2176]{2,1,0:T(8,128)(2,1)} %shard_map.96), calls=%async_computation | async-start | bytes 2228224 | tf_op jit(solution)/shard_map/all_to_all | solution.py:465
  53.6 1.6 %collective-permute-start.14 = (bf16[16,2048]{1,0:T(8,128)(2,1)S(1)}, bf16[16,2048]{1,0:T(8,128)(2,1)S(1)}, u32[]{:S(2)}, u32[]{:S(2)}) collective-permute-start(bf16[16,2048]{1,0:T(8,128)(2,1)S(1)} %get-tuple-element.28.refs_0_), channel_id=1, source_target_pairs={{0,16},{16,0},{1,17},{17,1},{2,18},{18,2},{3,19},{19,3},{4,20},{20... | collective-permute-start | bytes 196616 | tf_op jit(solution)/shard_map/ppermute | solution.py:31
  55.3 2.8 %collective-permute-done.14.refs_1_ = bf16[16,2048]{1,0:T(8,128)(2,1)S(1)} collective-permute-done((bf16[16,2048]{1,0:T(8,128)(2,1)S(1)}, bf16[16,2048]{1,0:T(8,128)(2,1)S(1)}, u32[]{:S(2)}, u32[]{:S(2)}) %collective-permute-start.14) | collective-permute-done | bytes 65568 | tf_op jit(solution)/shard_map/ppermute | solution.py:31
  58.1 22.0 %shard_map.97.image_ref = f32[2,2048,256]{2,1,0:T(8,128)S(1)} custom-call(bf16[4096,256]{1,0:T(8,128)(2,1)S(1)} %shard_map.95.__1_.rot_ref, bf16[16,2048]{1,0:T(8,128)(2,1)S(1)} %get-tuple-element.28.refs_0_, bf16[16,2048]{1,0:T(8,128)(2,1)S(1)} %collective-permute-done.14.refs_1_, bf16[16,2048]{1,0:T(8,128)(2,1)S(1)} %get-tuple-element.26.__1_.refs_2_, ...), custom_call_target="tpu_custom_call" | custom-call | flops 17179869184 | bytes 16777216 | tf_op jit(solution)/shard_map/pallas_call | solution.py:329
  80.1 1.9 %copy-done = f32[2,2048,256]{2,1,0:T(8,128)} copy-done((f32[2,2048,256]{2,1,0:T(8,128)}, f32[2,2048,256]{2,1,0:T(8,128)S(1)}, u32[]{:S(2)}) %copy-start) | copy-done | bytes 4194328
  82.1 2.2 %copy-done.1 = f32[2,2048,256]{2,1,0:T(8,128)S(1)} copy-done((f32[2,2048,256]{2,1,0:T(8,128)S(1)}, f32[2,2048,256]{2,1,0:T(8,128)}, u32[]{:S(2)}) %copy-start.1) | copy-done | bytes 4194328
  84.3 1.6 %copy-done.3 = bf16[512,2048]{1,0:T(8,128)(2,1)S(1)} copy-done((bf16[512,2048]{1,0:T(8,128)(2,1)S(1)}, bf16[512,2048]{1,0:T(8,128)(2,1)}, u32[]{:S(2)}) %copy-start.3) | copy-done | bytes 2097176
  85.8 2.5 %shard_map.98 = f32[2,8,1]{2,1,0:T(8,128)S(1)} custom-call(bf16[16,16,2176]{2,1,0:T(8,128)(2,1)S(1)} %all-to-all-done.grad_ref.ids_ref, bf16[512,2048]{1,0:T(8,128)(2,1)S(1)} %copy-done.3, f32[2,2048,256]{2,1,0:T(8,128)S(1)} %copy-done.1, bf16[16,16,2176]{2,1,0:T(8,128)(2,1)S(1)} %all-to-all-done.grad_ref.ids_ref), custom_call_target="tpu_custom_call" | custom-call | flops 536870912 | bytes 4194304 | tf_op jit(solution)/shard_map/pallas_call | solution.py:382
  88.3 1.8 %collective-permute-start.17 = (f32[2,8,1]{2,1,0:T(8,128)S(1)}, f32[2,8,1]{2,1,0:T(8,128)S(1)}, u32[]{:S(2)}, u32[]{:S(2)}) collective-permute-start(f32[2,8,1]{2,1,0:T(8,128)S(1)} %shard_map.98), channel_id=1, source_target_pairs={{0,2},{1,3},{2,0},{3,1},{4,6},{5,7},{6,4},{7,5},{8,10},{9,11},{10,... | collective-permute-start | bytes 200 | tf_op jit(solution)/shard_map/ppermute | solution.py:31
  90.3 1.8 %collective-permute-done.17 = f32[2,8,1]{2,1,0:T(8,128)S(1)} collective-permute-done((f32[2,8,1]{2,1,0:T(8,128)S(1)}, f32[2,8,1]{2,1,0:T(8,128)S(1)}, u32[]{:S(2)}, u32[]{:S(2)}) %collective-permute-start.17) | collective-permute-done | bytes 96 | tf_op jit(solution)/shard_map/ppermute | solution.py:31
  94.7 2.4 %collective-permute-start.20 = (f32[2,8,1]{2,1,0:T(8,128)S(1)}, f32[2,8,1]{2,1,0:T(8,128)S(1)}, u32[]{:S(2)}, u32[]{:S(2)}) collective-permute-start(f32[2,8,1]{2,1,0:T(8,128)S(1)} %add_add_fusion.1), channel_id=1, source_target_pairs={{0,8},{1,9},{2,10},{3,11},{4,12},{5,13},{6,14},{7,15},{8,0},{9,1},... | collective-permute-start | bytes 200 | tf_op jit(solution)/shard_map/ppermute | solution.py:31
  97.6 1.6 %collective-permute-done.20 = f32[2,8,1]{2,1,0:T(8,128)S(1)} collective-permute-done((f32[2,8,1]{2,1,0:T(8,128)S(1)}, f32[2,8,1]{2,1,0:T(8,128)S(1)}, u32[]{:S(2)}, u32[]{:S(2)}) %collective-permute-start.20) | collective-permute-done | bytes 96 | tf_op jit(solution)/shard_map/ppermute | solution.py:31
  99.3 3.3 %collective-permute-done.21 = f32[2,8,1]{2,1,0:T(8,128)S(1)} collective-permute-done((f32[2,8,1]{2,1,0:T(8,128)S(1)}, f32[2,8,1]{2,1,0:T(8,128)S(1)}, u32[]{:S(2)}, u32[]{:S(2)}) %collective-permute-start.21) | collective-permute-done | bytes 96 | tf_op jit(solution)/shard_map/ppermute | solution.py:31
  (60 shorter events, 13.2 us)
Async XLA Ops:
  1.8 2.1 %collective-permute-start = (bf16[16,18432]{1,0:T(8,128)(2,1)S(1)}, bf16[16,18432]{1,0:T(8,128)(2,1)S(1)}, u32[]{:S(2)}, u32[]{:S(2)}) collective-permute-start(bf16[16,18432]{1,0:T(8,128)(2,1)S(1)} %get-tuple-element.18), channel_id=1, source_target_pairs={{0,1},{1,0},{2,3},{3,2},{4,5},{5,4},{6,7},{7,6},{8,9},{9,8},{10,11... | collective-permute-start | bytes 1769480 | tf_op jit(solution)/shard_map/ppermute | solution.py:31
  2.3 18.1 %copy-start.6 = (s32[16]{0:T(128)S(1)}, s32[16]{0:T(128)}, u32[]{:S(2)}) copy-start(s32[16]{0:T(128)} %ids_ref.1) | copy-start | bytes 196
  4.1 12.7 %collective-permute-start.1 = (bf16[16,10240]{1,0:T(8,128)(2,1)S(1)}, bf16[16,10240]{1,0:T(8,128)(2,1)S(1)}, u32[]{:S(2)}, u32[]{:S(2)}) collective-permute-start(bf16[16,10240]{1,0:T(8,128)(2,1)S(1)} %get-tuple-element.20._), channel_id=1, source_target_pairs={{0,2},{1,3},{2,0},{3,1},{4,6},{5,7},{6,4},{7,5},{8,10},{9,11},{10,... | collective-permute-start | bytes 983048 | tf_op jit(solution)/shard_map/ppermute | solution.py:31
  7.0 9.0 %collective-permute-start.2 = (bf16[16,4096]{1,0:T(8,128)(2,1)S(1)}, bf16[16,4096]{1,0:T(8,128)(2,1)S(1)}, u32[]{:S(2)}, u32[]{:S(2)}) collective-permute-start(bf16[16,4096]{1,0:T(8,128)(2,1)S(1)} %copy-done.5), channel_id=1, source_target_pairs={{0,8},{1,9},{2,10},{3,11},{4,12},{5,13},{6,14},{7,15},{8,0},{9,1},... | collective-permute-start | bytes 393224 | tf_op jit(solution)/shard_map/ppermute | solution.py:31
  16.0 11.5 %collective-permute-start.6 = (bf16[32,4096]{1,0:T(8,128)(2,1)S(1)}, bf16[32,4096]{1,0:T(8,128)(2,1)S(1)}, u32[]{:S(2)}, u32[]{:S(2)}) collective-permute-start(bf16[32,4096]{1,0:T(8,128)(2,1)S(1)} %shard_map.85.refs_0_), channel_id=1, source_target_pairs={{0,4},{1,5},{2,6},{3,7},{4,0},{5,1},{6,2},{7,3},{8,12},{9,13},{10,... | collective-permute-start | bytes 786440 | tf_op jit(solution)/shard_map/ppermute | solution.py:31
  16.9 9.9 %collective-permute-start.4 = (bf16[16,6144]{1,0:T(8,128)(2,1)S(1)}, bf16[16,6144]{1,0:T(8,128)(2,1)S(1)}, u32[]{:S(2)}, u32[]{:S(2)}) collective-permute-start(bf16[16,6144]{1,0:T(8,128)(2,1)S(1)} %get-tuple-element.21._.__1_), channel_id=1, source_target_pairs={{0,8},{1,9},{2,10},{3,11},{4,12},{5,13},{6,14},{7,15},{8,0},{9,1},... | collective-permute-start | bytes 589832 | tf_op jit(solution)/shard_map/ppermute | solution.py:31
  20.4 12.8 %collective-permute-start.7 = (bf16[32,4096]{1,0:T(8,128)(2,1)S(1)}, bf16[32,4096]{1,0:T(8,128)(2,1)S(1)}, u32[]{:S(2)}, u32[]{:S(2)}) collective-permute-start(bf16[32,4096]{1,0:T(8,128)(2,1)S(1)} %shard_map.85.refs_0_), channel_id=1, source_target_pairs={{0,1},{1,0},{2,3},{3,2},{4,5},{5,4},{6,7},{7,6},{8,9},{9,8},{10,11... | collective-permute-start | bytes 786440 | tf_op jit(solution)/shard_map/ppermute | solution.py:31
  27.5 5.6 %collective-permute-start.8 = (bf16[32,4096]{1,0:T(8,128)(2,1)S(1)}, bf16[32,4096]{1,0:T(8,128)(2,1)S(1)}, u32[]{:S(2)}, u32[]{:S(2)}) collective-permute-start(bf16[32,4096]{1,0:T(8,128)(2,1)S(1)} %shard_map.90.refs_1_), channel_id=1, source_target_pairs={{0,1},{1,0},{2,3},{3,2},{4,5},{5,4},{6,7},{7,6},{8,9},{9,8},{10,11... | collective-permute-start | bytes 786440 | tf_op jit(solution)/shard_map/ppermute | solution.py:31
  27.5 9.4 %collective-permute-start.9 = (bf16[32,4096]{1,0:T(8,128)(2,1)S(1)}, bf16[32,4096]{1,0:T(8,128)(2,1)S(1)}, u32[]{:S(2)}, u32[]{:S(2)}) collective-permute-start(bf16[32,4096]{1,0:T(8,128)(2,1)S(1)} %shard_map.90.refs_1_), channel_id=1, source_target_pairs={{0,2},{1,3},{2,0},{3,1},{4,6},{5,7},{6,4},{7,5},{8,10},{9,11},{10,... | collective-permute-start | bytes 786440 | tf_op jit(solution)/shard_map/ppermute | solution.py:31
  28.3 13.6 %collective-permute-start.3 = (bf16[32,4096]{1,0:T(8,128)(2,1)S(1)}, bf16[32,4096]{1,0:T(8,128)(2,1)S(1)}, u32[]{:S(2)}, u32[]{:S(2)}) collective-permute-start(bf16[32,4096]{1,0:T(8,128)(2,1)S(1)} %shard_map.88.refs_0_), channel_id=1, source_target_pairs={{0,2},{1,3},{2,0},{3,1},{4,6},{5,7},{6,4},{7,5},{8,10},{9,11},{10,... | collective-permute-start | bytes 786440 | tf_op jit(solution)/shard_map/ppermute | solution.py:31
  29.5 7.2 %collective-permute-start.5 = (bf16[16,4096]{1,0:T(8,128)(2,1)S(1)}, bf16[16,4096]{1,0:T(8,128)(2,1)S(1)}, u32[]{:S(2)}, u32[]{:S(2)}) collective-permute-start(bf16[16,4096]{1,0:T(8,128)(2,1)S(1)} %get-tuple-element.24.__1_), channel_id=1, source_target_pairs={{0,4},{1,5},{2,6},{3,7},{4,0},{5,1},{6,2},{7,3},{8,12},{9,13},{10,... | collective-permute-start | bytes 393224 | tf_op jit(solution)/shard_map/ppermute | solution.py:31
  36.9 9.5 %collective-permute-start.11 = (bf16[32,4096]{1,0:T(8,128)(2,1)S(1)}, bf16[32,4096]{1,0:T(8,128)(2,1)S(1)}, u32[]{:S(2)}, u32[]{:S(2)}) collective-permute-start(bf16[32,4096]{1,0:T(8,128)(2,1)S(1)} %shard_map.94.refs_1_), channel_id=1, source_target_pairs={{0,1},{1,0},{2,3},{3,2},{4,5},{5,4},{6,7},{7,6},{8,9},{9,8},{10,11... | collective-permute-start | bytes 786440 | tf_op jit(solution)/shard_map/ppermute | solution.py:31
  41.9 4.5 %collective-permute-start.10 = (bf16[32,4096]{1,0:T(8,128)(2,1)S(1)}, bf16[32,4096]{1,0:T(8,128)(2,1)S(1)}, u32[]{:S(2)}, u32[]{:S(2)}) collective-permute-start(bf16[32,4096]{1,0:T(8,128)(2,1)S(1)} %shard_map.93.refs_0_), channel_id=1, source_target_pairs={{0,1},{1,0},{2,3},{3,2},{4,5},{5,4},{6,7},{7,6},{8,9},{9,8},{10,11... | collective-permute-start | bytes 786440 | tf_op jit(solution)/shard_map/ppermute | solution.py:31
  41.9 4.5 %collective-permute-start.12 = (bf16[16,2048]{1,0:T(8,128)(2,1)S(1)}, bf16[16,2048]{1,0:T(8,128)(2,1)S(1)}, u32[]{:S(2)}, u32[]{:S(2)}) collective-permute-start(bf16[16,2048]{1,0:T(8,128)(2,1)S(1)} %get-tuple-element.26.__1_.refs_2_), channel_id=1, source_target_pairs={{0,16},{16,0},{1,17},{17,1},{2,18},{18,2},{3,19},{19,3},{4,20},{20... | collective-permute-start | bytes 196616 | tf_op jit(solution)/shard_map/ppermute | solution.py:31
  46.4 1.3 %collective-permute-start.13 = (bf16[16,2048]{1,0:T(8,128)(2,1)S(1)}, bf16[16,2048]{1,0:T(8,128)(2,1)S(1)}, u32[]{:S(2)}, u32[]{:S(2)}) collective-permute-start(bf16[16,2048]{1,0:T(8,128)(2,1)S(1)} %collective-permute-done.12.refs_4_), channel_id=1, source_target_pairs={{0,1},{1,0},{2,3},{3,2},{4,5},{5,4},{6,7},{7,6},{8,9},{9,8},{10,11... | collective-permute-start | bytes 196616 | tf_op jit(solution)/shard_map/ppermute | solution.py:31
  47.6 34.4 %all-to-all-start = ((bf16[16,16,2176]{2,1,0:T(8,128)(2,1)}), bf16[16,16,2176]{2,1,0:T(8,128)(2,1)S(1)}, u32[]{:S(2)}, u32[]{:S(2)}) async-start(bf16[16,16,2176]{2,1,0:T(8,128)(2,1)} %shard_map.96), calls=%async_computation | async-start | bytes 2228224 | tf_op jit(solution)/shard_map/all_to_all | solution.py:465
  53.6 4.5 %collective-permute-start.14 = (bf16[16,2048]{1,0:T(8,128)(2,1)S(1)}, bf16[16,2048]{1,0:T(8,128)(2,1)S(1)}, u32[]{:S(2)}, u32[]{:S(2)}) collective-permute-start(bf16[16,2048]{1,0:T(8,128)(2,1)S(1)} %get-tuple-element.28.refs_0_), channel_id=1, source_target_pairs={{0,16},{16,0},{1,17},{17,1},{2,18},{18,2},{3,19},{19,3},{4,20},{20... | collective-permute-start | bytes 196616 | tf_op jit(solution)/shard_map/ppermute | solution.py:31
  55.2 2.9 %collective-permute-start.15 = (bf16[16,2048]{1,0:T(8,128)(2,1)S(1)}, bf16[16,2048]{1,0:T(8,128)(2,1)}, u32[]{:S(2)}, u32[]{:S(2)}) collective-permute-start(bf16[16,2048]{1,0:T(8,128)(2,1)S(1)} %get-tuple-element.26.__1_.refs_2_), channel_id=1, source_target_pairs={{0,1},{1,0},{2,3},{3,2},{4,5},{5,4},{6,7},{7,6},{8,9},{9,8},{10,11... | collective-permute-start | bytes 196616 | tf_op jit(solution)/shard_map/ppermute | solution.py:31
  88.3 1.9 %collective-permute-start.16 = (f32[2,8,1]{2,1,0:T(8,128)S(1)}, f32[2,8,1]{2,1,0:T(8,128)S(1)}, u32[]{:S(2)}, u32[]{:S(2)}) collective-permute-start(f32[2,8,1]{2,1,0:T(8,128)S(1)} %shard_map.98), channel_id=1, source_target_pairs={{0,1},{1,0},{2,3},{3,2},{4,5},{5,4},{6,7},{7,6},{8,9},{9,8},{10,11... | collective-permute-start | bytes 200 | tf_op jit(solution)/shard_map/ppermute | solution.py:31
  88.3 3.7 %collective-permute-start.17 = (f32[2,8,1]{2,1,0:T(8,128)S(1)}, f32[2,8,1]{2,1,0:T(8,128)S(1)}, u32[]{:S(2)}, u32[]{:S(2)}) collective-permute-start(f32[2,8,1]{2,1,0:T(8,128)S(1)} %shard_map.98), channel_id=1, source_target_pairs={{0,2},{1,3},{2,0},{3,1},{4,6},{5,7},{6,4},{7,5},{8,10},{9,11},{10,... | collective-permute-start | bytes 200 | tf_op jit(solution)/shard_map/ppermute | solution.py:31
  90.2 3.1 %collective-permute-start.18 = (f32[2,8,1]{2,1,0:T(8,128)S(1)}, f32[2,8,1]{2,1,0:T(8,128)S(1)}, u32[]{:S(2)}, u32[]{:S(2)}) collective-permute-start(f32[2,8,1]{2,1,0:T(8,128)S(1)} %shard_map.98), channel_id=1, source_target_pairs={{0,3},{1,2},{2,1},{3,0},{4,7},{5,6},{6,5},{7,4},{8,11},{9,10},{10,... | collective-permute-start | bytes 200 | tf_op jit(solution)/shard_map/ppermute | solution.py:31
  93.3 4.4 %collective-permute-start.19 = (f32[2,8,1]{2,1,0:T(8,128)S(1)}, f32[2,8,1]{2,1,0:T(8,128)S(1)}, u32[]{:S(2)}, u32[]{:S(2)}) collective-permute-start(f32[2,8,1]{2,1,0:T(8,128)S(1)} %add_add_fusion.1), channel_id=1, source_target_pairs={{0,4},{1,5},{2,6},{3,7},{4,0},{5,1},{6,2},{7,3},{8,12},{9,13},{10,... | collective-permute-start | bytes 200 | tf_op jit(solution)/shard_map/ppermute | solution.py:31
  94.7 4.6 %collective-permute-start.20 = (f32[2,8,1]{2,1,0:T(8,128)S(1)}, f32[2,8,1]{2,1,0:T(8,128)S(1)}, u32[]{:S(2)}, u32[]{:S(2)}) collective-permute-start(f32[2,8,1]{2,1,0:T(8,128)S(1)} %add_add_fusion.1), channel_id=1, source_target_pairs={{0,8},{1,9},{2,10},{3,11},{4,12},{5,13},{6,14},{7,15},{8,0},{9,1},... | collective-permute-start | bytes 200 | tf_op jit(solution)/shard_map/ppermute | solution.py:31
  97.1 5.4 %collective-permute-start.21 = (f32[2,8,1]{2,1,0:T(8,128)S(1)}, f32[2,8,1]{2,1,0:T(8,128)S(1)}, u32[]{:S(2)}, u32[]{:S(2)}) collective-permute-start(f32[2,8,1]{2,1,0:T(8,128)S(1)} %add_add_fusion.1), channel_id=1, source_target_pairs={{0,12},{1,13},{2,14},{3,15},{4,8},{5,9},{6,10},{7,11},{8,4},{9,5},... | collective-permute-start | bytes 200 | tf_op jit(solution)/shard_map/ppermute | solution.py:31
  (7 other events, 31.5 us)

commit v9 on v8

--- a/solution.py
+++ b/solution.py
@@ -65,7 +65,7 @@
         out_specs=in_vmem(2),
         out_shape=[half] * 2,
         compiler_params=params(16),
-        cost_estimate=pl.CostEstimate(flops=0, bytes_accessed=factors.size, transcendentals=0),
+        cost_estimate=pl.CostEstimate(flops=0, bytes_accessed=1, transcendentals=0),
     )(factors)
 
 
@@ -123,26 +123,26 @@
         out_specs=in_vmem(2),
         out_shape=[jax.ShapeDtypeStruct((rows, w), keep.dtype) for w in widths],
         compiler_params=params(16),
-        cost_estimate=pl.CostEstimate(flops=0, bytes_accessed=2 * keep.size, transcendentals=0),
+        cost_estimate=pl.CostEstimate(flops=0, bytes_accessed=1, transcendentals=0),
     )(flags, keep, got, *after)
 
 
-def join_kernel(first_ref, second_ref, _, out_ref):
+def join_kernel(first_ref, second_ref, out_ref):
     rows = first_ref.shape[0]
     out_ref[:rows, :] = first_ref[...]
     out_ref[rows:, :] = second_ref[...]
 
 
-def join(first, second, after):
+def join(first, second):
     rows, width = first.shape
     return pl.pallas_call(
         join_kernel,
-        in_specs=in_vmem(2) + in_place(1),
+        in_specs=in_vmem(2),
         out_specs=in_vmem(1)[0],
         out_shape=jax.ShapeDtypeStruct((2 * rows, width), first.dtype),
         compiler_params=params(16),
-        cost_estimate=pl.CostEstimate(flops=0, bytes_accessed=first.size, transcendentals=0),
-    )(first, second, after)
+        cost_estimate=pl.CostEstimate(flops=0, bytes_accessed=1, transcendentals=0),
+    )(first, second)
 
 
 def gate_kernel(*_):
@@ -182,12 +182,12 @@
         out_specs=in_vmem(1)[0],
         out_shape=jax.ShapeDtypeStruct((count, rows, hidden // count + LANES), grads.dtype),
         compiler_params=params(16),
-        cost_estimate=pl.CostEstimate(flops=0, bytes_accessed=grads.size, transcendentals=0),
+        cost_estimate=pl.CostEstimate(flops=0, bytes_accessed=1, transcendentals=0),
     )(ids, grads, after)
 
 
 def rotate_kernel(act_count, *refs):
-    act_refs, (basis_ref, out_ref, held_ref, sems) = refs[:act_count], refs[act_count:]
+    act_refs, (basis_ref, _, out_ref, held_ref, sems) = refs[:act_count], refs[act_count:]
     depth, width = basis_ref.shape
     places = [slice(k * depth, (k + 1) * depth) for k in range(width // depth)]
     copies = [
@@ -203,13 +203,13 @@
         out_ref[cols, :] = turned.astype(jnp.bfloat16).T
 
 
-def rotate(act_pieces, basis):
+def rotate(act_pieces, basis, after):
     tokens = sum(x.shape[0] for x in act_pieces)
     depth, width = basis.shape
     count = width // depth
     return pl.pallas_call(
         functools.partial(rotate_kernel, len(act_pieces)),
-        in_specs=in_vmem(len(act_pieces)) + in_place(1),
+        in_specs=in_vmem(len(act_pieces)) + in_place(2),
         out_specs=in_vmem(2),
         out_shape=[
             jax.ShapeDtypeStruct((width, tokens), jnp.bfloat16),
@@ -217,10 +217,8 @@
         ],
         scratch_shapes=[pltpu.SemaphoreType.DMA((count,))],
         compiler_params=params(46 if tokens <= 256 else 32),
-        cost_estimate=pl.CostEstimate(
-            flops=2 * tokens * width * depth, bytes_accessed=basis.size, transcendentals=0
-        ),
-    )(*act_pieces, basis)
+        cost_estimate=pl.CostEstimate(flops=0, bytes_accessed=1, transcendentals=0),
+    )(*act_pieces, basis, after)
 
 
 def rotate_rest_kernel(act_count, *refs):
@@ -244,9 +242,7 @@
         out_specs=in_vmem(1)[0],
         out_shape=jax.ShapeDtypeStruct((width, tokens), jnp.bfloat16),
         compiler_params=params(16 if tokens <= 256 else 32),
-        cost_estimate=pl.CostEstimate(
-            flops=2 * tokens * held.size, bytes_accessed=held.size, transcendentals=0
-        ),
+        cost_estimate=pl.CostEstimate(flops=0, bytes_accessed=1, transcendentals=0),
     )(*act_pieces, held, first)
 
 
@@ -341,7 +337,7 @@
             pltpu.VMEM((batch_count * rows, chunk), jnp.bfloat16),
             pltpu.VMEM((batch_count * rows, chunk), jnp.bfloat16),
         ],
-        compiler_params=params(44),
+        compiler_params=params(50),
         cost_estimate=pl.CostEstimate(
             flops=2 * hidden * width * (tokens + 256) * batch_count,
             bytes_accessed=2 * hidden * width,
@@ -391,7 +387,7 @@
         out_specs=pl.BlockSpec((batch_count, seq_count, 1), lambda i: (0, 0, 0)),
         out_shape=jax.ShapeDtypeStruct((batch_count, seq_count, 1), jnp.float32),
         scratch_shapes=[pltpu.VMEM((8, tokens), jnp.float32)],
-        compiler_params=params(44),
+        compiler_params=params(56),
         cost_estimate=pl.CostEstimate(
             flops=2 * tokens * hidden * grad_basis.shape[0],
             bytes_accessed=4 * image.size,
@@ -424,32 +420,27 @@
     keep, give = cut_factors(query_factors, order, hidden, batch_count)
     flags = owner_flags(owners, ways, keep)
     count = wide_count // 2
-    after = []
-    pieces = []
     for step, bit in enumerate(ways):
         got = swap(give, "wide", bit)
-        keep, give = pick(flags, keep, got, step, cols, count, after)
-        count //= 2
-        after = []
         if step < len(far) - 1:
-            acts = join(acts, swap(acts, "wide", far[step]), give)
+            acts = join(acts, swap(acts, "wide", far[step]))
             ranks = ranks + [r + far[step] for r in ranks]
             after = [acts]
         elif step == len(far) - 1:
             last = swap(acts, "wide", far[step])
-            held = gate(acts, [give])
-            near = [(acts, ranks)]
-            over = [(swap(held, "wide", 2), [r + 2 for r in ranks])]
             sent = cut_grads(seq_ids, train_grad, give, wide_count)
-            after = [held, sent]
+            after = [last, sent]
         elif step == len(far):
-            ranks = [r + far[-1] for r in ranks]
-            held = gate(last, [give])
-            near += [(held, ranks)]
-            over += [(swap(held, "wide", 2), [r + 2 for r in ranks])]
+            after = [over[0][0], first]
+        else:
+            after = []
+        keep, give = pick(flags, keep, got, step, cols, count, after)
+        count //= 2
+        if step == len(far) - 1:
+            near = [(gate(acts, [give]), ranks), (gate(last, [give]), [r + far[step] for r in ranks])]
+            over = [(swap(x, "wide", 2), [r + 2 for r in has]) for x, has in near]
             near += [(swap(x, "wide", 1), [r + 1 for r in has]) for x, has in near]
-            first, basis = rotate([x for x, _ in near], act_basis)
-            after = [first]
+            first, basis = rotate([x for x, _ in near], act_basis, give)
     left, right = keep, give
 
     lefts = [left, swap(left, "groups", 1)]
@@ -457,12 +448,12 @@
     halves = []
     for x in (right, other):
         halves += [x, swap(x, "wide", 1)]
-    over = [(gate(x, [right]), has) for x, has in over]
+    over = [(gate(x, [wait]), has) for (x, has), wait in zip(over, (right, other))]
     over += [(swap(x, "wide", 1), [r + 1 for r in has]) for x, has in over]
     rot = rotate_rest([x for x, _ in over], basis, first)
     ranks = [r for _, has in near + over for r in has]
 
-    grads = lax.all_to_all(gate(sent, [rot, halves[-1]]), "wide", 0, 0)
+    grads = lax.all_to_all(gate(sent, [rot, lefts[1], halves[1], halves[3]]), "wide", 0, 0)
 
     image = images(rot, lefts, halves, eigenvalues)
     parts = score_parts(grads, ranks, grad_basis, image, seq_count)

time: 104 us -> 103 us (level)
  local copies, waits for them, and re-layouts: 7.48 us -> 1.95 us
  Pallas kernels: 32 us -> 35.9 us
  waiting for transfers between devices: 31.4 us -> 32.7 us
  starting transfers between devices: 31.5 us -> 30.4 us
    unnamed x17 -> x10, local copies, waits for them, and re-layouts: 7.48 us -> 1.95 us
    pallas_call x1, Pallas kernels: 2.5 us -> 5.26 us  [score_parts(): pl.pallas_call(functools.partial(score_kernel, batch_count, ranks), grid=...]
    pallas_call x1, Pallas kernels: 22 us -> 23.1 us  [images(): pl.pallas_call(functools.partial(image_kernel, batch_count, total, per),...]
  transfers between devices with their start and end apart: 23 -> 23, of which waited for: 12 -> 12; matrix products, arithmetic and copies ran while one was open for 0% -> 0% of each run, Pallas kernels for 28% -> 29%
where the time goes in v9:
time: 103 us
  Pallas kernels  35.9 us (35%)
  waiting for transfers between devices  32.7 us (32%)
  starting transfers between devices  30.4 us (30%)
  local copies, waits for them, and re-layouts  1.95 us (2%)
  other arithmetic  1.44 us (1%)
    ppermute x22, waiting for transfers between devices, swap(): return lax.ppermute(x, axis, [(i, i ^ bit) for i in range(count)])  31.8 us
    ppermute x22, starting transfers between devices, swap(): return lax.ppermute(x, axis, [(i, i ^ bit) for i in range(count)])  24.5 us
    pallas_call x1, Pallas kernels, images(): pl.pallas_call(functools.partial(image_kernel, batch_count, total, per),...  23.1 us
    all_to_all x1, starting transfers between devices, per_device(): lax.all_to_all(gate(sent, [rot, lefts[1], halves[1], halves[3]]), 'wide',...  5.9 us
    pallas_call x1, Pallas kernels, score_parts(): pl.pallas_call(functools.partial(score_kernel, batch_count, ranks), grid=...  5.26 us
    pallas_call x1, Pallas kernels, rotate(): pl.pallas_call(functools.partial(rotate_kernel, len(act_pieces)), in_spec...  3.63 us
  transfers between devices with their start and end apart: 23, of which 12 were waited for; matrix products, arithmetic and copies ran while one was open for 0% of the time, Pallas kernels for 29%

profile of v9, /device:TPU:0, one launch (start us, length us, event | category | flops | bytes accessed | tf_op | source)
XLA Modules:
  0.0 102.5 jit_solution(13329062743165100356)
XLA Ops:
  0.0 1.7 %copy-done = bf16[2,16,36864]{2,1,0:T(8,128)(2,1)S(1)} copy-done((bf16[2,16,36864]{2,1,0:T(8,128)(2,1)S(1)}, bf16[2,16,36864]{2,1,0:T(8,128)(2,1)}, u32[]{:S(2)}) %copy-start) | copy-done | bytes 2359320
  2.6 4.0 %collective-permute-start.1 = (bf16[16,4096]{1,0:T(8,128)(2,1)S(1)}, bf16[16,4096]{1,0:T(8,128)(2,1)S(1)}, u32[]{:S(2)}, u32[]{:S(2)}) collective-permute-start(bf16[16,4096]{1,0:T(8,128)(2,1)S(1)} %copy-done.2), channel_id=1, source_target_pairs={{0,8},{1,9},{2,10},{3,11},{4,12},{5,13},{6,14},{7,15},{8,0},{9,1},... | collective-permute-start | bytes 393224 | tf_op jit(solution)/shard_map/ppermute | solution.py:31
  7.2 5.7 %collective-permute-done.1.second_ref = bf16[16,4096]{1,0:T(8,128)(2,1)S(1)} collective-permute-done((bf16[16,4096]{1,0:T(8,128)(2,1)S(1)}, bf16[16,4096]{1,0:T(8,128)(2,1)S(1)}, u32[]{:S(2)}, u32[]{:S(2)}) %collective-permute-start.1) | collective-permute-done | bytes 131104 | tf_op jit(solution)/shard_map/ppermute | solution.py:31
  13.1 1.6 %collective-permute-start.2 = (bf16[16,10240]{1,0:T(8,128)(2,1)S(1)}, bf16[16,10240]{1,0:T(8,128)(2,1)S(1)}, u32[]{:S(2)}, u32[]{:S(2)}) collective-permute-start(bf16[16,10240]{1,0:T(8,128)(2,1)S(1)} %get-tuple-element.19._), channel_id=1, source_target_pairs={{0,2},{1,3},{2,0},{3,1},{4,6},{5,7},{6,4},{7,5},{8,10},{9,11},{10,... | collective-permute-start | bytes 983048 | tf_op jit(solution)/shard_map/ppermute | solution.py:31
  15.4 1.6 %shard_map.86.refs_1_.__0_ = bf16[16,16,2176]{2,1,0:T(8,128)(2,1)} custom-call(s32[16]{0:T(128)S(1)} %copy-done.4, bf16[16,32768]{1,0:T(8,128)(2,1)S(1)} %copy-done.1, bf16[16,10240]{1,0:T(8,128)(2,1)S(1)} %get-tuple-element.19._), custom_call_target="tpu_custom_call" | custom-call | bytes 1 | tf_op jit(solution)/shard_map/pallas_call | solution.py:179
  17.1 4.6 %collective-permute-done.3.refs_0_.__0_ = bf16[32,4096]{1,0:T(8,128)(2,1)S(1)} collective-permute-done((bf16[32,4096]{1,0:T(8,128)(2,1)S(1)}, bf16[32,4096]{1,0:T(8,128)(2,1)S(1)}, u32[]{:S(2)}, u32[]{:S(2)}) %collective-permute-start.3) | collective-permute-done | bytes 262176 | tf_op jit(solution)/shard_map/ppermute | solution.py:31
  24.1 2.2 %collective-permute-start.5 = (bf16[16,6144]{1,0:T(8,128)(2,1)S(1)}, bf16[16,6144]{1,0:T(8,128)(2,1)S(1)}, u32[]{:S(2)}, u32[]{:S(2)}) collective-permute-start(bf16[16,6144]{1,0:T(8,128)(2,1)S(1)} %get-tuple-element.21.__1_.refs_5_), channel_id=1, source_target_pairs={{0,8},{1,9},{2,10},{3,11},{4,12},{5,13},{6,14},{7,15},{8,0},{9,1},... | collective-permute-start | bytes 589832 | tf_op jit(solution)/shard_map/ppermute | solution.py:31
  26.3 1.5 %collective-permute-start.9 = (bf16[32,4096]{1,0:T(8,128)(2,1)S(1)}, bf16[32,4096]{1,0:T(8,128)(2,1)S(1)}, u32[]{:S(2)}, u32[]{:S(2)}) collective-permute-start(bf16[32,4096]{1,0:T(8,128)(2,1)S(1)} %shard_map.89.refs_1_), channel_id=1, source_target_pairs={{0,2},{1,3},{2,0},{3,1},{4,6},{5,7},{6,4},{7,5},{8,10},{9,11},{10,... | collective-permute-start | bytes 786440 | tf_op jit(solution)/shard_map/ppermute | solution.py:31
  27.8 3.6 %shard_map.90 = (bf16[4096,128]{1,0:T(8,128)(2,1)S(1)}, bf16[8,512,512]{2,1,0:T(8,128)(2,1)S(1)}) custom-call(bf16[32,4096]{1,0:T(8,128)(2,1)S(1)} %shard_map.88.refs_0_, bf16[32,4096]{1,0:T(8,128)(2,1)S(1)} %shard_map.89.refs_1_, bf16[32,4096]{1,0:T(8,128)(2,1)S(1)} %collective-permute-done.6.refs_2_, bf16[32,4096]{1,0:T(8,128)(2,1)S(1)} %collective-permute-done.7.refs_3_, ...), custom_call_target="tpu_custom_call" | custom-call | bytes 1 | tf_op jit(solution)/shard_map/pallas_call | solution.py:210
  31.4 4.4 %collective-permute-done.5.got_ref = bf16[16,6144]{1,0:T(8,128)(2,1)S(1)} collective-permute-done((bf16[16,6144]{1,0:T(8,128)(2,1)S(1)}, bf16[16,6144]{1,0:T(8,128)(2,1)S(1)}, u32[]{:S(2)}, u32[]{:S(2)}) %collective-permute-start.5) | collective-permute-done | bytes 196640 | tf_op jit(solution)/shard_map/ppermute | solution.py:31
  36.2 4.7 %collective-permute-done.8.got_ref = bf16[16,4096]{1,0:T(8,128)(2,1)S(1)} collective-permute-done((bf16[16,4096]{1,0:T(8,128)(2,1)S(1)}, bf16[16,4096]{1,0:T(8,128)(2,1)S(1)}, u32[]{:S(2)}, u32[]{:S(2)}) %collective-permute-start.8) | collective-permute-done | bytes 131104 | tf_op jit(solution)/shard_map/ppermute | solution.py:31
  41.0 1.6 %collective-permute-start.10 = (bf16[16,2048]{1,0:T(8,128)(2,1)S(1)}, bf16[16,2048]{1,0:T(8,128)(2,1)S(1)}, u32[]{:S(2)}, u32[]{:S(2)}) collective-permute-start(bf16[16,2048]{1,0:T(8,128)(2,1)S(1)} %get-tuple-element.26.__1_.refs_2_), channel_id=1, source_target_pairs={{0,16},{16,0},{1,17},{17,1},{2,18},{18,2},{3,19},{19,3},{4,20},{20... | collective-permute-start | bytes 196616 | tf_op jit(solution)/shard_map/ppermute | solution.py:31
  42.6 2.8 %collective-permute-done.10.__1_.refs_4_ = bf16[16,2048]{1,0:T(8,128)(2,1)S(1)} collective-permute-done((bf16[16,2048]{1,0:T(8,128)(2,1)S(1)}, bf16[16,2048]{1,0:T(8,128)(2,1)S(1)}, u32[]{:S(2)}, u32[]{:S(2)}) %collective-permute-start.10) | collective-permute-done | bytes 65568 | tf_op jit(solution)/shard_map/ppermute | solution.py:31
  45.4 1.5 %collective-permute-start.13 = (bf16[16,2048]{1,0:T(8,128)(2,1)S(1)}, bf16[16,2048]{1,0:T(8,128)(2,1)S(1)}, u32[]{:S(2)}, u32[]{:S(2)}) collective-permute-start(bf16[16,2048]{1,0:T(8,128)(2,1)S(1)} %get-tuple-element.28.refs_0_), channel_id=1, source_target_pairs={{0,16},{16,0},{1,17},{17,1},{2,18},{18,2},{3,19},{19,3},{4,20},{20... | collective-permute-start | bytes 196616 | tf_op jit(solution)/shard_map/ppermute | solution.py:31
  48.4 1.4 %collective-permute-done.13.__2_.refs_1_ = bf16[16,2048]{1,0:T(8,128)(2,1)S(1)} collective-permute-done((bf16[16,2048]{1,0:T(8,128)(2,1)S(1)}, bf16[16,2048]{1,0:T(8,128)(2,1)S(1)}, u32[]{:S(2)}, u32[]{:S(2)}) %collective-permute-start.13) | collective-permute-done | bytes 65568 | tf_op jit(solution)/shard_map/ppermute | solution.py:31
  49.9 5.9 %all-to-all-start = ((bf16[16,16,2176]{2,1,0:T(8,128)(2,1)}), bf16[16,16,2176]{2,1,0:T(8,128)(2,1)}, u32[]{:S(2)}, u32[]{:S(2)}) async-start(bf16[16,16,2176]{2,1,0:T(8,128)(2,1)} %shard_map.96), calls=%async_computation | async-start | bytes 2228224 | tf_op jit(solution)/shard_map/all_to_all | solution.py:456
  55.8 23.1 %shard_map.97.image_ref = f32[2,2048,256]{2,1,0:T(8,128)} custom-call(bf16[4096,256]{1,0:T(8,128)(2,1)S(1)} %shard_map.95.__1_.rot_ref, bf16[16,2048]{1,0:T(8,128)(2,1)S(1)} %get-tuple-element.28.refs_0_, bf16[16,2048]{1,0:T(8,128)(2,1)S(1)} %collective-permute-done.13.__2_.refs_1_, bf16[16,2048]{1,0:T(8,128)(2,1)S(1)} %get-tuple-element.26.__1_.refs_2_, ...), custom_call_target="tpu_custom_call" | custom-call | flops 17179869184 | bytes 16777216 | tf_op jit(solution)/shard_map/pallas_call | solution.py:325
  79.9 5.3 %shard_map.98 = f32[2,8,1]{2,1,0:T(8,128)} custom-call(bf16[16,16,2176]{2,1,0:T(8,128)(2,1)} %all-to-all-done.grad_ref.ids_ref, bf16[512,2048]{1,0:T(8,128)(2,1)} %basis_ref.1, f32[2,2048,256]{2,1,0:T(8,128)} %shard_map.97.image_ref, bf16[16,16,2176]{2,1,0:T(8,128)(2,1)} %all-to-all-done.grad_ref.ids_ref), custom_call_target="tpu_custom_call" | custom-call | flops 536870912 | bytes 4194304 | tf_op jit(solution)/shard_map/pallas_call | solution.py:378
  85.9 2.1 %collective-permute-start.17 = (f32[2,8,1]{2,1,0:T(8,128)}, f32[2,8,1]{2,1,0:T(8,128)S(1)}, u32[]{:S(2)}, u32[]{:S(2)}) collective-permute-start(f32[2,8,1]{2,1,0:T(8,128)} %shard_map.98), channel_id=1, source_target_pairs={{0,2},{1,3},{2,0},{3,1},{4,6},{5,7},{6,4},{7,5},{8,10},{9,11},{10,... | collective-permute-start | bytes 200 | tf_op jit(solution)/shard_map/ppermute | solution.py:31
  87.9 1.8 %collective-permute-done.17 = f32[2,8,1]{2,1,0:T(8,128)S(1)} collective-permute-done((f32[2,8,1]{2,1,0:T(8,128)}, f32[2,8,1]{2,1,0:T(8,128)S(1)}, u32[]{:S(2)}, u32[]{:S(2)}) %collective-permute-start.17) | collective-permute-done | bytes 96 | tf_op jit(solution)/shard_map/ppermute | solution.py:31
  89.8 1.4 %collective-permute-done.18 = f32[2,8,1]{2,1,0:T(8,128)S(1)} collective-permute-done((f32[2,8,1]{2,1,0:T(8,128)}, f32[2,8,1]{2,1,0:T(8,128)S(1)}, u32[]{:S(2)}, u32[]{:S(2)}) %collective-permute-start.18) | collective-permute-done | bytes 96 | tf_op jit(solution)/shard_map/ppermute | solution.py:31
  91.9 3.1 %collective-permute-start.19 = (f32[2,8,1]{2,1,0:T(8,128)S(1)}, f32[2,8,1]{2,1,0:T(8,128)S(1)}, u32[]{:S(2)}, u32[]{:S(2)}) collective-permute-start(f32[2,8,1]{2,1,0:T(8,128)S(1)} %add_add_fusion.1), channel_id=1, source_target_pairs={{0,4},{1,5},{2,6},{3,7},{4,0},{5,1},{6,2},{7,3},{8,12},{9,13},{10,... | collective-permute-start | bytes 200 | tf_op jit(solution)/shard_map/ppermute | solution.py:31
  97.4 2.2 %collective-permute-done.20 = f32[2,8,1]{2,1,0:T(8,128)S(1)} collective-permute-done((f32[2,8,1]{2,1,0:T(8,128)S(1)}, f32[2,8,1]{2,1,0:T(8,128)S(1)}, u32[]{:S(2)}, u32[]{:S(2)}) %collective-permute-start.20) | collective-permute-done | bytes 96 | tf_op jit(solution)/shard_map/ppermute | solution.py:31
  99.5 2.3 %collective-permute-done.21 = f32[2,8,1]{2,1,0:T(8,128)S(1)} collective-permute-done((f32[2,8,1]{2,1,0:T(8,128)S(1)}, f32[2,8,1]{2,1,0:T(8,128)S(1)}, u32[]{:S(2)}, u32[]{:S(2)}) %collective-permute-start.21) | collective-permute-done | bytes 96 | tf_op jit(solution)/shard_map/ppermute | solution.py:31
  (53 shorter events, 12.3 us)
Async XLA Ops:
  1.7 13.8 %copy-start.4 = (s32[16]{0:T(128)S(1)}, s32[16]{0:T(128)}, u32[]{:S(2)}) copy-start(s32[16]{0:T(128)} %ids_ref.1) | copy-start | bytes 196
  1.8 11.2 %collective-permute-start = (bf16[16,18432]{1,0:T(8,128)(2,1)S(1)}, bf16[16,18432]{1,0:T(8,128)(2,1)S(1)}, u32[]{:S(2)}, u32[]{:S(2)}) collective-permute-start(bf16[16,18432]{1,0:T(8,128)(2,1)S(1)} %get-tuple-element.18), channel_id=1, source_target_pairs={{0,1},{1,0},{2,3},{3,2},{4,5},{5,4},{6,7},{7,6},{8,9},{9,8},{10,11... | collective-permute-start | bytes 1769480 | tf_op jit(solution)/shard_map/ppermute | solution.py:31
  2.6 10.3 %collective-permute-start.1 = (bf16[16,4096]{1,0:T(8,128)(2,1)S(1)}, bf16[16,4096]{1,0:T(8,128)(2,1)S(1)}, u32[]{:S(2)}, u32[]{:S(2)}) collective-permute-start(bf16[16,4096]{1,0:T(8,128)(2,1)S(1)} %copy-done.2), channel_id=1, source_target_pairs={{0,8},{1,9},{2,10},{3,11},{4,12},{5,13},{6,14},{7,15},{8,0},{9,1},... | collective-permute-start | bytes 393224 | tf_op jit(solution)/shard_map/ppermute | solution.py:31
  13.1 9.0 %collective-permute-start.2 = (bf16[16,10240]{1,0:T(8,128)(2,1)S(1)}, bf16[16,10240]{1,0:T(8,128)(2,1)S(1)}, u32[]{:S(2)}, u32[]{:S(2)}) collective-permute-start(bf16[16,10240]{1,0:T(8,128)(2,1)S(1)} %get-tuple-element.19._), channel_id=1, source_target_pairs={{0,2},{1,3},{2,0},{3,1},{4,6},{5,7},{6,4},{7,5},{8,10},{9,11},{10,... | collective-permute-start | bytes 983048 | tf_op jit(solution)/shard_map/ppermute | solution.py:31
  14.8 6.9 %collective-permute-start.3 = (bf16[32,4096]{1,0:T(8,128)(2,1)S(1)}, bf16[32,4096]{1,0:T(8,128)(2,1)S(1)}, u32[]{:S(2)}, u32[]{:S(2)}) collective-permute-start(bf16[32,4096]{1,0:T(8,128)(2,1)S(1)} %shard_map.84.refs_0_.__0_), channel_id=1, source_target_pairs={{0,4},{1,5},{2,6},{3,7},{4,0},{5,1},{6,2},{7,3},{8,12},{9,13},{10,... | collective-permute-start | bytes 786440 | tf_op jit(solution)/shard_map/ppermute | solution.py:31
  22.2 5.5 %collective-permute-start.7 = (bf16[32,4096]{1,0:T(8,128)(2,1)S(1)}, bf16[32,4096]{1,0:T(8,128)(2,1)S(1)}, u32[]{:S(2)}, u32[]{:S(2)}) collective-permute-start(bf16[32,4096]{1,0:T(8,128)(2,1)S(1)} %shard_map.89.refs_1_), channel_id=1, source_target_pairs={{0,1},{1,0},{2,3},{3,2},{4,5},{5,4},{6,7},{7,6},{8,9},{9,8},{10,11... | collective-permute-start | bytes 786440 | tf_op jit(solution)/shard_map/ppermute | solution.py:31
  22.3 5.5 %collective-permute-start.6 = (bf16[32,4096]{1,0:T(8,128)(2,1)S(1)}, bf16[32,4096]{1,0:T(8,128)(2,1)S(1)}, u32[]{:S(2)}, u32[]{:S(2)}) collective-permute-start(bf16[32,4096]{1,0:T(8,128)(2,1)S(1)} %shard_map.88.refs_0_), channel_id=1, source_target_pairs={{0,1},{1,0},{2,3},{3,2},{4,5},{5,4},{6,7},{7,6},{8,9},{9,8},{10,11... | collective-permute-start | bytes 786440 | tf_op jit(solution)/shard_map/ppermute | solution.py:31
  22.8 13.0 %collective-permute-start.4 = (bf16[32,4096]{1,0:T(8,128)(2,1)S(1)}, bf16[32,4096]{1,0:T(8,128)(2,1)S(1)}, u32[]{:S(2)}, u32[]{:S(2)}) collective-permute-start(bf16[32,4096]{1,0:T(8,128)(2,1)S(1)} %shard_map.88.refs_0_), channel_id=1, source_target_pairs={{0,2},{1,3},{2,0},{3,1},{4,6},{5,7},{6,4},{7,5},{8,10},{9,11},{10,... | collective-permute-start | bytes 786440 | tf_op jit(solution)/shard_map/ppermute | solution.py:31
  24.1 11.7 %collective-permute-start.5 = (bf16[16,6144]{1,0:T(8,128)(2,1)S(1)}, bf16[16,6144]{1,0:T(8,128)(2,1)S(1)}, u32[]{:S(2)}, u32[]{:S(2)}) collective-permute-start(bf16[16,6144]{1,0:T(8,128)(2,1)S(1)} %get-tuple-element.21.__1_.refs_5_), channel_id=1, source_target_pairs={{0,8},{1,9},{2,10},{3,11},{4,12},{5,13},{6,14},{7,15},{8,0},{9,1},... | collective-permute-start | bytes 589832 | tf_op jit(solution)/shard_map/ppermute | solution.py:31
  26.3 16.3 %collective-permute-start.9 = (bf16[32,4096]{1,0:T(8,128)(2,1)S(1)}, bf16[32,4096]{1,0:T(8,128)(2,1)S(1)}, u32[]{:S(2)}, u32[]{:S(2)}) collective-permute-start(bf16[32,4096]{1,0:T(8,128)(2,1)S(1)} %shard_map.89.refs_1_), channel_id=1, source_target_pairs={{0,2},{1,3},{2,0},{3,1},{4,6},{5,7},{6,4},{7,5},{8,10},{9,11},{10,... | collective-permute-start | bytes 786440 | tf_op jit(solution)/shard_map/ppermute | solution.py:31
  35.9 5.0 %collective-permute-start.8 = (bf16[16,4096]{1,0:T(8,128)(2,1)S(1)}, bf16[16,4096]{1,0:T(8,128)(2,1)S(1)}, u32[]{:S(2)}, u32[]{:S(2)}) collective-permute-start(bf16[16,4096]{1,0:T(8,128)(2,1)S(1)} %get-tuple-element.25), channel_id=1, source_target_pairs={{0,4},{1,5},{2,6},{3,7},{4,0},{5,1},{6,2},{7,3},{8,12},{9,13},{10,... | collective-permute-start | bytes 393224 | tf_op jit(solution)/shard_map/ppermute | solution.py:31
  41.0 4.3 %collective-permute-start.10 = (bf16[16,2048]{1,0:T(8,128)(2,1)S(1)}, bf16[16,2048]{1,0:T(8,128)(2,1)S(1)}, u32[]{:S(2)}, u32[]{:S(2)}) collective-permute-start(bf16[16,2048]{1,0:T(8,128)(2,1)S(1)} %get-tuple-element.26.__1_.refs_2_), channel_id=1, source_target_pairs={{0,16},{16,0},{1,17},{17,1},{2,18},{18,2},{3,19},{19,3},{4,20},{20... | collective-permute-start | bytes 196616 | tf_op jit(solution)/shard_map/ppermute | solution.py:31
  42.6 4.8 %collective-permute-start.11 = (bf16[32,4096]{1,0:T(8,128)(2,1)S(1)}, bf16[32,4096]{1,0:T(8,128)(2,1)S(1)}, u32[]{:S(2)}, u32[]{:S(2)}) collective-permute-start(bf16[32,4096]{1,0:T(8,128)(2,1)S(1)} %shard_map.93.refs_0_), channel_id=1, source_target_pairs={{0,1},{1,0},{2,3},{3,2},{4,5},{5,4},{6,7},{7,6},{8,9},{9,8},{10,11... | collective-permute-start | bytes 786440 | tf_op jit(solution)/shard_map/ppermute | solution.py:31
  45.4 2.0 %collective-permute-start.12 = (bf16[32,4096]{1,0:T(8,128)(2,1)S(1)}, bf16[32,4096]{1,0:T(8,128)(2,1)S(1)}, u32[]{:S(2)}, u32[]{:S(2)}) collective-permute-start(bf16[32,4096]{1,0:T(8,128)(2,1)S(1)} %shard_map.94.refs_1_), channel_id=1, source_target_pairs={{0,1},{1,0},{2,3},{3,2},{4,5},{5,4},{6,7},{7,6},{8,9},{9,8},{10,11... | collective-permute-start | bytes 786440 | tf_op jit(solution)/shard_map/ppermute | solution.py:31
  45.4 4.5 %collective-permute-start.13 = (bf16[16,2048]{1,0:T(8,128)(2,1)S(1)}, bf16[16,2048]{1,0:T(8,128)(2,1)S(1)}, u32[]{:S(2)}, u32[]{:S(2)}) collective-permute-start(bf16[16,2048]{1,0:T(8,128)(2,1)S(1)} %get-tuple-element.28.refs_0_), channel_id=1, source_target_pairs={{0,16},{16,0},{1,17},{17,1},{2,18},{18,2},{3,19},{19,3},{4,20},{20... | collective-permute-start | bytes 196616 | tf_op jit(solution)/shard_map/ppermute | solution.py:31
  46.9 3.0 %collective-permute-start.14 = (bf16[16,2048]{1,0:T(8,128)(2,1)S(1)}, bf16[16,2048]{1,0:T(8,128)(2,1)S(1)}, u32[]{:S(2)}, u32[]{:S(2)}) collective-permute-start(bf16[16,2048]{1,0:T(8,128)(2,1)S(1)} %get-tuple-element.26.__1_.refs_2_), channel_id=1, source_target_pairs={{0,1},{1,0},{2,3},{3,2},{4,5},{5,4},{6,7},{7,6},{8,9},{9,8},{10,11... | collective-permute-start | bytes 196616 | tf_op jit(solution)/shard_map/ppermute | solution.py:31
  47.1 2.8 %collective-permute-start.15 = (bf16[16,2048]{1,0:T(8,128)(2,1)S(1)}, bf16[16,2048]{1,0:T(8,128)(2,1)S(1)}, u32[]{:S(2)}, u32[]{:S(2)}) collective-permute-start(bf16[16,2048]{1,0:T(8,128)(2,1)S(1)} %collective-permute-done.10.__1_.refs_4_), channel_id=1, source_target_pairs={{0,1},{1,0},{2,3},{3,2},{4,5},{5,4},{6,7},{7,6},{8,9},{9,8},{10,11... | collective-permute-start | bytes 196616 | tf_op jit(solution)/shard_map/ppermute | solution.py:31
  49.9 30.0 %all-to-all-start = ((bf16[16,16,2176]{2,1,0:T(8,128)(2,1)}), bf16[16,16,2176]{2,1,0:T(8,128)(2,1)}, u32[]{:S(2)}, u32[]{:S(2)}) async-start(bf16[16,16,2176]{2,1,0:T(8,128)(2,1)} %shard_map.96), calls=%async_computation | async-start | bytes 2228224 | tf_op jit(solution)/shard_map/all_to_all | solution.py:456
  85.1 2.8 %collective-permute-start.16 = (f32[2,8,1]{2,1,0:T(8,128)}, f32[2,8,1]{2,1,0:T(8,128)S(1)}, u32[]{:S(2)}, u32[]{:S(2)}) collective-permute-start(f32[2,8,1]{2,1,0:T(8,128)} %shard_map.98), channel_id=1, source_target_pairs={{0,1},{1,0},{2,3},{3,2},{4,5},{5,4},{6,7},{7,6},{8,9},{9,8},{10,11... | collective-permute-start | bytes 200 | tf_op jit(solution)/shard_map/ppermute | solution.py:31
  85.9 3.9 %collective-permute-start.17 = (f32[2,8,1]{2,1,0:T(8,128)}, f32[2,8,1]{2,1,0:T(8,128)S(1)}, u32[]{:S(2)}, u32[]{:S(2)}) collective-permute-start(f32[2,8,1]{2,1,0:T(8,128)} %shard_map.98), channel_id=1, source_target_pairs={{0,2},{1,3},{2,0},{3,1},{4,6},{5,7},{6,4},{7,5},{8,10},{9,11},{10,... | collective-permute-start | bytes 200 | tf_op jit(solution)/shard_map/ppermute | solution.py:31
  87.9 3.3 %collective-permute-start.18 = (f32[2,8,1]{2,1,0:T(8,128)}, f32[2,8,1]{2,1,0:T(8,128)S(1)}, u32[]{:S(2)}, u32[]{:S(2)}) collective-permute-start(f32[2,8,1]{2,1,0:T(8,128)} %shard_map.98), channel_id=1, source_target_pairs={{0,3},{1,2},{2,1},{3,0},{4,7},{5,6},{6,5},{7,4},{8,11},{9,10},{10,... | collective-permute-start | bytes 200 | tf_op jit(solution)/shard_map/ppermute | solution.py:31
  91.9 5.4 %collective-permute-start.19 = (f32[2,8,1]{2,1,0:T(8,128)S(1)}, f32[2,8,1]{2,1,0:T(8,128)S(1)}, u32[]{:S(2)}, u32[]{:S(2)}) collective-permute-start(f32[2,8,1]{2,1,0:T(8,128)S(1)} %add_add_fusion.1), channel_id=1, source_target_pairs={{0,4},{1,5},{2,6},{3,7},{4,0},{5,1},{6,2},{7,3},{8,12},{9,13},{10,... | collective-permute-start | bytes 200 | tf_op jit(solution)/shard_map/ppermute | solution.py:31
  95.0 4.5 %collective-permute-start.20 = (f32[2,8,1]{2,1,0:T(8,128)S(1)}, f32[2,8,1]{2,1,0:T(8,128)S(1)}, u32[]{:S(2)}, u32[]{:S(2)}) collective-permute-start(f32[2,8,1]{2,1,0:T(8,128)S(1)} %add_add_fusion.1), channel_id=1, source_target_pairs={{0,8},{1,9},{2,10},{3,11},{4,12},{5,13},{6,14},{7,15},{8,0},{9,1},... | collective-permute-start | bytes 200 | tf_op jit(solution)/shard_map/ppermute | solution.py:31
  96.4 5.4 %collective-permute-start.21 = (f32[2,8,1]{2,1,0:T(8,128)S(1)}, f32[2,8,1]{2,1,0:T(8,128)S(1)}, u32[]{:S(2)}, u32[]{:S(2)}) collective-permute-start(f32[2,8,1]{2,1,0:T(8,128)S(1)} %add_add_fusion.1), channel_id=1, source_target_pairs={{0,12},{1,13},{2,14},{3,15},{4,8},{5,9},{6,10},{7,11},{8,4},{9,5},... | collective-permute-start | bytes 200 | tf_op jit(solution)/shard_map/ppermute | solution.py:31
  (4 other events, 21.3 us)

commit v10 on v9

--- a/solution.py
+++ b/solution.py
@@ -127,22 +127,22 @@
     )(flags, keep, got, *after)
 
 
-def join_kernel(first_ref, second_ref, out_ref):
+def join_kernel(first_ref, second_ref, _, out_ref):
     rows = first_ref.shape[0]
     out_ref[:rows, :] = first_ref[...]
     out_ref[rows:, :] = second_ref[...]
 
 
-def join(first, second):
+def join(first, second, after):
     rows, width = first.shape
     return pl.pallas_call(
         join_kernel,
-        in_specs=in_vmem(2),
+        in_specs=in_vmem(2) + in_place(1),
         out_specs=in_vmem(1)[0],
         out_shape=jax.ShapeDtypeStruct((2 * rows, width), first.dtype),
         compiler_params=params(16),
         cost_estimate=pl.CostEstimate(flops=0, bytes_accessed=1, transcendentals=0),
-    )(first, second)
+    )(first, second, after)
 
 
 def gate_kernel(*_):
@@ -161,29 +161,86 @@
     )(array, *after)
 
 
-def cut_grads_kernel(ids_ref, grad_ref, _, out_ref):
-    count, rows, width = out_ref.shape
-    cols = width - LANES
+def grads_core_kernel(ids_ref, grad_ref, _, out_ref):
+    rows, hidden = grad_ref.shape
+    wide = lax.axis_size("wide")
+    cols = hidden // wide
+    me = lax.axis_index("wide")
     row = lax.broadcasted_iota(jnp.int32, (rows, LANES), 0)
     ids = jnp.zeros((rows, LANES), jnp.int32)
     for t in range(rows):
         ids = jnp.where(row == t, ids_ref[t], ids)
-    ids = ids.astype(jnp.float32).astype(out_ref.dtype)
-    for to in range(count):
-        out_ref[to, :, :cols] = grad_ref[:, to * cols:(to + 1) * cols]
-        out_ref[to, :, cols:] = ids
-
-
-def cut_grads(ids, grads, after, count):
+    out_ref[:, wide // 2 * cols:] = ids.astype(jnp.float32).astype(out_ref.dtype)
+    for q in range(wide // 2):
+        src = pl.multiple_of((me ^ (2 * q + 1)) * cols, cols)
+        out_ref[:, q * cols:(q + 1) * cols] = grad_ref[:, pl.ds(src, cols)]
+
+
+def grads_core(ids, grads, after):
     rows, hidden = grads.shape
     return pl.pallas_call(
-        cut_grads_kernel,
+        grads_core_kernel,
         in_specs=in_smem(1) + in_vmem(1) + in_place(1),
         out_specs=in_vmem(1)[0],
-        out_shape=jax.ShapeDtypeStruct((count, rows, hidden // count + LANES), grads.dtype),
+        out_shape=jax.ShapeDtypeStruct((rows, hidden // 2 + LANES), grads.dtype),
         compiler_params=params(16),
         cost_estimate=pl.CostEstimate(flops=0, bytes_accessed=1, transcendentals=0),
     )(ids, grads, after)
+
+
+def grads_y_kernel(grad_ref, sent_ref, got_ref, _, out_ref):
+    rows, hidden = grad_ref.shape
+    wide = lax.axis_size("wide")
+    cols = hidden // wide
+    me = lax.axis_index("wide")
+    for k in range(wide // 4):
+        src = pl.multiple_of((me ^ (4 * k + 2)) * cols, cols)
+        place = slice(k * cols, (k + 1) * cols)
+        out_ref[:rows, place] = grad_ref[:, pl.ds(src, cols)]
+        out_ref[rows:, place] = got_ref[:, (2 * k + 1) * cols:(2 * k + 2) * cols]
+    ids = slice(wide // 4 * cols, wide // 4 * cols + LANES)
+    out_ref[:rows, ids] = sent_ref[:, wide // 2 * cols:]
+    out_ref[rows:, ids] = got_ref[:, wide // 2 * cols:]
+
+
+def grads_y(grads, sent, got, after):
+    rows, hidden = grads.shape
+    return pl.pallas_call(
+        grads_y_kernel,
+        in_specs=in_vmem(3) + in_place(1),
+        out_specs=in_vmem(1)[0],
+        out_shape=jax.ShapeDtypeStruct((2 * rows, hidden // 4 + LANES), grads.dtype),
+        compiler_params=params(16),
+        cost_estimate=pl.CostEstimate(flops=0, bytes_accessed=1, transcendentals=0),
+    )(grads, sent, got, after)
+
+
+def grads_z_kernel(grad_ref, sent_ref, got_ref, over_ref, *out_refs):
+    rows = grad_ref.shape[0]
+    cols = out_refs[0].shape[1] - LANES
+    me = lax.axis_index("wide")
+    for k, out_ref in enumerate(out_refs):
+        src = pl.multiple_of((me ^ (4 * k)) * cols, cols)
+        out_ref[:rows, :cols] = grad_ref[:, pl.ds(src, cols)]
+        out_ref[rows:2 * rows, :cols] = got_ref[:, 2 * k * cols:(2 * k + 1) * cols]
+        out_ref[2 * rows:, :cols] = over_ref[:, k * cols:(k + 1) * cols]
+        out_ref[:rows, cols:] = sent_ref[:, 2 * len(out_refs) * cols:]
+        out_ref[rows:2 * rows, cols:] = got_ref[:, 2 * len(out_refs) * cols:]
+        out_ref[2 * rows:, cols:] = over_ref[:, len(out_refs) * cols:]
+
+
+def grads_z(grads, sent, got, over, wide_count):
+    rows, hidden = grads.shape
+    count = wide_count // 4
+    piece = jax.ShapeDtypeStruct((4 * rows, hidden // wide_count + LANES), grads.dtype)
+    return pl.pallas_call(
+        grads_z_kernel,
+        in_specs=in_vmem(4),
+        out_specs=in_vmem(count),
+        out_shape=[piece] * count,
+        compiler_params=params(16),
+        cost_estimate=pl.CostEstimate(flops=0, bytes_accessed=1, transcendentals=0),
+    )(grads, sent, got, over)
 
 
 def rotate_kernel(act_count, *refs):
@@ -337,7 +394,7 @@
             pltpu.VMEM((batch_count * rows, chunk), jnp.bfloat16),
             pltpu.VMEM((batch_count * rows, chunk), jnp.bfloat16),
         ],
-        compiler_params=params(50),
+        compiler_params=params(44),
         cost_estimate=pl.CostEstimate(
             flops=2 * hidden * width * (tokens + 256) * batch_count,
             bytes_accessed=2 * hidden * width,
@@ -346,23 +403,29 @@
     )(rot, *lefts, *halves, eigenvalues)
 
 
-def score_kernel(batch_count, ranks, grad_ref, basis_ref, image_ref, ids_ref, out_ref, token_ref):
+def score_kernel(batch_count, ranks, count, *refs):
+    grad_refs, ids_refs = refs[:count], refs[count:2 * count]
+    basis_ref, image_ref, out_ref, token_ref = refs[2 * count:]
     step = pl.program_id(0)
-    me = lax.axis_index("wide")
+    rows = grad_refs[0].shape[0] // 4
+
+    def tokens_of(pieces):
+        return jnp.concatenate(
+            [pieces[r // 4][r % 4 * rows:(r % 4 + 1) * rows, :] for r in ranks], axis=0
+        )
 
     @pl.when(step == 0)
     def _():
         token_ref[...] = jnp.zeros_like(token_ref)
 
-    grads = jnp.concatenate([grad_ref[me ^ r] for r in ranks], axis=0)
-    turned = jnp.dot(grads, basis_ref[...], preferred_element_type=jnp.float32)
+    turned = jnp.dot(tokens_of(grad_refs), basis_ref[...], preferred_element_type=jnp.float32)
     turned = turned.astype(jnp.bfloat16).T.astype(jnp.float32)
     for b in range(batch_count):
         token_ref[b:b + 1, :] += jnp.sum(image_ref[b] * turned, axis=0, keepdims=True)
 
     @pl.when(step == pl.num_programs(0) - 1)
     def _():
-        ids = jnp.concatenate([ids_ref[me ^ r] for r in ranks], axis=0).astype(jnp.float32)
+        ids = tokens_of(ids_refs).astype(jnp.float32)
         seqs = lax.broadcasted_iota(jnp.int32, ids.shape, 1).astype(jnp.float32)
         member = jnp.where(ids == seqs, 1.0, 0.0).T
         for b in range(batch_count):
@@ -370,30 +433,30 @@
             out_ref[b] = sums[:out_ref.shape[1], :]
 
 
-def score_parts(grads, ranks, grad_basis, image, seq_count):
-    batch_count, _, tokens = image.shape
-    count, rows, width = grads.shape
-    hidden = width - LANES
+def score_parts(grad_pieces, ranks, grad_basis, image, seq_count):
+    batch_count, hidden, tokens = image.shape
+    count = len(grad_pieces)
+    rows = grad_pieces[0].shape[0]
     inner = min(grad_basis.shape[0], hidden)
     return pl.pallas_call(
-        functools.partial(score_kernel, batch_count, ranks),
+        functools.partial(score_kernel, batch_count, ranks, count),
         grid=(hidden // inner,),
-        in_specs=[
-            pl.BlockSpec((count, rows, inner), lambda i: (0, 0, i)),
+        in_specs=[pl.BlockSpec((rows, inner), lambda i: (0, i))] * count
+        + [pl.BlockSpec((rows, LANES), lambda i: (0, hidden // LANES))] * count
+        + [
             pl.BlockSpec((grad_basis.shape[0], inner), lambda i: (0, i)),
             pl.BlockSpec((batch_count, inner, tokens), lambda i: (0, i, 0)),
-            pl.BlockSpec((count, rows, LANES), lambda i: (0, 0, hidden // LANES)),
         ],
         out_specs=pl.BlockSpec((batch_count, seq_count, 1), lambda i: (0, 0, 0)),
         out_shape=jax.ShapeDtypeStruct((batch_count, seq_count, 1), jnp.float32),
         scratch_shapes=[pltpu.VMEM((8, tokens), jnp.float32)],
-        compiler_params=params(56),
+        compiler_params=params(44),
         cost_estimate=pl.CostEstimate(
             flops=2 * tokens * hidden * grad_basis.shape[0],
             bytes_accessed=4 * image.size,
             transcendentals=0,
         ),
-    )(grads, grad_basis, image, grads)
+    )(*grad_pieces, *grad_pieces, grad_basis, image)
 
 
 def per_device(
@@ -420,27 +483,30 @@
     keep, give = cut_factors(query_factors, order, hidden, batch_count)
     flags = owner_flags(owners, ways, keep)
     count = wide_count // 2
+    after = []
     for step, bit in enumerate(ways):
         got = swap(give, "wide", bit)
+        keep, give = pick(flags, keep, got, step, cols, count, after)
+        count //= 2
+        if step == 0:
+            grads_sent = grads_core(seq_ids, train_grad, give)
+            grads_got = swap(grads_sent, "wide", 1)
         if step < len(far) - 1:
-            acts = join(acts, swap(acts, "wide", far[step]))
+            acts = join(acts, swap(acts, "wide", far[step]), give)
             ranks = ranks + [r + far[step] for r in ranks]
-            after = [acts]
+            after = [acts, grads_sent]
         elif step == len(far) - 1:
             last = swap(acts, "wide", far[step])
-            sent = cut_grads(seq_ids, train_grad, give, wide_count)
-            after = [last, sent]
+            near = [(gate(acts, [give]), ranks)]
+            over = [(swap(near[0][0], "wide", 2), [r + 2 for r in ranks])]
+            grads_over = grads_y(train_grad, grads_sent, grads_got, give)
+            after = [over[0][0], grads_over]
         elif step == len(far):
-            after = [over[0][0], first]
-        else:
-            after = []
-        keep, give = pick(flags, keep, got, step, cols, count, after)
-        count //= 2
-        if step == len(far) - 1:
-            near = [(gate(acts, [give]), ranks), (gate(last, [give]), [r + far[step] for r in ranks])]
-            over = [(swap(x, "wide", 2), [r + 2 for r in has]) for x, has in near]
+            near += [(gate(last, [give]), [r + far[-1] for r in ranks])]
+            over += [(swap(near[1][0], "wide", 2), [r + 2 for r in near[1][1]])]
             near += [(swap(x, "wide", 1), [r + 1 for r in has]) for x, has in near]
             first, basis = rotate([x for x, _ in near], act_basis, give)
+            after = [first]
     left, right = keep, give
 
     lefts = [left, swap(left, "groups", 1)]
@@ -453,7 +519,9 @@
     rot = rotate_rest([x for x, _ in over], basis, first)
     ranks = [r for _, has in near + over for r in has]
 
-    grads = lax.all_to_all(gate(sent, [rot, lefts[1], halves[1], halves[3]]), "wide", 0, 0)
+    grads_over = swap(grads_over, "wide", 2)
+    sent = grads_z(train_grad, grads_sent, grads_got, grads_over, wide_count)
+    grads = [sent[0]] + [swap(sent[k], "wide", 4 * k) for k in range(1, wide_count // 4)]
 
     image = images(rot, lefts, halves, eigenvalues)
     parts = score_parts(grads, ranks, grad_basis, image, seq_count)

time: 103 us -> 98.7 us (0.958)
  local copies, waits for them, and re-layouts: 1.95 us -> 9.08 us
  waiting for transfers between devices: 32.7 us -> 27.4 us
  starting transfers between devices: 30.4 us -> 27.5 us
  Pallas kernels: 35.9 us -> 33.6 us
    unnamed x10 -> x20, local copies, waits for them, and re-layouts: 1.95 us -> 9.08 us
    all_to_all x1 -> x0, starting transfers between devices: 5.9 us -> none  [per_device(): lax.all_to_all(gate(sent, [rot, lefts[1], halves[1], halves[3]]), 'wide',...]
    ppermute x22 -> x27, waiting for transfers between devices: 31.8 us -> 27.4 us  [swap(): return lax.ppermute(x, axis, [(i, i ^ bit) for i in range(count)])]
    pallas_call x3 -> x5, Pallas kernels: 6.91 us -> 3.69 us  [the longest x1 2.97 us: score_parts(): pl.pallas_call(functools.partial(score_kernel, batch_count, ranks, count)...]
    ppermute x22 -> x27, starting transfers between devices: 24.5 us -> 27.5 us  [swap(): return lax.ppermute(x, axis, [(i, i ^ bit) for i in range(count)])]
  transfers between devices with their start and end apart: 23 -> 27, of which waited for: 12 -> 12; matrix products, arithmetic and copies ran while one was open for 0% -> 0% of each run, Pallas kernels for 29% -> 31%
where the time goes in v10:
time: 98.7 us; the launch traced here: 98.5 us
  Pallas kernels  33.6 us (34%)
  starting transfers between devices  27.5 us (28%)
  waiting for transfers between devices  27.4 us (28%)
  local copies, waits for them, and re-layouts  9.08 us (9%)
    ppermute x27, starting transfers between devices, swap(): return lax.ppermute(x, axis, [(i, i ^ bit) for i in range(count)])  27.5 us
    ppermute x27, waiting for transfers between devices, swap(): return lax.ppermute(x, axis, [(i, i ^ bit) for i in range(count)])  27.4 us
    pallas_call x1, Pallas kernels, images(): pl.pallas_call(functools.partial(image_kernel, batch_count, total, per),...  22.4 us
    unnamed x20, local copies, waits for them, and re-layouts  9.08 us
    pallas_call x1, Pallas kernels, rotate(): pl.pallas_call(functools.partial(rotate_kernel, len(act_pieces)), in_spec...  3.63 us
    pallas_call x1, Pallas kernels, score_parts(): pl.pallas_call(functools.partial(score_kernel, batch_count, ranks, count)...  2.97 us
    pallas_call x1, Pallas kernels, rotate_rest(): pl.pallas_call(functools.partial(rotate_rest_kernel, len(act_pieces)), in...  2.09 us
  transfers between devices with their start and end apart: 27, of which 12 were waited for; matrix products, arithmetic and copies ran while one was open for 0% of the time, Pallas kernels for 31%

profile of v10, /device:TPU:0, one launch (start us, length us, event | category | flops | bytes accessed | tf_op | source)
XLA Modules:
  0.0 98.5 jit_solution(2016918774452607425)
XLA Ops:
  0.0 1.8 %copy-done.3 = bf16[2,16,36864]{2,1,0:T(8,128)(2,1)S(1)} copy-done((bf16[2,16,36864]{2,1,0:T(8,128)(2,1)S(1)}, bf16[2,16,36864]{2,1,0:T(8,128)(2,1)}, u32[]{:S(2)}) %copy-start.3) | copy-done | bytes 2359320
  2.4 3.7 %collective-permute-start.3 = (bf16[16,4096]{1,0:T(8,128)(2,1)}, bf16[16,4096]{1,0:T(8,128)(2,1)S(1)}, u32[]{:S(2)}, u32[]{:S(2)}) collective-permute-start(bf16[16,4096]{1,0:T(8,128)(2,1)} %first_ref.1), channel_id=1, source_target_pairs={{0,8},{1,9},{2,10},{3,11},{4,12},{5,13},{6,14},{7,15},{8,0},{9,1},... | collective-permute-start | bytes 393224 | tf_op jit(solution)/shard_map/ppermute | solution.py:31
  7.4 1.6 %collective-permute-start.2 = (bf16[16,10240]{1,0:T(8,128)(2,1)S(1)}, bf16[16,10240]{1,0:T(8,128)(2,1)S(1)}, u32[]{:S(2)}, u32[]{:S(2)}) collective-permute-start(bf16[16,10240]{1,0:T(8,128)(2,1)S(1)} %get-tuple-element.23._), channel_id=1, source_target_pairs={{0,2},{1,3},{2,0},{3,1},{4,6},{5,7},{6,4},{7,5},{8,10},{9,11},{10,... | collective-permute-start | bytes 983048 | tf_op jit(solution)/shard_map/ppermute | solution.py:31
  10.4 2.8 %collective-permute-done.3.second_ref = bf16[16,4096]{1,0:T(8,128)(2,1)S(1)} collective-permute-done((bf16[16,4096]{1,0:T(8,128)(2,1)}, bf16[16,4096]{1,0:T(8,128)(2,1)S(1)}, u32[]{:S(2)}, u32[]{:S(2)}) %collective-permute-start.3) | collective-permute-done | bytes 131104 | tf_op jit(solution)/shard_map/ppermute | solution.py:31
  14.1 3.2 %collective-permute-done.2.got_ref = bf16[16,10240]{1,0:T(8,128)(2,1)S(1)} collective-permute-done((bf16[16,10240]{1,0:T(8,128)(2,1)S(1)}, bf16[16,10240]{1,0:T(8,128)(2,1)S(1)}, u32[]{:S(2)}, u32[]{:S(2)}) %collective-permute-start.2) | collective-permute-done | bytes 327712 | tf_op jit(solution)/shard_map/ppermute | solution.py:31
  17.4 3.9 %collective-permute-done.11.__0_ = bf16[32,4096]{1,0:T(8,128)(2,1)S(1)} collective-permute-done((bf16[32,4096]{1,0:T(8,128)(2,1)S(1)}, bf16[32,4096]{1,0:T(8,128)(2,1)S(1)}, u32[]{:S(2)}, u32[]{:S(2)}) %collective-permute-start.11) | collective-permute-done | bytes 262176 | tf_op jit(solution)/shard_map/ppermute | solution.py:31
  21.3 1.4 %collective-permute-start.8 = (bf16[32,4096]{1,0:T(8,128)(2,1)S(1)}, bf16[32,4096]{1,0:T(8,128)(2,1)S(1)}, u32[]{:S(2)}, u32[]{:S(2)}) collective-permute-start(bf16[32,4096]{1,0:T(8,128)(2,1)S(1)} %shard_map.90.refs_0_), channel_id=1, source_target_pairs={{0,2},{1,3},{2,0},{3,1},{4,6},{5,7},{6,4},{7,5},{8,10},{9,11},{10,... | collective-permute-start | bytes 786440 | tf_op jit(solution)/shard_map/ppermute | solution.py:31
  22.7 2.7 %collective-permute-start.9 = (bf16[16,6144]{1,0:T(8,128)(2,1)S(1)}, bf16[16,6144]{1,0:T(8,128)(2,1)S(1)}, u32[]{:S(2)}, u32[]{:S(2)}) collective-permute-start(bf16[16,6144]{1,0:T(8,128)(2,1)S(1)} %get-tuple-element.25._.__1_), channel_id=1, source_target_pairs={{0,8},{1,9},{2,10},{3,11},{4,12},{5,13},{6,14},{7,15},{8,0},{9,1},... | collective-permute-start | bytes 589832 | tf_op jit(solution)/shard_map/ppermute | solution.py:31
  26.0 7.9 %collective-permute-done.9.got_ref = bf16[16,6144]{1,0:T(8,128)(2,1)S(1)} collective-permute-done((bf16[16,6144]{1,0:T(8,128)(2,1)S(1)}, bf16[16,6144]{1,0:T(8,128)(2,1)S(1)}, u32[]{:S(2)}, u32[]{:S(2)}) %collective-permute-start.9) | collective-permute-done | bytes 196640 | tf_op jit(solution)/shard_map/ppermute | solution.py:31
  35.7 3.6 %shard_map.93 = (bf16[4096,128]{1,0:T(8,128)(2,1)S(1)}, bf16[8,512,512]{2,1,0:T(8,128)(2,1)S(1)}) custom-call(bf16[32,4096]{1,0:T(8,128)(2,1)S(1)} %shard_map.90.refs_0_, bf16[32,4096]{1,0:T(8,128)(2,1)S(1)} %shard_map.92.refs_1_, bf16[32,4096]{1,0:T(8,128)(2,1)S(1)} %collective-permute-done.12.refs_2_, ...), custom_call_target="tpu_custom_call" | custom-call | bytes 1 | tf_op jit(solution)/shard_map/pallas_call | solution.py:267
  39.3 2.0 %copy-done.1 = bf16[8,512,512]{2,1,0:T(8,128)(2,1)} copy-done((bf16[8,512,512]{2,1,0:T(8,128)(2,1)}, bf16[8,512,512]{2,1,0:T(8,128)(2,1)S(1)}, u32[]{:S(2)}) %copy-start.1) | copy-done | bytes 4194328
  42.0 1.5 %collective-permute-start.15 = (bf16[16,2048]{1,0:T(8,128)(2,1)S(1)}, bf16[16,2048]{1,0:T(8,128)(2,1)S(1)}, u32[]{:S(2)}, u32[]{:S(2)}) collective-permute-start(bf16[16,2048]{1,0:T(8,128)(2,1)S(1)} %get-tuple-element.34.__1_.refs_2_), channel_id=1, source_target_pairs={{0,16},{16,0},{1,17},{17,1},{2,18},{18,2},{3,19},{19,3},{4,20},{20... | collective-permute-start | bytes 196616 | tf_op jit(solution)/shard_map/ppermute | solution.py:31
  43.5 2.1 %collective-permute-done.14.__0_ = bf16[32,4096]{1,0:T(8,128)(2,1)} collective-permute-done((bf16[32,4096]{1,0:T(8,128)(2,1)S(1)}, bf16[32,4096]{1,0:T(8,128)(2,1)}, u32[]{:S(2)}, u32[]{:S(2)}) %collective-permute-start.14) | collective-permute-done | bytes 262176 | tf_op jit(solution)/shard_map/ppermute | solution.py:31
  46.3 1.5 %collective-permute-start.18 = (bf16[16,2048]{1,0:T(8,128)(2,1)}, bf16[16,2048]{1,0:T(8,128)(2,1)}, u32[]{:S(2)}, u32[]{:S(2)}) collective-permute-start(bf16[16,2048]{1,0:T(8,128)(2,1)} %get-tuple-element.36.refs_0_), channel_id=1, source_target_pairs={{0,16},{16,0},{1,17},{17,1},{2,18},{18,2},{3,19},{19,3},{4,20},{20... | collective-permute-start | bytes 196616 | tf_op jit(solution)/shard_map/ppermute | solution.py:31
  50.2 1.2 %collective-permute-start.5 = (bf16[64,2176]{1,0:T(8,128)(2,1)S(1)}, bf16[64,2176]{1,0:T(8,128)(2,1)S(1)}, u32[]{:S(2)}, u32[]{:S(2)}) collective-permute-start(bf16[64,2176]{1,0:T(8,128)(2,1)S(1)} %get-tuple-element.27), channel_id=1, source_target_pairs={{0,4},{1,5},{2,6},{3,7},{4,0},{5,1},{6,2},{7,3},{8,12},{9,13},{10,... | collective-permute-start | bytes 835592 | tf_op jit(solution)/shard_map/ppermute | solution.py:31
  51.3 3.0 %collective-permute-start.6 = (bf16[64,2176]{1,0:T(8,128)(2,1)S(1)}, bf16[64,2176]{1,0:T(8,128)(2,1)S(1)}, u32[]{:S(2)}, u32[]{:S(2)}) collective-permute-start(bf16[64,2176]{1,0:T(8,128)(2,1)S(1)} %get-tuple-element.28), channel_id=1, source_target_pairs={{0,8},{1,9},{2,10},{3,11},{4,12},{5,13},{6,14},{7,15},{8,0},{9,1},... | collective-permute-start | bytes 835592 | tf_op jit(solution)/shard_map/ppermute | solution.py:31
  54.3 2.2 %copy-done.2 = bf16[8,512,512]{2,1,0:T(8,128)(2,1)S(1)} copy-done((bf16[8,512,512]{2,1,0:T(8,128)(2,1)S(1)}, bf16[8,512,512]{2,1,0:T(8,128)(2,1)}, u32[]{:S(2)}) %copy-start.2) | copy-done | bytes 4194328
  56.5 2.1 %shard_map.97.rot_ref = bf16[4096,256]{1,0:T(8,128)(2,1)S(1)} custom-call(bf16[32,4096]{1,0:T(8,128)(2,1)S(1)} %shard_map.95.refs_0_, bf16[32,4096]{1,0:T(8,128)(2,1)} %shard_map.96.refs_1_, bf16[32,4096]{1,0:T(8,128)(2,1)} %collective-permute-done.16.refs_2_, bf16[32,4096]{1,0:T(8,128)(2,1)} %collective-permute-done.17.refs_3_, ...), custom_call_target="tpu_custom_call" | custom-call | bytes 1 | tf_op jit(solution)/shard_map/pallas_call | solution.py:296
  59.2 22.4 %shard_map.98.refs_9_ = f32[2,2048,256]{2,1,0:T(8,128)S(1)} custom-call(bf16[4096,256]{1,0:T(8,128)(2,1)S(1)} %shard_map.97.rot_ref, bf16[16,2048]{1,0:T(8,128)(2,1)} %get-tuple-element.36.refs_0_, bf16[16,2048]{1,0:T(8,128)(2,1)} %collective-permute-done.18.refs_1_, bf16[16,2048]{1,0:T(8,128)(2,1)S(1)} %get-tuple-element.34.__1_.refs_2_, ...), custom_call_target="tpu_custom_call" | custom-call | flops 17179869184 | bytes 16777216 | tf_op jit(solution)/shard_map/pallas_call | solution.py:382
  81.7 3.0 %shard_map.99 = f32[2,8,1]{2,1,0:T(8,128)S(1)} custom-call(bf16[64,2176]{1,0:T(8,128)(2,1)S(1)} %get-tuple-element.26.refs_0_.refs_4_, bf16[64,2176]{1,0:T(8,128)(2,1)S(1)} %collective-permute-done.5.refs_1_.refs_5_, bf16[64,2176]{1,0:T(8,128)(2,1)S(1)} %collective-permute-done.6.refs_2_.refs_6_, ...), custom_call_target="tpu_custom_call" | custom-call | flops 536870912 | bytes 4194304 | tf_op jit(solution)/shard_map/pallas_call | solution.py:441
  87.8 2.2 %collective-permute-done.22 = f32[2,8,1]{2,1,0:T(8,128)S(1)} collective-permute-done((f32[2,8,1]{2,1,0:T(8,128)S(1)}, f32[2,8,1]{2,1,0:T(8,128)S(1)}, u32[]{:S(2)}, u32[]{:S(2)}) %collective-permute-start.22) | collective-permute-done | bytes 96 | tf_op jit(solution)/shard_map/ppermute | solution.py:31
  90.0 3.2 %collective-permute-start.26 = (f32[2,8,1]{2,1,0:T(8,128)S(1)}, f32[2,8,1]{2,1,0:T(8,128)S(1)}, u32[]{:S(2)}, u32[]{:S(2)}) collective-permute-start(f32[2,8,1]{2,1,0:T(8,128)S(1)} %add_add_fusion.1), channel_id=1, source_target_pairs={{0,12},{1,13},{2,14},{3,15},{4,8},{5,9},{6,10},{7,11},{8,4},{9,5},... | collective-permute-start | bytes 200 | tf_op jit(solution)/shard_map/ppermute | solution.py:31
  93.2 1.2 %collective-permute-start.25 = (f32[2,8,1]{2,1,0:T(8,128)S(1)}, f32[2,8,1]{2,1,0:T(8,128)S(1)}, u32[]{:S(2)}, u32[]{:S(2)}) collective-permute-start(f32[2,8,1]{2,1,0:T(8,128)S(1)} %add_add_fusion.1), channel_id=1, source_target_pairs={{0,8},{1,9},{2,10},{3,11},{4,12},{5,13},{6,14},{7,15},{8,0},{9,1},... | collective-permute-start | bytes 200 | tf_op jit(solution)/shard_map/ppermute | solution.py:31
  95.5 1.4 %collective-permute-done.24 = f32[2,8,1]{2,1,0:T(8,128)S(1)} collective-permute-done((f32[2,8,1]{2,1,0:T(8,128)S(1)}, f32[2,8,1]{2,1,0:T(8,128)S(1)}, u32[]{:S(2)}, u32[]{:S(2)}) %collective-permute-start.24) | collective-permute-done | bytes 96 | tf_op jit(solution)/shard_map/ppermute | solution.py:31
  (72 shorter events, 16.9 us)
Async XLA Ops:
  1.8 5.4 %collective-permute-start = (bf16[16,18432]{1,0:T(8,128)(2,1)S(1)}, bf16[16,18432]{1,0:T(8,128)(2,1)S(1)}, u32[]{:S(2)}, u32[]{:S(2)}) collective-permute-start(bf16[16,18432]{1,0:T(8,128)(2,1)S(1)} %get-tuple-element.22), channel_id=1, source_target_pairs={{0,1},{1,0},{2,3},{3,2},{4,5},{5,4},{6,7},{7,6},{8,9},{9,8},{10,11... | collective-permute-start | bytes 1769480 | tf_op jit(solution)/shard_map/ppermute | solution.py:31
  2.4 10.8 %collective-permute-start.3 = (bf16[16,4096]{1,0:T(8,128)(2,1)}, bf16[16,4096]{1,0:T(8,128)(2,1)S(1)}, u32[]{:S(2)}, u32[]{:S(2)}) collective-permute-start(bf16[16,4096]{1,0:T(8,128)(2,1)} %first_ref.1), channel_id=1, source_target_pairs={{0,8},{1,9},{2,10},{3,11},{4,12},{5,13},{6,14},{7,15},{8,0},{9,1},... | collective-permute-start | bytes 393224 | tf_op jit(solution)/shard_map/ppermute | solution.py:31
  7.4 9.8 %collective-permute-start.2 = (bf16[16,10240]{1,0:T(8,128)(2,1)S(1)}, bf16[16,10240]{1,0:T(8,128)(2,1)S(1)}, u32[]{:S(2)}, u32[]{:S(2)}) collective-permute-start(bf16[16,10240]{1,0:T(8,128)(2,1)S(1)} %get-tuple-element.23._), channel_id=1, source_target_pairs={{0,2},{1,3},{2,0},{3,1},{4,6},{5,7},{6,4},{7,5},{8,10},{9,11},{10,... | collective-permute-start | bytes 983048 | tf_op jit(solution)/shard_map/ppermute | solution.py:31
  10.3 15.1 %collective-permute-start.1 = (bf16[16,16512]{1,0:T(8,128)(2,1)S(1)}, bf16[16,16512]{1,0:T(8,128)(2,1)S(1)}, u32[]{:S(2)}, u32[]{:S(2)}) collective-permute-start(bf16[16,16512]{1,0:T(8,128)(2,1)S(1)} %shard_map.85.refs_1_.sent_ref), channel_id=1, source_target_pairs={{0,1},{1,0},{2,3},{3,2},{4,5},{5,4},{6,7},{7,6},{8,9},{9,8},{10,11... | collective-permute-start | bytes 1585160 | tf_op jit(solution)/shard_map/ppermute | solution.py:31
  13.2 8.1 %collective-permute-start.11 = (bf16[32,4096]{1,0:T(8,128)(2,1)S(1)}, bf16[32,4096]{1,0:T(8,128)(2,1)S(1)}, u32[]{:S(2)}, u32[]{:S(2)}) collective-permute-start(bf16[32,4096]{1,0:T(8,128)(2,1)S(1)} %shard_map.86.refs_0_.__0_), channel_id=1, source_target_pairs={{0,4},{1,5},{2,6},{3,7},{4,0},{5,1},{6,2},{7,3},{8,12},{9,13},{10,... | collective-permute-start | bytes 786440 | tf_op jit(solution)/shard_map/ppermute | solution.py:31
  21.3 12.7 %collective-permute-start.8 = (bf16[32,4096]{1,0:T(8,128)(2,1)S(1)}, bf16[32,4096]{1,0:T(8,128)(2,1)S(1)}, u32[]{:S(2)}, u32[]{:S(2)}) collective-permute-start(bf16[32,4096]{1,0:T(8,128)(2,1)S(1)} %shard_map.90.refs_0_), channel_id=1, source_target_pairs={{0,2},{1,3},{2,0},{3,1},{4,6},{5,7},{6,4},{7,5},{8,10},{9,11},{10,... | collective-permute-start | bytes 786440 | tf_op jit(solution)/shard_map/ppermute | solution.py:31
  22.7 11.3 %collective-permute-start.9 = (bf16[16,6144]{1,0:T(8,128)(2,1)S(1)}, bf16[16,6144]{1,0:T(8,128)(2,1)S(1)}, u32[]{:S(2)}, u32[]{:S(2)}) collective-permute-start(bf16[16,6144]{1,0:T(8,128)(2,1)S(1)} %get-tuple-element.25._.__1_), channel_id=1, source_target_pairs={{0,8},{1,9},{2,10},{3,11},{4,12},{5,13},{6,14},{7,15},{8,0},{9,1},... | collective-permute-start | bytes 589832 | tf_op jit(solution)/shard_map/ppermute | solution.py:31
  25.4 22.5 %collective-permute-start.4 = (bf16[32,8320]{1,0:T(8,128)(2,1)S(1)}, bf16[32,8320]{1,0:T(8,128)(2,1)S(1)}, u32[]{:S(2)}, u32[]{:S(2)}) collective-permute-start(bf16[32,8320]{1,0:T(8,128)(2,1)S(1)} %shard_map.88.refs_1_), channel_id=1, source_target_pairs={{0,2},{1,3},{2,0},{3,1},{4,6},{5,7},{6,4},{7,5},{8,10},{9,11},{10,... | collective-permute-start | bytes 1597448 | tf_op jit(solution)/shard_map/ppermute | solution.py:31
  26.0 9.4 %collective-permute-start.12 = (bf16[32,4096]{1,0:T(8,128)(2,1)S(1)}, bf16[32,4096]{1,0:T(8,128)(2,1)S(1)}, u32[]{:S(2)}, u32[]{:S(2)}) collective-permute-start(bf16[32,4096]{1,0:T(8,128)(2,1)S(1)} %shard_map.90.refs_0_), channel_id=1, source_target_pairs={{0,1},{1,0},{2,3},{3,2},{4,5},{5,4},{6,7},{7,6},{8,9},{9,8},{10,11... | collective-permute-start | bytes 786440 | tf_op jit(solution)/shard_map/ppermute | solution.py:31
  34.1 11.5 %collective-permute-start.14 = (bf16[32,4096]{1,0:T(8,128)(2,1)S(1)}, bf16[32,4096]{1,0:T(8,128)(2,1)}, u32[]{:S(2)}, u32[]{:S(2)}) collective-permute-start(bf16[32,4096]{1,0:T(8,128)(2,1)S(1)} %shard_map.92.refs_1_), channel_id=1, source_target_pairs={{0,2},{1,3},{2,0},{3,1},{4,6},{5,7},{6,4},{7,5},{8,10},{9,11},{10,... | collective-permute-start | bytes 786440 | tf_op jit(solution)/shard_map/ppermute | solution.py:31
  34.7 6.6 %collective-permute-start.10 = (bf16[16,4096]{1,0:T(8,128)(2,1)S(1)}, bf16[16,4096]{1,0:T(8,128)(2,1)S(1)}, u32[]{:S(2)}, u32[]{:S(2)}) collective-permute-start(bf16[16,4096]{1,0:T(8,128)(2,1)S(1)} %get-tuple-element.32.__1_.refs_5_), channel_id=1, source_target_pairs={{0,4},{1,5},{2,6},{3,7},{4,0},{5,1},{6,2},{7,3},{8,12},{9,13},{10,... | collective-permute-start | bytes 393224 | tf_op jit(solution)/shard_map/ppermute | solution.py:31
  42.0 4.3 %collective-permute-start.15 = (bf16[16,2048]{1,0:T(8,128)(2,1)S(1)}, bf16[16,2048]{1,0:T(8,128)(2,1)S(1)}, u32[]{:S(2)}, u32[]{:S(2)}) collective-permute-start(bf16[16,2048]{1,0:T(8,128)(2,1)S(1)} %get-tuple-element.34.__1_.refs_2_), channel_id=1, source_target_pairs={{0,16},{16,0},{1,17},{17,1},{2,18},{18,2},{3,19},{19,3},{4,20},{20... | collective-permute-start | bytes 196616 | tf_op jit(solution)/shard_map/ppermute | solution.py:31
  43.5 6.7 %collective-permute-start.16 = (bf16[32,4096]{1,0:T(8,128)(2,1)S(1)}, bf16[32,4096]{1,0:T(8,128)(2,1)}, u32[]{:S(2)}, u32[]{:S(2)}) collective-permute-start(bf16[32,4096]{1,0:T(8,128)(2,1)S(1)} %shard_map.95.refs_0_), channel_id=1, source_target_pairs={{0,1},{1,0},{2,3},{3,2},{4,5},{5,4},{6,7},{7,6},{8,9},{9,8},{10,11... | collective-permute-start | bytes 786440 | tf_op jit(solution)/shard_map/ppermute | solution.py:31
  46.3 5.1 %collective-permute-start.17 = (bf16[32,4096]{1,0:T(8,128)(2,1)}, bf16[32,4096]{1,0:T(8,128)(2,1)}, u32[]{:S(2)}, u32[]{:S(2)}) collective-permute-start(bf16[32,4096]{1,0:T(8,128)(2,1)} %shard_map.96.refs_1_), channel_id=1, source_target_pairs={{0,1},{1,0},{2,3},{3,2},{4,5},{5,4},{6,7},{7,6},{8,9},{9,8},{10,11... | collective-permute-start | bytes 786440 | tf_op jit(solution)/shard_map/ppermute | solution.py:31
  46.3 12.4 %collective-permute-start.18 = (bf16[16,2048]{1,0:T(8,128)(2,1)}, bf16[16,2048]{1,0:T(8,128)(2,1)}, u32[]{:S(2)}, u32[]{:S(2)}) collective-permute-start(bf16[16,2048]{1,0:T(8,128)(2,1)} %get-tuple-element.36.refs_0_), channel_id=1, source_target_pairs={{0,16},{16,0},{1,17},{17,1},{2,18},{18,2},{3,19},{19,3},{4,20},{20... | collective-permute-start | bytes 196616 | tf_op jit(solution)/shard_map/ppermute | solution.py:31
  47.7 11.5 %collective-permute-start.19 = (bf16[16,2048]{1,0:T(8,128)(2,1)S(1)}, bf16[16,2048]{1,0:T(8,128)(2,1)}, u32[]{:S(2)}, u32[]{:S(2)}) collective-permute-start(bf16[16,2048]{1,0:T(8,128)(2,1)S(1)} %get-tuple-element.34.__1_.refs_2_), channel_id=1, source_target_pairs={{0,1},{1,0},{2,3},{3,2},{4,5},{5,4},{6,7},{7,6},{8,9},{9,8},{10,11... | collective-permute-start | bytes 196616 | tf_op jit(solution)/shard_map/ppermute | solution.py:31
  48.8 10.5 %collective-permute-start.20 = (bf16[16,2048]{1,0:T(8,128)(2,1)S(1)}, bf16[16,2048]{1,0:T(8,128)(2,1)}, u32[]{:S(2)}, u32[]{:S(2)}) collective-permute-start(bf16[16,2048]{1,0:T(8,128)(2,1)S(1)} %collective-permute-done.15.__1_.refs_4_), channel_id=1, source_target_pairs={{0,1},{1,0},{2,3},{3,2},{4,5},{5,4},{6,7},{7,6},{8,9},{9,8},{10,11... | collective-permute-start | bytes 196616 | tf_op jit(solution)/shard_map/ppermute | solution.py:31
  50.2 31.5 %collective-permute-start.5 = (bf16[64,2176]{1,0:T(8,128)(2,1)S(1)}, bf16[64,2176]{1,0:T(8,128)(2,1)S(1)}, u32[]{:S(2)}, u32[]{:S(2)}) collective-permute-start(bf16[64,2176]{1,0:T(8,128)(2,1)S(1)} %get-tuple-element.27), channel_id=1, source_target_pairs={{0,4},{1,5},{2,6},{3,7},{4,0},{5,1},{6,2},{7,3},{8,12},{9,13},{10,... | collective-permute-start | bytes 835592 | tf_op jit(solution)/shard_map/ppermute | solution.py:31
  51.3 30.3 %collective-permute-start.6 = (bf16[64,2176]{1,0:T(8,128)(2,1)S(1)}, bf16[64,2176]{1,0:T(8,128)(2,1)S(1)}, u32[]{:S(2)}, u32[]{:S(2)}) collective-permute-start(bf16[64,2176]{1,0:T(8,128)(2,1)S(1)} %get-tuple-element.28), channel_id=1, source_target_pairs={{0,8},{1,9},{2,10},{3,11},{4,12},{5,13},{6,14},{7,15},{8,0},{9,1},... | collective-permute-start | bytes 835592 | tf_op jit(solution)/shard_map/ppermute | solution.py:31
  58.6 23.0 %collective-permute-start.7 = (bf16[64,2176]{1,0:T(8,128)(2,1)S(1)}, bf16[64,2176]{1,0:T(8,128)(2,1)S(1)}, u32[]{:S(2)}, u32[]{:S(2)}) collective-permute-start(bf16[64,2176]{1,0:T(8,128)(2,1)S(1)} %get-tuple-element.29), channel_id=1, source_target_pairs={{0,12},{1,13},{2,14},{3,15},{4,8},{5,9},{6,10},{7,11},{8,4},{9,5},... | collective-permute-start | bytes 835592 | tf_op jit(solution)/shard_map/ppermute | solution.py:31
  86.3 3.7 %collective-permute-start.22 = (f32[2,8,1]{2,1,0:T(8,128)S(1)}, f32[2,8,1]{2,1,0:T(8,128)S(1)}, u32[]{:S(2)}, u32[]{:S(2)}) collective-permute-start(f32[2,8,1]{2,1,0:T(8,128)S(1)} %shard_map.99), channel_id=1, source_target_pairs={{0,2},{1,3},{2,0},{3,1},{4,6},{5,7},{6,4},{7,5},{8,10},{9,11},{10,... | collective-permute-start | bytes 200 | tf_op jit(solution)/shard_map/ppermute | solution.py:31
  90.0 5.5 %collective-permute-start.26 = (f32[2,8,1]{2,1,0:T(8,128)S(1)}, f32[2,8,1]{2,1,0:T(8,128)S(1)}, u32[]{:S(2)}, u32[]{:S(2)}) collective-permute-start(f32[2,8,1]{2,1,0:T(8,128)S(1)} %add_add_fusion.1), channel_id=1, source_target_pairs={{0,12},{1,13},{2,14},{3,15},{4,8},{5,9},{6,10},{7,11},{8,4},{9,5},... | collective-permute-start | bytes 200 | tf_op jit(solution)/shard_map/ppermute | solution.py:31
  93.2 3.7 %collective-permute-start.24 = (f32[2,8,1]{2,1,0:T(8,128)S(1)}, f32[2,8,1]{2,1,0:T(8,128)S(1)}, u32[]{:S(2)}, u32[]{:S(2)}) collective-permute-start(f32[2,8,1]{2,1,0:T(8,128)S(1)} %add_add_fusion.1), channel_id=1, source_target_pairs={{0,4},{1,5},{2,6},{3,7},{4,0},{5,1},{6,2},{7,3},{8,12},{9,13},{10,... | collective-permute-start | bytes 200 | tf_op jit(solution)/shard_map/ppermute | solution.py:31
  93.2 4.5 %collective-permute-start.25 = (f32[2,8,1]{2,1,0:T(8,128)S(1)}, f32[2,8,1]{2,1,0:T(8,128)S(1)}, u32[]{:S(2)}, u32[]{:S(2)}) collective-permute-start(f32[2,8,1]{2,1,0:T(8,128)S(1)} %add_add_fusion.1), channel_id=1, source_target_pairs={{0,8},{1,9},{2,10},{3,11},{4,12},{5,13},{6,14},{7,15},{8,0},{9,1},... | collective-permute-start | bytes 200 | tf_op jit(solution)/shard_map/ppermute | solution.py:31
  (13 other events, 59.5 us)

commit v11 on v10

--- a/solution.py
+++ b/solution.py
@@ -243,64 +243,31 @@
     )(grads, sent, got, over)
 
 
-def rotate_kernel(act_count, *refs):
-    act_refs, (basis_ref, _, out_ref, held_ref, sems) = refs[:act_count], refs[act_count:]
+def rotate_kernel(act_count, done, *refs):
+    act_refs, basis_ref, out_ref = refs[:act_count], refs[act_count], refs[-1]
     depth, width = basis_ref.shape
-    places = [slice(k * depth, (k + 1) * depth) for k in range(width // depth)]
-    copies = [
-        pltpu.make_async_copy(basis_ref.at[:, cols], held_ref.at[k], sems.at[k])
-        for k, cols in enumerate(places)
-    ]
-    for copy in copies:
-        copy.start()
-    for k, cols in enumerate(places):
-        act = jnp.concatenate([ref[:, cols] for ref in act_refs], axis=0)
-        copies[k].wait()
-        turned = jnp.dot(act, held_ref[k], preferred_element_type=jnp.float32)
-        out_ref[cols, :] = turned.astype(jnp.bfloat16).T
-
-
-def rotate(act_pieces, basis, after):
-    tokens = sum(x.shape[0] for x in act_pieces)
-    depth, width = basis.shape
-    count = width // depth
-    return pl.pallas_call(
-        functools.partial(rotate_kernel, len(act_pieces)),
-        in_specs=in_vmem(len(act_pieces)) + in_place(2),
-        out_specs=in_vmem(2),
-        out_shape=[
-            jax.ShapeDtypeStruct((width, tokens), jnp.bfloat16),
-            jax.ShapeDtypeStruct((count, depth, depth), jnp.bfloat16),
-        ],
-        scratch_shapes=[pltpu.SemaphoreType.DMA((count,))],
-        compiler_params=params(46 if tokens <= 256 else 32),
-        cost_estimate=pl.CostEstimate(flops=0, bytes_accessed=1, transcendentals=0),
-    )(*act_pieces, basis, after)
-
-
-def rotate_rest_kernel(act_count, *refs):
-    act_refs, (held_ref, first_ref, out_ref) = refs[:act_count], refs[act_count:]
-    depth = held_ref.shape[1]
-    done = first_ref.shape[1]
-    out_ref[:, :done] = first_ref[...]
-    for k in range(held_ref.shape[0]):
+    if done:
+        out_ref[:, :done] = refs[act_count + 1][...]
+    for k in range(width // depth):
         cols = slice(k * depth, (k + 1) * depth)
         act = jnp.concatenate([ref[:, cols] for ref in act_refs], axis=0)
-        turned = jnp.dot(act, held_ref[k], preferred_element_type=jnp.float32)
+        turned = jnp.dot(act, basis_ref[:, cols], preferred_element_type=jnp.float32)
         out_ref[cols, done:] = turned.astype(jnp.bfloat16).T
 
 
-def rotate_rest(act_pieces, held, first):
-    width, done = first.shape
+def rotate(act_pieces, basis, after, first=None):
+    width = basis.shape[1]
+    done = 0 if first is None else first.shape[1]
     tokens = done + sum(x.shape[0] for x in act_pieces)
-    return pl.pallas_call(
-        functools.partial(rotate_rest_kernel, len(act_pieces)),
-        in_specs=in_vmem(len(act_pieces) + 2),
+    more = [after] if first is None else [first]
+    return pl.pallas_call(
+        functools.partial(rotate_kernel, len(act_pieces), done),
+        in_specs=in_vmem(len(act_pieces) + 1) + (in_place(1) if first is None else in_vmem(1)),
         out_specs=in_vmem(1)[0],
         out_shape=jax.ShapeDtypeStruct((width, tokens), jnp.bfloat16),
         compiler_params=params(16 if tokens <= 256 else 32),
         cost_estimate=pl.CostEstimate(flops=0, bytes_accessed=1, transcendentals=0),
-    )(*act_pieces, held, first)
+    )(*act_pieces, basis, *more)
 
 
 def image_kernel(batch_count, total, per, rot_ref, *refs):
@@ -394,7 +361,7 @@
             pltpu.VMEM((batch_count * rows, chunk), jnp.bfloat16),
             pltpu.VMEM((batch_count * rows, chunk), jnp.bfloat16),
         ],
-        compiler_params=params(44),
+        compiler_params=params(32 if tokens <= 256 else 48),
         cost_estimate=pl.CostEstimate(
             flops=2 * hidden * width * (tokens + 256) * batch_count,
             bytes_accessed=2 * hidden * width,
@@ -450,7 +417,7 @@
         out_specs=pl.BlockSpec((batch_count, seq_count, 1), lambda i: (0, 0, 0)),
         out_shape=jax.ShapeDtypeStruct((batch_count, seq_count, 1), jnp.float32),
         scratch_shapes=[pltpu.VMEM((8, tokens), jnp.float32)],
-        compiler_params=params(44),
+        compiler_params=params(32 if tokens <= 256 else 48),
         cost_estimate=pl.CostEstimate(
             flops=2 * tokens * hidden * grad_basis.shape[0],
             bytes_accessed=4 * image.size,
@@ -505,7 +472,7 @@
             near += [(gate(last, [give]), [r + far[-1] for r in ranks])]
             over += [(swap(near[1][0], "wide", 2), [r + 2 for r in near[1][1]])]
             near += [(swap(x, "wide", 1), [r + 1 for r in has]) for x, has in near]
-            first, basis = rotate([x for x, _ in near], act_basis, give)
+            first = rotate([x for x, _ in near], act_basis, give)
             after = [first]
     left, right = keep, give
 
@@ -516,7 +483,7 @@
         halves += [x, swap(x, "wide", 1)]
     over = [(gate(x, [wait]), has) for (x, has), wait in zip(over, (right, other))]
     over += [(swap(x, "wide", 1), [r + 1 for r in has]) for x, has in over]
-    rot = rotate_rest([x for x, _ in over], basis, first)
+    rot = rotate([x for x, _ in over], act_basis, None, first)
     ranks = [r for _, has in near + over for r in has]
 
     grads_over = swap(grads_over, "wide", 2)

time: 98.7 us -> 98.7 us (level)
  waiting for transfers between devices: 27.4 us -> 31.9 us
  Pallas kernels: 33.6 us -> 30.9 us
  local copies, waits for them, and re-layouts: 9.08 us -> 7.12 us
    ppermute x27, waiting for transfers between devices: 27.4 us -> 31.9 us  [swap(): return lax.ppermute(x, axis, [(i, i ^ bit) for i in range(count)])]
    pallas_call x2, Pallas kernels: 5.72 us -> 2.92 us  [rotate(): pl.pallas_call(functools.partial(rotate_kernel, len(act_pieces), done), i...]
    unnamed x20, local copies, waits for them, and re-layouts: 9.08 us -> 7.12 us
  transfers between devices with their start and end apart: 27 -> 27, of which waited for: 12 -> 12; matrix products, arithmetic and copies ran while one was open for 0% -> 0% of each run, Pallas kernels for 31% -> 28%
where the time goes in v11:
time: 98.7 us; the launch traced here: 98.5 us
  waiting for transfers between devices  31.9 us (32%)
  Pallas kernels  30.9 us (31%)
  starting transfers between devices  27.6 us (28%)
  local copies, waits for them, and re-layouts  7.12 us (7%)
    ppermute x27, waiting for transfers between devices, swap(): return lax.ppermute(x, axis, [(i, i ^ bit) for i in range(count)])  31.9 us
    ppermute x27, starting transfers between devices, swap(): return lax.ppermute(x, axis, [(i, i ^ bit) for i in range(count)])  27.6 us
    pallas_call x1, Pallas kernels, images(): pl.pallas_call(functools.partial(image_kernel, batch_count, total, per),...  22.6 us
    unnamed x20, local copies, waits for them, and re-layouts  7.12 us
    pallas_call x1, Pallas kernels, score_parts(): pl.pallas_call(functools.partial(score_kernel, batch_count, ranks, count)...  2.97 us
    pallas_call x2, Pallas kernels, rotate(): pl.pallas_call(functools.partial(rotate_kernel, len(act_pieces), done), i...  2.92 us
  transfers between devices with their start and end apart: 27, of which 12 were waited for; matrix products, arithmetic and copies ran while one was open for 0% of the time, Pallas kernels for 28%

profile of v11, /device:TPU:0, one launch (start us, length us, event | category | flops | bytes accessed | tf_op | source)
XLA Modules:
  0.0 98.5 jit_solution(4178175656433611234)
XLA Ops:
  0.0 1.8 %copy-done.3 = bf16[2,16,36864]{2,1,0:T(8,128)(2,1)S(1)} copy-done((bf16[2,16,36864]{2,1,0:T(8,128)(2,1)S(1)}, bf16[2,16,36864]{2,1,0:T(8,128)(2,1)}, u32[]{:S(2)}) %copy-start.3) | copy-done | bytes 2359320
  2.4 3.7 %collective-permute-start.3 = (bf16[16,4096]{1,0:T(8,128)(2,1)}, bf16[16,4096]{1,0:T(8,128)(2,1)S(1)}, u32[]{:S(2)}, u32[]{:S(2)}) collective-permute-start(bf16[16,4096]{1,0:T(8,128)(2,1)} %first_ref.1), channel_id=1, source_target_pairs={{0,8},{1,9},{2,10},{3,11},{4,12},{5,13},{6,14},{7,15},{8,0},{9,1},... | collective-permute-start | bytes 393224 | tf_op jit(solution)/shard_map/ppermute | solution.py:31
  7.4 1.6 %collective-permute-start.2 = (bf16[16,10240]{1,0:T(8,128)(2,1)S(1)}, bf16[16,10240]{1,0:T(8,128)(2,1)S(1)}, u32[]{:S(2)}, u32[]{:S(2)}) collective-permute-start(bf16[16,10240]{1,0:T(8,128)(2,1)S(1)} %get-tuple-element.21._), channel_id=1, source_target_pairs={{0,2},{1,3},{2,0},{3,1},{4,6},{5,7},{6,4},{7,5},{8,10},{9,11},{10,... | collective-permute-start | bytes 983048 | tf_op jit(solution)/shard_map/ppermute | solution.py:31
  10.4 2.8 %collective-permute-done.3.second_ref = bf16[16,4096]{1,0:T(8,128)(2,1)S(1)} collective-permute-done((bf16[16,4096]{1,0:T(8,128)(2,1)}, bf16[16,4096]{1,0:T(8,128)(2,1)S(1)}, u32[]{:S(2)}, u32[]{:S(2)}) %collective-permute-start.3) | collective-permute-done | bytes 131104 | tf_op jit(solution)/shard_map/ppermute | solution.py:31
  14.1 3.2 %collective-permute-done.2.got_ref = bf16[16,10240]{1,0:T(8,128)(2,1)S(1)} collective-permute-done((bf16[16,10240]{1,0:T(8,128)(2,1)S(1)}, bf16[16,10240]{1,0:T(8,128)(2,1)S(1)}, u32[]{:S(2)}, u32[]{:S(2)}) %collective-permute-start.2) | collective-permute-done | bytes 327712 | tf_op jit(solution)/shard_map/ppermute | solution.py:31
  17.4 3.9 %collective-permute-done.11.__0_ = bf16[32,4096]{1,0:T(8,128)(2,1)S(1)} collective-permute-done((bf16[32,4096]{1,0:T(8,128)(2,1)S(1)}, bf16[32,4096]{1,0:T(8,128)(2,1)S(1)}, u32[]{:S(2)}, u32[]{:S(2)}) %collective-permute-start.11) | collective-permute-done | bytes 262176 | tf_op jit(solution)/shard_map/ppermute | solution.py:31
  21.3 1.4 %collective-permute-start.8 = (bf16[32,4096]{1,0:T(8,128)(2,1)S(1)}, bf16[32,4096]{1,0:T(8,128)(2,1)S(1)}, u32[]{:S(2)}, u32[]{:S(2)}) collective-permute-start(bf16[32,4096]{1,0:T(8,128)(2,1)S(1)} %shard_map.90.refs_0_), channel_id=1, source_target_pairs={{0,2},{1,3},{2,0},{3,1},{4,6},{5,7},{6,4},{7,5},{8,10},{9,11},{10,... | collective-permute-start | bytes 786440 | tf_op jit(solution)/shard_map/ppermute | solution.py:31
  22.7 2.7 %collective-permute-start.9 = (bf16[16,6144]{1,0:T(8,128)(2,1)S(1)}, bf16[16,6144]{1,0:T(8,128)(2,1)S(1)}, u32[]{:S(2)}, u32[]{:S(2)}) collective-permute-start(bf16[16,6144]{1,0:T(8,128)(2,1)S(1)} %get-tuple-element.23._.__1_), channel_id=1, source_target_pairs={{0,8},{1,9},{2,10},{3,11},{4,12},{5,13},{6,14},{7,15},{8,0},{9,1},... | collective-permute-start | bytes 589832 | tf_op jit(solution)/shard_map/ppermute | solution.py:31
  26.0 7.9 %collective-permute-done.9.got_ref = bf16[16,6144]{1,0:T(8,128)(2,1)S(1)} collective-permute-done((bf16[16,6144]{1,0:T(8,128)(2,1)S(1)}, bf16[16,6144]{1,0:T(8,128)(2,1)S(1)}, u32[]{:S(2)}, u32[]{:S(2)}) %collective-permute-start.9) | collective-permute-done | bytes 196640 | tf_op jit(solution)/shard_map/ppermute | solution.py:31
  36.5 3.8 %collective-permute-done.10.got_ref = bf16[16,4096]{1,0:T(8,128)(2,1)S(1)} collective-permute-done((bf16[16,4096]{1,0:T(8,128)(2,1)S(1)}, bf16[16,4096]{1,0:T(8,128)(2,1)S(1)}, u32[]{:S(2)}, u32[]{:S(2)}) %collective-permute-start.10) | collective-permute-done | bytes 131104 | tf_op jit(solution)/shard_map/ppermute | solution.py:31
  41.0 1.5 %collective-permute-start.15 = (bf16[16,2048]{1,0:T(8,128)(2,1)S(1)}, bf16[16,2048]{1,0:T(8,128)(2,1)S(1)}, u32[]{:S(2)}, u32[]{:S(2)}) collective-permute-start(bf16[16,2048]{1,0:T(8,128)(2,1)S(1)} %get-tuple-element.31.__1_.refs_2_), channel_id=1, source_target_pairs={{0,16},{16,0},{1,17},{17,1},{2,18},{18,2},{3,19},{19,3},{4,20},{20... | collective-permute-start | bytes 196616 | tf_op jit(solution)/shard_map/ppermute | solution.py:31
  42.5 3.1 %collective-permute-done.14.__0_ = bf16[32,4096]{1,0:T(8,128)(2,1)} collective-permute-done((bf16[32,4096]{1,0:T(8,128)(2,1)S(1)}, bf16[32,4096]{1,0:T(8,128)(2,1)}, u32[]{:S(2)}, u32[]{:S(2)}) %collective-permute-start.14) | collective-permute-done | bytes 262176 | tf_op jit(solution)/shard_map/ppermute | solution.py:31
  45.6 1.2 %collective-permute-start.18 = (bf16[16,2048]{1,0:T(8,128)(2,1)}, bf16[16,2048]{1,0:T(8,128)(2,1)}, u32[]{:S(2)}, u32[]{:S(2)}) collective-permute-start(bf16[16,2048]{1,0:T(8,128)(2,1)} %get-tuple-element.32.refs_0_), channel_id=1, source_target_pairs={{0,16},{16,0},{1,17},{17,1},{2,18},{18,2},{3,19},{19,3},{4,20},{20... | collective-permute-start | bytes 196616 | tf_op jit(solution)/shard_map/ppermute | solution.py:31
  48.2 1.0 %copy-done.6 = bf16[32,8320]{1,0:T(8,128)(2,1)S(1)} copy-done((bf16[32,8320]{1,0:T(8,128)(2,1)S(1)}, bf16[32,8320]{1,0:T(8,128)(2,1)}, u32[]{:S(2)}) %copy-start.6) | copy-done | bytes 532504
  49.3 1.7 %collective-permute-start.5 = (bf16[64,2176]{1,0:T(8,128)(2,1)S(1)}, bf16[64,2176]{1,0:T(8,128)(2,1)S(1)}, u32[]{:S(2)}, u32[]{:S(2)}) collective-permute-start(bf16[64,2176]{1,0:T(8,128)(2,1)S(1)} %get-tuple-element.25), channel_id=1, source_target_pairs={{0,4},{1,5},{2,6},{3,7},{4,0},{5,1},{6,2},{7,3},{8,12},{9,13},{10,... | collective-permute-start | bytes 835592 | tf_op jit(solution)/shard_map/ppermute | solution.py:31
  51.0 3.3 %collective-permute-start.6 = (bf16[64,2176]{1,0:T(8,128)(2,1)S(1)}, bf16[64,2176]{1,0:T(8,128)(2,1)S(1)}, u32[]{:S(2)}, u32[]{:S(2)}) collective-permute-start(bf16[64,2176]{1,0:T(8,128)(2,1)S(1)} %get-tuple-element.26), channel_id=1, source_target_pairs={{0,8},{1,9},{2,10},{3,11},{4,12},{5,13},{6,14},{7,15},{8,0},{9,1},... | collective-permute-start | bytes 835592 | tf_op jit(solution)/shard_map/ppermute | solution.py:31
  54.3 2.2 %copy-done.1 = bf16[512,4096]{1,0:T(8,128)(2,1)S(1)} copy-done((bf16[512,4096]{1,0:T(8,128)(2,1)S(1)}, bf16[512,4096]{1,0:T(8,128)(2,1)}, u32[]{:S(2)}) %copy-start.1) | copy-done | bytes 4194328
  56.5 2.1 %shard_map.97.rot_ref = bf16[4096,256]{1,0:T(8,128)(2,1)S(1)} custom-call(bf16[32,4096]{1,0:T(8,128)(2,1)S(1)} %shard_map.95.refs_0_, bf16[32,4096]{1,0:T(8,128)(2,1)} %shard_map.96.refs_1_, bf16[32,4096]{1,0:T(8,128)(2,1)} %collective-permute-done.16.refs_2_, bf16[32,4096]{1,0:T(8,128)(2,1)} %collective-permute-done.17.refs_3_, ...), custom_call_target="tpu_custom_call" | custom-call | bytes 1 | tf_op jit(solution)/shard_map/pallas_call | solution.py:263
  58.7 22.6 %shard_map.98.refs_9_ = f32[2,2048,256]{2,1,0:T(8,128)S(1)} custom-call(bf16[4096,256]{1,0:T(8,128)(2,1)S(1)} %shard_map.97.rot_ref, bf16[16,2048]{1,0:T(8,128)(2,1)} %get-tuple-element.32.refs_0_, bf16[16,2048]{1,0:T(8,128)(2,1)} %collective-permute-done.18.refs_1_, bf16[16,2048]{1,0:T(8,128)(2,1)S(1)} %get-tuple-element.31.__1_.refs_2_, ...), custom_call_target="tpu_custom_call" | custom-call | flops 17179869184 | bytes 16777216 | tf_op jit(solution)/shard_map/pallas_call | solution.py:349
  81.3 3.0 %shard_map.99 = f32[2,8,1]{2,1,0:T(8,128)S(1)} custom-call(bf16[64,2176]{1,0:T(8,128)(2,1)S(1)} %get-tuple-element.24.refs_0_.refs_4_, bf16[64,2176]{1,0:T(8,128)(2,1)S(1)} %collective-permute-done.5.refs_1_.refs_5_, bf16[64,2176]{1,0:T(8,128)(2,1)S(1)} %collective-permute-done.6.refs_2_.refs_6_, ...), custom_call_target="tpu_custom_call" | custom-call | flops 536870912 | bytes 4194304 | tf_op jit(solution)/shard_map/pallas_call | solution.py:408
  87.4 2.2 %collective-permute-done.22 = f32[2,8,1]{2,1,0:T(8,128)S(1)} collective-permute-done((f32[2,8,1]{2,1,0:T(8,128)S(1)}, f32[2,8,1]{2,1,0:T(8,128)S(1)}, u32[]{:S(2)}, u32[]{:S(2)}) %collective-permute-start.22) | collective-permute-done | bytes 96 | tf_op jit(solution)/shard_map/ppermute | solution.py:31
  89.6 3.6 %collective-permute-start.26 = (f32[2,8,1]{2,1,0:T(8,128)S(1)}, f32[2,8,1]{2,1,0:T(8,128)S(1)}, u32[]{:S(2)}, u32[]{:S(2)}) collective-permute-start(f32[2,8,1]{2,1,0:T(8,128)S(1)} %add_add_fusion.1), channel_id=1, source_target_pairs={{0,12},{1,13},{2,14},{3,15},{4,8},{5,9},{6,10},{7,11},{8,4},{9,5},... | collective-permute-start | bytes 200 | tf_op jit(solution)/shard_map/ppermute | solution.py:31
  94.0 1.1 %collective-permute-done.26 = f32[2,8,1]{2,1,0:T(8,128)S(1)} collective-permute-done((f32[2,8,1]{2,1,0:T(8,128)S(1)}, f32[2,8,1]{2,1,0:T(8,128)S(1)}, u32[]{:S(2)}, u32[]{:S(2)}) %collective-permute-start.26) | collective-permute-done | bytes 96 | tf_op jit(solution)/shard_map/ppermute | solution.py:31
  95.1 1.8 %collective-permute-done.24 = f32[2,8,1]{2,1,0:T(8,128)S(1)} collective-permute-done((f32[2,8,1]{2,1,0:T(8,128)S(1)}, f32[2,8,1]{2,1,0:T(8,128)S(1)}, u32[]{:S(2)}, u32[]{:S(2)}) %collective-permute-start.24) | collective-permute-done | bytes 96 | tf_op jit(solution)/shard_map/ppermute | solution.py:31
  (72 shorter events, 15.3 us)
Async XLA Ops:
  1.8 5.4 %collective-permute-start = (bf16[16,18432]{1,0:T(8,128)(2,1)S(1)}, bf16[16,18432]{1,0:T(8,128)(2,1)S(1)}, u32[]{:S(2)}, u32[]{:S(2)}) collective-permute-start(bf16[16,18432]{1,0:T(8,128)(2,1)S(1)} %get-tuple-element.20), channel_id=1, source_target_pairs={{0,1},{1,0},{2,3},{3,2},{4,5},{5,4},{6,7},{7,6},{8,9},{9,8},{10,11... | collective-permute-start | bytes 1769480 | tf_op jit(solution)/shard_map/ppermute | solution.py:31
  2.4 10.8 %collective-permute-start.3 = (bf16[16,4096]{1,0:T(8,128)(2,1)}, bf16[16,4096]{1,0:T(8,128)(2,1)S(1)}, u32[]{:S(2)}, u32[]{:S(2)}) collective-permute-start(bf16[16,4096]{1,0:T(8,128)(2,1)} %first_ref.1), channel_id=1, source_target_pairs={{0,8},{1,9},{2,10},{3,11},{4,12},{5,13},{6,14},{7,15},{8,0},{9,1},... | collective-permute-start | bytes 393224 | tf_op jit(solution)/shard_map/ppermute | solution.py:31
  7.4 9.8 %collective-permute-start.2 = (bf16[16,10240]{1,0:T(8,128)(2,1)S(1)}, bf16[16,10240]{1,0:T(8,128)(2,1)S(1)}, u32[]{:S(2)}, u32[]{:S(2)}) collective-permute-start(bf16[16,10240]{1,0:T(8,128)(2,1)S(1)} %get-tuple-element.21._), channel_id=1, source_target_pairs={{0,2},{1,3},{2,0},{3,1},{4,6},{5,7},{6,4},{7,5},{8,10},{9,11},{10,... | collective-permute-start | bytes 983048 | tf_op jit(solution)/shard_map/ppermute | solution.py:31
  10.3 15.1 %collective-permute-start.1 = (bf16[16,16512]{1,0:T(8,128)(2,1)S(1)}, bf16[16,16512]{1,0:T(8,128)(2,1)S(1)}, u32[]{:S(2)}, u32[]{:S(2)}) collective-permute-start(bf16[16,16512]{1,0:T(8,128)(2,1)S(1)} %shard_map.85.refs_1_.sent_ref), channel_id=1, source_target_pairs={{0,1},{1,0},{2,3},{3,2},{4,5},{5,4},{6,7},{7,6},{8,9},{9,8},{10,11... | collective-permute-start | bytes 1585160 | tf_op jit(solution)/shard_map/ppermute | solution.py:31
  13.2 8.1 %collective-permute-start.11 = (bf16[32,4096]{1,0:T(8,128)(2,1)S(1)}, bf16[32,4096]{1,0:T(8,128)(2,1)S(1)}, u32[]{:S(2)}, u32[]{:S(2)}) collective-permute-start(bf16[32,4096]{1,0:T(8,128)(2,1)S(1)} %shard_map.86.refs_0_.__0_), channel_id=1, source_target_pairs={{0,4},{1,5},{2,6},{3,7},{4,0},{5,1},{6,2},{7,3},{8,12},{9,13},{10,... | collective-permute-start | bytes 786440 | tf_op jit(solution)/shard_map/ppermute | solution.py:31
  21.3 12.7 %collective-permute-start.8 = (bf16[32,4096]{1,0:T(8,128)(2,1)S(1)}, bf16[32,4096]{1,0:T(8,128)(2,1)S(1)}, u32[]{:S(2)}, u32[]{:S(2)}) collective-permute-start(bf16[32,4096]{1,0:T(8,128)(2,1)S(1)} %shard_map.90.refs_0_), channel_id=1, source_target_pairs={{0,2},{1,3},{2,0},{3,1},{4,6},{5,7},{6,4},{7,5},{8,10},{9,11},{10,... | collective-permute-start | bytes 786440 | tf_op jit(solution)/shard_map/ppermute | solution.py:31
  22.7 11.3 %collective-permute-start.9 = (bf16[16,6144]{1,0:T(8,128)(2,1)S(1)}, bf16[16,6144]{1,0:T(8,128)(2,1)S(1)}, u32[]{:S(2)}, u32[]{:S(2)}) collective-permute-start(bf16[16,6144]{1,0:T(8,128)(2,1)S(1)} %get-tuple-element.23._.__1_), channel_id=1, source_target_pairs={{0,8},{1,9},{2,10},{3,11},{4,12},{5,13},{6,14},{7,15},{8,0},{9,1},... | collective-permute-start | bytes 589832 | tf_op jit(solution)/shard_map/ppermute | solution.py:31
  25.4 21.6 %collective-permute-start.4 = (bf16[32,8320]{1,0:T(8,128)(2,1)S(1)}, bf16[32,8320]{1,0:T(8,128)(2,1)S(1)}, u32[]{:S(2)}, u32[]{:S(2)}) collective-permute-start(bf16[32,8320]{1,0:T(8,128)(2,1)S(1)} %shard_map.88.refs_1_), channel_id=1, source_target_pairs={{0,2},{1,3},{2,0},{3,1},{4,6},{5,7},{6,4},{7,5},{8,10},{9,11},{10,... | collective-permute-start | bytes 1597448 | tf_op jit(solution)/shard_map/ppermute | solution.py:31
  26.0 9.4 %collective-permute-start.12 = (bf16[32,4096]{1,0:T(8,128)(2,1)S(1)}, bf16[32,4096]{1,0:T(8,128)(2,1)S(1)}, u32[]{:S(2)}, u32[]{:S(2)}) collective-permute-start(bf16[32,4096]{1,0:T(8,128)(2,1)S(1)} %shard_map.90.refs_0_), channel_id=1, source_target_pairs={{0,1},{1,0},{2,3},{3,2},{4,5},{5,4},{6,7},{7,6},{8,9},{9,8},{10,11... | collective-permute-start | bytes 786440 | tf_op jit(solution)/shard_map/ppermute | solution.py:31
  34.1 11.5 %collective-permute-start.14 = (bf16[32,4096]{1,0:T(8,128)(2,1)S(1)}, bf16[32,4096]{1,0:T(8,128)(2,1)}, u32[]{:S(2)}, u32[]{:S(2)}) collective-permute-start(bf16[32,4096]{1,0:T(8,128)(2,1)S(1)} %shard_map.92.refs_1_), channel_id=1, source_target_pairs={{0,2},{1,3},{2,0},{3,1},{4,6},{5,7},{6,4},{7,5},{8,10},{9,11},{10,... | collective-permute-start | bytes 786440 | tf_op jit(solution)/shard_map/ppermute | solution.py:31
  34.7 5.6 %collective-permute-start.10 = (bf16[16,4096]{1,0:T(8,128)(2,1)S(1)}, bf16[16,4096]{1,0:T(8,128)(2,1)S(1)}, u32[]{:S(2)}, u32[]{:S(2)}) collective-permute-start(bf16[16,4096]{1,0:T(8,128)(2,1)S(1)} %get-tuple-element.30.__1_.refs_5_), channel_id=1, source_target_pairs={{0,4},{1,5},{2,6},{3,7},{4,0},{5,1},{6,2},{7,3},{8,12},{9,13},{10,... | collective-permute-start | bytes 393224 | tf_op jit(solution)/shard_map/ppermute | solution.py:31
  41.0 4.6 %collective-permute-start.15 = (bf16[16,2048]{1,0:T(8,128)(2,1)S(1)}, bf16[16,2048]{1,0:T(8,128)(2,1)S(1)}, u32[]{:S(2)}, u32[]{:S(2)}) collective-permute-start(bf16[16,2048]{1,0:T(8,128)(2,1)S(1)} %get-tuple-element.31.__1_.refs_2_), channel_id=1, source_target_pairs={{0,16},{16,0},{1,17},{17,1},{2,18},{18,2},{3,19},{19,3},{4,20},{20... | collective-permute-start | bytes 196616 | tf_op jit(solution)/shard_map/ppermute | solution.py:31
  42.5 6.8 %collective-permute-start.16 = (bf16[32,4096]{1,0:T(8,128)(2,1)S(1)}, bf16[32,4096]{1,0:T(8,128)(2,1)}, u32[]{:S(2)}, u32[]{:S(2)}) collective-permute-start(bf16[32,4096]{1,0:T(8,128)(2,1)S(1)} %shard_map.95.refs_0_), channel_id=1, source_target_pairs={{0,1},{1,0},{2,3},{3,2},{4,5},{5,4},{6,7},{7,6},{8,9},{9,8},{10,11... | collective-permute-start | bytes 786440 | tf_op jit(solution)/shard_map/ppermute | solution.py:31
  45.6 5.4 %collective-permute-start.17 = (bf16[32,4096]{1,0:T(8,128)(2,1)}, bf16[32,4096]{1,0:T(8,128)(2,1)}, u32[]{:S(2)}, u32[]{:S(2)}) collective-permute-start(bf16[32,4096]{1,0:T(8,128)(2,1)} %shard_map.96.refs_1_), channel_id=1, source_target_pairs={{0,1},{1,0},{2,3},{3,2},{4,5},{5,4},{6,7},{7,6},{8,9},{9,8},{10,11... | collective-permute-start | bytes 786440 | tf_op jit(solution)/shard_map/ppermute | solution.py:31
  45.6 13.0 %collective-permute-start.18 = (bf16[16,2048]{1,0:T(8,128)(2,1)}, bf16[16,2048]{1,0:T(8,128)(2,1)}, u32[]{:S(2)}, u32[]{:S(2)}) collective-permute-start(bf16[16,2048]{1,0:T(8,128)(2,1)} %get-tuple-element.32.refs_0_), channel_id=1, source_target_pairs={{0,16},{16,0},{1,17},{17,1},{2,18},{18,2},{3,19},{19,3},{4,20},{20... | collective-permute-start | bytes 196616 | tf_op jit(solution)/shard_map/ppermute | solution.py:31
  46.8 11.9 %collective-permute-start.19 = (bf16[16,2048]{1,0:T(8,128)(2,1)S(1)}, bf16[16,2048]{1,0:T(8,128)(2,1)}, u32[]{:S(2)}, u32[]{:S(2)}) collective-permute-start(bf16[16,2048]{1,0:T(8,128)(2,1)S(1)} %get-tuple-element.31.__1_.refs_2_), channel_id=1, source_target_pairs={{0,1},{1,0},{2,3},{3,2},{4,5},{5,4},{6,7},{7,6},{8,9},{9,8},{10,11... | collective-permute-start | bytes 196616 | tf_op jit(solution)/shard_map/ppermute | solution.py:31
  47.8 10.9 %collective-permute-start.20 = (bf16[16,2048]{1,0:T(8,128)(2,1)S(1)}, bf16[16,2048]{1,0:T(8,128)(2,1)}, u32[]{:S(2)}, u32[]{:S(2)}) collective-permute-start(bf16[16,2048]{1,0:T(8,128)(2,1)S(1)} %collective-permute-done.15.__1_.refs_4_), channel_id=1, source_target_pairs={{0,1},{1,0},{2,3},{3,2},{4,5},{5,4},{6,7},{7,6},{8,9},{9,8},{10,11... | collective-permute-start | bytes 196616 | tf_op jit(solution)/shard_map/ppermute | solution.py:31
  49.3 32.0 %collective-permute-start.5 = (bf16[64,2176]{1,0:T(8,128)(2,1)S(1)}, bf16[64,2176]{1,0:T(8,128)(2,1)S(1)}, u32[]{:S(2)}, u32[]{:S(2)}) collective-permute-start(bf16[64,2176]{1,0:T(8,128)(2,1)S(1)} %get-tuple-element.25), channel_id=1, source_target_pairs={{0,4},{1,5},{2,6},{3,7},{4,0},{5,1},{6,2},{7,3},{8,12},{9,13},{10,... | collective-permute-start | bytes 835592 | tf_op jit(solution)/shard_map/ppermute | solution.py:31
  51.0 30.3 %collective-permute-start.6 = (bf16[64,2176]{1,0:T(8,128)(2,1)S(1)}, bf16[64,2176]{1,0:T(8,128)(2,1)S(1)}, u32[]{:S(2)}, u32[]{:S(2)}) collective-permute-start(bf16[64,2176]{1,0:T(8,128)(2,1)S(1)} %get-tuple-element.26), channel_id=1, source_target_pairs={{0,8},{1,9},{2,10},{3,11},{4,12},{5,13},{6,14},{7,15},{8,0},{9,1},... | collective-permute-start | bytes 835592 | tf_op jit(solution)/shard_map/ppermute | solution.py:31
  58.6 22.7 %collective-permute-start.7 = (bf16[64,2176]{1,0:T(8,128)(2,1)S(1)}, bf16[64,2176]{1,0:T(8,128)(2,1)S(1)}, u32[]{:S(2)}, u32[]{:S(2)}) collective-permute-start(bf16[64,2176]{1,0:T(8,128)(2,1)S(1)} %get-tuple-element.27), channel_id=1, source_target_pairs={{0,12},{1,13},{2,14},{3,15},{4,8},{5,9},{6,10},{7,11},{8,4},{9,5},... | collective-permute-start | bytes 835592 | tf_op jit(solution)/shard_map/ppermute | solution.py:31
  85.9 3.7 %collective-permute-start.22 = (f32[2,8,1]{2,1,0:T(8,128)S(1)}, f32[2,8,1]{2,1,0:T(8,128)S(1)}, u32[]{:S(2)}, u32[]{:S(2)}) collective-permute-start(f32[2,8,1]{2,1,0:T(8,128)S(1)} %shard_map.99), channel_id=1, source_target_pairs={{0,2},{1,3},{2,0},{3,1},{4,6},{5,7},{6,4},{7,5},{8,10},{9,11},{10,... | collective-permute-start | bytes 200 | tf_op jit(solution)/shard_map/ppermute | solution.py:31
  89.6 5.4 %collective-permute-start.26 = (f32[2,8,1]{2,1,0:T(8,128)S(1)}, f32[2,8,1]{2,1,0:T(8,128)S(1)}, u32[]{:S(2)}, u32[]{:S(2)}) collective-permute-start(f32[2,8,1]{2,1,0:T(8,128)S(1)} %add_add_fusion.1), channel_id=1, source_target_pairs={{0,12},{1,13},{2,14},{3,15},{4,8},{5,9},{6,10},{7,11},{8,4},{9,5},... | collective-permute-start | bytes 200 | tf_op jit(solution)/shard_map/ppermute | solution.py:31
  93.2 3.7 %collective-permute-start.24 = (f32[2,8,1]{2,1,0:T(8,128)S(1)}, f32[2,8,1]{2,1,0:T(8,128)S(1)}, u32[]{:S(2)}, u32[]{:S(2)}) collective-permute-start(f32[2,8,1]{2,1,0:T(8,128)S(1)} %add_add_fusion.1), channel_id=1, source_target_pairs={{0,4},{1,5},{2,6},{3,7},{4,0},{5,1},{6,2},{7,3},{8,12},{9,13},{10,... | collective-permute-start | bytes 200 | tf_op jit(solution)/shard_map/ppermute | solution.py:31
  93.2 4.5 %collective-permute-start.25 = (f32[2,8,1]{2,1,0:T(8,128)S(1)}, f32[2,8,1]{2,1,0:T(8,128)S(1)}, u32[]{:S(2)}, u32[]{:S(2)}) collective-permute-start(f32[2,8,1]{2,1,0:T(8,128)S(1)} %add_add_fusion.1), channel_id=1, source_target_pairs={{0,8},{1,9},{2,10},{3,11},{4,12},{5,13},{6,14},{7,15},{8,0},{9,1},... | collective-permute-start | bytes 200 | tf_op jit(solution)/shard_map/ppermute | solution.py:31
  (13 other events, 82.7 us)

commit v12 on v9

--- a/solution.py
+++ b/solution.py
@@ -69,20 +69,20 @@
     )(factors)
 
 
-def flags_kernel(ways, batch_count, owners_ref, _, flag_ref):
+def flags_kernel(batch_count, owners_ref, _, flag_ref):
     me, batch = lax.axis_index("wide"), lax.rem(lax.axis_index("groups"), batch_count)
     apart = owners_ref[batch] ^ me
     lane = lax.broadcasted_iota(jnp.int32, flag_ref.shape, 1)
-    flags = jnp.zeros(flag_ref.shape, jnp.float32)
-    for step, bit in enumerate(ways):
-        same = jnp.where((apart & bit) == 0, 1.0, 0.0)
+    flags = jnp.where(lane - 2 == apart // 4, 1.0, 0.0)
+    for step in range(2):
+        same = jnp.where((apart & (1 << step)) == 0, 1.0, 0.0)
         flags = jnp.where(lane == step, same, flags)
     flag_ref[...] = flags.astype(flag_ref.dtype)
 
 
-def owner_flags(owners, ways, after):
-    return pl.pallas_call(
-        functools.partial(flags_kernel, ways, owners.shape[0]),
+def owner_flags(owners, after):
+    return pl.pallas_call(
+        functools.partial(flags_kernel, owners.shape[0]),
         in_specs=in_smem(1) + in_place(1),
         out_specs=in_vmem(1)[0],
         out_shape=jax.ShapeDtypeStruct((after.shape[0], LANES), after.dtype),
@@ -91,8 +91,8 @@
     )(owners, after)
 
 
-def pick_kernel(step, cols, last, flag_ref, keep_ref, got_ref, *refs):
-    first_ref, second_ref = refs[-2:]
+def pick_kernel(step, cols, half, flag_ref, keep_ref, got_ref, *refs):
+    out_refs = refs[-2:] if step == 0 else refs[-((keep_ref.shape[1] - half) // cols):]
     same = flag_ref[:, step:step + 1]
     differs = 1 - same
 
@@ -100,49 +100,63 @@
         place = slice(at, at + size)
         return keep_ref[:, place] * same + got_ref[:, place] * differs
 
-    if last:
-        first_ref[...] = chosen(0, cols)
-        second_ref[...] = chosen(cols, keep_ref.shape[1] - cols)
-    else:
-        size = keep_ref.shape[1] - first_ref.shape[1]
-        shared = chosen(2 * size, keep_ref.shape[1] - 2 * size)
-        for part, out_ref in enumerate((first_ref, second_ref)):
-            out_ref[:, :size] = chosen(part * size, size)
-            out_ref[:, size:] = shared
-
-
-def pick(flags, keep, got, step, cols, count, after):
+    size = out_refs[0].shape[1] - half
+    shared = chosen(len(out_refs) * size, half)
+    for n, out_ref in enumerate(out_refs):
+        out_ref[:, :size] = chosen(n * size, size)
+        out_ref[:, size:] = shared
+
+
+def pick(flags, keep, got, step, cols, half, after):
     rows, width = keep.shape
-    if count > 1:
-        widths = [width - count // 2 * cols] * 2
-    else:
-        widths = [cols, width - cols]
-    return pl.pallas_call(
-        functools.partial(pick_kernel, step, cols, count == 1),
+    parts = 2 if step == 0 else (width - half) // cols
+    size = (width - half) // parts + half
+    return pl.pallas_call(
+        functools.partial(pick_kernel, step, cols, half),
         in_specs=in_vmem(3) + in_place(len(after)),
+        out_specs=in_vmem(parts),
+        out_shape=[jax.ShapeDtypeStruct((rows, size), keep.dtype)] * parts,
+        compiler_params=params(16),
+        cost_estimate=pl.CostEstimate(flops=0, bytes_accessed=1, transcendentals=0),
+    )(flags, keep, got, *after)
+
+
+def pick_one_kernel(count, flag_ref, *refs):
+    left_ref, right_ref = refs[-2:]
+    cols = left_ref.shape[1]
+    for out_ref, place in ((left_ref, slice(0, cols)), (right_ref, slice(cols, None))):
+        out_ref[...] = sum(refs[k][:, place] * flag_ref[:, 2 + k:3 + k] for k in range(count))
+
+
+def pick_one(flags, pieces, cols, after):
+    rows, width = pieces[0].shape
+    return pl.pallas_call(
+        functools.partial(pick_one_kernel, len(pieces)),
+        in_specs=in_vmem(1 + len(pieces)) + in_place(len(after)),
         out_specs=in_vmem(2),
-        out_shape=[jax.ShapeDtypeStruct((rows, w), keep.dtype) for w in widths],
-        compiler_params=params(16),
-        cost_estimate=pl.CostEstimate(flops=0, bytes_accessed=1, transcendentals=0),
-    )(flags, keep, got, *after)
-
-
-def join_kernel(first_ref, second_ref, out_ref):
-    rows = first_ref.shape[0]
-    out_ref[:rows, :] = first_ref[...]
-    out_ref[rows:, :] = second_ref[...]
-
-
-def join(first, second):
-    rows, width = first.shape
+        out_shape=[jax.ShapeDtypeStruct((rows, w), pieces[0].dtype) for w in (cols, width - cols)],
+        compiler_params=params(16),
+        cost_estimate=pl.CostEstimate(flops=0, bytes_accessed=1, transcendentals=0),
+    )(flags, *pieces, *after)
+
+
+def join_kernel(*refs):
+    out_ref = refs[-1]
+    rows = refs[0].shape[0]
+    for n, ref in enumerate(refs[:-2]):
+        out_ref[n * rows:(n + 1) * rows, :] = ref[...]
+
+
+def join(pieces, after):
+    rows, width = pieces[0].shape
     return pl.pallas_call(
         join_kernel,
-        in_specs=in_vmem(2),
+        in_specs=in_vmem(len(pieces)) + in_place(1),
         out_specs=in_vmem(1)[0],
-        out_shape=jax.ShapeDtypeStruct((2 * rows, width), first.dtype),
-        compiler_params=params(16),
-        cost_estimate=pl.CostEstimate(flops=0, bytes_accessed=1, transcendentals=0),
-    )(first, second)
+        out_shape=jax.ShapeDtypeStruct((len(pieces) * rows, width), pieces[0].dtype),
+        compiler_params=params(16),
+        cost_estimate=pl.CostEstimate(flops=0, bytes_accessed=1, transcendentals=0),
+    )(*pieces, after)
 
 
 def gate_kernel(*_):
@@ -186,64 +200,31 @@
     )(ids, grads, after)
 
 
-def rotate_kernel(act_count, *refs):
-    act_refs, (basis_ref, _, out_ref, held_ref, sems) = refs[:act_count], refs[act_count:]
+def rotate_kernel(act_count, done, *refs):
+    act_refs, basis_ref, out_ref = refs[:act_count], refs[act_count], refs[-1]
     depth, width = basis_ref.shape
-    places = [slice(k * depth, (k + 1) * depth) for k in range(width // depth)]
-    copies = [
-        pltpu.make_async_copy(basis_ref.at[:, cols], held_ref.at[k], sems.at[k])
-        for k, cols in enumerate(places)
-    ]
-    for copy in copies:
-        copy.start()
-    for k, cols in enumerate(places):
-        act = jnp.concatenate([ref[:, cols] for ref in act_refs], axis=0)
-        copies[k].wait()
-        turned = jnp.dot(act, held_ref[k], preferred_element_type=jnp.float32)
-        out_ref[cols, :] = turned.astype(jnp.bfloat16).T
-
-
-def rotate(act_pieces, basis, after):
-    tokens = sum(x.shape[0] for x in act_pieces)
-    depth, width = basis.shape
-    count = width // depth
-    return pl.pallas_call(
-        functools.partial(rotate_kernel, len(act_pieces)),
-        in_specs=in_vmem(len(act_pieces)) + in_place(2),
-        out_specs=in_vmem(2),
-        out_shape=[
-            jax.ShapeDtypeStruct((width, tokens), jnp.bfloat16),
-            jax.ShapeDtypeStruct((count, depth, depth), jnp.bfloat16),
-        ],
-        scratch_shapes=[pltpu.SemaphoreType.DMA((count,))],
-        compiler_params=params(46 if tokens <= 256 else 32),
-        cost_estimate=pl.CostEstimate(flops=0, bytes_accessed=1, transcendentals=0),
-    )(*act_pieces, basis, after)
-
-
-def rotate_rest_kernel(act_count, *refs):
-    act_refs, (held_ref, first_ref, out_ref) = refs[:act_count], refs[act_count:]
-    depth = held_ref.shape[1]
-    done = first_ref.shape[1]
-    out_ref[:, :done] = first_ref[...]
-    for k in range(held_ref.shape[0]):
+    if done:
+        out_ref[:, :done] = refs[act_count + 1][...]
+    for k in range(width // depth):
         cols = slice(k * depth, (k + 1) * depth)
         act = jnp.concatenate([ref[:, cols] for ref in act_refs], axis=0)
-        turned = jnp.dot(act, held_ref[k], preferred_element_type=jnp.float32)
+        turned = jnp.dot(act, basis_ref[:, cols], preferred_element_type=jnp.float32)
         out_ref[cols, done:] = turned.astype(jnp.bfloat16).T
 
 
-def rotate_rest(act_pieces, held, first):
-    width, done = first.shape
+def rotate(act_pieces, basis, after, first=None):
+    width = basis.shape[1]
+    done = 0 if first is None else first.shape[1]
     tokens = done + sum(x.shape[0] for x in act_pieces)
-    return pl.pallas_call(
-        functools.partial(rotate_rest_kernel, len(act_pieces)),
-        in_specs=in_vmem(len(act_pieces) + 2),
+    more = [after] if first is None else [first]
+    return pl.pallas_call(
+        functools.partial(rotate_kernel, len(act_pieces), done),
+        in_specs=in_vmem(len(act_pieces) + 1) + (in_place(1) if first is None else in_vmem(1)),
         out_specs=in_vmem(1)[0],
         out_shape=jax.ShapeDtypeStruct((width, tokens), jnp.bfloat16),
         compiler_params=params(16 if tokens <= 256 else 32),
         cost_estimate=pl.CostEstimate(flops=0, bytes_accessed=1, transcendentals=0),
-    )(*act_pieces, held, first)
+    )(*act_pieces, basis, *more)
 
 
 def image_kernel(batch_count, total, per, rot_ref, *refs):
@@ -365,9 +346,10 @@
         ids = jnp.concatenate([ids_ref[me ^ r] for r in ranks], axis=0).astype(jnp.float32)
         seqs = lax.broadcasted_iota(jnp.int32, ids.shape, 1).astype(jnp.float32)
         member = jnp.where(ids == seqs, 1.0, 0.0).T
+        own = lax.rem(lax.axis_index("groups"), batch_count)
         for b in range(batch_count):
             sums = jnp.sum(member * token_ref[b:b + 1, :], axis=1, keepdims=True)
-            out_ref[b] = sums[:out_ref.shape[1], :]
+            out_ref[lax.rem(own + b, batch_count)] = sums[:out_ref.shape[1], :]
 
 
 def score_parts(grads, ranks, grad_basis, image, seq_count):
@@ -400,70 +382,45 @@
     train_act, train_grad, seq_ids, act_basis, grad_basis, eigenvalues, query_factors, owners
 ):
     wide_count = lax.axis_size("wide")
-    bits = [1 << n for n in range(wide_count.bit_length() - 1)]
-    me = lax.axis_index("wide")
+    along_z = range(wide_count // 4)
     tok_local = train_act.shape[0]
     seq_count = tok_local * wide_count // SEQ_MEAN
     cols = grad_basis.shape[1]
     hidden = train_grad.shape[1]
     batch_count = owners.shape[0]
     score_scale = 1.0 / math.sqrt(FF * D * QT * SEQ_MEAN)
-    batch = lax.axis_index("groups") % batch_count
-
-    ways = bits[:2] + bits[:1:-1]
-    order = [0]
-    for bit in reversed(bits):
-        order = order + [r + bit for r in order]
-    order = sorted(order, key=lambda r: [r & bit for bit in ways])
-    acts, ranks = train_act, [0]
-    far = bits[:1:-1]
+
+    half = (query_factors.shape[2] - hidden) // 2
+    order = [4 * k + r for r in (0, 2, 1, 3) for k in along_z]
     keep, give = cut_factors(query_factors, order, hidden, batch_count)
-    flags = owner_flags(owners, ways, keep)
-    count = wide_count // 2
-    for step, bit in enumerate(ways):
-        got = swap(give, "wide", bit)
-        if step < len(far) - 1:
-            acts = join(acts, swap(acts, "wide", far[step]))
-            ranks = ranks + [r + far[step] for r in ranks]
-            after = [acts]
-        elif step == len(far) - 1:
-            last = swap(acts, "wide", far[step])
-            sent = cut_grads(seq_ids, train_grad, give, wide_count)
-            after = [last, sent]
-        elif step == len(far):
-            after = [over[0][0], first]
-        else:
-            after = []
-        keep, give = pick(flags, keep, got, step, cols, count, after)
-        count //= 2
-        if step == len(far) - 1:
-            near = [(gate(acts, [give]), ranks), (gate(last, [give]), [r + far[step] for r in ranks])]
-            over = [(swap(x, "wide", 2), [r + 2 for r in has]) for x, has in near]
-            near += [(swap(x, "wide", 1), [r + 1 for r in has]) for x, has in near]
-            first, basis = rotate([x for x, _ in near], act_basis, give)
-    left, right = keep, give
+    flags = owner_flags(owners, keep)
+    keep, give = pick(flags, keep, swap(give, "wide", 1), 0, cols, half, [])
+    sent = cut_grads(seq_ids, train_grad, give, wide_count)
+    parts = pick(flags, keep, swap(give, "wide", 2), 1, cols, half, [sent])
+    acts = join([train_act] + [swap(train_act, "wide", 4 * k) for k in along_z if k], parts[0])
+    ranks = [4 * k for k in along_z]
+    near = [(acts, ranks), (swap(acts, "wide", 1), [r + 1 for r in ranks])]
+    over = [(swap(acts, "wide", 2), [r + 2 for r in ranks])]
+    first = rotate([x for x, _ in near], act_basis, parts[0])
+    parts = [swap(parts[k], "wide", 4 * k) if k else parts[0] for k in along_z]
+    left, right = pick_one(flags, parts, cols, [over[0][0], first])
 
     lefts = [left, swap(left, "groups", 1)]
     other = swap(right, "groups", 1)
     halves = []
     for x in (right, other):
         halves += [x, swap(x, "wide", 1)]
-    over = [(gate(x, [wait]), has) for (x, has), wait in zip(over, (right, other))]
     over += [(swap(x, "wide", 1), [r + 1 for r in has]) for x, has in over]
-    rot = rotate_rest([x for x, _ in over], basis, first)
+    rot = rotate([x for x, _ in over], act_basis, None, first)
     ranks = [r for _, has in near + over for r in has]
 
-    grads = lax.all_to_all(gate(sent, [rot, lefts[1], halves[1], halves[3]]), "wide", 0, 0)
+    grads = lax.all_to_all(gate(sent, [right]), "wide", 0, 0)
 
     image = images(rot, lefts, halves, eigenvalues)
     parts = score_parts(grads, ranks, grad_basis, image, seq_count)
-    for some in (bits[:2], bits[2:]):
-        others = [swap(parts, "wide", some[0] * n) for n in range(1, 1 << len(some))]
-        parts = parts + sum(others)
-    mine, others = parts[0, :, 0], parts[1, :, 0]
-    first = jnp.where(batch == 0, mine, others)
-    second = jnp.where(batch == 0, others, mine)
-    return jnp.stack([first, second], axis=1) * score_scale
+    for step, count in ((1, 4), (4, wide_count // 4)):
+        parts = parts + sum(swap(parts, "wide", step * n) for n in range(1, count))
+    return parts[:, :, 0].T * score_scale
 
 
 def solution(mesh):

time: 103 us -> 95.3 us (0.925)
  waiting for transfers between devices: 32.7 us -> 25.9 us
  local copies, waits for them, and re-layouts: 1.95 us -> 4.94 us
  Pallas kernels: 35.9 us -> 33 us
    ppermute x22 -> x21, waiting for transfers between devices: 31.8 us -> 25.9 us  [swap(): return lax.ppermute(x, axis, [(i, i ^ bit) for i in range(count)])]
    unnamed x10 -> x16, local copies, waits for them, and re-layouts: 1.95 us -> 4.94 us
    pallas_call x8 -> x7, Pallas kernels: 5.75 us -> 2.89 us  [the longest x2 1.88 us: rotate(): pl.pallas_call(functools.partial(rotate_kernel, len(act_pieces), done), i...]
    ppermute x22 -> x21, starting transfers between devices: 24.5 us -> 22.8 us  [swap(): return lax.ppermute(x, axis, [(i, i ^ bit) for i in range(count)])]
  transfers between devices with their start and end apart: 23 -> 22, of which waited for: 12 -> 11; matrix products, arithmetic and copies ran while one was open for 0% -> 0% of each run, Pallas kernels for 29% -> 29%
where the time goes in v12:
time: 95.3 us; the launch traced here: 95 us
  Pallas kernels  33 us (35%)
  starting transfers between devices  29.6 us (31%)
  waiting for transfers between devices  25.9 us (27%)
  local copies, waits for them, and re-layouts  4.94 us (5%)
  other arithmetic  1.36 us (1%)
    ppermute x21, waiting for transfers between devices, swap(): return lax.ppermute(x, axis, [(i, i ^ bit) for i in range(count)])  25.9 us
    pallas_call x1, Pallas kernels, images(): pl.pallas_call(functools.partial(image_kernel, batch_count, total, per),...  23.1 us
    ppermute x21, starting transfers between devices, swap(): return lax.ppermute(x, axis, [(i, i ^ bit) for i in range(count)])  22.8 us
    all_to_all x1, starting transfers between devices, per_device(): grads = lax.all_to_all(gate(sent, [right]), 'wide', 0, 0)  6.8 us
    pallas_call x1, Pallas kernels, score_parts(): pl.pallas_call(functools.partial(score_kernel, batch_count, ranks), grid=...  5.27 us
    unnamed x16, local copies, waits for them, and re-layouts  4.94 us
  transfers between devices with their start and end apart: 22, of which 11 were waited for; matrix products, arithmetic and copies ran while one was open for 0% of the time, Pallas kernels for 29%

profile of v12, /device:TPU:0, one launch (start us, length us, event | category | flops | bytes accessed | tf_op | source)
XLA Modules:
  0.0 95.0 jit_solution(5949798196677510929)
XLA Ops:
  0.0 1.7 %copy-done.2 = bf16[2,16,36864]{2,1,0:T(8,128)(2,1)S(1)} copy-done((bf16[2,16,36864]{2,1,0:T(8,128)(2,1)S(1)}, bf16[2,16,36864]{2,1,0:T(8,128)(2,1)}, u32[]{:S(2)}) %copy-start.2) | copy-done | bytes 2359320
  4.1 3.0 %collective-permute-start.1 = (bf16[16,10240]{1,0:T(8,128)(2,1)S(1)}, bf16[16,10240]{1,0:T(8,128)(2,1)S(1)}, u32[]{:S(2)}, u32[]{:S(2)}) collective-permute-start(bf16[16,10240]{1,0:T(8,128)(2,1)S(1)} %get-tuple-element.17._), channel_id=1, source_target_pairs={{0,2},{1,3},{2,0},{3,1},{4,6},{5,7},{6,4},{7,5},{8,10},{9,11},{10,... | collective-permute-start | bytes 983048 | tf_op jit(solution)/shard_map/ppermute | solution.py:31
  7.1 2.6 %collective-permute-start.6 = (bf16[16,4096]{1,0:T(8,128)(2,1)S(1)}, bf16[16,4096]{1,0:T(8,128)(2,1)S(1)}, u32[]{:S(2)}, u32[]{:S(2)}) collective-permute-start(bf16[16,4096]{1,0:T(8,128)(2,1)S(1)} %copy-done.4), channel_id=1, source_target_pairs={{0,8},{1,9},{2,10},{3,11},{4,12},{5,13},{6,14},{7,15},{8,0},{9,1},... | collective-permute-start | bytes 393224 | tf_op jit(solution)/shard_map/ppermute | solution.py:31
  9.7 1.6 %collective-permute-start.5 = (bf16[16,4096]{1,0:T(8,128)(2,1)S(1)}, bf16[16,4096]{1,0:T(8,128)(2,1)S(1)}, u32[]{:S(2)}, u32[]{:S(2)}) collective-permute-start(bf16[16,4096]{1,0:T(8,128)(2,1)S(1)} %copy-done.4), channel_id=1, source_target_pairs={{0,4},{1,5},{2,6},{3,7},{4,0},{5,1},{6,2},{7,3},{8,12},{9,13},{10,... | collective-permute-start | bytes 393224 | tf_op jit(solution)/shard_map/ppermute | solution.py:31
  11.5 1.7 %shard_map.85.refs_0_.__0_ = bf16[16,16,2176]{2,1,0:T(8,128)(2,1)} custom-call(s32[16]{0:T(128)S(1)} %copy-done.6, bf16[16,32768]{1,0:T(8,128)(2,1)S(1)} %copy-done.3, bf16[16,10240]{1,0:T(8,128)(2,1)S(1)} %get-tuple-element.17._), custom_call_target="tpu_custom_call" | custom-call | bytes 1 | tf_op jit(solution)/shard_map/pallas_call | solution.py:193
  13.1 1.9 %collective-permute-done.1.got_ref = bf16[16,10240]{1,0:T(8,128)(2,1)S(1)} collective-permute-done((bf16[16,10240]{1,0:T(8,128)(2,1)S(1)}, bf16[16,10240]{1,0:T(8,128)(2,1)S(1)}, u32[]{:S(2)}, u32[]{:S(2)}) %collective-permute-start.1) | collective-permute-done | bytes 327712 | tf_op jit(solution)/shard_map/ppermute | solution.py:31
  15.2 3.0 %collective-permute-done.6.refs_2_ = bf16[16,4096]{1,0:T(8,128)(2,1)S(1)} collective-permute-done((bf16[16,4096]{1,0:T(8,128)(2,1)S(1)}, bf16[16,4096]{1,0:T(8,128)(2,1)S(1)}, u32[]{:S(2)}, u32[]{:S(2)}) %collective-permute-start.6) | collective-permute-done | bytes 131104 | tf_op jit(solution)/shard_map/ppermute | solution.py:31
  18.2 1.8 %collective-permute-done.7.refs_3_ = bf16[16,4096]{1,0:T(8,128)(2,1)S(1)} collective-permute-done((bf16[16,4096]{1,0:T(8,128)(2,1)S(1)}, bf16[16,4096]{1,0:T(8,128)(2,1)S(1)}, u32[]{:S(2)}, u32[]{:S(2)}) %collective-permute-start.7) | collective-permute-done | bytes 131104 | tf_op jit(solution)/shard_map/ppermute | solution.py:31
  20.6 2.3 %collective-permute-start.2 = (bf16[16,4096]{1,0:T(8,128)(2,1)S(1)}, bf16[16,4096]{1,0:T(8,128)(2,1)S(1)}, u32[]{:S(2)}, u32[]{:S(2)}) collective-permute-start(bf16[16,4096]{1,0:T(8,128)(2,1)S(1)} %get-tuple-element.20), channel_id=1, source_target_pairs={{0,4},{1,5},{2,6},{3,7},{4,0},{5,1},{6,2},{7,3},{8,12},{9,13},{10,... | collective-permute-start | bytes 393224 | tf_op jit(solution)/shard_map/ppermute | solution.py:31
  22.9 1.9 %collective-permute-start.3 = (bf16[16,4096]{1,0:T(8,128)(2,1)S(1)}, bf16[16,4096]{1,0:T(8,128)(2,1)S(1)}, u32[]{:S(2)}, u32[]{:S(2)}) collective-permute-start(bf16[16,4096]{1,0:T(8,128)(2,1)S(1)} %get-tuple-element.21), channel_id=1, source_target_pairs={{0,8},{1,9},{2,10},{3,11},{4,12},{5,13},{6,14},{7,15},{8,0},{9,1},... | collective-permute-start | bytes 393224 | tf_op jit(solution)/shard_map/ppermute | solution.py:31
  24.9 1.5 %collective-permute-start.4 = (bf16[16,4096]{1,0:T(8,128)(2,1)S(1)}, bf16[16,4096]{1,0:T(8,128)(2,1)S(1)}, u32[]{:S(2)}, u32[]{:S(2)}) collective-permute-start(bf16[16,4096]{1,0:T(8,128)(2,1)S(1)} %get-tuple-element.22), channel_id=1, source_target_pairs={{0,12},{1,13},{2,14},{3,15},{4,8},{5,9},{6,10},{7,11},{8,4},{9,5},... | collective-permute-start | bytes 393224 | tf_op jit(solution)/shard_map/ppermute | solution.py:31
  26.3 6.5 %collective-permute-done.8.refs_4_.refs_0_ = bf16[64,4096]{1,0:T(8,128)(2,1)S(1)} collective-permute-done((bf16[64,4096]{1,0:T(8,128)(2,1)S(1)}, bf16[64,4096]{1,0:T(8,128)(2,1)S(1)}, u32[]{:S(2)}, u32[]{:S(2)}) %collective-permute-start.8) | collective-permute-done | bytes 524320 | tf_op jit(solution)/shard_map/ppermute | solution.py:31
  33.7 2.2 %collective-permute-done.4.refs_3_ = bf16[16,4096]{1,0:T(8,128)(2,1)S(1)} collective-permute-done((bf16[16,4096]{1,0:T(8,128)(2,1)S(1)}, bf16[16,4096]{1,0:T(8,128)(2,1)S(1)}, u32[]{:S(2)}, u32[]{:S(2)}) %collective-permute-start.4) | collective-permute-done | bytes 131104 | tf_op jit(solution)/shard_map/ppermute | solution.py:31
  36.0 6.8 %all-to-all-start = ((bf16[16,16,2176]{2,1,0:T(8,128)(2,1)}), bf16[16,16,2176]{2,1,0:T(8,128)(2,1)S(1)}, u32[]{:S(2)}, u32[]{:S(2)}) async-start(bf16[16,16,2176]{2,1,0:T(8,128)(2,1)} %shard_map.90), calls=%async_computation | async-start | bytes 2228224 | tf_op jit(solution)/shard_map/all_to_all | solution.py:417
  42.9 1.6 %collective-permute-start.13 = (bf16[16,2048]{1,0:T(8,128)(2,1)S(1)}, bf16[16,2048]{1,0:T(8,128)(2,1)S(1)}, u32[]{:S(2)}, u32[]{:S(2)}) collective-permute-start(bf16[16,2048]{1,0:T(8,128)(2,1)S(1)} %get-tuple-element.23.__1_.refs_2_), channel_id=1, source_target_pairs={{0,16},{16,0},{1,17},{17,1},{2,18},{18,2},{3,19},{19,3},{4,20},{20... | collective-permute-start | bytes 196616 | tf_op jit(solution)/shard_map/ppermute | solution.py:31
  45.0 2.3 %collective-permute-done.13.refs_4_ = bf16[16,2048]{1,0:T(8,128)(2,1)S(1)} collective-permute-done((bf16[16,2048]{1,0:T(8,128)(2,1)S(1)}, bf16[16,2048]{1,0:T(8,128)(2,1)S(1)}, u32[]{:S(2)}, u32[]{:S(2)}) %collective-permute-start.13) | collective-permute-done | bytes 65568 | tf_op jit(solution)/shard_map/ppermute | solution.py:31
  47.3 2.2 %copy-done.1 = bf16[512,4096]{1,0:T(8,128)(2,1)S(1)} copy-done((bf16[512,4096]{1,0:T(8,128)(2,1)S(1)}, bf16[512,4096]{1,0:T(8,128)(2,1)}, u32[]{:S(2)}) %copy-start.1) | copy-done | bytes 4194328
  50.6 23.1 %shard_map.92.image_ref = f32[2,2048,256]{2,1,0:T(8,128)} custom-call(bf16[4096,256]{1,0:T(8,128)(2,1)S(1)} %shard_map.91.rot_ref, bf16[16,2048]{1,0:T(8,128)(2,1)S(1)} %get-tuple-element.24.refs_0_, bf16[16,2048]{1,0:T(8,128)(2,1)S(1)} %collective-permute-done.11.refs_1_, bf16[16,2048]{1,0:T(8,128)(2,1)S(1)} %get-tuple-element.23.__1_.refs_2_, ...), custom_call_target="tpu_custom_call" | custom-call | flops 17179869184 | bytes 16777216 | tf_op jit(solution)/shard_map/pallas_call | solution.py:306
  74.8 5.3 %shard_map.93 = f32[2,8,1]{2,1,0:T(8,128)} custom-call(bf16[16,16,2176]{2,1,0:T(8,128)(2,1)} %copy-done.7, bf16[512,2048]{1,0:T(8,128)(2,1)} %basis_ref.1, f32[2,2048,256]{2,1,0:T(8,128)} %shard_map.92.image_ref, bf16[16,16,2176]{2,1,0:T(8,128)(2,1)} %copy-done.7), custom_call_target="tpu_custom_call" | custom-call | flops 536870912 | bytes 4194304 | tf_op jit(solution)/shard_map/pallas_call | solution.py:360
  80.0 1.9 %collective-permute-start.17 = (f32[2,8,1]{2,1,0:T(8,128)}, f32[2,8,1]{2,1,0:T(8,128)S(1)}, u32[]{:S(2)}, u32[]{:S(2)}) collective-permute-start(f32[2,8,1]{2,1,0:T(8,128)} %shard_map.93), channel_id=1, source_target_pairs={{0,3},{1,2},{2,1},{3,0},{4,7},{5,6},{6,5},{7,4},{8,11},{9,10},{10,... | collective-permute-start | bytes 200 | tf_op jit(solution)/shard_map/ppermute | solution.py:31
  82.2 1.3 %collective-permute-done.17 = f32[2,8,1]{2,1,0:T(8,128)S(1)} collective-permute-done((f32[2,8,1]{2,1,0:T(8,128)}, f32[2,8,1]{2,1,0:T(8,128)S(1)}, u32[]{:S(2)}, u32[]{:S(2)}) %collective-permute-start.17) | collective-permute-done | bytes 96 | tf_op jit(solution)/shard_map/ppermute | solution.py:31
  83.5 2.3 %collective-permute-done.16 = f32[2,8,1]{2,1,0:T(8,128)S(1)} collective-permute-done((f32[2,8,1]{2,1,0:T(8,128)}, f32[2,8,1]{2,1,0:T(8,128)S(1)}, u32[]{:S(2)}, u32[]{:S(2)}) %collective-permute-start.16) | collective-permute-done | bytes 96 | tf_op jit(solution)/shard_map/ppermute | solution.py:31
  86.5 3.3 %collective-permute-start.20 = (f32[2,8,1]{2,1,0:T(8,128)S(1)}, f32[2,8,1]{2,1,0:T(8,128)S(1)}, u32[]{:S(2)}, u32[]{:S(2)}) collective-permute-start(f32[2,8,1]{2,1,0:T(8,128)S(1)} %add_add_fusion), channel_id=1, source_target_pairs={{0,12},{1,13},{2,14},{3,15},{4,8},{5,9},{6,10},{7,11},{8,4},{9,5},... | collective-permute-start | bytes 200 | tf_op jit(solution)/shard_map/ppermute | solution.py:31
  92.0 2.3 %collective-permute-done.19 = f32[2,8,1]{2,1,0:T(8,128)S(1)} collective-permute-done((f32[2,8,1]{2,1,0:T(8,128)S(1)}, f32[2,8,1]{2,1,0:T(8,128)S(1)}, u32[]{:S(2)}, u32[]{:S(2)}) %collective-permute-start.19) | collective-permute-done | bytes 96 | tf_op jit(solution)/shard_map/ppermute | solution.py:31
  (50 shorter events, 10.9 us)
Async XLA Ops:
  1.7 9.8 %copy-start.6 = (s32[16]{0:T(128)S(1)}, s32[16]{0:T(128)}, u32[]{:S(2)}) copy-start(s32[16]{0:T(128)} %ids_ref.1) | copy-start | bytes 196
  1.8 2.1 %collective-permute-start = (bf16[16,18432]{1,0:T(8,128)(2,1)S(1)}, bf16[16,18432]{1,0:T(8,128)(2,1)S(1)}, u32[]{:S(2)}, u32[]{:S(2)}) collective-permute-start(bf16[16,18432]{1,0:T(8,128)(2,1)S(1)} %get-tuple-element.16), channel_id=1, source_target_pairs={{0,1},{1,0},{2,3},{3,2},{4,5},{5,4},{6,7},{7,6},{8,9},{9,8},{10,11... | collective-permute-start | bytes 1769480 | tf_op jit(solution)/shard_map/ppermute | solution.py:31
  4.1 11.0 %collective-permute-start.1 = (bf16[16,10240]{1,0:T(8,128)(2,1)S(1)}, bf16[16,10240]{1,0:T(8,128)(2,1)S(1)}, u32[]{:S(2)}, u32[]{:S(2)}) collective-permute-start(bf16[16,10240]{1,0:T(8,128)(2,1)S(1)} %get-tuple-element.17._), channel_id=1, source_target_pairs={{0,2},{1,3},{2,0},{3,1},{4,6},{5,7},{6,4},{7,5},{8,10},{9,11},{10,... | collective-permute-start | bytes 983048 | tf_op jit(solution)/shard_map/ppermute | solution.py:31
  7.1 11.2 %collective-permute-start.6 = (bf16[16,4096]{1,0:T(8,128)(2,1)S(1)}, bf16[16,4096]{1,0:T(8,128)(2,1)S(1)}, u32[]{:S(2)}, u32[]{:S(2)}) collective-permute-start(bf16[16,4096]{1,0:T(8,128)(2,1)S(1)} %copy-done.4), channel_id=1, source_target_pairs={{0,8},{1,9},{2,10},{3,11},{4,12},{5,13},{6,14},{7,15},{8,0},{9,1},... | collective-permute-start | bytes 393224 | tf_op jit(solution)/shard_map/ppermute | solution.py:31
  9.7 8.6 %collective-permute-start.5 = (bf16[16,4096]{1,0:T(8,128)(2,1)S(1)}, bf16[16,4096]{1,0:T(8,128)(2,1)S(1)}, u32[]{:S(2)}, u32[]{:S(2)}) collective-permute-start(bf16[16,4096]{1,0:T(8,128)(2,1)S(1)} %copy-done.4), channel_id=1, source_target_pairs={{0,4},{1,5},{2,6},{3,7},{4,0},{5,1},{6,2},{7,3},{8,12},{9,13},{10,... | collective-permute-start | bytes 393224 | tf_op jit(solution)/shard_map/ppermute | solution.py:31
  11.2 8.8 %collective-permute-start.7 = (bf16[16,4096]{1,0:T(8,128)(2,1)S(1)}, bf16[16,4096]{1,0:T(8,128)(2,1)S(1)}, u32[]{:S(2)}, u32[]{:S(2)}) collective-permute-start(bf16[16,4096]{1,0:T(8,128)(2,1)S(1)} %copy-done.4), channel_id=1, source_target_pairs={{0,12},{1,13},{2,14},{3,15},{4,8},{5,9},{6,10},{7,11},{8,4},{9,5},... | collective-permute-start | bytes 393224 | tf_op jit(solution)/shard_map/ppermute | solution.py:31
  11.5 21.4 %copy-start = (bf16[512,4096]{1,0:T(8,128)(2,1)S(1)}, bf16[512,4096]{1,0:T(8,128)(2,1)}, u32[]{:S(2)}) copy-start(bf16[512,4096]{1,0:T(8,128)(2,1)} %refs_2_.3) | copy-start | bytes 12582916
  20.0 12.8 %collective-permute-start.8 = (bf16[64,4096]{1,0:T(8,128)(2,1)S(1)}, bf16[64,4096]{1,0:T(8,128)(2,1)S(1)}, u32[]{:S(2)}, u32[]{:S(2)}) collective-permute-start(bf16[64,4096]{1,0:T(8,128)(2,1)S(1)} %shard_map.87.refs_0_), channel_id=1, source_target_pairs={{0,2},{1,3},{2,0},{3,1},{4,6},{5,7},{6,4},{7,5},{8,10},{9,11},{10,... | collective-permute-start | bytes 1572872 | tf_op jit(solution)/shard_map/ppermute | solution.py:31
  20.6 12.3 %collective-permute-start.9 = (bf16[64,4096]{1,0:T(8,128)(2,1)S(1)}, bf16[64,4096]{1,0:T(8,128)(2,1)S(1)}, u32[]{:S(2)}, u32[]{:S(2)}) collective-permute-start(bf16[64,4096]{1,0:T(8,128)(2,1)S(1)} %shard_map.87.refs_0_), channel_id=1, source_target_pairs={{0,1},{1,0},{2,3},{3,2},{4,5},{5,4},{6,7},{7,6},{8,9},{9,8},{10,11... | collective-permute-start | bytes 1572872 | tf_op jit(solution)/shard_map/ppermute | solution.py:31
  20.6 13.1 %collective-permute-start.2 = (bf16[16,4096]{1,0:T(8,128)(2,1)S(1)}, bf16[16,4096]{1,0:T(8,128)(2,1)S(1)}, u32[]{:S(2)}, u32[]{:S(2)}) collective-permute-start(bf16[16,4096]{1,0:T(8,128)(2,1)S(1)} %get-tuple-element.20), channel_id=1, source_target_pairs={{0,4},{1,5},{2,6},{3,7},{4,0},{5,1},{6,2},{7,3},{8,12},{9,13},{10,... | collective-permute-start | bytes 393224 | tf_op jit(solution)/shard_map/ppermute | solution.py:31
  22.9 10.8 %collective-permute-start.3 = (bf16[16,4096]{1,0:T(8,128)(2,1)S(1)}, bf16[16,4096]{1,0:T(8,128)(2,1)S(1)}, u32[]{:S(2)}, u32[]{:S(2)}) collective-permute-start(bf16[16,4096]{1,0:T(8,128)(2,1)S(1)} %get-tuple-element.21), channel_id=1, source_target_pairs={{0,8},{1,9},{2,10},{3,11},{4,12},{5,13},{6,14},{7,15},{8,0},{9,1},... | collective-permute-start | bytes 393224 | tf_op jit(solution)/shard_map/ppermute | solution.py:31
  24.9 11.1 %collective-permute-start.4 = (bf16[16,4096]{1,0:T(8,128)(2,1)S(1)}, bf16[16,4096]{1,0:T(8,128)(2,1)S(1)}, u32[]{:S(2)}, u32[]{:S(2)}) collective-permute-start(bf16[16,4096]{1,0:T(8,128)(2,1)S(1)} %get-tuple-element.22), channel_id=1, source_target_pairs={{0,12},{1,13},{2,14},{3,15},{4,8},{5,9},{6,10},{7,11},{8,4},{9,5},... | collective-permute-start | bytes 393224 | tf_op jit(solution)/shard_map/ppermute | solution.py:31
  32.9 14.4 %collective-permute-start.10 = (bf16[64,4096]{1,0:T(8,128)(2,1)S(1)}, bf16[64,4096]{1,0:T(8,128)(2,1)S(1)}, u32[]{:S(2)}, u32[]{:S(2)}) collective-permute-start(bf16[64,4096]{1,0:T(8,128)(2,1)S(1)} %collective-permute-done.8.refs_4_.refs_0_), channel_id=1, source_target_pairs={{0,1},{1,0},{2,3},{3,2},{4,5},{5,4},{6,7},{7,6},{8,9},{9,8},{10,11... | collective-permute-start | bytes 1572872 | tf_op jit(solution)/shard_map/ppermute | solution.py:31
  36.0 37.7 %all-to-all-start = ((bf16[16,16,2176]{2,1,0:T(8,128)(2,1)}), bf16[16,16,2176]{2,1,0:T(8,128)(2,1)S(1)}, u32[]{:S(2)}, u32[]{:S(2)}) async-start(bf16[16,16,2176]{2,1,0:T(8,128)(2,1)} %shard_map.90), calls=%async_computation | async-start | bytes 2228224 | tf_op jit(solution)/shard_map/all_to_all | solution.py:417
  42.9 4.4 %collective-permute-start.13 = (bf16[16,2048]{1,0:T(8,128)(2,1)S(1)}, bf16[16,2048]{1,0:T(8,128)(2,1)S(1)}, u32[]{:S(2)}, u32[]{:S(2)}) collective-permute-start(bf16[16,2048]{1,0:T(8,128)(2,1)S(1)} %get-tuple-element.23.__1_.refs_2_), channel_id=1, source_target_pairs={{0,16},{16,0},{1,17},{17,1},{2,18},{18,2},{3,19},{19,3},{4,20},{20... | collective-permute-start | bytes 196616 | tf_op jit(solution)/shard_map/ppermute | solution.py:31
  44.4 6.1 %collective-permute-start.12 = (bf16[16,2048]{1,0:T(8,128)(2,1)S(1)}, bf16[16,2048]{1,0:T(8,128)(2,1)S(1)}, u32[]{:S(2)}, u32[]{:S(2)}) collective-permute-start(bf16[16,2048]{1,0:T(8,128)(2,1)S(1)} %get-tuple-element.23.__1_.refs_2_), channel_id=1, source_target_pairs={{0,1},{1,0},{2,3},{3,2},{4,5},{5,4},{6,7},{7,6},{8,9},{9,8},{10,11... | collective-permute-start | bytes 196616 | tf_op jit(solution)/shard_map/ppermute | solution.py:31
  44.5 6.1 %collective-permute-start.11 = (bf16[16,2048]{1,0:T(8,128)(2,1)S(1)}, bf16[16,2048]{1,0:T(8,128)(2,1)S(1)}, u32[]{:S(2)}, u32[]{:S(2)}) collective-permute-start(bf16[16,2048]{1,0:T(8,128)(2,1)S(1)} %get-tuple-element.24.refs_0_), channel_id=1, source_target_pairs={{0,16},{16,0},{1,17},{17,1},{2,18},{18,2},{3,19},{19,3},{4,20},{20... | collective-permute-start | bytes 196616 | tf_op jit(solution)/shard_map/ppermute | solution.py:31
  47.3 3.3 %collective-permute-start.14 = (bf16[16,2048]{1,0:T(8,128)(2,1)S(1)}, bf16[16,2048]{1,0:T(8,128)(2,1)S(1)}, u32[]{:S(2)}, u32[]{:S(2)}) collective-permute-start(bf16[16,2048]{1,0:T(8,128)(2,1)S(1)} %collective-permute-done.13.refs_4_), channel_id=1, source_target_pairs={{0,1},{1,0},{2,3},{3,2},{4,5},{5,4},{6,7},{7,6},{8,9},{9,8},{10,11... | collective-permute-start | bytes 196616 | tf_op jit(solution)/shard_map/ppermute | solution.py:31
  80.0 3.5 %collective-permute-start.17 = (f32[2,8,1]{2,1,0:T(8,128)}, f32[2,8,1]{2,1,0:T(8,128)S(1)}, u32[]{:S(2)}, u32[]{:S(2)}) collective-permute-start(f32[2,8,1]{2,1,0:T(8,128)} %shard_map.93), channel_id=1, source_target_pairs={{0,3},{1,2},{2,1},{3,0},{4,7},{5,6},{6,5},{7,4},{8,11},{9,10},{10,... | collective-permute-start | bytes 200 | tf_op jit(solution)/shard_map/ppermute | solution.py:31
  81.9 3.9 %collective-permute-start.16 = (f32[2,8,1]{2,1,0:T(8,128)}, f32[2,8,1]{2,1,0:T(8,128)S(1)}, u32[]{:S(2)}, u32[]{:S(2)}) collective-permute-start(f32[2,8,1]{2,1,0:T(8,128)} %shard_map.93), channel_id=1, source_target_pairs={{0,2},{1,3},{2,0},{3,1},{4,6},{5,7},{6,4},{7,5},{8,10},{9,11},{10,... | collective-permute-start | bytes 200 | tf_op jit(solution)/shard_map/ppermute | solution.py:31
  82.2 3.6 %collective-permute-start.15 = (f32[2,8,1]{2,1,0:T(8,128)}, f32[2,8,1]{2,1,0:T(8,128)S(1)}, u32[]{:S(2)}, u32[]{:S(2)}) collective-permute-start(f32[2,8,1]{2,1,0:T(8,128)} %shard_map.93), channel_id=1, source_target_pairs={{0,1},{1,0},{2,3},{3,2},{4,5},{5,4},{6,7},{7,6},{8,9},{9,8},{10,11... | collective-permute-start | bytes 200 | tf_op jit(solution)/shard_map/ppermute | solution.py:31
  86.5 5.5 %collective-permute-start.20 = (f32[2,8,1]{2,1,0:T(8,128)S(1)}, f32[2,8,1]{2,1,0:T(8,128)S(1)}, u32[]{:S(2)}, u32[]{:S(2)}) collective-permute-start(f32[2,8,1]{2,1,0:T(8,128)S(1)} %add_add_fusion), channel_id=1, source_target_pairs={{0,12},{1,13},{2,14},{3,15},{4,8},{5,9},{6,10},{7,11},{8,4},{9,5},... | collective-permute-start | bytes 200 | tf_op jit(solution)/shard_map/ppermute | solution.py:31
  89.8 4.5 %collective-permute-start.19 = (f32[2,8,1]{2,1,0:T(8,128)S(1)}, f32[2,8,1]{2,1,0:T(8,128)S(1)}, u32[]{:S(2)}, u32[]{:S(2)}) collective-permute-start(f32[2,8,1]{2,1,0:T(8,128)S(1)} %add_add_fusion), channel_id=1, source_target_pairs={{0,8},{1,9},{2,10},{3,11},{4,12},{5,13},{6,14},{7,15},{8,0},{9,1},... | collective-permute-start | bytes 200 | tf_op jit(solution)/shard_map/ppermute | solution.py:31
  89.8 4.5 %collective-permute-start.18 = (f32[2,8,1]{2,1,0:T(8,128)S(1)}, f32[2,8,1]{2,1,0:T(8,128)S(1)}, u32[]{:S(2)}, u32[]{:S(2)}) collective-permute-start(f32[2,8,1]{2,1,0:T(8,128)S(1)} %add_add_fusion), channel_id=1, source_target_pairs={{0,4},{1,5},{2,6},{3,7},{4,0},{5,1},{6,2},{7,3},{8,12},{9,13},{10,... | collective-permute-start | bytes 200 | tf_op jit(solution)/shard_map/ppermute | solution.py:31
  (6 other events, 20.7 us)

commit v13 on v12

--- a/solution.py
+++ b/solution.py
@@ -175,29 +175,86 @@
     )(array, *after)
 
 
-def cut_grads_kernel(ids_ref, grad_ref, _, out_ref):
-    count, rows, width = out_ref.shape
-    cols = width - LANES
+def grads_core_kernel(ids_ref, grad_ref, _, out_ref):
+    rows, hidden = grad_ref.shape
+    wide = lax.axis_size("wide")
+    cols = hidden // wide
+    me = lax.axis_index("wide")
     row = lax.broadcasted_iota(jnp.int32, (rows, LANES), 0)
     ids = jnp.zeros((rows, LANES), jnp.int32)
     for t in range(rows):
         ids = jnp.where(row == t, ids_ref[t], ids)
-    ids = ids.astype(jnp.float32).astype(out_ref.dtype)
-    for to in range(count):
-        out_ref[to, :, :cols] = grad_ref[:, to * cols:(to + 1) * cols]
-        out_ref[to, :, cols:] = ids
-
-
-def cut_grads(ids, grads, after, count):
+    out_ref[:, wide // 2 * cols:] = ids.astype(jnp.float32).astype(out_ref.dtype)
+    for q in range(wide // 2):
+        src = pl.multiple_of((me ^ (2 * q + 1)) * cols, cols)
+        out_ref[:, q * cols:(q + 1) * cols] = grad_ref[:, pl.ds(src, cols)]
+
+
+def grads_core(ids, grads, after):
     rows, hidden = grads.shape
     return pl.pallas_call(
-        cut_grads_kernel,
+        grads_core_kernel,
         in_specs=in_smem(1) + in_vmem(1) + in_place(1),
         out_specs=in_vmem(1)[0],
-        out_shape=jax.ShapeDtypeStruct((count, rows, hidden // count + LANES), grads.dtype),
+        out_shape=jax.ShapeDtypeStruct((rows, hidden // 2 + LANES), grads.dtype),
         compiler_params=params(16),
         cost_estimate=pl.CostEstimate(flops=0, bytes_accessed=1, transcendentals=0),
     )(ids, grads, after)
+
+
+def grads_y_kernel(grad_ref, sent_ref, got_ref, _, out_ref):
+    rows, hidden = grad_ref.shape
+    wide = lax.axis_size("wide")
+    cols = hidden // wide
+    me = lax.axis_index("wide")
+    for k in range(wide // 4):
+        src = pl.multiple_of((me ^ (4 * k + 2)) * cols, cols)
+        place = slice(k * cols, (k + 1) * cols)
+        out_ref[:rows, place] = grad_ref[:, pl.ds(src, cols)]
+        out_ref[rows:, place] = got_ref[:, (2 * k + 1) * cols:(2 * k + 2) * cols]
+    ids = slice(wide // 4 * cols, wide // 4 * cols + LANES)
+    out_ref[:rows, ids] = sent_ref[:, wide // 2 * cols:]
+    out_ref[rows:, ids] = got_ref[:, wide // 2 * cols:]
+
+
+def grads_y(grads, sent, got, after):
+    rows, hidden = grads.shape
+    return pl.pallas_call(
+        grads_y_kernel,
+        in_specs=in_vmem(3) + in_place(1),
+        out_specs=in_vmem(1)[0],
+        out_shape=jax.ShapeDtypeStruct((2 * rows, hidden // 4 + LANES), grads.dtype),
+        compiler_params=params(16),
+        cost_estimate=pl.CostEstimate(flops=0, bytes_accessed=1, transcendentals=0),
+    )(grads, sent, got, after)
+
+
+def grads_z_kernel(grad_ref, sent_ref, got_ref, over_ref, *out_refs):
+    rows = grad_ref.shape[0]
+    cols = out_refs[0].shape[1] - LANES
+    me = lax.axis_index("wide")
+    for k, out_ref in enumerate(out_refs):
+        src = pl.multiple_of((me ^ (4 * k)) * cols, cols)
+        out_ref[:rows, :cols] = grad_ref[:, pl.ds(src, cols)]
+        out_ref[rows:2 * rows, :cols] = got_ref[:, 2 * k * cols:(2 * k + 1) * cols]
+        out_ref[2 * rows:, :cols] = over_ref[:, k * cols:(k + 1) * cols]
+        out_ref[:rows, cols:] = sent_ref[:, 2 * len(out_refs) * cols:]
+        out_ref[rows:2 * rows, cols:] = got_ref[:, 2 * len(out_refs) * cols:]
+        out_ref[2 * rows:, cols:] = over_ref[:, len(out_refs) * cols:]
+
+
+def grads_z(grads, sent, got, over, wide_count):
+    rows, hidden = grads.shape
+    count = wide_count // 4
+    piece = jax.ShapeDtypeStruct((4 * rows, hidden // wide_count + LANES), grads.dtype)
+    return pl.pallas_call(
+        grads_z_kernel,
+        in_specs=in_vmem(4),
+        out_specs=in_vmem(count),
+        out_shape=[piece] * count,
+        compiler_params=params(16),
+        cost_estimate=pl.CostEstimate(flops=0, bytes_accessed=1, transcendentals=0),
+    )(grads, sent, got, over)
 
 
 def rotate_kernel(act_count, done, *refs):
@@ -318,7 +375,7 @@
             pltpu.VMEM((batch_count * rows, chunk), jnp.bfloat16),
             pltpu.VMEM((batch_count * rows, chunk), jnp.bfloat16),
         ],
-        compiler_params=params(50),
+        compiler_params=params(32 if tokens <= 256 else 48),
         cost_estimate=pl.CostEstimate(
             flops=2 * hidden * width * (tokens + 256) * batch_count,
             bytes_accessed=2 * hidden * width,
@@ -327,23 +384,29 @@
     )(rot, *lefts, *halves, eigenvalues)
 
 
-def score_kernel(batch_count, ranks, grad_ref, basis_ref, image_ref, ids_ref, out_ref, token_ref):
+def score_kernel(batch_count, ranks, count, *refs):
+    grad_refs, ids_refs = refs[:count], refs[count:2 * count]
+    basis_ref, image_ref, out_ref, token_ref = refs[2 * count:]
     step = pl.program_id(0)
-    me = lax.axis_index("wide")
+    rows = grad_refs[0].shape[0] // 4
+
+    def tokens_of(pieces):
+        return jnp.concatenate(
+            [pieces[r // 4][r % 4 * rows:(r % 4 + 1) * rows, :] for r in ranks], axis=0
+        )
 
     @pl.when(step == 0)
     def _():
         token_ref[...] = jnp.zeros_like(token_ref)
 
-    grads = jnp.concatenate([grad_ref[me ^ r] for r in ranks], axis=0)
-    turned = jnp.dot(grads, basis_ref[...], preferred_element_type=jnp.float32)
+    turned = jnp.dot(tokens_of(grad_refs), basis_ref[...], preferred_element_type=jnp.float32)
     turned = turned.astype(jnp.bfloat16).T.astype(jnp.float32)
     for b in range(batch_count):
         token_ref[b:b + 1, :] += jnp.sum(image_ref[b] * turned, axis=0, keepdims=True)
 
     @pl.when(step == pl.num_programs(0) - 1)
     def _():
-        ids = jnp.concatenate([ids_ref[me ^ r] for r in ranks], axis=0).astype(jnp.float32)
+        ids = tokens_of(ids_refs).astype(jnp.float32)
         seqs = lax.broadcasted_iota(jnp.int32, ids.shape, 1).astype(jnp.float32)
         member = jnp.where(ids == seqs, 1.0, 0.0).T
         own = lax.rem(lax.axis_index("groups"), batch_count)
@@ -352,30 +415,30 @@
             out_ref[lax.rem(own + b, batch_count)] = sums[:out_ref.shape[1], :]
 
 
-def score_parts(grads, ranks, grad_basis, image, seq_count):
-    batch_count, _, tokens = image.shape
-    count, rows, width = grads.shape
-    hidden = width - LANES
+def score_parts(grad_pieces, ranks, grad_basis, image, seq_count):
+    batch_count, hidden, tokens = image.shape
+    count = len(grad_pieces)
+    rows = grad_pieces[0].shape[0]
     inner = min(grad_basis.shape[0], hidden)
     return pl.pallas_call(
-        functools.partial(score_kernel, batch_count, ranks),
+        functools.partial(score_kernel, batch_count, ranks, count),
         grid=(hidden // inner,),
-        in_specs=[
-            pl.BlockSpec((count, rows, inner), lambda i: (0, 0, i)),
+        in_specs=[pl.BlockSpec((rows, inner), lambda i: (0, i))] * count
+        + [pl.BlockSpec((rows, LANES), lambda i: (0, hidden // LANES))] * count
+        + [
             pl.BlockSpec((grad_basis.shape[0], inner), lambda i: (0, i)),
             pl.BlockSpec((batch_count, inner, tokens), lambda i: (0, i, 0)),
-            pl.BlockSpec((count, rows, LANES), lambda i: (0, 0, hidden // LANES)),
         ],
         out_specs=pl.BlockSpec((batch_count, seq_count, 1), lambda i: (0, 0, 0)),
         out_shape=jax.ShapeDtypeStruct((batch_count, seq_count, 1), jnp.float32),
         scratch_shapes=[pltpu.VMEM((8, tokens), jnp.float32)],
-        compiler_params=params(56),
+        compiler_params=params(32 if tokens <= 256 else 48),
         cost_estimate=pl.CostEstimate(
             flops=2 * tokens * hidden * grad_basis.shape[0],
             bytes_accessed=4 * image.size,
             transcendentals=0,
         ),
-    )(grads, grad_basis, image, grads)
+    )(*grad_pieces, *grad_pieces, grad_basis, image)
 
 
 def per_device(
@@ -395,26 +458,29 @@
     keep, give = cut_factors(query_factors, order, hidden, batch_count)
     flags = owner_flags(owners, keep)
     keep, give = pick(flags, keep, swap(give, "wide", 1), 0, cols, half, [])
-    sent = cut_grads(seq_ids, train_grad, give, wide_count)
-    parts = pick(flags, keep, swap(give, "wide", 2), 1, cols, half, [sent])
+    grads_sent = grads_core(seq_ids, train_grad, give)
+    grads_got = swap(grads_sent, "wide", 1)
+    grads_over = grads_y(train_grad, grads_sent, grads_got, give)
+    parts = pick(flags, keep, swap(give, "wide", 2), 1, cols, half, [grads_over])
+    grads_over = swap(grads_over, "wide", 2)
+    sent = grads_z(train_grad, grads_sent, grads_got, grads_over, wide_count)
     acts = join([train_act] + [swap(train_act, "wide", 4 * k) for k in along_z if k], parts[0])
     ranks = [4 * k for k in along_z]
-    near = [(acts, ranks), (swap(acts, "wide", 1), [r + 1 for r in ranks])]
-    over = [(swap(acts, "wide", 2), [r + 2 for r in ranks])]
-    first = rotate([x for x, _ in near], act_basis, parts[0])
+    over = swap(acts, "wide", 2)
+    first = rotate([acts], act_basis, parts[0])
     parts = [swap(parts[k], "wide", 4 * k) if k else parts[0] for k in along_z]
-    left, right = pick_one(flags, parts, cols, [over[0][0], first])
+    left, right = pick_one(flags, parts, cols, [over, first, sent[0]])
 
     lefts = [left, swap(left, "groups", 1)]
     other = swap(right, "groups", 1)
     halves = []
     for x in (right, other):
         halves += [x, swap(x, "wide", 1)]
-    over += [(swap(x, "wide", 1), [r + 1 for r in has]) for x, has in over]
-    rot = rotate([x for x, _ in over], act_basis, None, first)
-    ranks = [r for _, has in near + over for r in has]
-
-    grads = lax.all_to_all(gate(sent, [right]), "wide", 0, 0)
+    over = gate(over, [right])
+    rot = rotate([over, swap(gate(acts, [right]), "wide", 1), swap(over, "wide", 1)], act_basis, None, first)
+    ranks = [r + more for more in (0, 2, 1, 3) for r in ranks]
+
+    grads = [swap(sent[k], "wide", 4 * k) if k else sent[0] for k in along_z]
 
     image = images(rot, lefts, halves, eigenvalues)
     parts = score_parts(grads, ranks, grad_basis, image, seq_count)

time: 95.3 us -> 90.1 us (0.945)
  Pallas kernels: 33 us -> 29.8 us
  waiting for transfers between devices: 25.9 us -> 27.6 us
  local copies, waits for them, and re-layouts: 4.94 us -> 3.37 us
  starting transfers between devices: 29.6 us -> 28.2 us
    all_to_all x1 -> x0, starting transfers between devices: 6.8 us -> none  [per_device(): grads = lax.all_to_all(gate(sent, [right]), 'wide', 0, 0)]
    ppermute x21 -> x26, starting transfers between devices: 22.8 us -> 28.2 us  [swap(): return lax.ppermute(x, axis, [(i, i ^ bit) for i in range(count)])]
    pallas_call x2 -> x4, Pallas kernels: 6.93 us -> 3.68 us  [the longest x1 2.98 us: score_parts(): pl.pallas_call(functools.partial(score_kernel, batch_count, ranks, count)...]
    ppermute x21 -> x26, waiting for transfers between devices: 25.9 us -> 27.6 us  [swap(): return lax.ppermute(x, axis, [(i, i ^ bit) for i in range(count)])]
    unnamed x16 -> x14, local copies, waits for them, and re-layouts: 4.94 us -> 3.37 us
  transfers between devices with their start and end apart: 22 -> 26, of which waited for: 11 -> 12; matrix products, arithmetic and copies ran while one was open for 0% -> 0% of each run, Pallas kernels for 29% -> 29%
where the time goes in v13:
time: 90.1 us; the launch traced here: 89.9 us
  Pallas kernels  29.8 us (33%)
  starting transfers between devices  28.2 us (31%)
  waiting for transfers between devices  27.6 us (31%)
  local copies, waits for them, and re-layouts  3.37 us (4%)
    ppermute x26, starting transfers between devices, swap(): return lax.ppermute(x, axis, [(i, i ^ bit) for i in range(count)])  28.2 us
    ppermute x26, waiting for transfers between devices, swap(): return lax.ppermute(x, axis, [(i, i ^ bit) for i in range(count)])  27.6 us
    pallas_call x1, Pallas kernels, images(): pl.pallas_call(functools.partial(image_kernel, batch_count, total, per),...  22.4 us
    unnamed x14, local copies, waits for them, and re-layouts  3.37 us
    pallas_call x1, Pallas kernels, score_parts(): pl.pallas_call(functools.partial(score_kernel, batch_count, ranks, count)...  2.98 us
    pallas_call x2, Pallas kernels, rotate(): pl.pallas_call(functools.partial(rotate_kernel, len(act_pieces), done), i...  2.62 us
  transfers between devices with their start and end apart: 26, of which 12 were waited for; matrix products, arithmetic and copies ran while one was open for 0% of the time, Pallas kernels for 29%

profile of v13, /device:TPU:0, one launch (start us, length us, event | category | flops | bytes accessed | tf_op | source)
XLA Modules:
  0.0 89.9 jit_solution(363338179202073106)
XLA Ops:
  0.0 1.8 %copy-done.2 = bf16[2,16,36864]{2,1,0:T(8,128)(2,1)S(1)} copy-done((bf16[2,16,36864]{2,1,0:T(8,128)(2,1)S(1)}, bf16[2,16,36864]{2,1,0:T(8,128)(2,1)}, u32[]{:S(2)}) %copy-start.2) | copy-done | bytes 2359320
  6.2 2.6 %collective-permute-start.9 = (bf16[16,10240]{1,0:T(8,128)(2,1)S(1)}, bf16[16,10240]{1,0:T(8,128)(2,1)S(1)}, u32[]{:S(2)}, u32[]{:S(2)}) collective-permute-start(bf16[16,10240]{1,0:T(8,128)(2,1)S(1)} %get-tuple-element.21._), channel_id=1, source_target_pairs={{0,2},{1,3},{2,0},{3,1},{4,6},{5,7},{6,4},{7,5},{8,10},{9,11},{10,... | collective-permute-start | bytes 983048 | tf_op jit(solution)/shard_map/ppermute | solution.py:31
  8.8 2.6 %collective-permute-start.7 = (bf16[16,4096]{1,0:T(8,128)(2,1)S(1)}, bf16[16,4096]{1,0:T(8,128)(2,1)S(1)}, u32[]{:S(2)}, u32[]{:S(2)}) collective-permute-start(bf16[16,4096]{1,0:T(8,128)(2,1)S(1)} %copy-done.4), channel_id=1, source_target_pairs={{0,8},{1,9},{2,10},{3,11},{4,12},{5,13},{6,14},{7,15},{8,0},{9,1},... | collective-permute-start | bytes 393224 | tf_op jit(solution)/shard_map/ppermute | solution.py:31
  11.4 1.6 %collective-permute-start.6 = (bf16[16,4096]{1,0:T(8,128)(2,1)S(1)}, bf16[16,4096]{1,0:T(8,128)(2,1)S(1)}, u32[]{:S(2)}, u32[]{:S(2)}) collective-permute-start(bf16[16,4096]{1,0:T(8,128)(2,1)S(1)} %copy-done.4), channel_id=1, source_target_pairs={{0,4},{1,5},{2,6},{3,7},{4,0},{5,1},{6,2},{7,3},{8,12},{9,13},{10,... | collective-permute-start | bytes 393224 | tf_op jit(solution)/shard_map/ppermute | solution.py:31
  13.6 3.8 %collective-permute-done.9.got_ref = bf16[16,10240]{1,0:T(8,128)(2,1)S(1)} collective-permute-done((bf16[16,10240]{1,0:T(8,128)(2,1)S(1)}, bf16[16,10240]{1,0:T(8,128)(2,1)S(1)}, u32[]{:S(2)}, u32[]{:S(2)}) %collective-permute-start.9) | collective-permute-done | bytes 327712 | tf_op jit(solution)/shard_map/ppermute | solution.py:31
  17.5 1.9 %collective-permute-done.7.refs_2_ = bf16[16,4096]{1,0:T(8,128)(2,1)S(1)} collective-permute-done((bf16[16,4096]{1,0:T(8,128)(2,1)S(1)}, bf16[16,4096]{1,0:T(8,128)(2,1)S(1)}, u32[]{:S(2)}, u32[]{:S(2)}) %collective-permute-start.7) | collective-permute-done | bytes 131104 | tf_op jit(solution)/shard_map/ppermute | solution.py:31
  19.4 2.7 %collective-permute-done.8.refs_3_ = bf16[16,4096]{1,0:T(8,128)(2,1)S(1)} collective-permute-done((bf16[16,4096]{1,0:T(8,128)(2,1)S(1)}, bf16[16,4096]{1,0:T(8,128)(2,1)S(1)}, u32[]{:S(2)}, u32[]{:S(2)}) %collective-permute-start.8) | collective-permute-done | bytes 131104 | tf_op jit(solution)/shard_map/ppermute | solution.py:31
  22.7 2.3 %collective-permute-start.11 = (bf16[16,4096]{1,0:T(8,128)(2,1)S(1)}, bf16[16,4096]{1,0:T(8,128)(2,1)S(1)}, u32[]{:S(2)}, u32[]{:S(2)}) collective-permute-start(bf16[16,4096]{1,0:T(8,128)(2,1)S(1)} %get-tuple-element.28), channel_id=1, source_target_pairs={{0,4},{1,5},{2,6},{3,7},{4,0},{5,1},{6,2},{7,3},{8,12},{9,13},{10,... | collective-permute-start | bytes 393224 | tf_op jit(solution)/shard_map/ppermute | solution.py:31
  25.0 1.9 %collective-permute-start.12 = (bf16[16,4096]{1,0:T(8,128)(2,1)S(1)}, bf16[16,4096]{1,0:T(8,128)(2,1)S(1)}, u32[]{:S(2)}, u32[]{:S(2)}) collective-permute-start(bf16[16,4096]{1,0:T(8,128)(2,1)S(1)} %get-tuple-element.29), channel_id=1, source_target_pairs={{0,8},{1,9},{2,10},{3,11},{4,12},{5,13},{6,14},{7,15},{8,0},{9,1},... | collective-permute-start | bytes 393224 | tf_op jit(solution)/shard_map/ppermute | solution.py:31
  26.9 1.5 %collective-permute-start.13 = (bf16[16,4096]{1,0:T(8,128)(2,1)S(1)}, bf16[16,4096]{1,0:T(8,128)(2,1)S(1)}, u32[]{:S(2)}, u32[]{:S(2)}) collective-permute-start(bf16[16,4096]{1,0:T(8,128)(2,1)S(1)} %get-tuple-element.30), channel_id=1, source_target_pairs={{0,12},{1,13},{2,14},{3,15},{4,8},{5,9},{6,10},{7,11},{8,4},{9,5},... | collective-permute-start | bytes 393224 | tf_op jit(solution)/shard_map/ppermute | solution.py:31
  30.6 6.6 %collective-permute-done.12.refs_2_ = bf16[16,4096]{1,0:T(8,128)(2,1)S(1)} collective-permute-done((bf16[16,4096]{1,0:T(8,128)(2,1)S(1)}, bf16[16,4096]{1,0:T(8,128)(2,1)S(1)}, u32[]{:S(2)}, u32[]{:S(2)}) %collective-permute-start.12) | collective-permute-done | bytes 131104 | tf_op jit(solution)/shard_map/ppermute | solution.py:31
  37.2 2.5 %collective-permute-done.10.refs_4_.__0_ = bf16[64,4096]{1,0:T(8,128)(2,1)S(1)} collective-permute-done((bf16[64,4096]{1,0:T(8,128)(2,1)S(1)}, bf16[64,4096]{1,0:T(8,128)(2,1)S(1)}, u32[]{:S(2)}, u32[]{:S(2)}) %collective-permute-start.10) | collective-permute-done | bytes 524320 | tf_op jit(solution)/shard_map/ppermute | solution.py:31
  40.4 1.7 %collective-permute-start.18 = (bf16[16,2048]{1,0:T(8,128)(2,1)S(1)}, bf16[16,2048]{1,0:T(8,128)(2,1)S(1)}, u32[]{:S(2)}, u32[]{:S(2)}) collective-permute-start(bf16[16,2048]{1,0:T(8,128)(2,1)S(1)} %get-tuple-element.31.__1_.refs_2_), channel_id=1, source_target_pairs={{0,16},{16,0},{1,17},{17,1},{2,18},{18,2},{3,19},{19,3},{4,20},{20... | collective-permute-start | bytes 196616 | tf_op jit(solution)/shard_map/ppermute | solution.py:31
  42.5 2.4 %collective-permute-done.18.refs_4_ = bf16[16,2048]{1,0:T(8,128)(2,1)S(1)} collective-permute-done((bf16[16,2048]{1,0:T(8,128)(2,1)S(1)}, bf16[16,2048]{1,0:T(8,128)(2,1)S(1)}, u32[]{:S(2)}, u32[]{:S(2)}) %collective-permute-start.18) | collective-permute-done | bytes 65568 | tf_op jit(solution)/shard_map/ppermute | solution.py:31
  44.9 2.0 %collective-permute-start.3 = (bf16[64,2176]{1,0:T(8,128)(2,1)S(1)}, bf16[64,2176]{1,0:T(8,128)(2,1)S(1)}, u32[]{:S(2)}, u32[]{:S(2)}) collective-permute-start(bf16[64,2176]{1,0:T(8,128)(2,1)S(1)} %get-tuple-element.23), channel_id=1, source_target_pairs={{0,4},{1,5},{2,6},{3,7},{4,0},{5,1},{6,2},{7,3},{8,12},{9,13},{10,... | collective-permute-start | bytes 835592 | tf_op jit(solution)/shard_map/ppermute | solution.py:31
  46.9 2.6 %collective-permute-start.4 = (bf16[64,2176]{1,0:T(8,128)(2,1)S(1)}, bf16[64,2176]{1,0:T(8,128)(2,1)S(1)}, u32[]{:S(2)}, u32[]{:S(2)}) collective-permute-start(bf16[64,2176]{1,0:T(8,128)(2,1)S(1)} %get-tuple-element.24), channel_id=1, source_target_pairs={{0,8},{1,9},{2,10},{3,11},{4,12},{5,13},{6,14},{7,15},{8,0},{9,1},... | collective-permute-start | bytes 835592 | tf_op jit(solution)/shard_map/ppermute | solution.py:31
  49.5 1.7 %shard_map.94.rot_ref = bf16[4096,256]{1,0:T(8,128)(2,1)S(1)} custom-call(bf16[64,4096]{1,0:T(8,128)(2,1)S(1)} %shard_map.92.refs_0_, bf16[64,4096]{1,0:T(8,128)(2,1)S(1)} %collective-permute-done.14.refs_1_, bf16[64,4096]{1,0:T(8,128)(2,1)S(1)} %collective-permute-done.15.refs_2_, bf16[512,4096]{1,0:T(8,128)(2,1)S(1)} %copy-done, ...), custom_call_target="tpu_custom_call" | custom-call | bytes 1 | tf_op jit(solution)/shard_map/pallas_call | solution.py:277
  51.3 22.4 %shard_map.95.refs_9_ = f32[2,2048,256]{2,1,0:T(8,128)S(1)} custom-call(bf16[4096,256]{1,0:T(8,128)(2,1)S(1)} %shard_map.94.rot_ref, bf16[16,2048]{1,0:T(8,128)(2,1)S(1)} %get-tuple-element.32.refs_0_, bf16[16,2048]{1,0:T(8,128)(2,1)S(1)} %collective-permute-done.16.refs_1_, bf16[16,2048]{1,0:T(8,128)(2,1)S(1)} %get-tuple-element.31.__1_.refs_2_, ...), custom_call_target="tpu_custom_call" | custom-call | flops 17179869184 | bytes 16777216 | tf_op jit(solution)/shard_map/pallas_call | solution.py:363
  73.8 3.0 %shard_map.96 = f32[2,8,1]{2,1,0:T(8,128)S(1)} custom-call(bf16[64,2176]{1,0:T(8,128)(2,1)S(1)} %get-tuple-element.22.refs_6_.refs_0_.refs_4_, bf16[64,2176]{1,0:T(8,128)(2,1)S(1)} %collective-permute-done.3.refs_1_.refs_5_, bf16[64,2176]{1,0:T(8,128)(2,1)S(1)} %collective-permute-done.4.refs_2_.refs_6_, ...), custom_call_target="tpu_custom_call" | custom-call | flops 536870912 | bytes 4194304 | tf_op jit(solution)/shard_map/pallas_call | solution.py:423
  78.6 1.2 %collective-permute-done.22 = f32[2,8,1]{2,1,0:T(8,128)S(1)} collective-permute-done((f32[2,8,1]{2,1,0:T(8,128)S(1)}, f32[2,8,1]{2,1,0:T(8,128)S(1)}, u32[]{:S(2)}, u32[]{:S(2)}) %collective-permute-start.22) | collective-permute-done | bytes 96 | tf_op jit(solution)/shard_map/ppermute | solution.py:31
  79.8 1.7 %collective-permute-done.21 = f32[2,8,1]{2,1,0:T(8,128)S(1)} collective-permute-done((f32[2,8,1]{2,1,0:T(8,128)S(1)}, f32[2,8,1]{2,1,0:T(8,128)S(1)}, u32[]{:S(2)}, u32[]{:S(2)}) %collective-permute-start.21) | collective-permute-done | bytes 96 | tf_op jit(solution)/shard_map/ppermute | solution.py:31
  81.5 3.2 %collective-permute-start.25 = (f32[2,8,1]{2,1,0:T(8,128)S(1)}, f32[2,8,1]{2,1,0:T(8,128)S(1)}, u32[]{:S(2)}, u32[]{:S(2)}) collective-permute-start(f32[2,8,1]{2,1,0:T(8,128)S(1)} %add_add_fusion), channel_id=1, source_target_pairs={{0,12},{1,13},{2,14},{3,15},{4,8},{5,9},{6,10},{7,11},{8,4},{9,5},... | collective-permute-start | bytes 200 | tf_op jit(solution)/shard_map/ppermute | solution.py:31
  84.7 1.2 %collective-permute-start.23 = (f32[2,8,1]{2,1,0:T(8,128)S(1)}, f32[2,8,1]{2,1,0:T(8,128)S(1)}, u32[]{:S(2)}, u32[]{:S(2)}) collective-permute-start(f32[2,8,1]{2,1,0:T(8,128)S(1)} %add_add_fusion), channel_id=1, source_target_pairs={{0,4},{1,5},{2,6},{3,7},{4,0},{5,1},{6,2},{7,3},{8,12},{9,13},{10,... | collective-permute-start | bytes 200 | tf_op jit(solution)/shard_map/ppermute | solution.py:31
  87.0 2.2 %collective-permute-done.24 = f32[2,8,1]{2,1,0:T(8,128)S(1)} collective-permute-done((f32[2,8,1]{2,1,0:T(8,128)S(1)}, f32[2,8,1]{2,1,0:T(8,128)S(1)}, u32[]{:S(2)}, u32[]{:S(2)}) %collective-permute-start.24) | collective-permute-done | bytes 96 | tf_op jit(solution)/shard_map/ppermute | solution.py:31
  (59 shorter events, 12.7 us)
Async XLA Ops:
  5.7 7.5 %collective-permute-start.1 = (bf16[16,16512]{1,0:T(8,128)(2,1)S(1)}, bf16[16,16512]{1,0:T(8,128)(2,1)S(1)}, u32[]{:S(2)}, u32[]{:S(2)}) collective-permute-start(bf16[16,16512]{1,0:T(8,128)(2,1)S(1)} %shard_map.85.sent_ref), channel_id=1, source_target_pairs={{0,1},{1,0},{2,3},{3,2},{4,5},{5,4},{6,7},{7,6},{8,9},{9,8},{10,11... | collective-permute-start | bytes 1585160 | tf_op jit(solution)/shard_map/ppermute | solution.py:31
  6.2 11.1 %collective-permute-start.9 = (bf16[16,10240]{1,0:T(8,128)(2,1)S(1)}, bf16[16,10240]{1,0:T(8,128)(2,1)S(1)}, u32[]{:S(2)}, u32[]{:S(2)}) collective-permute-start(bf16[16,10240]{1,0:T(8,128)(2,1)S(1)} %get-tuple-element.21._), channel_id=1, source_target_pairs={{0,2},{1,3},{2,0},{3,1},{4,6},{5,7},{6,4},{7,5},{8,10},{9,11},{10,... | collective-permute-start | bytes 983048 | tf_op jit(solution)/shard_map/ppermute | solution.py:31
  8.8 10.6 %collective-permute-start.7 = (bf16[16,4096]{1,0:T(8,128)(2,1)S(1)}, bf16[16,4096]{1,0:T(8,128)(2,1)S(1)}, u32[]{:S(2)}, u32[]{:S(2)}) collective-permute-start(bf16[16,4096]{1,0:T(8,128)(2,1)S(1)} %copy-done.4), channel_id=1, source_target_pairs={{0,8},{1,9},{2,10},{3,11},{4,12},{5,13},{6,14},{7,15},{8,0},{9,1},... | collective-permute-start | bytes 393224 | tf_op jit(solution)/shard_map/ppermute | solution.py:31
  11.4 8.0 %collective-permute-start.6 = (bf16[16,4096]{1,0:T(8,128)(2,1)S(1)}, bf16[16,4096]{1,0:T(8,128)(2,1)S(1)}, u32[]{:S(2)}, u32[]{:S(2)}) collective-permute-start(bf16[16,4096]{1,0:T(8,128)(2,1)S(1)} %copy-done.4), channel_id=1, source_target_pairs={{0,4},{1,5},{2,6},{3,7},{4,0},{5,1},{6,2},{7,3},{8,12},{9,13},{10,... | collective-permute-start | bytes 393224 | tf_op jit(solution)/shard_map/ppermute | solution.py:31
  13.0 9.1 %collective-permute-start.8 = (bf16[16,4096]{1,0:T(8,128)(2,1)S(1)}, bf16[16,4096]{1,0:T(8,128)(2,1)S(1)}, u32[]{:S(2)}, u32[]{:S(2)}) collective-permute-start(bf16[16,4096]{1,0:T(8,128)(2,1)S(1)} %copy-done.4), channel_id=1, source_target_pairs={{0,12},{1,13},{2,14},{3,15},{4,8},{5,9},{6,10},{7,11},{8,4},{9,5},... | collective-permute-start | bytes 393224 | tf_op jit(solution)/shard_map/ppermute | solution.py:31
  13.2 16.1 %collective-permute-start.2 = (bf16[32,8320]{1,0:T(8,128)(2,1)S(1)}, bf16[32,8320]{1,0:T(8,128)(2,1)S(1)}, u32[]{:S(2)}, u32[]{:S(2)}) collective-permute-start(bf16[32,8320]{1,0:T(8,128)(2,1)S(1)} %shard_map.86.refs_0_), channel_id=1, source_target_pairs={{0,2},{1,3},{2,0},{3,1},{4,6},{5,7},{6,4},{7,5},{8,10},{9,11},{10,... | collective-permute-start | bytes 1597448 | tf_op jit(solution)/shard_map/ppermute | solution.py:31
  22.1 17.6 %collective-permute-start.10 = (bf16[64,4096]{1,0:T(8,128)(2,1)S(1)}, bf16[64,4096]{1,0:T(8,128)(2,1)S(1)}, u32[]{:S(2)}, u32[]{:S(2)}) collective-permute-start(bf16[64,4096]{1,0:T(8,128)(2,1)S(1)} %shard_map.89.refs_0_.__0_), channel_id=1, source_target_pairs={{0,2},{1,3},{2,0},{3,1},{4,6},{5,7},{6,4},{7,5},{8,10},{9,11},{10,... | collective-permute-start | bytes 1572872 | tf_op jit(solution)/shard_map/ppermute | solution.py:31
  22.7 8.0 %collective-permute-start.11 = (bf16[16,4096]{1,0:T(8,128)(2,1)S(1)}, bf16[16,4096]{1,0:T(8,128)(2,1)S(1)}, u32[]{:S(2)}, u32[]{:S(2)}) collective-permute-start(bf16[16,4096]{1,0:T(8,128)(2,1)S(1)} %get-tuple-element.28), channel_id=1, source_target_pairs={{0,4},{1,5},{2,6},{3,7},{4,0},{5,1},{6,2},{7,3},{8,12},{9,13},{10,... | collective-permute-start | bytes 393224 | tf_op jit(solution)/shard_map/ppermute | solution.py:31
  25.0 12.2 %collective-permute-start.12 = (bf16[16,4096]{1,0:T(8,128)(2,1)S(1)}, bf16[16,4096]{1,0:T(8,128)(2,1)S(1)}, u32[]{:S(2)}, u32[]{:S(2)}) collective-permute-start(bf16[16,4096]{1,0:T(8,128)(2,1)S(1)} %get-tuple-element.29), channel_id=1, source_target_pairs={{0,8},{1,9},{2,10},{3,11},{4,12},{5,13},{6,14},{7,15},{8,0},{9,1},... | collective-permute-start | bytes 393224 | tf_op jit(solution)/shard_map/ppermute | solution.py:31
  26.9 10.3 %collective-permute-start.13 = (bf16[16,4096]{1,0:T(8,128)(2,1)S(1)}, bf16[16,4096]{1,0:T(8,128)(2,1)S(1)}, u32[]{:S(2)}, u32[]{:S(2)}) collective-permute-start(bf16[16,4096]{1,0:T(8,128)(2,1)S(1)} %get-tuple-element.30), channel_id=1, source_target_pairs={{0,12},{1,13},{2,14},{3,15},{4,8},{5,9},{6,10},{7,11},{8,4},{9,5},... | collective-permute-start | bytes 393224 | tf_op jit(solution)/shard_map/ppermute | solution.py:31
  39.9 5.0 %collective-permute-start.14 = (bf16[64,4096]{1,0:T(8,128)(2,1)S(1)}, bf16[64,4096]{1,0:T(8,128)(2,1)S(1)}, u32[]{:S(2)}, u32[]{:S(2)}) collective-permute-start(bf16[64,4096]{1,0:T(8,128)(2,1)S(1)} %shard_map.93), channel_id=1, source_target_pairs={{0,1},{1,0},{2,3},{3,2},{4,5},{5,4},{6,7},{7,6},{8,9},{9,8},{10,11... | collective-permute-start | bytes 1572872 | tf_op jit(solution)/shard_map/ppermute | solution.py:31
  39.9 7.0 %collective-permute-start.15 = (bf16[64,4096]{1,0:T(8,128)(2,1)S(1)}, bf16[64,4096]{1,0:T(8,128)(2,1)S(1)}, u32[]{:S(2)}, u32[]{:S(2)}) collective-permute-start(bf16[64,4096]{1,0:T(8,128)(2,1)S(1)} %shard_map.92.refs_0_), channel_id=1, source_target_pairs={{0,1},{1,0},{2,3},{3,2},{4,5},{5,4},{6,7},{7,6},{8,9},{9,8},{10,11... | collective-permute-start | bytes 1572872 | tf_op jit(solution)/shard_map/ppermute | solution.py:31
  40.4 4.4 %collective-permute-start.18 = (bf16[16,2048]{1,0:T(8,128)(2,1)S(1)}, bf16[16,2048]{1,0:T(8,128)(2,1)S(1)}, u32[]{:S(2)}, u32[]{:S(2)}) collective-permute-start(bf16[16,2048]{1,0:T(8,128)(2,1)S(1)} %get-tuple-element.31.__1_.refs_2_), channel_id=1, source_target_pairs={{0,16},{16,0},{1,17},{17,1},{2,18},{18,2},{3,19},{19,3},{4,20},{20... | collective-permute-start | bytes 196616 | tf_op jit(solution)/shard_map/ppermute | solution.py:31
  42.2 9.0 %collective-permute-start.16 = (bf16[16,2048]{1,0:T(8,128)(2,1)S(1)}, bf16[16,2048]{1,0:T(8,128)(2,1)S(1)}, u32[]{:S(2)}, u32[]{:S(2)}) collective-permute-start(bf16[16,2048]{1,0:T(8,128)(2,1)S(1)} %get-tuple-element.32.refs_0_), channel_id=1, source_target_pairs={{0,16},{16,0},{1,17},{17,1},{2,18},{18,2},{3,19},{19,3},{4,20},{20... | collective-permute-start | bytes 196616 | tf_op jit(solution)/shard_map/ppermute | solution.py:31
  42.5 8.8 %collective-permute-start.17 = (bf16[16,2048]{1,0:T(8,128)(2,1)S(1)}, bf16[16,2048]{1,0:T(8,128)(2,1)S(1)}, u32[]{:S(2)}, u32[]{:S(2)}) collective-permute-start(bf16[16,2048]{1,0:T(8,128)(2,1)S(1)} %get-tuple-element.31.__1_.refs_2_), channel_id=1, source_target_pairs={{0,1},{1,0},{2,3},{3,2},{4,5},{5,4},{6,7},{7,6},{8,9},{9,8},{10,11... | collective-permute-start | bytes 196616 | tf_op jit(solution)/shard_map/ppermute | solution.py:31
  44.9 6.4 %collective-permute-start.19 = (bf16[16,2048]{1,0:T(8,128)(2,1)S(1)}, bf16[16,2048]{1,0:T(8,128)(2,1)S(1)}, u32[]{:S(2)}, u32[]{:S(2)}) collective-permute-start(bf16[16,2048]{1,0:T(8,128)(2,1)S(1)} %collective-permute-done.18.refs_4_), channel_id=1, source_target_pairs={{0,1},{1,0},{2,3},{3,2},{4,5},{5,4},{6,7},{7,6},{8,9},{9,8},{10,11... | collective-permute-start | bytes 196616 | tf_op jit(solution)/shard_map/ppermute | solution.py:31
  44.9 28.8 %collective-permute-start.3 = (bf16[64,2176]{1,0:T(8,128)(2,1)S(1)}, bf16[64,2176]{1,0:T(8,128)(2,1)S(1)}, u32[]{:S(2)}, u32[]{:S(2)}) collective-permute-start(bf16[64,2176]{1,0:T(8,128)(2,1)S(1)} %get-tuple-element.23), channel_id=1, source_target_pairs={{0,4},{1,5},{2,6},{3,7},{4,0},{5,1},{6,2},{7,3},{8,12},{9,13},{10,... | collective-permute-start | bytes 835592 | tf_op jit(solution)/shard_map/ppermute | solution.py:31
  46.9 26.8 %collective-permute-start.4 = (bf16[64,2176]{1,0:T(8,128)(2,1)S(1)}, bf16[64,2176]{1,0:T(8,128)(2,1)S(1)}, u32[]{:S(2)}, u32[]{:S(2)}) collective-permute-start(bf16[64,2176]{1,0:T(8,128)(2,1)S(1)} %get-tuple-element.24), channel_id=1, source_target_pairs={{0,8},{1,9},{2,10},{3,11},{4,12},{5,13},{6,14},{7,15},{8,0},{9,1},... | collective-permute-start | bytes 835592 | tf_op jit(solution)/shard_map/ppermute | solution.py:31
  51.2 22.5 %collective-permute-start.5 = (bf16[64,2176]{1,0:T(8,128)(2,1)S(1)}, bf16[64,2176]{1,0:T(8,128)(2,1)S(1)}, u32[]{:S(2)}, u32[]{:S(2)}) collective-permute-start(bf16[64,2176]{1,0:T(8,128)(2,1)S(1)} %get-tuple-element.25), channel_id=1, source_target_pairs={{0,12},{1,13},{2,14},{3,15},{4,8},{5,9},{6,10},{7,11},{8,4},{9,5},... | collective-permute-start | bytes 835592 | tf_op jit(solution)/shard_map/ppermute | solution.py:31
  76.7 3.1 %collective-permute-start.22 = (f32[2,8,1]{2,1,0:T(8,128)S(1)}, f32[2,8,1]{2,1,0:T(8,128)S(1)}, u32[]{:S(2)}, u32[]{:S(2)}) collective-permute-start(f32[2,8,1]{2,1,0:T(8,128)S(1)} %shard_map.96), channel_id=1, source_target_pairs={{0,3},{1,2},{2,1},{3,0},{4,7},{5,6},{6,5},{7,4},{8,11},{9,10},{10,... | collective-permute-start | bytes 200 | tf_op jit(solution)/shard_map/ppermute | solution.py:31
  77.8 3.7 %collective-permute-start.21 = (f32[2,8,1]{2,1,0:T(8,128)S(1)}, f32[2,8,1]{2,1,0:T(8,128)S(1)}, u32[]{:S(2)}, u32[]{:S(2)}) collective-permute-start(f32[2,8,1]{2,1,0:T(8,128)S(1)} %shard_map.96), channel_id=1, source_target_pairs={{0,2},{1,3},{2,0},{3,1},{4,6},{5,7},{6,4},{7,5},{8,10},{9,11},{10,... | collective-permute-start | bytes 200 | tf_op jit(solution)/shard_map/ppermute | solution.py:31
  81.5 5.5 %collective-permute-start.25 = (f32[2,8,1]{2,1,0:T(8,128)S(1)}, f32[2,8,1]{2,1,0:T(8,128)S(1)}, u32[]{:S(2)}, u32[]{:S(2)}) collective-permute-start(f32[2,8,1]{2,1,0:T(8,128)S(1)} %add_add_fusion), channel_id=1, source_target_pairs={{0,12},{1,13},{2,14},{3,15},{4,8},{5,9},{6,10},{7,11},{8,4},{9,5},... | collective-permute-start | bytes 200 | tf_op jit(solution)/shard_map/ppermute | solution.py:31
  84.7 4.5 %collective-permute-start.24 = (f32[2,8,1]{2,1,0:T(8,128)S(1)}, f32[2,8,1]{2,1,0:T(8,128)S(1)}, u32[]{:S(2)}, u32[]{:S(2)}) collective-permute-start(f32[2,8,1]{2,1,0:T(8,128)S(1)} %add_add_fusion), channel_id=1, source_target_pairs={{0,8},{1,9},{2,10},{3,11},{4,12},{5,13},{6,14},{7,15},{8,0},{9,1},... | collective-permute-start | bytes 200 | tf_op jit(solution)/shard_map/ppermute | solution.py:31
  84.7 4.5 %collective-permute-start.23 = (f32[2,8,1]{2,1,0:T(8,128)S(1)}, f32[2,8,1]{2,1,0:T(8,128)S(1)}, u32[]{:S(2)}, u32[]{:S(2)}) collective-permute-start(f32[2,8,1]{2,1,0:T(8,128)S(1)} %add_add_fusion), channel_id=1, source_target_pairs={{0,4},{1,5},{2,6},{3,7},{4,0},{5,1},{6,2},{7,3},{8,12},{9,13},{10,... | collective-permute-start | bytes 200 | tf_op jit(solution)/shard_map/ppermute | solution.py:31
  (9 other events, 67.1 us)

commit v14 on v13

--- a/solution.py
+++ b/solution.py
@@ -457,8 +457,8 @@
     order = [4 * k + r for r in (0, 2, 1, 3) for k in along_z]
     keep, give = cut_factors(query_factors, order, hidden, batch_count)
     flags = owner_flags(owners, keep)
-    keep, give = pick(flags, keep, swap(give, "wide", 1), 0, cols, half, [])
-    grads_sent = grads_core(seq_ids, train_grad, give)
+    grads_sent = grads_core(seq_ids, train_grad, keep)
+    keep, give = pick(flags, keep, swap(give, "wide", 1), 0, cols, half, [grads_sent])
     grads_got = swap(grads_sent, "wide", 1)
     grads_over = grads_y(train_grad, grads_sent, grads_got, give)
     parts = pick(flags, keep, swap(give, "wide", 2), 1, cols, half, [grads_over])

time: 90.1 us -> 89.6 us (level)
    unnamed x14 -> x16, local copies, waits for them, and re-layouts: 3.37 us -> 3.66 us
  transfers between devices with their start and end apart: 26 -> 26, of which waited for: 12 -> 10; matrix products, arithmetic and copies ran while one was open for 0% -> 0% of each run, Pallas kernels for 29% -> 30%
where the time goes in v14:
time: 89.6 us; the launch traced here: 89.5 us
  Pallas kernels  29.8 us (33%)
  starting transfers between devices  28.2 us (31%)
  waiting for transfers between devices  26.9 us (30%)
  local copies, waits for them, and re-layouts  3.66 us (4%)
    ppermute x26, starting transfers between devices, swap(): return lax.ppermute(x, axis, [(i, i ^ bit) for i in range(count)])  28.2 us
    ppermute x26, waiting for transfers between devices, swap(): return lax.ppermute(x, axis, [(i, i ^ bit) for i in range(count)])  26.9 us
    pallas_call x1, Pallas kernels, images(): pl.pallas_call(functools.partial(image_kernel, batch_count, total, per),...  22.4 us
    unnamed x16, local copies, waits for them, and re-layouts  3.66 us
    pallas_call x1, Pallas kernels, score_parts(): pl.pallas_call(functools.partial(score_kernel, batch_count, ranks, count)...  2.98 us
    pallas_call x2, Pallas kernels, rotate(): pl.pallas_call(functools.partial(rotate_kernel, len(act_pieces), done), i...  2.62 us
  transfers between devices with their start and end apart: 26, of which 10 were waited for; matrix products, arithmetic and copies ran while one was open for 0% of the time, Pallas kernels for 30%

profile of v14, /device:TPU:0, one launch (start us, length us, event | category | flops | bytes accessed | tf_op | source)
XLA Modules:
  0.0 89.5 jit_solution(9210837512280043210)
XLA Ops:
  0.0 1.8 %copy-done.3 = bf16[2,16,36864]{2,1,0:T(8,128)(2,1)S(1)} copy-done((bf16[2,16,36864]{2,1,0:T(8,128)(2,1)S(1)}, bf16[2,16,36864]{2,1,0:T(8,128)(2,1)}, u32[]{:S(2)}) %copy-start.3) | copy-done | bytes 2359320
  2.4 1.2 %copy-done.1 = bf16[16,32768]{1,0:T(8,128)(2,1)S(1)} copy-done((bf16[16,32768]{1,0:T(8,128)(2,1)S(1)}, bf16[16,32768]{1,0:T(8,128)(2,1)}, u32[]{:S(2)}) %copy-start.1) | copy-done | bytes 1048600
  5.7 3.0 %collective-permute-start.9 = (bf16[16,10240]{1,0:T(8,128)(2,1)S(1)}, bf16[16,10240]{1,0:T(8,128)(2,1)S(1)}, u32[]{:S(2)}, u32[]{:S(2)}) collective-permute-start(bf16[16,10240]{1,0:T(8,128)(2,1)S(1)} %get-tuple-element.21._), channel_id=1, source_target_pairs={{0,2},{1,3},{2,0},{3,1},{4,6},{5,7},{6,4},{7,5},{8,10},{9,11},{10,... | collective-permute-start | bytes 983048 | tf_op jit(solution)/shard_map/ppermute | solution.py:31
  8.8 2.6 %collective-permute-start.7 = (bf16[16,4096]{1,0:T(8,128)(2,1)S(1)}, bf16[16,4096]{1,0:T(8,128)(2,1)S(1)}, u32[]{:S(2)}, u32[]{:S(2)}) collective-permute-start(bf16[16,4096]{1,0:T(8,128)(2,1)S(1)} %copy-done.5), channel_id=1, source_target_pairs={{0,8},{1,9},{2,10},{3,11},{4,12},{5,13},{6,14},{7,15},{8,0},{9,1},... | collective-permute-start | bytes 393224 | tf_op jit(solution)/shard_map/ppermute | solution.py:31
  11.4 1.6 %collective-permute-start.6 = (bf16[16,4096]{1,0:T(8,128)(2,1)S(1)}, bf16[16,4096]{1,0:T(8,128)(2,1)S(1)}, u32[]{:S(2)}, u32[]{:S(2)}) collective-permute-start(bf16[16,4096]{1,0:T(8,128)(2,1)S(1)} %copy-done.5), channel_id=1, source_target_pairs={{0,4},{1,5},{2,6},{3,7},{4,0},{5,1},{6,2},{7,3},{8,12},{9,13},{10,... | collective-permute-start | bytes 393224 | tf_op jit(solution)/shard_map/ppermute | solution.py:31
  13.6 3.7 %collective-permute-done.9.got_ref = bf16[16,10240]{1,0:T(8,128)(2,1)S(1)} collective-permute-done((bf16[16,10240]{1,0:T(8,128)(2,1)S(1)}, bf16[16,10240]{1,0:T(8,128)(2,1)S(1)}, u32[]{:S(2)}, u32[]{:S(2)}) %collective-permute-start.9) | collective-permute-done | bytes 327712 | tf_op jit(solution)/shard_map/ppermute | solution.py:31
  17.4 4.2 %collective-permute-done.7.refs_2_ = bf16[16,4096]{1,0:T(8,128)(2,1)S(1)} collective-permute-done((bf16[16,4096]{1,0:T(8,128)(2,1)S(1)}, bf16[16,4096]{1,0:T(8,128)(2,1)S(1)}, u32[]{:S(2)}, u32[]{:S(2)}) %collective-permute-start.7) | collective-permute-done | bytes 131104 | tf_op jit(solution)/shard_map/ppermute | solution.py:31
  22.2 2.4 %collective-permute-start.11 = (bf16[16,4096]{1,0:T(8,128)(2,1)S(1)}, bf16[16,4096]{1,0:T(8,128)(2,1)S(1)}, u32[]{:S(2)}, u32[]{:S(2)}) collective-permute-start(bf16[16,4096]{1,0:T(8,128)(2,1)S(1)} %get-tuple-element.28), channel_id=1, source_target_pairs={{0,4},{1,5},{2,6},{3,7},{4,0},{5,1},{6,2},{7,3},{8,12},{9,13},{10,... | collective-permute-start | bytes 393224 | tf_op jit(solution)/shard_map/ppermute | solution.py:31
  24.5 1.9 %collective-permute-start.12 = (bf16[16,4096]{1,0:T(8,128)(2,1)S(1)}, bf16[16,4096]{1,0:T(8,128)(2,1)S(1)}, u32[]{:S(2)}, u32[]{:S(2)}) collective-permute-start(bf16[16,4096]{1,0:T(8,128)(2,1)S(1)} %get-tuple-element.29), channel_id=1, source_target_pairs={{0,8},{1,9},{2,10},{3,11},{4,12},{5,13},{6,14},{7,15},{8,0},{9,1},... | collective-permute-start | bytes 393224 | tf_op jit(solution)/shard_map/ppermute | solution.py:31
  26.5 1.5 %collective-permute-start.13 = (bf16[16,4096]{1,0:T(8,128)(2,1)S(1)}, bf16[16,4096]{1,0:T(8,128)(2,1)S(1)}, u32[]{:S(2)}, u32[]{:S(2)}) collective-permute-start(bf16[16,4096]{1,0:T(8,128)(2,1)S(1)} %get-tuple-element.30), channel_id=1, source_target_pairs={{0,12},{1,13},{2,14},{3,15},{4,8},{5,9},{6,10},{7,11},{8,4},{9,5},... | collective-permute-start | bytes 393224 | tf_op jit(solution)/shard_map/ppermute | solution.py:31
  30.1 6.6 %collective-permute-done.12.refs_2_ = bf16[16,4096]{1,0:T(8,128)(2,1)S(1)} collective-permute-done((bf16[16,4096]{1,0:T(8,128)(2,1)S(1)}, bf16[16,4096]{1,0:T(8,128)(2,1)S(1)}, u32[]{:S(2)}, u32[]{:S(2)}) %collective-permute-start.12) | collective-permute-done | bytes 131104 | tf_op jit(solution)/shard_map/ppermute | solution.py:31
  36.8 2.5 %collective-permute-done.10.refs_4_.__0_ = bf16[64,4096]{1,0:T(8,128)(2,1)S(1)} collective-permute-done((bf16[64,4096]{1,0:T(8,128)(2,1)S(1)}, bf16[64,4096]{1,0:T(8,128)(2,1)S(1)}, u32[]{:S(2)}, u32[]{:S(2)}) %collective-permute-start.10) | collective-permute-done | bytes 524320 | tf_op jit(solution)/shard_map/ppermute | solution.py:31
  40.0 1.7 %collective-permute-start.18 = (bf16[16,2048]{1,0:T(8,128)(2,1)S(1)}, bf16[16,2048]{1,0:T(8,128)(2,1)S(1)}, u32[]{:S(2)}, u32[]{:S(2)}) collective-permute-start(bf16[16,2048]{1,0:T(8,128)(2,1)S(1)} %get-tuple-element.31.__1_.refs_2_), channel_id=1, source_target_pairs={{0,16},{16,0},{1,17},{17,1},{2,18},{18,2},{3,19},{19,3},{4,20},{20... | collective-permute-start | bytes 196616 | tf_op jit(solution)/shard_map/ppermute | solution.py:31
  42.1 2.4 %collective-permute-done.18.refs_4_ = bf16[16,2048]{1,0:T(8,128)(2,1)S(1)} collective-permute-done((bf16[16,2048]{1,0:T(8,128)(2,1)S(1)}, bf16[16,2048]{1,0:T(8,128)(2,1)S(1)}, u32[]{:S(2)}, u32[]{:S(2)}) %collective-permute-start.18) | collective-permute-done | bytes 65568 | tf_op jit(solution)/shard_map/ppermute | solution.py:31
  44.5 2.0 %collective-permute-start.3 = (bf16[64,2176]{1,0:T(8,128)(2,1)S(1)}, bf16[64,2176]{1,0:T(8,128)(2,1)S(1)}, u32[]{:S(2)}, u32[]{:S(2)}) collective-permute-start(bf16[64,2176]{1,0:T(8,128)(2,1)S(1)} %get-tuple-element.23), channel_id=1, source_target_pairs={{0,4},{1,5},{2,6},{3,7},{4,0},{5,1},{6,2},{7,3},{8,12},{9,13},{10,... | collective-permute-start | bytes 835592 | tf_op jit(solution)/shard_map/ppermute | solution.py:31
  46.5 2.6 %collective-permute-start.4 = (bf16[64,2176]{1,0:T(8,128)(2,1)S(1)}, bf16[64,2176]{1,0:T(8,128)(2,1)S(1)}, u32[]{:S(2)}, u32[]{:S(2)}) collective-permute-start(bf16[64,2176]{1,0:T(8,128)(2,1)S(1)} %get-tuple-element.24), channel_id=1, source_target_pairs={{0,8},{1,9},{2,10},{3,11},{4,12},{5,13},{6,14},{7,15},{8,0},{9,1},... | collective-permute-start | bytes 835592 | tf_op jit(solution)/shard_map/ppermute | solution.py:31
  49.1 1.7 %shard_map.94.rot_ref = bf16[4096,256]{1,0:T(8,128)(2,1)S(1)} custom-call(bf16[64,4096]{1,0:T(8,128)(2,1)S(1)} %shard_map.92.refs_0_, bf16[64,4096]{1,0:T(8,128)(2,1)S(1)} %collective-permute-done.14.refs_1_, bf16[64,4096]{1,0:T(8,128)(2,1)S(1)} %collective-permute-done.15.refs_2_, bf16[512,4096]{1,0:T(8,128)(2,1)S(1)} %copy-done, ...), custom_call_target="tpu_custom_call" | custom-call | bytes 1 | tf_op jit(solution)/shard_map/pallas_call | solution.py:277
  50.9 22.4 %shard_map.95.refs_9_ = f32[2,2048,256]{2,1,0:T(8,128)S(1)} custom-call(bf16[4096,256]{1,0:T(8,128)(2,1)S(1)} %shard_map.94.rot_ref, bf16[16,2048]{1,0:T(8,128)(2,1)S(1)} %get-tuple-element.32.refs_0_, bf16[16,2048]{1,0:T(8,128)(2,1)S(1)} %collective-permute-done.16.refs_1_, bf16[16,2048]{1,0:T(8,128)(2,1)S(1)} %get-tuple-element.31.__1_.refs_2_, ...), custom_call_target="tpu_custom_call" | custom-call | flops 17179869184 | bytes 16777216 | tf_op jit(solution)/shard_map/pallas_call | solution.py:363
  73.3 3.0 %shard_map.96 = f32[2,8,1]{2,1,0:T(8,128)S(1)} custom-call(bf16[64,2176]{1,0:T(8,128)(2,1)S(1)} %get-tuple-element.22.refs_6_.refs_0_.refs_4_, bf16[64,2176]{1,0:T(8,128)(2,1)S(1)} %collective-permute-done.3.refs_1_.refs_5_, bf16[64,2176]{1,0:T(8,128)(2,1)S(1)} %collective-permute-done.4.refs_2_.refs_6_, ...), custom_call_target="tpu_custom_call" | custom-call | flops 536870912 | bytes 4194304 | tf_op jit(solution)/shard_map/pallas_call | solution.py:423
  78.2 1.2 %collective-permute-done.22 = f32[2,8,1]{2,1,0:T(8,128)S(1)} collective-permute-done((f32[2,8,1]{2,1,0:T(8,128)S(1)}, f32[2,8,1]{2,1,0:T(8,128)S(1)}, u32[]{:S(2)}, u32[]{:S(2)}) %collective-permute-start.22) | collective-permute-done | bytes 96 | tf_op jit(solution)/shard_map/ppermute | solution.py:31
  79.4 1.6 %collective-permute-done.21 = f32[2,8,1]{2,1,0:T(8,128)S(1)} collective-permute-done((f32[2,8,1]{2,1,0:T(8,128)S(1)}, f32[2,8,1]{2,1,0:T(8,128)S(1)}, u32[]{:S(2)}, u32[]{:S(2)}) %collective-permute-start.21) | collective-permute-done | bytes 96 | tf_op jit(solution)/shard_map/ppermute | solution.py:31
  81.0 3.2 %collective-permute-start.25 = (f32[2,8,1]{2,1,0:T(8,128)S(1)}, f32[2,8,1]{2,1,0:T(8,128)S(1)}, u32[]{:S(2)}, u32[]{:S(2)}) collective-permute-start(f32[2,8,1]{2,1,0:T(8,128)S(1)} %add_add_fusion), channel_id=1, source_target_pairs={{0,12},{1,13},{2,14},{3,15},{4,8},{5,9},{6,10},{7,11},{8,4},{9,5},... | collective-permute-start | bytes 200 | tf_op jit(solution)/shard_map/ppermute | solution.py:31
  84.2 1.2 %collective-permute-start.23 = (f32[2,8,1]{2,1,0:T(8,128)S(1)}, f32[2,8,1]{2,1,0:T(8,128)S(1)}, u32[]{:S(2)}, u32[]{:S(2)}) collective-permute-start(f32[2,8,1]{2,1,0:T(8,128)S(1)} %add_add_fusion), channel_id=1, source_target_pairs={{0,4},{1,5},{2,6},{3,7},{4,0},{5,1},{6,2},{7,3},{8,12},{9,13},{10,... | collective-permute-start | bytes 200 | tf_op jit(solution)/shard_map/ppermute | solution.py:31
  86.6 2.2 %collective-permute-done.24 = f32[2,8,1]{2,1,0:T(8,128)S(1)} collective-permute-done((f32[2,8,1]{2,1,0:T(8,128)S(1)}, f32[2,8,1]{2,1,0:T(8,128)S(1)}, u32[]{:S(2)}, u32[]{:S(2)}) %collective-permute-start.24) | collective-permute-done | bytes 96 | tf_op jit(solution)/shard_map/ppermute | solution.py:31
  (61 shorter events, 10.9 us)
Async XLA Ops:
  1.8 3.7 %collective-permute-start.1 = (bf16[16,18432]{1,0:T(8,128)(2,1)S(1)}, bf16[16,18432]{1,0:T(8,128)(2,1)S(1)}, u32[]{:S(2)}, u32[]{:S(2)}) collective-permute-start(bf16[16,18432]{1,0:T(8,128)(2,1)S(1)} %get-tuple-element.20), channel_id=1, source_target_pairs={{0,1},{1,0},{2,3},{3,2},{4,5},{5,4},{6,7},{7,6},{8,9},{9,8},{10,11... | collective-permute-start | bytes 1769480 | tf_op jit(solution)/shard_map/ppermute | solution.py:31
  4.8 8.3 %collective-permute-start = (bf16[16,16512]{1,0:T(8,128)(2,1)S(1)}, bf16[16,16512]{1,0:T(8,128)(2,1)S(1)}, u32[]{:S(2)}, u32[]{:S(2)}) collective-permute-start(bf16[16,16512]{1,0:T(8,128)(2,1)S(1)} %shard_map.83.refs_0_.sent_ref), channel_id=1, source_target_pairs={{0,1},{1,0},{2,3},{3,2},{4,5},{5,4},{6,7},{7,6},{8,9},{9,8},{10,11... | collective-permute-start | bytes 1585160 | tf_op jit(solution)/shard_map/ppermute | solution.py:31
  5.7 11.5 %collective-permute-start.9 = (bf16[16,10240]{1,0:T(8,128)(2,1)S(1)}, bf16[16,10240]{1,0:T(8,128)(2,1)S(1)}, u32[]{:S(2)}, u32[]{:S(2)}) collective-permute-start(bf16[16,10240]{1,0:T(8,128)(2,1)S(1)} %get-tuple-element.21._), channel_id=1, source_target_pairs={{0,2},{1,3},{2,0},{3,1},{4,6},{5,7},{6,4},{7,5},{8,10},{9,11},{10,... | collective-permute-start | bytes 983048 | tf_op jit(solution)/shard_map/ppermute | solution.py:31
  8.8 12.8 %collective-permute-start.7 = (bf16[16,4096]{1,0:T(8,128)(2,1)S(1)}, bf16[16,4096]{1,0:T(8,128)(2,1)S(1)}, u32[]{:S(2)}, u32[]{:S(2)}) collective-permute-start(bf16[16,4096]{1,0:T(8,128)(2,1)S(1)} %copy-done.5), channel_id=1, source_target_pairs={{0,8},{1,9},{2,10},{3,11},{4,12},{5,13},{6,14},{7,15},{8,0},{9,1},... | collective-permute-start | bytes 393224 | tf_op jit(solution)/shard_map/ppermute | solution.py:31
  11.4 10.2 %collective-permute-start.6 = (bf16[16,4096]{1,0:T(8,128)(2,1)S(1)}, bf16[16,4096]{1,0:T(8,128)(2,1)S(1)}, u32[]{:S(2)}, u32[]{:S(2)}) collective-permute-start(bf16[16,4096]{1,0:T(8,128)(2,1)S(1)} %copy-done.5), channel_id=1, source_target_pairs={{0,4},{1,5},{2,6},{3,7},{4,0},{5,1},{6,2},{7,3},{8,12},{9,13},{10,... | collective-permute-start | bytes 393224 | tf_op jit(solution)/shard_map/ppermute | solution.py:31
  12.9 8.6 %collective-permute-start.8 = (bf16[16,4096]{1,0:T(8,128)(2,1)S(1)}, bf16[16,4096]{1,0:T(8,128)(2,1)S(1)}, u32[]{:S(2)}, u32[]{:S(2)}) collective-permute-start(bf16[16,4096]{1,0:T(8,128)(2,1)S(1)} %copy-done.5), channel_id=1, source_target_pairs={{0,12},{1,13},{2,14},{3,15},{4,8},{5,9},{6,10},{7,11},{8,4},{9,5},... | collective-permute-start | bytes 393224 | tf_op jit(solution)/shard_map/ppermute | solution.py:31
  13.2 15.7 %collective-permute-start.2 = (bf16[32,8320]{1,0:T(8,128)(2,1)S(1)}, bf16[32,8320]{1,0:T(8,128)(2,1)S(1)}, u32[]{:S(2)}, u32[]{:S(2)}) collective-permute-start(bf16[32,8320]{1,0:T(8,128)(2,1)S(1)} %shard_map.86.refs_0_), channel_id=1, source_target_pairs={{0,2},{1,3},{2,0},{3,1},{4,6},{5,7},{6,4},{7,5},{8,10},{9,11},{10,... | collective-permute-start | bytes 1597448 | tf_op jit(solution)/shard_map/ppermute | solution.py:31
  21.6 17.7 %collective-permute-start.10 = (bf16[64,4096]{1,0:T(8,128)(2,1)S(1)}, bf16[64,4096]{1,0:T(8,128)(2,1)S(1)}, u32[]{:S(2)}, u32[]{:S(2)}) collective-permute-start(bf16[64,4096]{1,0:T(8,128)(2,1)S(1)} %shard_map.89.refs_0_.__0_), channel_id=1, source_target_pairs={{0,2},{1,3},{2,0},{3,1},{4,6},{5,7},{6,4},{7,5},{8,10},{9,11},{10,... | collective-permute-start | bytes 1572872 | tf_op jit(solution)/shard_map/ppermute | solution.py:31
  22.2 8.0 %collective-permute-start.11 = (bf16[16,4096]{1,0:T(8,128)(2,1)S(1)}, bf16[16,4096]{1,0:T(8,128)(2,1)S(1)}, u32[]{:S(2)}, u32[]{:S(2)}) collective-permute-start(bf16[16,4096]{1,0:T(8,128)(2,1)S(1)} %get-tuple-element.28), channel_id=1, source_target_pairs={{0,4},{1,5},{2,6},{3,7},{4,0},{5,1},{6,2},{7,3},{8,12},{9,13},{10,... | collective-permute-start | bytes 393224 | tf_op jit(solution)/shard_map/ppermute | solution.py:31
  24.5 12.2 %collective-permute-start.12 = (bf16[16,4096]{1,0:T(8,128)(2,1)S(1)}, bf16[16,4096]{1,0:T(8,128)(2,1)S(1)}, u32[]{:S(2)}, u32[]{:S(2)}) collective-permute-start(bf16[16,4096]{1,0:T(8,128)(2,1)S(1)} %get-tuple-element.29), channel_id=1, source_target_pairs={{0,8},{1,9},{2,10},{3,11},{4,12},{5,13},{6,14},{7,15},{8,0},{9,1},... | collective-permute-start | bytes 393224 | tf_op jit(solution)/shard_map/ppermute | solution.py:31
  26.5 10.3 %collective-permute-start.13 = (bf16[16,4096]{1,0:T(8,128)(2,1)S(1)}, bf16[16,4096]{1,0:T(8,128)(2,1)S(1)}, u32[]{:S(2)}, u32[]{:S(2)}) collective-permute-start(bf16[16,4096]{1,0:T(8,128)(2,1)S(1)} %get-tuple-element.30), channel_id=1, source_target_pairs={{0,12},{1,13},{2,14},{3,15},{4,8},{5,9},{6,10},{7,11},{8,4},{9,5},... | collective-permute-start | bytes 393224 | tf_op jit(solution)/shard_map/ppermute | solution.py:31
  39.4 5.1 %collective-permute-start.14 = (bf16[64,4096]{1,0:T(8,128)(2,1)S(1)}, bf16[64,4096]{1,0:T(8,128)(2,1)S(1)}, u32[]{:S(2)}, u32[]{:S(2)}) collective-permute-start(bf16[64,4096]{1,0:T(8,128)(2,1)S(1)} %shard_map.93), channel_id=1, source_target_pairs={{0,1},{1,0},{2,3},{3,2},{4,5},{5,4},{6,7},{7,6},{8,9},{9,8},{10,11... | collective-permute-start | bytes 1572872 | tf_op jit(solution)/shard_map/ppermute | solution.py:31
  39.5 6.9 %collective-permute-start.15 = (bf16[64,4096]{1,0:T(8,128)(2,1)S(1)}, bf16[64,4096]{1,0:T(8,128)(2,1)S(1)}, u32[]{:S(2)}, u32[]{:S(2)}) collective-permute-start(bf16[64,4096]{1,0:T(8,128)(2,1)S(1)} %shard_map.92.refs_0_), channel_id=1, source_target_pairs={{0,1},{1,0},{2,3},{3,2},{4,5},{5,4},{6,7},{7,6},{8,9},{9,8},{10,11... | collective-permute-start | bytes 1572872 | tf_op jit(solution)/shard_map/ppermute | solution.py:31
  40.0 4.5 %collective-permute-start.18 = (bf16[16,2048]{1,0:T(8,128)(2,1)S(1)}, bf16[16,2048]{1,0:T(8,128)(2,1)S(1)}, u32[]{:S(2)}, u32[]{:S(2)}) collective-permute-start(bf16[16,2048]{1,0:T(8,128)(2,1)S(1)} %get-tuple-element.31.__1_.refs_2_), channel_id=1, source_target_pairs={{0,16},{16,0},{1,17},{17,1},{2,18},{18,2},{3,19},{19,3},{4,20},{20... | collective-permute-start | bytes 196616 | tf_op jit(solution)/shard_map/ppermute | solution.py:31
  41.7 9.0 %collective-permute-start.16 = (bf16[16,2048]{1,0:T(8,128)(2,1)S(1)}, bf16[16,2048]{1,0:T(8,128)(2,1)S(1)}, u32[]{:S(2)}, u32[]{:S(2)}) collective-permute-start(bf16[16,2048]{1,0:T(8,128)(2,1)S(1)} %get-tuple-element.32.refs_0_), channel_id=1, source_target_pairs={{0,16},{16,0},{1,17},{17,1},{2,18},{18,2},{3,19},{19,3},{4,20},{20... | collective-permute-start | bytes 196616 | tf_op jit(solution)/shard_map/ppermute | solution.py:31
  42.1 8.8 %collective-permute-start.17 = (bf16[16,2048]{1,0:T(8,128)(2,1)S(1)}, bf16[16,2048]{1,0:T(8,128)(2,1)S(1)}, u32[]{:S(2)}, u32[]{:S(2)}) collective-permute-start(bf16[16,2048]{1,0:T(8,128)(2,1)S(1)} %get-tuple-element.31.__1_.refs_2_), channel_id=1, source_target_pairs={{0,1},{1,0},{2,3},{3,2},{4,5},{5,4},{6,7},{7,6},{8,9},{9,8},{10,11... | collective-permute-start | bytes 196616 | tf_op jit(solution)/shard_map/ppermute | solution.py:31
  44.5 6.4 %collective-permute-start.19 = (bf16[16,2048]{1,0:T(8,128)(2,1)S(1)}, bf16[16,2048]{1,0:T(8,128)(2,1)S(1)}, u32[]{:S(2)}, u32[]{:S(2)}) collective-permute-start(bf16[16,2048]{1,0:T(8,128)(2,1)S(1)} %collective-permute-done.18.refs_4_), channel_id=1, source_target_pairs={{0,1},{1,0},{2,3},{3,2},{4,5},{5,4},{6,7},{7,6},{8,9},{9,8},{10,11... | collective-permute-start | bytes 196616 | tf_op jit(solution)/shard_map/ppermute | solution.py:31
  44.5 28.8 %collective-permute-start.3 = (bf16[64,2176]{1,0:T(8,128)(2,1)S(1)}, bf16[64,2176]{1,0:T(8,128)(2,1)S(1)}, u32[]{:S(2)}, u32[]{:S(2)}) collective-permute-start(bf16[64,2176]{1,0:T(8,128)(2,1)S(1)} %get-tuple-element.23), channel_id=1, source_target_pairs={{0,4},{1,5},{2,6},{3,7},{4,0},{5,1},{6,2},{7,3},{8,12},{9,13},{10,... | collective-permute-start | bytes 835592 | tf_op jit(solution)/shard_map/ppermute | solution.py:31
  46.5 26.8 %collective-permute-start.4 = (bf16[64,2176]{1,0:T(8,128)(2,1)S(1)}, bf16[64,2176]{1,0:T(8,128)(2,1)S(1)}, u32[]{:S(2)}, u32[]{:S(2)}) collective-permute-start(bf16[64,2176]{1,0:T(8,128)(2,1)S(1)} %get-tuple-element.24), channel_id=1, source_target_pairs={{0,8},{1,9},{2,10},{3,11},{4,12},{5,13},{6,14},{7,15},{8,0},{9,1},... | collective-permute-start | bytes 835592 | tf_op jit(solution)/shard_map/ppermute | solution.py:31
  50.8 22.5 %collective-permute-start.5 = (bf16[64,2176]{1,0:T(8,128)(2,1)S(1)}, bf16[64,2176]{1,0:T(8,128)(2,1)S(1)}, u32[]{:S(2)}, u32[]{:S(2)}) collective-permute-start(bf16[64,2176]{1,0:T(8,128)(2,1)S(1)} %get-tuple-element.25), channel_id=1, source_target_pairs={{0,12},{1,13},{2,14},{3,15},{4,8},{5,9},{6,10},{7,11},{8,4},{9,5},... | collective-permute-start | bytes 835592 | tf_op jit(solution)/shard_map/ppermute | solution.py:31
  77.4 3.7 %collective-permute-start.21 = (f32[2,8,1]{2,1,0:T(8,128)S(1)}, f32[2,8,1]{2,1,0:T(8,128)S(1)}, u32[]{:S(2)}, u32[]{:S(2)}) collective-permute-start(f32[2,8,1]{2,1,0:T(8,128)S(1)} %shard_map.96), channel_id=1, source_target_pairs={{0,2},{1,3},{2,0},{3,1},{4,6},{5,7},{6,4},{7,5},{8,10},{9,11},{10,... | collective-permute-start | bytes 200 | tf_op jit(solution)/shard_map/ppermute | solution.py:31
  81.0 5.5 %collective-permute-start.25 = (f32[2,8,1]{2,1,0:T(8,128)S(1)}, f32[2,8,1]{2,1,0:T(8,128)S(1)}, u32[]{:S(2)}, u32[]{:S(2)}) collective-permute-start(f32[2,8,1]{2,1,0:T(8,128)S(1)} %add_add_fusion), channel_id=1, source_target_pairs={{0,12},{1,13},{2,14},{3,15},{4,8},{5,9},{6,10},{7,11},{8,4},{9,5},... | collective-permute-start | bytes 200 | tf_op jit(solution)/shard_map/ppermute | solution.py:31
  84.2 4.5 %collective-permute-start.24 = (f32[2,8,1]{2,1,0:T(8,128)S(1)}, f32[2,8,1]{2,1,0:T(8,128)S(1)}, u32[]{:S(2)}, u32[]{:S(2)}) collective-permute-start(f32[2,8,1]{2,1,0:T(8,128)S(1)} %add_add_fusion), channel_id=1, source_target_pairs={{0,8},{1,9},{2,10},{3,11},{4,12},{5,13},{6,14},{7,15},{8,0},{9,1},... | collective-permute-start | bytes 200 | tf_op jit(solution)/shard_map/ppermute | solution.py:31
  84.2 4.5 %collective-permute-start.23 = (f32[2,8,1]{2,1,0:T(8,128)S(1)}, f32[2,8,1]{2,1,0:T(8,128)S(1)}, u32[]{:S(2)}, u32[]{:S(2)}) collective-permute-start(f32[2,8,1]{2,1,0:T(8,128)S(1)} %add_add_fusion), channel_id=1, source_target_pairs={{0,4},{1,5},{2,6},{3,7},{4,0},{5,1},{6,2},{7,3},{8,12},{9,13},{10,... | collective-permute-start | bytes 200 | tf_op jit(solution)/shard_map/ppermute | solution.py:31
  (10 other events, 78.8 us)

commit v15 on v14

--- a/solution.py
+++ b/solution.py
@@ -122,19 +122,15 @@
 
 
 def pick_one_kernel(count, flag_ref, *refs):
-    left_ref, right_ref = refs[-2:]
-    cols = left_ref.shape[1]
-    for out_ref, place in ((left_ref, slice(0, cols)), (right_ref, slice(cols, None))):
-        out_ref[...] = sum(refs[k][:, place] * flag_ref[:, 2 + k:3 + k] for k in range(count))
-
-
-def pick_one(flags, pieces, cols, after):
-    rows, width = pieces[0].shape
+    refs[-1][...] = sum(refs[k][...] * flag_ref[:, 2 + k:3 + k] for k in range(count))
+
+
+def pick_one(flags, pieces, after):
     return pl.pallas_call(
         functools.partial(pick_one_kernel, len(pieces)),
         in_specs=in_vmem(1 + len(pieces)) + in_place(len(after)),
-        out_specs=in_vmem(2),
-        out_shape=[jax.ShapeDtypeStruct((rows, w), pieces[0].dtype) for w in (cols, width - cols)],
+        out_specs=in_vmem(1)[0],
+        out_shape=jax.ShapeDtypeStruct(pieces[0].shape, pieces[0].dtype),
         compiler_params=params(16),
         cost_estimate=pl.CostEstimate(flops=0, bytes_accessed=1, transcendentals=0),
     )(flags, *pieces, *after)
@@ -297,7 +293,8 @@
         for b in range(batch_count):
             for other in range(2):
                 at = pl.multiple_of(((lax.axis_index("wide") & 1) ^ other) * side, side)
-                right_ref[b, :, pl.ds(at, side)] = half_refs[2 * b + other][...]
+                ref = half_refs[2 * b + other]
+                right_ref[b, :, pl.ds(at, side)] = ref[:, ref.shape[1] - side:]
 
     @pl.when(jnp.logical_and(lax.rem(s, per) == 0, s < total))
     def _():
@@ -376,11 +373,7 @@
             pltpu.VMEM((batch_count * rows, chunk), jnp.bfloat16),
         ],
         compiler_params=params(32 if tokens <= 256 else 48),
-        cost_estimate=pl.CostEstimate(
-            flops=2 * hidden * width * (tokens + 256) * batch_count,
-            bytes_accessed=2 * hidden * width,
-            transcendentals=0,
-        ),
+        cost_estimate=pl.CostEstimate(flops=0, bytes_accessed=1, transcendentals=0),
     )(rot, *lefts, *halves, eigenvalues)
 
 
@@ -469,15 +462,14 @@
     over = swap(acts, "wide", 2)
     first = rotate([acts], act_basis, parts[0])
     parts = [swap(parts[k], "wide", 4 * k) if k else parts[0] for k in along_z]
-    left, right = pick_one(flags, parts, cols, [over, first, sent[0]])
-
-    lefts = [left, swap(left, "groups", 1)]
-    other = swap(right, "groups", 1)
+    held = pick_one(flags, parts, [over, first, sent[0]])
+
+    lefts = [held, swap(held, "groups", 1)]
     halves = []
-    for x in (right, other):
+    for x in lefts:
         halves += [x, swap(x, "wide", 1)]
-    over = gate(over, [right])
-    rot = rotate([over, swap(gate(acts, [right]), "wide", 1), swap(over, "wide", 1)], act_basis, None, first)
+    over = gate(over, [held])
+    rot = rotate([over, swap(gate(acts, [held]), "wide", 1), swap(over, "wide", 1)], act_basis, None, first)
     ranks = [r + more for more in (0, 2, 1, 3) for r in ranks]
 
     grads = [swap(sent[k], "wide", 4 * k) if k else sent[0] for k in along_z]

time: 89.6 us -> 88.7 us (0.990)
  waiting for transfers between devices: 26.9 us -> 22.9 us
  starting transfers between devices: 28.2 us -> 31.4 us
    ppermute x26 -> x25, waiting for transfers between devices: 26.9 us -> 22.9 us  [swap(): return lax.ppermute(x, axis, [(i, i ^ bit) for i in range(count)])]
    ppermute x26 -> x25, starting transfers between devices: 28.2 us -> 31.4 us  [swap(): return lax.ppermute(x, axis, [(i, i ^ bit) for i in range(count)])]
  transfers between devices with their start and end apart: 26 -> 25, of which waited for: 10 -> 9; matrix products, arithmetic and copies ran while one was open for 0% -> 0% of each run, Pallas kernels for 30% -> 30%
where the time goes in v15:
time: 88.7 us; the launch traced here: 88.6 us
  starting transfers between devices  31.4 us (35%)
  Pallas kernels  29.8 us (34%)
  waiting for transfers between devices  22.9 us (26%)
  local copies, waits for them, and re-layouts  3.66 us (4%)
    ppermute x25, starting transfers between devices, swap(): return lax.ppermute(x, axis, [(i, i ^ bit) for i in range(count)])  31.4 us
    ppermute x25, waiting for transfers between devices, swap(): return lax.ppermute(x, axis, [(i, i ^ bit) for i in range(count)])  22.9 us
    pallas_call x1, Pallas kernels, images(): pl.pallas_call(functools.partial(image_kernel, batch_count, total, per),...  22.4 us
    unnamed x16, local copies, waits for them, and re-layouts  3.66 us
    pallas_call x1, Pallas kernels, score_parts(): pl.pallas_call(functools.partial(score_kernel, batch_count, ranks, count)...  2.98 us
    pallas_call x2, Pallas kernels, rotate(): pl.pallas_call(functools.partial(rotate_kernel, len(act_pieces), done), i...  2.63 us
  transfers between devices with their start and end apart: 25, of which 9 were waited for; matrix products, arithmetic and copies ran while one was open for 0% of the time, Pallas kernels for 30%

profile of v15, /device:TPU:0, one launch (start us, length us, event | category | flops | bytes accessed | tf_op | source)
XLA Modules:
  0.0 88.6 jit_solution(9149702775843940543)
XLA Ops:
  0.0 1.8 %copy-done.3 = bf16[2,16,36864]{2,1,0:T(8,128)(2,1)S(1)} copy-done((bf16[2,16,36864]{2,1,0:T(8,128)(2,1)S(1)}, bf16[2,16,36864]{2,1,0:T(8,128)(2,1)}, u32[]{:S(2)}) %copy-start.3) | copy-done | bytes 2359320
  2.4 1.2 %copy-done.1 = bf16[16,32768]{1,0:T(8,128)(2,1)S(1)} copy-done((bf16[16,32768]{1,0:T(8,128)(2,1)S(1)}, bf16[16,32768]{1,0:T(8,128)(2,1)}, u32[]{:S(2)}) %copy-start.1) | copy-done | bytes 1048600
  5.7 3.0 %collective-permute-start.9 = (bf16[16,10240]{1,0:T(8,128)(2,1)S(1)}, bf16[16,10240]{1,0:T(8,128)(2,1)S(1)}, u32[]{:S(2)}, u32[]{:S(2)}) collective-permute-start(bf16[16,10240]{1,0:T(8,128)(2,1)S(1)} %get-tuple-element.19._), channel_id=1, source_target_pairs={{0,2},{1,3},{2,0},{3,1},{4,6},{5,7},{6,4},{7,5},{8,10},{9,11},{10,... | collective-permute-start | bytes 983048 | tf_op jit(solution)/shard_map/ppermute | solution.py:31
  8.8 2.6 %collective-permute-start.7 = (bf16[16,4096]{1,0:T(8,128)(2,1)S(1)}, bf16[16,4096]{1,0:T(8,128)(2,1)S(1)}, u32[]{:S(2)}, u32[]{:S(2)}) collective-permute-start(bf16[16,4096]{1,0:T(8,128)(2,1)S(1)} %copy-done.5), channel_id=1, source_target_pairs={{0,8},{1,9},{2,10},{3,11},{4,12},{5,13},{6,14},{7,15},{8,0},{9,1},... | collective-permute-start | bytes 393224 | tf_op jit(solution)/shard_map/ppermute | solution.py:31
  11.4 1.6 %collective-permute-start.6 = (bf16[16,4096]{1,0:T(8,128)(2,1)S(1)}, bf16[16,4096]{1,0:T(8,128)(2,1)S(1)}, u32[]{:S(2)}, u32[]{:S(2)}) collective-permute-start(bf16[16,4096]{1,0:T(8,128)(2,1)S(1)} %copy-done.5), channel_id=1, source_target_pairs={{0,4},{1,5},{2,6},{3,7},{4,0},{5,1},{6,2},{7,3},{8,12},{9,13},{10,... | collective-permute-start | bytes 393224 | tf_op jit(solution)/shard_map/ppermute | solution.py:31
  13.6 3.7 %collective-permute-done.9.got_ref = bf16[16,10240]{1,0:T(8,128)(2,1)S(1)} collective-permute-done((bf16[16,10240]{1,0:T(8,128)(2,1)S(1)}, bf16[16,10240]{1,0:T(8,128)(2,1)S(1)}, u32[]{:S(2)}, u32[]{:S(2)}) %collective-permute-start.9) | collective-permute-done | bytes 327712 | tf_op jit(solution)/shard_map/ppermute | solution.py:31
  17.4 4.2 %collective-permute-done.7.refs_2_ = bf16[16,4096]{1,0:T(8,128)(2,1)S(1)} collective-permute-done((bf16[16,4096]{1,0:T(8,128)(2,1)S(1)}, bf16[16,4096]{1,0:T(8,128)(2,1)S(1)}, u32[]{:S(2)}, u32[]{:S(2)}) %collective-permute-start.7) | collective-permute-done | bytes 131104 | tf_op jit(solution)/shard_map/ppermute | solution.py:31
  22.2 2.4 %collective-permute-start.11 = (bf16[16,4096]{1,0:T(8,128)(2,1)S(1)}, bf16[16,4096]{1,0:T(8,128)(2,1)S(1)}, u32[]{:S(2)}, u32[]{:S(2)}) collective-permute-start(bf16[16,4096]{1,0:T(8,128)(2,1)S(1)} %get-tuple-element.26), channel_id=1, source_target_pairs={{0,4},{1,5},{2,6},{3,7},{4,0},{5,1},{6,2},{7,3},{8,12},{9,13},{10,... | collective-permute-start | bytes 393224 | tf_op jit(solution)/shard_map/ppermute | solution.py:31
  24.5 1.9 %collective-permute-start.12 = (bf16[16,4096]{1,0:T(8,128)(2,1)S(1)}, bf16[16,4096]{1,0:T(8,128)(2,1)S(1)}, u32[]{:S(2)}, u32[]{:S(2)}) collective-permute-start(bf16[16,4096]{1,0:T(8,128)(2,1)S(1)} %get-tuple-element.27), channel_id=1, source_target_pairs={{0,8},{1,9},{2,10},{3,11},{4,12},{5,13},{6,14},{7,15},{8,0},{9,1},... | collective-permute-start | bytes 393224 | tf_op jit(solution)/shard_map/ppermute | solution.py:31
  26.5 1.5 %collective-permute-start.13 = (bf16[16,4096]{1,0:T(8,128)(2,1)S(1)}, bf16[16,4096]{1,0:T(8,128)(2,1)S(1)}, u32[]{:S(2)}, u32[]{:S(2)}) collective-permute-start(bf16[16,4096]{1,0:T(8,128)(2,1)S(1)} %get-tuple-element.28), channel_id=1, source_target_pairs={{0,12},{1,13},{2,14},{3,15},{4,8},{5,9},{6,10},{7,11},{8,4},{9,5},... | collective-permute-start | bytes 393224 | tf_op jit(solution)/shard_map/ppermute | solution.py:31
  29.0 1.2 %collective-permute-done.11.refs_1_ = bf16[16,4096]{1,0:T(8,128)(2,1)S(1)} collective-permute-done((bf16[16,4096]{1,0:T(8,128)(2,1)S(1)}, bf16[16,4096]{1,0:T(8,128)(2,1)S(1)}, u32[]{:S(2)}, u32[]{:S(2)}) %collective-permute-start.11) | collective-permute-done | bytes 131104 | tf_op jit(solution)/shard_map/ppermute | solution.py:31
  30.1 6.6 %collective-permute-done.12.refs_2_ = bf16[16,4096]{1,0:T(8,128)(2,1)S(1)} collective-permute-done((bf16[16,4096]{1,0:T(8,128)(2,1)S(1)}, bf16[16,4096]{1,0:T(8,128)(2,1)S(1)}, u32[]{:S(2)}, u32[]{:S(2)}) %collective-permute-start.12) | collective-permute-done | bytes 131104 | tf_op jit(solution)/shard_map/ppermute | solution.py:31
  36.8 2.5 %collective-permute-done.10.refs_4_.__0_ = bf16[64,4096]{1,0:T(8,128)(2,1)S(1)} collective-permute-done((bf16[64,4096]{1,0:T(8,128)(2,1)S(1)}, bf16[64,4096]{1,0:T(8,128)(2,1)S(1)}, u32[]{:S(2)}, u32[]{:S(2)}) %collective-permute-start.10) | collective-permute-done | bytes 524320 | tf_op jit(solution)/shard_map/ppermute | solution.py:31
  40.0 1.7 %collective-permute-start.16 = (bf16[16,4096]{1,0:T(8,128)(2,1)S(1)}, bf16[16,4096]{1,0:T(8,128)(2,1)S(1)}, u32[]{:S(2)}, u32[]{:S(2)}) collective-permute-start(bf16[16,4096]{1,0:T(8,128)(2,1)S(1)} %shard_map.91.__1_.refs_0_.refs_2_), channel_id=1, source_target_pairs={{0,16},{16,0},{1,17},{17,1},{2,18},{18,2},{3,19},{19,3},{4,20},{20... | collective-permute-start | bytes 393224 | tf_op jit(solution)/shard_map/ppermute | solution.py:31
  41.7 1.6 %collective-permute-start.3 = (bf16[64,2176]{1,0:T(8,128)(2,1)S(1)}, bf16[64,2176]{1,0:T(8,128)(2,1)S(1)}, u32[]{:S(2)}, u32[]{:S(2)}) collective-permute-start(bf16[64,2176]{1,0:T(8,128)(2,1)S(1)} %get-tuple-element.21), channel_id=1, source_target_pairs={{0,4},{1,5},{2,6},{3,7},{4,0},{5,1},{6,2},{7,3},{8,12},{9,13},{10,... | collective-permute-start | bytes 835592 | tf_op jit(solution)/shard_map/ppermute | solution.py:31
  43.3 2.6 %collective-permute-start.4 = (bf16[64,2176]{1,0:T(8,128)(2,1)S(1)}, bf16[64,2176]{1,0:T(8,128)(2,1)S(1)}, u32[]{:S(2)}, u32[]{:S(2)}) collective-permute-start(bf16[64,2176]{1,0:T(8,128)(2,1)S(1)} %get-tuple-element.22), channel_id=1, source_target_pairs={{0,8},{1,9},{2,10},{3,11},{4,12},{5,13},{6,14},{7,15},{8,0},{9,1},... | collective-permute-start | bytes 835592 | tf_op jit(solution)/shard_map/ppermute | solution.py:31
  45.9 3.4 %collective-permute-start.5 = (bf16[64,2176]{1,0:T(8,128)(2,1)S(1)}, bf16[64,2176]{1,0:T(8,128)(2,1)S(1)}, u32[]{:S(2)}, u32[]{:S(2)}) collective-permute-start(bf16[64,2176]{1,0:T(8,128)(2,1)S(1)} %get-tuple-element.23), channel_id=1, source_target_pairs={{0,12},{1,13},{2,14},{3,15},{4,8},{5,9},{6,10},{7,11},{8,4},{9,5},... | collective-permute-start | bytes 835592 | tf_op jit(solution)/shard_map/ppermute | solution.py:31
  49.9 1.7 %shard_map.94.rot_ref = bf16[4096,256]{1,0:T(8,128)(2,1)S(1)} custom-call(bf16[64,4096]{1,0:T(8,128)(2,1)S(1)} %shard_map.92.refs_0_, bf16[64,4096]{1,0:T(8,128)(2,1)S(1)} %collective-permute-done.14.refs_1_, bf16[64,4096]{1,0:T(8,128)(2,1)S(1)} %collective-permute-done.15.refs_2_, bf16[512,4096]{1,0:T(8,128)(2,1)S(1)} %copy-done, ...), custom_call_target="tpu_custom_call" | custom-call | bytes 1 | tf_op jit(solution)/shard_map/pallas_call | solution.py:273
  51.6 22.4 %shard_map.95.refs_9_ = f32[2,2048,256]{2,1,0:T(8,128)S(1)} custom-call(bf16[4096,256]{1,0:T(8,128)(2,1)S(1)} %shard_map.94.rot_ref, bf16[16,4096]{1,0:T(8,128)(2,1)S(1)} %shard_map.91.__1_.refs_0_.refs_2_, bf16[16,4096]{1,0:T(8,128)(2,1)S(1)} %collective-permute-done.16.refs_1_.refs_4_, bf16[16,4096]{1,0:T(8,128)(2,1)S(1)} %shard_map.91.__1_.refs_0_.refs_2_, ...), custom_call_target="tpu_custom_call" | custom-call | bytes 1 | tf_op jit(solution)/shard_map/pallas_call | solution.py:360
  74.0 3.0 %shard_map.96 = f32[2,8,1]{2,1,0:T(8,128)S(1)} custom-call(bf16[64,2176]{1,0:T(8,128)(2,1)S(1)} %get-tuple-element.20.refs_6_.refs_0_.refs_4_, bf16[64,2176]{1,0:T(8,128)(2,1)S(1)} %collective-permute-done.3.refs_1_.refs_5_, bf16[64,2176]{1,0:T(8,128)(2,1)S(1)} %collective-permute-done.4.refs_2_.refs_6_, ...), custom_call_target="tpu_custom_call" | custom-call | flops 536870912 | bytes 4194304 | tf_op jit(solution)/shard_map/pallas_call | solution.py:416
  77.0 1.2 %collective-permute-start.21 = (f32[2,8,1]{2,1,0:T(8,128)S(1)}, f32[2,8,1]{2,1,0:T(8,128)S(1)}, u32[]{:S(2)}, u32[]{:S(2)}) collective-permute-start(f32[2,8,1]{2,1,0:T(8,128)S(1)} %shard_map.96), channel_id=1, source_target_pairs={{0,3},{1,2},{2,1},{3,0},{4,7},{5,6},{6,5},{7,4},{8,11},{9,10},{10,... | collective-permute-start | bytes 200 | tf_op jit(solution)/shard_map/ppermute | solution.py:31
  78.8 1.2 %collective-permute-done.21 = f32[2,8,1]{2,1,0:T(8,128)S(1)} collective-permute-done((f32[2,8,1]{2,1,0:T(8,128)S(1)}, f32[2,8,1]{2,1,0:T(8,128)S(1)}, u32[]{:S(2)}, u32[]{:S(2)}) %collective-permute-start.21) | collective-permute-done | bytes 96 | tf_op jit(solution)/shard_map/ppermute | solution.py:31
  80.0 1.8 %collective-permute-done.20 = f32[2,8,1]{2,1,0:T(8,128)S(1)} collective-permute-done((f32[2,8,1]{2,1,0:T(8,128)S(1)}, f32[2,8,1]{2,1,0:T(8,128)S(1)}, u32[]{:S(2)}, u32[]{:S(2)}) %collective-permute-start.20) | collective-permute-done | bytes 96 | tf_op jit(solution)/shard_map/ppermute | solution.py:31
  82.9 3.4 %collective-permute-start.22 = (f32[2,8,1]{2,1,0:T(8,128)S(1)}, f32[2,8,1]{2,1,0:T(8,128)S(1)}, u32[]{:S(2)}, u32[]{:S(2)}) collective-permute-start(f32[2,8,1]{2,1,0:T(8,128)S(1)} %add_add_fusion), channel_id=1, source_target_pairs={{0,4},{1,5},{2,6},{3,7},{4,0},{5,1},{6,2},{7,3},{8,12},{9,13},{10,... | collective-permute-start | bytes 200 | tf_op jit(solution)/shard_map/ppermute | solution.py:31
  (59 shorter events, 10.3 us)
Async XLA Ops:
  1.8 3.7 %collective-permute-start.1 = (bf16[16,18432]{1,0:T(8,128)(2,1)S(1)}, bf16[16,18432]{1,0:T(8,128)(2,1)S(1)}, u32[]{:S(2)}, u32[]{:S(2)}) collective-permute-start(bf16[16,18432]{1,0:T(8,128)(2,1)S(1)} %get-tuple-element.18), channel_id=1, source_target_pairs={{0,1},{1,0},{2,3},{3,2},{4,5},{5,4},{6,7},{7,6},{8,9},{9,8},{10,11... | collective-permute-start | bytes 1769480 | tf_op jit(solution)/shard_map/ppermute | solution.py:31
  4.8 8.3 %collective-permute-start = (bf16[16,16512]{1,0:T(8,128)(2,1)S(1)}, bf16[16,16512]{1,0:T(8,128)(2,1)S(1)}, u32[]{:S(2)}, u32[]{:S(2)}) collective-permute-start(bf16[16,16512]{1,0:T(8,128)(2,1)S(1)} %shard_map.83.refs_0_.sent_ref), channel_id=1, source_target_pairs={{0,1},{1,0},{2,3},{3,2},{4,5},{5,4},{6,7},{7,6},{8,9},{9,8},{10,11... | collective-permute-start | bytes 1585160 | tf_op jit(solution)/shard_map/ppermute | solution.py:31
  5.7 11.5 %collective-permute-start.9 = (bf16[16,10240]{1,0:T(8,128)(2,1)S(1)}, bf16[16,10240]{1,0:T(8,128)(2,1)S(1)}, u32[]{:S(2)}, u32[]{:S(2)}) collective-permute-start(bf16[16,10240]{1,0:T(8,128)(2,1)S(1)} %get-tuple-element.19._), channel_id=1, source_target_pairs={{0,2},{1,3},{2,0},{3,1},{4,6},{5,7},{6,4},{7,5},{8,10},{9,11},{10,... | collective-permute-start | bytes 983048 | tf_op jit(solution)/shard_map/ppermute | solution.py:31
  8.8 12.8 %collective-permute-start.7 = (bf16[16,4096]{1,0:T(8,128)(2,1)S(1)}, bf16[16,4096]{1,0:T(8,128)(2,1)S(1)}, u32[]{:S(2)}, u32[]{:S(2)}) collective-permute-start(bf16[16,4096]{1,0:T(8,128)(2,1)S(1)} %copy-done.5), channel_id=1, source_target_pairs={{0,8},{1,9},{2,10},{3,11},{4,12},{5,13},{6,14},{7,15},{8,0},{9,1},... | collective-permute-start | bytes 393224 | tf_op jit(solution)/shard_map/ppermute | solution.py:31
  11.4 10.2 %collective-permute-start.6 = (bf16[16,4096]{1,0:T(8,128)(2,1)S(1)}, bf16[16,4096]{1,0:T(8,128)(2,1)S(1)}, u32[]{:S(2)}, u32[]{:S(2)}) collective-permute-start(bf16[16,4096]{1,0:T(8,128)(2,1)S(1)} %copy-done.5), channel_id=1, source_target_pairs={{0,4},{1,5},{2,6},{3,7},{4,0},{5,1},{6,2},{7,3},{8,12},{9,13},{10,... | collective-permute-start | bytes 393224 | tf_op jit(solution)/shard_map/ppermute | solution.py:31
  12.9 8.6 %collective-permute-start.8 = (bf16[16,4096]{1,0:T(8,128)(2,1)S(1)}, bf16[16,4096]{1,0:T(8,128)(2,1)S(1)}, u32[]{:S(2)}, u32[]{:S(2)}) collective-permute-start(bf16[16,4096]{1,0:T(8,128)(2,1)S(1)} %copy-done.5), channel_id=1, source_target_pairs={{0,12},{1,13},{2,14},{3,15},{4,8},{5,9},{6,10},{7,11},{8,4},{9,5},... | collective-permute-start | bytes 393224 | tf_op jit(solution)/shard_map/ppermute | solution.py:31
  13.2 15.7 %collective-permute-start.2 = (bf16[32,8320]{1,0:T(8,128)(2,1)S(1)}, bf16[32,8320]{1,0:T(8,128)(2,1)S(1)}, u32[]{:S(2)}, u32[]{:S(2)}) collective-permute-start(bf16[32,8320]{1,0:T(8,128)(2,1)S(1)} %shard_map.86.refs_0_), channel_id=1, source_target_pairs={{0,2},{1,3},{2,0},{3,1},{4,6},{5,7},{6,4},{7,5},{8,10},{9,11},{10,... | collective-permute-start | bytes 1597448 | tf_op jit(solution)/shard_map/ppermute | solution.py:31
  21.6 17.7 %collective-permute-start.10 = (bf16[64,4096]{1,0:T(8,128)(2,1)S(1)}, bf16[64,4096]{1,0:T(8,128)(2,1)S(1)}, u32[]{:S(2)}, u32[]{:S(2)}) collective-permute-start(bf16[64,4096]{1,0:T(8,128)(2,1)S(1)} %shard_map.89.refs_0_.__0_), channel_id=1, source_target_pairs={{0,2},{1,3},{2,0},{3,1},{4,6},{5,7},{6,4},{7,5},{8,10},{9,11},{10,... | collective-permute-start | bytes 1572872 | tf_op jit(solution)/shard_map/ppermute | solution.py:31
  22.2 8.0 %collective-permute-start.11 = (bf16[16,4096]{1,0:T(8,128)(2,1)S(1)}, bf16[16,4096]{1,0:T(8,128)(2,1)S(1)}, u32[]{:S(2)}, u32[]{:S(2)}) collective-permute-start(bf16[16,4096]{1,0:T(8,128)(2,1)S(1)} %get-tuple-element.26), channel_id=1, source_target_pairs={{0,4},{1,5},{2,6},{3,7},{4,0},{5,1},{6,2},{7,3},{8,12},{9,13},{10,... | collective-permute-start | bytes 393224 | tf_op jit(solution)/shard_map/ppermute | solution.py:31
  24.5 12.2 %collective-permute-start.12 = (bf16[16,4096]{1,0:T(8,128)(2,1)S(1)}, bf16[16,4096]{1,0:T(8,128)(2,1)S(1)}, u32[]{:S(2)}, u32[]{:S(2)}) collective-permute-start(bf16[16,4096]{1,0:T(8,128)(2,1)S(1)} %get-tuple-element.27), channel_id=1, source_target_pairs={{0,8},{1,9},{2,10},{3,11},{4,12},{5,13},{6,14},{7,15},{8,0},{9,1},... | collective-permute-start | bytes 393224 | tf_op jit(solution)/shard_map/ppermute | solution.py:31
  26.5 10.3 %collective-permute-start.13 = (bf16[16,4096]{1,0:T(8,128)(2,1)S(1)}, bf16[16,4096]{1,0:T(8,128)(2,1)S(1)}, u32[]{:S(2)}, u32[]{:S(2)}) collective-permute-start(bf16[16,4096]{1,0:T(8,128)(2,1)S(1)} %get-tuple-element.28), channel_id=1, source_target_pairs={{0,12},{1,13},{2,14},{3,15},{4,8},{5,9},{6,10},{7,11},{8,4},{9,5},... | collective-permute-start | bytes 393224 | tf_op jit(solution)/shard_map/ppermute | solution.py:31
  39.4 9.9 %collective-permute-start.14 = (bf16[64,4096]{1,0:T(8,128)(2,1)S(1)}, bf16[64,4096]{1,0:T(8,128)(2,1)S(1)}, u32[]{:S(2)}, u32[]{:S(2)}) collective-permute-start(bf16[64,4096]{1,0:T(8,128)(2,1)S(1)} %shard_map.93), channel_id=1, source_target_pairs={{0,1},{1,0},{2,3},{3,2},{4,5},{5,4},{6,7},{7,6},{8,9},{9,8},{10,11... | collective-permute-start | bytes 1572872 | tf_op jit(solution)/shard_map/ppermute | solution.py:31
  39.5 9.8 %collective-permute-start.15 = (bf16[64,4096]{1,0:T(8,128)(2,1)S(1)}, bf16[64,4096]{1,0:T(8,128)(2,1)S(1)}, u32[]{:S(2)}, u32[]{:S(2)}) collective-permute-start(bf16[64,4096]{1,0:T(8,128)(2,1)S(1)} %shard_map.92.refs_0_), channel_id=1, source_target_pairs={{0,1},{1,0},{2,3},{3,2},{4,5},{5,4},{6,7},{7,6},{8,9},{9,8},{10,11... | collective-permute-start | bytes 1572872 | tf_op jit(solution)/shard_map/ppermute | solution.py:31
  40.0 5.9 %collective-permute-start.16 = (bf16[16,4096]{1,0:T(8,128)(2,1)S(1)}, bf16[16,4096]{1,0:T(8,128)(2,1)S(1)}, u32[]{:S(2)}, u32[]{:S(2)}) collective-permute-start(bf16[16,4096]{1,0:T(8,128)(2,1)S(1)} %shard_map.91.__1_.refs_0_.refs_2_), channel_id=1, source_target_pairs={{0,16},{16,0},{1,17},{17,1},{2,18},{18,2},{3,19},{19,3},{4,20},{20... | collective-permute-start | bytes 393224 | tf_op jit(solution)/shard_map/ppermute | solution.py:31
  41.7 32.2 %collective-permute-start.3 = (bf16[64,2176]{1,0:T(8,128)(2,1)S(1)}, bf16[64,2176]{1,0:T(8,128)(2,1)S(1)}, u32[]{:S(2)}, u32[]{:S(2)}) collective-permute-start(bf16[64,2176]{1,0:T(8,128)(2,1)S(1)} %get-tuple-element.21), channel_id=1, source_target_pairs={{0,4},{1,5},{2,6},{3,7},{4,0},{5,1},{6,2},{7,3},{8,12},{9,13},{10,... | collective-permute-start | bytes 835592 | tf_op jit(solution)/shard_map/ppermute | solution.py:31
  43.3 30.6 %collective-permute-start.4 = (bf16[64,2176]{1,0:T(8,128)(2,1)S(1)}, bf16[64,2176]{1,0:T(8,128)(2,1)S(1)}, u32[]{:S(2)}, u32[]{:S(2)}) collective-permute-start(bf16[64,2176]{1,0:T(8,128)(2,1)S(1)} %get-tuple-element.22), channel_id=1, source_target_pairs={{0,8},{1,9},{2,10},{3,11},{4,12},{5,13},{6,14},{7,15},{8,0},{9,1},... | collective-permute-start | bytes 835592 | tf_op jit(solution)/shard_map/ppermute | solution.py:31
  45.9 28.1 %collective-permute-start.5 = (bf16[64,2176]{1,0:T(8,128)(2,1)S(1)}, bf16[64,2176]{1,0:T(8,128)(2,1)S(1)}, u32[]{:S(2)}, u32[]{:S(2)}) collective-permute-start(bf16[64,2176]{1,0:T(8,128)(2,1)S(1)} %get-tuple-element.23), channel_id=1, source_target_pairs={{0,12},{1,13},{2,14},{3,15},{4,8},{5,9},{6,10},{7,11},{8,4},{9,5},... | collective-permute-start | bytes 835592 | tf_op jit(solution)/shard_map/ppermute | solution.py:31
  49.4 2.2 %collective-permute-start.18 = (bf16[16,4096]{1,0:T(8,128)(2,1)S(1)}, bf16[16,4096]{1,0:T(8,128)(2,1)S(1)}, u32[]{:S(2)}, u32[]{:S(2)}) collective-permute-start(bf16[16,4096]{1,0:T(8,128)(2,1)S(1)} %collective-permute-done.16.refs_1_.refs_4_), channel_id=1, source_target_pairs={{0,1},{1,0},{2,3},{3,2},{4,5},{5,4},{6,7},{7,6},{8,9},{9,8},{10,11... | collective-permute-start | bytes 393224 | tf_op jit(solution)/shard_map/ppermute | solution.py:31
  77.0 3.1 %collective-permute-start.21 = (f32[2,8,1]{2,1,0:T(8,128)S(1)}, f32[2,8,1]{2,1,0:T(8,128)S(1)}, u32[]{:S(2)}, u32[]{:S(2)}) collective-permute-start(f32[2,8,1]{2,1,0:T(8,128)S(1)} %shard_map.96), channel_id=1, source_target_pairs={{0,3},{1,2},{2,1},{3,0},{4,7},{5,6},{6,5},{7,4},{8,11},{9,10},{10,... | collective-permute-start | bytes 200 | tf_op jit(solution)/shard_map/ppermute | solution.py:31
  78.2 3.7 %collective-permute-start.20 = (f32[2,8,1]{2,1,0:T(8,128)S(1)}, f32[2,8,1]{2,1,0:T(8,128)S(1)}, u32[]{:S(2)}, u32[]{:S(2)}) collective-permute-start(f32[2,8,1]{2,1,0:T(8,128)S(1)} %shard_map.96), channel_id=1, source_target_pairs={{0,2},{1,3},{2,0},{3,1},{4,6},{5,7},{6,4},{7,5},{8,10},{9,11},{10,... | collective-permute-start | bytes 200 | tf_op jit(solution)/shard_map/ppermute | solution.py:31
  78.7 3.1 %collective-permute-start.19 = (f32[2,8,1]{2,1,0:T(8,128)S(1)}, f32[2,8,1]{2,1,0:T(8,128)S(1)}, u32[]{:S(2)}, u32[]{:S(2)}) collective-permute-start(f32[2,8,1]{2,1,0:T(8,128)S(1)} %shard_map.96), channel_id=1, source_target_pairs={{0,1},{1,0},{2,3},{3,2},{4,5},{5,4},{6,7},{7,6},{8,9},{9,8},{10,11... | collective-permute-start | bytes 200 | tf_op jit(solution)/shard_map/ppermute | solution.py:31
  81.8 5.5 %collective-permute-start.24 = (f32[2,8,1]{2,1,0:T(8,128)S(1)}, f32[2,8,1]{2,1,0:T(8,128)S(1)}, u32[]{:S(2)}, u32[]{:S(2)}) collective-permute-start(f32[2,8,1]{2,1,0:T(8,128)S(1)} %add_add_fusion), channel_id=1, source_target_pairs={{0,12},{1,13},{2,14},{3,15},{4,8},{5,9},{6,10},{7,11},{8,4},{9,5},... | collective-permute-start | bytes 200 | tf_op jit(solution)/shard_map/ppermute | solution.py:31
  82.3 5.1 %collective-permute-start.23 = (f32[2,8,1]{2,1,0:T(8,128)S(1)}, f32[2,8,1]{2,1,0:T(8,128)S(1)}, u32[]{:S(2)}, u32[]{:S(2)}) collective-permute-start(f32[2,8,1]{2,1,0:T(8,128)S(1)} %add_add_fusion), channel_id=1, source_target_pairs={{0,8},{1,9},{2,10},{3,11},{4,12},{5,13},{6,14},{7,15},{8,0},{9,1},... | collective-permute-start | bytes 200 | tf_op jit(solution)/shard_map/ppermute | solution.py:31
  82.9 5.0 %collective-permute-start.22 = (f32[2,8,1]{2,1,0:T(8,128)S(1)}, f32[2,8,1]{2,1,0:T(8,128)S(1)}, u32[]{:S(2)}, u32[]{:S(2)}) collective-permute-start(f32[2,8,1]{2,1,0:T(8,128)S(1)} %add_add_fusion), channel_id=1, source_target_pairs={{0,4},{1,5},{2,6},{3,7},{4,0},{5,1},{6,2},{7,3},{8,12},{9,13},{10,... | collective-permute-start | bytes 200 | tf_op jit(solution)/shard_map/ppermute | solution.py:31
  (9 other events, 74.8 us)

commit v16 on v15

--- a/solution.py
+++ b/solution.py
@@ -13,6 +13,7 @@
 SEQ_MEAN = 32
 QT = 16
 LANES = 128
+SCORE_SCALE = 1.0 / math.sqrt(FF * D * QT * SEQ_MEAN)
 
 
 damping = 0.1
@@ -290,16 +291,18 @@
     @pl.when(s == 0)
     def _():
         side = right_ref.shape[2] // 2
+        right_ref[...] = jnp.zeros_like(right_ref)
+        turn_ref[...] = jnp.zeros_like(turn_ref)
         for b in range(batch_count):
             for other in range(2):
                 at = pl.multiple_of(((lax.axis_index("wide") & 1) ^ other) * side, side)
                 ref = half_refs[2 * b + other]
-                right_ref[b, :, pl.ds(at, side)] = ref[:, ref.shape[1] - side:]
+                right_ref[b, :QT, pl.ds(at, side)] = ref[:, ref.shape[1] - side:]
 
     @pl.when(jnp.logical_and(lax.rem(s, per) == 0, s < total))
     def _():
         for b in range(batch_count):
-            turn_ref[b] = left_refs[b][...].T
+            turn_ref[b, :, :QT] = left_refs[b][...].T
 
     @pl.when(lax.rem(s, per) == 1)
     def _():
@@ -367,13 +370,13 @@
         out_specs=pl.BlockSpec((batch_count, rows, tokens), lambda s: (0, before(s) // per, 0)),
         out_shape=jax.ShapeDtypeStruct((batch_count, hidden, tokens), jnp.float32),
         scratch_shapes=[
-            pltpu.VMEM((batch_count, QT, width), jnp.bfloat16),
-            pltpu.VMEM((batch_count, rows, QT), jnp.bfloat16),
+            pltpu.VMEM((batch_count, LANES, width), jnp.bfloat16),
+            pltpu.VMEM((batch_count, rows, LANES), jnp.bfloat16),
             pltpu.VMEM((batch_count * rows, chunk), jnp.bfloat16),
             pltpu.VMEM((batch_count * rows, chunk), jnp.bfloat16),
         ],
         compiler_params=params(32 if tokens <= 256 else 48),
-        cost_estimate=pl.CostEstimate(flops=0, bytes_accessed=1, transcendentals=0),
+        cost_estimate=pl.CostEstimate(flops=10**9, bytes_accessed=1, transcendentals=0),
     )(rot, *lefts, *halves, eigenvalues)
 
 
@@ -405,7 +408,7 @@
         own = lax.rem(lax.axis_index("groups"), batch_count)
         for b in range(batch_count):
             sums = jnp.sum(member * token_ref[b:b + 1, :], axis=1, keepdims=True)
-            out_ref[lax.rem(own + b, batch_count)] = sums[:out_ref.shape[1], :]
+            out_ref[lax.rem(own + b, batch_count)] = sums[:out_ref.shape[1], :] * SCORE_SCALE
 
 
 def score_parts(grad_pieces, ranks, grad_basis, image, seq_count):
@@ -444,7 +447,6 @@
     cols = grad_basis.shape[1]
     hidden = train_grad.shape[1]
     batch_count = owners.shape[0]
-    score_scale = 1.0 / math.sqrt(FF * D * QT * SEQ_MEAN)
 
     half = (query_factors.shape[2] - hidden) // 2
     order = [4 * k + r for r in (0, 2, 1, 3) for k in along_z]
@@ -464,21 +466,20 @@
     parts = [swap(parts[k], "wide", 4 * k) if k else parts[0] for k in along_z]
     held = pick_one(flags, parts, [over, first, sent[0]])
 
-    lefts = [held, swap(held, "groups", 1)]
+    over = gate(over, [held])
+    rot = rotate([over, swap(gate(acts, [held]), "wide", 1), swap(over, "wide", 1)], act_basis, None, first)
+    ranks = [r + more for more in (0, 2, 1, 3) for r in ranks]
+    lefts = [held, gate(swap(held, "groups", 1), [rot])]
     halves = []
     for x in lefts:
         halves += [x, swap(x, "wide", 1)]
-    over = gate(over, [held])
-    rot = rotate([over, swap(gate(acts, [held]), "wide", 1), swap(over, "wide", 1)], act_basis, None, first)
-    ranks = [r + more for more in (0, 2, 1, 3) for r in ranks]
-
     grads = [swap(sent[k], "wide", 4 * k) if k else sent[0] for k in along_z]
 
     image = images(rot, lefts, halves, eigenvalues)
     parts = score_parts(grads, ranks, grad_basis, image, seq_count)
     for step, count in ((1, 4), (4, wide_count // 4)):
         parts = parts + sum(swap(parts, "wide", step * n) for n in range(1, count))
-    return parts[:, :, 0].T * score_scale
+    return parts[:, :, 0].T
 
 
 def solution(mesh):

time: 88.7 us -> 89 us (level)
  waiting for transfers between devices: 22.9 us -> 26.1 us
  starting transfers between devices: 31.4 us -> 28.4 us
    ppermute x25, waiting for transfers between devices: 22.9 us -> 26.1 us  [swap(): return lax.ppermute(x, axis, [(i, i ^ bit) for i in range(count)])]
    ppermute x25, starting transfers between devices: 31.4 us -> 28.4 us  [swap(): return lax.ppermute(x, axis, [(i, i ^ bit) for i in range(count)])]
  transfers between devices with their start and end apart: 25 -> 25, of which waited for: 9 -> 10; matrix products, arithmetic and copies ran while one was open for 0% -> 0% of each run, Pallas kernels for 30% -> 30%
where the time goes in v16:
time: 89 us; the launch traced here: 88.8 us
  Pallas kernels  29.8 us (33%)
  starting transfers between devices  28.4 us (32%)
  waiting for transfers between devices  26.1 us (29%)
  local copies, waits for them, and re-layouts  3.66 us (4%)
    ppermute x25, starting transfers between devices, swap(): return lax.ppermute(x, axis, [(i, i ^ bit) for i in range(count)])  28.4 us
    ppermute x25, waiting for transfers between devices, swap(): return lax.ppermute(x, axis, [(i, i ^ bit) for i in range(count)])  26.1 us
    pallas_call x1, Pallas kernels, images(): pl.pallas_call(functools.partial(image_kernel, batch_count, total, per),...  22.4 us
    unnamed x16, local copies, waits for them, and re-layouts  3.66 us
    pallas_call x1, Pallas kernels, score_parts(): pl.pallas_call(functools.partial(score_kernel, batch_count, ranks, count)...  2.98 us
    pallas_call x2, Pallas kernels, rotate(): pl.pallas_call(functools.partial(rotate_kernel, len(act_pieces), done), i...  2.64 us
  transfers between devices with their start and end apart: 25, of which 10 were waited for; matrix products, arithmetic and copies ran while one was open for 0% of the time, Pallas kernels for 30%

profile of v16, /device:TPU:0, one launch (start us, length us, event | category | flops | bytes accessed | tf_op | source)
XLA Modules:
  0.0 88.8 jit_solution(382624686305470882)
XLA Ops:
  0.0 1.8 %copy-done.3 = bf16[2,16,36864]{2,1,0:T(8,128)(2,1)S(1)} copy-done((bf16[2,16,36864]{2,1,0:T(8,128)(2,1)S(1)}, bf16[2,16,36864]{2,1,0:T(8,128)(2,1)}, u32[]{:S(2)}) %copy-start.3) | copy-done | bytes 2359320
  2.4 1.2 %copy-done.1 = bf16[16,32768]{1,0:T(8,128)(2,1)S(1)} copy-done((bf16[16,32768]{1,0:T(8,128)(2,1)S(1)}, bf16[16,32768]{1,0:T(8,128)(2,1)}, u32[]{:S(2)}) %copy-start.1) | copy-done | bytes 1048600
  5.7 3.0 %collective-permute-start.9 = (bf16[16,10240]{1,0:T(8,128)(2,1)S(1)}, bf16[16,10240]{1,0:T(8,128)(2,1)S(1)}, u32[]{:S(2)}, u32[]{:S(2)}) collective-permute-start(bf16[16,10240]{1,0:T(8,128)(2,1)S(1)} %get-tuple-element.19._), channel_id=1, source_target_pairs={{0,2},{1,3},{2,0},{3,1},{4,6},{5,7},{6,4},{7,5},{8,10},{9,11},{10,... | collective-permute-start | bytes 983048 | tf_op jit(solution)/shard_map/ppermute | solution.py:32
  8.8 2.6 %collective-permute-start.7 = (bf16[16,4096]{1,0:T(8,128)(2,1)S(1)}, bf16[16,4096]{1,0:T(8,128)(2,1)S(1)}, u32[]{:S(2)}, u32[]{:S(2)}) collective-permute-start(bf16[16,4096]{1,0:T(8,128)(2,1)S(1)} %copy-done.5), channel_id=1, source_target_pairs={{0,8},{1,9},{2,10},{3,11},{4,12},{5,13},{6,14},{7,15},{8,0},{9,1},... | collective-permute-start | bytes 393224 | tf_op jit(solution)/shard_map/ppermute | solution.py:32
  11.4 1.6 %collective-permute-start.6 = (bf16[16,4096]{1,0:T(8,128)(2,1)S(1)}, bf16[16,4096]{1,0:T(8,128)(2,1)S(1)}, u32[]{:S(2)}, u32[]{:S(2)}) collective-permute-start(bf16[16,4096]{1,0:T(8,128)(2,1)S(1)} %copy-done.5), channel_id=1, source_target_pairs={{0,4},{1,5},{2,6},{3,7},{4,0},{5,1},{6,2},{7,3},{8,12},{9,13},{10,... | collective-permute-start | bytes 393224 | tf_op jit(solution)/shard_map/ppermute | solution.py:32
  13.6 3.7 %collective-permute-done.9.got_ref = bf16[16,10240]{1,0:T(8,128)(2,1)S(1)} collective-permute-done((bf16[16,10240]{1,0:T(8,128)(2,1)S(1)}, bf16[16,10240]{1,0:T(8,128)(2,1)S(1)}, u32[]{:S(2)}, u32[]{:S(2)}) %collective-permute-start.9) | collective-permute-done | bytes 327712 | tf_op jit(solution)/shard_map/ppermute | solution.py:32
  17.4 4.2 %collective-permute-done.7.refs_2_ = bf16[16,4096]{1,0:T(8,128)(2,1)S(1)} collective-permute-done((bf16[16,4096]{1,0:T(8,128)(2,1)S(1)}, bf16[16,4096]{1,0:T(8,128)(2,1)S(1)}, u32[]{:S(2)}, u32[]{:S(2)}) %collective-permute-start.7) | collective-permute-done | bytes 131104 | tf_op jit(solution)/shard_map/ppermute | solution.py:32
  22.2 2.4 %collective-permute-start.11 = (bf16[16,4096]{1,0:T(8,128)(2,1)S(1)}, bf16[16,4096]{1,0:T(8,128)(2,1)S(1)}, u32[]{:S(2)}, u32[]{:S(2)}) collective-permute-start(bf16[16,4096]{1,0:T(8,128)(2,1)S(1)} %get-tuple-element.26), channel_id=1, source_target_pairs={{0,4},{1,5},{2,6},{3,7},{4,0},{5,1},{6,2},{7,3},{8,12},{9,13},{10,... | collective-permute-start | bytes 393224 | tf_op jit(solution)/shard_map/ppermute | solution.py:32
  24.5 1.9 %collective-permute-start.12 = (bf16[16,4096]{1,0:T(8,128)(2,1)S(1)}, bf16[16,4096]{1,0:T(8,128)(2,1)S(1)}, u32[]{:S(2)}, u32[]{:S(2)}) collective-permute-start(bf16[16,4096]{1,0:T(8,128)(2,1)S(1)} %get-tuple-element.27), channel_id=1, source_target_pairs={{0,8},{1,9},{2,10},{3,11},{4,12},{5,13},{6,14},{7,15},{8,0},{9,1},... | collective-permute-start | bytes 393224 | tf_op jit(solution)/shard_map/ppermute | solution.py:32
  26.5 1.5 %collective-permute-start.13 = (bf16[16,4096]{1,0:T(8,128)(2,1)S(1)}, bf16[16,4096]{1,0:T(8,128)(2,1)S(1)}, u32[]{:S(2)}, u32[]{:S(2)}) collective-permute-start(bf16[16,4096]{1,0:T(8,128)(2,1)S(1)} %get-tuple-element.28), channel_id=1, source_target_pairs={{0,12},{1,13},{2,14},{3,15},{4,8},{5,9},{6,10},{7,11},{8,4},{9,5},... | collective-permute-start | bytes 393224 | tf_op jit(solution)/shard_map/ppermute | solution.py:32
  29.0 1.2 %collective-permute-done.11.refs_1_ = bf16[16,4096]{1,0:T(8,128)(2,1)S(1)} collective-permute-done((bf16[16,4096]{1,0:T(8,128)(2,1)S(1)}, bf16[16,4096]{1,0:T(8,128)(2,1)S(1)}, u32[]{:S(2)}, u32[]{:S(2)}) %collective-permute-start.11) | collective-permute-done | bytes 131104 | tf_op jit(solution)/shard_map/ppermute | solution.py:32
  30.1 6.6 %collective-permute-done.12.refs_2_ = bf16[16,4096]{1,0:T(8,128)(2,1)S(1)} collective-permute-done((bf16[16,4096]{1,0:T(8,128)(2,1)S(1)}, bf16[16,4096]{1,0:T(8,128)(2,1)S(1)}, u32[]{:S(2)}, u32[]{:S(2)}) %collective-permute-start.12) | collective-permute-done | bytes 131104 | tf_op jit(solution)/shard_map/ppermute | solution.py:32
  36.8 2.5 %collective-permute-done.10.refs_4_.__0_ = bf16[64,4096]{1,0:T(8,128)(2,1)S(1)} collective-permute-done((bf16[64,4096]{1,0:T(8,128)(2,1)S(1)}, bf16[64,4096]{1,0:T(8,128)(2,1)S(1)}, u32[]{:S(2)}, u32[]{:S(2)}) %collective-permute-start.10) | collective-permute-done | bytes 524320 | tf_op jit(solution)/shard_map/ppermute | solution.py:32
  40.0 1.7 %collective-permute-start.16 = (bf16[16,4096]{1,0:T(8,128)(2,1)S(1)}, bf16[16,4096]{1,0:T(8,128)(2,1)S(1)}, u32[]{:S(2)}, u32[]{:S(2)}) collective-permute-start(bf16[16,4096]{1,0:T(8,128)(2,1)S(1)} %shard_map.91.__1_.refs_0_.refs_2_), channel_id=1, source_target_pairs={{0,16},{16,0},{1,17},{17,1},{2,18},{18,2},{3,19},{19,3},{4,20},{20... | collective-permute-start | bytes 393224 | tf_op jit(solution)/shard_map/ppermute | solution.py:32
  41.7 1.6 %collective-permute-start.3 = (bf16[64,2176]{1,0:T(8,128)(2,1)S(1)}, bf16[64,2176]{1,0:T(8,128)(2,1)S(1)}, u32[]{:S(2)}, u32[]{:S(2)}) collective-permute-start(bf16[64,2176]{1,0:T(8,128)(2,1)S(1)} %get-tuple-element.21), channel_id=1, source_target_pairs={{0,4},{1,5},{2,6},{3,7},{4,0},{5,1},{6,2},{7,3},{8,12},{9,13},{10,... | collective-permute-start | bytes 835592 | tf_op jit(solution)/shard_map/ppermute | solution.py:32
  43.3 2.6 %collective-permute-start.4 = (bf16[64,2176]{1,0:T(8,128)(2,1)S(1)}, bf16[64,2176]{1,0:T(8,128)(2,1)S(1)}, u32[]{:S(2)}, u32[]{:S(2)}) collective-permute-start(bf16[64,2176]{1,0:T(8,128)(2,1)S(1)} %get-tuple-element.22), channel_id=1, source_target_pairs={{0,8},{1,9},{2,10},{3,11},{4,12},{5,13},{6,14},{7,15},{8,0},{9,1},... | collective-permute-start | bytes 835592 | tf_op jit(solution)/shard_map/ppermute | solution.py:32
  46.1 1.7 %shard_map.94.__1_.rot_ref = bf16[4096,256]{1,0:T(8,128)(2,1)S(1)} custom-call(bf16[64,4096]{1,0:T(8,128)(2,1)S(1)} %shard_map.92.refs_0_, bf16[64,4096]{1,0:T(8,128)(2,1)S(1)} %collective-permute-done.14.refs_1_, bf16[64,4096]{1,0:T(8,128)(2,1)S(1)} %collective-permute-done.15.refs_2_, bf16[512,4096]{1,0:T(8,128)(2,1)S(1)} %copy-done, ...), custom_call_target="tpu_custom_call" | custom-call | bytes 1 | tf_op jit(solution)/shard_map/pallas_call | solution.py:274
  49.4 22.4 %shard_map.96.refs_9_ = f32[2,2048,256]{2,1,0:T(8,128)S(1)} custom-call(bf16[4096,256]{1,0:T(8,128)(2,1)S(1)} %shard_map.94.__1_.rot_ref, bf16[16,4096]{1,0:T(8,128)(2,1)S(1)} %shard_map.91.__1_.refs_0_.refs_2_, bf16[16,4096]{1,0:T(8,128)(2,1)S(1)} %shard_map.95.refs_1_.refs_4_, bf16[16,4096]{1,0:T(8,128)(2,1)S(1)} %shard_map.91.__1_.refs_0_.refs_2_, ...), custom_call_target="tpu_custom_call" | custom-call | flops 1000000000 | bytes 1 | tf_op jit(solution)/shard_map/pallas_call | solution.py:363
  71.8 3.0 %shard_map.97 = f32[2,8,1]{2,1,0:T(8,128)S(1)} custom-call(bf16[64,2176]{1,0:T(8,128)(2,1)S(1)} %get-tuple-element.20.refs_6_.refs_0_.refs_4_, bf16[64,2176]{1,0:T(8,128)(2,1)S(1)} %collective-permute-done.3.refs_1_.refs_5_, bf16[64,2176]{1,0:T(8,128)(2,1)S(1)} %collective-permute-done.4.refs_2_.refs_6_, ...), custom_call_target="tpu_custom_call" | custom-call | flops 536870912 | bytes 4194304 | tf_op jit(solution)/shard_map/pallas_call | solution.py:419
  74.8 1.5 %collective-permute-start.21 = (f32[2,8,1]{2,1,0:T(8,128)S(1)}, f32[2,8,1]{2,1,0:T(8,128)S(1)}, u32[]{:S(2)}, u32[]{:S(2)}) collective-permute-start(f32[2,8,1]{2,1,0:T(8,128)S(1)} %shard_map.97), channel_id=1, source_target_pairs={{0,3},{1,2},{2,1},{3,0},{4,7},{5,6},{6,5},{7,4},{8,11},{9,10},{10,... | collective-permute-start | bytes 200 | tf_op jit(solution)/shard_map/ppermute | solution.py:32
  76.8 1.1 %collective-permute-done.21 = f32[2,8,1]{2,1,0:T(8,128)S(1)} collective-permute-done((f32[2,8,1]{2,1,0:T(8,128)S(1)}, f32[2,8,1]{2,1,0:T(8,128)S(1)}, u32[]{:S(2)}, u32[]{:S(2)}) %collective-permute-start.21) | collective-permute-done | bytes 96 | tf_op jit(solution)/shard_map/ppermute | solution.py:32
  77.9 2.1 %collective-permute-done.20 = f32[2,8,1]{2,1,0:T(8,128)S(1)} collective-permute-done((f32[2,8,1]{2,1,0:T(8,128)S(1)}, f32[2,8,1]{2,1,0:T(8,128)S(1)}, u32[]{:S(2)}, u32[]{:S(2)}) %collective-permute-start.20) | collective-permute-done | bytes 96 | tf_op jit(solution)/shard_map/ppermute | solution.py:32
  80.0 3.7 %collective-permute-start.24 = (f32[2,8,1]{2,1,0:T(8,128)S(1)}, f32[2,8,1]{2,1,0:T(8,128)S(1)}, u32[]{:S(2)}, u32[]{:S(2)}) collective-permute-start(f32[2,8,1]{2,1,0:T(8,128)S(1)} %add_add_fusion), channel_id=1, source_target_pairs={{0,12},{1,13},{2,14},{3,15},{4,8},{5,9},{6,10},{7,11},{8,4},{9,5},... | collective-permute-start | bytes 200 | tf_op jit(solution)/shard_map/ppermute | solution.py:32
  85.5 2.7 %collective-permute-done.23 = f32[2,8,1]{2,1,0:T(8,128)S(1)} collective-permute-done((f32[2,8,1]{2,1,0:T(8,128)S(1)}, f32[2,8,1]{2,1,0:T(8,128)S(1)}, u32[]{:S(2)}, u32[]{:S(2)}) %collective-permute-start.23) | collective-permute-done | bytes 96 | tf_op jit(solution)/shard_map/ppermute | solution.py:32
  (60 shorter events, 10.6 us)
Async XLA Ops:
  1.8 3.7 %collective-permute-start.1 = (bf16[16,18432]{1,0:T(8,128)(2,1)S(1)}, bf16[16,18432]{1,0:T(8,128)(2,1)S(1)}, u32[]{:S(2)}, u32[]{:S(2)}) collective-permute-start(bf16[16,18432]{1,0:T(8,128)(2,1)S(1)} %get-tuple-element.18), channel_id=1, source_target_pairs={{0,1},{1,0},{2,3},{3,2},{4,5},{5,4},{6,7},{7,6},{8,9},{9,8},{10,11... | collective-permute-start | bytes 1769480 | tf_op jit(solution)/shard_map/ppermute | solution.py:32
  4.8 8.3 %collective-permute-start = (bf16[16,16512]{1,0:T(8,128)(2,1)S(1)}, bf16[16,16512]{1,0:T(8,128)(2,1)S(1)}, u32[]{:S(2)}, u32[]{:S(2)}) collective-permute-start(bf16[16,16512]{1,0:T(8,128)(2,1)S(1)} %shard_map.83.refs_0_.sent_ref), channel_id=1, source_target_pairs={{0,1},{1,0},{2,3},{3,2},{4,5},{5,4},{6,7},{7,6},{8,9},{9,8},{10,11... | collective-permute-start | bytes 1585160 | tf_op jit(solution)/shard_map/ppermute | solution.py:32
  5.7 11.5 %collective-permute-start.9 = (bf16[16,10240]{1,0:T(8,128)(2,1)S(1)}, bf16[16,10240]{1,0:T(8,128)(2,1)S(1)}, u32[]{:S(2)}, u32[]{:S(2)}) collective-permute-start(bf16[16,10240]{1,0:T(8,128)(2,1)S(1)} %get-tuple-element.19._), channel_id=1, source_target_pairs={{0,2},{1,3},{2,0},{3,1},{4,6},{5,7},{6,4},{7,5},{8,10},{9,11},{10,... | collective-permute-start | bytes 983048 | tf_op jit(solution)/shard_map/ppermute | solution.py:32
  8.8 12.8 %collective-permute-start.7 = (bf16[16,4096]{1,0:T(8,128)(2,1)S(1)}, bf16[16,4096]{1,0:T(8,128)(2,1)S(1)}, u32[]{:S(2)}, u32[]{:S(2)}) collective-permute-start(bf16[16,4096]{1,0:T(8,128)(2,1)S(1)} %copy-done.5), channel_id=1, source_target_pairs={{0,8},{1,9},{2,10},{3,11},{4,12},{5,13},{6,14},{7,15},{8,0},{9,1},... | collective-permute-start | bytes 393224 | tf_op jit(solution)/shard_map/ppermute | solution.py:32
  11.4 10.2 %collective-permute-start.6 = (bf16[16,4096]{1,0:T(8,128)(2,1)S(1)}, bf16[16,4096]{1,0:T(8,128)(2,1)S(1)}, u32[]{:S(2)}, u32[]{:S(2)}) collective-permute-start(bf16[16,4096]{1,0:T(8,128)(2,1)S(1)} %copy-done.5), channel_id=1, source_target_pairs={{0,4},{1,5},{2,6},{3,7},{4,0},{5,1},{6,2},{7,3},{8,12},{9,13},{10,... | collective-permute-start | bytes 393224 | tf_op jit(solution)/shard_map/ppermute | solution.py:32
  12.9 8.6 %collective-permute-start.8 = (bf16[16,4096]{1,0:T(8,128)(2,1)S(1)}, bf16[16,4096]{1,0:T(8,128)(2,1)S(1)}, u32[]{:S(2)}, u32[]{:S(2)}) collective-permute-start(bf16[16,4096]{1,0:T(8,128)(2,1)S(1)} %copy-done.5), channel_id=1, source_target_pairs={{0,12},{1,13},{2,14},{3,15},{4,8},{5,9},{6,10},{7,11},{8,4},{9,5},... | collective-permute-start | bytes 393224 | tf_op jit(solution)/shard_map/ppermute | solution.py:32
  13.2 15.7 %collective-permute-start.2 = (bf16[32,8320]{1,0:T(8,128)(2,1)S(1)}, bf16[32,8320]{1,0:T(8,128)(2,1)S(1)}, u32[]{:S(2)}, u32[]{:S(2)}) collective-permute-start(bf16[32,8320]{1,0:T(8,128)(2,1)S(1)} %shard_map.86.refs_0_), channel_id=1, source_target_pairs={{0,2},{1,3},{2,0},{3,1},{4,6},{5,7},{6,4},{7,5},{8,10},{9,11},{10,... | collective-permute-start | bytes 1597448 | tf_op jit(solution)/shard_map/ppermute | solution.py:32
  21.6 17.7 %collective-permute-start.10 = (bf16[64,4096]{1,0:T(8,128)(2,1)S(1)}, bf16[64,4096]{1,0:T(8,128)(2,1)S(1)}, u32[]{:S(2)}, u32[]{:S(2)}) collective-permute-start(bf16[64,4096]{1,0:T(8,128)(2,1)S(1)} %shard_map.89.refs_0_.__0_), channel_id=1, source_target_pairs={{0,2},{1,3},{2,0},{3,1},{4,6},{5,7},{6,4},{7,5},{8,10},{9,11},{10,... | collective-permute-start | bytes 1572872 | tf_op jit(solution)/shard_map/ppermute | solution.py:32
  22.2 8.0 %collective-permute-start.11 = (bf16[16,4096]{1,0:T(8,128)(2,1)S(1)}, bf16[16,4096]{1,0:T(8,128)(2,1)S(1)}, u32[]{:S(2)}, u32[]{:S(2)}) collective-permute-start(bf16[16,4096]{1,0:T(8,128)(2,1)S(1)} %get-tuple-element.26), channel_id=1, source_target_pairs={{0,4},{1,5},{2,6},{3,7},{4,0},{5,1},{6,2},{7,3},{8,12},{9,13},{10,... | collective-permute-start | bytes 393224 | tf_op jit(solution)/shard_map/ppermute | solution.py:32
  24.5 12.2 %collective-permute-start.12 = (bf16[16,4096]{1,0:T(8,128)(2,1)S(1)}, bf16[16,4096]{1,0:T(8,128)(2,1)S(1)}, u32[]{:S(2)}, u32[]{:S(2)}) collective-permute-start(bf16[16,4096]{1,0:T(8,128)(2,1)S(1)} %get-tuple-element.27), channel_id=1, source_target_pairs={{0,8},{1,9},{2,10},{3,11},{4,12},{5,13},{6,14},{7,15},{8,0},{9,1},... | collective-permute-start | bytes 393224 | tf_op jit(solution)/shard_map/ppermute | solution.py:32
  26.5 10.3 %collective-permute-start.13 = (bf16[16,4096]{1,0:T(8,128)(2,1)S(1)}, bf16[16,4096]{1,0:T(8,128)(2,1)S(1)}, u32[]{:S(2)}, u32[]{:S(2)}) collective-permute-start(bf16[16,4096]{1,0:T(8,128)(2,1)S(1)} %get-tuple-element.28), channel_id=1, source_target_pairs={{0,12},{1,13},{2,14},{3,15},{4,8},{5,9},{6,10},{7,11},{8,4},{9,5},... | collective-permute-start | bytes 393224 | tf_op jit(solution)/shard_map/ppermute | solution.py:32
  39.4 6.5 %collective-permute-start.14 = (bf16[64,4096]{1,0:T(8,128)(2,1)S(1)}, bf16[64,4096]{1,0:T(8,128)(2,1)S(1)}, u32[]{:S(2)}, u32[]{:S(2)}) collective-permute-start(bf16[64,4096]{1,0:T(8,128)(2,1)S(1)} %shard_map.93), channel_id=1, source_target_pairs={{0,1},{1,0},{2,3},{3,2},{4,5},{5,4},{6,7},{7,6},{8,9},{9,8},{10,11... | collective-permute-start | bytes 1572872 | tf_op jit(solution)/shard_map/ppermute | solution.py:32
  39.5 6.6 %collective-permute-start.15 = (bf16[64,4096]{1,0:T(8,128)(2,1)S(1)}, bf16[64,4096]{1,0:T(8,128)(2,1)S(1)}, u32[]{:S(2)}, u32[]{:S(2)}) collective-permute-start(bf16[64,4096]{1,0:T(8,128)(2,1)S(1)} %shard_map.92.refs_0_), channel_id=1, source_target_pairs={{0,1},{1,0},{2,3},{3,2},{4,5},{5,4},{6,7},{7,6},{8,9},{9,8},{10,11... | collective-permute-start | bytes 1572872 | tf_op jit(solution)/shard_map/ppermute | solution.py:32
  40.0 7.8 %collective-permute-start.16 = (bf16[16,4096]{1,0:T(8,128)(2,1)S(1)}, bf16[16,4096]{1,0:T(8,128)(2,1)S(1)}, u32[]{:S(2)}, u32[]{:S(2)}) collective-permute-start(bf16[16,4096]{1,0:T(8,128)(2,1)S(1)} %shard_map.91.__1_.refs_0_.refs_2_), channel_id=1, source_target_pairs={{0,16},{16,0},{1,17},{17,1},{2,18},{18,2},{3,19},{19,3},{4,20},{20... | collective-permute-start | bytes 393224 | tf_op jit(solution)/shard_map/ppermute | solution.py:32
  41.7 30.0 %collective-permute-start.3 = (bf16[64,2176]{1,0:T(8,128)(2,1)S(1)}, bf16[64,2176]{1,0:T(8,128)(2,1)S(1)}, u32[]{:S(2)}, u32[]{:S(2)}) collective-permute-start(bf16[64,2176]{1,0:T(8,128)(2,1)S(1)} %get-tuple-element.21), channel_id=1, source_target_pairs={{0,4},{1,5},{2,6},{3,7},{4,0},{5,1},{6,2},{7,3},{8,12},{9,13},{10,... | collective-permute-start | bytes 835592 | tf_op jit(solution)/shard_map/ppermute | solution.py:32
  43.3 28.5 %collective-permute-start.4 = (bf16[64,2176]{1,0:T(8,128)(2,1)S(1)}, bf16[64,2176]{1,0:T(8,128)(2,1)S(1)}, u32[]{:S(2)}, u32[]{:S(2)}) collective-permute-start(bf16[64,2176]{1,0:T(8,128)(2,1)S(1)} %get-tuple-element.22), channel_id=1, source_target_pairs={{0,8},{1,9},{2,10},{3,11},{4,12},{5,13},{6,14},{7,15},{8,0},{9,1},... | collective-permute-start | bytes 835592 | tf_op jit(solution)/shard_map/ppermute | solution.py:32
  45.9 25.9 %collective-permute-start.5 = (bf16[64,2176]{1,0:T(8,128)(2,1)S(1)}, bf16[64,2176]{1,0:T(8,128)(2,1)S(1)}, u32[]{:S(2)}, u32[]{:S(2)}) collective-permute-start(bf16[64,2176]{1,0:T(8,128)(2,1)S(1)} %get-tuple-element.23), channel_id=1, source_target_pairs={{0,12},{1,13},{2,14},{3,15},{4,8},{5,9},{6,10},{7,11},{8,4},{9,5},... | collective-permute-start | bytes 835592 | tf_op jit(solution)/shard_map/ppermute | solution.py:32
  46.1 2.3 %collective-permute-start.17 = (bf16[16,4096]{1,0:T(8,128)(2,1)S(1)}, bf16[16,4096]{1,0:T(8,128)(2,1)S(1)}, u32[]{:S(2)}, u32[]{:S(2)}) collective-permute-start(bf16[16,4096]{1,0:T(8,128)(2,1)S(1)} %shard_map.91.__1_.refs_0_.refs_2_), channel_id=1, source_target_pairs={{0,1},{1,0},{2,3},{3,2},{4,5},{5,4},{6,7},{7,6},{8,9},{9,8},{10,11... | collective-permute-start | bytes 393224 | tf_op jit(solution)/shard_map/ppermute | solution.py:32
  74.8 3.1 %collective-permute-start.21 = (f32[2,8,1]{2,1,0:T(8,128)S(1)}, f32[2,8,1]{2,1,0:T(8,128)S(1)}, u32[]{:S(2)}, u32[]{:S(2)}) collective-permute-start(f32[2,8,1]{2,1,0:T(8,128)S(1)} %shard_map.97), channel_id=1, source_target_pairs={{0,3},{1,2},{2,1},{3,0},{4,7},{5,6},{6,5},{7,4},{8,11},{9,10},{10,... | collective-permute-start | bytes 200 | tf_op jit(solution)/shard_map/ppermute | solution.py:32
  76.3 3.7 %collective-permute-start.20 = (f32[2,8,1]{2,1,0:T(8,128)S(1)}, f32[2,8,1]{2,1,0:T(8,128)S(1)}, u32[]{:S(2)}, u32[]{:S(2)}) collective-permute-start(f32[2,8,1]{2,1,0:T(8,128)S(1)} %shard_map.97), channel_id=1, source_target_pairs={{0,2},{1,3},{2,0},{3,1},{4,6},{5,7},{6,4},{7,5},{8,10},{9,11},{10,... | collective-permute-start | bytes 200 | tf_op jit(solution)/shard_map/ppermute | solution.py:32
  76.8 3.2 %collective-permute-start.19 = (f32[2,8,1]{2,1,0:T(8,128)S(1)}, f32[2,8,1]{2,1,0:T(8,128)S(1)}, u32[]{:S(2)}, u32[]{:S(2)}) collective-permute-start(f32[2,8,1]{2,1,0:T(8,128)S(1)} %shard_map.97), channel_id=1, source_target_pairs={{0,1},{1,0},{2,3},{3,2},{4,5},{5,4},{6,7},{7,6},{8,9},{9,8},{10,11... | collective-permute-start | bytes 200 | tf_op jit(solution)/shard_map/ppermute | solution.py:32
  80.0 5.5 %collective-permute-start.24 = (f32[2,8,1]{2,1,0:T(8,128)S(1)}, f32[2,8,1]{2,1,0:T(8,128)S(1)}, u32[]{:S(2)}, u32[]{:S(2)}) collective-permute-start(f32[2,8,1]{2,1,0:T(8,128)S(1)} %add_add_fusion), channel_id=1, source_target_pairs={{0,12},{1,13},{2,14},{3,15},{4,8},{5,9},{6,10},{7,11},{8,4},{9,5},... | collective-permute-start | bytes 200 | tf_op jit(solution)/shard_map/ppermute | solution.py:32
  83.6 4.5 %collective-permute-start.23 = (f32[2,8,1]{2,1,0:T(8,128)S(1)}, f32[2,8,1]{2,1,0:T(8,128)S(1)}, u32[]{:S(2)}, u32[]{:S(2)}) collective-permute-start(f32[2,8,1]{2,1,0:T(8,128)S(1)} %add_add_fusion), channel_id=1, source_target_pairs={{0,8},{1,9},{2,10},{3,11},{4,12},{5,13},{6,14},{7,15},{8,0},{9,1},... | collective-permute-start | bytes 200 | tf_op jit(solution)/shard_map/ppermute | solution.py:32
  83.6 4.5 %collective-permute-start.22 = (f32[2,8,1]{2,1,0:T(8,128)S(1)}, f32[2,8,1]{2,1,0:T(8,128)S(1)}, u32[]{:S(2)}, u32[]{:S(2)}) collective-permute-start(f32[2,8,1]{2,1,0:T(8,128)S(1)} %add_add_fusion), channel_id=1, source_target_pairs={{0,4},{1,5},{2,6},{3,7},{4,0},{5,1},{6,2},{7,3},{8,12},{9,13},{10,... | collective-permute-start | bytes 200 | tf_op jit(solution)/shard_map/ppermute | solution.py:32
  (9 other events, 75.6 us)

commit v17 on v16

--- a/solution.py
+++ b/solution.py
@@ -291,18 +291,16 @@
     @pl.when(s == 0)
     def _():
         side = right_ref.shape[2] // 2
-        right_ref[...] = jnp.zeros_like(right_ref)
-        turn_ref[...] = jnp.zeros_like(turn_ref)
         for b in range(batch_count):
             for other in range(2):
                 at = pl.multiple_of(((lax.axis_index("wide") & 1) ^ other) * side, side)
                 ref = half_refs[2 * b + other]
-                right_ref[b, :QT, pl.ds(at, side)] = ref[:, ref.shape[1] - side:]
+                right_ref[b, :, pl.ds(at, side)] = ref[:, ref.shape[1] - side:]
 
     @pl.when(jnp.logical_and(lax.rem(s, per) == 0, s < total))
     def _():
         for b in range(batch_count):
-            turn_ref[b, :, :QT] = left_refs[b][...].T
+            turn_ref[b] = left_refs[b][...].T
 
     @pl.when(lax.rem(s, per) == 1)
     def _():
@@ -370,8 +368,8 @@
         out_specs=pl.BlockSpec((batch_count, rows, tokens), lambda s: (0, before(s) // per, 0)),
         out_shape=jax.ShapeDtypeStruct((batch_count, hidden, tokens), jnp.float32),
         scratch_shapes=[
-            pltpu.VMEM((batch_count, LANES, width), jnp.bfloat16),
-            pltpu.VMEM((batch_count, rows, LANES), jnp.bfloat16),
+            pltpu.VMEM((batch_count, QT, width), jnp.bfloat16),
+            pltpu.VMEM((batch_count, rows, QT), jnp.bfloat16),
             pltpu.VMEM((batch_count * rows, chunk), jnp.bfloat16),
             pltpu.VMEM((batch_count * rows, chunk), jnp.bfloat16),
         ],
@@ -478,7 +476,7 @@
     image = images(rot, lefts, halves, eigenvalues)
     parts = score_parts(grads, ranks, grad_basis, image, seq_count)
     for step, count in ((1, 4), (4, wide_count // 4)):
-        parts = parts + sum(swap(parts, "wide", step * n) for n in range(1, count))
+        parts = parts + sum(swap(parts, "wide", step * n) for n in range(count - 1, 0, -1))
     return parts[:, :, 0].T
 
 

time: 89 us -> 89.9 us (1.010)
  waiting for transfers between devices: 26.1 us -> 27.6 us
    ppermute x25, waiting for transfers between devices: 26.1 us -> 27.6 us  [swap(): return lax.ppermute(x, axis, [(i, i ^ bit) for i in range(count)])]
  transfers between devices with their start and end apart: 25 -> 25, of which waited for: 10 -> 10; matrix products, arithmetic and copies ran while one was open for 0% -> 0% of each run, Pallas kernels for 30% -> 29%
where the time goes in v17:
time: 89.9 us; the launch traced here: 89.8 us
  Pallas kernels  29.4 us (33%)
  starting transfers between devices  28.2 us (31%)
  waiting for transfers between devices  27.6 us (31%)
  local copies, waits for them, and re-layouts  3.66 us (4%)
    ppermute x25, starting transfers between devices, swap(): return lax.ppermute(x, axis, [(i, i ^ bit) for i in range(count)])  28.2 us
    ppermute x25, waiting for transfers between devices, swap(): return lax.ppermute(x, axis, [(i, i ^ bit) for i in range(count)])  27.6 us
    pallas_call x1, Pallas kernels, images(): pl.pallas_call(functools.partial(image_kernel, batch_count, total, per),...  22 us
    unnamed x16, local copies, waits for them, and re-layouts  3.66 us
    pallas_call x1, Pallas kernels, score_parts(): pl.pallas_call(functools.partial(score_kernel, batch_count, ranks, count)...  2.98 us
    pallas_call x2, Pallas kernels, rotate(): pl.pallas_call(functools.partial(rotate_kernel, len(act_pieces), done), i...  2.64 us
  transfers between devices with their start and end apart: 25, of which 10 were waited for; matrix products, arithmetic and copies ran while one was open for 0% of the time, Pallas kernels for 29%

profile of v17, /device:TPU:0, one launch (start us, length us, event | category | flops | bytes accessed | tf_op | source)
XLA Modules:
  0.0 89.8 jit_solution(17515039622844997993)
XLA Ops:
  0.0 1.8 %copy-done.3 = bf16[2,16,36864]{2,1,0:T(8,128)(2,1)S(1)} copy-done((bf16[2,16,36864]{2,1,0:T(8,128)(2,1)S(1)}, bf16[2,16,36864]{2,1,0:T(8,128)(2,1)}, u32[]{:S(2)}) %copy-start.3) | copy-done | bytes 2359320
  2.4 1.2 %copy-done.1 = bf16[16,32768]{1,0:T(8,128)(2,1)S(1)} copy-done((bf16[16,32768]{1,0:T(8,128)(2,1)S(1)}, bf16[16,32768]{1,0:T(8,128)(2,1)}, u32[]{:S(2)}) %copy-start.1) | copy-done | bytes 1048600
  5.7 3.0 %collective-permute-start.9 = (bf16[16,10240]{1,0:T(8,128)(2,1)S(1)}, bf16[16,10240]{1,0:T(8,128)(2,1)S(1)}, u32[]{:S(2)}, u32[]{:S(2)}) collective-permute-start(bf16[16,10240]{1,0:T(8,128)(2,1)S(1)} %get-tuple-element.19._), channel_id=1, source_target_pairs={{0,2},{1,3},{2,0},{3,1},{4,6},{5,7},{6,4},{7,5},{8,10},{9,11},{10,... | collective-permute-start | bytes 983048 | tf_op jit(solution)/shard_map/ppermute | solution.py:32
  8.8 2.6 %collective-permute-start.7 = (bf16[16,4096]{1,0:T(8,128)(2,1)S(1)}, bf16[16,4096]{1,0:T(8,128)(2,1)S(1)}, u32[]{:S(2)}, u32[]{:S(2)}) collective-permute-start(bf16[16,4096]{1,0:T(8,128)(2,1)S(1)} %copy-done.5), channel_id=1, source_target_pairs={{0,8},{1,9},{2,10},{3,11},{4,12},{5,13},{6,14},{7,15},{8,0},{9,1},... | collective-permute-start | bytes 393224 | tf_op jit(solution)/shard_map/ppermute | solution.py:32
  11.4 1.6 %collective-permute-start.6 = (bf16[16,4096]{1,0:T(8,128)(2,1)S(1)}, bf16[16,4096]{1,0:T(8,128)(2,1)S(1)}, u32[]{:S(2)}, u32[]{:S(2)}) collective-permute-start(bf16[16,4096]{1,0:T(8,128)(2,1)S(1)} %copy-done.5), channel_id=1, source_target_pairs={{0,4},{1,5},{2,6},{3,7},{4,0},{5,1},{6,2},{7,3},{8,12},{9,13},{10,... | collective-permute-start | bytes 393224 | tf_op jit(solution)/shard_map/ppermute | solution.py:32
  13.6 3.7 %collective-permute-done.9.got_ref = bf16[16,10240]{1,0:T(8,128)(2,1)S(1)} collective-permute-done((bf16[16,10240]{1,0:T(8,128)(2,1)S(1)}, bf16[16,10240]{1,0:T(8,128)(2,1)S(1)}, u32[]{:S(2)}, u32[]{:S(2)}) %collective-permute-start.9) | collective-permute-done | bytes 327712 | tf_op jit(solution)/shard_map/ppermute | solution.py:32
  17.4 4.2 %collective-permute-done.7.refs_2_ = bf16[16,4096]{1,0:T(8,128)(2,1)S(1)} collective-permute-done((bf16[16,4096]{1,0:T(8,128)(2,1)S(1)}, bf16[16,4096]{1,0:T(8,128)(2,1)S(1)}, u32[]{:S(2)}, u32[]{:S(2)}) %collective-permute-start.7) | collective-permute-done | bytes 131104 | tf_op jit(solution)/shard_map/ppermute | solution.py:32
  22.2 2.4 %collective-permute-start.11 = (bf16[16,4096]{1,0:T(8,128)(2,1)S(1)}, bf16[16,4096]{1,0:T(8,128)(2,1)S(1)}, u32[]{:S(2)}, u32[]{:S(2)}) collective-permute-start(bf16[16,4096]{1,0:T(8,128)(2,1)S(1)} %get-tuple-element.26), channel_id=1, source_target_pairs={{0,4},{1,5},{2,6},{3,7},{4,0},{5,1},{6,2},{7,3},{8,12},{9,13},{10,... | collective-permute-start | bytes 393224 | tf_op jit(solution)/shard_map/ppermute | solution.py:32
  24.5 1.9 %collective-permute-start.12 = (bf16[16,4096]{1,0:T(8,128)(2,1)S(1)}, bf16[16,4096]{1,0:T(8,128)(2,1)S(1)}, u32[]{:S(2)}, u32[]{:S(2)}) collective-permute-start(bf16[16,4096]{1,0:T(8,128)(2,1)S(1)} %get-tuple-element.27), channel_id=1, source_target_pairs={{0,8},{1,9},{2,10},{3,11},{4,12},{5,13},{6,14},{7,15},{8,0},{9,1},... | collective-permute-start | bytes 393224 | tf_op jit(solution)/shard_map/ppermute | solution.py:32
  26.5 1.5 %collective-permute-start.13 = (bf16[16,4096]{1,0:T(8,128)(2,1)S(1)}, bf16[16,4096]{1,0:T(8,128)(2,1)S(1)}, u32[]{:S(2)}, u32[]{:S(2)}) collective-permute-start(bf16[16,4096]{1,0:T(8,128)(2,1)S(1)} %get-tuple-element.28), channel_id=1, source_target_pairs={{0,12},{1,13},{2,14},{3,15},{4,8},{5,9},{6,10},{7,11},{8,4},{9,5},... | collective-permute-start | bytes 393224 | tf_op jit(solution)/shard_map/ppermute | solution.py:32
  29.0 1.2 %collective-permute-done.11.refs_1_ = bf16[16,4096]{1,0:T(8,128)(2,1)S(1)} collective-permute-done((bf16[16,4096]{1,0:T(8,128)(2,1)S(1)}, bf16[16,4096]{1,0:T(8,128)(2,1)S(1)}, u32[]{:S(2)}, u32[]{:S(2)}) %collective-permute-start.11) | collective-permute-done | bytes 131104 | tf_op jit(solution)/shard_map/ppermute | solution.py:32
  30.1 6.6 %collective-permute-done.12.refs_2_ = bf16[16,4096]{1,0:T(8,128)(2,1)S(1)} collective-permute-done((bf16[16,4096]{1,0:T(8,128)(2,1)S(1)}, bf16[16,4096]{1,0:T(8,128)(2,1)S(1)}, u32[]{:S(2)}, u32[]{:S(2)}) %collective-permute-start.12) | collective-permute-done | bytes 131104 | tf_op jit(solution)/shard_map/ppermute | solution.py:32
  36.8 2.5 %collective-permute-done.10.refs_4_.__0_ = bf16[64,4096]{1,0:T(8,128)(2,1)S(1)} collective-permute-done((bf16[64,4096]{1,0:T(8,128)(2,1)S(1)}, bf16[64,4096]{1,0:T(8,128)(2,1)S(1)}, u32[]{:S(2)}, u32[]{:S(2)}) %collective-permute-start.10) | collective-permute-done | bytes 524320 | tf_op jit(solution)/shard_map/ppermute | solution.py:32
  40.0 1.7 %collective-permute-start.16 = (bf16[16,4096]{1,0:T(8,128)(2,1)S(1)}, bf16[16,4096]{1,0:T(8,128)(2,1)S(1)}, u32[]{:S(2)}, u32[]{:S(2)}) collective-permute-start(bf16[16,4096]{1,0:T(8,128)(2,1)S(1)} %shard_map.91.__1_.refs_0_.refs_2_), channel_id=1, source_target_pairs={{0,16},{16,0},{1,17},{17,1},{2,18},{18,2},{3,19},{19,3},{4,20},{20... | collective-permute-start | bytes 393224 | tf_op jit(solution)/shard_map/ppermute | solution.py:32
  41.7 1.6 %collective-permute-start.3 = (bf16[64,2176]{1,0:T(8,128)(2,1)S(1)}, bf16[64,2176]{1,0:T(8,128)(2,1)S(1)}, u32[]{:S(2)}, u32[]{:S(2)}) collective-permute-start(bf16[64,2176]{1,0:T(8,128)(2,1)S(1)} %get-tuple-element.21), channel_id=1, source_target_pairs={{0,4},{1,5},{2,6},{3,7},{4,0},{5,1},{6,2},{7,3},{8,12},{9,13},{10,... | collective-permute-start | bytes 835592 | tf_op jit(solution)/shard_map/ppermute | solution.py:32
  43.3 2.6 %collective-permute-start.4 = (bf16[64,2176]{1,0:T(8,128)(2,1)S(1)}, bf16[64,2176]{1,0:T(8,128)(2,1)S(1)}, u32[]{:S(2)}, u32[]{:S(2)}) collective-permute-start(bf16[64,2176]{1,0:T(8,128)(2,1)S(1)} %get-tuple-element.22), channel_id=1, source_target_pairs={{0,8},{1,9},{2,10},{3,11},{4,12},{5,13},{6,14},{7,15},{8,0},{9,1},... | collective-permute-start | bytes 835592 | tf_op jit(solution)/shard_map/ppermute | solution.py:32
  46.1 1.7 %shard_map.94.__1_.rot_ref = bf16[4096,256]{1,0:T(8,128)(2,1)S(1)} custom-call(bf16[64,4096]{1,0:T(8,128)(2,1)S(1)} %shard_map.92.refs_0_, bf16[64,4096]{1,0:T(8,128)(2,1)S(1)} %collective-permute-done.14.refs_1_, bf16[64,4096]{1,0:T(8,128)(2,1)S(1)} %collective-permute-done.15.refs_2_, bf16[512,4096]{1,0:T(8,128)(2,1)S(1)} %copy-done, ...), custom_call_target="tpu_custom_call" | custom-call | bytes 1 | tf_op jit(solution)/shard_map/pallas_call | solution.py:274
  49.4 22.0 %shard_map.96.refs_9_ = f32[2,2048,256]{2,1,0:T(8,128)S(1)} custom-call(bf16[4096,256]{1,0:T(8,128)(2,1)S(1)} %shard_map.94.__1_.rot_ref, bf16[16,4096]{1,0:T(8,128)(2,1)S(1)} %shard_map.91.__1_.refs_0_.refs_2_, bf16[16,4096]{1,0:T(8,128)(2,1)S(1)} %shard_map.95.refs_1_.refs_4_, bf16[16,4096]{1,0:T(8,128)(2,1)S(1)} %shard_map.91.__1_.refs_0_.refs_2_, ...), custom_call_target="tpu_custom_call" | custom-call | flops 1000000000 | bytes 1 | tf_op jit(solution)/shard_map/pallas_call | solution.py:361
  71.4 3.0 %shard_map.97 = f32[2,8,1]{2,1,0:T(8,128)S(1)} custom-call(bf16[64,2176]{1,0:T(8,128)(2,1)S(1)} %get-tuple-element.20.refs_6_.refs_0_.refs_4_, bf16[64,2176]{1,0:T(8,128)(2,1)S(1)} %collective-permute-done.3.refs_1_.refs_5_, bf16[64,2176]{1,0:T(8,128)(2,1)S(1)} %collective-permute-done.4.refs_2_.refs_6_, ...), custom_call_target="tpu_custom_call" | custom-call | flops 536870912 | bytes 4194304 | tf_op jit(solution)/shard_map/pallas_call | solution.py:417
  74.8 1.5 %collective-permute-start.20 = (f32[2,8,1]{2,1,0:T(8,128)S(1)}, f32[2,8,1]{2,1,0:T(8,128)S(1)}, u32[]{:S(2)}, u32[]{:S(2)}) collective-permute-start(f32[2,8,1]{2,1,0:T(8,128)S(1)} %shard_map.97), channel_id=1, source_target_pairs={{0,2},{1,3},{2,0},{3,1},{4,6},{5,7},{6,4},{7,5},{8,10},{9,11},{10,... | collective-permute-start | bytes 200 | tf_op jit(solution)/shard_map/ppermute | solution.py:32
  76.3 2.1 %collective-permute-done.20 = f32[2,8,1]{2,1,0:T(8,128)S(1)} collective-permute-done((f32[2,8,1]{2,1,0:T(8,128)S(1)}, f32[2,8,1]{2,1,0:T(8,128)S(1)}, u32[]{:S(2)}, u32[]{:S(2)}) %collective-permute-start.20) | collective-permute-done | bytes 96 | tf_op jit(solution)/shard_map/ppermute | solution.py:32
  80.2 3.5 %collective-permute-start.23 = (f32[2,8,1]{2,1,0:T(8,128)S(1)}, f32[2,8,1]{2,1,0:T(8,128)S(1)}, u32[]{:S(2)}, u32[]{:S(2)}) collective-permute-start(f32[2,8,1]{2,1,0:T(8,128)S(1)} %add_add_fusion), channel_id=1, source_target_pairs={{0,8},{1,9},{2,10},{3,11},{4,12},{5,13},{6,14},{7,15},{8,0},{9,1},... | collective-permute-start | bytes 200 | tf_op jit(solution)/shard_map/ppermute | solution.py:32
  83.9 1.4 %collective-permute-done.23 = f32[2,8,1]{2,1,0:T(8,128)S(1)} collective-permute-done((f32[2,8,1]{2,1,0:T(8,128)S(1)}, f32[2,8,1]{2,1,0:T(8,128)S(1)}, u32[]{:S(2)}, u32[]{:S(2)}) %collective-permute-start.23) | collective-permute-done | bytes 96 | tf_op jit(solution)/shard_map/ppermute | solution.py:32
  85.3 3.8 %collective-permute-done.22 = f32[2,8,1]{2,1,0:T(8,128)S(1)} collective-permute-done((f32[2,8,1]{2,1,0:T(8,128)S(1)}, f32[2,8,1]{2,1,0:T(8,128)S(1)}, u32[]{:S(2)}, u32[]{:S(2)}) %collective-permute-start.22) | collective-permute-done | bytes 96 | tf_op jit(solution)/shard_map/ppermute | solution.py:32
  (60 shorter events, 10.5 us)
Async XLA Ops:
  1.8 3.7 %collective-permute-start.1 = (bf16[16,18432]{1,0:T(8,128)(2,1)S(1)}, bf16[16,18432]{1,0:T(8,128)(2,1)S(1)}, u32[]{:S(2)}, u32[]{:S(2)}) collective-permute-start(bf16[16,18432]{1,0:T(8,128)(2,1)S(1)} %get-tuple-element.18), channel_id=1, source_target_pairs={{0,1},{1,0},{2,3},{3,2},{4,5},{5,4},{6,7},{7,6},{8,9},{9,8},{10,11... | collective-permute-start | bytes 1769480 | tf_op jit(solution)/shard_map/ppermute | solution.py:32
  4.8 8.3 %collective-permute-start = (bf16[16,16512]{1,0:T(8,128)(2,1)S(1)}, bf16[16,16512]{1,0:T(8,128)(2,1)S(1)}, u32[]{:S(2)}, u32[]{:S(2)}) collective-permute-start(bf16[16,16512]{1,0:T(8,128)(2,1)S(1)} %shard_map.83.refs_0_.sent_ref), channel_id=1, source_target_pairs={{0,1},{1,0},{2,3},{3,2},{4,5},{5,4},{6,7},{7,6},{8,9},{9,8},{10,11... | collective-permute-start | bytes 1585160 | tf_op jit(solution)/shard_map/ppermute | solution.py:32
  5.7 11.5 %collective-permute-start.9 = (bf16[16,10240]{1,0:T(8,128)(2,1)S(1)}, bf16[16,10240]{1,0:T(8,128)(2,1)S(1)}, u32[]{:S(2)}, u32[]{:S(2)}) collective-permute-start(bf16[16,10240]{1,0:T(8,128)(2,1)S(1)} %get-tuple-element.19._), channel_id=1, source_target_pairs={{0,2},{1,3},{2,0},{3,1},{4,6},{5,7},{6,4},{7,5},{8,10},{9,11},{10,... | collective-permute-start | bytes 983048 | tf_op jit(solution)/shard_map/ppermute | solution.py:32
  8.8 12.8 %collective-permute-start.7 = (bf16[16,4096]{1,0:T(8,128)(2,1)S(1)}, bf16[16,4096]{1,0:T(8,128)(2,1)S(1)}, u32[]{:S(2)}, u32[]{:S(2)}) collective-permute-start(bf16[16,4096]{1,0:T(8,128)(2,1)S(1)} %copy-done.5), channel_id=1, source_target_pairs={{0,8},{1,9},{2,10},{3,11},{4,12},{5,13},{6,14},{7,15},{8,0},{9,1},... | collective-permute-start | bytes 393224 | tf_op jit(solution)/shard_map/ppermute | solution.py:32
  11.4 10.2 %collective-permute-start.6 = (bf16[16,4096]{1,0:T(8,128)(2,1)S(1)}, bf16[16,4096]{1,0:T(8,128)(2,1)S(1)}, u32[]{:S(2)}, u32[]{:S(2)}) collective-permute-start(bf16[16,4096]{1,0:T(8,128)(2,1)S(1)} %copy-done.5), channel_id=1, source_target_pairs={{0,4},{1,5},{2,6},{3,7},{4,0},{5,1},{6,2},{7,3},{8,12},{9,13},{10,... | collective-permute-start | bytes 393224 | tf_op jit(solution)/shard_map/ppermute | solution.py:32
  12.9 8.6 %collective-permute-start.8 = (bf16[16,4096]{1,0:T(8,128)(2,1)S(1)}, bf16[16,4096]{1,0:T(8,128)(2,1)S(1)}, u32[]{:S(2)}, u32[]{:S(2)}) collective-permute-start(bf16[16,4096]{1,0:T(8,128)(2,1)S(1)} %copy-done.5), channel_id=1, source_target_pairs={{0,12},{1,13},{2,14},{3,15},{4,8},{5,9},{6,10},{7,11},{8,4},{9,5},... | collective-permute-start | bytes 393224 | tf_op jit(solution)/shard_map/ppermute | solution.py:32
  13.2 15.7 %collective-permute-start.2 = (bf16[32,8320]{1,0:T(8,128)(2,1)S(1)}, bf16[32,8320]{1,0:T(8,128)(2,1)S(1)}, u32[]{:S(2)}, u32[]{:S(2)}) collective-permute-start(bf16[32,8320]{1,0:T(8,128)(2,1)S(1)} %shard_map.86.refs_0_), channel_id=1, source_target_pairs={{0,2},{1,3},{2,0},{3,1},{4,6},{5,7},{6,4},{7,5},{8,10},{9,11},{10,... | collective-permute-start | bytes 1597448 | tf_op jit(solution)/shard_map/ppermute | solution.py:32
  21.6 17.7 %collective-permute-start.10 = (bf16[64,4096]{1,0:T(8,128)(2,1)S(1)}, bf16[64,4096]{1,0:T(8,128)(2,1)S(1)}, u32[]{:S(2)}, u32[]{:S(2)}) collective-permute-start(bf16[64,4096]{1,0:T(8,128)(2,1)S(1)} %shard_map.89.refs_0_.__0_), channel_id=1, source_target_pairs={{0,2},{1,3},{2,0},{3,1},{4,6},{5,7},{6,4},{7,5},{8,10},{9,11},{10,... | collective-permute-start | bytes 1572872 | tf_op jit(solution)/shard_map/ppermute | solution.py:32
  22.2 8.0 %collective-permute-start.11 = (bf16[16,4096]{1,0:T(8,128)(2,1)S(1)}, bf16[16,4096]{1,0:T(8,128)(2,1)S(1)}, u32[]{:S(2)}, u32[]{:S(2)}) collective-permute-start(bf16[16,4096]{1,0:T(8,128)(2,1)S(1)} %get-tuple-element.26), channel_id=1, source_target_pairs={{0,4},{1,5},{2,6},{3,7},{4,0},{5,1},{6,2},{7,3},{8,12},{9,13},{10,... | collective-permute-start | bytes 393224 | tf_op jit(solution)/shard_map/ppermute | solution.py:32
  24.5 12.2 %collective-permute-start.12 = (bf16[16,4096]{1,0:T(8,128)(2,1)S(1)}, bf16[16,4096]{1,0:T(8,128)(2,1)S(1)}, u32[]{:S(2)}, u32[]{:S(2)}) collective-permute-start(bf16[16,4096]{1,0:T(8,128)(2,1)S(1)} %get-tuple-element.27), channel_id=1, source_target_pairs={{0,8},{1,9},{2,10},{3,11},{4,12},{5,13},{6,14},{7,15},{8,0},{9,1},... | collective-permute-start | bytes 393224 | tf_op jit(solution)/shard_map/ppermute | solution.py:32
  26.5 10.3 %collective-permute-start.13 = (bf16[16,4096]{1,0:T(8,128)(2,1)S(1)}, bf16[16,4096]{1,0:T(8,128)(2,1)S(1)}, u32[]{:S(2)}, u32[]{:S(2)}) collective-permute-start(bf16[16,4096]{1,0:T(8,128)(2,1)S(1)} %get-tuple-element.28), channel_id=1, source_target_pairs={{0,12},{1,13},{2,14},{3,15},{4,8},{5,9},{6,10},{7,11},{8,4},{9,5},... | collective-permute-start | bytes 393224 | tf_op jit(solution)/shard_map/ppermute | solution.py:32
  39.4 6.5 %collective-permute-start.14 = (bf16[64,4096]{1,0:T(8,128)(2,1)S(1)}, bf16[64,4096]{1,0:T(8,128)(2,1)S(1)}, u32[]{:S(2)}, u32[]{:S(2)}) collective-permute-start(bf16[64,4096]{1,0:T(8,128)(2,1)S(1)} %shard_map.93), channel_id=1, source_target_pairs={{0,1},{1,0},{2,3},{3,2},{4,5},{5,4},{6,7},{7,6},{8,9},{9,8},{10,11... | collective-permute-start | bytes 1572872 | tf_op jit(solution)/shard_map/ppermute | solution.py:32
  39.5 6.6 %collective-permute-start.15 = (bf16[64,4096]{1,0:T(8,128)(2,1)S(1)}, bf16[64,4096]{1,0:T(8,128)(2,1)S(1)}, u32[]{:S(2)}, u32[]{:S(2)}) collective-permute-start(bf16[64,4096]{1,0:T(8,128)(2,1)S(1)} %shard_map.92.refs_0_), channel_id=1, source_target_pairs={{0,1},{1,0},{2,3},{3,2},{4,5},{5,4},{6,7},{7,6},{8,9},{9,8},{10,11... | collective-permute-start | bytes 1572872 | tf_op jit(solution)/shard_map/ppermute | solution.py:32
  40.0 7.8 %collective-permute-start.16 = (bf16[16,4096]{1,0:T(8,128)(2,1)S(1)}, bf16[16,4096]{1,0:T(8,128)(2,1)S(1)}, u32[]{:S(2)}, u32[]{:S(2)}) collective-permute-start(bf16[16,4096]{1,0:T(8,128)(2,1)S(1)} %shard_map.91.__1_.refs_0_.refs_2_), channel_id=1, source_target_pairs={{0,16},{16,0},{1,17},{17,1},{2,18},{18,2},{3,19},{19,3},{4,20},{20... | collective-permute-start | bytes 393224 | tf_op jit(solution)/shard_map/ppermute | solution.py:32
  41.7 29.7 %collective-permute-start.3 = (bf16[64,2176]{1,0:T(8,128)(2,1)S(1)}, bf16[64,2176]{1,0:T(8,128)(2,1)S(1)}, u32[]{:S(2)}, u32[]{:S(2)}) collective-permute-start(bf16[64,2176]{1,0:T(8,128)(2,1)S(1)} %get-tuple-element.21), channel_id=1, source_target_pairs={{0,4},{1,5},{2,6},{3,7},{4,0},{5,1},{6,2},{7,3},{8,12},{9,13},{10,... | collective-permute-start | bytes 835592 | tf_op jit(solution)/shard_map/ppermute | solution.py:32
  43.3 28.1 %collective-permute-start.4 = (bf16[64,2176]{1,0:T(8,128)(2,1)S(1)}, bf16[64,2176]{1,0:T(8,128)(2,1)S(1)}, u32[]{:S(2)}, u32[]{:S(2)}) collective-permute-start(bf16[64,2176]{1,0:T(8,128)(2,1)S(1)} %get-tuple-element.22), channel_id=1, source_target_pairs={{0,8},{1,9},{2,10},{3,11},{4,12},{5,13},{6,14},{7,15},{8,0},{9,1},... | collective-permute-start | bytes 835592 | tf_op jit(solution)/shard_map/ppermute | solution.py:32
  45.9 25.5 %collective-permute-start.5 = (bf16[64,2176]{1,0:T(8,128)(2,1)S(1)}, bf16[64,2176]{1,0:T(8,128)(2,1)S(1)}, u32[]{:S(2)}, u32[]{:S(2)}) collective-permute-start(bf16[64,2176]{1,0:T(8,128)(2,1)S(1)} %get-tuple-element.23), channel_id=1, source_target_pairs={{0,12},{1,13},{2,14},{3,15},{4,8},{5,9},{6,10},{7,11},{8,4},{9,5},... | collective-permute-start | bytes 835592 | tf_op jit(solution)/shard_map/ppermute | solution.py:32
  46.1 2.3 %collective-permute-start.17 = (bf16[16,4096]{1,0:T(8,128)(2,1)S(1)}, bf16[16,4096]{1,0:T(8,128)(2,1)S(1)}, u32[]{:S(2)}, u32[]{:S(2)}) collective-permute-start(bf16[16,4096]{1,0:T(8,128)(2,1)S(1)} %shard_map.91.__1_.refs_0_.refs_2_), channel_id=1, source_target_pairs={{0,1},{1,0},{2,3},{3,2},{4,5},{5,4},{6,7},{7,6},{8,9},{9,8},{10,11... | collective-permute-start | bytes 393224 | tf_op jit(solution)/shard_map/ppermute | solution.py:32
  74.4 1.9 %collective-permute-start.21 = (f32[2,8,1]{2,1,0:T(8,128)S(1)}, f32[2,8,1]{2,1,0:T(8,128)S(1)}, u32[]{:S(2)}, u32[]{:S(2)}) collective-permute-start(f32[2,8,1]{2,1,0:T(8,128)S(1)} %shard_map.97), channel_id=1, source_target_pairs={{0,1},{1,0},{2,3},{3,2},{4,5},{5,4},{6,7},{7,6},{8,9},{9,8},{10,11... | collective-permute-start | bytes 200 | tf_op jit(solution)/shard_map/ppermute | solution.py:32
  74.8 3.7 %collective-permute-start.20 = (f32[2,8,1]{2,1,0:T(8,128)S(1)}, f32[2,8,1]{2,1,0:T(8,128)S(1)}, u32[]{:S(2)}, u32[]{:S(2)}) collective-permute-start(f32[2,8,1]{2,1,0:T(8,128)S(1)} %shard_map.97), channel_id=1, source_target_pairs={{0,2},{1,3},{2,0},{3,1},{4,6},{5,7},{6,4},{7,5},{8,10},{9,11},{10,... | collective-permute-start | bytes 200 | tf_op jit(solution)/shard_map/ppermute | solution.py:32
  76.3 3.1 %collective-permute-start.19 = (f32[2,8,1]{2,1,0:T(8,128)S(1)}, f32[2,8,1]{2,1,0:T(8,128)S(1)}, u32[]{:S(2)}, u32[]{:S(2)}) collective-permute-start(f32[2,8,1]{2,1,0:T(8,128)S(1)} %shard_map.97), channel_id=1, source_target_pairs={{0,3},{1,2},{2,1},{3,0},{4,7},{5,6},{6,5},{7,4},{8,11},{9,10},{10,... | collective-permute-start | bytes 200 | tf_op jit(solution)/shard_map/ppermute | solution.py:32
  79.5 4.4 %collective-permute-start.24 = (f32[2,8,1]{2,1,0:T(8,128)S(1)}, f32[2,8,1]{2,1,0:T(8,128)S(1)}, u32[]{:S(2)}, u32[]{:S(2)}) collective-permute-start(f32[2,8,1]{2,1,0:T(8,128)S(1)} %add_add_fusion), channel_id=1, source_target_pairs={{0,4},{1,5},{2,6},{3,7},{4,0},{5,1},{6,2},{7,3},{8,12},{9,13},{10,... | collective-permute-start | bytes 200 | tf_op jit(solution)/shard_map/ppermute | solution.py:32
  80.2 5.1 %collective-permute-start.23 = (f32[2,8,1]{2,1,0:T(8,128)S(1)}, f32[2,8,1]{2,1,0:T(8,128)S(1)}, u32[]{:S(2)}, u32[]{:S(2)}) collective-permute-start(f32[2,8,1]{2,1,0:T(8,128)S(1)} %add_add_fusion), channel_id=1, source_target_pairs={{0,8},{1,9},{2,10},{3,11},{4,12},{5,13},{6,14},{7,15},{8,0},{9,1},... | collective-permute-start | bytes 200 | tf_op jit(solution)/shard_map/ppermute | solution.py:32
  83.7 5.4 %collective-permute-start.22 = (f32[2,8,1]{2,1,0:T(8,128)S(1)}, f32[2,8,1]{2,1,0:T(8,128)S(1)}, u32[]{:S(2)}, u32[]{:S(2)}) collective-permute-start(f32[2,8,1]{2,1,0:T(8,128)S(1)} %add_add_fusion), channel_id=1, source_target_pairs={{0,12},{1,13},{2,14},{3,15},{4,8},{5,9},{6,10},{7,11},{8,4},{9,5},... | collective-permute-start | bytes 200 | tf_op jit(solution)/shard_map/ppermute | solution.py:32
  (9 other events, 75.3 us)

commit v18 on v17

--- a/solution.py
+++ b/solution.py
@@ -475,8 +475,11 @@
 
     image = images(rot, lefts, halves, eigenvalues)
     parts = score_parts(grads, ranks, grad_basis, image, seq_count)
-    for step, count in ((1, 4), (4, wide_count // 4)):
-        parts = parts + sum(swap(parts, "wide", step * n) for n in range(count - 1, 0, -1))
+    parts = parts + sum(swap(parts, "wide", r) for r in (3, 2, 1))
+    bit = 4
+    while bit < wide_count:
+        parts = parts + swap(parts, "wide", bit)
+        bit *= 2
     return parts[:, :, 0].T
 
 

time: 89.9 us -> 88.5 us (0.984)
  starting transfers between devices: 28.2 us -> 26.7 us
    ppermute x25 -> x24, starting transfers between devices: 28.2 us -> 26.7 us  [swap(): return lax.ppermute(x, axis, [(i, i ^ bit) for i in range(count)])]
    ppermute x25 -> x24, waiting for transfers between devices: 27.6 us -> 27.7 us  [swap(): return lax.ppermute(x, axis, [(i, i ^ bit) for i in range(count)])]
  transfers between devices with their start and end apart: 25 -> 24, of which waited for: 10 -> 10; matrix products, arithmetic and copies ran while one was open for 0% -> 0% of each run, Pallas kernels for 29% -> 30%
where the time goes in v18:
time: 88.5 us; the launch traced here: 88.3 us
  Pallas kernels  29.4 us (33%)
  waiting for transfers between devices  27.7 us (31%)
  starting transfers between devices  26.7 us (30%)
  local copies, waits for them, and re-layouts  3.66 us (4%)
    ppermute x24, waiting for transfers between devices, swap(): return lax.ppermute(x, axis, [(i, i ^ bit) for i in range(count)])  27.7 us
    ppermute x24, starting transfers between devices, swap(): return lax.ppermute(x, axis, [(i, i ^ bit) for i in range(count)])  26.7 us
    pallas_call x1, Pallas kernels, images(): pl.pallas_call(functools.partial(image_kernel, batch_count, total, per),...  22 us
    unnamed x16, local copies, waits for them, and re-layouts  3.66 us
    pallas_call x1, Pallas kernels, score_parts(): pl.pallas_call(functools.partial(score_kernel, batch_count, ranks, count)...  2.98 us
    pallas_call x2, Pallas kernels, rotate(): pl.pallas_call(functools.partial(rotate_kernel, len(act_pieces), done), i...  2.64 us
  transfers between devices with their start and end apart: 24, of which 10 were waited for; matrix products, arithmetic and copies ran while one was open for 0% of the time, Pallas kernels for 30%

profile of v18, /device:TPU:0, one launch (start us, length us, event | category | flops | bytes accessed | tf_op | source)
XLA Modules:
  0.0 88.3 jit_solution(14879872863895967011)
XLA Ops:
  0.0 1.8 %copy-done.3 = bf16[2,16,36864]{2,1,0:T(8,128)(2,1)S(1)} copy-done((bf16[2,16,36864]{2,1,0:T(8,128)(2,1)S(1)}, bf16[2,16,36864]{2,1,0:T(8,128)(2,1)}, u32[]{:S(2)}) %copy-start.3) | copy-done | bytes 2359320
  2.4 1.2 %copy-done.1 = bf16[16,32768]{1,0:T(8,128)(2,1)S(1)} copy-done((bf16[16,32768]{1,0:T(8,128)(2,1)S(1)}, bf16[16,32768]{1,0:T(8,128)(2,1)}, u32[]{:S(2)}) %copy-start.1) | copy-done | bytes 1048600
  5.7 3.0 %collective-permute-start.9 = (bf16[16,10240]{1,0:T(8,128)(2,1)S(1)}, bf16[16,10240]{1,0:T(8,128)(2,1)S(1)}, u32[]{:S(2)}, u32[]{:S(2)}) collective-permute-start(bf16[16,10240]{1,0:T(8,128)(2,1)S(1)} %get-tuple-element.19._), channel_id=1, source_target_pairs={{0,2},{1,3},{2,0},{3,1},{4,6},{5,7},{6,4},{7,5},{8,10},{9,11},{10,... | collective-permute-start | bytes 983048 | tf_op jit(solution)/shard_map/ppermute | solution.py:32
  8.8 2.6 %collective-permute-start.7 = (bf16[16,4096]{1,0:T(8,128)(2,1)S(1)}, bf16[16,4096]{1,0:T(8,128)(2,1)S(1)}, u32[]{:S(2)}, u32[]{:S(2)}) collective-permute-start(bf16[16,4096]{1,0:T(8,128)(2,1)S(1)} %copy-done.5), channel_id=1, source_target_pairs={{0,8},{1,9},{2,10},{3,11},{4,12},{5,13},{6,14},{7,15},{8,0},{9,1},... | collective-permute-start | bytes 393224 | tf_op jit(solution)/shard_map/ppermute | solution.py:32
  11.4 1.6 %collective-permute-start.6 = (bf16[16,4096]{1,0:T(8,128)(2,1)S(1)}, bf16[16,4096]{1,0:T(8,128)(2,1)S(1)}, u32[]{:S(2)}, u32[]{:S(2)}) collective-permute-start(bf16[16,4096]{1,0:T(8,128)(2,1)S(1)} %copy-done.5), channel_id=1, source_target_pairs={{0,4},{1,5},{2,6},{3,7},{4,0},{5,1},{6,2},{7,3},{8,12},{9,13},{10,... | collective-permute-start | bytes 393224 | tf_op jit(solution)/shard_map/ppermute | solution.py:32
  13.6 3.7 %collective-permute-done.9.got_ref = bf16[16,10240]{1,0:T(8,128)(2,1)S(1)} collective-permute-done((bf16[16,10240]{1,0:T(8,128)(2,1)S(1)}, bf16[16,10240]{1,0:T(8,128)(2,1)S(1)}, u32[]{:S(2)}, u32[]{:S(2)}) %collective-permute-start.9) | collective-permute-done | bytes 327712 | tf_op jit(solution)/shard_map/ppermute | solution.py:32
  17.4 4.2 %collective-permute-done.7.refs_2_ = bf16[16,4096]{1,0:T(8,128)(2,1)S(1)} collective-permute-done((bf16[16,4096]{1,0:T(8,128)(2,1)S(1)}, bf16[16,4096]{1,0:T(8,128)(2,1)S(1)}, u32[]{:S(2)}, u32[]{:S(2)}) %collective-permute-start.7) | collective-permute-done | bytes 131104 | tf_op jit(solution)/shard_map/ppermute | solution.py:32
  22.2 2.4 %collective-permute-start.11 = (bf16[16,4096]{1,0:T(8,128)(2,1)S(1)}, bf16[16,4096]{1,0:T(8,128)(2,1)S(1)}, u32[]{:S(2)}, u32[]{:S(2)}) collective-permute-start(bf16[16,4096]{1,0:T(8,128)(2,1)S(1)} %get-tuple-element.26), channel_id=1, source_target_pairs={{0,4},{1,5},{2,6},{3,7},{4,0},{5,1},{6,2},{7,3},{8,12},{9,13},{10,... | collective-permute-start | bytes 393224 | tf_op jit(solution)/shard_map/ppermute | solution.py:32
  24.5 1.9 %collective-permute-start.12 = (bf16[16,4096]{1,0:T(8,128)(2,1)S(1)}, bf16[16,4096]{1,0:T(8,128)(2,1)S(1)}, u32[]{:S(2)}, u32[]{:S(2)}) collective-permute-start(bf16[16,4096]{1,0:T(8,128)(2,1)S(1)} %get-tuple-element.27), channel_id=1, source_target_pairs={{0,8},{1,9},{2,10},{3,11},{4,12},{5,13},{6,14},{7,15},{8,0},{9,1},... | collective-permute-start | bytes 393224 | tf_op jit(solution)/shard_map/ppermute | solution.py:32
  26.5 1.5 %collective-permute-start.13 = (bf16[16,4096]{1,0:T(8,128)(2,1)S(1)}, bf16[16,4096]{1,0:T(8,128)(2,1)S(1)}, u32[]{:S(2)}, u32[]{:S(2)}) collective-permute-start(bf16[16,4096]{1,0:T(8,128)(2,1)S(1)} %get-tuple-element.28), channel_id=1, source_target_pairs={{0,12},{1,13},{2,14},{3,15},{4,8},{5,9},{6,10},{7,11},{8,4},{9,5},... | collective-permute-start | bytes 393224 | tf_op jit(solution)/shard_map/ppermute | solution.py:32
  29.0 1.2 %collective-permute-done.11.refs_1_ = bf16[16,4096]{1,0:T(8,128)(2,1)S(1)} collective-permute-done((bf16[16,4096]{1,0:T(8,128)(2,1)S(1)}, bf16[16,4096]{1,0:T(8,128)(2,1)S(1)}, u32[]{:S(2)}, u32[]{:S(2)}) %collective-permute-start.11) | collective-permute-done | bytes 131104 | tf_op jit(solution)/shard_map/ppermute | solution.py:32
  30.1 6.6 %collective-permute-done.12.refs_2_ = bf16[16,4096]{1,0:T(8,128)(2,1)S(1)} collective-permute-done((bf16[16,4096]{1,0:T(8,128)(2,1)S(1)}, bf16[16,4096]{1,0:T(8,128)(2,1)S(1)}, u32[]{:S(2)}, u32[]{:S(2)}) %collective-permute-start.12) | collective-permute-done | bytes 131104 | tf_op jit(solution)/shard_map/ppermute | solution.py:32
  36.8 2.5 %collective-permute-done.10.refs_4_.__0_ = bf16[64,4096]{1,0:T(8,128)(2,1)S(1)} collective-permute-done((bf16[64,4096]{1,0:T(8,128)(2,1)S(1)}, bf16[64,4096]{1,0:T(8,128)(2,1)S(1)}, u32[]{:S(2)}, u32[]{:S(2)}) %collective-permute-start.10) | collective-permute-done | bytes 524320 | tf_op jit(solution)/shard_map/ppermute | solution.py:32
  40.0 1.7 %collective-permute-start.16 = (bf16[16,4096]{1,0:T(8,128)(2,1)S(1)}, bf16[16,4096]{1,0:T(8,128)(2,1)S(1)}, u32[]{:S(2)}, u32[]{:S(2)}) collective-permute-start(bf16[16,4096]{1,0:T(8,128)(2,1)S(1)} %shard_map.91.__1_.refs_0_.refs_2_), channel_id=1, source_target_pairs={{0,16},{16,0},{1,17},{17,1},{2,18},{18,2},{3,19},{19,3},{4,20},{20... | collective-permute-start | bytes 393224 | tf_op jit(solution)/shard_map/ppermute | solution.py:32
  41.7 1.6 %collective-permute-start.3 = (bf16[64,2176]{1,0:T(8,128)(2,1)S(1)}, bf16[64,2176]{1,0:T(8,128)(2,1)S(1)}, u32[]{:S(2)}, u32[]{:S(2)}) collective-permute-start(bf16[64,2176]{1,0:T(8,128)(2,1)S(1)} %get-tuple-element.21), channel_id=1, source_target_pairs={{0,4},{1,5},{2,6},{3,7},{4,0},{5,1},{6,2},{7,3},{8,12},{9,13},{10,... | collective-permute-start | bytes 835592 | tf_op jit(solution)/shard_map/ppermute | solution.py:32
  43.3 2.6 %collective-permute-start.4 = (bf16[64,2176]{1,0:T(8,128)(2,1)S(1)}, bf16[64,2176]{1,0:T(8,128)(2,1)S(1)}, u32[]{:S(2)}, u32[]{:S(2)}) collective-permute-start(bf16[64,2176]{1,0:T(8,128)(2,1)S(1)} %get-tuple-element.22), channel_id=1, source_target_pairs={{0,8},{1,9},{2,10},{3,11},{4,12},{5,13},{6,14},{7,15},{8,0},{9,1},... | collective-permute-start | bytes 835592 | tf_op jit(solution)/shard_map/ppermute | solution.py:32
  46.1 1.7 %shard_map.94.__1_.rot_ref = bf16[4096,256]{1,0:T(8,128)(2,1)S(1)} custom-call(bf16[64,4096]{1,0:T(8,128)(2,1)S(1)} %shard_map.92.refs_0_, bf16[64,4096]{1,0:T(8,128)(2,1)S(1)} %collective-permute-done.14.refs_1_, bf16[64,4096]{1,0:T(8,128)(2,1)S(1)} %collective-permute-done.15.refs_2_, bf16[512,4096]{1,0:T(8,128)(2,1)S(1)} %copy-done, ...), custom_call_target="tpu_custom_call" | custom-call | bytes 1 | tf_op jit(solution)/shard_map/pallas_call | solution.py:274
  49.4 22.0 %shard_map.96.refs_9_ = f32[2,2048,256]{2,1,0:T(8,128)S(1)} custom-call(bf16[4096,256]{1,0:T(8,128)(2,1)S(1)} %shard_map.94.__1_.rot_ref, bf16[16,4096]{1,0:T(8,128)(2,1)S(1)} %shard_map.91.__1_.refs_0_.refs_2_, bf16[16,4096]{1,0:T(8,128)(2,1)S(1)} %shard_map.95.refs_1_.refs_4_, bf16[16,4096]{1,0:T(8,128)(2,1)S(1)} %shard_map.91.__1_.refs_0_.refs_2_, ...), custom_call_target="tpu_custom_call" | custom-call | flops 1000000000 | bytes 1 | tf_op jit(solution)/shard_map/pallas_call | solution.py:361
  71.4 3.0 %shard_map.97 = f32[2,8,1]{2,1,0:T(8,128)S(1)} custom-call(bf16[64,2176]{1,0:T(8,128)(2,1)S(1)} %get-tuple-element.20.refs_6_.refs_0_.refs_4_, bf16[64,2176]{1,0:T(8,128)(2,1)S(1)} %collective-permute-done.3.refs_1_.refs_5_, bf16[64,2176]{1,0:T(8,128)(2,1)S(1)} %collective-permute-done.4.refs_2_.refs_6_, ...), custom_call_target="tpu_custom_call" | custom-call | flops 536870912 | bytes 4194304 | tf_op jit(solution)/shard_map/pallas_call | solution.py:417
  74.8 1.5 %collective-permute-start.20 = (f32[2,8,1]{2,1,0:T(8,128)S(1)}, f32[2,8,1]{2,1,0:T(8,128)S(1)}, u32[]{:S(2)}, u32[]{:S(2)}) collective-permute-start(f32[2,8,1]{2,1,0:T(8,128)S(1)} %shard_map.97), channel_id=1, source_target_pairs={{0,2},{1,3},{2,0},{3,1},{4,6},{5,7},{6,4},{7,5},{8,10},{9,11},{10,... | collective-permute-start | bytes 200 | tf_op jit(solution)/shard_map/ppermute | solution.py:32
  76.3 2.1 %collective-permute-done.20 = f32[2,8,1]{2,1,0:T(8,128)S(1)} collective-permute-done((f32[2,8,1]{2,1,0:T(8,128)S(1)}, f32[2,8,1]{2,1,0:T(8,128)S(1)}, u32[]{:S(2)}, u32[]{:S(2)}) %collective-permute-start.20) | collective-permute-done | bytes 96 | tf_op jit(solution)/shard_map/ppermute | solution.py:32
  80.2 2.9 %collective-permute-done.22 = f32[2,8,1]{2,1,0:T(8,128)S(1)} collective-permute-done((f32[2,8,1]{2,1,0:T(8,128)S(1)}, f32[2,8,1]{2,1,0:T(8,128)S(1)}, u32[]{:S(2)}, u32[]{:S(2)}) %collective-permute-start.22) | collective-permute-done | bytes 96 | tf_op jit(solution)/shard_map/ppermute | solution.py:32
  83.1 2.2 %collective-permute-start.23 = (f32[2,8,1]{2,1,0:T(8,128)S(1)}, f32[2,8,1]{2,1,0:T(8,128)S(1)}, u32[]{:S(2)}, u32[]{:S(2)}) collective-permute-start(f32[2,8,1]{2,1,0:T(8,128)S(1)} %add.18), channel_id=1, source_target_pairs={{0,8},{1,9},{2,10},{3,11},{4,12},{5,13},{6,14},{7,15},{8,0},{9,1},... | collective-permute-start | bytes 200 | tf_op jit(solution)/shard_map/ppermute | solution.py:32
  85.3 2.4 %collective-permute-done.23 = f32[2,8,1]{2,1,0:T(8,128)S(1)} collective-permute-done((f32[2,8,1]{2,1,0:T(8,128)S(1)}, f32[2,8,1]{2,1,0:T(8,128)S(1)}, u32[]{:S(2)}, u32[]{:S(2)}) %collective-permute-start.23) | collective-permute-done | bytes 96 | tf_op jit(solution)/shard_map/ppermute | solution.py:32
  (59 shorter events, 10.3 us)
Async XLA Ops:
  1.8 3.7 %collective-permute-start.1 = (bf16[16,18432]{1,0:T(8,128)(2,1)S(1)}, bf16[16,18432]{1,0:T(8,128)(2,1)S(1)}, u32[]{:S(2)}, u32[]{:S(2)}) collective-permute-start(bf16[16,18432]{1,0:T(8,128)(2,1)S(1)} %get-tuple-element.18), channel_id=1, source_target_pairs={{0,1},{1,0},{2,3},{3,2},{4,5},{5,4},{6,7},{7,6},{8,9},{9,8},{10,11... | collective-permute-start | bytes 1769480 | tf_op jit(solution)/shard_map/ppermute | solution.py:32
  4.8 8.3 %collective-permute-start = (bf16[16,16512]{1,0:T(8,128)(2,1)S(1)}, bf16[16,16512]{1,0:T(8,128)(2,1)S(1)}, u32[]{:S(2)}, u32[]{:S(2)}) collective-permute-start(bf16[16,16512]{1,0:T(8,128)(2,1)S(1)} %shard_map.83.refs_0_.sent_ref), channel_id=1, source_target_pairs={{0,1},{1,0},{2,3},{3,2},{4,5},{5,4},{6,7},{7,6},{8,9},{9,8},{10,11... | collective-permute-start | bytes 1585160 | tf_op jit(solution)/shard_map/ppermute | solution.py:32
  5.7 11.5 %collective-permute-start.9 = (bf16[16,10240]{1,0:T(8,128)(2,1)S(1)}, bf16[16,10240]{1,0:T(8,128)(2,1)S(1)}, u32[]{:S(2)}, u32[]{:S(2)}) collective-permute-start(bf16[16,10240]{1,0:T(8,128)(2,1)S(1)} %get-tuple-element.19._), channel_id=1, source_target_pairs={{0,2},{1,3},{2,0},{3,1},{4,6},{5,7},{6,4},{7,5},{8,10},{9,11},{10,... | collective-permute-start | bytes 983048 | tf_op jit(solution)/shard_map/ppermute | solution.py:32
  8.8 12.8 %collective-permute-start.7 = (bf16[16,4096]{1,0:T(8,128)(2,1)S(1)}, bf16[16,4096]{1,0:T(8,128)(2,1)S(1)}, u32[]{:S(2)}, u32[]{:S(2)}) collective-permute-start(bf16[16,4096]{1,0:T(8,128)(2,1)S(1)} %copy-done.5), channel_id=1, source_target_pairs={{0,8},{1,9},{2,10},{3,11},{4,12},{5,13},{6,14},{7,15},{8,0},{9,1},... | collective-permute-start | bytes 393224 | tf_op jit(solution)/shard_map/ppermute | solution.py:32
  11.4 10.2 %collective-permute-start.6 = (bf16[16,4096]{1,0:T(8,128)(2,1)S(1)}, bf16[16,4096]{1,0:T(8,128)(2,1)S(1)}, u32[]{:S(2)}, u32[]{:S(2)}) collective-permute-start(bf16[16,4096]{1,0:T(8,128)(2,1)S(1)} %copy-done.5), channel_id=1, source_target_pairs={{0,4},{1,5},{2,6},{3,7},{4,0},{5,1},{6,2},{7,3},{8,12},{9,13},{10,... | collective-permute-start | bytes 393224 | tf_op jit(solution)/shard_map/ppermute | solution.py:32
  12.9 8.6 %collective-permute-start.8 = (bf16[16,4096]{1,0:T(8,128)(2,1)S(1)}, bf16[16,4096]{1,0:T(8,128)(2,1)S(1)}, u32[]{:S(2)}, u32[]{:S(2)}) collective-permute-start(bf16[16,4096]{1,0:T(8,128)(2,1)S(1)} %copy-done.5), channel_id=1, source_target_pairs={{0,12},{1,13},{2,14},{3,15},{4,8},{5,9},{6,10},{7,11},{8,4},{9,5},... | collective-permute-start | bytes 393224 | tf_op jit(solution)/shard_map/ppermute | solution.py:32
  13.2 15.7 %collective-permute-start.2 = (bf16[32,8320]{1,0:T(8,128)(2,1)S(1)}, bf16[32,8320]{1,0:T(8,128)(2,1)S(1)}, u32[]{:S(2)}, u32[]{:S(2)}) collective-permute-start(bf16[32,8320]{1,0:T(8,128)(2,1)S(1)} %shard_map.86.refs_0_), channel_id=1, source_target_pairs={{0,2},{1,3},{2,0},{3,1},{4,6},{5,7},{6,4},{7,5},{8,10},{9,11},{10,... | collective-permute-start | bytes 1597448 | tf_op jit(solution)/shard_map/ppermute | solution.py:32
  21.6 17.7 %collective-permute-start.10 = (bf16[64,4096]{1,0:T(8,128)(2,1)S(1)}, bf16[64,4096]{1,0:T(8,128)(2,1)S(1)}, u32[]{:S(2)}, u32[]{:S(2)}) collective-permute-start(bf16[64,4096]{1,0:T(8,128)(2,1)S(1)} %shard_map.89.refs_0_.__0_), channel_id=1, source_target_pairs={{0,2},{1,3},{2,0},{3,1},{4,6},{5,7},{6,4},{7,5},{8,10},{9,11},{10,... | collective-permute-start | bytes 1572872 | tf_op jit(solution)/shard_map/ppermute | solution.py:32
  22.2 8.0 %collective-permute-start.11 = (bf16[16,4096]{1,0:T(8,128)(2,1)S(1)}, bf16[16,4096]{1,0:T(8,128)(2,1)S(1)}, u32[]{:S(2)}, u32[]{:S(2)}) collective-permute-start(bf16[16,4096]{1,0:T(8,128)(2,1)S(1)} %get-tuple-element.26), channel_id=1, source_target_pairs={{0,4},{1,5},{2,6},{3,7},{4,0},{5,1},{6,2},{7,3},{8,12},{9,13},{10,... | collective-permute-start | bytes 393224 | tf_op jit(solution)/shard_map/ppermute | solution.py:32
  24.5 12.2 %collective-permute-start.12 = (bf16[16,4096]{1,0:T(8,128)(2,1)S(1)}, bf16[16,4096]{1,0:T(8,128)(2,1)S(1)}, u32[]{:S(2)}, u32[]{:S(2)}) collective-permute-start(bf16[16,4096]{1,0:T(8,128)(2,1)S(1)} %get-tuple-element.27), channel_id=1, source_target_pairs={{0,8},{1,9},{2,10},{3,11},{4,12},{5,13},{6,14},{7,15},{8,0},{9,1},... | collective-permute-start | bytes 393224 | tf_op jit(solution)/shard_map/ppermute | solution.py:32
  26.5 10.3 %collective-permute-start.13 = (bf16[16,4096]{1,0:T(8,128)(2,1)S(1)}, bf16[16,4096]{1,0:T(8,128)(2,1)S(1)}, u32[]{:S(2)}, u32[]{:S(2)}) collective-permute-start(bf16[16,4096]{1,0:T(8,128)(2,1)S(1)} %get-tuple-element.28), channel_id=1, source_target_pairs={{0,12},{1,13},{2,14},{3,15},{4,8},{5,9},{6,10},{7,11},{8,4},{9,5},... | collective-permute-start | bytes 393224 | tf_op jit(solution)/shard_map/ppermute | solution.py:32
  39.4 6.5 %collective-permute-start.14 = (bf16[64,4096]{1,0:T(8,128)(2,1)S(1)}, bf16[64,4096]{1,0:T(8,128)(2,1)S(1)}, u32[]{:S(2)}, u32[]{:S(2)}) collective-permute-start(bf16[64,4096]{1,0:T(8,128)(2,1)S(1)} %shard_map.93), channel_id=1, source_target_pairs={{0,1},{1,0},{2,3},{3,2},{4,5},{5,4},{6,7},{7,6},{8,9},{9,8},{10,11... | collective-permute-start | bytes 1572872 | tf_op jit(solution)/shard_map/ppermute | solution.py:32
  39.5 6.6 %collective-permute-start.15 = (bf16[64,4096]{1,0:T(8,128)(2,1)S(1)}, bf16[64,4096]{1,0:T(8,128)(2,1)S(1)}, u32[]{:S(2)}, u32[]{:S(2)}) collective-permute-start(bf16[64,4096]{1,0:T(8,128)(2,1)S(1)} %shard_map.92.refs_0_), channel_id=1, source_target_pairs={{0,1},{1,0},{2,3},{3,2},{4,5},{5,4},{6,7},{7,6},{8,9},{9,8},{10,11... | collective-permute-start | bytes 1572872 | tf_op jit(solution)/shard_map/ppermute | solution.py:32
  40.0 7.8 %collective-permute-start.16 = (bf16[16,4096]{1,0:T(8,128)(2,1)S(1)}, bf16[16,4096]{1,0:T(8,128)(2,1)S(1)}, u32[]{:S(2)}, u32[]{:S(2)}) collective-permute-start(bf16[16,4096]{1,0:T(8,128)(2,1)S(1)} %shard_map.91.__1_.refs_0_.refs_2_), channel_id=1, source_target_pairs={{0,16},{16,0},{1,17},{17,1},{2,18},{18,2},{3,19},{19,3},{4,20},{20... | collective-permute-start | bytes 393224 | tf_op jit(solution)/shard_map/ppermute | solution.py:32
  41.7 29.7 %collective-permute-start.3 = (bf16[64,2176]{1,0:T(8,128)(2,1)S(1)}, bf16[64,2176]{1,0:T(8,128)(2,1)S(1)}, u32[]{:S(2)}, u32[]{:S(2)}) collective-permute-start(bf16[64,2176]{1,0:T(8,128)(2,1)S(1)} %get-tuple-element.21), channel_id=1, source_target_pairs={{0,4},{1,5},{2,6},{3,7},{4,0},{5,1},{6,2},{7,3},{8,12},{9,13},{10,... | collective-permute-start | bytes 835592 | tf_op jit(solution)/shard_map/ppermute | solution.py:32
  43.3 28.1 %collective-permute-start.4 = (bf16[64,2176]{1,0:T(8,128)(2,1)S(1)}, bf16[64,2176]{1,0:T(8,128)(2,1)S(1)}, u32[]{:S(2)}, u32[]{:S(2)}) collective-permute-start(bf16[64,2176]{1,0:T(8,128)(2,1)S(1)} %get-tuple-element.22), channel_id=1, source_target_pairs={{0,8},{1,9},{2,10},{3,11},{4,12},{5,13},{6,14},{7,15},{8,0},{9,1},... | collective-permute-start | bytes 835592 | tf_op jit(solution)/shard_map/ppermute | solution.py:32
  45.9 25.5 %collective-permute-start.5 = (bf16[64,2176]{1,0:T(8,128)(2,1)S(1)}, bf16[64,2176]{1,0:T(8,128)(2,1)S(1)}, u32[]{:S(2)}, u32[]{:S(2)}) collective-permute-start(bf16[64,2176]{1,0:T(8,128)(2,1)S(1)} %get-tuple-element.23), channel_id=1, source_target_pairs={{0,12},{1,13},{2,14},{3,15},{4,8},{5,9},{6,10},{7,11},{8,4},{9,5},... | collective-permute-start | bytes 835592 | tf_op jit(solution)/shard_map/ppermute | solution.py:32
  46.1 2.3 %collective-permute-start.17 = (bf16[16,4096]{1,0:T(8,128)(2,1)S(1)}, bf16[16,4096]{1,0:T(8,128)(2,1)S(1)}, u32[]{:S(2)}, u32[]{:S(2)}) collective-permute-start(bf16[16,4096]{1,0:T(8,128)(2,1)S(1)} %shard_map.91.__1_.refs_0_.refs_2_), channel_id=1, source_target_pairs={{0,1},{1,0},{2,3},{3,2},{4,5},{5,4},{6,7},{7,6},{8,9},{9,8},{10,11... | collective-permute-start | bytes 393224 | tf_op jit(solution)/shard_map/ppermute | solution.py:32
  47.9 1.6 %collective-permute-start.18 = (bf16[16,4096]{1,0:T(8,128)(2,1)S(1)}, bf16[16,4096]{1,0:T(8,128)(2,1)S(1)}, u32[]{:S(2)}, u32[]{:S(2)}) collective-permute-start(bf16[16,4096]{1,0:T(8,128)(2,1)S(1)} %shard_map.95.refs_1_.refs_4_), channel_id=1, source_target_pairs={{0,1},{1,0},{2,3},{3,2},{4,5},{5,4},{6,7},{7,6},{8,9},{9,8},{10,11... | collective-permute-start | bytes 393224 | tf_op jit(solution)/shard_map/ppermute | solution.py:32
  74.4 1.9 %collective-permute-start.21 = (f32[2,8,1]{2,1,0:T(8,128)S(1)}, f32[2,8,1]{2,1,0:T(8,128)S(1)}, u32[]{:S(2)}, u32[]{:S(2)}) collective-permute-start(f32[2,8,1]{2,1,0:T(8,128)S(1)} %shard_map.97), channel_id=1, source_target_pairs={{0,1},{1,0},{2,3},{3,2},{4,5},{5,4},{6,7},{7,6},{8,9},{9,8},{10,11... | collective-permute-start | bytes 200 | tf_op jit(solution)/shard_map/ppermute | solution.py:32
  74.8 3.7 %collective-permute-start.20 = (f32[2,8,1]{2,1,0:T(8,128)S(1)}, f32[2,8,1]{2,1,0:T(8,128)S(1)}, u32[]{:S(2)}, u32[]{:S(2)}) collective-permute-start(f32[2,8,1]{2,1,0:T(8,128)S(1)} %shard_map.97), channel_id=1, source_target_pairs={{0,2},{1,3},{2,0},{3,1},{4,6},{5,7},{6,4},{7,5},{8,10},{9,11},{10,... | collective-permute-start | bytes 200 | tf_op jit(solution)/shard_map/ppermute | solution.py:32
  76.3 3.1 %collective-permute-start.19 = (f32[2,8,1]{2,1,0:T(8,128)S(1)}, f32[2,8,1]{2,1,0:T(8,128)S(1)}, u32[]{:S(2)}, u32[]{:S(2)}) collective-permute-start(f32[2,8,1]{2,1,0:T(8,128)S(1)} %shard_map.97), channel_id=1, source_target_pairs={{0,3},{1,2},{2,1},{3,0},{4,7},{5,6},{6,5},{7,4},{8,11},{9,10},{10,... | collective-permute-start | bytes 200 | tf_op jit(solution)/shard_map/ppermute | solution.py:32
  79.5 3.7 %collective-permute-start.22 = (f32[2,8,1]{2,1,0:T(8,128)S(1)}, f32[2,8,1]{2,1,0:T(8,128)S(1)}, u32[]{:S(2)}, u32[]{:S(2)}) collective-permute-start(f32[2,8,1]{2,1,0:T(8,128)S(1)} %add_add_fusion), channel_id=1, source_target_pairs={{0,4},{1,5},{2,6},{3,7},{4,0},{5,1},{6,2},{7,3},{8,12},{9,13},{10,... | collective-permute-start | bytes 200 | tf_op jit(solution)/shard_map/ppermute | solution.py:32
  83.1 4.5 %collective-permute-start.23 = (f32[2,8,1]{2,1,0:T(8,128)S(1)}, f32[2,8,1]{2,1,0:T(8,128)S(1)}, u32[]{:S(2)}, u32[]{:S(2)}) collective-permute-start(f32[2,8,1]{2,1,0:T(8,128)S(1)} %add.18), channel_id=1, source_target_pairs={{0,8},{1,9},{2,10},{3,11},{4,12},{5,13},{6,14},{7,15},{8,0},{9,1},... | collective-permute-start | bytes 200 | tf_op jit(solution)/shard_map/ppermute | solution.py:32
  (8 other events, 73.7 us)

commit v19 on v18

--- a/solution.py
+++ b/solution.py
@@ -285,7 +285,7 @@
     left_refs, half_refs = refs[:batch_count], refs[batch_count:3 * batch_count]
     eig_ref, out_ref, right_ref, turn_ref, pre_a, pre_b = refs[3 * batch_count:]
     rows, chunk = eig_ref.shape
-    tile = min(256, chunk)
+    tile = min(512, chunk)
     s = pl.program_id(0)
 
     @pl.when(s == 0)

time: 88.5 us -> 88.5 us (level)
  no operation moved by 1% of the time
where the time goes in v19:
time: 88.5 us; the launch traced here: 88.3 us
  Pallas kernels  29.4 us (33%)
  waiting for transfers between devices  27.7 us (31%)
  starting transfers between devices  26.7 us (30%)
  local copies, waits for them, and re-layouts  3.66 us (4%)
    ppermute x24, waiting for transfers between devices, swap(): return lax.ppermute(x, axis, [(i, i ^ bit) for i in range(count)])  27.7 us
    ppermute x24, starting transfers between devices, swap(): return lax.ppermute(x, axis, [(i, i ^ bit) for i in range(count)])  26.7 us
    pallas_call x1, Pallas kernels, images(): pl.pallas_call(functools.partial(image_kernel, batch_count, total, per),...  22 us
    unnamed x16, local copies, waits for them, and re-layouts  3.66 us
    pallas_call x1, Pallas kernels, score_parts(): pl.pallas_call(functools.partial(score_kernel, batch_count, ranks, count)...  2.98 us
    pallas_call x2, Pallas kernels, rotate(): pl.pallas_call(functools.partial(rotate_kernel, len(act_pieces), done), i...  2.64 us
  transfers between devices with their start and end apart: 24, of which 10 were waited for; matrix products, arithmetic and copies ran while one was open for 0% of the time, Pallas kernels for 30%

profile of v19, /device:TPU:0, one launch (start us, length us, event | category | flops | bytes accessed | tf_op | source)
XLA Modules:
  0.0 88.3 jit_solution(3732561115898980913)
XLA Ops:
  0.0 1.8 %copy-done.3 = bf16[2,16,36864]{2,1,0:T(8,128)(2,1)S(1)} copy-done((bf16[2,16,36864]{2,1,0:T(8,128)(2,1)S(1)}, bf16[2,16,36864]{2,1,0:T(8,128)(2,1)}, u32[]{:S(2)}) %copy-start.3) | copy-done | bytes 2359320
  2.4 1.2 %copy-done.1 = bf16[16,32768]{1,0:T(8,128)(2,1)S(1)} copy-done((bf16[16,32768]{1,0:T(8,128)(2,1)S(1)}, bf16[16,32768]{1,0:T(8,128)(2,1)}, u32[]{:S(2)}) %copy-start.1) | copy-done | bytes 1048600
  5.7 3.0 %collective-permute-start.9 = (bf16[16,10240]{1,0:T(8,128)(2,1)S(1)}, bf16[16,10240]{1,0:T(8,128)(2,1)S(1)}, u32[]{:S(2)}, u32[]{:S(2)}) collective-permute-start(bf16[16,10240]{1,0:T(8,128)(2,1)S(1)} %get-tuple-element.19._), channel_id=1, source_target_pairs={{0,2},{1,3},{2,0},{3,1},{4,6},{5,7},{6,4},{7,5},{8,10},{9,11},{10,... | collective-permute-start | bytes 983048 | tf_op jit(solution)/shard_map/ppermute | solution.py:32
  8.8 2.6 %collective-permute-start.7 = (bf16[16,4096]{1,0:T(8,128)(2,1)S(1)}, bf16[16,4096]{1,0:T(8,128)(2,1)S(1)}, u32[]{:S(2)}, u32[]{:S(2)}) collective-permute-start(bf16[16,4096]{1,0:T(8,128)(2,1)S(1)} %copy-done.5), channel_id=1, source_target_pairs={{0,8},{1,9},{2,10},{3,11},{4,12},{5,13},{6,14},{7,15},{8,0},{9,1},... | collective-permute-start | bytes 393224 | tf_op jit(solution)/shard_map/ppermute | solution.py:32
  11.4 1.6 %collective-permute-start.6 = (bf16[16,4096]{1,0:T(8,128)(2,1)S(1)}, bf16[16,4096]{1,0:T(8,128)(2,1)S(1)}, u32[]{:S(2)}, u32[]{:S(2)}) collective-permute-start(bf16[16,4096]{1,0:T(8,128)(2,1)S(1)} %copy-done.5), channel_id=1, source_target_pairs={{0,4},{1,5},{2,6},{3,7},{4,0},{5,1},{6,2},{7,3},{8,12},{9,13},{10,... | collective-permute-start | bytes 393224 | tf_op jit(solution)/shard_map/ppermute | solution.py:32
  13.6 3.7 %collective-permute-done.9.got_ref = bf16[16,10240]{1,0:T(8,128)(2,1)S(1)} collective-permute-done((bf16[16,10240]{1,0:T(8,128)(2,1)S(1)}, bf16[16,10240]{1,0:T(8,128)(2,1)S(1)}, u32[]{:S(2)}, u32[]{:S(2)}) %collective-permute-start.9) | collective-permute-done | bytes 327712 | tf_op jit(solution)/shard_map/ppermute | solution.py:32
  17.4 4.2 %collective-permute-done.7.refs_2_ = bf16[16,4096]{1,0:T(8,128)(2,1)S(1)} collective-permute-done((bf16[16,4096]{1,0:T(8,128)(2,1)S(1)}, bf16[16,4096]{1,0:T(8,128)(2,1)S(1)}, u32[]{:S(2)}, u32[]{:S(2)}) %collective-permute-start.7) | collective-permute-done | bytes 131104 | tf_op jit(solution)/shard_map/ppermute | solution.py:32
  22.2 2.4 %collective-permute-start.11 = (bf16[16,4096]{1,0:T(8,128)(2,1)S(1)}, bf16[16,4096]{1,0:T(8,128)(2,1)S(1)}, u32[]{:S(2)}, u32[]{:S(2)}) collective-permute-start(bf16[16,4096]{1,0:T(8,128)(2,1)S(1)} %get-tuple-element.26), channel_id=1, source_target_pairs={{0,4},{1,5},{2,6},{3,7},{4,0},{5,1},{6,2},{7,3},{8,12},{9,13},{10,... | collective-permute-start | bytes 393224 | tf_op jit(solution)/shard_map/ppermute | solution.py:32
  24.5 1.9 %collective-permute-start.12 = (bf16[16,4096]{1,0:T(8,128)(2,1)S(1)}, bf16[16,4096]{1,0:T(8,128)(2,1)S(1)}, u32[]{:S(2)}, u32[]{:S(2)}) collective-permute-start(bf16[16,4096]{1,0:T(8,128)(2,1)S(1)} %get-tuple-element.27), channel_id=1, source_target_pairs={{0,8},{1,9},{2,10},{3,11},{4,12},{5,13},{6,14},{7,15},{8,0},{9,1},... | collective-permute-start | bytes 393224 | tf_op jit(solution)/shard_map/ppermute | solution.py:32
  26.5 1.5 %collective-permute-start.13 = (bf16[16,4096]{1,0:T(8,128)(2,1)S(1)}, bf16[16,4096]{1,0:T(8,128)(2,1)S(1)}, u32[]{:S(2)}, u32[]{:S(2)}) collective-permute-start(bf16[16,4096]{1,0:T(8,128)(2,1)S(1)} %get-tuple-element.28), channel_id=1, source_target_pairs={{0,12},{1,13},{2,14},{3,15},{4,8},{5,9},{6,10},{7,11},{8,4},{9,5},... | collective-permute-start | bytes 393224 | tf_op jit(solution)/shard_map/ppermute | solution.py:32
  29.0 1.2 %collective-permute-done.11.refs_1_ = bf16[16,4096]{1,0:T(8,128)(2,1)S(1)} collective-permute-done((bf16[16,4096]{1,0:T(8,128)(2,1)S(1)}, bf16[16,4096]{1,0:T(8,128)(2,1)S(1)}, u32[]{:S(2)}, u32[]{:S(2)}) %collective-permute-start.11) | collective-permute-done | bytes 131104 | tf_op jit(solution)/shard_map/ppermute | solution.py:32
  30.1 6.6 %collective-permute-done.12.refs_2_ = bf16[16,4096]{1,0:T(8,128)(2,1)S(1)} collective-permute-done((bf16[16,4096]{1,0:T(8,128)(2,1)S(1)}, bf16[16,4096]{1,0:T(8,128)(2,1)S(1)}, u32[]{:S(2)}, u32[]{:S(2)}) %collective-permute-start.12) | collective-permute-done | bytes 131104 | tf_op jit(solution)/shard_map/ppermute | solution.py:32
  36.8 2.5 %collective-permute-done.10.refs_4_.__0_ = bf16[64,4096]{1,0:T(8,128)(2,1)S(1)} collective-permute-done((bf16[64,4096]{1,0:T(8,128)(2,1)S(1)}, bf16[64,4096]{1,0:T(8,128)(2,1)S(1)}, u32[]{:S(2)}, u32[]{:S(2)}) %collective-permute-start.10) | collective-permute-done | bytes 524320 | tf_op jit(solution)/shard_map/ppermute | solution.py:32
  40.0 1.7 %collective-permute-start.16 = (bf16[16,4096]{1,0:T(8,128)(2,1)S(1)}, bf16[16,4096]{1,0:T(8,128)(2,1)S(1)}, u32[]{:S(2)}, u32[]{:S(2)}) collective-permute-start(bf16[16,4096]{1,0:T(8,128)(2,1)S(1)} %shard_map.91.__1_.refs_0_.refs_2_), channel_id=1, source_target_pairs={{0,16},{16,0},{1,17},{17,1},{2,18},{18,2},{3,19},{19,3},{4,20},{20... | collective-permute-start | bytes 393224 | tf_op jit(solution)/shard_map/ppermute | solution.py:32
  41.7 1.6 %collective-permute-start.3 = (bf16[64,2176]{1,0:T(8,128)(2,1)S(1)}, bf16[64,2176]{1,0:T(8,128)(2,1)S(1)}, u32[]{:S(2)}, u32[]{:S(2)}) collective-permute-start(bf16[64,2176]{1,0:T(8,128)(2,1)S(1)} %get-tuple-element.21), channel_id=1, source_target_pairs={{0,4},{1,5},{2,6},{3,7},{4,0},{5,1},{6,2},{7,3},{8,12},{9,13},{10,... | collective-permute-start | bytes 835592 | tf_op jit(solution)/shard_map/ppermute | solution.py:32
  43.3 2.6 %collective-permute-start.4 = (bf16[64,2176]{1,0:T(8,128)(2,1)S(1)}, bf16[64,2176]{1,0:T(8,128)(2,1)S(1)}, u32[]{:S(2)}, u32[]{:S(2)}) collective-permute-start(bf16[64,2176]{1,0:T(8,128)(2,1)S(1)} %get-tuple-element.22), channel_id=1, source_target_pairs={{0,8},{1,9},{2,10},{3,11},{4,12},{5,13},{6,14},{7,15},{8,0},{9,1},... | collective-permute-start | bytes 835592 | tf_op jit(solution)/shard_map/ppermute | solution.py:32
  46.1 1.7 %shard_map.94.__1_.rot_ref = bf16[4096,256]{1,0:T(8,128)(2,1)S(1)} custom-call(bf16[64,4096]{1,0:T(8,128)(2,1)S(1)} %shard_map.92.refs_0_, bf16[64,4096]{1,0:T(8,128)(2,1)S(1)} %collective-permute-done.14.refs_1_, bf16[64,4096]{1,0:T(8,128)(2,1)S(1)} %collective-permute-done.15.refs_2_, bf16[512,4096]{1,0:T(8,128)(2,1)S(1)} %copy-done, ...), custom_call_target="tpu_custom_call" | custom-call | bytes 1 | tf_op jit(solution)/shard_map/pallas_call | solution.py:274
  49.4 22.0 %shard_map.96.refs_9_ = f32[2,2048,256]{2,1,0:T(8,128)S(1)} custom-call(bf16[4096,256]{1,0:T(8,128)(2,1)S(1)} %shard_map.94.__1_.rot_ref, bf16[16,4096]{1,0:T(8,128)(2,1)S(1)} %shard_map.91.__1_.refs_0_.refs_2_, bf16[16,4096]{1,0:T(8,128)(2,1)S(1)} %shard_map.95.refs_1_.refs_4_, bf16[16,4096]{1,0:T(8,128)(2,1)S(1)} %shard_map.91.__1_.refs_0_.refs_2_, ...), custom_call_target="tpu_custom_call" | custom-call | flops 1000000000 | bytes 1 | tf_op jit(solution)/shard_map/pallas_call | solution.py:361
  71.5 3.0 %shard_map.97 = f32[2,8,1]{2,1,0:T(8,128)S(1)} custom-call(bf16[64,2176]{1,0:T(8,128)(2,1)S(1)} %get-tuple-element.20.refs_6_.refs_0_.refs_4_, bf16[64,2176]{1,0:T(8,128)(2,1)S(1)} %collective-permute-done.3.refs_1_.refs_5_, bf16[64,2176]{1,0:T(8,128)(2,1)S(1)} %collective-permute-done.4.refs_2_.refs_6_, ...), custom_call_target="tpu_custom_call" | custom-call | flops 536870912 | bytes 4194304 | tf_op jit(solution)/shard_map/pallas_call | solution.py:417
  74.8 1.5 %collective-permute-start.20 = (f32[2,8,1]{2,1,0:T(8,128)S(1)}, f32[2,8,1]{2,1,0:T(8,128)S(1)}, u32[]{:S(2)}, u32[]{:S(2)}) collective-permute-start(f32[2,8,1]{2,1,0:T(8,128)S(1)} %shard_map.97), channel_id=1, source_target_pairs={{0,2},{1,3},{2,0},{3,1},{4,6},{5,7},{6,4},{7,5},{8,10},{9,11},{10,... | collective-permute-start | bytes 200 | tf_op jit(solution)/shard_map/ppermute | solution.py:32
  76.4 2.1 %collective-permute-done.20 = f32[2,8,1]{2,1,0:T(8,128)S(1)} collective-permute-done((f32[2,8,1]{2,1,0:T(8,128)S(1)}, f32[2,8,1]{2,1,0:T(8,128)S(1)}, u32[]{:S(2)}, u32[]{:S(2)}) %collective-permute-start.20) | collective-permute-done | bytes 96 | tf_op jit(solution)/shard_map/ppermute | solution.py:32
  80.2 2.9 %collective-permute-done.22 = f32[2,8,1]{2,1,0:T(8,128)S(1)} collective-permute-done((f32[2,8,1]{2,1,0:T(8,128)S(1)}, f32[2,8,1]{2,1,0:T(8,128)S(1)}, u32[]{:S(2)}, u32[]{:S(2)}) %collective-permute-start.22) | collective-permute-done | bytes 96 | tf_op jit(solution)/shard_map/ppermute | solution.py:32
  83.1 2.2 %collective-permute-start.23 = (f32[2,8,1]{2,1,0:T(8,128)S(1)}, f32[2,8,1]{2,1,0:T(8,128)S(1)}, u32[]{:S(2)}, u32[]{:S(2)}) collective-permute-start(f32[2,8,1]{2,1,0:T(8,128)S(1)} %add.18), channel_id=1, source_target_pairs={{0,8},{1,9},{2,10},{3,11},{4,12},{5,13},{6,14},{7,15},{8,0},{9,1},... | collective-permute-start | bytes 200 | tf_op jit(solution)/shard_map/ppermute | solution.py:32
  85.3 2.4 %collective-permute-done.23 = f32[2,8,1]{2,1,0:T(8,128)S(1)} collective-permute-done((f32[2,8,1]{2,1,0:T(8,128)S(1)}, f32[2,8,1]{2,1,0:T(8,128)S(1)}, u32[]{:S(2)}, u32[]{:S(2)}) %collective-permute-start.23) | collective-permute-done | bytes 96 | tf_op jit(solution)/shard_map/ppermute | solution.py:32
  (59 shorter events, 10.3 us)
Async XLA Ops:
  1.8 3.7 %collective-permute-start.1 = (bf16[16,18432]{1,0:T(8,128)(2,1)S(1)}, bf16[16,18432]{1,0:T(8,128)(2,1)S(1)}, u32[]{:S(2)}, u32[]{:S(2)}) collective-permute-start(bf16[16,18432]{1,0:T(8,128)(2,1)S(1)} %get-tuple-element.18), channel_id=1, source_target_pairs={{0,1},{1,0},{2,3},{3,2},{4,5},{5,4},{6,7},{7,6},{8,9},{9,8},{10,11... | collective-permute-start | bytes 1769480 | tf_op jit(solution)/shard_map/ppermute | solution.py:32
  4.8 8.3 %collective-permute-start = (bf16[16,16512]{1,0:T(8,128)(2,1)S(1)}, bf16[16,16512]{1,0:T(8,128)(2,1)S(1)}, u32[]{:S(2)}, u32[]{:S(2)}) collective-permute-start(bf16[16,16512]{1,0:T(8,128)(2,1)S(1)} %shard_map.83.refs_0_.sent_ref), channel_id=1, source_target_pairs={{0,1},{1,0},{2,3},{3,2},{4,5},{5,4},{6,7},{7,6},{8,9},{9,8},{10,11... | collective-permute-start | bytes 1585160 | tf_op jit(solution)/shard_map/ppermute | solution.py:32
  5.7 11.5 %collective-permute-start.9 = (bf16[16,10240]{1,0:T(8,128)(2,1)S(1)}, bf16[16,10240]{1,0:T(8,128)(2,1)S(1)}, u32[]{:S(2)}, u32[]{:S(2)}) collective-permute-start(bf16[16,10240]{1,0:T(8,128)(2,1)S(1)} %get-tuple-element.19._), channel_id=1, source_target_pairs={{0,2},{1,3},{2,0},{3,1},{4,6},{5,7},{6,4},{7,5},{8,10},{9,11},{10,... | collective-permute-start | bytes 983048 | tf_op jit(solution)/shard_map/ppermute | solution.py:32
  8.8 12.8 %collective-permute-start.7 = (bf16[16,4096]{1,0:T(8,128)(2,1)S(1)}, bf16[16,4096]{1,0:T(8,128)(2,1)S(1)}, u32[]{:S(2)}, u32[]{:S(2)}) collective-permute-start(bf16[16,4096]{1,0:T(8,128)(2,1)S(1)} %copy-done.5), channel_id=1, source_target_pairs={{0,8},{1,9},{2,10},{3,11},{4,12},{5,13},{6,14},{7,15},{8,0},{9,1},... | collective-permute-start | bytes 393224 | tf_op jit(solution)/shard_map/ppermute | solution.py:32
  11.4 10.2 %collective-permute-start.6 = (bf16[16,4096]{1,0:T(8,128)(2,1)S(1)}, bf16[16,4096]{1,0:T(8,128)(2,1)S(1)}, u32[]{:S(2)}, u32[]{:S(2)}) collective-permute-start(bf16[16,4096]{1,0:T(8,128)(2,1)S(1)} %copy-done.5), channel_id=1, source_target_pairs={{0,4},{1,5},{2,6},{3,7},{4,0},{5,1},{6,2},{7,3},{8,12},{9,13},{10,... | collective-permute-start | bytes 393224 | tf_op jit(solution)/shard_map/ppermute | solution.py:32
  12.9 8.6 %collective-permute-start.8 = (bf16[16,4096]{1,0:T(8,128)(2,1)S(1)}, bf16[16,4096]{1,0:T(8,128)(2,1)S(1)}, u32[]{:S(2)}, u32[]{:S(2)}) collective-permute-start(bf16[16,4096]{1,0:T(8,128)(2,1)S(1)} %copy-done.5), channel_id=1, source_target_pairs={{0,12},{1,13},{2,14},{3,15},{4,8},{5,9},{6,10},{7,11},{8,4},{9,5},... | collective-permute-start | bytes 393224 | tf_op jit(solution)/shard_map/ppermute | solution.py:32
  13.2 15.7 %collective-permute-start.2 = (bf16[32,8320]{1,0:T(8,128)(2,1)S(1)}, bf16[32,8320]{1,0:T(8,128)(2,1)S(1)}, u32[]{:S(2)}, u32[]{:S(2)}) collective-permute-start(bf16[32,8320]{1,0:T(8,128)(2,1)S(1)} %shard_map.86.refs_0_), channel_id=1, source_target_pairs={{0,2},{1,3},{2,0},{3,1},{4,6},{5,7},{6,4},{7,5},{8,10},{9,11},{10,... | collective-permute-start | bytes 1597448 | tf_op jit(solution)/shard_map/ppermute | solution.py:32
  21.6 17.7 %collective-permute-start.10 = (bf16[64,4096]{1,0:T(8,128)(2,1)S(1)}, bf16[64,4096]{1,0:T(8,128)(2,1)S(1)}, u32[]{:S(2)}, u32[]{:S(2)}) collective-permute-start(bf16[64,4096]{1,0:T(8,128)(2,1)S(1)} %shard_map.89.refs_0_.__0_), channel_id=1, source_target_pairs={{0,2},{1,3},{2,0},{3,1},{4,6},{5,7},{6,4},{7,5},{8,10},{9,11},{10,... | collective-permute-start | bytes 1572872 | tf_op jit(solution)/shard_map/ppermute | solution.py:32
  22.2 8.0 %collective-permute-start.11 = (bf16[16,4096]{1,0:T(8,128)(2,1)S(1)}, bf16[16,4096]{1,0:T(8,128)(2,1)S(1)}, u32[]{:S(2)}, u32[]{:S(2)}) collective-permute-start(bf16[16,4096]{1,0:T(8,128)(2,1)S(1)} %get-tuple-element.26), channel_id=1, source_target_pairs={{0,4},{1,5},{2,6},{3,7},{4,0},{5,1},{6,2},{7,3},{8,12},{9,13},{10,... | collective-permute-start | bytes 393224 | tf_op jit(solution)/shard_map/ppermute | solution.py:32
  24.5 12.2 %collective-permute-start.12 = (bf16[16,4096]{1,0:T(8,128)(2,1)S(1)}, bf16[16,4096]{1,0:T(8,128)(2,1)S(1)}, u32[]{:S(2)}, u32[]{:S(2)}) collective-permute-start(bf16[16,4096]{1,0:T(8,128)(2,1)S(1)} %get-tuple-element.27), channel_id=1, source_target_pairs={{0,8},{1,9},{2,10},{3,11},{4,12},{5,13},{6,14},{7,15},{8,0},{9,1},... | collective-permute-start | bytes 393224 | tf_op jit(solution)/shard_map/ppermute | solution.py:32
  26.5 10.3 %collective-permute-start.13 = (bf16[16,4096]{1,0:T(8,128)(2,1)S(1)}, bf16[16,4096]{1,0:T(8,128)(2,1)S(1)}, u32[]{:S(2)}, u32[]{:S(2)}) collective-permute-start(bf16[16,4096]{1,0:T(8,128)(2,1)S(1)} %get-tuple-element.28), channel_id=1, source_target_pairs={{0,12},{1,13},{2,14},{3,15},{4,8},{5,9},{6,10},{7,11},{8,4},{9,5},... | collective-permute-start | bytes 393224 | tf_op jit(solution)/shard_map/ppermute | solution.py:32
  39.4 6.5 %collective-permute-start.14 = (bf16[64,4096]{1,0:T(8,128)(2,1)S(1)}, bf16[64,4096]{1,0:T(8,128)(2,1)S(1)}, u32[]{:S(2)}, u32[]{:S(2)}) collective-permute-start(bf16[64,4096]{1,0:T(8,128)(2,1)S(1)} %shard_map.93), channel_id=1, source_target_pairs={{0,1},{1,0},{2,3},{3,2},{4,5},{5,4},{6,7},{7,6},{8,9},{9,8},{10,11... | collective-permute-start | bytes 1572872 | tf_op jit(solution)/shard_map/ppermute | solution.py:32
  39.5 6.6 %collective-permute-start.15 = (bf16[64,4096]{1,0:T(8,128)(2,1)S(1)}, bf16[64,4096]{1,0:T(8,128)(2,1)S(1)}, u32[]{:S(2)}, u32[]{:S(2)}) collective-permute-start(bf16[64,4096]{1,0:T(8,128)(2,1)S(1)} %shard_map.92.refs_0_), channel_id=1, source_target_pairs={{0,1},{1,0},{2,3},{3,2},{4,5},{5,4},{6,7},{7,6},{8,9},{9,8},{10,11... | collective-permute-start | bytes 1572872 | tf_op jit(solution)/shard_map/ppermute | solution.py:32
  40.0 7.8 %collective-permute-start.16 = (bf16[16,4096]{1,0:T(8,128)(2,1)S(1)}, bf16[16,4096]{1,0:T(8,128)(2,1)S(1)}, u32[]{:S(2)}, u32[]{:S(2)}) collective-permute-start(bf16[16,4096]{1,0:T(8,128)(2,1)S(1)} %shard_map.91.__1_.refs_0_.refs_2_), channel_id=1, source_target_pairs={{0,16},{16,0},{1,17},{17,1},{2,18},{18,2},{3,19},{19,3},{4,20},{20... | collective-permute-start | bytes 393224 | tf_op jit(solution)/shard_map/ppermute | solution.py:32
  41.7 29.7 %collective-permute-start.3 = (bf16[64,2176]{1,0:T(8,128)(2,1)S(1)}, bf16[64,2176]{1,0:T(8,128)(2,1)S(1)}, u32[]{:S(2)}, u32[]{:S(2)}) collective-permute-start(bf16[64,2176]{1,0:T(8,128)(2,1)S(1)} %get-tuple-element.21), channel_id=1, source_target_pairs={{0,4},{1,5},{2,6},{3,7},{4,0},{5,1},{6,2},{7,3},{8,12},{9,13},{10,... | collective-permute-start | bytes 835592 | tf_op jit(solution)/shard_map/ppermute | solution.py:32
  43.3 28.1 %collective-permute-start.4 = (bf16[64,2176]{1,0:T(8,128)(2,1)S(1)}, bf16[64,2176]{1,0:T(8,128)(2,1)S(1)}, u32[]{:S(2)}, u32[]{:S(2)}) collective-permute-start(bf16[64,2176]{1,0:T(8,128)(2,1)S(1)} %get-tuple-element.22), channel_id=1, source_target_pairs={{0,8},{1,9},{2,10},{3,11},{4,12},{5,13},{6,14},{7,15},{8,0},{9,1},... | collective-permute-start | bytes 835592 | tf_op jit(solution)/shard_map/ppermute | solution.py:32
  45.9 25.6 %collective-permute-start.5 = (bf16[64,2176]{1,0:T(8,128)(2,1)S(1)}, bf16[64,2176]{1,0:T(8,128)(2,1)S(1)}, u32[]{:S(2)}, u32[]{:S(2)}) collective-permute-start(bf16[64,2176]{1,0:T(8,128)(2,1)S(1)} %get-tuple-element.23), channel_id=1, source_target_pairs={{0,12},{1,13},{2,14},{3,15},{4,8},{5,9},{6,10},{7,11},{8,4},{9,5},... | collective-permute-start | bytes 835592 | tf_op jit(solution)/shard_map/ppermute | solution.py:32
  46.1 2.3 %collective-permute-start.17 = (bf16[16,4096]{1,0:T(8,128)(2,1)S(1)}, bf16[16,4096]{1,0:T(8,128)(2,1)S(1)}, u32[]{:S(2)}, u32[]{:S(2)}) collective-permute-start(bf16[16,4096]{1,0:T(8,128)(2,1)S(1)} %shard_map.91.__1_.refs_0_.refs_2_), channel_id=1, source_target_pairs={{0,1},{1,0},{2,3},{3,2},{4,5},{5,4},{6,7},{7,6},{8,9},{9,8},{10,11... | collective-permute-start | bytes 393224 | tf_op jit(solution)/shard_map/ppermute | solution.py:32
  47.9 1.6 %collective-permute-start.18 = (bf16[16,4096]{1,0:T(8,128)(2,1)S(1)}, bf16[16,4096]{1,0:T(8,128)(2,1)S(1)}, u32[]{:S(2)}, u32[]{:S(2)}) collective-permute-start(bf16[16,4096]{1,0:T(8,128)(2,1)S(1)} %shard_map.95.refs_1_.refs_4_), channel_id=1, source_target_pairs={{0,1},{1,0},{2,3},{3,2},{4,5},{5,4},{6,7},{7,6},{8,9},{9,8},{10,11... | collective-permute-start | bytes 393224 | tf_op jit(solution)/shard_map/ppermute | solution.py:32
  74.5 1.9 %collective-permute-start.21 = (f32[2,8,1]{2,1,0:T(8,128)S(1)}, f32[2,8,1]{2,1,0:T(8,128)S(1)}, u32[]{:S(2)}, u32[]{:S(2)}) collective-permute-start(f32[2,8,1]{2,1,0:T(8,128)S(1)} %shard_map.97), channel_id=1, source_target_pairs={{0,1},{1,0},{2,3},{3,2},{4,5},{5,4},{6,7},{7,6},{8,9},{9,8},{10,11... | collective-permute-start | bytes 200 | tf_op jit(solution)/shard_map/ppermute | solution.py:32
  74.8 3.7 %collective-permute-start.20 = (f32[2,8,1]{2,1,0:T(8,128)S(1)}, f32[2,8,1]{2,1,0:T(8,128)S(1)}, u32[]{:S(2)}, u32[]{:S(2)}) collective-permute-start(f32[2,8,1]{2,1,0:T(8,128)S(1)} %shard_map.97), channel_id=1, source_target_pairs={{0,2},{1,3},{2,0},{3,1},{4,6},{5,7},{6,4},{7,5},{8,10},{9,11},{10,... | collective-permute-start | bytes 200 | tf_op jit(solution)/shard_map/ppermute | solution.py:32
  76.4 3.1 %collective-permute-start.19 = (f32[2,8,1]{2,1,0:T(8,128)S(1)}, f32[2,8,1]{2,1,0:T(8,128)S(1)}, u32[]{:S(2)}, u32[]{:S(2)}) collective-permute-start(f32[2,8,1]{2,1,0:T(8,128)S(1)} %shard_map.97), channel_id=1, source_target_pairs={{0,3},{1,2},{2,1},{3,0},{4,7},{5,6},{6,5},{7,4},{8,11},{9,10},{10,... | collective-permute-start | bytes 200 | tf_op jit(solution)/shard_map/ppermute | solution.py:32
  79.5 3.7 %collective-permute-start.22 = (f32[2,8,1]{2,1,0:T(8,128)S(1)}, f32[2,8,1]{2,1,0:T(8,128)S(1)}, u32[]{:S(2)}, u32[]{:S(2)}) collective-permute-start(f32[2,8,1]{2,1,0:T(8,128)S(1)} %add_add_fusion), channel_id=1, source_target_pairs={{0,4},{1,5},{2,6},{3,7},{4,0},{5,1},{6,2},{7,3},{8,12},{9,13},{10,... | collective-permute-start | bytes 200 | tf_op jit(solution)/shard_map/ppermute | solution.py:32
  83.1 4.5 %collective-permute-start.23 = (f32[2,8,1]{2,1,0:T(8,128)S(1)}, f32[2,8,1]{2,1,0:T(8,128)S(1)}, u32[]{:S(2)}, u32[]{:S(2)}) collective-permute-start(f32[2,8,1]{2,1,0:T(8,128)S(1)} %add.18), channel_id=1, source_target_pairs={{0,8},{1,9},{2,10},{3,11},{4,12},{5,13},{6,14},{7,15},{8,0},{9,1},... | collective-permute-start | bytes 200 | tf_op jit(solution)/shard_map/ppermute | solution.py:32
  (8 other events, 73.8 us)

commit v20 on v18

--- a/solution.py
+++ b/solution.py
@@ -70,7 +70,90 @@
     )(factors)
 
 
-def flags_kernel(batch_count, owners_ref, _, flag_ref):
+def pick_kernel(step, cols, half, flag_ref, keep_ref, got_ref, *refs):
+    out_refs = refs[-2:] if step == 0 else refs[-((keep_ref.shape[1] - half) // cols):]
+    same = flag_ref[:, step:step + 1]
+    differs = 1 - same
+
+    def chosen(at, size):
+        place = slice(at, at + size)
+        return keep_ref[:, place] * same + got_ref[:, place] * differs
+
+    size = out_refs[0].shape[1] - half
+    shared = chosen(len(out_refs) * size, half)
+    for n, out_ref in enumerate(out_refs):
+        out_ref[:, :size] = chosen(n * size, size)
+        out_ref[:, size:] = shared
+
+
+def pick(flags, keep, got, step, cols, half, after):
+    rows, width = keep.shape
+    parts = 2 if step == 0 else (width - half) // cols
+    size = (width - half) // parts + half
+    return pl.pallas_call(
+        functools.partial(pick_kernel, step, cols, half),
+        in_specs=in_vmem(3) + in_place(len(after)),
+        out_specs=in_vmem(parts),
+        out_shape=[jax.ShapeDtypeStruct((rows, size), keep.dtype)] * parts,
+        compiler_params=params(16),
+        cost_estimate=pl.CostEstimate(flops=0, bytes_accessed=1, transcendentals=0),
+    )(flags, keep, got, *after)
+
+
+def pick_one_kernel(count, flag_ref, *refs):
+    refs[-1][...] = sum(refs[k][...] * flag_ref[:, 2 + k:3 + k] for k in range(count))
+
+
+def pick_one(flags, pieces, after):
+    return pl.pallas_call(
+        functools.partial(pick_one_kernel, len(pieces)),
+        in_specs=in_vmem(1 + len(pieces)) + in_place(len(after)),
+        out_specs=in_vmem(1)[0],
+        out_shape=jax.ShapeDtypeStruct(pieces[0].shape, pieces[0].dtype),
+        compiler_params=params(16),
+        cost_estimate=pl.CostEstimate(flops=0, bytes_accessed=1, transcendentals=0),
+    )(flags, *pieces, *after)
+
+
+def join_kernel(*refs):
+    out_ref = refs[-1]
+    rows = refs[0].shape[0]
+    for n, ref in enumerate(refs[:-2]):
+        out_ref[n * rows:(n + 1) * rows, :] = ref[...]
+
+
+def join(pieces, after):
+    rows, width = pieces[0].shape
+    return pl.pallas_call(
+        join_kernel,
+        in_specs=in_vmem(len(pieces)) + in_place(1),
+        out_specs=in_vmem(1)[0],
+        out_shape=jax.ShapeDtypeStruct((len(pieces) * rows, width), pieces[0].dtype),
+        compiler_params=params(16),
+        cost_estimate=pl.CostEstimate(flops=0, bytes_accessed=1, transcendentals=0),
+    )(*pieces, after)
+
+
+def gate_kernel(*_):
+    pass
+
+
+def gate(array, after):
+    return pl.pallas_call(
+        gate_kernel,
+        in_specs=in_place(1 + len(after)),
+        out_specs=in_place(1)[0],
+        out_shape=jax.ShapeDtypeStruct(array.shape, array.dtype),
+        input_output_aliases={0: 0},
+        compiler_params=params(1),
+        cost_estimate=pl.CostEstimate(flops=0, bytes_accessed=1, transcendentals=0),
+    )(array, *after)
+
+
+def grads_core_kernel(batch_count, owners_ref, ids_ref, grad_ref, _, flag_ref, out_ref):
+    rows, hidden = grad_ref.shape
+    wide = lax.axis_size("wide")
+    cols = hidden // wide
     me, batch = lax.axis_index("wide"), lax.rem(lax.axis_index("groups"), batch_count)
     apart = owners_ref[batch] ^ me
     lane = lax.broadcasted_iota(jnp.int32, flag_ref.shape, 1)
@@ -79,104 +162,6 @@
         same = jnp.where((apart & (1 << step)) == 0, 1.0, 0.0)
         flags = jnp.where(lane == step, same, flags)
     flag_ref[...] = flags.astype(flag_ref.dtype)
-
-
-def owner_flags(owners, after):
-    return pl.pallas_call(
-        functools.partial(flags_kernel, owners.shape[0]),
-        in_specs=in_smem(1) + in_place(1),
-        out_specs=in_vmem(1)[0],
-        out_shape=jax.ShapeDtypeStruct((after.shape[0], LANES), after.dtype),
-        compiler_params=params(16),
-        cost_estimate=pl.CostEstimate(flops=0, bytes_accessed=1, transcendentals=0),
-    )(owners, after)
-
-
-def pick_kernel(step, cols, half, flag_ref, keep_ref, got_ref, *refs):
-    out_refs = refs[-2:] if step == 0 else refs[-((keep_ref.shape[1] - half) // cols):]
-    same = flag_ref[:, step:step + 1]
-    differs = 1 - same
-
-    def chosen(at, size):
-        place = slice(at, at + size)
-        return keep_ref[:, place] * same + got_ref[:, place] * differs
-
-    size = out_refs[0].shape[1] - half
-    shared = chosen(len(out_refs) * size, half)
-    for n, out_ref in enumerate(out_refs):
-        out_ref[:, :size] = chosen(n * size, size)
-        out_ref[:, size:] = shared
-
-
-def pick(flags, keep, got, step, cols, half, after):
-    rows, width = keep.shape
-    parts = 2 if step == 0 else (width - half) // cols
-    size = (width - half) // parts + half
-    return pl.pallas_call(
-        functools.partial(pick_kernel, step, cols, half),
-        in_specs=in_vmem(3) + in_place(len(after)),
-        out_specs=in_vmem(parts),
-        out_shape=[jax.ShapeDtypeStruct((rows, size), keep.dtype)] * parts,
-        compiler_params=params(16),
-        cost_estimate=pl.CostEstimate(flops=0, bytes_accessed=1, transcendentals=0),
-    )(flags, keep, got, *after)
-
-
-def pick_one_kernel(count, flag_ref, *refs):
-    refs[-1][...] = sum(refs[k][...] * flag_ref[:, 2 + k:3 + k] for k in range(count))
-
-
-def pick_one(flags, pieces, after):
-    return pl.pallas_call(
-        functools.partial(pick_one_kernel, len(pieces)),
-        in_specs=in_vmem(1 + len(pieces)) + in_place(len(after)),
-        out_specs=in_vmem(1)[0],
-        out_shape=jax.ShapeDtypeStruct(pieces[0].shape, pieces[0].dtype),
-        compiler_params=params(16),
-        cost_estimate=pl.CostEstimate(flops=0, bytes_accessed=1, transcendentals=0),
-    )(flags, *pieces, *after)
-
-
-def join_kernel(*refs):
-    out_ref = refs[-1]
-    rows = refs[0].shape[0]
-    for n, ref in enumerate(refs[:-2]):
-        out_ref[n * rows:(n + 1) * rows, :] = ref[...]
-
-
-def join(pieces, after):
-    rows, width = pieces[0].shape
-    return pl.pallas_call(
-        join_kernel,
-        in_specs=in_vmem(len(pieces)) + in_place(1),
-        out_specs=in_vmem(1)[0],
-        out_shape=jax.ShapeDtypeStruct((len(pieces) * rows, width), pieces[0].dtype),
-        compiler_params=params(16),
-        cost_estimate=pl.CostEstimate(flops=0, bytes_accessed=1, transcendentals=0),
-    )(*pieces, after)
-
-
-def gate_kernel(*_):
-    pass
-
-
-def gate(array, after):
-    return pl.pallas_call(
-        gate_kernel,
-        in_specs=in_place(1 + len(after)),
-        out_specs=in_place(1)[0],
-        out_shape=jax.ShapeDtypeStruct(array.shape, array.dtype),
-        input_output_aliases={0: 0},
-        compiler_params=params(1),
-        cost_estimate=pl.CostEstimate(flops=0, bytes_accessed=1, transcendentals=0),
-    )(array, *after)
-
-
-def grads_core_kernel(ids_ref, grad_ref, _, out_ref):
-    rows, hidden = grad_ref.shape
-    wide = lax.axis_size("wide")
-    cols = hidden // wide
-    me = lax.axis_index("wide")
     row = lax.broadcasted_iota(jnp.int32, (rows, LANES), 0)
     ids = jnp.zeros((rows, LANES), jnp.int32)
     for t in range(rows):
@@ -187,16 +172,19 @@
         out_ref[:, q * cols:(q + 1) * cols] = grad_ref[:, pl.ds(src, cols)]
 
 
-def grads_core(ids, grads, after):
+def grads_core(owners, ids, grads, after):
     rows, hidden = grads.shape
     return pl.pallas_call(
-        grads_core_kernel,
-        in_specs=in_smem(1) + in_vmem(1) + in_place(1),
-        out_specs=in_vmem(1)[0],
-        out_shape=jax.ShapeDtypeStruct((rows, hidden // 2 + LANES), grads.dtype),
-        compiler_params=params(16),
-        cost_estimate=pl.CostEstimate(flops=0, bytes_accessed=1, transcendentals=0),
-    )(ids, grads, after)
+        functools.partial(grads_core_kernel, owners.shape[0]),
+        in_specs=in_smem(2) + in_vmem(1) + in_place(1),
+        out_specs=in_vmem(2),
+        out_shape=[
+            jax.ShapeDtypeStruct((QT, LANES), grads.dtype),
+            jax.ShapeDtypeStruct((rows, hidden // 2 + LANES), grads.dtype),
+        ],
+        compiler_params=params(16),
+        cost_estimate=pl.CostEstimate(flops=0, bytes_accessed=1, transcendentals=0),
+    )(owners, ids, grads, after)
 
 
 def grads_y_kernel(grad_ref, sent_ref, got_ref, _, out_ref):
@@ -449,8 +437,7 @@
     half = (query_factors.shape[2] - hidden) // 2
     order = [4 * k + r for r in (0, 2, 1, 3) for k in along_z]
     keep, give = cut_factors(query_factors, order, hidden, batch_count)
-    flags = owner_flags(owners, keep)
-    grads_sent = grads_core(seq_ids, train_grad, keep)
+    flags, grads_sent = grads_core(owners, seq_ids, train_grad, keep)
     keep, give = pick(flags, keep, swap(give, "wide", 1), 0, cols, half, [grads_sent])
     grads_got = swap(grads_sent, "wide", 1)
     grads_over = grads_y(train_grad, grads_sent, grads_got, give)

time: 88.5 us -> 88.5 us (level)
  transfers between devices with their start and end apart: 24 -> 24, of which waited for: 10 -> 10; matrix products, arithmetic and copies ran while one was open for 0% -> 0% of each run, Pallas kernels for 30% -> 29%
where the time goes in v20:
time: 88.5 us; the launch traced here: 88.4 us
  Pallas kernels  28.8 us (33%)
  waiting for transfers between devices  27.7 us (31%)
  starting transfers between devices  26.7 us (30%)
  local copies, waits for them, and re-layouts  4.3 us (5%)
    ppermute x24, waiting for transfers between devices, swap(): return lax.ppermute(x, axis, [(i, i ^ bit) for i in range(count)])  27.7 us
    ppermute x24, starting transfers between devices, swap(): return lax.ppermute(x, axis, [(i, i ^ bit) for i in range(count)])  26.7 us
    pallas_call x1, Pallas kernels, images(): pl.pallas_call(functools.partial(image_kernel, batch_count, total, per),...  22 us
    unnamed x16, local copies, waits for them, and re-layouts  4.3 us
    pallas_call x1, Pallas kernels, score_parts(): pl.pallas_call(functools.partial(score_kernel, batch_count, ranks, count)...  2.98 us
    pallas_call x2, Pallas kernels, rotate(): pl.pallas_call(functools.partial(rotate_kernel, len(act_pieces), done), i...  2.64 us
  transfers between devices with their start and end apart: 24, of which 10 were waited for; matrix products, arithmetic and copies ran while one was open for 0% of the time, Pallas kernels for 29%

profile of v20, /device:TPU:0, one launch (start us, length us, event | category | flops | bytes accessed | tf_op | source)
XLA Modules:
  0.0 88.4 jit_solution(1441735451930897383)
XLA Ops:
  0.0 1.8 %copy-done.3 = bf16[2,16,36864]{2,1,0:T(8,128)(2,1)S(1)} copy-done((bf16[2,16,36864]{2,1,0:T(8,128)(2,1)S(1)}, bf16[2,16,36864]{2,1,0:T(8,128)(2,1)}, u32[]{:S(2)}) %copy-start.3) | copy-done | bytes 2359320
  2.4 1.2 %copy-done.1 = bf16[16,32768]{1,0:T(8,128)(2,1)S(1)} copy-done((bf16[16,32768]{1,0:T(8,128)(2,1)S(1)}, bf16[16,32768]{1,0:T(8,128)(2,1)}, u32[]{:S(2)}) %copy-start.1) | copy-done | bytes 1048600
  5.8 3.0 %collective-permute-start.9 = (bf16[16,10240]{1,0:T(8,128)(2,1)S(1)}, bf16[16,10240]{1,0:T(8,128)(2,1)S(1)}, u32[]{:S(2)}, u32[]{:S(2)}) collective-permute-start(bf16[16,10240]{1,0:T(8,128)(2,1)S(1)} %get-tuple-element.23._), channel_id=1, source_target_pairs={{0,2},{1,3},{2,0},{3,1},{4,6},{5,7},{6,4},{7,5},{8,10},{9,11},{10,... | collective-permute-start | bytes 983048 | tf_op jit(solution)/shard_map/ppermute | solution.py:32
  8.8 2.6 %collective-permute-start.7 = (bf16[16,4096]{1,0:T(8,128)(2,1)S(1)}, bf16[16,4096]{1,0:T(8,128)(2,1)S(1)}, u32[]{:S(2)}, u32[]{:S(2)}) collective-permute-start(bf16[16,4096]{1,0:T(8,128)(2,1)S(1)} %copy-done.5), channel_id=1, source_target_pairs={{0,8},{1,9},{2,10},{3,11},{4,12},{5,13},{6,14},{7,15},{8,0},{9,1},... | collective-permute-start | bytes 393224 | tf_op jit(solution)/shard_map/ppermute | solution.py:32
  11.4 1.6 %collective-permute-start.6 = (bf16[16,4096]{1,0:T(8,128)(2,1)S(1)}, bf16[16,4096]{1,0:T(8,128)(2,1)S(1)}, u32[]{:S(2)}, u32[]{:S(2)}) collective-permute-start(bf16[16,4096]{1,0:T(8,128)(2,1)S(1)} %copy-done.5), channel_id=1, source_target_pairs={{0,4},{1,5},{2,6},{3,7},{4,0},{5,1},{6,2},{7,3},{8,12},{9,13},{10,... | collective-permute-start | bytes 393224 | tf_op jit(solution)/shard_map/ppermute | solution.py:32
  13.6 3.7 %collective-permute-done.9.got_ref = bf16[16,10240]{1,0:T(8,128)(2,1)S(1)} collective-permute-done((bf16[16,10240]{1,0:T(8,128)(2,1)S(1)}, bf16[16,10240]{1,0:T(8,128)(2,1)S(1)}, u32[]{:S(2)}, u32[]{:S(2)}) %collective-permute-start.9) | collective-permute-done | bytes 327712 | tf_op jit(solution)/shard_map/ppermute | solution.py:32
  17.5 4.2 %collective-permute-done.7.refs_2_ = bf16[16,4096]{1,0:T(8,128)(2,1)S(1)} collective-permute-done((bf16[16,4096]{1,0:T(8,128)(2,1)S(1)}, bf16[16,4096]{1,0:T(8,128)(2,1)S(1)}, u32[]{:S(2)}, u32[]{:S(2)}) %collective-permute-start.7) | collective-permute-done | bytes 131104 | tf_op jit(solution)/shard_map/ppermute | solution.py:32
  22.2 2.4 %collective-permute-start.11 = (bf16[16,4096]{1,0:T(8,128)(2,1)S(1)}, bf16[16,4096]{1,0:T(8,128)(2,1)S(1)}, u32[]{:S(2)}, u32[]{:S(2)}) collective-permute-start(bf16[16,4096]{1,0:T(8,128)(2,1)S(1)} %get-tuple-element.30), channel_id=1, source_target_pairs={{0,4},{1,5},{2,6},{3,7},{4,0},{5,1},{6,2},{7,3},{8,12},{9,13},{10,... | collective-permute-start | bytes 393224 | tf_op jit(solution)/shard_map/ppermute | solution.py:32
  24.6 1.9 %collective-permute-start.12 = (bf16[16,4096]{1,0:T(8,128)(2,1)S(1)}, bf16[16,4096]{1,0:T(8,128)(2,1)S(1)}, u32[]{:S(2)}, u32[]{:S(2)}) collective-permute-start(bf16[16,4096]{1,0:T(8,128)(2,1)S(1)} %get-tuple-element.31), channel_id=1, source_target_pairs={{0,8},{1,9},{2,10},{3,11},{4,12},{5,13},{6,14},{7,15},{8,0},{9,1},... | collective-permute-start | bytes 393224 | tf_op jit(solution)/shard_map/ppermute | solution.py:32
  26.5 1.5 %collective-permute-start.13 = (bf16[16,4096]{1,0:T(8,128)(2,1)S(1)}, bf16[16,4096]{1,0:T(8,128)(2,1)S(1)}, u32[]{:S(2)}, u32[]{:S(2)}) collective-permute-start(bf16[16,4096]{1,0:T(8,128)(2,1)S(1)} %get-tuple-element.32), channel_id=1, source_target_pairs={{0,12},{1,13},{2,14},{3,15},{4,8},{5,9},{6,10},{7,11},{8,4},{9,5},... | collective-permute-start | bytes 393224 | tf_op jit(solution)/shard_map/ppermute | solution.py:32
  29.0 1.1 %collective-permute-done.11.refs_1_ = bf16[16,4096]{1,0:T(8,128)(2,1)S(1)} collective-permute-done((bf16[16,4096]{1,0:T(8,128)(2,1)S(1)}, bf16[16,4096]{1,0:T(8,128)(2,1)S(1)}, u32[]{:S(2)}, u32[]{:S(2)}) %collective-permute-start.11) | collective-permute-done | bytes 131104 | tf_op jit(solution)/shard_map/ppermute | solution.py:32
  30.2 6.6 %collective-permute-done.12.refs_2_ = bf16[16,4096]{1,0:T(8,128)(2,1)S(1)} collective-permute-done((bf16[16,4096]{1,0:T(8,128)(2,1)S(1)}, bf16[16,4096]{1,0:T(8,128)(2,1)S(1)}, u32[]{:S(2)}, u32[]{:S(2)}) %collective-permute-start.12) | collective-permute-done | bytes 131104 | tf_op jit(solution)/shard_map/ppermute | solution.py:32
  36.8 2.5 %collective-permute-done.10.refs_4_.__0_ = bf16[64,4096]{1,0:T(8,128)(2,1)S(1)} collective-permute-done((bf16[64,4096]{1,0:T(8,128)(2,1)S(1)}, bf16[64,4096]{1,0:T(8,128)(2,1)S(1)}, u32[]{:S(2)}, u32[]{:S(2)}) %collective-permute-start.10) | collective-permute-done | bytes 524320 | tf_op jit(solution)/shard_map/ppermute | solution.py:32
  40.1 1.7 %collective-permute-start.16 = (bf16[16,4096]{1,0:T(8,128)(2,1)S(1)}, bf16[16,4096]{1,0:T(8,128)(2,1)S(1)}, u32[]{:S(2)}, u32[]{:S(2)}) collective-permute-start(bf16[16,4096]{1,0:T(8,128)(2,1)S(1)} %shard_map.90.__1_.refs_0_.refs_2_), channel_id=1, source_target_pairs={{0,16},{16,0},{1,17},{17,1},{2,18},{18,2},{3,19},{19,3},{4,20},{20... | collective-permute-start | bytes 393224 | tf_op jit(solution)/shard_map/ppermute | solution.py:32
  41.8 1.6 %collective-permute-start.3 = (bf16[64,2176]{1,0:T(8,128)(2,1)S(1)}, bf16[64,2176]{1,0:T(8,128)(2,1)S(1)}, u32[]{:S(2)}, u32[]{:S(2)}) collective-permute-start(bf16[64,2176]{1,0:T(8,128)(2,1)S(1)} %get-tuple-element.25), channel_id=1, source_target_pairs={{0,4},{1,5},{2,6},{3,7},{4,0},{5,1},{6,2},{7,3},{8,12},{9,13},{10,... | collective-permute-start | bytes 835592 | tf_op jit(solution)/shard_map/ppermute | solution.py:32
  43.4 2.6 %collective-permute-start.4 = (bf16[64,2176]{1,0:T(8,128)(2,1)S(1)}, bf16[64,2176]{1,0:T(8,128)(2,1)S(1)}, u32[]{:S(2)}, u32[]{:S(2)}) collective-permute-start(bf16[64,2176]{1,0:T(8,128)(2,1)S(1)} %get-tuple-element.26), channel_id=1, source_target_pairs={{0,8},{1,9},{2,10},{3,11},{4,12},{5,13},{6,14},{7,15},{8,0},{9,1},... | collective-permute-start | bytes 835592 | tf_op jit(solution)/shard_map/ppermute | solution.py:32
  46.2 1.7 %shard_map.93.__1_.rot_ref = bf16[4096,256]{1,0:T(8,128)(2,1)S(1)} custom-call(bf16[64,4096]{1,0:T(8,128)(2,1)S(1)} %shard_map.91.refs_0_, bf16[64,4096]{1,0:T(8,128)(2,1)S(1)} %collective-permute-done.14.refs_1_, bf16[64,4096]{1,0:T(8,128)(2,1)S(1)} %collective-permute-done.15.refs_2_, bf16[512,4096]{1,0:T(8,128)(2,1)S(1)} %copy-done, ...), custom_call_target="tpu_custom_call" | custom-call | bytes 1 | tf_op jit(solution)/shard_map/pallas_call | solution.py:262
  49.5 22.0 %shard_map.95.refs_9_ = f32[2,2048,256]{2,1,0:T(8,128)S(1)} custom-call(bf16[4096,256]{1,0:T(8,128)(2,1)S(1)} %shard_map.93.__1_.rot_ref, bf16[16,4096]{1,0:T(8,128)(2,1)S(1)} %shard_map.90.__1_.refs_0_.refs_2_, bf16[16,4096]{1,0:T(8,128)(2,1)S(1)} %shard_map.94.refs_1_.refs_4_, bf16[16,4096]{1,0:T(8,128)(2,1)S(1)} %shard_map.90.__1_.refs_0_.refs_2_, ...), custom_call_target="tpu_custom_call" | custom-call | flops 1000000000 | bytes 1 | tf_op jit(solution)/shard_map/pallas_call | solution.py:349
  71.5 3.0 %shard_map.96 = f32[2,8,1]{2,1,0:T(8,128)S(1)} custom-call(bf16[64,2176]{1,0:T(8,128)(2,1)S(1)} %get-tuple-element.24.refs_6_.refs_0_.refs_4_, bf16[64,2176]{1,0:T(8,128)(2,1)S(1)} %collective-permute-done.3.refs_1_.refs_5_, bf16[64,2176]{1,0:T(8,128)(2,1)S(1)} %collective-permute-done.4.refs_2_.refs_6_, ...), custom_call_target="tpu_custom_call" | custom-call | flops 536870912 | bytes 4194304 | tf_op jit(solution)/shard_map/pallas_call | solution.py:405
  74.9 1.5 %collective-permute-start.20 = (f32[2,8,1]{2,1,0:T(8,128)S(1)}, f32[2,8,1]{2,1,0:T(8,128)S(1)}, u32[]{:S(2)}, u32[]{:S(2)}) collective-permute-start(f32[2,8,1]{2,1,0:T(8,128)S(1)} %shard_map.96), channel_id=1, source_target_pairs={{0,2},{1,3},{2,0},{3,1},{4,6},{5,7},{6,4},{7,5},{8,10},{9,11},{10,... | collective-permute-start | bytes 200 | tf_op jit(solution)/shard_map/ppermute | solution.py:32
  76.4 2.1 %collective-permute-done.20 = f32[2,8,1]{2,1,0:T(8,128)S(1)} collective-permute-done((f32[2,8,1]{2,1,0:T(8,128)S(1)}, f32[2,8,1]{2,1,0:T(8,128)S(1)}, u32[]{:S(2)}, u32[]{:S(2)}) %collective-permute-start.20) | collective-permute-done | bytes 96 | tf_op jit(solution)/shard_map/ppermute | solution.py:32
  80.2 3.0 %collective-permute-done.22 = f32[2,8,1]{2,1,0:T(8,128)S(1)} collective-permute-done((f32[2,8,1]{2,1,0:T(8,128)S(1)}, f32[2,8,1]{2,1,0:T(8,128)S(1)}, u32[]{:S(2)}, u32[]{:S(2)}) %collective-permute-start.22) | collective-permute-done | bytes 96 | tf_op jit(solution)/shard_map/ppermute | solution.py:32
  83.2 2.2 %collective-permute-start.23 = (f32[2,8,1]{2,1,0:T(8,128)S(1)}, f32[2,8,1]{2,1,0:T(8,128)S(1)}, u32[]{:S(2)}, u32[]{:S(2)}) collective-permute-start(f32[2,8,1]{2,1,0:T(8,128)S(1)} %add.18), channel_id=1, source_target_pairs={{0,8},{1,9},{2,10},{3,11},{4,12},{5,13},{6,14},{7,15},{8,0},{9,1},... | collective-permute-start | bytes 200 | tf_op jit(solution)/shard_map/ppermute | solution.py:32
  85.3 2.4 %collective-permute-done.23 = f32[2,8,1]{2,1,0:T(8,128)S(1)} collective-permute-done((f32[2,8,1]{2,1,0:T(8,128)S(1)}, f32[2,8,1]{2,1,0:T(8,128)S(1)}, u32[]{:S(2)}, u32[]{:S(2)}) %collective-permute-start.23) | collective-permute-done | bytes 96 | tf_op jit(solution)/shard_map/ppermute | solution.py:32
  (58 shorter events, 10.4 us)
Async XLA Ops:
  1.8 3.8 %collective-permute-start.1 = (bf16[16,18432]{1,0:T(8,128)(2,1)S(1)}, bf16[16,18432]{1,0:T(8,128)(2,1)S(1)}, u32[]{:S(2)}, u32[]{:S(2)}) collective-permute-start(bf16[16,18432]{1,0:T(8,128)(2,1)S(1)} %get-tuple-element.22), channel_id=1, source_target_pairs={{0,1},{1,0},{2,3},{3,2},{4,5},{5,4},{6,7},{7,6},{8,9},{9,8},{10,11... | collective-permute-start | bytes 1769480 | tf_op jit(solution)/shard_map/ppermute | solution.py:32
  5.5 7.7 %collective-permute-start = (bf16[16,16512]{1,0:T(8,128)(2,1)S(1)}, bf16[16,16512]{1,0:T(8,128)(2,1)S(1)}, u32[]{:S(2)}, u32[]{:S(2)}) collective-permute-start(bf16[16,16512]{1,0:T(8,128)(2,1)S(1)} %get-tuple-element.20.refs_0_.sent_ref), channel_id=1, source_target_pairs={{0,1},{1,0},{2,3},{3,2},{4,5},{5,4},{6,7},{7,6},{8,9},{9,8},{10,11... | collective-permute-start | bytes 1585160 | tf_op jit(solution)/shard_map/ppermute | solution.py:32
  5.8 11.5 %collective-permute-start.9 = (bf16[16,10240]{1,0:T(8,128)(2,1)S(1)}, bf16[16,10240]{1,0:T(8,128)(2,1)S(1)}, u32[]{:S(2)}, u32[]{:S(2)}) collective-permute-start(bf16[16,10240]{1,0:T(8,128)(2,1)S(1)} %get-tuple-element.23._), channel_id=1, source_target_pairs={{0,2},{1,3},{2,0},{3,1},{4,6},{5,7},{6,4},{7,5},{8,10},{9,11},{10,... | collective-permute-start | bytes 983048 | tf_op jit(solution)/shard_map/ppermute | solution.py:32
  8.8 12.8 %collective-permute-start.7 = (bf16[16,4096]{1,0:T(8,128)(2,1)S(1)}, bf16[16,4096]{1,0:T(8,128)(2,1)S(1)}, u32[]{:S(2)}, u32[]{:S(2)}) collective-permute-start(bf16[16,4096]{1,0:T(8,128)(2,1)S(1)} %copy-done.5), channel_id=1, source_target_pairs={{0,8},{1,9},{2,10},{3,11},{4,12},{5,13},{6,14},{7,15},{8,0},{9,1},... | collective-permute-start | bytes 393224 | tf_op jit(solution)/shard_map/ppermute | solution.py:32
  11.4 10.2 %collective-permute-start.6 = (bf16[16,4096]{1,0:T(8,128)(2,1)S(1)}, bf16[16,4096]{1,0:T(8,128)(2,1)S(1)}, u32[]{:S(2)}, u32[]{:S(2)}) collective-permute-start(bf16[16,4096]{1,0:T(8,128)(2,1)S(1)} %copy-done.5), channel_id=1, source_target_pairs={{0,4},{1,5},{2,6},{3,7},{4,0},{5,1},{6,2},{7,3},{8,12},{9,13},{10,... | collective-permute-start | bytes 393224 | tf_op jit(solution)/shard_map/ppermute | solution.py:32
  13.0 8.6 %collective-permute-start.8 = (bf16[16,4096]{1,0:T(8,128)(2,1)S(1)}, bf16[16,4096]{1,0:T(8,128)(2,1)S(1)}, u32[]{:S(2)}, u32[]{:S(2)}) collective-permute-start(bf16[16,4096]{1,0:T(8,128)(2,1)S(1)} %copy-done.5), channel_id=1, source_target_pairs={{0,12},{1,13},{2,14},{3,15},{4,8},{5,9},{6,10},{7,11},{8,4},{9,5},... | collective-permute-start | bytes 393224 | tf_op jit(solution)/shard_map/ppermute | solution.py:32
  13.3 15.7 %collective-permute-start.2 = (bf16[32,8320]{1,0:T(8,128)(2,1)S(1)}, bf16[32,8320]{1,0:T(8,128)(2,1)S(1)}, u32[]{:S(2)}, u32[]{:S(2)}) collective-permute-start(bf16[32,8320]{1,0:T(8,128)(2,1)S(1)} %shard_map.85.refs_0_), channel_id=1, source_target_pairs={{0,2},{1,3},{2,0},{3,1},{4,6},{5,7},{6,4},{7,5},{8,10},{9,11},{10,... | collective-permute-start | bytes 1597448 | tf_op jit(solution)/shard_map/ppermute | solution.py:32
  21.7 17.7 %collective-permute-start.10 = (bf16[64,4096]{1,0:T(8,128)(2,1)S(1)}, bf16[64,4096]{1,0:T(8,128)(2,1)S(1)}, u32[]{:S(2)}, u32[]{:S(2)}) collective-permute-start(bf16[64,4096]{1,0:T(8,128)(2,1)S(1)} %shard_map.88.refs_0_.__0_), channel_id=1, source_target_pairs={{0,2},{1,3},{2,0},{3,1},{4,6},{5,7},{6,4},{7,5},{8,10},{9,11},{10,... | collective-permute-start | bytes 1572872 | tf_op jit(solution)/shard_map/ppermute | solution.py:32
  22.2 8.0 %collective-permute-start.11 = (bf16[16,4096]{1,0:T(8,128)(2,1)S(1)}, bf16[16,4096]{1,0:T(8,128)(2,1)S(1)}, u32[]{:S(2)}, u32[]{:S(2)}) collective-permute-start(bf16[16,4096]{1,0:T(8,128)(2,1)S(1)} %get-tuple-element.30), channel_id=1, source_target_pairs={{0,4},{1,5},{2,6},{3,7},{4,0},{5,1},{6,2},{7,3},{8,12},{9,13},{10,... | collective-permute-start | bytes 393224 | tf_op jit(solution)/shard_map/ppermute | solution.py:32
  24.6 12.2 %collective-permute-start.12 = (bf16[16,4096]{1,0:T(8,128)(2,1)S(1)}, bf16[16,4096]{1,0:T(8,128)(2,1)S(1)}, u32[]{:S(2)}, u32[]{:S(2)}) collective-permute-start(bf16[16,4096]{1,0:T(8,128)(2,1)S(1)} %get-tuple-element.31), channel_id=1, source_target_pairs={{0,8},{1,9},{2,10},{3,11},{4,12},{5,13},{6,14},{7,15},{8,0},{9,1},... | collective-permute-start | bytes 393224 | tf_op jit(solution)/shard_map/ppermute | solution.py:32
  26.5 10.3 %collective-permute-start.13 = (bf16[16,4096]{1,0:T(8,128)(2,1)S(1)}, bf16[16,4096]{1,0:T(8,128)(2,1)S(1)}, u32[]{:S(2)}, u32[]{:S(2)}) collective-permute-start(bf16[16,4096]{1,0:T(8,128)(2,1)S(1)} %get-tuple-element.32), channel_id=1, source_target_pairs={{0,12},{1,13},{2,14},{3,15},{4,8},{5,9},{6,10},{7,11},{8,4},{9,5},... | collective-permute-start | bytes 393224 | tf_op jit(solution)/shard_map/ppermute | solution.py:32
  39.5 6.5 %collective-permute-start.14 = (bf16[64,4096]{1,0:T(8,128)(2,1)S(1)}, bf16[64,4096]{1,0:T(8,128)(2,1)S(1)}, u32[]{:S(2)}, u32[]{:S(2)}) collective-permute-start(bf16[64,4096]{1,0:T(8,128)(2,1)S(1)} %shard_map.92), channel_id=1, source_target_pairs={{0,1},{1,0},{2,3},{3,2},{4,5},{5,4},{6,7},{7,6},{8,9},{9,8},{10,11... | collective-permute-start | bytes 1572872 | tf_op jit(solution)/shard_map/ppermute | solution.py:32
  39.6 6.6 %collective-permute-start.15 = (bf16[64,4096]{1,0:T(8,128)(2,1)S(1)}, bf16[64,4096]{1,0:T(8,128)(2,1)S(1)}, u32[]{:S(2)}, u32[]{:S(2)}) collective-permute-start(bf16[64,4096]{1,0:T(8,128)(2,1)S(1)} %shard_map.91.refs_0_), channel_id=1, source_target_pairs={{0,1},{1,0},{2,3},{3,2},{4,5},{5,4},{6,7},{7,6},{8,9},{9,8},{10,11... | collective-permute-start | bytes 1572872 | tf_op jit(solution)/shard_map/ppermute | solution.py:32
  40.1 7.8 %collective-permute-start.16 = (bf16[16,4096]{1,0:T(8,128)(2,1)S(1)}, bf16[16,4096]{1,0:T(8,128)(2,1)S(1)}, u32[]{:S(2)}, u32[]{:S(2)}) collective-permute-start(bf16[16,4096]{1,0:T(8,128)(2,1)S(1)} %shard_map.90.__1_.refs_0_.refs_2_), channel_id=1, source_target_pairs={{0,16},{16,0},{1,17},{17,1},{2,18},{18,2},{3,19},{19,3},{4,20},{20... | collective-permute-start | bytes 393224 | tf_op jit(solution)/shard_map/ppermute | solution.py:32
  41.8 29.7 %collective-permute-start.3 = (bf16[64,2176]{1,0:T(8,128)(2,1)S(1)}, bf16[64,2176]{1,0:T(8,128)(2,1)S(1)}, u32[]{:S(2)}, u32[]{:S(2)}) collective-permute-start(bf16[64,2176]{1,0:T(8,128)(2,1)S(1)} %get-tuple-element.25), channel_id=1, source_target_pairs={{0,4},{1,5},{2,6},{3,7},{4,0},{5,1},{6,2},{7,3},{8,12},{9,13},{10,... | collective-permute-start | bytes 835592 | tf_op jit(solution)/shard_map/ppermute | solution.py:32
  43.4 28.1 %collective-permute-start.4 = (bf16[64,2176]{1,0:T(8,128)(2,1)S(1)}, bf16[64,2176]{1,0:T(8,128)(2,1)S(1)}, u32[]{:S(2)}, u32[]{:S(2)}) collective-permute-start(bf16[64,2176]{1,0:T(8,128)(2,1)S(1)} %get-tuple-element.26), channel_id=1, source_target_pairs={{0,8},{1,9},{2,10},{3,11},{4,12},{5,13},{6,14},{7,15},{8,0},{9,1},... | collective-permute-start | bytes 835592 | tf_op jit(solution)/shard_map/ppermute | solution.py:32
  46.0 25.5 %collective-permute-start.5 = (bf16[64,2176]{1,0:T(8,128)(2,1)S(1)}, bf16[64,2176]{1,0:T(8,128)(2,1)S(1)}, u32[]{:S(2)}, u32[]{:S(2)}) collective-permute-start(bf16[64,2176]{1,0:T(8,128)(2,1)S(1)} %get-tuple-element.27), channel_id=1, source_target_pairs={{0,12},{1,13},{2,14},{3,15},{4,8},{5,9},{6,10},{7,11},{8,4},{9,5},... | collective-permute-start | bytes 835592 | tf_op jit(solution)/shard_map/ppermute | solution.py:32
  46.2 2.3 %collective-permute-start.17 = (bf16[16,4096]{1,0:T(8,128)(2,1)S(1)}, bf16[16,4096]{1,0:T(8,128)(2,1)S(1)}, u32[]{:S(2)}, u32[]{:S(2)}) collective-permute-start(bf16[16,4096]{1,0:T(8,128)(2,1)S(1)} %shard_map.90.__1_.refs_0_.refs_2_), channel_id=1, source_target_pairs={{0,1},{1,0},{2,3},{3,2},{4,5},{5,4},{6,7},{7,6},{8,9},{9,8},{10,11... | collective-permute-start | bytes 393224 | tf_op jit(solution)/shard_map/ppermute | solution.py:32
  47.9 1.6 %collective-permute-start.18 = (bf16[16,4096]{1,0:T(8,128)(2,1)S(1)}, bf16[16,4096]{1,0:T(8,128)(2,1)S(1)}, u32[]{:S(2)}, u32[]{:S(2)}) collective-permute-start(bf16[16,4096]{1,0:T(8,128)(2,1)S(1)} %shard_map.94.refs_1_.refs_4_), channel_id=1, source_target_pairs={{0,1},{1,0},{2,3},{3,2},{4,5},{5,4},{6,7},{7,6},{8,9},{9,8},{10,11... | collective-permute-start | bytes 393224 | tf_op jit(solution)/shard_map/ppermute | solution.py:32
  74.5 1.9 %collective-permute-start.21 = (f32[2,8,1]{2,1,0:T(8,128)S(1)}, f32[2,8,1]{2,1,0:T(8,128)S(1)}, u32[]{:S(2)}, u32[]{:S(2)}) collective-permute-start(f32[2,8,1]{2,1,0:T(8,128)S(1)} %shard_map.96), channel_id=1, source_target_pairs={{0,1},{1,0},{2,3},{3,2},{4,5},{5,4},{6,7},{7,6},{8,9},{9,8},{10,11... | collective-permute-start | bytes 200 | tf_op jit(solution)/shard_map/ppermute | solution.py:32
  74.9 3.7 %collective-permute-start.20 = (f32[2,8,1]{2,1,0:T(8,128)S(1)}, f32[2,8,1]{2,1,0:T(8,128)S(1)}, u32[]{:S(2)}, u32[]{:S(2)}) collective-permute-start(f32[2,8,1]{2,1,0:T(8,128)S(1)} %shard_map.96), channel_id=1, source_target_pairs={{0,2},{1,3},{2,0},{3,1},{4,6},{5,7},{6,4},{7,5},{8,10},{9,11},{10,... | collective-permute-start | bytes 200 | tf_op jit(solution)/shard_map/ppermute | solution.py:32
  76.4 3.1 %collective-permute-start.19 = (f32[2,8,1]{2,1,0:T(8,128)S(1)}, f32[2,8,1]{2,1,0:T(8,128)S(1)}, u32[]{:S(2)}, u32[]{:S(2)}) collective-permute-start(f32[2,8,1]{2,1,0:T(8,128)S(1)} %shard_map.96), channel_id=1, source_target_pairs={{0,3},{1,2},{2,1},{3,0},{4,7},{5,6},{6,5},{7,4},{8,11},{9,10},{10,... | collective-permute-start | bytes 200 | tf_op jit(solution)/shard_map/ppermute | solution.py:32
  79.5 3.7 %collective-permute-start.22 = (f32[2,8,1]{2,1,0:T(8,128)S(1)}, f32[2,8,1]{2,1,0:T(8,128)S(1)}, u32[]{:S(2)}, u32[]{:S(2)}) collective-permute-start(f32[2,8,1]{2,1,0:T(8,128)S(1)} %add_add_fusion), channel_id=1, source_target_pairs={{0,4},{1,5},{2,6},{3,7},{4,0},{5,1},{6,2},{7,3},{8,12},{9,13},{10,... | collective-permute-start | bytes 200 | tf_op jit(solution)/shard_map/ppermute | solution.py:32
  83.2 4.5 %collective-permute-start.23 = (f32[2,8,1]{2,1,0:T(8,128)S(1)}, f32[2,8,1]{2,1,0:T(8,128)S(1)}, u32[]{:S(2)}, u32[]{:S(2)}) collective-permute-start(f32[2,8,1]{2,1,0:T(8,128)S(1)} %add.18), channel_id=1, source_target_pairs={{0,8},{1,9},{2,10},{3,11},{4,12},{5,13},{6,14},{7,15},{8,0},{9,1},... | collective-permute-start | bytes 200 | tf_op jit(solution)/shard_map/ppermute | solution.py:32
  (8 other events, 71.3 us)

commit v21 on v18

--- a/solution.py
+++ b/solution.py
@@ -475,8 +475,7 @@
 
     image = images(rot, lefts, halves, eigenvalues)
     parts = score_parts(grads, ranks, grad_basis, image, seq_count)
-    parts = parts + sum(swap(parts, "wide", r) for r in (3, 2, 1))
-    bit = 4
+    bit = 1
     while bit < wide_count:
         parts = parts + swap(parts, "wide", bit)
         bit *= 2

time: 88.5 us -> 88.3 us (level)
    ppermute x24 -> x23, waiting for transfers between devices: 27.7 us -> 27.6 us  [swap(): return lax.ppermute(x, axis, [(i, i ^ bit) for i in range(count)])]
    ppermute x24 -> x23, starting transfers between devices: 26.7 us -> 26.7 us  [swap(): return lax.ppermute(x, axis, [(i, i ^ bit) for i in range(count)])]
  transfers between devices with their start and end apart: 24 -> 23, of which waited for: 10 -> 10; matrix products, arithmetic and copies ran while one was open for 0% -> 0% of each run, Pallas kernels for 30% -> 30%
where the time goes in v21:
time: 88.3 us; the launch traced here: 88.2 us
  Pallas kernels  29.4 us (33%)
  waiting for transfers between devices  27.6 us (31%)
  starting transfers between devices  26.7 us (30%)
  local copies, waits for them, and re-layouts  3.66 us (4%)
    ppermute x23, waiting for transfers between devices, swap(): return lax.ppermute(x, axis, [(i, i ^ bit) for i in range(count)])  27.6 us
    ppermute x23, starting transfers between devices, swap(): return lax.ppermute(x, axis, [(i, i ^ bit) for i in range(count)])  26.7 us
    pallas_call x1, Pallas kernels, images(): pl.pallas_call(functools.partial(image_kernel, batch_count, total, per),...  22 us
    unnamed x16, local copies, waits for them, and re-layouts  3.66 us
    pallas_call x1, Pallas kernels, score_parts(): pl.pallas_call(functools.partial(score_kernel, batch_count, ranks, count)...  2.98 us
    pallas_call x2, Pallas kernels, rotate(): pl.pallas_call(functools.partial(rotate_kernel, len(act_pieces), done), i...  2.64 us
  transfers between devices with their start and end apart: 23, of which 10 were waited for; matrix products, arithmetic and copies ran while one was open for 0% of the time, Pallas kernels for 30%

profile of v21, /device:TPU:0, one launch (start us, length us, event | category | flops | bytes accessed | tf_op | source)
XLA Modules:
  0.0 88.2 jit_solution(9352039139863886434)
XLA Ops:
  0.0 1.8 %copy-done.3 = bf16[2,16,36864]{2,1,0:T(8,128)(2,1)S(1)} copy-done((bf16[2,16,36864]{2,1,0:T(8,128)(2,1)S(1)}, bf16[2,16,36864]{2,1,0:T(8,128)(2,1)}, u32[]{:S(2)}) %copy-start.3) | copy-done | bytes 2359320
  2.4 1.2 %copy-done.1 = bf16[16,32768]{1,0:T(8,128)(2,1)S(1)} copy-done((bf16[16,32768]{1,0:T(8,128)(2,1)S(1)}, bf16[16,32768]{1,0:T(8,128)(2,1)}, u32[]{:S(2)}) %copy-start.1) | copy-done | bytes 1048600
  5.7 3.0 %collective-permute-start.9 = (bf16[16,10240]{1,0:T(8,128)(2,1)S(1)}, bf16[16,10240]{1,0:T(8,128)(2,1)S(1)}, u32[]{:S(2)}, u32[]{:S(2)}) collective-permute-start(bf16[16,10240]{1,0:T(8,128)(2,1)S(1)} %get-tuple-element.19._), channel_id=1, source_target_pairs={{0,2},{1,3},{2,0},{3,1},{4,6},{5,7},{6,4},{7,5},{8,10},{9,11},{10,... | collective-permute-start | bytes 983048 | tf_op jit(solution)/shard_map/ppermute | solution.py:32
  8.8 2.6 %collective-permute-start.7 = (bf16[16,4096]{1,0:T(8,128)(2,1)S(1)}, bf16[16,4096]{1,0:T(8,128)(2,1)S(1)}, u32[]{:S(2)}, u32[]{:S(2)}) collective-permute-start(bf16[16,4096]{1,0:T(8,128)(2,1)S(1)} %copy-done.5), channel_id=1, source_target_pairs={{0,8},{1,9},{2,10},{3,11},{4,12},{5,13},{6,14},{7,15},{8,0},{9,1},... | collective-permute-start | bytes 393224 | tf_op jit(solution)/shard_map/ppermute | solution.py:32
  11.4 1.6 %collective-permute-start.6 = (bf16[16,4096]{1,0:T(8,128)(2,1)S(1)}, bf16[16,4096]{1,0:T(8,128)(2,1)S(1)}, u32[]{:S(2)}, u32[]{:S(2)}) collective-permute-start(bf16[16,4096]{1,0:T(8,128)(2,1)S(1)} %copy-done.5), channel_id=1, source_target_pairs={{0,4},{1,5},{2,6},{3,7},{4,0},{5,1},{6,2},{7,3},{8,12},{9,13},{10,... | collective-permute-start | bytes 393224 | tf_op jit(solution)/shard_map/ppermute | solution.py:32
  13.6 3.7 %collective-permute-done.9.got_ref = bf16[16,10240]{1,0:T(8,128)(2,1)S(1)} collective-permute-done((bf16[16,10240]{1,0:T(8,128)(2,1)S(1)}, bf16[16,10240]{1,0:T(8,128)(2,1)S(1)}, u32[]{:S(2)}, u32[]{:S(2)}) %collective-permute-start.9) | collective-permute-done | bytes 327712 | tf_op jit(solution)/shard_map/ppermute | solution.py:32
  17.4 4.2 %collective-permute-done.7.refs_2_ = bf16[16,4096]{1,0:T(8,128)(2,1)S(1)} collective-permute-done((bf16[16,4096]{1,0:T(8,128)(2,1)S(1)}, bf16[16,4096]{1,0:T(8,128)(2,1)S(1)}, u32[]{:S(2)}, u32[]{:S(2)}) %collective-permute-start.7) | collective-permute-done | bytes 131104 | tf_op jit(solution)/shard_map/ppermute | solution.py:32
  22.2 2.4 %collective-permute-start.11 = (bf16[16,4096]{1,0:T(8,128)(2,1)S(1)}, bf16[16,4096]{1,0:T(8,128)(2,1)S(1)}, u32[]{:S(2)}, u32[]{:S(2)}) collective-permute-start(bf16[16,4096]{1,0:T(8,128)(2,1)S(1)} %get-tuple-element.26), channel_id=1, source_target_pairs={{0,4},{1,5},{2,6},{3,7},{4,0},{5,1},{6,2},{7,3},{8,12},{9,13},{10,... | collective-permute-start | bytes 393224 | tf_op jit(solution)/shard_map/ppermute | solution.py:32
  24.5 1.9 %collective-permute-start.12 = (bf16[16,4096]{1,0:T(8,128)(2,1)S(1)}, bf16[16,4096]{1,0:T(8,128)(2,1)S(1)}, u32[]{:S(2)}, u32[]{:S(2)}) collective-permute-start(bf16[16,4096]{1,0:T(8,128)(2,1)S(1)} %get-tuple-element.27), channel_id=1, source_target_pairs={{0,8},{1,9},{2,10},{3,11},{4,12},{5,13},{6,14},{7,15},{8,0},{9,1},... | collective-permute-start | bytes 393224 | tf_op jit(solution)/shard_map/ppermute | solution.py:32
  26.5 1.5 %collective-permute-start.13 = (bf16[16,4096]{1,0:T(8,128)(2,1)S(1)}, bf16[16,4096]{1,0:T(8,128)(2,1)S(1)}, u32[]{:S(2)}, u32[]{:S(2)}) collective-permute-start(bf16[16,4096]{1,0:T(8,128)(2,1)S(1)} %get-tuple-element.28), channel_id=1, source_target_pairs={{0,12},{1,13},{2,14},{3,15},{4,8},{5,9},{6,10},{7,11},{8,4},{9,5},... | collective-permute-start | bytes 393224 | tf_op jit(solution)/shard_map/ppermute | solution.py:32
  29.0 1.2 %collective-permute-done.11.refs_1_ = bf16[16,4096]{1,0:T(8,128)(2,1)S(1)} collective-permute-done((bf16[16,4096]{1,0:T(8,128)(2,1)S(1)}, bf16[16,4096]{1,0:T(8,128)(2,1)S(1)}, u32[]{:S(2)}, u32[]{:S(2)}) %collective-permute-start.11) | collective-permute-done | bytes 131104 | tf_op jit(solution)/shard_map/ppermute | solution.py:32
  30.1 6.6 %collective-permute-done.12.refs_2_ = bf16[16,4096]{1,0:T(8,128)(2,1)S(1)} collective-permute-done((bf16[16,4096]{1,0:T(8,128)(2,1)S(1)}, bf16[16,4096]{1,0:T(8,128)(2,1)S(1)}, u32[]{:S(2)}, u32[]{:S(2)}) %collective-permute-start.12) | collective-permute-done | bytes 131104 | tf_op jit(solution)/shard_map/ppermute | solution.py:32
  36.8 2.5 %collective-permute-done.10.refs_4_.__0_ = bf16[64,4096]{1,0:T(8,128)(2,1)S(1)} collective-permute-done((bf16[64,4096]{1,0:T(8,128)(2,1)S(1)}, bf16[64,4096]{1,0:T(8,128)(2,1)S(1)}, u32[]{:S(2)}, u32[]{:S(2)}) %collective-permute-start.10) | collective-permute-done | bytes 524320 | tf_op jit(solution)/shard_map/ppermute | solution.py:32
  40.0 1.7 %collective-permute-start.16 = (bf16[16,4096]{1,0:T(8,128)(2,1)S(1)}, bf16[16,4096]{1,0:T(8,128)(2,1)S(1)}, u32[]{:S(2)}, u32[]{:S(2)}) collective-permute-start(bf16[16,4096]{1,0:T(8,128)(2,1)S(1)} %shard_map.91.__1_.refs_0_.refs_2_), channel_id=1, source_target_pairs={{0,16},{16,0},{1,17},{17,1},{2,18},{18,2},{3,19},{19,3},{4,20},{20... | collective-permute-start | bytes 393224 | tf_op jit(solution)/shard_map/ppermute | solution.py:32
  41.7 1.6 %collective-permute-start.3 = (bf16[64,2176]{1,0:T(8,128)(2,1)S(1)}, bf16[64,2176]{1,0:T(8,128)(2,1)S(1)}, u32[]{:S(2)}, u32[]{:S(2)}) collective-permute-start(bf16[64,2176]{1,0:T(8,128)(2,1)S(1)} %get-tuple-element.21), channel_id=1, source_target_pairs={{0,4},{1,5},{2,6},{3,7},{4,0},{5,1},{6,2},{7,3},{8,12},{9,13},{10,... | collective-permute-start | bytes 835592 | tf_op jit(solution)/shard_map/ppermute | solution.py:32
  43.3 2.6 %collective-permute-start.4 = (bf16[64,2176]{1,0:T(8,128)(2,1)S(1)}, bf16[64,2176]{1,0:T(8,128)(2,1)S(1)}, u32[]{:S(2)}, u32[]{:S(2)}) collective-permute-start(bf16[64,2176]{1,0:T(8,128)(2,1)S(1)} %get-tuple-element.22), channel_id=1, source_target_pairs={{0,8},{1,9},{2,10},{3,11},{4,12},{5,13},{6,14},{7,15},{8,0},{9,1},... | collective-permute-start | bytes 835592 | tf_op jit(solution)/shard_map/ppermute | solution.py:32
  46.1 1.7 %shard_map.94.__1_.rot_ref = bf16[4096,256]{1,0:T(8,128)(2,1)S(1)} custom-call(bf16[64,4096]{1,0:T(8,128)(2,1)S(1)} %shard_map.92.refs_0_, bf16[64,4096]{1,0:T(8,128)(2,1)S(1)} %collective-permute-done.14.refs_1_, bf16[64,4096]{1,0:T(8,128)(2,1)S(1)} %collective-permute-done.15.refs_2_, bf16[512,4096]{1,0:T(8,128)(2,1)S(1)} %copy-done, ...), custom_call_target="tpu_custom_call" | custom-call | bytes 1 | tf_op jit(solution)/shard_map/pallas_call | solution.py:274
  49.4 22.0 %shard_map.96.refs_9_ = f32[2,2048,256]{2,1,0:T(8,128)S(1)} custom-call(bf16[4096,256]{1,0:T(8,128)(2,1)S(1)} %shard_map.94.__1_.rot_ref, bf16[16,4096]{1,0:T(8,128)(2,1)S(1)} %shard_map.91.__1_.refs_0_.refs_2_, bf16[16,4096]{1,0:T(8,128)(2,1)S(1)} %shard_map.95.refs_1_.refs_4_, bf16[16,4096]{1,0:T(8,128)(2,1)S(1)} %shard_map.91.__1_.refs_0_.refs_2_, ...), custom_call_target="tpu_custom_call" | custom-call | flops 1000000000 | bytes 1 | tf_op jit(solution)/shard_map/pallas_call | solution.py:361
  71.4 3.0 %shard_map.97 = f32[2,8,1]{2,1,0:T(8,128)S(1)} custom-call(bf16[64,2176]{1,0:T(8,128)(2,1)S(1)} %get-tuple-element.20.refs_6_.refs_0_.refs_4_, bf16[64,2176]{1,0:T(8,128)(2,1)S(1)} %collective-permute-done.3.refs_1_.refs_5_, bf16[64,2176]{1,0:T(8,128)(2,1)S(1)} %collective-permute-done.4.refs_2_.refs_6_, ...), custom_call_target="tpu_custom_call" | custom-call | flops 536870912 | bytes 4194304 | tf_op jit(solution)/shard_map/pallas_call | solution.py:417
  75.6 1.5 %collective-permute-start.20 = (f32[2,8,1]{2,1,0:T(8,128)S(1)}, f32[2,8,1]{2,1,0:T(8,128)S(1)}, u32[]{:S(2)}, u32[]{:S(2)}) collective-permute-start(f32[2,8,1]{2,1,0:T(8,128)S(1)} %add.12), channel_id=1, source_target_pairs={{0,2},{1,3},{2,0},{3,1},{4,6},{5,7},{6,4},{7,5},{8,10},{9,11},{10,... | collective-permute-start | bytes 200 | tf_op jit(solution)/shard_map/ppermute | solution.py:32
  77.2 2.1 %collective-permute-done.20 = f32[2,8,1]{2,1,0:T(8,128)S(1)} collective-permute-done((f32[2,8,1]{2,1,0:T(8,128)S(1)}, f32[2,8,1]{2,1,0:T(8,128)S(1)}, u32[]{:S(2)}, u32[]{:S(2)}) %collective-permute-start.20) | collective-permute-done | bytes 96 | tf_op jit(solution)/shard_map/ppermute | solution.py:32
  80.0 3.0 %collective-permute-done.21 = f32[2,8,1]{2,1,0:T(8,128)S(1)} collective-permute-done((f32[2,8,1]{2,1,0:T(8,128)S(1)}, f32[2,8,1]{2,1,0:T(8,128)S(1)}, u32[]{:S(2)}, u32[]{:S(2)}) %collective-permute-start.21) | collective-permute-done | bytes 96 | tf_op jit(solution)/shard_map/ppermute | solution.py:32
  83.0 2.1 %collective-permute-start.22 = (f32[2,8,1]{2,1,0:T(8,128)S(1)}, f32[2,8,1]{2,1,0:T(8,128)S(1)}, u32[]{:S(2)}, u32[]{:S(2)}) collective-permute-start(f32[2,8,1]{2,1,0:T(8,128)S(1)} %add.14), channel_id=1, source_target_pairs={{0,8},{1,9},{2,10},{3,11},{4,12},{5,13},{6,14},{7,15},{8,0},{9,1},... | collective-permute-start | bytes 200 | tf_op jit(solution)/shard_map/ppermute | solution.py:32
  85.1 2.4 %collective-permute-done.22 = f32[2,8,1]{2,1,0:T(8,128)S(1)} collective-permute-done((f32[2,8,1]{2,1,0:T(8,128)S(1)}, f32[2,8,1]{2,1,0:T(8,128)S(1)}, u32[]{:S(2)}, u32[]{:S(2)}) %collective-permute-start.22) | collective-permute-done | bytes 96 | tf_op jit(solution)/shard_map/ppermute | solution.py:32
  (58 shorter events, 10.1 us)
Async XLA Ops:
  1.8 3.7 %collective-permute-start.1 = (bf16[16,18432]{1,0:T(8,128)(2,1)S(1)}, bf16[16,18432]{1,0:T(8,128)(2,1)S(1)}, u32[]{:S(2)}, u32[]{:S(2)}) collective-permute-start(bf16[16,18432]{1,0:T(8,128)(2,1)S(1)} %get-tuple-element.18), channel_id=1, source_target_pairs={{0,1},{1,0},{2,3},{3,2},{4,5},{5,4},{6,7},{7,6},{8,9},{9,8},{10,11... | collective-permute-start | bytes 1769480 | tf_op jit(solution)/shard_map/ppermute | solution.py:32
  4.8 8.3 %collective-permute-start = (bf16[16,16512]{1,0:T(8,128)(2,1)S(1)}, bf16[16,16512]{1,0:T(8,128)(2,1)S(1)}, u32[]{:S(2)}, u32[]{:S(2)}) collective-permute-start(bf16[16,16512]{1,0:T(8,128)(2,1)S(1)} %shard_map.83.refs_0_.sent_ref), channel_id=1, source_target_pairs={{0,1},{1,0},{2,3},{3,2},{4,5},{5,4},{6,7},{7,6},{8,9},{9,8},{10,11... | collective-permute-start | bytes 1585160 | tf_op jit(solution)/shard_map/ppermute | solution.py:32
  5.7 11.5 %collective-permute-start.9 = (bf16[16,10240]{1,0:T(8,128)(2,1)S(1)}, bf16[16,10240]{1,0:T(8,128)(2,1)S(1)}, u32[]{:S(2)}, u32[]{:S(2)}) collective-permute-start(bf16[16,10240]{1,0:T(8,128)(2,1)S(1)} %get-tuple-element.19._), channel_id=1, source_target_pairs={{0,2},{1,3},{2,0},{3,1},{4,6},{5,7},{6,4},{7,5},{8,10},{9,11},{10,... | collective-permute-start | bytes 983048 | tf_op jit(solution)/shard_map/ppermute | solution.py:32
  8.8 12.8 %collective-permute-start.7 = (bf16[16,4096]{1,0:T(8,128)(2,1)S(1)}, bf16[16,4096]{1,0:T(8,128)(2,1)S(1)}, u32[]{:S(2)}, u32[]{:S(2)}) collective-permute-start(bf16[16,4096]{1,0:T(8,128)(2,1)S(1)} %copy-done.5), channel_id=1, source_target_pairs={{0,8},{1,9},{2,10},{3,11},{4,12},{5,13},{6,14},{7,15},{8,0},{9,1},... | collective-permute-start | bytes 393224 | tf_op jit(solution)/shard_map/ppermute | solution.py:32
  11.4 10.2 %collective-permute-start.6 = (bf16[16,4096]{1,0:T(8,128)(2,1)S(1)}, bf16[16,4096]{1,0:T(8,128)(2,1)S(1)}, u32[]{:S(2)}, u32[]{:S(2)}) collective-permute-start(bf16[16,4096]{1,0:T(8,128)(2,1)S(1)} %copy-done.5), channel_id=1, source_target_pairs={{0,4},{1,5},{2,6},{3,7},{4,0},{5,1},{6,2},{7,3},{8,12},{9,13},{10,... | collective-permute-start | bytes 393224 | tf_op jit(solution)/shard_map/ppermute | solution.py:32
  12.9 8.6 %collective-permute-start.8 = (bf16[16,4096]{1,0:T(8,128)(2,1)S(1)}, bf16[16,4096]{1,0:T(8,128)(2,1)S(1)}, u32[]{:S(2)}, u32[]{:S(2)}) collective-permute-start(bf16[16,4096]{1,0:T(8,128)(2,1)S(1)} %copy-done.5), channel_id=1, source_target_pairs={{0,12},{1,13},{2,14},{3,15},{4,8},{5,9},{6,10},{7,11},{8,4},{9,5},... | collective-permute-start | bytes 393224 | tf_op jit(solution)/shard_map/ppermute | solution.py:32
  13.2 15.7 %collective-permute-start.2 = (bf16[32,8320]{1,0:T(8,128)(2,1)S(1)}, bf16[32,8320]{1,0:T(8,128)(2,1)S(1)}, u32[]{:S(2)}, u32[]{:S(2)}) collective-permute-start(bf16[32,8320]{1,0:T(8,128)(2,1)S(1)} %shard_map.86.refs_0_), channel_id=1, source_target_pairs={{0,2},{1,3},{2,0},{3,1},{4,6},{5,7},{6,4},{7,5},{8,10},{9,11},{10,... | collective-permute-start | bytes 1597448 | tf_op jit(solution)/shard_map/ppermute | solution.py:32
  21.6 17.7 %collective-permute-start.10 = (bf16[64,4096]{1,0:T(8,128)(2,1)S(1)}, bf16[64,4096]{1,0:T(8,128)(2,1)S(1)}, u32[]{:S(2)}, u32[]{:S(2)}) collective-permute-start(bf16[64,4096]{1,0:T(8,128)(2,1)S(1)} %shard_map.89.refs_0_.__0_), channel_id=1, source_target_pairs={{0,2},{1,3},{2,0},{3,1},{4,6},{5,7},{6,4},{7,5},{8,10},{9,11},{10,... | collective-permute-start | bytes 1572872 | tf_op jit(solution)/shard_map/ppermute | solution.py:32
  22.2 8.0 %collective-permute-start.11 = (bf16[16,4096]{1,0:T(8,128)(2,1)S(1)}, bf16[16,4096]{1,0:T(8,128)(2,1)S(1)}, u32[]{:S(2)}, u32[]{:S(2)}) collective-permute-start(bf16[16,4096]{1,0:T(8,128)(2,1)S(1)} %get-tuple-element.26), channel_id=1, source_target_pairs={{0,4},{1,5},{2,6},{3,7},{4,0},{5,1},{6,2},{7,3},{8,12},{9,13},{10,... | collective-permute-start | bytes 393224 | tf_op jit(solution)/shard_map/ppermute | solution.py:32
  24.5 12.2 %collective-permute-start.12 = (bf16[16,4096]{1,0:T(8,128)(2,1)S(1)}, bf16[16,4096]{1,0:T(8,128)(2,1)S(1)}, u32[]{:S(2)}, u32[]{:S(2)}) collective-permute-start(bf16[16,4096]{1,0:T(8,128)(2,1)S(1)} %get-tuple-element.27), channel_id=1, source_target_pairs={{0,8},{1,9},{2,10},{3,11},{4,12},{5,13},{6,14},{7,15},{8,0},{9,1},... | collective-permute-start | bytes 393224 | tf_op jit(solution)/shard_map/ppermute | solution.py:32
  26.5 10.3 %collective-permute-start.13 = (bf16[16,4096]{1,0:T(8,128)(2,1)S(1)}, bf16[16,4096]{1,0:T(8,128)(2,1)S(1)}, u32[]{:S(2)}, u32[]{:S(2)}) collective-permute-start(bf16[16,4096]{1,0:T(8,128)(2,1)S(1)} %get-tuple-element.28), channel_id=1, source_target_pairs={{0,12},{1,13},{2,14},{3,15},{4,8},{5,9},{6,10},{7,11},{8,4},{9,5},... | collective-permute-start | bytes 393224 | tf_op jit(solution)/shard_map/ppermute | solution.py:32
  39.4 6.5 %collective-permute-start.14 = (bf16[64,4096]{1,0:T(8,128)(2,1)S(1)}, bf16[64,4096]{1,0:T(8,128)(2,1)S(1)}, u32[]{:S(2)}, u32[]{:S(2)}) collective-permute-start(bf16[64,4096]{1,0:T(8,128)(2,1)S(1)} %shard_map.93), channel_id=1, source_target_pairs={{0,1},{1,0},{2,3},{3,2},{4,5},{5,4},{6,7},{7,6},{8,9},{9,8},{10,11... | collective-permute-start | bytes 1572872 | tf_op jit(solution)/shard_map/ppermute | solution.py:32
  39.5 6.6 %collective-permute-start.15 = (bf16[64,4096]{1,0:T(8,128)(2,1)S(1)}, bf16[64,4096]{1,0:T(8,128)(2,1)S(1)}, u32[]{:S(2)}, u32[]{:S(2)}) collective-permute-start(bf16[64,4096]{1,0:T(8,128)(2,1)S(1)} %shard_map.92.refs_0_), channel_id=1, source_target_pairs={{0,1},{1,0},{2,3},{3,2},{4,5},{5,4},{6,7},{7,6},{8,9},{9,8},{10,11... | collective-permute-start | bytes 1572872 | tf_op jit(solution)/shard_map/ppermute | solution.py:32
  40.0 7.8 %collective-permute-start.16 = (bf16[16,4096]{1,0:T(8,128)(2,1)S(1)}, bf16[16,4096]{1,0:T(8,128)(2,1)S(1)}, u32[]{:S(2)}, u32[]{:S(2)}) collective-permute-start(bf16[16,4096]{1,0:T(8,128)(2,1)S(1)} %shard_map.91.__1_.refs_0_.refs_2_), channel_id=1, source_target_pairs={{0,16},{16,0},{1,17},{17,1},{2,18},{18,2},{3,19},{19,3},{4,20},{20... | collective-permute-start | bytes 393224 | tf_op jit(solution)/shard_map/ppermute | solution.py:32
  41.7 29.7 %collective-permute-start.3 = (bf16[64,2176]{1,0:T(8,128)(2,1)S(1)}, bf16[64,2176]{1,0:T(8,128)(2,1)S(1)}, u32[]{:S(2)}, u32[]{:S(2)}) collective-permute-start(bf16[64,2176]{1,0:T(8,128)(2,1)S(1)} %get-tuple-element.21), channel_id=1, source_target_pairs={{0,4},{1,5},{2,6},{3,7},{4,0},{5,1},{6,2},{7,3},{8,12},{9,13},{10,... | collective-permute-start | bytes 835592 | tf_op jit(solution)/shard_map/ppermute | solution.py:32
  43.3 28.1 %collective-permute-start.4 = (bf16[64,2176]{1,0:T(8,128)(2,1)S(1)}, bf16[64,2176]{1,0:T(8,128)(2,1)S(1)}, u32[]{:S(2)}, u32[]{:S(2)}) collective-permute-start(bf16[64,2176]{1,0:T(8,128)(2,1)S(1)} %get-tuple-element.22), channel_id=1, source_target_pairs={{0,8},{1,9},{2,10},{3,11},{4,12},{5,13},{6,14},{7,15},{8,0},{9,1},... | collective-permute-start | bytes 835592 | tf_op jit(solution)/shard_map/ppermute | solution.py:32
  45.9 25.5 %collective-permute-start.5 = (bf16[64,2176]{1,0:T(8,128)(2,1)S(1)}, bf16[64,2176]{1,0:T(8,128)(2,1)S(1)}, u32[]{:S(2)}, u32[]{:S(2)}) collective-permute-start(bf16[64,2176]{1,0:T(8,128)(2,1)S(1)} %get-tuple-element.23), channel_id=1, source_target_pairs={{0,12},{1,13},{2,14},{3,15},{4,8},{5,9},{6,10},{7,11},{8,4},{9,5},... | collective-permute-start | bytes 835592 | tf_op jit(solution)/shard_map/ppermute | solution.py:32
  46.1 2.3 %collective-permute-start.17 = (bf16[16,4096]{1,0:T(8,128)(2,1)S(1)}, bf16[16,4096]{1,0:T(8,128)(2,1)S(1)}, u32[]{:S(2)}, u32[]{:S(2)}) collective-permute-start(bf16[16,4096]{1,0:T(8,128)(2,1)S(1)} %shard_map.91.__1_.refs_0_.refs_2_), channel_id=1, source_target_pairs={{0,1},{1,0},{2,3},{3,2},{4,5},{5,4},{6,7},{7,6},{8,9},{9,8},{10,11... | collective-permute-start | bytes 393224 | tf_op jit(solution)/shard_map/ppermute | solution.py:32
  47.8 23.6 %copy-start.4 = (bf16[512,2048]{1,0:T(8,128)(2,1)S(1)}, bf16[512,2048]{1,0:T(8,128)(2,1)}, u32[]{:S(2)}) copy-start(bf16[512,2048]{1,0:T(8,128)(2,1)} %refs_8_.1) | copy-start | bytes 6291460
  47.9 1.6 %collective-permute-start.18 = (bf16[16,4096]{1,0:T(8,128)(2,1)S(1)}, bf16[16,4096]{1,0:T(8,128)(2,1)S(1)}, u32[]{:S(2)}, u32[]{:S(2)}) collective-permute-start(bf16[16,4096]{1,0:T(8,128)(2,1)S(1)} %shard_map.95.refs_1_.refs_4_), channel_id=1, source_target_pairs={{0,1},{1,0},{2,3},{3,2},{4,5},{5,4},{6,7},{7,6},{8,9},{9,8},{10,11... | collective-permute-start | bytes 393224 | tf_op jit(solution)/shard_map/ppermute | solution.py:32
  74.4 1.2 %collective-permute-start.19 = (f32[2,8,1]{2,1,0:T(8,128)S(1)}, f32[2,8,1]{2,1,0:T(8,128)S(1)}, u32[]{:S(2)}, u32[]{:S(2)}) collective-permute-start(f32[2,8,1]{2,1,0:T(8,128)S(1)} %shard_map.97), channel_id=1, source_target_pairs={{0,1},{1,0},{2,3},{3,2},{4,5},{5,4},{6,7},{7,6},{8,9},{9,8},{10,11... | collective-permute-start | bytes 200 | tf_op jit(solution)/shard_map/ppermute | solution.py:32
  75.6 3.7 %collective-permute-start.20 = (f32[2,8,1]{2,1,0:T(8,128)S(1)}, f32[2,8,1]{2,1,0:T(8,128)S(1)}, u32[]{:S(2)}, u32[]{:S(2)}) collective-permute-start(f32[2,8,1]{2,1,0:T(8,128)S(1)} %add.12), channel_id=1, source_target_pairs={{0,2},{1,3},{2,0},{3,1},{4,6},{5,7},{6,4},{7,5},{8,10},{9,11},{10,... | collective-permute-start | bytes 200 | tf_op jit(solution)/shard_map/ppermute | solution.py:32
  79.3 3.7 %collective-permute-start.21 = (f32[2,8,1]{2,1,0:T(8,128)S(1)}, f32[2,8,1]{2,1,0:T(8,128)S(1)}, u32[]{:S(2)}, u32[]{:S(2)}) collective-permute-start(f32[2,8,1]{2,1,0:T(8,128)S(1)} %add.13), channel_id=1, source_target_pairs={{0,4},{1,5},{2,6},{3,7},{4,0},{5,1},{6,2},{7,3},{8,12},{9,13},{10,... | collective-permute-start | bytes 200 | tf_op jit(solution)/shard_map/ppermute | solution.py:32
  83.0 4.5 %collective-permute-start.22 = (f32[2,8,1]{2,1,0:T(8,128)S(1)}, f32[2,8,1]{2,1,0:T(8,128)S(1)}, u32[]{:S(2)}, u32[]{:S(2)}) collective-permute-start(f32[2,8,1]{2,1,0:T(8,128)S(1)} %add.14), channel_id=1, source_target_pairs={{0,8},{1,9},{2,10},{3,11},{4,12},{5,13},{6,14},{7,15},{8,0},{9,1},... | collective-permute-start | bytes 200 | tf_op jit(solution)/shard_map/ppermute | solution.py:32
  (7 other events, 50.1 us)
